TPU v7x, 32 devices: a whole 2x2x4 slice. The times are simulated.
32 devices in a mesh: row: 4 (over x, core), col: 2 (over y), gz: 4 (over z).
Axes of the slice: x: 2, y: 2, z: 4, core: 2. Of those that a mesh axis runs over, the one named last changes fastest.
Arguments:
- volume_field: bfloat16 [128, 32, 16, 512], P(None, 'row', 'col', 'gz'), may hold values from -6 to 6
- volume_load: bfloat16 [128, 32, 16, 512], P(None, 'row', 'col', 'gz'), may hold values from -6 to 6
- coefficient: float32 [32, 16, 512], P('row', 'col', 'gz'), may hold values from 0.25 to 2
- surface_block: bfloat16 [1024, 32768], P('row', 'col'), may hold values from -0.046875 to 0.046875
- trace_cell: int32 [4, 2, 4, 1024], P('row', 'col', 'gz'), may hold values from 0 to 8191, as said below
- flux_cell: int32 [4, 2, 4, 32], P('row', 'col', 'gz'), may hold values from 0 to 8191, as said below
Outputs:
- new_field: bfloat16 [128, 32, 16, 512], P(None, 'row', 'col', 'gz')
- surface_flux: float32 [128, 1024], P('gz', ('row', 'col'))
Inputs may be any that keep to these rules, and one draw needn't show every extreme that they name: `trace_cell`: within each device's 1024 entries, entry values are local cell numbers, one from each aligned run of 8 consecutive cells, in a permuted order; the first and last cells of the block are always chosen. `flux_cell`: within each device's 32 entries, entry values are local cell numbers, one from each aligned run of 256 consecutive cells, in a permuted order; the first and last cells of the block are always chosen.
All inputs are finite; a program needn't handle non-finite values.
Results may differ from a plain program's by a relative error of at most 0.0032.
Values may be sent and summed in bfloat16 or wider, within the bound.
No kernel may reach another device: no remote copies, remote signals or barrier semaphores. Data moves between devices by JAX's collectives and lax.ppermute only.
A program may use at most 128 MiB of HBM per device.

v0:
```python
import jax
import jax.numpy as jnp
from jax import lax
from jax.sharding import PartitionSpec as P

OMEGA = 0.8


def padded_2(array, sides, width):
    for axis, dim in sides:
        peers, length = (lax.axis_size(axis), array.shape[dim])
        up = [(i, (i + 1) % peers) for i in range(peers - 1)]
        down = [(j, i) for i, j in up]
        last = lax.slice_in_dim(array, length - width, length, axis=dim)
        first = lax.slice_in_dim(array, 0, width, axis=dim)
        before = lax.ppermute(last, axis, up)
        after = lax.ppermute(first, axis, down)
        array = jnp.concatenate([before, array, after], axis=dim)
    return array


def relax(current, source, diagonal):
    padded = padded_2(current, (("row", 1), ("col", 2), ("gz", 3)), 1).astype(jnp.float32)
    centre = current.astype(jnp.float32)
    beside = padded[:, 2:, 1:-1, 1:-1] + padded[:, :-2, 1:-1, 1:-1]
    beside = beside + padded[:, 1:-1, 2:, 1:-1] + padded[:, 1:-1, :-2, 1:-1]
    beside = beside + padded[:, 1:-1, 1:-1, 2:] + padded[:, 1:-1, 1:-1, :-2]
    return (centre + OMEGA * (source - (diagonal * centre - beside)) / diagonal).astype(
        jnp.bfloat16
    )


def per_device(volume_field, volume_load, coefficient, surface_block, trace_cell, flux_cell):
    side_count, first_span, second_span, third_span = volume_field.shape
    cell_count = first_span * second_span * third_span
    slot_count = trace_cell.shape[3]
    flux_slots = flux_cell.shape[3]
    flat_field = volume_field.reshape(side_count, cell_count)
    picker = (
        lax.broadcasted_iota(jnp.int32, (cell_count, slot_count), 0)
        == trace_cell.reshape(1, slot_count)
    ).astype(jnp.bfloat16)
    trace_values = jnp.dot(flat_field, picker, preferred_element_type=jnp.float32).astype(
        jnp.bfloat16
    )
    regrouped = lax.all_to_all(trace_values, "gz", split_axis=0, concat_axis=1, tiled=True)
    partial_flux = lax.dot_general(
        lax.all_gather(regrouped, "row", axis=1, tiled=True),
        surface_block,
        (((1,), (1,)), ((), ())),
        preferred_element_type=jnp.float32,
    )
    surface_flux = lax.psum_scatter(partial_flux, "col", scatter_dimension=1, tiled=True)
    owned_flux = lax.all_to_all(surface_flux, "gz", split_axis=1, concat_axis=0, tiled=True)
    placer = (
        flux_cell.reshape(flux_slots, 1)
        == lax.broadcasted_iota(jnp.int32, (flux_slots, cell_count), 1)
    ).astype(jnp.float32)
    placed = jnp.dot(
        owned_flux, placer, precision=lax.Precision.HIGHEST, preferred_element_type=jnp.float32
    )
    source = volume_load.astype(jnp.float32) + placed.reshape(
        side_count, first_span, second_span, third_span
    )
    diagonal = 6.0 + coefficient
    current = volume_field
    for repeat in range(3):
        current = relax(current, source, diagonal)
    return (current, surface_flux)


def solution(mesh):
    in_specs = (
        P(None, "row", "col", "gz"),
        P(None, "row", "col", "gz"),
        P("row", "col", "gz"),
        P("row", "col"),
        P("row", "col", "gz", None),
        P("row", "col", "gz", None),
    )
    out_specs = (P(None, "row", "col", "gz"), P("gz", ("row", "col")))
    return jax.shard_map(
        per_device, mesh=mesh, in_specs=in_specs, out_specs=out_specs, check_vma=False
    )
```

profile of v0, /device:TPU:0, one launch (start us, length us, event | category | flops | bytes accessed | tf_op | source)
XLA Modules:
  0.0 190.8 jit_solution(7890692623972707570)
XLA Ops:
  7.2 7.6 %fusion.19 = bf16[1024,128]{0,1:T(8,128)(2,1)S(1)} fusion(bf16[16,8,64,128]{3,2,1,0:T(8,128)(2,1)} %bitcast.27, s32[1024]{0:T(1024)} %bitcast.33), kind=kOutput, calls=%fused_computation.45 | convolution fusion | flops 2156003328 | bytes 2363392 | tf_op jit(solution)/shard_map/dot_general | solution.py:43
  14.8 15.0 %all_to_all.38 = bf16[4,32,1024]{2,1,0:T(8,128)(2,1)S(1)} all-to-all(bf16[4,32,1024]{2,1,0:T(8,128)(2,1)S(1)} %bitcast.31), channel_id=1, replica_groups=mesh['row'=4,'col'=2,'gz'=4] {'gz'}, dimensions={0} | all-to-all | bytes 524288 | tf_op jit(solution)/shard_map/all_to_all | solution.py:46
  30.6 3.3 %copy.23 = bf16[128,8,8,128]{0,3,2,1:T(8,128)(2,1)S(1)} copy(bf16[128,8,8,128]{3,2,1,0:T(8,128)(2,1)} %param.6) | data formatting | bytes 4194304 | tf_op args[0]
  36.6 3.8 %collective-permute-done.1 = bf16[128,1,8,128]{0,3,2,1:T(8,128)(2,1)S(1)} collective-permute-done((bf16[128,1,8,128]{0,3,2,1:T(8,128)(2,1)S(1)}, bf16[128,1,8,128]{0,3,2,1:T(8,128)(2,1)S(1)}, u32[]{:S(2)}, u32[]{:S(2)}) %collective-permute-start.1) | collective-permute-done | bytes 262176 | tf_op jit(solution)/shard_map/ppermute | solution.py:17
  40.5 3.4 %collective-permute-start.2 = (bf16[128,10,1,128]{0,3,2,1:T(8,128)(2,1)S(1)}, bf16[128,10,1,128]{0,3,2,1:T(8,128)(2,1)S(1)}, u32[]{:S(2)}, u32[]{:S(2)}) collective-permute-start(bf16[128,10,1,128]{0,3,2,1:T(8,128)(2,1)S(1)} %get-tuple-element.18), channel_id=1, source_target_pairs={{0,4},{1,5},{2,6},{3,7},{8,12},{9,13},{10,14},{11,15},{16,20},{17,... | collective-permute-start | bytes 983048 | tf_op jit(solution)/shard_map/ppermute | solution.py:16
  45.3 3.2 %collective-permute-done.2 = bf16[128,10,1,128]{0,3,2,1:T(8,128)(2,1)S(1)} collective-permute-done((bf16[128,10,1,128]{0,3,2,1:T(8,128)(2,1)S(1)}, bf16[128,10,1,128]{0,3,2,1:T(8,128)(2,1)S(1)}, u32[]{:S(2)}, u32[]{:S(2)}) %collective-permute-start.2) | collective-permute-done | bytes 327712 | tf_op jit(solution)/shard_map/ppermute | solution.py:16
  48.5 4.4 %collective-permute-done.3 = bf16[128,10,1,128]{0,3,2,1:T(8,128)(2,1)S(1)} collective-permute-done((bf16[128,10,1,128]{0,3,2,1:T(8,128)(2,1)S(1)}, bf16[128,10,1,128]{0,3,2,1:T(8,128)(2,1)S(1)}, u32[]{:S(2)}, u32[]{:S(2)}) %collective-permute-start.3) | collective-permute-done | bytes 327712 | tf_op jit(solution)/shard_map/ppermute | solution.py:17
  53.7 2.1 %collective-permute-start.4 = (bf16[128,10,10,1]{0,3,2,1:T(2,128)(2,1)}, bf16[128,10,10,1]{0,3,2,1:T(2,128)(2,1)S(1)}, u32[]{:S(2)}, u32[]{:S(2)}) collective-permute-start(bf16[128,10,10,1]{0,3,2,1:T(2,128)(2,1)} %get-tuple-element.12), channel_id=1, source_target_pairs={{0,1},{1,2},{2,3},{4,5},{5,6},{6,7},{8,9},{9,10},{10,11},{12,13},{... | collective-permute-start | bytes 76808 | tf_op jit(solution)/shard_map/ppermute | solution.py:16
  57.1 7.0 %fusion.28 = f32[32,256]{1,0:T(8,128)} fusion(bf16[32,16384]{1,0:T(8,128)(2,1)} %all-gather.2.cloned.1.call-done, bf16[256,16384]{1,0:T(8,128)(2,1)} %param.9), kind=kOutput, calls=%fused_computation.79 | convolution fusion | flops 268435456 | bytes 9469952 | tf_op jit(solution)/shard_map/dot_general | solution.py:47
  64.7 4.2 %copy.24 = bf16[128,8,8,128]{0,3,2,1:T(8,128)(2,1)} copy(bf16[128,8,8,128]{3,2,1,0:T(8,128)(2,1)} %param.7) | data formatting | bytes 4194304 | tf_op args[1]
  68.9 13.1 %reduce-scatter.2.cloned.1.call-done = f32[32,128]{1,0:T(8,128)} async-done(((f32[32,256]{1,0:T(8,128)}), f32[32,128]{1,0:T(8,128)}) %reduce-scatter.2.cloned.1.call-update) | async-done | bytes 16400 | tf_op jit(solution)/shard_map/reduce_scatter | solution.py:53
  83.5 4.6 %all-to-all-start.1 = ((f32[4,1,1024]{2,1,0:T(1,128)}), f32[4,1,1024]{2,1,0:T(1,128)S(1)}, u32[]{:S(2)}, u32[]{:S(2)}) async-start(f32[4,1,1024]{2,1,0:T(1,128)} %reshape.43), calls=%async_computation.2 | async-start | bytes 32768 | tf_op jit(solution)/shard_map/all_to_all | solution.py:54
  88.1 4.8 %maximum_convert_fusion = f32[128,10,10,130]{0,3,2,1:T(8,128)} fusion(bf16[128,10,10,1]{0,3,2,1:T(2,128)(2,1)S(1)} %collective-permute-done.5, bf16[128,10,1,128]{0,3,2,1:T(8,128)(2,1)S(1)} %collective-permute-done.3, bf16[128,1,8,128]{0,3,2,1:T(8,128)(2,1)S(1)} %collective-permute-done.1, bf16[128,8,8,128]{0,3,2,1:T(8,128)(2,1)S(1)} %copy.23, ...), kind=kLoop, calls=%fused_computation.40 | loop fusion | flops 23296000 | bytes 9984000 | tf_op jit(solution)/shard_map/convert_element_type | solution.py:23
  95.1 14.1 %fusion.14 = (bf16[128,8,8,128]{0,3,2,1:T(8,128)(2,1)S(1)}, f32[128,8,8,128]{0,3,2,1:T(8,128)}) fusion(f32[128,10,10,130]{0,3,2,1:T(8,128)} %maximum_convert_fusion, bf16[128,8,8,128]{0,3,2,1:T(8,128)(2,1)S(1)} %copy.23, f32[8,8,128]{2,1,0:T(8,128)S(1)} %broadcast_add_fusion, f32[128,32,1,1]{1,0,3,2:T(8,128)S(1)} %bitcast.32, ...), kind=kOutput, calls=%fused_computation.37 | convolution fusion | flops 418643968 | bytes 35733632 | tf_op jit(solution)/shard_map/dot_general | solution.py:59
  111.8 3.8 %collective-permute-done.7 = bf16[128,1,8,128]{0,3,2,1:T(8,128)(2,1)S(1)} collective-permute-done((bf16[128,1,8,128]{0,3,2,1:T(8,128)(2,1)S(1)}, bf16[128,1,8,128]{0,3,2,1:T(8,128)(2,1)S(1)}, u32[]{:S(2)}, u32[]{:S(2)}) %collective-permute-start.7) | collective-permute-done | bytes 262176 | tf_op jit(solution)/shard_map/ppermute | solution.py:17
  115.8 2.5 %collective-permute-start.8 = (bf16[128,10,1,128]{0,3,2,1:T(8,128)(2,1)S(1)}, bf16[128,10,1,128]{0,3,2,1:T(8,128)(2,1)S(1)}, u32[]{:S(2)}, u32[]{:S(2)}) collective-permute-start(bf16[128,10,1,128]{0,3,2,1:T(8,128)(2,1)S(1)} %get-tuple-element.16), channel_id=1, source_target_pairs={{0,4},{1,5},{2,6},{3,7},{8,12},{9,13},{10,14},{11,15},{16,20},{17,... | collective-permute-start | bytes 983048 | tf_op jit(solution)/shard_map/ppermute | solution.py:16
  119.5 3.3 %collective-permute-done.8 = bf16[128,10,1,128]{0,3,2,1:T(8,128)(2,1)S(1)} collective-permute-done((bf16[128,10,1,128]{0,3,2,1:T(8,128)(2,1)S(1)}, bf16[128,10,1,128]{0,3,2,1:T(8,128)(2,1)S(1)}, u32[]{:S(2)}, u32[]{:S(2)}) %collective-permute-start.8) | collective-permute-done | bytes 327712 | tf_op jit(solution)/shard_map/ppermute | solution.py:16
  122.8 4.4 %collective-permute-done.9 = bf16[128,10,1,128]{0,3,2,1:T(8,128)(2,1)S(1)} collective-permute-done((bf16[128,10,1,128]{0,3,2,1:T(8,128)(2,1)S(1)}, bf16[128,10,1,128]{0,3,2,1:T(8,128)(2,1)S(1)}, u32[]{:S(2)}, u32[]{:S(2)}) %collective-permute-start.9) | collective-permute-done | bytes 327712 | tf_op jit(solution)/shard_map/ppermute | solution.py:17
  127.3 3.1 %collective-permute-start.10 = (bf16[128,10,10,1]{0,3,2,1:T(2,128)(2,1)S(1)}, bf16[128,10,10,1]{0,3,2,1:T(2,128)(2,1)S(1)}, u32[]{:S(2)}, u32[]{:S(2)}) collective-permute-start(bf16[128,10,10,1]{0,3,2,1:T(2,128)(2,1)S(1)} %get-tuple-element.10), channel_id=1, source_target_pairs={{0,1},{1,2},{2,3},{4,5},{5,6},{6,7},{8,9},{9,10},{10,11},{12,13},{... | collective-permute-start | bytes 76808 | tf_op jit(solution)/shard_map/ppermute | solution.py:16
  130.4 1.6 collective-permute-start.11
  132.1 4.5 %collective-permute-done.11 = bf16[128,10,10,1]{0,3,2,1:T(2,128)(2,1)S(1)} collective-permute-done((bf16[128,10,10,1]{0,3,2,1:T(2,128)(2,1)S(1)}, bf16[128,10,10,1]{0,3,2,1:T(2,128)(2,1)S(1)}, u32[]{:S(2)}, u32[]{:S(2)}) %collective-permute-start.11) | collective-permute-done | bytes 25632 | tf_op jit(solution)/shard_map/ppermute | solution.py:17
  136.7 3.0 %maximum_convert_fusion.1 = f32[128,10,10,130]{0,3,2,1:T(8,128)S(1)} fusion(bf16[128,10,10,1]{0,3,2,1:T(2,128)(2,1)S(1)} %collective-permute-done.11, bf16[128,10,1,128]{0,3,2,1:T(8,128)(2,1)S(1)} %collective-permute-done.9, bf16[128,1,8,128]{0,3,2,1:T(8,128)(2,1)S(1)} %collective-permute-done.7, bf16[128,8,8,128]{0,3,2,1:T(8,128)(2,1)S(1)} %get-tuple-element.26, ...), kind=kLoop, calls=%fused_computation.41 | loop fusion | flops 23296000 | bytes 9984000 | tf_op jit(solution)/shard_map/convert_element_type | solution.py:23
  139.7 4.5 %fusion.15 = bf16[128,8,8,128]{0,3,2,1:T(8,128)(2,1)S(1)} fusion(f32[128,8,8,128]{0,3,2,1:T(8,128)S(1)} %copy-done, f32[128,10,10,130]{0,3,2,1:T(8,128)S(1)} %maximum_convert_fusion.1, bf16[128,8,8,128]{0,3,2,1:T(8,128)(2,1)S(1)} %get-tuple-element.26, f32[8,8,128]{2,1,0:T(8,128)S(1)} %broadcast_add_fusion), kind=kLoop, calls=%fused_computation.38 | loop fusion | flops 13631488 | bytes 33587200 | tf_op jit(solution)/shard_map/convert_element_type | solution.py:28
  144.3 3.8 %collective-permute-start.12 = (bf16[128,1,8,128]{0,3,2,1:T(8,128)(2,1)S(1)}, bf16[128,1,8,128]{0,3,2,1:T(8,128)(2,1)S(1)}, u32[]{:S(2)}, u32[]{:S(2)}) collective-permute-start(bf16[128,1,8,128]{0,3,2,1:T(8,128)(2,1)S(1)} %get-tuple-element.20), channel_id=1, source_target_pairs={{0,8},{8,16},{16,24},{1,9},{9,17},{17,25},{2,10},{10,18},{18,26},{... | collective-permute-start | bytes 786440 | tf_op jit(solution)/shard_map/ppermute | solution.py:16
  149.4 4.3 %collective-permute-done.13 = bf16[128,1,8,128]{0,3,2,1:T(8,128)(2,1)S(1)} collective-permute-done((bf16[128,1,8,128]{0,3,2,1:T(8,128)(2,1)S(1)}, bf16[128,1,8,128]{0,3,2,1:T(8,128)(2,1)S(1)}, u32[]{:S(2)}, u32[]{:S(2)}) %collective-permute-start.13) | collective-permute-done | bytes 262176 | tf_op jit(solution)/shard_map/ppermute | solution.py:17
  156.6 3.3 %collective-permute-done.14 = bf16[128,10,1,128]{0,3,2,1:T(8,128)(2,1)S(1)} collective-permute-done((bf16[128,10,1,128]{0,3,2,1:T(8,128)(2,1)S(1)}, bf16[128,10,1,128]{0,3,2,1:T(8,128)(2,1)S(1)}, u32[]{:S(2)}, u32[]{:S(2)}) %collective-permute-start.14) | collective-permute-done | bytes 327712 | tf_op jit(solution)/shard_map/ppermute | solution.py:16
  159.8 4.4 %collective-permute-done.15 = bf16[128,10,1,128]{0,3,2,1:T(8,128)(2,1)S(1)} collective-permute-done((bf16[128,10,1,128]{0,3,2,1:T(8,128)(2,1)S(1)}, bf16[128,10,1,128]{0,3,2,1:T(8,128)(2,1)S(1)}, u32[]{:S(2)}, u32[]{:S(2)}) %collective-permute-start.15) | collective-permute-done | bytes 327712 | tf_op jit(solution)/shard_map/ppermute | solution.py:17
  164.3 3.4 %collective-permute-start.16 = (bf16[128,10,10,1]{0,3,2,1:T(2,128)(2,1)S(1)}, bf16[128,10,10,1]{0,3,2,1:T(2,128)(2,1)S(1)}, u32[]{:S(2)}, u32[]{:S(2)}) collective-permute-start(bf16[128,10,10,1]{0,3,2,1:T(2,128)(2,1)S(1)} %get-tuple-element.8), channel_id=1, source_target_pairs={{0,1},{1,2},{2,3},{4,5},{5,6},{6,7},{8,9},{9,10},{10,11},{12,13},{... | collective-permute-start | bytes 76808 | tf_op jit(solution)/shard_map/ppermute | solution.py:16
  169.4 4.3 %collective-permute-done.17 = bf16[128,10,10,1]{0,3,2,1:T(2,128)(2,1)S(1)} collective-permute-done((bf16[128,10,10,1]{0,3,2,1:T(2,128)(2,1)S(1)}, bf16[128,10,10,1]{0,3,2,1:T(2,128)(2,1)S(1)}, u32[]{:S(2)}, u32[]{:S(2)}) %collective-permute-start.17) | collective-permute-done | bytes 25632 | tf_op jit(solution)/shard_map/ppermute | solution.py:17
  173.7 3.0 %maximum_convert_fusion.2 = f32[128,10,10,130]{0,3,2,1:T(8,128)S(1)} fusion(bf16[128,10,10,1]{0,3,2,1:T(2,128)(2,1)S(1)} %collective-permute-done.17, bf16[128,10,1,128]{0,3,2,1:T(8,128)(2,1)S(1)} %collective-permute-done.15, bf16[128,1,8,128]{0,3,2,1:T(8,128)(2,1)S(1)} %collective-permute-done.13, bf16[128,8,8,128]{0,3,2,1:T(8,128)(2,1)S(1)} %fusion.15, ...), kind=kLoop, calls=%fused_computation.42 | loop fusion | flops 23296000 | bytes 9984000 | tf_op jit(solution)/shard_map/convert_element_type | solution.py:23
  176.7 4.5 %fusion.16 = bf16[128,8,8,128]{0,3,2,1:T(8,128)(2,1)S(1)} fusion(f32[128,8,8,128]{0,3,2,1:T(8,128)S(1)} %copy-done, f32[128,10,10,130]{0,3,2,1:T(8,128)S(1)} %maximum_convert_fusion.2, bf16[128,8,8,128]{0,3,2,1:T(8,128)(2,1)S(1)} %fusion.15, f32[8,8,128]{2,1,0:T(8,128)S(1)} %broadcast_add_fusion), kind=kLoop, calls=%fused_computation.39 | loop fusion | flops 13631488 | bytes 33587200 | tf_op jit(solution)/shard_map/convert_element_type | solution.py:28
  181.2 2.8 %copy.31 = bf16[128,8,8,128]{3,2,1,0:T(8,128)(2,1)} copy(bf16[128,8,8,128]{0,3,2,1:T(8,128)(2,1)S(1)} %fusion.16) | data formatting | bytes 4194304
  (50 shorter events, 21.5 us)
Async XLA Ops:
  7.2 49.9 %all-gather.2.cloned.1.call-start = ((), (), s32[]{:S(2)}) async-start(), calls=%async_computation.3 | async-start | bytes 1310720 | tf_op jit(solution)/shard_map/all_gather | solution.py:48
  30.5 14.7 %copy-start.1 = (f32[8,8,128]{2,1,0:T(8,128)S(1)}, f32[8,8,128]{2,1,0:T(8,128)}, u32[]{:S(2)}) copy-start(f32[8,8,128]{2,1,0:T(8,128)} %param.8) | copy-start | bytes 98308
  30.6 51.4 %reduce-scatter.2.cloned.1.call-start = ((), (), s32[]{:S(2)}) async-start(), calls=%async_computation.4 | async-start | bytes 49152 | tf_op jit(solution)/shard_map/reduce_scatter | solution.py:53
  34.0 2.6 %collective-permute-start = (bf16[128,1,8,128]{0,3,2,1:T(8,128)(2,1)S(1)}, bf16[128,1,8,128]{0,3,2,1:T(8,128)(2,1)S(1)}, u32[]{:S(2)}, u32[]{:S(2)}) collective-permute-start(bf16[128,1,8,128]{0,3,2,1:T(8,128)(2,1)S(1)} %get-tuple-element.24), channel_id=1, source_target_pairs={{0,8},{8,16},{16,24},{1,9},{9,17},{17,25},{2,10},{10,18},{18,26},{... | collective-permute-start | bytes 786440 | tf_op jit(solution)/shard_map/ppermute | solution.py:16
  35.3 5.1 %collective-permute-start.1 = (bf16[128,1,8,128]{0,3,2,1:T(8,128)(2,1)S(1)}, bf16[128,1,8,128]{0,3,2,1:T(8,128)(2,1)S(1)}, u32[]{:S(2)}, u32[]{:S(2)}) collective-permute-start(bf16[128,1,8,128]{0,3,2,1:T(8,128)(2,1)S(1)} %get-tuple-element.25), channel_id=1, source_target_pairs={{8,0},{16,8},{24,16},{9,1},{17,9},{25,17},{10,2},{18,10},{26,18},{... | collective-permute-start | bytes 786440 | tf_op jit(solution)/shard_map/ppermute | solution.py:17
  40.5 8.0 %collective-permute-start.2 = (bf16[128,10,1,128]{0,3,2,1:T(8,128)(2,1)S(1)}, bf16[128,10,1,128]{0,3,2,1:T(8,128)(2,1)S(1)}, u32[]{:S(2)}, u32[]{:S(2)}) collective-permute-start(bf16[128,10,1,128]{0,3,2,1:T(8,128)(2,1)S(1)} %get-tuple-element.18), channel_id=1, source_target_pairs={{0,4},{1,5},{2,6},{3,7},{8,12},{9,13},{10,14},{11,15},{16,20},{17,... | collective-permute-start | bytes 983048 | tf_op jit(solution)/shard_map/ppermute | solution.py:16
  44.0 9.0 %collective-permute-start.3 = (bf16[128,10,1,128]{0,3,2,1:T(8,128)(2,1)S(1)}, bf16[128,10,1,128]{0,3,2,1:T(8,128)(2,1)S(1)}, u32[]{:S(2)}, u32[]{:S(2)}) collective-permute-start(bf16[128,10,1,128]{0,3,2,1:T(8,128)(2,1)S(1)} %get-tuple-element.19), channel_id=1, source_target_pairs={{4,0},{5,1},{6,2},{7,3},{12,8},{13,9},{14,10},{15,11},{20,16},{21,... | collective-permute-start | bytes 983048 | tf_op jit(solution)/shard_map/ppermute | solution.py:17
  53.7 34.4 %collective-permute-start.4 = (bf16[128,10,10,1]{0,3,2,1:T(2,128)(2,1)}, bf16[128,10,10,1]{0,3,2,1:T(2,128)(2,1)S(1)}, u32[]{:S(2)}, u32[]{:S(2)}) collective-permute-start(bf16[128,10,10,1]{0,3,2,1:T(2,128)(2,1)} %get-tuple-element.12), channel_id=1, source_target_pairs={{0,1},{1,2},{2,3},{4,5},{5,6},{6,7},{8,9},{9,10},{10,11},{12,13},{... | collective-permute-start | bytes 76808 | tf_op jit(solution)/shard_map/ppermute | solution.py:16
  55.8 32.3 %collective-permute-start.5 = (bf16[128,10,10,1]{0,3,2,1:T(2,128)(2,1)}, bf16[128,10,10,1]{0,3,2,1:T(2,128)(2,1)S(1)}, u32[]{:S(2)}, u32[]{:S(2)}) collective-permute-start(bf16[128,10,10,1]{0,3,2,1:T(2,128)(2,1)} %get-tuple-element.13), channel_id=1, source_target_pairs={{1,0},{2,1},{3,2},{5,4},{6,5},{7,6},{9,8},{10,9},{11,10},{13,12},{... | collective-permute-start | bytes 76808 | tf_op jit(solution)/shard_map/ppermute | solution.py:17
  83.5 10.2 %all-to-all-start.1 = ((f32[4,1,1024]{2,1,0:T(1,128)}), f32[4,1,1024]{2,1,0:T(1,128)S(1)}, u32[]{:S(2)}, u32[]{:S(2)}) async-start(f32[4,1,1024]{2,1,0:T(1,128)} %reshape.43), calls=%async_computation.2 | async-start | bytes 32768 | tf_op jit(solution)/shard_map/all_to_all | solution.py:54
  88.1 7.0 %copy-start.2 = (s32[8,8,128]{2,1,0:T(8,128)S(1)}, s32[8,8,128]{2,1,0:T(8,128)}, u32[]{:S(2)}) copy-start(s32[8,8,128]{2,1,0:T(8,128)} %multiply_add_fusion) | copy-start | bytes 98308
  88.1 7.0 %copy-start.3 = (s32[1,1,1,32]{3,2,1,0:T(1,128)S(1)}, s32[1,1,1,32]{3,2,1,0:T(1,128)}, u32[]{:S(2)}) copy-start(s32[1,1,1,32]{3,2,1,0:T(1,128)} %param.11) | copy-start | bytes 388
  109.2 2.6 %collective-permute-start.6 = (bf16[128,1,8,128]{0,3,2,1:T(8,128)(2,1)S(1)}, bf16[128,1,8,128]{0,3,2,1:T(8,128)(2,1)S(1)}, u32[]{:S(2)}, u32[]{:S(2)}) collective-permute-start(bf16[128,1,8,128]{0,3,2,1:T(8,128)(2,1)S(1)} %get-tuple-element.22), channel_id=1, source_target_pairs={{0,8},{8,16},{16,24},{1,9},{9,17},{17,25},{2,10},{10,18},{18,26},{... | collective-permute-start | bytes 786440 | tf_op jit(solution)/shard_map/ppermute | solution.py:16
  110.5 5.1 %collective-permute-start.7 = (bf16[128,1,8,128]{0,3,2,1:T(8,128)(2,1)S(1)}, bf16[128,1,8,128]{0,3,2,1:T(8,128)(2,1)S(1)}, u32[]{:S(2)}, u32[]{:S(2)}) collective-permute-start(bf16[128,1,8,128]{0,3,2,1:T(8,128)(2,1)S(1)} %get-tuple-element.23), channel_id=1, source_target_pairs={{8,0},{16,8},{24,16},{9,1},{17,9},{25,17},{10,2},{18,10},{26,18},{... | collective-permute-start | bytes 786440 | tf_op jit(solution)/shard_map/ppermute | solution.py:17
  115.8 7.0 %collective-permute-start.8 = (bf16[128,10,1,128]{0,3,2,1:T(8,128)(2,1)S(1)}, bf16[128,10,1,128]{0,3,2,1:T(8,128)(2,1)S(1)}, u32[]{:S(2)}, u32[]{:S(2)}) collective-permute-start(bf16[128,10,1,128]{0,3,2,1:T(8,128)(2,1)S(1)} %get-tuple-element.16), channel_id=1, source_target_pairs={{0,4},{1,5},{2,6},{3,7},{8,12},{9,13},{10,14},{11,15},{16,20},{17,... | collective-permute-start | bytes 983048 | tf_op jit(solution)/shard_map/ppermute | solution.py:16
  118.2 9.0 %collective-permute-start.9 = (bf16[128,10,1,128]{0,3,2,1:T(8,128)(2,1)S(1)}, bf16[128,10,1,128]{0,3,2,1:T(8,128)(2,1)S(1)}, u32[]{:S(2)}, u32[]{:S(2)}) collective-permute-start(bf16[128,10,1,128]{0,3,2,1:T(8,128)(2,1)S(1)} %get-tuple-element.17), channel_id=1, source_target_pairs={{4,0},{5,1},{6,2},{7,3},{12,8},{13,9},{14,10},{15,11},{20,16},{21,... | collective-permute-start | bytes 983048 | tf_op jit(solution)/shard_map/ppermute | solution.py:17
  127.3 4.9 %collective-permute-start.10 = (bf16[128,10,10,1]{0,3,2,1:T(2,128)(2,1)S(1)}, bf16[128,10,10,1]{0,3,2,1:T(2,128)(2,1)S(1)}, u32[]{:S(2)}, u32[]{:S(2)}) collective-permute-start(bf16[128,10,10,1]{0,3,2,1:T(2,128)(2,1)S(1)} %get-tuple-element.10), channel_id=1, source_target_pairs={{0,1},{1,2},{2,3},{4,5},{5,6},{6,7},{8,9},{9,10},{10,11},{12,13},{... | collective-permute-start | bytes 76808 | tf_op jit(solution)/shard_map/ppermute | solution.py:16
  130.4 9.2 %copy-start = (f32[128,8,8,128]{0,3,2,1:T(8,128)S(1)}, f32[128,8,8,128]{0,3,2,1:T(8,128)}, u32[]{:S(2)}) copy-start(f32[128,8,8,128]{0,3,2,1:T(8,128)} %get-tuple-element.27) | copy-start | bytes 12582916
  130.4 6.3 %collective-permute-start.11 = (bf16[128,10,10,1]{0,3,2,1:T(2,128)(2,1)S(1)}, bf16[128,10,10,1]{0,3,2,1:T(2,128)(2,1)S(1)}, u32[]{:S(2)}, u32[]{:S(2)}) collective-permute-start(bf16[128,10,10,1]{0,3,2,1:T(2,128)(2,1)S(1)} %get-tuple-element.11), channel_id=1, source_target_pairs={{1,0},{2,1},{3,2},{5,4},{6,5},{7,6},{9,8},{10,9},{11,10},{13,12},{... | collective-permute-start | bytes 76808 | tf_op jit(solution)/shard_map/ppermute | solution.py:17
  144.3 5.1 %collective-permute-start.12 = (bf16[128,1,8,128]{0,3,2,1:T(8,128)(2,1)S(1)}, bf16[128,1,8,128]{0,3,2,1:T(8,128)(2,1)S(1)}, u32[]{:S(2)}, u32[]{:S(2)}) collective-permute-start(bf16[128,1,8,128]{0,3,2,1:T(8,128)(2,1)S(1)} %get-tuple-element.20), channel_id=1, source_target_pairs={{0,8},{8,16},{16,24},{1,9},{9,17},{17,25},{2,10},{10,18},{18,26},{... | collective-permute-start | bytes 786440 | tf_op jit(solution)/shard_map/ppermute | solution.py:16
  148.1 5.6 %collective-permute-start.13 = (bf16[128,1,8,128]{0,3,2,1:T(8,128)(2,1)S(1)}, bf16[128,1,8,128]{0,3,2,1:T(8,128)(2,1)S(1)}, u32[]{:S(2)}, u32[]{:S(2)}) collective-permute-start(bf16[128,1,8,128]{0,3,2,1:T(8,128)(2,1)S(1)} %get-tuple-element.21), channel_id=1, source_target_pairs={{8,0},{16,8},{24,16},{9,1},{17,9},{25,17},{10,2},{18,10},{26,18},{... | collective-permute-start | bytes 786440 | tf_op jit(solution)/shard_map/ppermute | solution.py:17
  153.8 6.0 %collective-permute-start.14 = (bf16[128,10,1,128]{0,3,2,1:T(8,128)(2,1)S(1)}, bf16[128,10,1,128]{0,3,2,1:T(8,128)(2,1)S(1)}, u32[]{:S(2)}, u32[]{:S(2)}) collective-permute-start(bf16[128,10,1,128]{0,3,2,1:T(8,128)(2,1)S(1)} %get-tuple-element.14), channel_id=1, source_target_pairs={{0,4},{1,5},{2,6},{3,7},{8,12},{9,13},{10,14},{11,15},{16,20},{17,... | collective-permute-start | bytes 983048 | tf_op jit(solution)/shard_map/ppermute | solution.py:16
  155.3 9.0 %collective-permute-start.15 = (bf16[128,10,1,128]{0,3,2,1:T(8,128)(2,1)S(1)}, bf16[128,10,1,128]{0,3,2,1:T(8,128)(2,1)S(1)}, u32[]{:S(2)}, u32[]{:S(2)}) collective-permute-start(bf16[128,10,1,128]{0,3,2,1:T(8,128)(2,1)S(1)} %get-tuple-element.15), channel_id=1, source_target_pairs={{4,0},{5,1},{6,2},{7,3},{12,8},{13,9},{14,10},{15,11},{20,16},{21,... | collective-permute-start | bytes 983048 | tf_op jit(solution)/shard_map/ppermute | solution.py:17
  164.3 5.1 %collective-permute-start.16 = (bf16[128,10,10,1]{0,3,2,1:T(2,128)(2,1)S(1)}, bf16[128,10,10,1]{0,3,2,1:T(2,128)(2,1)S(1)}, u32[]{:S(2)}, u32[]{:S(2)}) collective-permute-start(bf16[128,10,10,1]{0,3,2,1:T(2,128)(2,1)S(1)} %get-tuple-element.8), channel_id=1, source_target_pairs={{0,1},{1,2},{2,3},{4,5},{5,6},{6,7},{8,9},{9,10},{10,11},{12,13},{... | collective-permute-start | bytes 76808 | tf_op jit(solution)/shard_map/ppermute | solution.py:16
  167.7 6.0 %collective-permute-start.17 = (bf16[128,10,10,1]{0,3,2,1:T(2,128)(2,1)S(1)}, bf16[128,10,10,1]{0,3,2,1:T(2,128)(2,1)S(1)}, u32[]{:S(2)}, u32[]{:S(2)}) collective-permute-start(bf16[128,10,10,1]{0,3,2,1:T(2,128)(2,1)S(1)} %get-tuple-element.9), channel_id=1, source_target_pairs={{1,0},{2,1},{3,2},{5,4},{6,5},{7,6},{9,8},{10,9},{11,10},{13,12},{... | collective-permute-start | bytes 76808 | tf_op jit(solution)/shard_map/ppermute | solution.py:17
Sparse Core Ops, SparseCore 0:
  30.7 17.1 all-gather.1
  64.2 17.6 reduce-scatter.1
where the time goes:
time: 193 us; the launch traced here: 191 us
  waiting for transfers between devices  58.3 us (30%)
  starting transfers between devices  39 us (20%)
  matrix products  28.6 us (15%)
  other arithmetic  22.2 us (12%)
  blocking collectives  15 us (8%)
  between operations  14.4 us (7%)
  local copies, waits for them, and re-layouts  13.3 us (7%)
    ppermute x9, waiting for transfers between devices, padded_2(): after = lax.ppermute(first, axis, down)  34 us
    ppermute x9, starting transfers between devices, padded_2(): before = lax.ppermute(last, axis, up)  22.4 us
    all_to_all x1, blocking collectives, per_device(): lax.all_to_all(trace_values, 'gz', split_axis=0, concat_axis=1, tiled=True)  15 us
    dot_general x1, matrix products, per_device(): jnp.dot(owned_flux, placer, precision=lax.Precision.HIGHEST, preferred_el...  14.1 us
    reduce_scatter x1, waiting for transfers between devices, per_device(): lax.psum_scatter(partial_flux, 'col', scatter_dimension=1, tiled=True)  13.1 us
    ppermute x9, starting transfers between devices, padded_2(): after = lax.ppermute(first, axis, down)  11.9 us
    unnamed x13, local copies, waits for them, and re-layouts  11.1 us
    convert_element_type x3, other arithmetic, relax(): padded_2(current, (('row', 1), ('col', 2), ('gz', 3)), 1)  10.7 us
  transfers between devices with their start and end apart: 21, of which 15 were waited for; matrix products, arithmetic and copies ran while one was open for 11% of the time, Pallas kernels for 0%

commit v1 on v0

v1 whole, which is shorter than its diff:
```python
import functools

import jax
import jax.numpy as jnp
from jax import lax
from jax.experimental import pallas as pl
from jax.experimental.pallas import tpu as pltpu
from jax.sharding import PartitionSpec as P

OMEGA = 0.8
BF = jnp.bfloat16
F32 = jnp.float32
VMEM_LIMIT = 40 * 1024 * 1024


def iota(shape, dim):
    return lax.broadcasted_iota(jnp.int32, shape, dim)


def dot(a, b):
    return jnp.dot(a, b, preferred_element_type=F32)


def dot_nt(a, b):
    return lax.dot_general(a, b, (((1,), (1,)), ((), ())), preferred_element_type=F32)


def params():
    return pltpu.CompilerParams(vmem_limit_bytes=VMEM_LIMIT)


def trace_kernel(stride, field_ref, cell_ref, out_ref, perm, pick, rsum, picked):
    step = pl.program_id(0)
    sides, rows, lanes = field_ref.shape
    slots = cell_ref.shape[3]
    per_row = lanes // stride
    group = 16
    width = group * per_row

    @pl.when(step == 0)
    def _():
        cell = cell_ref[0, 0]
        perm[...] = (iota((slots, slots), 0) == cell // stride).astype(BF)
        offset = jnp.broadcast_to((cell % stride).astype(BF), (16, slots))
        sorted_offset = dot_nt(offset, perm[...])[0:1].astype(jnp.int32)
        place = (iota((1, slots), 1) % per_row) * stride + sorted_offset
        pick[...] = (iota((lanes, slots), 0) == place).astype(BF)
        shape = (sides, sides * group)
        rsum[...] = (iota(shape, 1) // group == iota(shape, 0)).astype(BF)

    shape = (sides * group, width)
    own = iota(shape, 0) % group == iota(shape, 1) // per_row
    for part in range(rows // group):
        values = field_ref[:, part * group : (part + 1) * group, :].reshape(sides * group, lanes)
        cols = slice(part * width, (part + 1) * width)
        spread = dot(values, pick[:, cols])
        spread = jnp.where(own, spread, 0.0).astype(BF)
        picked[pl.ds(pl.multiple_of(step * sides, sides), sides), cols] = dot(
            rsum[...], spread
        ).astype(BF)

    @pl.when(step == pl.num_programs(0) - 1)
    def _():
        out_ref[...] = dot(picked[...], perm[...]).astype(BF)


def traces(field, trace_cell, block):
    sides, rows, lanes = field.shape
    slots = trace_cell.shape[3]
    stride = rows * lanes // slots
    return pl.pallas_call(
        functools.partial(trace_kernel, stride),
        grid=(sides // block,),
        in_specs=[
            pl.BlockSpec((block, rows, lanes), lambda i: (i, 0, 0)),
            pl.BlockSpec(trace_cell.shape, lambda i: (0, 0, 0, 0)),
        ],
        out_specs=pl.BlockSpec((sides, slots), lambda i: (0, 0)),
        out_shape=jax.ShapeDtypeStruct((sides, slots), BF),
        scratch_shapes=[
            pltpu.VMEM((slots, slots), BF),
            pltpu.VMEM((lanes, slots), BF),
            pltpu.VMEM((block, block * 16), BF),
            pltpu.VMEM((sides, slots), BF),
        ],
        compiler_params=params(),
        cost_estimate=pl.CostEstimate(
            flops=4 * sides * rows * lanes * 128, bytes_accessed=field.size * 2, transcendentals=0
        ),
    )(field, trace_cell)


def xor_gather(value, axis):
    peers = lax.axis_size(axis)
    held = {0: value}
    bit = peers // 2
    while bit:
        swap = [(i, i ^ bit) for i in range(peers)]
        for key in sorted(held, reverse=True):
            held[key ^ bit] = lax.ppermute(held[key], axis, swap)
        bit //= 2
    return [held[key] for key in range(peers)]


def surface_kernel(row, gz, peers, gzs, cols, *refs):
    parts = refs[:peers]
    block_ref, out_ref, held, sems = refs[peers:]
    sides, slots = parts[0].shape
    me, group = lax.axis_index(row), lax.axis_index(gz)
    copies = []
    for key in range(peers):
        start = pl.multiple_of((jnp.bitwise_xor(me, key) * gzs + group) * slots, slots)
        copies.append(
            pltpu.make_async_copy(block_ref.at[:, pl.ds(start, slots)], held.at[key], sems.at[key])
        )
        copies[-1].start()
    total = None
    for key in range(peers):
        copies[key].wait()
        term = dot_nt(parts[key][...], held[key])
        total = term if total is None else total + term
    turned = total.T
    lines = total.shape[1]
    out_ref[...] = jnp.zeros_like(out_ref)
    s_count, l_count, f_count = sides // gzs, lines // cols, lines // (cols * gzs)
    for c in range(cols):
        for g in range(gzs):
            dest = c * gzs + g
            out_ref[dest, :s_count, :l_count] = total[
                g * s_count : (g + 1) * s_count, c * l_count : (c + 1) * l_count
            ].astype(out_ref.dtype)
            out_ref[dest, s_count : s_count + f_count, :sides] = turned[
                dest * f_count : (dest + 1) * f_count
            ].astype(out_ref.dtype)


def surface(parts, block, dtype):
    peers, gzs, cols = lax.axis_size("row"), lax.axis_size("gz"), lax.axis_size("col")
    sides, slots = parts[0].shape
    lines = block.shape[0]
    depth = sides // gzs + lines // (cols * gzs)
    shape = (cols * gzs, depth, max(sides, lines // cols))
    whole = pl.BlockSpec(memory_space=pltpu.VMEM)
    return pl.pallas_call(
        functools.partial(surface_kernel, "row", "gz", peers, gzs, cols),
        in_specs=[whole] * peers + [pl.BlockSpec(memory_space=pl.ANY)],
        out_specs=whole,
        out_shape=jax.ShapeDtypeStruct(shape, dtype),
        scratch_shapes=[
            pltpu.VMEM((peers, lines, slots), BF),
            pltpu.SemaphoreType.DMA((peers,)),
        ],
        compiler_params=params(),
        cost_estimate=pl.CostEstimate(
            flops=2 * sides * lines * slots * peers,
            bytes_accessed=2 * lines * slots * peers,
            transcendentals=0,
        ),
    )(*parts, block)


class Shape:
    def __init__(self, sides, first, second, lanes, cols, block):
        self.sides, self.x, self.y, self.lanes = sides, first, second, lanes
        self.cells = first * second
        self.paired = cols == 2
        self.block = block
        self.chunk = max(1, 256 // self.cells)
        self.rows = self.chunk * self.cells
        self.faces = 3 if self.paired else 4

    def face_len(self, face):
        return self.y if face < 2 else self.x


def face_select(shape, second, halo):
    dims = (shape.rows, shape.chunk * shape.y * 2 + shape.chunk * shape.x * (shape.faces - 2))
    row = iota(dims, 0)
    side, cell = row // shape.cells, row % shape.cells
    x, y = cell // shape.y, cell % shape.y
    col = iota(dims, 1)
    hit = None
    base = 0
    for face in range(shape.faces):
        length = shape.face_len(face)
        span = shape.chunk * length
        inside = col - base
        if face < 2:
            edge = 0 if face == 0 else shape.x - 1
            place = (x == edge) & (inside == side * length + y)
        else:
            if shape.paired:
                edge = jnp.where(second == 0, shape.y - 1, 0)
            else:
                edge = 0 if face == 2 else shape.y - 1
            place = (y == edge) & (inside == side * length + x)
        hit = place if hit is None else hit | place
        base += span
    return hit.astype(BF)


def z_mask(shape):
    dims = (shape.cells, 2 * shape.cells)
    return iota(dims, 1) % shape.cells == iota(dims, 0)


def build_out(shape, second, faces_m, ends_m, rsum):
    faces_m[...] = face_select(shape, second, False).T
    dims = (shape.lanes, 2 * shape.cells)
    edge = jnp.where(iota(dims, 1) < shape.cells, 0, shape.lanes - 1)
    ends_m[...] = (iota(dims, 0) == edge).astype(BF)
    dims = (shape.block, shape.block * shape.cells)
    rsum[...] = (iota(dims, 1) // shape.cells == iota(dims, 0)).astype(BF)


def emit_faces(shape, index, values, face_refs, faces_m, ends_m, rsum, ends):
    cut = dot(faces_m[...], values).astype(BF)
    base = 0
    for face in range(shape.faces):
        span = shape.chunk * shape.face_len(face)
        face_refs[face][index * span : (index + 1) * span, :] = cut[base : base + span]
        base += span
    tips = dot(values, ends_m[...])
    mask = jnp.concatenate([z_mask(shape)] * shape.chunk, axis=0)
    tips = jnp.where(mask, tips, 0.0).astype(BF)
    part = dot(rsum[:, index * shape.rows : (index + 1) * shape.rows], tips)
    return part if ends is None else ends + part


def faces_kernel(shape, field_ref, *refs):
    face_refs, z_ref = refs[: shape.faces], refs[shape.faces]
    faces_m, ends_m, rsum = refs[shape.faces + 1 :]

    @pl.when(pl.program_id(0) == 0)
    def _():
        build_out(shape, lax.axis_index("col"), faces_m, ends_m, rsum)

    ends = None
    for index in range(shape.block // shape.chunk):
        values = field_ref[index * shape.rows : (index + 1) * shape.rows, :]
        ends = emit_faces(shape, index, values, face_refs, faces_m, ends_m, rsum, ends)
    z_ref[...] = ends.astype(BF)


def face_outputs(shape):
    specs, shapes = [], []
    for face in range(shape.faces):
        length = shape.face_len(face)
        specs.append(pl.BlockSpec((shape.block * length, shape.lanes), lambda i: (i, 0)))
        shapes.append(jax.ShapeDtypeStruct((shape.sides * length, shape.lanes), BF))
    specs.append(pl.BlockSpec((shape.block, 2 * shape.cells), lambda i: (i, 0)))
    shapes.append(jax.ShapeDtypeStruct((shape.sides, 2 * shape.cells), BF))
    return specs, shapes


def face_scratch(shape):
    cut = shape.chunk * shape.y * 2 + shape.chunk * shape.x * (shape.faces - 2)
    return [
        pltpu.VMEM((cut, shape.rows), BF),
        pltpu.VMEM((shape.lanes, 2 * shape.cells), BF),
        pltpu.VMEM((shape.block, shape.block * shape.cells), BF),
    ]


def first_faces(shape, field):
    specs, shapes = face_outputs(shape)
    return pl.pallas_call(
        functools.partial(faces_kernel, shape),
        grid=(shape.sides // shape.block,),
        in_specs=[pl.BlockSpec((shape.block * shape.cells, shape.lanes), lambda i: (i, 0))],
        out_specs=specs,
        out_shape=shapes,
        scratch_shapes=face_scratch(shape),
        compiler_params=params(),
        cost_estimate=pl.CostEstimate(
            flops=4 * field.size * 128, bytes_accessed=4 * field.size, transcendentals=0
        ),
    )(field)


def sweep_kernel(shape, with_flux, last, *refs):
    refs = list(refs)
    take = lambda count: [refs.pop(0) for _ in range(count)]
    field_ref, load_ref, coef_ref = take(3)
    halo_refs = take(shape.faces)
    below_ref, above_ref = take(2)
    if with_flux:
        recv_ref, cell_ref = take(2)
    (out_ref,) = take(1)
    if not last:
        face_refs = take(shape.faces)
        (z_ref,) = take(1)
    if with_flux:
        source_ref, flux_ref = take(2)
    weight, near_m, halo_m, line_m = take(4)
    if not last:
        faces_m, ends_m, rsum = take(3)
    if with_flux:
        phi, cell_m = take(2)

    step = pl.program_id(0)
    cells, lanes = shape.cells, shape.lanes

    @pl.when(step == 0)
    def _():
        second = lax.axis_index("col")
        weight[...] = OMEGA / (6.0 + coef_ref[...])
        dims = (shape.rows, shape.rows)
        row, col = iota(dims, 0), iota(dims, 1)
        x, y = row % cells // shape.y, row % shape.y
        x2, y2 = col % cells // shape.y, col % shape.y
        near = ((x == x2) & (jnp.abs(y - y2) == 1)) | ((y == y2) & (jnp.abs(x - x2) == 1))
        near_m[...] = (near & (row // cells == col // cells)).astype(BF)
        halo_m[...] = face_select(shape, second, True)
        dims = (lanes, lanes)
        line_m[:lanes, :] = (jnp.abs(iota(dims, 0) - iota(dims, 1)) == 1).astype(BF)
        dims = (2 * cells, lanes)
        edge = jnp.where(iota(dims, 0) < cells, lanes - 1, 0)
        line_m[lanes:, :] = (iota(dims, 1) == edge).astype(BF)
        if not last:
            build_out(shape, second, faces_m, ends_m, rsum)
        if with_flux:
            total = recv_ref[0].astype(F32)
            for peer in range(1, recv_ref.shape[0]):
                total = total + recv_ref[peer].astype(F32)
            s_count, l_count = flux_ref.shape
            slots = cell_ref.shape[3]
            flux_ref[...] = total[:s_count, :l_count]
            owned = total[s_count : s_count + slots, : shape.sides]
            high = owned.astype(BF).astype(F32)
            both = jnp.concatenate([high, owned - high], axis=0)
            phi[...] = both.T
            cell = jnp.concatenate([cell_ref[0, 0]] * 2, axis=1)
            cell_m[...] = (iota((lanes, 2 * slots), 0) == cell % lanes).astype(BF)

    mask = z_mask(shape)
    zs = jnp.where(
        iota((shape.block, 2 * cells), 1) < cells,
        above_ref[...].astype(F32),
        below_ref[...].astype(F32),
    )
    if with_flux:
        slots = cell_ref.shape[3]
        cell = jnp.concatenate([cell_ref[0, 0]] * 2, axis=1)
        cell_mask = iota((cells, 2 * slots), 0) == cell // lanes
        phis = phi[pl.ds(pl.multiple_of(step * shape.block, shape.block), shape.block), :]
    weights = jnp.concatenate([weight[...]] * shape.chunk, axis=0)
    ends = None
    for index in range(shape.block // shape.chunk):
        span = slice(index * shape.rows, (index + 1) * shape.rows)
        values = field_ref[span, :]
        halos = []
        for face in range(shape.faces):
            length = shape.chunk * shape.face_len(face)
            halos.append(halo_refs[face][index * length : (index + 1) * length, :])
        spread = []
        for side in range(shape.chunk):
            at = index * shape.chunk + side
            spread.append(jnp.where(mask, jnp.broadcast_to(zs[at : at + 1], mask.shape), 0.0))
        spread = jnp.concatenate(spread, axis=0).astype(BF)
        near = dot(near_m[...], values) + dot(halo_m[...], jnp.concatenate(halos, axis=0))
        near = near + dot(jnp.concatenate([values, spread], axis=1), line_m[...])
        source = load_ref[span, :].astype(F32)
        if with_flux:
            spread = []
            for side in range(shape.chunk):
                at = index * shape.chunk + side
                line = jnp.broadcast_to(phis[at : at + 1], cell_mask.shape)
                spread.append(jnp.where(cell_mask, line, 0.0))
            spread = jnp.concatenate(spread, axis=0).astype(BF)
            source = source + dot_nt(spread, cell_m[...])
            source_ref[span, :] = source.astype(BF)
        fresh = (1.0 - OMEGA) * values.astype(F32) + weights * (source + near)
        fresh = fresh.astype(BF)
        out_ref[span, :] = fresh
        if not last:
            ends = emit_faces(shape, index, fresh, face_refs, faces_m, ends_m, rsum, ends)
    if not last:
        z_ref[...] = ends.astype(BF)


def sweep(shape, field, load, coef, halos, recv=None, flux_cell=None, last=False):
    with_flux = recv is not None
    block, lanes, cells = shape.block, shape.lanes, shape.cells
    big = pl.BlockSpec((block * cells, lanes), lambda i: (i, 0))
    specs, shapes = face_outputs(shape)
    in_specs = [big, big, pl.BlockSpec(coef.shape, lambda i: (0, 0))] + specs + specs[-1:]
    operands = [field, load, coef, *halos]
    out_specs, out_shapes = [big], [jax.ShapeDtypeStruct(field.shape, BF)]
    cut = shape.chunk * shape.y * 2 + shape.chunk * shape.x * (shape.faces - 2)
    scratch = [
        pltpu.VMEM(coef.shape, F32),
        pltpu.VMEM((shape.rows, shape.rows), BF),
        pltpu.VMEM((shape.rows, cut), BF),
        pltpu.VMEM((lanes + 2 * cells, lanes), BF),
    ]
    if not last:
        out_specs, out_shapes = out_specs + specs, out_shapes + shapes
        scratch += face_scratch(shape)
    if with_flux:
        slots = flux_cell.shape[3]
        gzs = lax.axis_size("gz")
        in_specs += [
            pl.BlockSpec(recv.shape, lambda i: (0, 0, 0)),
            pl.BlockSpec(flux_cell.shape, lambda i: (0, 0, 0, 0)),
        ]
        operands += [recv, flux_cell]
        flux_shape = (shape.sides // gzs, slots * gzs)
        out_specs += [big, pl.BlockSpec(flux_shape, lambda i: (0, 0))]
        out_shapes += [
            jax.ShapeDtypeStruct(field.shape, BF),
            jax.ShapeDtypeStruct(flux_shape, F32),
        ]
        scratch += [pltpu.VMEM((shape.sides, 2 * slots), F32), pltpu.VMEM((lanes, 2 * slots), BF)]
    return pl.pallas_call(
        functools.partial(sweep_kernel, shape, with_flux, last),
        grid=(shape.sides // block,),
        in_specs=in_specs,
        out_specs=out_specs,
        out_shape=out_shapes,
        scratch_shapes=scratch,
        compiler_params=params(),
        cost_estimate=pl.CostEstimate(
            flops=10 * field.size * 128, bytes_accessed=8 * field.size, transcendentals=0
        ),
    )(*operands)


def exchange(shape, faces):
    def ways(axis):
        peers = lax.axis_size(axis)
        up = [(i, i + 1) for i in range(peers - 1)]
        return up, [(j, i) for i, j in up]

    *cut, ends = faces
    if shape.paired:
        y = [lax.ppermute(cut[2], "col", [(0, 1), (1, 0)])]
    else:
        up, down = ways("col")
        y = [lax.ppermute(cut[3], "col", up), lax.ppermute(cut[2], "col", down)]
    up, down = ways("row")
    x = [lax.ppermute(cut[1], "row", up), lax.ppermute(cut[0], "row", down)]
    up, down = ways("gz")
    z = [lax.ppermute(ends, "gz", up), lax.ppermute(ends, "gz", down)]
    return x + y + z


def per_device(volume_field, volume_load, coefficient, surface_block, trace_cell, flux_cell):
    sides, first, second, lanes = volume_field.shape
    cells = first * second
    block = min(32, sides)
    shape = Shape(sides, first, second, lanes, lax.axis_size("col"), block)
    field = volume_field.reshape(sides * cells, lanes)
    load = volume_load.reshape(sides * cells, lanes)
    coef = coefficient.reshape(cells, lanes)

    trace = traces(volume_field.reshape(sides, cells, lanes), trace_cell, block)
    parts = xor_gather(trace, "row")
    halos = exchange(shape, first_faces(shape, field))
    sent = surface(parts, surface_block, F32)
    recv = lax.all_to_all(sent, ("col", "gz"), split_axis=0, concat_axis=0, tiled=True)

    current, *faces, source, surface_flux = sweep(
        shape, field, load, coef, halos, recv=recv, flux_cell=flux_cell
    )
    current, *faces = sweep(shape, current, source, coef, exchange(shape, faces))
    (current,) = sweep(shape, current, source, coef, exchange(shape, faces), last=True)
    return current.reshape(volume_field.shape), surface_flux


def solution(mesh):
    in_specs = (
        P(None, "row", "col", "gz"),
        P(None, "row", "col", "gz"),
        P("row", "col", "gz"),
        P("row", "col"),
        P("row", "col", "gz", None),
        P("row", "col", "gz", None),
    )
    out_specs = (P(None, "row", "col", "gz"), P("gz", ("row", "col")))
    return jax.shard_map(
        per_device, mesh=mesh, in_specs=in_specs, out_specs=out_specs, check_vma=False
    )
```

time: 193 us -> 112 us (0.58)
  the two profiles are of different devices: /device:TPU:0 before, /device:TPU:26 now
where the time goes in v1:
time: 112 us; the launch traced here: 111 us
  Pallas kernels  42.4 us (38%)
  starting transfers between devices  38.3 us (34%)
  waiting for transfers between devices  22.6 us (20%)
  local copies, waits for them, and re-layouts  7.26 us (6%)
    pallas_call x3, Pallas kernels, sweep(): pl.pallas_call(functools.partial(sweep_kernel, shape, with_flux, last), g...  28.5 us
    ppermute x6, starting transfers between devices, exchange(): x = [lax.ppermute(cut[1], 'row', up), lax.ppermute(cut[0], 'row', down)]  16.7 us
    ppermute x6, waiting for transfers between devices, exchange(): z = [lax.ppermute(ends, 'gz', up), lax.ppermute(ends, 'gz', down)]  13.5 us
    ppermute x6, starting transfers between devices, exchange(): z = [lax.ppermute(ends, 'gz', up), lax.ppermute(ends, 'gz', down)]  11.3 us
    ppermute x3, waiting for transfers between devices, xor_gather(): held[key ^ bit] = lax.ppermute(held[key], axis, swap)  9.04 us
    unnamed x14, local copies, waits for them, and re-layouts  7.26 us
    pallas_call x1, Pallas kernels, traces(): pl.pallas_call(functools.partial(trace_kernel, stride), grid=(sides // bl...  6.3 us
    all_to_all x1, starting transfers between devices, per_device(): lax.all_to_all(sent, ('col', 'gz'), split_axis=0, concat_axis=0, tiled=True)  6.07 us
  transfers between devices with their start and end apart: 19, of which 8 were waited for; matrix products, arithmetic and copies ran while one was open for 0% of the time, Pallas kernels for 5%

profile of v1, /device:TPU:26, one launch (start us, length us, event | category | flops | bytes accessed | tf_op | source)
XLA Modules:
  0.0 111.3 jit_solution(13042679976237729238)
XLA Ops:
  0.6 1.6 %copy-done = bf16[128,8,8,128]{3,2,1,0:T(8,128)(2,1)S(1)} copy-done((bf16[128,8,8,128]{3,2,1,0:T(8,128)(2,1)S(1)}, bf16[128,8,8,128]{3,2,1,0:T(8,128)(2,1)}, u32[]{:S(2)}) %copy-start) | copy-done | bytes 2097176
  2.2 0.7 copy-done.5
  2.9 6.3 %shard_map.78.refs_0_ = bf16[128,1024]{1,0:T(8,128)(2,1)S(1)} custom-call(bf16[128,64,128]{2,1,0:T(8,128)(2,1)S(1)} %bitcast.5, s32[1,1,1,1024]{3,2,1,0:T(1,128)S(1)} %copy-done.5), custom_call_target="tpu_custom_call" | custom-call | flops 536870912 | bytes 2097152 | tf_op jit(solution)/shard_map/pallas_call | solution.py:71
  9.2 0.6 collective-permute-start.6
  9.8 7.5 %collective-permute-done.6.refs_2_ = bf16[128,1024]{1,0:T(8,128)(2,1)S(1)} collective-permute-done((bf16[128,1024]{1,0:T(8,128)(2,1)S(1)}, bf16[128,1024]{1,0:T(8,128)(2,1)S(1)}, u32[]{:S(2)}, u32[]{:S(2)}) %collective-permute-start.6) | collective-permute-done | bytes 262176 | tf_op jit(solution)/shard_map/ppermute | solution.py:100
  17.3 1.5 %collective-permute-done.7.refs_3_ = bf16[128,1024]{1,0:T(8,128)(2,1)S(1)} collective-permute-done((bf16[128,1024]{1,0:T(8,128)(2,1)S(1)}, bf16[128,1024]{1,0:T(8,128)(2,1)S(1)}, u32[]{:S(2)}, u32[]{:S(2)}) %collective-permute-start.7) | collective-permute-done | bytes 262176 | tf_op jit(solution)/shard_map/ppermute | solution.py:100
  18.9 3.4 %copy-done.2 = bf16[256,16384]{1,0:T(8,128)(2,1)S(1)} copy-done((bf16[256,16384]{1,0:T(8,128)(2,1)S(1)}, bf16[256,16384]{1,0:T(8,128)(2,1)}, u32[]{:S(2)}) %copy-start.2) | copy-done | bytes 8388632
  22.3 2.5 %shard_map.79 = f32[8,64,128]{2,1,0:T(8,128)} custom-call(bf16[128,1024]{1,0:T(8,128)(2,1)S(1)} %shard_map.78.refs_0_, bf16[128,1024]{1,0:T(8,128)(2,1)S(1)} %collective-permute-done.5.refs_1_, bf16[128,1024]{1,0:T(8,128)(2,1)S(1)} %collective-permute-done.6.refs_2_, bf16[128,1024]{1,0:T(8,128)(2,1)S(1)} %collective-permute-done.7.refs_3_, ...), custom_call_target="tpu_custom_call" | custom-call | flops 268435456 | bytes 2097152 | tf_op jit(solution)/shard_map/pallas_call | solution.py:144
  24.8 6.1 %all-to-all-start = ((f32[8,64,128]{2,1,0:T(8,128)}), f32[8,64,128]{2,1,0:T(8,128)S(1)}, u32[]{:S(2)}, u32[]{:S(2)}) async-start(f32[8,64,128]{2,1,0:T(8,128)} %shard_map.79), calls=%async_computation | async-start | bytes 524288 | tf_op jit(solution)/shard_map/all_to_all | solution.py:461
  30.9 5.1 %shard_map.77 = (bf16[1024,128]{1,0:T(8,128)(2,1)S(1)}, bf16[1024,128]{1,0:T(8,128)(2,1)S(1)}, bf16[1024,128]{1,0:T(8,128)(2,1)S(1)}, bf16[128,128]{1,0:T(8,128)(2,1)S(1)}) custom-call(bf16[8192,128]{1,0:T(8,128)(2,1)S(1)} %bitcast.6), custom_call_target="tpu_custom_call" | custom-call | flops 536870912 | bytes 4194304 | tf_op jit(solution)/shard_map/pallas_call | solution.py:267
  36.0 1.9 %collective-permute-start = (bf16[1024,128]{1,0:T(8,128)(2,1)S(1)}, bf16[1024,128]{1,0:T(8,128)(2,1)S(1)}, u32[]{:S(2)}, u32[]{:S(2)}) collective-permute-start(bf16[1024,128]{1,0:T(8,128)(2,1)S(1)} %get-tuple-element.18), channel_id=1, source_target_pairs={{0,8},{8,16},{16,24},{1,9},{9,17},{17,25},{2,10},{10,18},{18,26},{... | collective-permute-start | bytes 786440 | tf_op jit(solution)/shard_map/ppermute | solution.py:442
  37.9 3.6 %collective-permute-start.1 = (bf16[1024,128]{1,0:T(8,128)(2,1)S(1)}, bf16[1024,128]{1,0:T(8,128)(2,1)S(1)}, u32[]{:S(2)}, u32[]{:S(2)}) collective-permute-start(bf16[1024,128]{1,0:T(8,128)(2,1)S(1)} %get-tuple-element.19), channel_id=1, source_target_pairs={{8,0},{16,8},{24,16},{9,1},{17,9},{25,17},{10,2},{18,10},{26,18},{... | collective-permute-start | bytes 786440 | tf_op jit(solution)/shard_map/ppermute | solution.py:442
  41.6 1.5 %collective-permute-start.2 = (bf16[1024,128]{1,0:T(8,128)(2,1)S(1)}, bf16[1024,128]{1,0:T(8,128)(2,1)S(1)}, u32[]{:S(2)}, u32[]{:S(2)}) collective-permute-start(bf16[1024,128]{1,0:T(8,128)(2,1)S(1)} %get-tuple-element.20), channel_id=1, source_target_pairs={{0,4},{4,0},{1,5},{5,1},{2,6},{6,2},{3,7},{7,3},{8,12},{12,8},{9,1... | collective-permute-start | bytes 786440 | tf_op jit(solution)/shard_map/ppermute | solution.py:437
  43.1 2.5 %collective-permute-start.4 = (bf16[128,128]{1,0:T(8,128)(2,1)S(1)}, bf16[128,128]{1,0:T(8,128)(2,1)S(1)}, u32[]{:S(2)}, u32[]{:S(2)}) collective-permute-start(bf16[128,128]{1,0:T(8,128)(2,1)S(1)} %get-tuple-element.21), channel_id=1, source_target_pairs={{1,0},{2,1},{3,2},{5,4},{6,5},{7,6},{9,8},{10,9},{11,10},{13,12},{... | collective-permute-start | bytes 98312 | tf_op jit(solution)/shard_map/ppermute | solution.py:444
  45.5 1.3 %collective-permute-start.3 = (bf16[128,128]{1,0:T(8,128)(2,1)S(1)}, bf16[128,128]{1,0:T(8,128)(2,1)S(1)}, u32[]{:S(2)}, u32[]{:S(2)}) collective-permute-start(bf16[128,128]{1,0:T(8,128)(2,1)S(1)} %get-tuple-element.21), channel_id=1, source_target_pairs={{0,1},{1,2},{2,3},{4,5},{5,6},{6,7},{8,9},{9,10},{10,11},{12,13},{... | collective-permute-start | bytes 98312 | tf_op jit(solution)/shard_map/ppermute | solution.py:444
  47.1 4.2 %collective-permute-done.3.refs_6_ = bf16[128,128]{1,0:T(8,128)(2,1)S(1)} collective-permute-done((bf16[128,128]{1,0:T(8,128)(2,1)S(1)}, bf16[128,128]{1,0:T(8,128)(2,1)S(1)}, u32[]{:S(2)}, u32[]{:S(2)}) %collective-permute-start.3) | collective-permute-done | bytes 32800 | tf_op jit(solution)/shard_map/ppermute | solution.py:444
  51.4 1.6 %copy-done.3 = bf16[128,8,8,128]{3,2,1,0:T(8,128)(2,1)S(1)} copy-done((bf16[128,8,8,128]{3,2,1,0:T(8,128)(2,1)S(1)}, bf16[128,8,8,128]{3,2,1,0:T(8,128)(2,1)}, u32[]{:S(2)}) %copy-start.3) | copy-done | bytes 2097176
  53.0 12.4 %shard_map.80 = (bf16[8192,128]{1,0:T(8,128)(2,1)S(1)}, bf16[1024,128]{1,0:T(8,128)(2,1)S(1)}, bf16[1024,128]{1,0:T(8,128)(2,1)S(1)}, bf16[1024,128]{1,0:T(8,128...) custom-call(bf16[8192,128]{1,0:T(8,128)(2,1)S(1)} %bitcast.7, ...), custom_call_target="tpu_custom_call" | custom-call | flops 1342177280 | bytes 8388608 | tf_op jit(solution)/shard_map/pallas_call | solution.py:415
  65.4 1.9 %collective-permute-start.8 = (bf16[1024,128]{1,0:T(8,128)(2,1)S(1)}, bf16[1024,128]{1,0:T(8,128)(2,1)S(1)}, u32[]{:S(2)}, u32[]{:S(2)}) collective-permute-start(bf16[1024,128]{1,0:T(8,128)(2,1)S(1)} %get-tuple-element.24), channel_id=1, source_target_pairs={{0,8},{8,16},{16,24},{1,9},{9,17},{17,25},{2,10},{10,18},{18,26},{... | collective-permute-start | bytes 786440 | tf_op jit(solution)/shard_map/ppermute | solution.py:442
  67.3 3.6 %collective-permute-start.9 = (bf16[1024,128]{1,0:T(8,128)(2,1)S(1)}, bf16[1024,128]{1,0:T(8,128)(2,1)S(1)}, u32[]{:S(2)}, u32[]{:S(2)}) collective-permute-start(bf16[1024,128]{1,0:T(8,128)(2,1)S(1)} %get-tuple-element.25), channel_id=1, source_target_pairs={{8,0},{16,8},{24,16},{9,1},{17,9},{25,17},{10,2},{18,10},{26,18},{... | collective-permute-start | bytes 786440 | tf_op jit(solution)/shard_map/ppermute | solution.py:442
  70.9 0.6 collective-permute-start.10
  71.5 2.5 %collective-permute-start.12 = (bf16[128,128]{1,0:T(8,128)(2,1)S(1)}, bf16[128,128]{1,0:T(8,128)(2,1)S(1)}, u32[]{:S(2)}, u32[]{:S(2)}) collective-permute-start(bf16[128,128]{1,0:T(8,128)(2,1)S(1)} %get-tuple-element.27), channel_id=1, source_target_pairs={{1,0},{2,1},{3,2},{5,4},{6,5},{7,6},{9,8},{10,9},{11,10},{13,12},{... | collective-permute-start | bytes 98312 | tf_op jit(solution)/shard_map/ppermute | solution.py:444
  74.0 1.3 %collective-permute-start.11 = (bf16[128,128]{1,0:T(8,128)(2,1)S(1)}, bf16[128,128]{1,0:T(8,128)(2,1)S(1)}, u32[]{:S(2)}, u32[]{:S(2)}) collective-permute-start(bf16[128,128]{1,0:T(8,128)(2,1)S(1)} %get-tuple-element.27), channel_id=1, source_target_pairs={{0,1},{1,2},{2,3},{4,5},{5,6},{6,7},{8,9},{9,10},{10,11},{12,13},{... | collective-permute-start | bytes 98312 | tf_op jit(solution)/shard_map/ppermute | solution.py:444
  75.6 4.2 %collective-permute-done.11.refs_6_ = bf16[128,128]{1,0:T(8,128)(2,1)S(1)} collective-permute-done((bf16[128,128]{1,0:T(8,128)(2,1)S(1)}, bf16[128,128]{1,0:T(8,128)(2,1)S(1)}, u32[]{:S(2)}, u32[]{:S(2)}) %collective-permute-start.11) | collective-permute-done | bytes 32800 | tf_op jit(solution)/shard_map/ppermute | solution.py:444
  79.8 11.7 %shard_map.81 = (bf16[8192,128]{1,0:T(8,128)(2,1)S(1)}, bf16[1024,128]{1,0:T(8,128)(2,1)S(1)}, bf16[1024,128]{1,0:T(8,128)(2,1)S(1)}, bf16[1024,128]{1,0:T(8,128)(2,1)S(1)}, bf16[128,128]{1,0:T(8,128)(2,1)S(1)}) custom-call(bf16[8192,128]{1,0:T(8,128)(2,1)S(1)} %get-tuple-element.22.refs_0_, bf16[8192,128]{1,0:T(8,128)(2,1)S(1)} %get-tuple-element.23.refs_1_, ...), custom_call_target="tpu_custom_call" | custom-call | flops 1342177280 | bytes 8388608 | tf_op jit(solution)/shard_map/pallas_call | solution.py:415
  91.5 1.9 %collective-permute-start.13 = (bf16[1024,128]{1,0:T(8,128)(2,1)S(1)}, bf16[1024,128]{1,0:T(8,128)(2,1)S(1)}, u32[]{:S(2)}, u32[]{:S(2)}) collective-permute-start(bf16[1024,128]{1,0:T(8,128)(2,1)S(1)} %get-tuple-element.29), channel_id=1, source_target_pairs={{0,8},{8,16},{16,24},{1,9},{9,17},{17,25},{2,10},{10,18},{18,26},{... | collective-permute-start | bytes 786440 | tf_op jit(solution)/shard_map/ppermute | solution.py:442
  93.4 3.6 %collective-permute-start.14 = (bf16[1024,128]{1,0:T(8,128)(2,1)S(1)}, bf16[1024,128]{1,0:T(8,128)(2,1)S(1)}, u32[]{:S(2)}, u32[]{:S(2)}) collective-permute-start(bf16[1024,128]{1,0:T(8,128)(2,1)S(1)} %get-tuple-element.30), channel_id=1, source_target_pairs={{8,0},{16,8},{24,16},{9,1},{17,9},{25,17},{10,2},{18,10},{26,18},{... | collective-permute-start | bytes 786440 | tf_op jit(solution)/shard_map/ppermute | solution.py:442
  97.1 1.5 %collective-permute-start.15 = (bf16[1024,128]{1,0:T(8,128)(2,1)S(1)}, bf16[1024,128]{1,0:T(8,128)(2,1)S(1)}, u32[]{:S(2)}, u32[]{:S(2)}) collective-permute-start(bf16[1024,128]{1,0:T(8,128)(2,1)S(1)} %get-tuple-element.31), channel_id=1, source_target_pairs={{0,4},{4,0},{1,5},{5,1},{2,6},{6,2},{3,7},{7,3},{8,12},{12,8},{9,1... | collective-permute-start | bytes 786440 | tf_op jit(solution)/shard_map/ppermute | solution.py:437
  98.6 2.5 %collective-permute-start.17 = (bf16[128,128]{1,0:T(8,128)(2,1)S(1)}, bf16[128,128]{1,0:T(8,128)(2,1)S(1)}, u32[]{:S(2)}, u32[]{:S(2)}) collective-permute-start(bf16[128,128]{1,0:T(8,128)(2,1)S(1)} %get-tuple-element.32), channel_id=1, source_target_pairs={{1,0},{2,1},{3,2},{5,4},{6,5},{7,6},{9,8},{10,9},{11,10},{13,12},{... | collective-permute-start | bytes 98312 | tf_op jit(solution)/shard_map/ppermute | solution.py:444
  101.1 1.3 %collective-permute-start.16 = (bf16[128,128]{1,0:T(8,128)(2,1)S(1)}, bf16[128,128]{1,0:T(8,128)(2,1)S(1)}, u32[]{:S(2)}, u32[]{:S(2)}) collective-permute-start(bf16[128,128]{1,0:T(8,128)(2,1)S(1)} %get-tuple-element.32), channel_id=1, source_target_pairs={{0,1},{1,2},{2,3},{4,5},{5,6},{6,7},{8,9},{9,10},{10,11},{12,13},{... | collective-permute-start | bytes 98312 | tf_op jit(solution)/shard_map/ppermute | solution.py:444
  102.7 4.2 %collective-permute-done.16.refs_6_ = bf16[128,128]{1,0:T(8,128)(2,1)S(1)} collective-permute-done((bf16[128,128]{1,0:T(8,128)(2,1)S(1)}, bf16[128,128]{1,0:T(8,128)(2,1)S(1)}, u32[]{:S(2)}, u32[]{:S(2)}) %collective-permute-start.16) | collective-permute-done | bytes 32800 | tf_op jit(solution)/shard_map/ppermute | solution.py:444
  106.9 4.4 %shard_map.82 = bf16[8192,128]{1,0:T(8,128)(2,1)} custom-call(bf16[8192,128]{1,0:T(8,128)(2,1)S(1)} %get-tuple-element.28.refs_0_, bf16[8192,128]{1,0:T(8,128)(2,1)S(1)} %get-tuple-element.23.refs_1_, f32[64,128]{1,0:T(8,128)S(1)} %bitcast.11, bf16[1024,128]{1,0:T(8,128)(2,1)S(1)} %collective-permute-done.13.refs_3_, ...), custom_call_target="tpu_custom_call" | custom-call | flops 1342177280 | bytes 8388608 | tf_op jit(solution)/shard_map/pallas_call | solution.py:415
  (26 shorter events, 0.9 us)
Async XLA Ops:
  0.6 1.6 %copy-start = (bf16[128,8,8,128]{3,2,1,0:T(8,128)(2,1)S(1)}, bf16[128,8,8,128]{3,2,1,0:T(8,128)(2,1)}, u32[]{:S(2)}) copy-start(bf16[128,8,8,128]{3,2,1,0:T(8,128)(2,1)} %param.6) | copy-start | bytes 6291460
  2.2 0.7 copy-start.5
  9.2 21.6 %copy-start.1 = (bf16[128,8,8,128]{3,2,1,0:T(8,128)(2,1)S(1)}, bf16[128,8,8,128]{3,2,1,0:T(8,128)(2,1)}, u32[]{:S(2)}) copy-start(bf16[128,8,8,128]{3,2,1,0:T(8,128)(2,1)} %param.6) | copy-start | bytes 6291460
  9.2 8.1 %collective-permute-start.6 = (bf16[128,1024]{1,0:T(8,128)(2,1)S(1)}, bf16[128,1024]{1,0:T(8,128)(2,1)S(1)}, u32[]{:S(2)}, u32[]{:S(2)}) collective-permute-start(bf16[128,1024]{1,0:T(8,128)(2,1)S(1)} %shard_map.78.refs_0_), channel_id=1, source_target_pairs={{0,16},{8,24},{16,0},{24,8},{1,17},{9,25},{17,1},{25,9},{2,18},{10... | collective-permute-start | bytes 786440 | tf_op jit(solution)/shard_map/ppermute | solution.py:100
  9.8 7.5 %collective-permute-start.5 = (bf16[128,1024]{1,0:T(8,128)(2,1)S(1)}, bf16[128,1024]{1,0:T(8,128)(2,1)S(1)}, u32[]{:S(2)}, u32[]{:S(2)}) collective-permute-start(bf16[128,1024]{1,0:T(8,128)(2,1)S(1)} %shard_map.78.refs_0_), channel_id=1, source_target_pairs={{0,8},{8,0},{16,24},{24,16},{1,9},{9,1},{17,25},{25,17},{2,10},{10... | collective-permute-start | bytes 786440 | tf_op jit(solution)/shard_map/ppermute | solution.py:100
  17.3 1.5 %collective-permute-start.7 = (bf16[128,1024]{1,0:T(8,128)(2,1)S(1)}, bf16[128,1024]{1,0:T(8,128)(2,1)S(1)}, u32[]{:S(2)}, u32[]{:S(2)}) collective-permute-start(bf16[128,1024]{1,0:T(8,128)(2,1)S(1)} %collective-permute-done.6.refs_2_), channel_id=1, source_target_pairs={{0,8},{8,0},{16,24},{24,16},{1,9},{9,1},{17,25},{25,17},{2,10},{10... | collective-permute-start | bytes 786440 | tf_op jit(solution)/shard_map/ppermute | solution.py:100
  18.9 3.4 %copy-start.2 = (bf16[256,16384]{1,0:T(8,128)(2,1)S(1)}, bf16[256,16384]{1,0:T(8,128)(2,1)}, u32[]{:S(2)}) copy-start(bf16[256,16384]{1,0:T(8,128)(2,1)} %refs_4_.1) | copy-start | bytes 25165828
  24.8 26.6 %copy-start.4 = (f32[8,8,128]{2,1,0:T(8,128)S(1)}, f32[8,8,128]{2,1,0:T(8,128)}, u32[]{:S(2)}) copy-start(f32[8,8,128]{2,1,0:T(8,128)} %param.8) | copy-start | bytes 98308
  24.8 26.6 %copy-start.6 = (s32[1,1,1,32]{3,2,1,0:T(1,128)S(1)}, s32[1,1,1,32]{3,2,1,0:T(1,128)}, u32[]{:S(2)}) copy-start(s32[1,1,1,32]{3,2,1,0:T(1,128)} %refs_9_.1) | copy-start | bytes 388
  24.8 26.6 %all-to-all-start = ((f32[8,64,128]{2,1,0:T(8,128)}), f32[8,64,128]{2,1,0:T(8,128)S(1)}, u32[]{:S(2)}, u32[]{:S(2)}) async-start(f32[8,64,128]{2,1,0:T(8,128)} %shard_map.79), calls=%async_computation | async-start | bytes 524288 | tf_op jit(solution)/shard_map/all_to_all | solution.py:461
  36.0 15.4 %collective-permute-start = (bf16[1024,128]{1,0:T(8,128)(2,1)S(1)}, bf16[1024,128]{1,0:T(8,128)(2,1)S(1)}, u32[]{:S(2)}, u32[]{:S(2)}) collective-permute-start(bf16[1024,128]{1,0:T(8,128)(2,1)S(1)} %get-tuple-element.18), channel_id=1, source_target_pairs={{0,8},{8,16},{16,24},{1,9},{9,17},{17,25},{2,10},{10,18},{18,26},{... | collective-permute-start | bytes 786440 | tf_op jit(solution)/shard_map/ppermute | solution.py:442
  37.9 13.5 %collective-permute-start.1 = (bf16[1024,128]{1,0:T(8,128)(2,1)S(1)}, bf16[1024,128]{1,0:T(8,128)(2,1)S(1)}, u32[]{:S(2)}, u32[]{:S(2)}) collective-permute-start(bf16[1024,128]{1,0:T(8,128)(2,1)S(1)} %get-tuple-element.19), channel_id=1, source_target_pairs={{8,0},{16,8},{24,16},{9,1},{17,9},{25,17},{10,2},{18,10},{26,18},{... | collective-permute-start | bytes 786440 | tf_op jit(solution)/shard_map/ppermute | solution.py:442
  41.6 9.8 %collective-permute-start.2 = (bf16[1024,128]{1,0:T(8,128)(2,1)S(1)}, bf16[1024,128]{1,0:T(8,128)(2,1)S(1)}, u32[]{:S(2)}, u32[]{:S(2)}) collective-permute-start(bf16[1024,128]{1,0:T(8,128)(2,1)S(1)} %get-tuple-element.20), channel_id=1, source_target_pairs={{0,4},{4,0},{1,5},{5,1},{2,6},{6,2},{3,7},{7,3},{8,12},{12,8},{9,1... | collective-permute-start | bytes 786440 | tf_op jit(solution)/shard_map/ppermute | solution.py:437
  43.1 4.0 %collective-permute-start.4 = (bf16[128,128]{1,0:T(8,128)(2,1)S(1)}, bf16[128,128]{1,0:T(8,128)(2,1)S(1)}, u32[]{:S(2)}, u32[]{:S(2)}) collective-permute-start(bf16[128,128]{1,0:T(8,128)(2,1)S(1)} %get-tuple-element.21), channel_id=1, source_target_pairs={{1,0},{2,1},{3,2},{5,4},{6,5},{7,6},{9,8},{10,9},{11,10},{13,12},{... | collective-permute-start | bytes 98312 | tf_op jit(solution)/shard_map/ppermute | solution.py:444
  45.5 5.8 %collective-permute-start.3 = (bf16[128,128]{1,0:T(8,128)(2,1)S(1)}, bf16[128,128]{1,0:T(8,128)(2,1)S(1)}, u32[]{:S(2)}, u32[]{:S(2)}) collective-permute-start(bf16[128,128]{1,0:T(8,128)(2,1)S(1)} %get-tuple-element.21), channel_id=1, source_target_pairs={{0,1},{1,2},{2,3},{4,5},{5,6},{6,7},{8,9},{9,10},{10,11},{12,13},{... | collective-permute-start | bytes 98312 | tf_op jit(solution)/shard_map/ppermute | solution.py:444
  51.4 1.6 %copy-start.3 = (bf16[128,8,8,128]{3,2,1,0:T(8,128)(2,1)S(1)}, bf16[128,8,8,128]{3,2,1,0:T(8,128)(2,1)}, u32[]{:S(2)}) copy-start(bf16[128,8,8,128]{3,2,1,0:T(8,128)(2,1)} %param.7) | copy-start | bytes 6291460
  65.4 14.5 %collective-permute-start.8 = (bf16[1024,128]{1,0:T(8,128)(2,1)S(1)}, bf16[1024,128]{1,0:T(8,128)(2,1)S(1)}, u32[]{:S(2)}, u32[]{:S(2)}) collective-permute-start(bf16[1024,128]{1,0:T(8,128)(2,1)S(1)} %get-tuple-element.24), channel_id=1, source_target_pairs={{0,8},{8,16},{16,24},{1,9},{9,17},{17,25},{2,10},{10,18},{18,26},{... | collective-permute-start | bytes 786440 | tf_op jit(solution)/shard_map/ppermute | solution.py:442
  67.3 12.6 %collective-permute-start.9 = (bf16[1024,128]{1,0:T(8,128)(2,1)S(1)}, bf16[1024,128]{1,0:T(8,128)(2,1)S(1)}, u32[]{:S(2)}, u32[]{:S(2)}) collective-permute-start(bf16[1024,128]{1,0:T(8,128)(2,1)S(1)} %get-tuple-element.25), channel_id=1, source_target_pairs={{8,0},{16,8},{24,16},{9,1},{17,9},{25,17},{10,2},{18,10},{26,18},{... | collective-permute-start | bytes 786440 | tf_op jit(solution)/shard_map/ppermute | solution.py:442
  70.9 8.9 %collective-permute-start.10 = (bf16[1024,128]{1,0:T(8,128)(2,1)S(1)}, bf16[1024,128]{1,0:T(8,128)(2,1)S(1)}, u32[]{:S(2)}, u32[]{:S(2)}) collective-permute-start(bf16[1024,128]{1,0:T(8,128)(2,1)S(1)} %get-tuple-element.26), channel_id=1, source_target_pairs={{0,4},{4,0},{1,5},{5,1},{2,6},{6,2},{3,7},{7,3},{8,12},{12,8},{9,1... | collective-permute-start | bytes 786440 | tf_op jit(solution)/shard_map/ppermute | solution.py:437
  71.5 4.0 %collective-permute-start.12 = (bf16[128,128]{1,0:T(8,128)(2,1)S(1)}, bf16[128,128]{1,0:T(8,128)(2,1)S(1)}, u32[]{:S(2)}, u32[]{:S(2)}) collective-permute-start(bf16[128,128]{1,0:T(8,128)(2,1)S(1)} %get-tuple-element.27), channel_id=1, source_target_pairs={{1,0},{2,1},{3,2},{5,4},{6,5},{7,6},{9,8},{10,9},{11,10},{13,12},{... | collective-permute-start | bytes 98312 | tf_op jit(solution)/shard_map/ppermute | solution.py:444
  74.0 5.8 %collective-permute-start.11 = (bf16[128,128]{1,0:T(8,128)(2,1)S(1)}, bf16[128,128]{1,0:T(8,128)(2,1)S(1)}, u32[]{:S(2)}, u32[]{:S(2)}) collective-permute-start(bf16[128,128]{1,0:T(8,128)(2,1)S(1)} %get-tuple-element.27), channel_id=1, source_target_pairs={{0,1},{1,2},{2,3},{4,5},{5,6},{6,7},{8,9},{9,10},{10,11},{12,13},{... | collective-permute-start | bytes 98312 | tf_op jit(solution)/shard_map/ppermute | solution.py:444
  91.5 15.4 %collective-permute-start.13 = (bf16[1024,128]{1,0:T(8,128)(2,1)S(1)}, bf16[1024,128]{1,0:T(8,128)(2,1)S(1)}, u32[]{:S(2)}, u32[]{:S(2)}) collective-permute-start(bf16[1024,128]{1,0:T(8,128)(2,1)S(1)} %get-tuple-element.29), channel_id=1, source_target_pairs={{0,8},{8,16},{16,24},{1,9},{9,17},{17,25},{2,10},{10,18},{18,26},{... | collective-permute-start | bytes 786440 | tf_op jit(solution)/shard_map/ppermute | solution.py:442
  93.4 13.5 %collective-permute-start.14 = (bf16[1024,128]{1,0:T(8,128)(2,1)S(1)}, bf16[1024,128]{1,0:T(8,128)(2,1)S(1)}, u32[]{:S(2)}, u32[]{:S(2)}) collective-permute-start(bf16[1024,128]{1,0:T(8,128)(2,1)S(1)} %get-tuple-element.30), channel_id=1, source_target_pairs={{8,0},{16,8},{24,16},{9,1},{17,9},{25,17},{10,2},{18,10},{26,18},{... | collective-permute-start | bytes 786440 | tf_op jit(solution)/shard_map/ppermute | solution.py:442
  97.1 9.8 %collective-permute-start.15 = (bf16[1024,128]{1,0:T(8,128)(2,1)S(1)}, bf16[1024,128]{1,0:T(8,128)(2,1)S(1)}, u32[]{:S(2)}, u32[]{:S(2)}) collective-permute-start(bf16[1024,128]{1,0:T(8,128)(2,1)S(1)} %get-tuple-element.31), channel_id=1, source_target_pairs={{0,4},{4,0},{1,5},{5,1},{2,6},{6,2},{3,7},{7,3},{8,12},{12,8},{9,1... | collective-permute-start | bytes 786440 | tf_op jit(solution)/shard_map/ppermute | solution.py:437
  98.6 4.0 %collective-permute-start.17 = (bf16[128,128]{1,0:T(8,128)(2,1)S(1)}, bf16[128,128]{1,0:T(8,128)(2,1)S(1)}, u32[]{:S(2)}, u32[]{:S(2)}) collective-permute-start(bf16[128,128]{1,0:T(8,128)(2,1)S(1)} %get-tuple-element.32), channel_id=1, source_target_pairs={{1,0},{2,1},{3,2},{5,4},{6,5},{7,6},{9,8},{10,9},{11,10},{13,12},{... | collective-permute-start | bytes 98312 | tf_op jit(solution)/shard_map/ppermute | solution.py:444
  101.1 5.8 %collective-permute-start.16 = (bf16[128,128]{1,0:T(8,128)(2,1)S(1)}, bf16[128,128]{1,0:T(8,128)(2,1)S(1)}, u32[]{:S(2)}, u32[]{:S(2)}) collective-permute-start(bf16[128,128]{1,0:T(8,128)(2,1)S(1)} %get-tuple-element.32), channel_id=1, source_target_pairs={{0,1},{1,2},{2,3},{4,5},{5,6},{6,7},{8,9},{9,10},{10,11},{12,13},{... | collective-permute-start | bytes 98312 | tf_op jit(solution)/shard_map/ppermute | solution.py:444

commit v2 on v1

v2 whole, which is shorter than its diff:
```python
import functools

import jax
import jax.numpy as jnp
from jax import lax
from jax.experimental import pallas as pl
from jax.experimental.pallas import tpu as pltpu
from jax.sharding import PartitionSpec as P

OMEGA = 0.8
BF = jnp.bfloat16
F32 = jnp.float32
WHOLE = pl.BlockSpec(memory_space=pltpu.VMEM)


def iota(shape, dim):
    return lax.broadcasted_iota(jnp.int32, shape, dim)


def dot(a, b):
    return jnp.dot(a, b, preferred_element_type=F32)


def dot_nt(a, b):
    return lax.dot_general(a, b, (((1,), (1,)), ((), ())), preferred_element_type=F32)


def params(mebibytes=24):
    return pltpu.CompilerParams(vmem_limit_bytes=mebibytes * 1024 * 1024)


def trace_kernel(stride, block, field_ref, cell_ref, out_ref, field, cell_v, perm, pick, rsum, sems):
    sides, rows, lanes = field.shape
    slots = cell_ref.shape[3]
    per_row = lanes // stride
    group = 16
    width = group * per_row
    cell_copy = pltpu.make_async_copy(cell_ref, cell_v, sems.at[sides // block])
    cell_copy.start()
    copies = []
    for step in range(sides // block):
        span = pl.ds(step * block, block)
        copies.append(pltpu.make_async_copy(field_ref.at[span], field.at[span], sems.at[step]))
        copies[-1].start()

    shape = (block, block * group)
    rsum[...] = (iota(shape, 1) // group == iota(shape, 0)).astype(BF)
    cell_copy.wait()
    cell = cell_v[0, 0]
    perm[...] = (iota((slots, slots), 0) == cell // stride).astype(BF)
    offset = jnp.broadcast_to((cell % stride).astype(BF), (16, slots))
    sorted_offset = dot_nt(offset, perm[...])[0:1].astype(jnp.int32)
    place = (iota((1, slots), 1) % per_row) * stride + sorted_offset
    pick[...] = (iota((lanes, slots), 0) == place).astype(BF)

    shape = (block * group, width)
    own = iota(shape, 0) % group == iota(shape, 1) // per_row
    picked = []
    for step in range(sides // block):
        copies[step].wait()
        parts = []
        for part in range(rows // group):
            values = field[step * block : (step + 1) * block, part * group : (part + 1) * group, :]
            cols = slice(part * width, (part + 1) * width)
            spread = dot(values.reshape(block * group, lanes), pick[:, cols])
            spread = jnp.where(own, spread, 0.0).astype(BF)
            parts.append(dot(rsum[...], spread).astype(BF))
        picked.append(jnp.concatenate(parts, axis=1))
    out_ref[...] = dot(jnp.concatenate(picked, axis=0), perm[...]).astype(BF)


def traces(field, trace_cell, block):
    sides, rows, lanes = field.shape
    slots = trace_cell.shape[3]
    stride = rows * lanes // slots
    hbm = pl.BlockSpec(memory_space=pltpu.HBM)
    return pl.pallas_call(
        functools.partial(trace_kernel, stride, block),
        in_specs=[hbm, hbm],
        out_specs=WHOLE,
        out_shape=jax.ShapeDtypeStruct((sides, slots), BF),
        scratch_shapes=[
            pltpu.VMEM(field.shape, BF),
            pltpu.VMEM(trace_cell.shape, jnp.int32),
            pltpu.VMEM((slots, slots), BF),
            pltpu.VMEM((lanes, slots), BF),
            pltpu.VMEM((block, block * 16), BF),
            pltpu.SemaphoreType.DMA((sides // block + 1,)),
        ],
        compiler_params=params(62),
        cost_estimate=pl.CostEstimate(
            flops=4 * sides * rows * lanes * 128, bytes_accessed=field.size * 2, transcendentals=0
        ),
    )(field, trace_cell)


def surface_kernel(row, gz, peers, gzs, cols, *refs):
    parts = refs[:peers]
    block_ref, out_ref, held, sems = refs[peers:]
    sides, slots = parts[0].shape
    me, group = lax.axis_index(row), lax.axis_index(gz)
    copies = []
    for key in range(peers):
        start = pl.multiple_of((jnp.bitwise_xor(me, key) * gzs + group) * slots, slots)
        copies.append(
            pltpu.make_async_copy(block_ref.at[:, pl.ds(start, slots)], held.at[key], sems.at[key])
        )
        copies[-1].start()
    total = None
    for key in range(peers):
        copies[key].wait()
        term = dot_nt(parts[key][...], held[key])
        total = term if total is None else total + term
    turned = total.T
    lines = total.shape[1]
    out_ref[...] = jnp.zeros_like(out_ref)
    s_count, l_count, f_count = sides // gzs, lines // cols, lines // (cols * gzs)
    for c in range(cols):
        for g in range(gzs):
            dest = c * gzs + g
            out_ref[dest, :s_count, :l_count] = total[
                g * s_count : (g + 1) * s_count, c * l_count : (c + 1) * l_count
            ].astype(out_ref.dtype)
            out_ref[dest, s_count : s_count + f_count, :sides] = turned[
                dest * f_count : (dest + 1) * f_count
            ].astype(out_ref.dtype)


def surface(parts, block, dtype):
    peers, gzs, cols = lax.axis_size("row"), lax.axis_size("gz"), lax.axis_size("col")
    sides, slots = parts[0].shape
    lines = block.shape[0]
    depth = sides // gzs + lines // (cols * gzs)
    shape = (cols * gzs, depth, max(sides, lines // cols))
    return pl.pallas_call(
        functools.partial(surface_kernel, "row", "gz", peers, gzs, cols),
        in_specs=[WHOLE] * peers + [pl.BlockSpec(memory_space=pltpu.HBM)],
        out_specs=WHOLE,
        out_shape=jax.ShapeDtypeStruct(shape, dtype),
        scratch_shapes=[
            pltpu.VMEM((peers, lines, slots), BF),
            pltpu.SemaphoreType.DMA((peers,)),
        ],
        compiler_params=params(58),
        cost_estimate=pl.CostEstimate(
            flops=2 * sides * lines * slots * peers,
            bytes_accessed=2 * lines * slots * peers,
            transcendentals=0,
        ),
    )(*parts, block)


def swaps(peers):
    pairs = [[(i, i + 1) for i in range(first, peers - 1, 2)] for first in (0, 1)]
    return [[(i, j) for i, j in part] + [(j, i) for i, j in part] for part in pairs if part]


class Shape:
    def __init__(self, sides, first, second, lanes):
        self.sides, self.x, self.y, self.lanes = sides, first, second, lanes
        self.cells = first * second
        self.chunk = max(1, 256 // self.cells)
        self.rows = self.chunk * self.cells
        self.block = min(sides, 16)
        self.faces = [("row", i) for i in range(len(swaps(lax.axis_size("row"))))]
        self.faces += [("col", i) for i in range(len(swaps(lax.axis_size("col"))))]
        self.ends = len(swaps(lax.axis_size("gz")))

    def face_len(self, face):
        return self.y if face[0] == "row" else self.x

    def halo_rows(self):
        return sum(self.chunk * self.face_len(face) for face in self.faces)

    def edge(self, face):
        axis, turn = face
        last = (self.x if axis == "row" else self.y) - 1
        return jnp.where(lax.axis_index(axis) % 2 == turn, last, 0)


def halo_place(shape):
    dims = (shape.rows, shape.halo_rows())
    row, col = iota(dims, 0), iota(dims, 1)
    side, cell = row // shape.cells, row % shape.cells
    x, y = cell // shape.y, cell % shape.y
    hit, base = None, 0
    for face in shape.faces:
        length = shape.face_len(face)
        along, across = (y, x) if face[0] == "row" else (x, y)
        place = (across == shape.edge(face)) & (col - base == side * length + along)
        hit = place if hit is None else hit | place
        base += shape.chunk * length
    return hit.astype(BF)


def z_mask(shape, count):
    dims = (count * shape.cells, 2 * shape.cells)
    return iota(dims, 1) % shape.cells == iota(dims, 0) % shape.cells


def build_out(shape, ends_m, rsum):
    dims = (shape.lanes, 2 * shape.cells)
    edge = jnp.where(iota(dims, 1) < shape.cells, 0, shape.lanes - 1)
    ends_m[...] = (iota(dims, 0) == edge).astype(BF)
    dims = (shape.block, shape.block * shape.cells)
    rsum[...] = (iota(dims, 1) // shape.cells == iota(dims, 0)).astype(BF)


def emit_faces(shape, at, values, tall, face_refs, z_ref, ends_m, rsum):
    for face, ref in zip(shape.faces, face_refs):
        length, edge = shape.face_len(face), shape.edge(face)
        lines = []
        for side in range(shape.block):
            start = side * shape.cells
            if face[0] == "row":
                lines.append(tall[pl.ds(pl.multiple_of(start + edge * length, 8), length), :])
            else:
                lines.append(tall[pl.ds(start + edge, length, stride=shape.y), :])
        span = shape.block * length
        ref[pl.ds(pl.multiple_of(at * length, span), span), :] = jnp.concatenate(
            lines, axis=0
        ).astype(BF)
    tips = jnp.where(z_mask(shape, shape.block), dot(values, ends_m[...]), 0.0).astype(BF)
    z_ref[pl.ds(pl.multiple_of(at, shape.block), shape.block), :] = dot(rsum[...], tips).astype(BF)


def faces_kernel(shape, field_ref, *refs):
    *face_refs, z_ref, tall, ends_m, rsum = refs
    build_out(shape, ends_m, rsum)

    @pl.loop(0, shape.sides // shape.block)
    def _(step):
        size = shape.block * shape.cells
        values = field_ref[pl.ds(pl.multiple_of(step * size, size), size), :]
        tall[...] = values.astype(F32)
        emit_faces(shape, step * shape.block, values, tall, face_refs, z_ref, ends_m, rsum)


def face_outputs(shape):
    shapes = [
        jax.ShapeDtypeStruct((shape.sides * shape.face_len(face), shape.lanes), BF)
        for face in shape.faces
    ]
    return shapes + [jax.ShapeDtypeStruct((shape.sides, 2 * shape.cells), BF)]


def face_scratch(shape):
    return [
        pltpu.VMEM((shape.block * shape.cells, shape.lanes), F32),
        pltpu.VMEM((shape.lanes, 2 * shape.cells), BF),
        pltpu.VMEM((shape.block, shape.block * shape.cells), BF),
    ]


def first_faces(shape, field):
    shapes = face_outputs(shape)
    return pl.pallas_call(
        functools.partial(faces_kernel, shape),
        in_specs=[WHOLE],
        out_specs=[WHOLE] * len(shapes),
        out_shape=shapes,
        scratch_shapes=face_scratch(shape),
        compiler_params=params(),
        cost_estimate=pl.CostEstimate(
            flops=field.size * 128, bytes_accessed=4 * field.size, transcendentals=0
        ),
    )(field)


def sweep_kernel(shape, with_flux, last, *refs):
    refs = list(refs)
    take = lambda count: [refs.pop(0) for _ in range(count)]
    field_ref, load_ref, coef_ref = take(3)
    halo_refs = take(len(shape.faces))
    end_refs = take(shape.ends)
    if with_flux:
        recv_ref, cell_ref = take(2)
    (out_ref,) = take(1)
    if not last:
        face_refs = take(len(shape.faces))
        (z_ref,) = take(1)
    if with_flux:
        source_ref, flux_ref = take(2)
    weight, near_m, line_m = take(3)
    if not last:
        tall, ends_m, rsum = take(3)
    if with_flux:
        phi, cell_m = take(2)

    grid_step = pl.program_id(0)
    cells, lanes = shape.cells, shape.lanes

    @pl.when(grid_step == 0)
    def _():
        weight[...] = OMEGA / (6.0 + coef_ref[...])
        dims = (shape.rows, shape.rows)
        row, col = iota(dims, 0), iota(dims, 1)
        x, y = row % cells // shape.y, row % shape.y
        x2, y2 = col % cells // shape.y, col % shape.y
        near = ((x == x2) & (jnp.abs(y - y2) == 1)) | ((y == y2) & (jnp.abs(x - x2) == 1))
        near_m[:, : shape.rows] = (near & (row // cells == col // cells)).astype(BF)
        near_m[:, shape.rows :] = halo_place(shape)
        dims = (lanes, lanes)
        line_m[:lanes, :] = (jnp.abs(iota(dims, 0) - iota(dims, 1)) == 1).astype(BF)
        dims = (2 * cells, lanes)
        edge = jnp.where(iota(dims, 0) < cells, lanes - 1, 0)
        line_m[lanes:, :] = (iota(dims, 1) == edge).astype(BF)
        if not last:
            build_out(shape, ends_m, rsum)
        if with_flux:
            total = recv_ref[0].astype(F32)
            for peer in range(1, recv_ref.shape[0]):
                total = total + recv_ref[peer].astype(F32)
            s_count, l_count = flux_ref.shape
            slots = cell_ref.shape[3]
            flux_ref[...] = total[:s_count, :l_count]
            owned = total[s_count : s_count + slots, : shape.sides]
            high = owned.astype(BF).astype(F32)
            both = jnp.concatenate([high, owned - high], axis=0)
            phi[...] = both.T
            cell = jnp.concatenate([cell_ref[0, 0]] * 2, axis=1)
            cell_m[...] = (iota((lanes, 2 * slots), 0) == cell % lanes).astype(BF)

    mask = z_mask(shape, 1)
    even = lax.axis_index("gz") % 2 == 0
    first_swap = (iota((shape.block, 2 * cells), 1) < cells) == even
    if with_flux:
        slots = cell_ref.shape[3]
        cell = jnp.concatenate([cell_ref[0, 0]] * 2, axis=1)
        cell_mask = iota((cells, 2 * slots), 0) == cell // lanes
    weights = jnp.concatenate([weight[...]] * shape.chunk, axis=0)
    out_sides = out_ref.shape[0] // cells

    @pl.loop(0, out_sides // shape.block)
    def _(step):
        local = step * shape.block
        at = grid_step * out_sides + local
        sides = pl.ds(pl.multiple_of(at, shape.block), shape.block)
        zs = end_refs[0][sides, :].astype(F32)
        other = end_refs[1][sides, :].astype(F32) if shape.ends > 1 else 0.0
        zs = jnp.where(first_swap, zs, other)
        if with_flux:
            phis = phi[sides, :]
        for index in range(shape.block // shape.chunk):
            offset = index * shape.rows
            span = pl.ds(pl.multiple_of(at * cells + offset, shape.rows), shape.rows)
            values = field_ref[span, :]
            stack = [values]
            for face, ref in zip(shape.faces, halo_refs):
                length = shape.face_len(face)
                size = shape.chunk * length
                start = pl.multiple_of(at * length + index * size, size)
                stack.append(ref[pl.ds(start, size), :])
            spread = []
            for side in range(index * shape.chunk, (index + 1) * shape.chunk):
                line = jnp.broadcast_to(zs[side : side + 1], mask.shape)
                spread.append(jnp.where(mask, line, 0.0))
            spread = jnp.concatenate(spread, axis=0).astype(BF)
            near = dot(near_m[...], jnp.concatenate(stack, axis=0))
            near = near + dot(jnp.concatenate([values, spread], axis=1), line_m[...])
            source = load_ref[span, :].astype(F32)
            if with_flux:
                spread = []
                for side in range(index * shape.chunk, (index + 1) * shape.chunk):
                    line = jnp.broadcast_to(phis[side : side + 1], cell_mask.shape)
                    spread.append(jnp.where(cell_mask, line, 0.0))
                spread = jnp.concatenate(spread, axis=0).astype(BF)
                source = source + dot_nt(spread, cell_m[...])
                source_ref[span, :] = source.astype(BF)
            fresh = (1.0 - OMEGA) * values.astype(F32) + weights * (source + near)
            out_span = pl.ds(pl.multiple_of(local * cells + offset, shape.rows), shape.rows)
            out_ref[out_span, :] = fresh.astype(BF)
            if not last:
                tall[offset : offset + shape.rows, :] = fresh
        if not last:
            size = shape.block * cells
            values = out_ref[pl.ds(pl.multiple_of(local * cells, size), size), :]
            emit_faces(shape, at, values, tall, face_refs, z_ref, ends_m, rsum)


def sweep(shape, field, load, coef, halos, recv=None, flux_cell=None, last=False):
    with_flux = recv is not None
    lanes, cells = shape.lanes, shape.cells
    operands = [field, load, coef, *halos]
    out_shapes = [jax.ShapeDtypeStruct(field.shape, BF)]
    scratch = [
        pltpu.VMEM(coef.shape, F32),
        pltpu.VMEM((shape.rows, shape.rows + shape.halo_rows()), BF),
        pltpu.VMEM((lanes + 2 * cells, lanes), BF),
    ]
    if not last:
        out_shapes += face_outputs(shape)
        scratch += face_scratch(shape)
    if with_flux:
        slots = flux_cell.shape[3]
        gzs = lax.axis_size("gz")
        operands += [recv, flux_cell]
        out_shapes += [
            jax.ShapeDtypeStruct(field.shape, BF),
            jax.ShapeDtypeStruct((shape.sides // gzs, slots * gzs), F32),
        ]
        scratch += [pltpu.VMEM((shape.sides, 2 * slots), F32), pltpu.VMEM((lanes, 2 * slots), BF)]
    steps = max(1, shape.sides // (2 * shape.block)) if last else 1
    out_specs = [WHOLE] * len(out_shapes)
    if last:
        out_specs = [pl.BlockSpec((field.shape[0] // steps, lanes), lambda i: (i, 0))]
    return pl.pallas_call(
        functools.partial(sweep_kernel, shape, with_flux, last),
        grid=(steps,),
        in_specs=[WHOLE] * len(operands),
        out_specs=out_specs,
        out_shape=out_shapes,
        scratch_shapes=scratch,
        compiler_params=params(),
        cost_estimate=pl.CostEstimate(
            flops=6 * field.size * 128, bytes_accessed=8 * field.size, transcendentals=0
        ),
    )(*operands)


def exchange(shape, faces):
    *cut, ends = faces
    halos = {}
    for face, value in sorted(zip(shape.faces, cut), key=lambda item: item[0][0]):
        pairs = swaps(lax.axis_size(face[0]))[face[1]]
        halos[face] = lax.ppermute(value, face[0], pairs)
    tips = [lax.ppermute(ends, "gz", pairs) for pairs in swaps(lax.axis_size("gz"))]
    return [halos[face] for face in shape.faces] + tips


def xor_gather(value, axis, hidden):
    peers = lax.axis_size(axis)
    held = {0: value}
    bit = peers // 2
    while bit:
        swap = [(i, i ^ bit) for i in range(peers)]
        fresh = {key ^ bit: lax.ppermute(held[key], axis, swap) for key in sorted(held, reverse=True)}
        held.update(fresh)
        if bit == peers // 2:
            held[bit], hidden = lax.optimization_barrier((held[bit], hidden))
        bit //= 2
    return [held[key] for key in range(peers)], hidden


def per_device(volume_field, volume_load, coefficient, surface_block, trace_cell, flux_cell):
    sides, first, second, lanes = volume_field.shape
    cells = first * second
    shape = Shape(sides, first, second, lanes)
    field = volume_field.reshape(sides * cells, lanes)
    load = volume_load.reshape(sides * cells, lanes)
    coef = coefficient.reshape(cells, lanes)

    trace = traces(volume_field.reshape(sides, cells, lanes), trace_cell, min(32, sides))
    parts, faces = xor_gather(trace, "row", first_faces(shape, field))
    halos = exchange(shape, faces)
    sent = surface(parts, surface_block, F32)
    recv = lax.all_to_all(sent, ("col", "gz"), split_axis=0, concat_axis=0, tiled=True)

    current, *faces, source, surface_flux = sweep(
        shape, field, load, coef, halos, recv=recv, flux_cell=flux_cell
    )
    current, *faces = sweep(shape, current, source, coef, exchange(shape, faces))
    (current,) = sweep(shape, current, source, coef, exchange(shape, faces), last=True)
    return current.reshape(volume_field.shape), surface_flux


def solution(mesh):
    in_specs = (
        P(None, "row", "col", "gz"),
        P(None, "row", "col", "gz"),
        P("row", "col", "gz"),
        P("row", "col"),
        P("row", "col", "gz", None),
        P("row", "col", "gz", None),
    )
    out_specs = (P(None, "row", "col", "gz"), P("gz", ("row", "col")))
    return jax.shard_map(
        per_device, mesh=mesh, in_specs=in_specs, out_specs=out_specs, check_vma=False
    )
```

time: 112 us -> 85.7 us (0.77)
  the two profiles are of different devices: /device:TPU:26 before, /device:TPU:0 now
where the time goes in v2:
time: 85.7 us; the launch traced here: 84.1 us
  Pallas kernels  37.6 us (44%)
  starting transfers between devices  32.4 us (38%)
  waiting for transfers between devices  9.37 us (11%)
  local copies, waits for them, and re-layouts  3.91 us (5%)
    pallas_call x3, Pallas kernels, sweep(): pl.pallas_call(functools.partial(sweep_kernel, shape, with_flux, last), g...  22 us
    ppermute x6, starting transfers between devices, exchange(): lax.ppermute(ends, 'gz', pairs)  13.7 us
    ppermute x9, starting transfers between devices, exchange(): halos[face] = lax.ppermute(value, face[0], pairs)  9.54 us
    pallas_call x1, Pallas kernels, traces(): pl.pallas_call(functools.partial(trace_kernel, stride, block), in_specs=[...  7.26 us
    all_to_all x1, starting transfers between devices, per_device(): lax.all_to_all(sent, ('col', 'gz'), split_axis=0, concat_axis=0, tiled=True)  6.1 us
    ppermute x6, waiting for transfers between devices, exchange(): lax.ppermute(ends, 'gz', pairs)  5.68 us
    pallas_call x1, Pallas kernels, surface(): pl.pallas_call(functools.partial(surface_kernel, 'row', 'gz', peers, gzs,...  4.65 us
    unnamed x16, local copies, waits for them, and re-layouts  3.91 us
  transfers between devices with their start and end apart: 19, of which 6 were waited for; matrix products, arithmetic and copies ran while one was open for 0% of the time, Pallas kernels for 4%

profile of v2, /device:TPU:0, one launch (start us, length us, event | category | flops | bytes accessed | tf_op | source)
XLA Modules:
  0.0 84.1 jit_solution(5475587536964282391)
XLA Ops:
  0.6 7.3 %shard_map.77.refs_0_ = bf16[128,1024]{1,0:T(8,128)(2,1)} custom-call(bf16[128,64,128]{2,1,0:T(8,128)(2,1)} %bitcast.5, s32[1,1,1,1024]{3,2,1,0:T(1,128)} %cell_ref.1), custom_call_target="tpu_custom_call" | custom-call | flops 536870912 | bytes 2097152 | tf_op jit(solution)/shard_map/pallas_call | solution.py:77
  7.9 3.0 %collective-permute-start = (bf16[128,1024]{1,0:T(8,128)(2,1)}, bf16[128,1024]{1,0:T(8,128)(2,1)S(1)}, u32[]{:S(2)}, u32[]{:S(2)}) collective-permute-start(bf16[128,1024]{1,0:T(8,128)(2,1)} %shard_map.77.refs_0_), channel_id=1, source_target_pairs={{0,16},{8,24},{16,0},{24,8},{1,17},{9,25},{17,1},{25,9},{2,18},{10... | collective-permute-start | bytes 786440 | tf_op jit(solution)/shard_map/ppermute | solution.py:437
  10.9 1.6 %copy-done = bf16[128,8,8,128]{3,2,1,0:T(8,128)(2,1)S(1)} copy-done((bf16[128,8,8,128]{3,2,1,0:T(8,128)(2,1)S(1)}, bf16[128,8,8,128]{3,2,1,0:T(8,128)(2,1)}, u32[]{:S(2)}) %copy-start) | copy-done | bytes 2097176
  12.5 3.7 %shard_map.78 = (bf16[1024,128]{1,0:T(8,128)(2,1)}, bf16[1024,128]{1,0:T(8,128)(2,1)}, bf16[1024,128]{1,0:T(8,128)(2,1)S(1)}, bf16[128,128]{1,0:T(8,128)(2,1)S(1)}) custom-call(bf16[8192,128]{1,0:T(8,128)(2,1)S(1)} %bitcast.6), custom_call_target="tpu_custom_call" | custom-call | flops 134217728 | bytes 4194304 | tf_op jit(solution)/shard_map/pallas_call | solution.py:257
  16.2 1.2 %collective-permute-done.refs_2_ = bf16[128,1024]{1,0:T(8,128)(2,1)S(1)} collective-permute-done((bf16[128,1024]{1,0:T(8,128)(2,1)}, bf16[128,1024]{1,0:T(8,128)(2,1)S(1)}, u32[]{:S(2)}, u32[]{:S(2)}) %collective-permute-start) | collective-permute-done | bytes 262176 | tf_op jit(solution)/shard_map/ppermute | solution.py:437
  17.4 0.1 collective-permute-start.7
  17.5 1.5 %collective-permute-done.7.refs_3_ = bf16[128,1024]{1,0:T(8,128)(2,1)S(1)} collective-permute-done((bf16[128,1024]{1,0:T(8,128)(2,1)S(1)}, bf16[128,1024]{1,0:T(8,128)(2,1)S(1)}, u32[]{:S(2)}, u32[]{:S(2)}) %collective-permute-start.7) | collective-permute-done | bytes 262176 | tf_op jit(solution)/shard_map/ppermute | solution.py:437
  19.0 0.7 copy-done.7
  19.7 4.7 %shard_map.79 = f32[8,64,128]{2,1,0:T(8,128)} custom-call(bf16[128,1024]{1,0:T(8,128)(2,1)} %shard_map.77.refs_0_, bf16[128,1024]{1,0:T(8,128)(2,1)} %copy-done.6, bf16[128,1024]{1,0:T(8,128)(2,1)} %copy-done.5, bf16[128,1024]{1,0:T(8,128)(2,1)} %copy-done.7, bf16[256,16384]{1,0:T(8,128)(2,1)} %refs_4_.1), custom_call_target="tpu_custom_call" | custom-call | flops 268435456 | bytes 2097152 | tf_op jit(solution)/shard_map/pallas_call | solution.py:135
  24.4 6.1 %all-to-all-start = ((f32[8,64,128]{2,1,0:T(8,128)}), f32[8,64,128]{2,1,0:T(8,128)S(1)}, u32[]{:S(2)}, u32[]{:S(2)}) async-start(f32[8,64,128]{2,1,0:T(8,128)} %shard_map.79), calls=%async_computation | async-start | bytes 524288 | tf_op jit(solution)/shard_map/all_to_all | solution.py:457
  30.5 0.7 collective-permute-start.2
  31.2 2.1 %collective-permute-start.3 = (bf16[1024,128]{1,0:T(8,128)(2,1)S(1)}, bf16[1024,128]{1,0:T(8,128)(2,1)S(1)}, u32[]{:S(2)}, u32[]{:S(2)}) collective-permute-start(bf16[1024,128]{1,0:T(8,128)(2,1)S(1)} %get-tuple-element.29), channel_id=1, source_target_pairs={{0,4},{4,0},{1,5},{5,1},{2,6},{6,2},{3,7},{7,3},{8,12},{12,8},{9,1... | collective-permute-start | bytes 786440 | tf_op jit(solution)/shard_map/ppermute | solution.py:426
  33.3 0.7 collective-permute-start.5
  33.9 4.2 %collective-permute-start.4 = (bf16[128,128]{1,0:T(8,128)(2,1)S(1)}, bf16[128,128]{1,0:T(8,128)(2,1)S(1)}, u32[]{:S(2)}, u32[]{:S(2)}) collective-permute-start(bf16[128,128]{1,0:T(8,128)(2,1)S(1)} %get-tuple-element.30), channel_id=1, source_target_pairs={{0,1},{2,3},{1,0},{3,2},{4,5},{6,7},{5,4},{7,6},{8,9},{10,11},{9,8... | collective-permute-start | bytes 98312 | tf_op jit(solution)/shard_map/ppermute | solution.py:427
  38.2 1.9 %collective-permute-done.4.refs_6_ = bf16[128,128]{1,0:T(8,128)(2,1)S(1)} collective-permute-done((bf16[128,128]{1,0:T(8,128)(2,1)S(1)}, bf16[128,128]{1,0:T(8,128)(2,1)S(1)}, u32[]{:S(2)}, u32[]{:S(2)}) %collective-permute-start.4) | collective-permute-done | bytes 32800 | tf_op jit(solution)/shard_map/ppermute | solution.py:427
  40.1 0.9 %collective-permute-done.3.refs_5_ = bf16[1024,128]{1,0:T(8,128)(2,1)S(1)} collective-permute-done((bf16[1024,128]{1,0:T(8,128)(2,1)S(1)}, bf16[1024,128]{1,0:T(8,128)(2,1)S(1)}, u32[]{:S(2)}, u32[]{:S(2)}) %collective-permute-start.3) | collective-permute-done | bytes 262176 | tf_op jit(solution)/shard_map/ppermute | solution.py:426
  41.0 1.6 %copy-done.2 = bf16[128,8,8,128]{3,2,1,0:T(8,128)(2,1)S(1)} copy-done((bf16[128,8,8,128]{3,2,1,0:T(8,128)(2,1)S(1)}, bf16[128,8,8,128]{3,2,1,0:T(8,128)(2,1)}, u32[]{:S(2)}) %copy-start.2) | copy-done | bytes 2097176
  42.6 9.2 %shard_map.80 = (bf16[8192,128]{1,0:T(8,128)(2,1)S(1)}, bf16[1024,128]{1,0:T(8,128)(2,1)S(1)}, bf16[1024,128]{1,0:T(8,128)(2,1)S(1)}, bf16[1024,128]{1,0:T(8,128...) custom-call(bf16[8192,128]{1,0:T(8,128)(2,1)S(1)} %bitcast.7, ...), custom_call_target="tpu_custom_call" | custom-call | flops 805306368 | bytes 8388608 | tf_op jit(solution)/shard_map/pallas_call | solution.py:407
  51.8 1.2 %collective-permute-start.8 = (bf16[1024,128]{1,0:T(8,128)(2,1)S(1)}, bf16[1024,128]{1,0:T(8,128)(2,1)S(1)}, u32[]{:S(2)}, u32[]{:S(2)}) collective-permute-start(bf16[1024,128]{1,0:T(8,128)(2,1)S(1)} %get-tuple-element.34), channel_id=1, source_target_pairs={{0,8},{16,24},{8,0},{24,16},{1,9},{17,25},{9,1},{25,17},{2,10},{18... | collective-permute-start | bytes 786440 | tf_op jit(solution)/shard_map/ppermute | solution.py:426
  53.0 0.7 collective-permute-start.9
  53.7 1.5 %collective-permute-start.10 = (bf16[1024,128]{1,0:T(8,128)(2,1)S(1)}, bf16[1024,128]{1,0:T(8,128)(2,1)S(1)}, u32[]{:S(2)}, u32[]{:S(2)}) collective-permute-start(bf16[1024,128]{1,0:T(8,128)(2,1)S(1)} %get-tuple-element.36), channel_id=1, source_target_pairs={{0,4},{4,0},{1,5},{5,1},{2,6},{6,2},{3,7},{7,3},{8,12},{12,8},{9,1... | collective-permute-start | bytes 786440 | tf_op jit(solution)/shard_map/ppermute | solution.py:426
  55.2 0.7 collective-permute-start.12
  55.9 3.7 %collective-permute-start.11 = (bf16[128,128]{1,0:T(8,128)(2,1)S(1)}, bf16[128,128]{1,0:T(8,128)(2,1)S(1)}, u32[]{:S(2)}, u32[]{:S(2)}) collective-permute-start(bf16[128,128]{1,0:T(8,128)(2,1)S(1)} %get-tuple-element.37), channel_id=1, source_target_pairs={{0,1},{2,3},{1,0},{3,2},{4,5},{6,7},{5,4},{7,6},{8,9},{10,11},{9,8... | collective-permute-start | bytes 98312 | tf_op jit(solution)/shard_map/ppermute | solution.py:427
  59.6 1.9 %collective-permute-done.11.refs_6_ = bf16[128,128]{1,0:T(8,128)(2,1)S(1)} collective-permute-done((bf16[128,128]{1,0:T(8,128)(2,1)S(1)}, bf16[128,128]{1,0:T(8,128)(2,1)S(1)}, u32[]{:S(2)}, u32[]{:S(2)}) %collective-permute-start.11) | collective-permute-done | bytes 32800 | tf_op jit(solution)/shard_map/ppermute | solution.py:427
  61.5 7.7 %shard_map.81 = (bf16[8192,128]{1,0:T(8,128)(2,1)S(1)}, bf16[1024,128]{1,0:T(8,128)(2,1)S(1)}, bf16[1024,128]{1,0:T(8,128)(2,1)S(1)}, bf16[1024,128]{1,0:T(8,128)(2,1)S(1)}, bf16[128,128]{1,0:T(8,128)(2,1)S(1)}) custom-call(bf16[8192,128]{1,0:T(8,128)(2,1)S(1)} %get-tuple-element.32.refs_0_, bf16[8192,128]{1,0:T(8,128)(2,1)S(1)} %get-tuple-element.33.refs_1_, ...), custom_call_target="tpu_custom_call" | custom-call | flops 805306368 | bytes 8388608 | tf_op jit(solution)/shard_map/pallas_call | solution.py:407
  69.2 1.3 %collective-permute-start.13 = (bf16[1024,128]{1,0:T(8,128)(2,1)S(1)}, bf16[1024,128]{1,0:T(8,128)(2,1)S(1)}, u32[]{:S(2)}, u32[]{:S(2)}) collective-permute-start(bf16[1024,128]{1,0:T(8,128)(2,1)S(1)} %get-tuple-element.39), channel_id=1, source_target_pairs={{0,8},{16,24},{8,0},{24,16},{1,9},{17,25},{9,1},{25,17},{2,10},{18... | collective-permute-start | bytes 786440 | tf_op jit(solution)/shard_map/ppermute | solution.py:426
  70.5 0.7 collective-permute-start.14
  71.2 1.4 %collective-permute-start.15 = (bf16[1024,128]{1,0:T(8,128)(2,1)S(1)}, bf16[1024,128]{1,0:T(8,128)(2,1)S(1)}, u32[]{:S(2)}, u32[]{:S(2)}) collective-permute-start(bf16[1024,128]{1,0:T(8,128)(2,1)S(1)} %get-tuple-element.41), channel_id=1, source_target_pairs={{0,4},{4,0},{1,5},{5,1},{2,6},{6,2},{3,7},{7,3},{8,12},{12,8},{9,1... | collective-permute-start | bytes 786440 | tf_op jit(solution)/shard_map/ppermute | solution.py:426
  72.6 0.7 collective-permute-start.17
  73.3 3.8 %collective-permute-start.16 = (bf16[128,128]{1,0:T(8,128)(2,1)S(1)}, bf16[128,128]{1,0:T(8,128)(2,1)S(1)}, u32[]{:S(2)}, u32[]{:S(2)}) collective-permute-start(bf16[128,128]{1,0:T(8,128)(2,1)S(1)} %get-tuple-element.42), channel_id=1, source_target_pairs={{0,1},{2,3},{1,0},{3,2},{4,5},{6,7},{5,4},{7,6},{8,9},{10,11},{9,8... | collective-permute-start | bytes 98312 | tf_op jit(solution)/shard_map/ppermute | solution.py:427
  77.0 1.9 %collective-permute-done.16.refs_6_ = bf16[128,128]{1,0:T(8,128)(2,1)S(1)} collective-permute-done((bf16[128,128]{1,0:T(8,128)(2,1)S(1)}, bf16[128,128]{1,0:T(8,128)(2,1)S(1)}, u32[]{:S(2)}, u32[]{:S(2)}) %collective-permute-start.16) | collective-permute-done | bytes 32800 | tf_op jit(solution)/shard_map/ppermute | solution.py:427
  78.9 5.1 %shard_map.82 = bf16[8192,128]{1,0:T(8,128)(2,1)} custom-call(bf16[8192,128]{1,0:T(8,128)(2,1)S(1)} %get-tuple-element.38.refs_0_, bf16[8192,128]{1,0:T(8,128)(2,1)S(1)} %get-tuple-element.33.refs_1_, f32[64,128]{1,0:T(8,128)S(1)} %bitcast.11, bf16[1024,128]{1,0:T(8,128)(2,1)S(1)} %collective-permute-done.13.refs_3_, ...), custom_call_target="tpu_custom_call" | custom-call | flops 805306368 | bytes 8388608 | tf_op jit(solution)/shard_map/pallas_call | solution.py:407
  (28 shorter events, 0.1 us)
Async XLA Ops:
  7.9 9.5 %collective-permute-start = (bf16[128,1024]{1,0:T(8,128)(2,1)}, bf16[128,1024]{1,0:T(8,128)(2,1)S(1)}, u32[]{:S(2)}, u32[]{:S(2)}) collective-permute-start(bf16[128,1024]{1,0:T(8,128)(2,1)} %shard_map.77.refs_0_), channel_id=1, source_target_pairs={{0,16},{8,24},{16,0},{24,8},{1,17},{9,25},{17,1},{25,9},{2,18},{10... | collective-permute-start | bytes 786440 | tf_op jit(solution)/shard_map/ppermute | solution.py:437
  10.9 6.6 %collective-permute-start.6 = (bf16[128,1024]{1,0:T(8,128)(2,1)}, bf16[128,1024]{1,0:T(8,128)(2,1)S(1)}, u32[]{:S(2)}, u32[]{:S(2)}) collective-permute-start(bf16[128,1024]{1,0:T(8,128)(2,1)} %shard_map.77.refs_0_), channel_id=1, source_target_pairs={{0,8},{8,0},{16,24},{24,16},{1,9},{9,1},{17,25},{25,17},{2,10},{10... | collective-permute-start | bytes 786440 | tf_op jit(solution)/shard_map/ppermute | solution.py:437
  10.9 1.6 %copy-start = (bf16[128,8,8,128]{3,2,1,0:T(8,128)(2,1)S(1)}, bf16[128,8,8,128]{3,2,1,0:T(8,128)(2,1)}, u32[]{:S(2)}) copy-start(bf16[128,8,8,128]{3,2,1,0:T(8,128)(2,1)} %param.6) | copy-start | bytes 6291460
  17.4 1.6 %copy-start.5 = (bf16[128,1024]{1,0:T(8,128)(2,1)}, bf16[128,1024]{1,0:T(8,128)(2,1)S(1)}, u32[]{:S(2)}) copy-start(bf16[128,1024]{1,0:T(8,128)(2,1)S(1)} %collective-permute-done.refs_2_) | copy-start | bytes 786436
  17.4 23.6 %copy-start.1 = (bf16[128,8,8,128]{3,2,1,0:T(8,128)(2,1)S(1)}, bf16[128,8,8,128]{3,2,1,0:T(8,128)(2,1)}, u32[]{:S(2)}) copy-start(bf16[128,8,8,128]{3,2,1,0:T(8,128)(2,1)} %param.6) | copy-start | bytes 6291460
  17.4 23.6 %copy-start.3 = (f32[8,8,128]{2,1,0:T(8,128)S(1)}, f32[8,8,128]{2,1,0:T(8,128)}, u32[]{:S(2)}) copy-start(f32[8,8,128]{2,1,0:T(8,128)} %param.8) | copy-start | bytes 98308
  17.4 23.6 %copy-start.4 = (s32[1,1,1,32]{3,2,1,0:T(1,128)S(1)}, s32[1,1,1,32]{3,2,1,0:T(1,128)}, u32[]{:S(2)}) copy-start(s32[1,1,1,32]{3,2,1,0:T(1,128)} %refs_9_.1) | copy-start | bytes 388
  17.4 1.6 %collective-permute-start.7 = (bf16[128,1024]{1,0:T(8,128)(2,1)S(1)}, bf16[128,1024]{1,0:T(8,128)(2,1)S(1)}, u32[]{:S(2)}, u32[]{:S(2)}) collective-permute-start(bf16[128,1024]{1,0:T(8,128)(2,1)S(1)} %collective-permute-done.refs_2_), channel_id=1, source_target_pairs={{0,8},{8,0},{16,24},{24,16},{1,9},{9,1},{17,25},{25,17},{2,10},{10... | collective-permute-start | bytes 786440 | tf_op jit(solution)/shard_map/ppermute | solution.py:437
  17.5 1.5 %copy-start.6 = (bf16[128,1024]{1,0:T(8,128)(2,1)}, bf16[128,1024]{1,0:T(8,128)(2,1)S(1)}, u32[]{:S(2)}) copy-start(bf16[128,1024]{1,0:T(8,128)(2,1)S(1)} %collective-permute-done.6.refs_1_) | copy-start | bytes 786436
  19.0 0.7 copy-start.7
  24.4 16.6 %all-to-all-start = ((f32[8,64,128]{2,1,0:T(8,128)}), f32[8,64,128]{2,1,0:T(8,128)S(1)}, u32[]{:S(2)}, u32[]{:S(2)}) async-start(f32[8,64,128]{2,1,0:T(8,128)} %shard_map.79), calls=%async_computation | async-start | bytes 524288 | tf_op jit(solution)/shard_map/all_to_all | solution.py:457
  30.5 9.6 %collective-permute-start.1 = (bf16[1024,128]{1,0:T(8,128)(2,1)}, bf16[1024,128]{1,0:T(8,128)(2,1)S(1)}, u32[]{:S(2)}, u32[]{:S(2)}) collective-permute-start(bf16[1024,128]{1,0:T(8,128)(2,1)} %get-tuple-element.27), channel_id=1, source_target_pairs={{0,8},{16,24},{8,0},{24,16},{1,9},{17,25},{9,1},{25,17},{2,10},{18... | collective-permute-start | bytes 786440 | tf_op jit(solution)/shard_map/ppermute | solution.py:426
  30.5 9.6 %collective-permute-start.2 = (bf16[1024,128]{1,0:T(8,128)(2,1)}, bf16[1024,128]{1,0:T(8,128)(2,1)S(1)}, u32[]{:S(2)}, u32[]{:S(2)}) collective-permute-start(bf16[1024,128]{1,0:T(8,128)(2,1)} %get-tuple-element.28), channel_id=1, source_target_pairs={{8,16},{16,8},{9,17},{17,9},{10,18},{18,10},{11,19},{19,11},{12,20... | collective-permute-start | bytes 786440 | tf_op jit(solution)/shard_map/ppermute | solution.py:426
  31.2 9.8 %collective-permute-start.3 = (bf16[1024,128]{1,0:T(8,128)(2,1)S(1)}, bf16[1024,128]{1,0:T(8,128)(2,1)S(1)}, u32[]{:S(2)}, u32[]{:S(2)}) collective-permute-start(bf16[1024,128]{1,0:T(8,128)(2,1)S(1)} %get-tuple-element.29), channel_id=1, source_target_pairs={{0,4},{4,0},{1,5},{5,1},{2,6},{6,2},{3,7},{7,3},{8,12},{12,8},{9,1... | collective-permute-start | bytes 786440 | tf_op jit(solution)/shard_map/ppermute | solution.py:426
  33.3 4.9 %collective-permute-start.5 = (bf16[128,128]{1,0:T(8,128)(2,1)S(1)}, bf16[128,128]{1,0:T(8,128)(2,1)S(1)}, u32[]{:S(2)}, u32[]{:S(2)}) collective-permute-start(bf16[128,128]{1,0:T(8,128)(2,1)S(1)} %get-tuple-element.30), channel_id=1, source_target_pairs={{1,2},{2,1},{5,6},{6,5},{9,10},{10,9},{13,14},{14,13},{17,18},{18,... | collective-permute-start | bytes 98312 | tf_op jit(solution)/shard_map/ppermute | solution.py:427
  33.9 6.1 %collective-permute-start.4 = (bf16[128,128]{1,0:T(8,128)(2,1)S(1)}, bf16[128,128]{1,0:T(8,128)(2,1)S(1)}, u32[]{:S(2)}, u32[]{:S(2)}) collective-permute-start(bf16[128,128]{1,0:T(8,128)(2,1)S(1)} %get-tuple-element.30), channel_id=1, source_target_pairs={{0,1},{2,3},{1,0},{3,2},{4,5},{6,7},{5,4},{7,6},{8,9},{10,11},{9,8... | collective-permute-start | bytes 98312 | tf_op jit(solution)/shard_map/ppermute | solution.py:427
  41.0 1.6 %copy-start.2 = (bf16[128,8,8,128]{3,2,1,0:T(8,128)(2,1)S(1)}, bf16[128,8,8,128]{3,2,1,0:T(8,128)(2,1)}, u32[]{:S(2)}) copy-start(bf16[128,8,8,128]{3,2,1,0:T(8,128)(2,1)} %param.7) | copy-start | bytes 6291460
  51.8 9.7 %collective-permute-start.8 = (bf16[1024,128]{1,0:T(8,128)(2,1)S(1)}, bf16[1024,128]{1,0:T(8,128)(2,1)S(1)}, u32[]{:S(2)}, u32[]{:S(2)}) collective-permute-start(bf16[1024,128]{1,0:T(8,128)(2,1)S(1)} %get-tuple-element.34), channel_id=1, source_target_pairs={{0,8},{16,24},{8,0},{24,16},{1,9},{17,25},{9,1},{25,17},{2,10},{18... | collective-permute-start | bytes 786440 | tf_op jit(solution)/shard_map/ppermute | solution.py:426
  53.0 8.5 %collective-permute-start.9 = (bf16[1024,128]{1,0:T(8,128)(2,1)S(1)}, bf16[1024,128]{1,0:T(8,128)(2,1)S(1)}, u32[]{:S(2)}, u32[]{:S(2)}) collective-permute-start(bf16[1024,128]{1,0:T(8,128)(2,1)S(1)} %get-tuple-element.35), channel_id=1, source_target_pairs={{8,16},{16,8},{9,17},{17,9},{10,18},{18,10},{11,19},{19,11},{12,20... | collective-permute-start | bytes 786440 | tf_op jit(solution)/shard_map/ppermute | solution.py:426
  53.7 7.8 %collective-permute-start.10 = (bf16[1024,128]{1,0:T(8,128)(2,1)S(1)}, bf16[1024,128]{1,0:T(8,128)(2,1)S(1)}, u32[]{:S(2)}, u32[]{:S(2)}) collective-permute-start(bf16[1024,128]{1,0:T(8,128)(2,1)S(1)} %get-tuple-element.36), channel_id=1, source_target_pairs={{0,4},{4,0},{1,5},{5,1},{2,6},{6,2},{3,7},{7,3},{8,12},{12,8},{9,1... | collective-permute-start | bytes 786440 | tf_op jit(solution)/shard_map/ppermute | solution.py:426
  55.2 4.4 %collective-permute-start.12 = (bf16[128,128]{1,0:T(8,128)(2,1)S(1)}, bf16[128,128]{1,0:T(8,128)(2,1)S(1)}, u32[]{:S(2)}, u32[]{:S(2)}) collective-permute-start(bf16[128,128]{1,0:T(8,128)(2,1)S(1)} %get-tuple-element.37), channel_id=1, source_target_pairs={{1,2},{2,1},{5,6},{6,5},{9,10},{10,9},{13,14},{14,13},{17,18},{18,... | collective-permute-start | bytes 98312 | tf_op jit(solution)/shard_map/ppermute | solution.py:427
  55.9 5.6 %collective-permute-start.11 = (bf16[128,128]{1,0:T(8,128)(2,1)S(1)}, bf16[128,128]{1,0:T(8,128)(2,1)S(1)}, u32[]{:S(2)}, u32[]{:S(2)}) collective-permute-start(bf16[128,128]{1,0:T(8,128)(2,1)S(1)} %get-tuple-element.37), channel_id=1, source_target_pairs={{0,1},{2,3},{1,0},{3,2},{4,5},{6,7},{5,4},{7,6},{8,9},{10,11},{9,8... | collective-permute-start | bytes 98312 | tf_op jit(solution)/shard_map/ppermute | solution.py:427
  69.2 9.8 %collective-permute-start.13 = (bf16[1024,128]{1,0:T(8,128)(2,1)S(1)}, bf16[1024,128]{1,0:T(8,128)(2,1)S(1)}, u32[]{:S(2)}, u32[]{:S(2)}) collective-permute-start(bf16[1024,128]{1,0:T(8,128)(2,1)S(1)} %get-tuple-element.39), channel_id=1, source_target_pairs={{0,8},{16,24},{8,0},{24,16},{1,9},{17,25},{9,1},{25,17},{2,10},{18... | collective-permute-start | bytes 786440 | tf_op jit(solution)/shard_map/ppermute | solution.py:426
  70.5 8.4 %collective-permute-start.14 = (bf16[1024,128]{1,0:T(8,128)(2,1)S(1)}, bf16[1024,128]{1,0:T(8,128)(2,1)S(1)}, u32[]{:S(2)}, u32[]{:S(2)}) collective-permute-start(bf16[1024,128]{1,0:T(8,128)(2,1)S(1)} %get-tuple-element.40), channel_id=1, source_target_pairs={{8,16},{16,8},{9,17},{17,9},{10,18},{18,10},{11,19},{19,11},{12,20... | collective-permute-start | bytes 786440 | tf_op jit(solution)/shard_map/ppermute | solution.py:426
  71.2 7.8 %collective-permute-start.15 = (bf16[1024,128]{1,0:T(8,128)(2,1)S(1)}, bf16[1024,128]{1,0:T(8,128)(2,1)S(1)}, u32[]{:S(2)}, u32[]{:S(2)}) collective-permute-start(bf16[1024,128]{1,0:T(8,128)(2,1)S(1)} %get-tuple-element.41), channel_id=1, source_target_pairs={{0,4},{4,0},{1,5},{5,1},{2,6},{6,2},{3,7},{7,3},{8,12},{12,8},{9,1... | collective-permute-start | bytes 786440 | tf_op jit(solution)/shard_map/ppermute | solution.py:426
  72.6 4.4 %collective-permute-start.17 = (bf16[128,128]{1,0:T(8,128)(2,1)S(1)}, bf16[128,128]{1,0:T(8,128)(2,1)S(1)}, u32[]{:S(2)}, u32[]{:S(2)}) collective-permute-start(bf16[128,128]{1,0:T(8,128)(2,1)S(1)} %get-tuple-element.42), channel_id=1, source_target_pairs={{1,2},{2,1},{5,6},{6,5},{9,10},{10,9},{13,14},{14,13},{17,18},{18,... | collective-permute-start | bytes 98312 | tf_op jit(solution)/shard_map/ppermute | solution.py:427
  73.3 5.7 %collective-permute-start.16 = (bf16[128,128]{1,0:T(8,128)(2,1)S(1)}, bf16[128,128]{1,0:T(8,128)(2,1)S(1)}, u32[]{:S(2)}, u32[]{:S(2)}) collective-permute-start(bf16[128,128]{1,0:T(8,128)(2,1)S(1)} %get-tuple-element.42), channel_id=1, source_target_pairs={{0,1},{2,3},{1,0},{3,2},{4,5},{6,7},{5,4},{7,6},{8,9},{10,11},{9,8... | collective-permute-start | bytes 98312 | tf_op jit(solution)/shard_map/ppermute | solution.py:427

commit v3 on v2

--- a/solution.py
+++ b/solution.py
@@ -23,6 +23,9 @@
 
 def dot_nt(a, b):
     return lax.dot_general(a, b, (((1,), (1,)), ((), ())), preferred_element_type=F32)
+
+
+FACES_MIB = 50
 
 
 def params(mebibytes=24):
@@ -66,7 +69,7 @@
             spread = jnp.where(own, spread, 0.0).astype(BF)
             parts.append(dot(rsum[...], spread).astype(BF))
         picked.append(jnp.concatenate(parts, axis=1))
-    out_ref[...] = dot(jnp.concatenate(picked, axis=0), perm[...]).astype(BF)
+    out_ref[...] = dot(jnp.concatenate(picked, axis=0), perm[...]).T.astype(BF)
 
 
 def traces(field, trace_cell, block):
@@ -78,7 +81,7 @@
         functools.partial(trace_kernel, stride, block),
         in_specs=[hbm, hbm],
         out_specs=WHOLE,
-        out_shape=jax.ShapeDtypeStruct((sides, slots), BF),
+        out_shape=jax.ShapeDtypeStruct((slots, sides), BF),
         scratch_shapes=[
             pltpu.VMEM(field.shape, BF),
             pltpu.VMEM(trace_cell.shape, jnp.int32),
@@ -94,74 +97,81 @@
     )(field, trace_cell)
 
 
-def surface_kernel(row, gz, peers, gzs, cols, *refs):
-    parts = refs[:peers]
-    block_ref, out_ref, held, sems = refs[peers:]
-    sides, slots = parts[0].shape
-    me, group = lax.axis_index(row), lax.axis_index(gz)
+def fetch_columns(block_ref, held, sems, slots):
+    me, group, gzs = lax.axis_index("row"), lax.axis_index("gz"), lax.axis_size("gz")
     copies = []
-    for key in range(peers):
+    for key in range(held.shape[0]):
         start = pl.multiple_of((jnp.bitwise_xor(me, key) * gzs + group) * slots, slots)
         copies.append(
             pltpu.make_async_copy(block_ref.at[:, pl.ds(start, slots)], held.at[key], sems.at[key])
         )
         copies[-1].start()
+    return copies
+
+
+def surface_kernel(gzs, cols, *refs):
+    *parts, held, out_ref = refs
+    sides = parts[0].shape[1]
     total = None
-    for key in range(peers):
-        copies[key].wait()
-        term = dot_nt(parts[key][...], held[key])
+    for key, part in enumerate(parts):
+        term = dot(held[key], part[...])
         total = term if total is None else total + term
     turned = total.T
-    lines = total.shape[1]
-    out_ref[...] = jnp.zeros_like(out_ref)
+    lines = total.shape[0]
+    if out_ref.shape[2] != sides or lines // cols != sides:
+        out_ref[...] = jnp.zeros_like(out_ref)
     s_count, l_count, f_count = sides // gzs, lines // cols, lines // (cols * gzs)
     for c in range(cols):
         for g in range(gzs):
             dest = c * gzs + g
-            out_ref[dest, :s_count, :l_count] = total[
+            out_ref[dest, :s_count, :l_count] = turned[
                 g * s_count : (g + 1) * s_count, c * l_count : (c + 1) * l_count
             ].astype(out_ref.dtype)
-            out_ref[dest, s_count : s_count + f_count, :sides] = turned[
+            out_ref[dest, s_count : s_count + f_count, :sides] = total[
                 dest * f_count : (dest + 1) * f_count
             ].astype(out_ref.dtype)
 
 
-def surface(parts, block, dtype):
-    peers, gzs, cols = lax.axis_size("row"), lax.axis_size("gz"), lax.axis_size("col")
-    sides, slots = parts[0].shape
-    lines = block.shape[0]
+def surface(parts, held, dtype):
+    gzs, cols = lax.axis_size("gz"), lax.axis_size("col")
+    sides = parts[0].shape[1]
+    lines = held.shape[1]
     depth = sides // gzs + lines // (cols * gzs)
     shape = (cols * gzs, depth, max(sides, lines // cols))
     return pl.pallas_call(
-        functools.partial(surface_kernel, "row", "gz", peers, gzs, cols),
-        in_specs=[WHOLE] * peers + [pl.BlockSpec(memory_space=pltpu.HBM)],
+        functools.partial(surface_kernel, gzs, cols),
+        in_specs=[WHOLE] * (len(parts) + 1),
         out_specs=WHOLE,
         out_shape=jax.ShapeDtypeStruct(shape, dtype),
-        scratch_shapes=[
-            pltpu.VMEM((peers, lines, slots), BF),
-            pltpu.SemaphoreType.DMA((peers,)),
-        ],
-        compiler_params=params(58),
+        compiler_params=params(),
         cost_estimate=pl.CostEstimate(
-            flops=2 * sides * lines * slots * peers,
-            bytes_accessed=2 * lines * slots * peers,
-            transcendentals=0,
+            flops=2 * sides * held.size, bytes_accessed=2 * held.size, transcendentals=0
         ),
-    )(*parts, block)
+    )(*parts, held)
 
 
 def swaps(peers):
-    pairs = [[(i, i + 1) for i in range(first, peers - 1, 2)] for first in (0, 1)]
-    return [[(i, j) for i, j in part] + [(j, i) for i, j in part] for part in pairs if part]
+    turns = [[(i, i + 1) for i in range(first, peers - 1, 2)] for first in (0, 1)]
+    if turns[1] and peers % 2 == 0:
+        turns[1].append((peers - 1, 0))
+    return [[(i, j) for i, j in part] + [(j, i) for i, j in part] for part in turns if part]
+
+
+def has_neighbour(axis, turn):
+    index = lax.axis_index(axis)
+    other = jnp.where(index % 2 == turn, index + 1, index - 1)
+    return (other >= 0) & (other < lax.axis_size(axis))
 
 
 class Shape:
     def __init__(self, sides, first, second, lanes):
         self.sides, self.x, self.y, self.lanes = sides, first, second, lanes
         self.cells = first * second
-        self.chunk = max(1, 256 // self.cells)
+        self.chunk = max(1, 128 // self.cells)
         self.rows = self.chunk * self.cells
         self.block = min(sides, 16)
+        self.half = self.block // 2
+        self.half_rows = self.half * self.cells
         self.faces = [("row", i) for i in range(len(swaps(lax.axis_size("row"))))]
         self.faces += [("col", i) for i in range(len(swaps(lax.axis_size("col"))))]
         self.ends = len(swaps(lax.axis_size("gz")))
@@ -188,6 +198,7 @@
         length = shape.face_len(face)
         along, across = (y, x) if face[0] == "row" else (x, y)
         place = (across == shape.edge(face)) & (col - base == side * length + along)
+        place = place & has_neighbour(*face)
         hit = place if hit is None else hit | place
         base += shape.chunk * length
     return hit.astype(BF)
@@ -198,11 +209,23 @@
     return iota(dims, 1) % shape.cells == iota(dims, 0) % shape.cells
 
 
+def twice(matrix):
+    zero = jnp.zeros_like(matrix)
+    return jnp.concatenate(
+        [jnp.concatenate([matrix, zero], axis=1), jnp.concatenate([zero, matrix], axis=1)], axis=0
+    )
+
+
+def beside(values):
+    half = values.shape[0] // 2
+    return jnp.concatenate([values[:half], values[half:]], axis=1)
+
+
 def build_out(shape, ends_m, rsum):
     dims = (shape.lanes, 2 * shape.cells)
     edge = jnp.where(iota(dims, 1) < shape.cells, 0, shape.lanes - 1)
-    ends_m[...] = (iota(dims, 0) == edge).astype(BF)
-    dims = (shape.block, shape.block * shape.cells)
+    ends_m[...] = twice((iota(dims, 0) == edge).astype(F32)).astype(BF)
+    dims = rsum.shape
     rsum[...] = (iota(dims, 1) // shape.cells == iota(dims, 0)).astype(BF)
 
 
@@ -220,12 +243,16 @@
         ref[pl.ds(pl.multiple_of(at * length, span), span), :] = jnp.concatenate(
             lines, axis=0
         ).astype(BF)
-    tips = jnp.where(z_mask(shape, shape.block), dot(values, ends_m[...]), 0.0).astype(BF)
-    z_ref[pl.ds(pl.multiple_of(at, shape.block), shape.block), :] = dot(rsum[...], tips).astype(BF)
-
-
-def faces_kernel(shape, field_ref, *refs):
-    *face_refs, z_ref, tall, ends_m, rsum = refs
+    mask = jnp.concatenate([z_mask(shape, shape.half)] * 2, axis=1)
+    tips = jnp.where(mask, dot(beside(values), ends_m[...]), 0.0).astype(BF)
+    tips = dot(rsum[...], tips)[: shape.half]
+    tips = jnp.concatenate([tips[:, : 2 * shape.cells], tips[:, 2 * shape.cells :]], axis=0)
+    z_ref[pl.ds(pl.multiple_of(at, shape.block), shape.block), :] = tips.astype(BF)
+
+
+def faces_kernel(shape, slots, field_ref, block_ref, *refs):
+    *face_refs, z_ref, held, tall, ends_m, rsum, sems = refs
+    copies = fetch_columns(block_ref, held, sems, slots)
     build_out(shape, ends_m, rsum)
 
     @pl.loop(0, shape.sides // shape.block)
@@ -235,6 +262,9 @@
         tall[...] = values.astype(F32)
         emit_faces(shape, step * shape.block, values, tall, face_refs, z_ref, ends_m, rsum)
 
+    for copy in copies:
+        copy.wait()
+
 
 def face_outputs(shape):
     shapes = [
@@ -247,24 +277,26 @@
 def face_scratch(shape):
     return [
         pltpu.VMEM((shape.block * shape.cells, shape.lanes), F32),
-        pltpu.VMEM((shape.lanes, 2 * shape.cells), BF),
-        pltpu.VMEM((shape.block, shape.block * shape.cells), BF),
+        pltpu.VMEM((2 * shape.lanes, 4 * shape.cells), BF),
+        pltpu.VMEM((max(8, shape.half), shape.half_rows), BF),
     ]
 
 
-def first_faces(shape, field):
+def first_faces(shape, field, block, slots):
+    peers = lax.axis_size("row")
     shapes = face_outputs(shape)
+    shapes.append(jax.ShapeDtypeStruct((peers, block.shape[0], slots), BF))
     return pl.pallas_call(
-        functools.partial(faces_kernel, shape),
-        in_specs=[WHOLE],
+        functools.partial(faces_kernel, shape, slots),
+        in_specs=[WHOLE, pl.BlockSpec(memory_space=pltpu.HBM)],
         out_specs=[WHOLE] * len(shapes),
         out_shape=shapes,
-        scratch_shapes=face_scratch(shape),
-        compiler_params=params(),
+        scratch_shapes=face_scratch(shape) + [pltpu.SemaphoreType.DMA((peers,))],
+        compiler_params=params(FACES_MIB),
         cost_estimate=pl.CostEstimate(
             flops=field.size * 128, bytes_accessed=4 * field.size, transcendentals=0
         ),
-    )(field)
+    )(field, block)
 
 
 def sweep_kernel(shape, with_flux, last, *refs):
@@ -281,11 +313,11 @@
         (z_ref,) = take(1)
     if with_flux:
         source_ref, flux_ref = take(2)
-    weight, near_m, line_m = take(3)
+    weight, near_m, line_m, lines = take(4)
     if not last:
         tall, ends_m, rsum = take(3)
     if with_flux:
-        phi, cell_m = take(2)
+        phi, cell_m, placed = take(3)
 
     grid_step = pl.program_id(0)
     cells, lanes = shape.cells, shape.lanes
@@ -301,10 +333,11 @@
         near_m[:, : shape.rows] = (near & (row // cells == col // cells)).astype(BF)
         near_m[:, shape.rows :] = halo_place(shape)
         dims = (lanes, lanes)
-        line_m[:lanes, :] = (jnp.abs(iota(dims, 0) - iota(dims, 1)) == 1).astype(BF)
+        line = (jnp.abs(iota(dims, 0) - iota(dims, 1)) == 1).astype(F32)
+        line_m[: 2 * lanes, :] = twice(line).astype(BF)
         dims = (2 * cells, lanes)
         edge = jnp.where(iota(dims, 0) < cells, lanes - 1, 0)
-        line_m[lanes:, :] = (iota(dims, 1) == edge).astype(BF)
+        line_m[2 * lanes :, :] = twice((iota(dims, 1) == edge).astype(F32)).astype(BF)
         if not last:
             build_out(shape, ends_m, rsum)
         if with_flux:
@@ -319,11 +352,11 @@
             both = jnp.concatenate([high, owned - high], axis=0)
             phi[...] = both.T
             cell = jnp.concatenate([cell_ref[0, 0]] * 2, axis=1)
-            cell_m[...] = (iota((lanes, 2 * slots), 0) == cell % lanes).astype(BF)
+            cell_m[...] = twice((iota((lanes, 2 * slots), 0) == cell % lanes).astype(F32)).astype(BF)
 
     mask = z_mask(shape, 1)
     even = lax.axis_index("gz") % 2 == 0
-    first_swap = (iota((shape.block, 2 * cells), 1) < cells) == even
+    filled = (iota((shape.block, 2 * cells), 1) < cells) == even
     if with_flux:
         slots = cell_ref.shape[3]
         cell = jnp.concatenate([cell_ref[0, 0]] * 2, axis=1)
@@ -331,51 +364,61 @@
     weights = jnp.concatenate([weight[...]] * shape.chunk, axis=0)
     out_sides = out_ref.shape[0] // cells
 
+    def expand(lines, where, first):
+        rows = []
+        for side in range(first, first + shape.half):
+            line = jnp.broadcast_to(lines[side : side + 1], where.shape)
+            rows.append(jnp.where(where, line, 0.0))
+        return jnp.concatenate(rows, axis=0).astype(BF)
+
     @pl.loop(0, out_sides // shape.block)
     def _(step):
         local = step * shape.block
         at = grid_step * out_sides + local
         sides = pl.ds(pl.multiple_of(at, shape.block), shape.block)
-        zs = end_refs[0][sides, :].astype(F32)
-        other = end_refs[1][sides, :].astype(F32) if shape.ends > 1 else 0.0
-        zs = jnp.where(first_swap, zs, other)
+        size = shape.block * cells
+        zs = 0.0
+        for turn in range(shape.ends):
+            wanted = (filled == (turn == 0)) & has_neighbour("gz", turn)
+            zs = jnp.where(wanted, end_refs[turn][sides, :].astype(F32), zs)
+        values = field_ref[pl.ds(pl.multiple_of(at * cells, size), size), :]
+        left = [beside(values), expand(zs, mask, 0), expand(zs, mask, shape.half)]
+        lines[...] = dot(jnp.concatenate(left, axis=1), line_m[...])
         if with_flux:
             phis = phi[sides, :]
-        for index in range(shape.block // shape.chunk):
+            left = [expand(phis, cell_mask, 0), expand(phis, cell_mask, shape.half)]
+            placed[...] = dot_nt(jnp.concatenate(left, axis=1), cell_m[...])
+        for index in range(shape.half // shape.chunk):
             offset = index * shape.rows
-            span = pl.ds(pl.multiple_of(at * cells + offset, shape.rows), shape.rows)
-            values = field_ref[span, :]
-            stack = [values]
-            for face, ref in zip(shape.faces, halo_refs):
-                length = shape.face_len(face)
-                size = shape.chunk * length
-                start = pl.multiple_of(at * length + index * size, size)
-                stack.append(ref[pl.ds(start, size), :])
-            spread = []
-            for side in range(index * shape.chunk, (index + 1) * shape.chunk):
-                line = jnp.broadcast_to(zs[side : side + 1], mask.shape)
-                spread.append(jnp.where(mask, line, 0.0))
-            spread = jnp.concatenate(spread, axis=0).astype(BF)
-            near = dot(near_m[...], jnp.concatenate(stack, axis=0))
-            near = near + dot(jnp.concatenate([values, spread], axis=1), line_m[...])
-            source = load_ref[span, :].astype(F32)
-            if with_flux:
-                spread = []
-                for side in range(index * shape.chunk, (index + 1) * shape.chunk):
-                    line = jnp.broadcast_to(phis[side : side + 1], cell_mask.shape)
-                    spread.append(jnp.where(cell_mask, line, 0.0))
-                spread = jnp.concatenate(spread, axis=0).astype(BF)
-                source = source + dot_nt(spread, cell_m[...])
-                source_ref[span, :] = source.astype(BF)
-            fresh = (1.0 - OMEGA) * values.astype(F32) + weights * (source + near)
-            out_span = pl.ds(pl.multiple_of(local * cells + offset, shape.rows), shape.rows)
-            out_ref[out_span, :] = fresh.astype(BF)
-            if not last:
-                tall[offset : offset + shape.rows, :] = fresh
+            starts = (offset, offset + shape.half_rows)
+            stacks = []
+            for start in starts:
+                rows = pl.ds(pl.multiple_of(at * cells + start, shape.rows), shape.rows)
+                stack = [field_ref[rows, :]]
+                for face, ref in zip(shape.faces, halo_refs):
+                    length = shape.face_len(face)
+                    count = shape.chunk * length
+                    first = pl.multiple_of(at * length + start // cells * length, count)
+                    stack.append(ref[pl.ds(first, count), :])
+                stacks.append(jnp.concatenate(stack, axis=0))
+            near = dot(near_m[...], jnp.concatenate(stacks, axis=1))
+            near = near + lines[offset : offset + shape.rows, :]
+            for part, start in enumerate(starts):
+                cols = slice(part * lanes, (part + 1) * lanes)
+                rows = pl.ds(pl.multiple_of(at * cells + start, shape.rows), shape.rows)
+                source = load_ref[rows, :].astype(F32)
+                if with_flux:
+                    source = source + placed[offset : offset + shape.rows, cols]
+                    source_ref[rows, :] = source.astype(BF)
+                centre = field_ref[rows, :].astype(F32)
+                fresh = (1.0 - OMEGA) * centre + weights * (source + near[:, cols])
+                to = pl.ds(pl.multiple_of(local * cells + start, shape.rows), shape.rows)
+                out_ref[to, :] = fresh.astype(BF)
+                if not last:
+                    tall[start : start + shape.rows, :] = fresh
         if not last:
-            size = shape.block * cells
-            values = out_ref[pl.ds(pl.multiple_of(local * cells, size), size), :]
-            emit_faces(shape, at, values, tall, face_refs, z_ref, ends_m, rsum)
+            fresh = out_ref[pl.ds(pl.multiple_of(local * cells, size), size), :]
+            emit_faces(shape, at, fresh, tall, face_refs, z_ref, ends_m, rsum)
 
 
 def sweep(shape, field, load, coef, halos, recv=None, flux_cell=None, last=False):
@@ -386,7 +429,8 @@
     scratch = [
         pltpu.VMEM(coef.shape, F32),
         pltpu.VMEM((shape.rows, shape.rows + shape.halo_rows()), BF),
-        pltpu.VMEM((lanes + 2 * cells, lanes), BF),
+        pltpu.VMEM((2 * lanes + 4 * cells, 2 * lanes), BF),
+        pltpu.VMEM((shape.half_rows, 2 * lanes), F32),
     ]
     if not last:
         out_shapes += face_outputs(shape)
@@ -399,7 +443,11 @@
             jax.ShapeDtypeStruct(field.shape, BF),
             jax.ShapeDtypeStruct((shape.sides // gzs, slots * gzs), F32),
         ]
-        scratch += [pltpu.VMEM((shape.sides, 2 * slots), F32), pltpu.VMEM((lanes, 2 * slots), BF)]
+        scratch += [
+            pltpu.VMEM((shape.sides, 2 * slots), F32),
+            pltpu.VMEM((2 * lanes, 4 * slots), BF),
+            pltpu.VMEM((shape.half_rows, 2 * lanes), F32),
+        ]
     steps = max(1, shape.sides // (2 * shape.block)) if last else 1
     out_specs = [WHOLE] * len(out_shapes)
     if last:
@@ -450,10 +498,13 @@
     load = volume_load.reshape(sides * cells, lanes)
     coef = coefficient.reshape(cells, lanes)
 
+    slots = trace_cell.shape[3]
     trace = traces(volume_field.reshape(sides, cells, lanes), trace_cell, min(32, sides))
-    parts, faces = xor_gather(trace, "row", first_faces(shape, field))
+    *faces, held = first_faces(shape, field, surface_block, slots)
+    parts, _ = xor_gather(trace, "row", faces)
     halos = exchange(shape, faces)
-    sent = surface(parts, surface_block, F32)
+    parts, halos = lax.optimization_barrier((parts, halos))
+    sent = surface(parts, held, F32)
     recv = lax.all_to_all(sent, ("col", "gz"), split_axis=0, concat_axis=0, tiled=True)
 
     current, *faces, source, surface_flux = sweep(

time: 85.7 us -> 82.2 us (0.959); the launches traced: 84.1 us -> 82 us
  starting transfers between devices: 32.4 us -> 14.3 us
  blocking collectives: 0 us -> 14 us
  waiting for transfers between devices: 9.37 us -> 20.5 us
  Pallas kernels: 37.6 us -> 32.4 us
  local copies, waits for them, and re-layouts: 3.91 us -> 0.03 us
    all_to_all x0 -> x1, blocking collectives: none -> 14 us  [per_device(): lax.all_to_all(sent, ('col', 'gz'), split_axis=0, concat_axis=0, tiled=True)]
    ppermute x9, waiting for transfers between devices: 0.95 us -> 9.37 us  [exchange(): halos[face] = lax.ppermute(value, face[0], pairs)]
    ppermute x6, starting transfers between devices: 13.7 us -> 5.64 us  [exchange(): lax.ppermute(ends, 'gz', pairs)]
    all_to_all x1 -> x0, starting transfers between devices: 6.1 us -> none  [per_device(): lax.all_to_all(sent, ('col', 'gz'), split_axis=0, concat_axis=0, tiled=True)]
    ppermute x6, waiting for transfers between devices: 5.68 us -> 11.1 us  [exchange(): lax.ppermute(ends, 'gz', pairs)]
    ppermute x9, starting transfers between devices: 9.54 us -> 5.62 us  [exchange(): halos[face] = lax.ppermute(value, face[0], pairs)]
    unnamed x16 -> x10, local copies, waits for them, and re-layouts: 3.91 us -> 0.03 us
    ppermute x3, waiting for transfers between devices: 2.74 us -> 0.01 us  [xor_gather(): lax.ppermute(held[key], axis, swap)]
  transfers between devices with their start and end apart: 19 -> 18, of which waited for: 6 -> 10; matrix products, arithmetic and copies ran while one was open for 0% -> 0% of each run, Pallas kernels for 4% -> 6%
where the time goes in v3:
time: 82.2 us; the launch traced here: 82 us
  Pallas kernels  32.4 us (39%)
  waiting for transfers between devices  20.5 us (25%)
  starting transfers between devices  14.3 us (17%)
  blocking collectives  14 us (17%)
    pallas_call x3, Pallas kernels, sweep(): pl.pallas_call(functools.partial(sweep_kernel, shape, with_flux, last), g...  19.3 us
    all_to_all x1, blocking collectives, per_device(): lax.all_to_all(sent, ('col', 'gz'), split_axis=0, concat_axis=0, tiled=True)  14 us
    ppermute x6, waiting for transfers between devices, exchange(): lax.ppermute(ends, 'gz', pairs)  11.1 us
    ppermute x9, waiting for transfers between devices, exchange(): halos[face] = lax.ppermute(value, face[0], pairs)  9.37 us
    pallas_call x1, Pallas kernels, traces(): pl.pallas_call(functools.partial(trace_kernel, stride, block), in_specs=[...  7.31 us
    ppermute x6, starting transfers between devices, exchange(): lax.ppermute(ends, 'gz', pairs)  5.64 us
    ppermute x9, starting transfers between devices, exchange(): halos[face] = lax.ppermute(value, face[0], pairs)  5.62 us
    pallas_call x1, Pallas kernels, first_faces(): pl.pallas_call(functools.partial(faces_kernel, shape, slots), in_specs=[W...  5.06 us
  transfers between devices with their start and end apart: 18, of which 10 were waited for; matrix products, arithmetic and copies ran while one was open for 0% of the time, Pallas kernels for 6%

profile of v3, /device:TPU:0, one launch (start us, length us, event | category | flops | bytes accessed | tf_op | source)
XLA Modules:
  0.0 82.0 jit_solution(11227842760219097984)
XLA Ops:
  0.6 7.3 %shard_map.77.refs_0_ = bf16[1024,128]{1,0:T(8,128)(2,1)} custom-call(bf16[128,64,128]{2,1,0:T(8,128)(2,1)} %bitcast.5, s32[1,1,1,1024]{3,2,1,0:T(1,128)} %cell_ref.1), custom_call_target="tpu_custom_call" | custom-call | flops 536870912 | bytes 2097152 | tf_op jit(solution)/shard_map/pallas_call | solution.py:80
  8.0 3.0 %collective-permute-start.1 = (bf16[1024,128]{1,0:T(8,128)(2,1)}, bf16[1024,128]{1,0:T(8,128)(2,1)S(1)}, u32[]{:S(2)}, u32[]{:S(2)}) collective-permute-start(bf16[1024,128]{1,0:T(8,128)(2,1)} %shard_map.77.refs_0_), channel_id=1, source_target_pairs={{0,16},{8,24},{16,0},{24,8},{1,17},{9,25},{17,1},{25,9},{2,18},{10... | collective-permute-start | bytes 786440 | tf_op jit(solution)/shard_map/ppermute | solution.py:485
  11.0 5.1 %shard_map.78 = (bf16[1024,128]{1,0:T(8,128)(2,1)S(1)}, bf16[1024,128]{1,0:T(8,128)(2,1)S(1)}, bf16[1024,128]{1,0:T(8,128)(2,1)S(1)}, bf16[128,128]{1,0:T(8,128)(2,1)S(1)}, bf16[4,256,1024]{2,1,0:T(8,128)(2,1)S(1)}) custom-call(bf16[8192,128]{1,0:T(8,128)(2,1)} %bitcast.6, bf16[256,16384]{1,0:T(8,128)(2,1)} %block_ref.1), custom_call_target="tpu_custom_call" | custom-call | flops 134217728 | bytes 4194304 | tf_op jit(solution)/shard_map/pallas_call | solution.py:289
  16.0 0.0 copy-start
  16.0 0.0 copy-start.3
  16.0 0.0 copy-start.4
  16.1 3.7 %collective-permute-start.7 = (bf16[128,128]{1,0:T(8,128)(2,1)S(1)}, bf16[128,128]{1,0:T(8,128)(2,1)S(1)}, u32[]{:S(2)}, u32[]{:S(2)}) collective-permute-start(bf16[128,128]{1,0:T(8,128)(2,1)S(1)} %get-tuple-element.32), channel_id=1, source_target_pairs={{1,2},{3,0},{2,1},{0,3},{5,6},{7,4},{6,5},{4,7},{9,10},{11,8},{10,... | collective-permute-start | bytes 98312 | tf_op jit(solution)/shard_map/ppermute | solution.py:475
  19.7 0.5 collective-permute-start.3
  20.2 0.2 collective-permute-start.4
  20.5 1.4 %collective-permute-done.7.refs_7_ = bf16[128,128]{1,0:T(8,128)(2,1)S(1)} collective-permute-done((bf16[128,128]{1,0:T(8,128)(2,1)S(1)}, bf16[128,128]{1,0:T(8,128)(2,1)S(1)}, u32[]{:S(2)}, u32[]{:S(2)}) %collective-permute-start.7) | collective-permute-done | bytes 32800 | tf_op jit(solution)/shard_map/ppermute | solution.py:475
  21.9 1.5 %collective-permute-start.5 = (bf16[1024,128]{1,0:T(8,128)(2,1)S(1)}, bf16[1024,128]{1,0:T(8,128)(2,1)S(1)}, u32[]{:S(2)}, u32[]{:S(2)}) collective-permute-start(bf16[1024,128]{1,0:T(8,128)(2,1)S(1)} %get-tuple-element.31), channel_id=1, source_target_pairs={{0,4},{4,0},{1,5},{5,1},{2,6},{6,2},{3,7},{7,3},{8,12},{12,8},{9,1... | collective-permute-start | bytes 786440 | tf_op jit(solution)/shard_map/ppermute | solution.py:474
  23.4 0.3 collective-permute-done.6.refs_6_
  23.7 4.9 %collective-permute-done.4.refs_4_ = bf16[1024,128]{1,0:T(8,128)(2,1)S(1)} collective-permute-done((bf16[1024,128]{1,0:T(8,128)(2,1)S(1)}, bf16[1024,128]{1,0:T(8,128)(2,1)S(1)}, u32[]{:S(2)}, u32[]{:S(2)}) %collective-permute-start.4) | collective-permute-done | bytes 262176 | tf_op jit(solution)/shard_map/ppermute | solution.py:474
  28.6 0.5 collective-permute-done.5.refs_5_
  29.1 0.8 shard_map.79
  29.9 14.0 %all_to_all.5.refs_8_ = f32[8,64,128]{2,1,0:T(8,128)S(1)} all-to-all(f32[8,64,128]{2,1,0:T(8,128)S(1)} %shard_map.79), channel_id=1, replica_groups=mesh['row'=4,'col'=2,'gz'=4] {'col','gz'}, dimensions={0} | all-to-all | bytes 524288 | tf_op jit(solution)/shard_map/all_to_all | solution.py:508
  43.9 8.0 %shard_map.80 = (bf16[8192,128]{1,0:T(8,128)(2,1)S(1)}, bf16[1024,128]{1,0:T(8,128)(2,1)S(1)}, bf16[1024,128]{1,0:T(8,128)(2,1)S(1)}, bf16[1024,128]{1,0:T(8,128...) custom-call(bf16[8192,128]{1,0:T(8,128)(2,1)S(1)} %bitcast.7, ...), custom_call_target="tpu_custom_call" | custom-call | flops 805306368 | bytes 8388608 | tf_op jit(solution)/shard_map/pallas_call | solution.py:455
  51.9 1.4 %collective-permute-start.9 = (bf16[1024,128]{1,0:T(8,128)(2,1)S(1)}, bf16[1024,128]{1,0:T(8,128)(2,1)S(1)}, u32[]{:S(2)}, u32[]{:S(2)}) collective-permute-start(bf16[1024,128]{1,0:T(8,128)(2,1)S(1)} %get-tuple-element.47), channel_id=1, source_target_pairs={{8,16},{24,0},{16,8},{0,24},{9,17},{25,1},{17,9},{1,25},{10,18},{2... | collective-permute-start | bytes 786440 | tf_op jit(solution)/shard_map/ppermute | solution.py:474
  53.3 0.6 collective-permute-start.10
  53.9 0.1 collective-permute-start.12
  54.0 0.9 %collective-permute-start.11 = (bf16[128,128]{1,0:T(8,128)(2,1)S(1)}, bf16[128,128]{1,0:T(8,128)(2,1)S(1)}, u32[]{:S(2)}, u32[]{:S(2)}) collective-permute-start(bf16[128,128]{1,0:T(8,128)(2,1)S(1)} %get-tuple-element.49), channel_id=1, source_target_pairs={{0,1},{2,3},{1,0},{3,2},{4,5},{6,7},{5,4},{7,6},{8,9},{10,11},{9,8... | collective-permute-start | bytes 98312 | tf_op jit(solution)/shard_map/ppermute | solution.py:475
  54.9 4.7 %collective-permute-done.12.refs_7_ = bf16[128,128]{1,0:T(8,128)(2,1)S(1)} collective-permute-done((bf16[128,128]{1,0:T(8,128)(2,1)S(1)}, bf16[128,128]{1,0:T(8,128)(2,1)S(1)}, u32[]{:S(2)}, u32[]{:S(2)}) %collective-permute-start.12) | collective-permute-done | bytes 32800 | tf_op jit(solution)/shard_map/ppermute | solution.py:475
  59.6 0.2 collective-permute-done.9.refs_4_
  59.9 1.7 %collective-permute-done.10.refs_5_ = bf16[1024,128]{1,0:T(8,128)(2,1)S(1)} collective-permute-done((bf16[1024,128]{1,0:T(8,128)(2,1)S(1)}, bf16[1024,128]{1,0:T(8,128)(2,1)S(1)}, u32[]{:S(2)}, u32[]{:S(2)}) %collective-permute-start.10) | collective-permute-done | bytes 262176 | tf_op jit(solution)/shard_map/ppermute | solution.py:474
  61.6 7.3 %shard_map.81 = (bf16[8192,128]{1,0:T(8,128)(2,1)S(1)}, bf16[1024,128]{1,0:T(8,128)(2,1)S(1)}, bf16[1024,128]{1,0:T(8,128)(2,1)S(1)}, bf16[1024,128]{1,0:T(8,128)(2,1)S(1)}, bf16[128,128]{1,0:T(8,128)(2,1)S(1)}) custom-call(bf16[8192,128]{1,0:T(8,128)(2,1)S(1)} %get-tuple-element.44.refs_0_, bf16[8192,128]{1,0:T(8,128)(2,1)S(1)} %get-tuple-element.45.refs_1_, ...), custom_call_target="tpu_custom_call" | custom-call | flops 805306368 | bytes 8388608 | tf_op jit(solution)/shard_map/pallas_call | solution.py:455
  68.8 0.8 %collective-permute-start.14 = (bf16[1024,128]{1,0:T(8,128)(2,1)S(1)}, bf16[1024,128]{1,0:T(8,128)(2,1)S(1)}, u32[]{:S(2)}, u32[]{:S(2)}) collective-permute-start(bf16[1024,128]{1,0:T(8,128)(2,1)S(1)} %get-tuple-element.52), channel_id=1, source_target_pairs={{8,16},{24,0},{16,8},{0,24},{9,17},{25,1},{17,9},{1,25},{10,18},{2... | collective-permute-start | bytes 786440 | tf_op jit(solution)/shard_map/ppermute | solution.py:474
  69.6 0.6 collective-permute-start.15
  70.2 1.0 %collective-permute-start.17 = (bf16[128,128]{1,0:T(8,128)(2,1)S(1)}, bf16[128,128]{1,0:T(8,128)(2,1)S(1)}, u32[]{:S(2)}, u32[]{:S(2)}) collective-permute-start(bf16[128,128]{1,0:T(8,128)(2,1)S(1)} %get-tuple-element.54), channel_id=1, source_target_pairs={{1,2},{3,0},{2,1},{0,3},{5,6},{7,4},{6,5},{4,7},{9,10},{11,8},{10,... | collective-permute-start | bytes 98312 | tf_op jit(solution)/shard_map/ppermute | solution.py:475
  71.2 4.7 %collective-permute-done.17.refs_7_ = bf16[128,128]{1,0:T(8,128)(2,1)S(1)} collective-permute-done((bf16[128,128]{1,0:T(8,128)(2,1)S(1)}, bf16[128,128]{1,0:T(8,128)(2,1)S(1)}, u32[]{:S(2)}, u32[]{:S(2)}) %collective-permute-start.17) | collective-permute-done | bytes 32800 | tf_op jit(solution)/shard_map/ppermute | solution.py:475
  75.9 0.9 %collective-permute-done.14.refs_4_ = bf16[1024,128]{1,0:T(8,128)(2,1)S(1)} collective-permute-done((bf16[1024,128]{1,0:T(8,128)(2,1)S(1)}, bf16[1024,128]{1,0:T(8,128)(2,1)S(1)}, u32[]{:S(2)}, u32[]{:S(2)}) %collective-permute-start.14) | collective-permute-done | bytes 262176 | tf_op jit(solution)/shard_map/ppermute | solution.py:474
  76.8 1.0 %collective-permute-done.15.refs_5_ = bf16[1024,128]{1,0:T(8,128)(2,1)S(1)} collective-permute-done((bf16[1024,128]{1,0:T(8,128)(2,1)S(1)}, bf16[1024,128]{1,0:T(8,128)(2,1)S(1)}, u32[]{:S(2)}, u32[]{:S(2)}) %collective-permute-start.15) | collective-permute-done | bytes 262176 | tf_op jit(solution)/shard_map/ppermute | solution.py:474
  77.9 4.1 %shard_map.82 = bf16[8192,128]{1,0:T(8,128)(2,1)} custom-call(bf16[8192,128]{1,0:T(8,128)(2,1)S(1)} %get-tuple-element.50.refs_0_, bf16[8192,128]{1,0:T(8,128)(2,1)S(1)} %get-tuple-element.45.refs_1_, f32[64,128]{1,0:T(8,128)S(1)} %bitcast.11, bf16[1024,128]{1,0:T(8,128)(2,1)S(1)} %collective-permute-done.13.refs_3_, ...), custom_call_target="tpu_custom_call" | custom-call | flops 805306368 | bytes 8388608 | tf_op jit(solution)/shard_map/pallas_call | solution.py:455
  (21 shorter events, 0.1 us)
Async XLA Ops:
  8.0 12.3 %collective-permute-start.1 = (bf16[1024,128]{1,0:T(8,128)(2,1)}, bf16[1024,128]{1,0:T(8,128)(2,1)S(1)}, u32[]{:S(2)}, u32[]{:S(2)}) collective-permute-start(bf16[1024,128]{1,0:T(8,128)(2,1)} %shard_map.77.refs_0_), channel_id=1, source_target_pairs={{0,16},{8,24},{16,0},{24,8},{1,17},{9,25},{17,1},{25,9},{2,18},{10... | collective-permute-start | bytes 786440 | tf_op jit(solution)/shard_map/ppermute | solution.py:485
  11.0 8.8 %copy-start.2 = (bf16[1024,128]{1,0:T(8,128)(2,1)S(1)}, bf16[1024,128]{1,0:T(8,128)(2,1)}, u32[]{:S(2)}) copy-start(bf16[1024,128]{1,0:T(8,128)(2,1)} %shard_map.77.refs_0_) | copy-start | bytes 786436
  11.0 33.0 %copy-start.1 = (bf16[128,8,8,128]{3,2,1,0:T(8,128)(2,1)S(1)}, bf16[128,8,8,128]{3,2,1,0:T(8,128)(2,1)}, u32[]{:S(2)}) copy-start(bf16[128,8,8,128]{3,2,1,0:T(8,128)(2,1)} %param.7) | copy-start | bytes 6291460
  16.0 27.9 %copy-start = (bf16[128,8,8,128]{3,2,1,0:T(8,128)(2,1)S(1)}, bf16[128,8,8,128]{3,2,1,0:T(8,128)(2,1)}, u32[]{:S(2)}) copy-start(bf16[128,8,8,128]{3,2,1,0:T(8,128)(2,1)} %param.6) | copy-start | bytes 6291460
  16.0 27.9 %copy-start.3 = (f32[8,8,128]{2,1,0:T(8,128)S(1)}, f32[8,8,128]{2,1,0:T(8,128)}, u32[]{:S(2)}) copy-start(f32[8,8,128]{2,1,0:T(8,128)} %param.8) | copy-start | bytes 98308
  16.0 27.9 %copy-start.4 = (s32[1,1,1,32]{3,2,1,0:T(1,128)S(1)}, s32[1,1,1,32]{3,2,1,0:T(1,128)}, u32[]{:S(2)}) copy-start(s32[1,1,1,32]{3,2,1,0:T(1,128)} %refs_9_.1) | copy-start | bytes 388
  16.1 5.8 %collective-permute-start.7 = (bf16[128,128]{1,0:T(8,128)(2,1)S(1)}, bf16[128,128]{1,0:T(8,128)(2,1)S(1)}, u32[]{:S(2)}, u32[]{:S(2)}) collective-permute-start(bf16[128,128]{1,0:T(8,128)(2,1)S(1)} %get-tuple-element.32), channel_id=1, source_target_pairs={{1,2},{3,0},{2,1},{0,3},{5,6},{7,4},{6,5},{4,7},{9,10},{11,8},{10,... | collective-permute-start | bytes 98312 | tf_op jit(solution)/shard_map/ppermute | solution.py:475
  19.7 3.9 %collective-permute-start.6 = (bf16[128,128]{1,0:T(8,128)(2,1)S(1)}, bf16[128,128]{1,0:T(8,128)(2,1)S(1)}, u32[]{:S(2)}, u32[]{:S(2)}) collective-permute-start(bf16[128,128]{1,0:T(8,128)(2,1)S(1)} %get-tuple-element.32), channel_id=1, source_target_pairs={{0,1},{2,3},{1,0},{3,2},{4,5},{6,7},{5,4},{7,6},{8,9},{10,11},{9,8... | collective-permute-start | bytes 98312 | tf_op jit(solution)/shard_map/ppermute | solution.py:475
  19.7 3.9 %collective-permute-start = (bf16[1024,128]{1,0:T(8,128)(2,1)S(1)}, bf16[1024,128]{1,0:T(8,128)(2,1)S(1)}, u32[]{:S(2)}, u32[]{:S(2)}) collective-permute-start(bf16[1024,128]{1,0:T(8,128)(2,1)S(1)} %copy-done.2), channel_id=1, source_target_pairs={{0,8},{8,0},{16,24},{24,16},{1,9},{9,1},{17,25},{25,17},{2,10},{10... | collective-permute-start | bytes 786440 | tf_op jit(solution)/shard_map/ppermute | solution.py:485
  19.7 3.9 %collective-permute-start.3 = (bf16[1024,128]{1,0:T(8,128)(2,1)S(1)}, bf16[1024,128]{1,0:T(8,128)(2,1)S(1)}, u32[]{:S(2)}, u32[]{:S(2)}) collective-permute-start(bf16[1024,128]{1,0:T(8,128)(2,1)S(1)} %get-tuple-element.29), channel_id=1, source_target_pairs={{0,8},{16,24},{8,0},{24,16},{1,9},{17,25},{9,1},{25,17},{2,10},{18... | collective-permute-start | bytes 786440 | tf_op jit(solution)/shard_map/ppermute | solution.py:474
  20.2 8.4 %collective-permute-start.4 = (bf16[1024,128]{1,0:T(8,128)(2,1)S(1)}, bf16[1024,128]{1,0:T(8,128)(2,1)S(1)}, u32[]{:S(2)}, u32[]{:S(2)}) collective-permute-start(bf16[1024,128]{1,0:T(8,128)(2,1)S(1)} %get-tuple-element.30), channel_id=1, source_target_pairs={{8,16},{24,0},{16,8},{0,24},{9,17},{25,1},{17,9},{1,25},{10,18},{2... | collective-permute-start | bytes 786440 | tf_op jit(solution)/shard_map/ppermute | solution.py:474
  21.9 7.2 %collective-permute-start.5 = (bf16[1024,128]{1,0:T(8,128)(2,1)S(1)}, bf16[1024,128]{1,0:T(8,128)(2,1)S(1)}, u32[]{:S(2)}, u32[]{:S(2)}) collective-permute-start(bf16[1024,128]{1,0:T(8,128)(2,1)S(1)} %get-tuple-element.31), channel_id=1, source_target_pairs={{0,4},{4,0},{1,5},{5,1},{2,6},{6,2},{3,7},{7,3},{8,12},{12,8},{9,1... | collective-permute-start | bytes 786440 | tf_op jit(solution)/shard_map/ppermute | solution.py:474
  23.6 5.5 %collective-permute-start.2 = (bf16[1024,128]{1,0:T(8,128)(2,1)S(1)}, bf16[1024,128]{1,0:T(8,128)(2,1)S(1)}, u32[]{:S(2)}, u32[]{:S(2)}) collective-permute-start(bf16[1024,128]{1,0:T(8,128)(2,1)S(1)} %collective-permute-done.1.refs_2_), channel_id=1, source_target_pairs={{0,8},{8,0},{16,24},{24,16},{1,9},{9,1},{17,25},{25,17},{2,10},{10... | collective-permute-start | bytes 786440 | tf_op jit(solution)/shard_map/ppermute | solution.py:485
  51.9 7.7 %collective-permute-start.8 = (bf16[1024,128]{1,0:T(8,128)(2,1)S(1)}, bf16[1024,128]{1,0:T(8,128)(2,1)S(1)}, u32[]{:S(2)}, u32[]{:S(2)}) collective-permute-start(bf16[1024,128]{1,0:T(8,128)(2,1)S(1)} %get-tuple-element.46), channel_id=1, source_target_pairs={{0,8},{16,24},{8,0},{24,16},{1,9},{17,25},{9,1},{25,17},{2,10},{18... | collective-permute-start | bytes 786440 | tf_op jit(solution)/shard_map/ppermute | solution.py:474
  51.9 8.0 %collective-permute-start.9 = (bf16[1024,128]{1,0:T(8,128)(2,1)S(1)}, bf16[1024,128]{1,0:T(8,128)(2,1)S(1)}, u32[]{:S(2)}, u32[]{:S(2)}) collective-permute-start(bf16[1024,128]{1,0:T(8,128)(2,1)S(1)} %get-tuple-element.47), channel_id=1, source_target_pairs={{8,16},{24,0},{16,8},{0,24},{9,17},{25,1},{17,9},{1,25},{10,18},{2... | collective-permute-start | bytes 786440 | tf_op jit(solution)/shard_map/ppermute | solution.py:474
  53.3 8.2 %collective-permute-start.10 = (bf16[1024,128]{1,0:T(8,128)(2,1)S(1)}, bf16[1024,128]{1,0:T(8,128)(2,1)S(1)}, u32[]{:S(2)}, u32[]{:S(2)}) collective-permute-start(bf16[1024,128]{1,0:T(8,128)(2,1)S(1)} %get-tuple-element.48), channel_id=1, source_target_pairs={{0,4},{4,0},{1,5},{5,1},{2,6},{6,2},{3,7},{7,3},{8,12},{12,8},{9,1... | collective-permute-start | bytes 786440 | tf_op jit(solution)/shard_map/ppermute | solution.py:474
  53.9 5.7 %collective-permute-start.12 = (bf16[128,128]{1,0:T(8,128)(2,1)S(1)}, bf16[128,128]{1,0:T(8,128)(2,1)S(1)}, u32[]{:S(2)}, u32[]{:S(2)}) collective-permute-start(bf16[128,128]{1,0:T(8,128)(2,1)S(1)} %get-tuple-element.49), channel_id=1, source_target_pairs={{1,2},{3,0},{2,1},{0,3},{5,6},{7,4},{6,5},{4,7},{9,10},{11,8},{10,... | collective-permute-start | bytes 98312 | tf_op jit(solution)/shard_map/ppermute | solution.py:475
  54.0 5.7 %collective-permute-start.11 = (bf16[128,128]{1,0:T(8,128)(2,1)S(1)}, bf16[128,128]{1,0:T(8,128)(2,1)S(1)}, u32[]{:S(2)}, u32[]{:S(2)}) collective-permute-start(bf16[128,128]{1,0:T(8,128)(2,1)S(1)} %get-tuple-element.49), channel_id=1, source_target_pairs={{0,1},{2,3},{1,0},{3,2},{4,5},{6,7},{5,4},{7,6},{8,9},{10,11},{9,8... | collective-permute-start | bytes 98312 | tf_op jit(solution)/shard_map/ppermute | solution.py:475
  68.8 7.1 %collective-permute-start.13 = (bf16[1024,128]{1,0:T(8,128)(2,1)S(1)}, bf16[1024,128]{1,0:T(8,128)(2,1)S(1)}, u32[]{:S(2)}, u32[]{:S(2)}) collective-permute-start(bf16[1024,128]{1,0:T(8,128)(2,1)S(1)} %get-tuple-element.51), channel_id=1, source_target_pairs={{0,8},{16,24},{8,0},{24,16},{1,9},{17,25},{9,1},{25,17},{2,10},{18... | collective-permute-start | bytes 786440 | tf_op jit(solution)/shard_map/ppermute | solution.py:474
  68.8 8.0 %collective-permute-start.14 = (bf16[1024,128]{1,0:T(8,128)(2,1)S(1)}, bf16[1024,128]{1,0:T(8,128)(2,1)S(1)}, u32[]{:S(2)}, u32[]{:S(2)}) collective-permute-start(bf16[1024,128]{1,0:T(8,128)(2,1)S(1)} %get-tuple-element.52), channel_id=1, source_target_pairs={{8,16},{24,0},{16,8},{0,24},{9,17},{25,1},{17,9},{1,25},{10,18},{2... | collective-permute-start | bytes 786440 | tf_op jit(solution)/shard_map/ppermute | solution.py:474
  69.6 8.2 %collective-permute-start.15 = (bf16[1024,128]{1,0:T(8,128)(2,1)S(1)}, bf16[1024,128]{1,0:T(8,128)(2,1)S(1)}, u32[]{:S(2)}, u32[]{:S(2)}) collective-permute-start(bf16[1024,128]{1,0:T(8,128)(2,1)S(1)} %get-tuple-element.53), channel_id=1, source_target_pairs={{0,4},{4,0},{1,5},{5,1},{2,6},{6,2},{3,7},{7,3},{8,12},{12,8},{9,1... | collective-permute-start | bytes 786440 | tf_op jit(solution)/shard_map/ppermute | solution.py:474
  70.2 5.7 %collective-permute-start.17 = (bf16[128,128]{1,0:T(8,128)(2,1)S(1)}, bf16[128,128]{1,0:T(8,128)(2,1)S(1)}, u32[]{:S(2)}, u32[]{:S(2)}) collective-permute-start(bf16[128,128]{1,0:T(8,128)(2,1)S(1)} %get-tuple-element.54), channel_id=1, source_target_pairs={{1,2},{3,0},{2,1},{0,3},{5,6},{7,4},{6,5},{4,7},{9,10},{11,8},{10,... | collective-permute-start | bytes 98312 | tf_op jit(solution)/shard_map/ppermute | solution.py:475
  71.2 4.7 %collective-permute-start.16 = (bf16[128,128]{1,0:T(8,128)(2,1)S(1)}, bf16[128,128]{1,0:T(8,128)(2,1)S(1)}, u32[]{:S(2)}, u32[]{:S(2)}) collective-permute-start(bf16[128,128]{1,0:T(8,128)(2,1)S(1)} %get-tuple-element.54), channel_id=1, source_target_pairs={{0,1},{2,3},{1,0},{3,2},{4,5},{6,7},{5,4},{7,6},{8,9},{10,11},{9,8... | collective-permute-start | bytes 98312 | tf_op jit(solution)/shard_map/ppermute | solution.py:475

commit v4 on v3

--- a/solution.py
+++ b/solution.py
@@ -32,12 +32,13 @@
     return pltpu.CompilerParams(vmem_limit_bytes=mebibytes * 1024 * 1024)
 
 
-def trace_kernel(stride, block, field_ref, cell_ref, out_ref, field, cell_v, perm, pick, rsum, sems):
+def trace_kernel(stride, block, field_ref, cell_ref, out_ref, field, cell_v, near, pick, rsum, sems):
     sides, rows, lanes = field.shape
     slots = cell_ref.shape[3]
     per_row = lanes // stride
     group = 16
     width = group * per_row
+    parts = rows // group
     cell_copy = pltpu.make_async_copy(cell_ref, cell_v, sems.at[sides // block])
     cell_copy.start()
     copies = []
@@ -50,32 +51,41 @@
     rsum[...] = (iota(shape, 1) // group == iota(shape, 0)).astype(BF)
     cell_copy.wait()
     cell = cell_v[0, 0]
-    perm[...] = (iota((slots, slots), 0) == cell // stride).astype(BF)
-    offset = jnp.broadcast_to((cell % stride).astype(BF), (16, slots))
-    sorted_offset = dot_nt(offset, perm[...])[0:1].astype(jnp.int32)
-    place = (iota((1, slots), 1) % per_row) * stride + sorted_offset
-    pick[...] = (iota((lanes, slots), 0) == place).astype(BF)
+    run = cell // stride
+    digit = jnp.zeros_like(cell)
+    for part in range(parts):
+        digit = jnp.where(run // width == part, (cell % stride) * stride**part, digit)
+    hit = iota((width, slots), 0) == run % width
+    near[...] = hit.astype(BF)
+    digits = jnp.sum(jnp.where(hit, digit.astype(F32), 0.0), axis=1, keepdims=True)
+    digits = digits.astype(jnp.int32)
+    for part in range(parts):
+        offset = digits // stride**part % stride
+        place = iota((width, lanes), 0) % per_row * stride + offset
+        pick[part] = (iota((width, lanes), 1) == place).astype(BF)
 
     shape = (block * group, width)
     own = iota(shape, 0) % group == iota(shape, 1) // per_row
-    picked = []
+    picked = [[] for _ in range(parts)]
     for step in range(sides // block):
         copies[step].wait()
-        parts = []
-        for part in range(rows // group):
+        for part in range(parts):
             values = field[step * block : (step + 1) * block, part * group : (part + 1) * group, :]
-            cols = slice(part * width, (part + 1) * width)
-            spread = dot(values.reshape(block * group, lanes), pick[:, cols])
+            spread = dot_nt(values.reshape(block * group, lanes), pick[part])
             spread = jnp.where(own, spread, 0.0).astype(BF)
-            parts.append(dot(rsum[...], spread).astype(BF))
-        picked.append(jnp.concatenate(parts, axis=1))
-    out_ref[...] = dot(jnp.concatenate(picked, axis=0), perm[...]).T.astype(BF)
+            picked[part].append(dot(rsum[...], spread).astype(BF))
+    total = jnp.zeros((sides, slots), F32)
+    for part in range(parts):
+        placed = dot(jnp.concatenate(picked[part], axis=0), near[...])
+        total = jnp.where(run // width == part, placed, total)
+    out_ref[...] = total.T.astype(BF)
 
 
 def traces(field, trace_cell, block):
     sides, rows, lanes = field.shape
     slots = trace_cell.shape[3]
     stride = rows * lanes // slots
+    width = 16 * lanes // stride
     hbm = pl.BlockSpec(memory_space=pltpu.HBM)
     return pl.pallas_call(
         functools.partial(trace_kernel, stride, block),
@@ -85,8 +95,8 @@
         scratch_shapes=[
             pltpu.VMEM(field.shape, BF),
             pltpu.VMEM(trace_cell.shape, jnp.int32),
-            pltpu.VMEM((slots, slots), BF),
-            pltpu.VMEM((lanes, slots), BF),
+            pltpu.VMEM((width, slots), BF),
+            pltpu.VMEM((slots // width, width, lanes), BF),
             pltpu.VMEM((block, block * 16), BF),
             pltpu.SemaphoreType.DMA((sides // block + 1,)),
         ],
@@ -151,10 +161,13 @@
 
 
 def swaps(peers):
-    turns = [[(i, i + 1) for i in range(first, peers - 1, 2)] for first in (0, 1)]
-    if turns[1] and peers % 2 == 0:
-        turns[1].append((peers - 1, 0))
-    return [[(i, j) for i, j in part] + [(j, i) for i, j in part] for part in turns if part]
+    turns = []
+    for turn in (0, 1):
+        partner = {i: i + 1 if i % 2 == turn else i - 1 for i in range(peers)}
+        pairs = [(i, j if 0 <= j < peers else i) for i, j in partner.items()]
+        if any(i != j for i, j in pairs):
+            turns.append(pairs)
+    return turns
 
 
 def has_neighbour(axis, turn):
@@ -169,7 +182,7 @@
         self.cells = first * second
         self.chunk = max(1, 128 // self.cells)
         self.rows = self.chunk * self.cells
-        self.block = min(sides, 16)
+        self.block = min(sides, 32)
         self.half = self.block // 2
         self.half_rows = self.half * self.cells
         self.faces = [("row", i) for i in range(len(swaps(lax.axis_size("row"))))]

time: 82.2 us -> 80 us (0.973)
  starting transfers between devices: 14.3 us -> 21.8 us
  waiting for transfers between devices: 20.5 us -> 14.5 us
  Pallas kernels: 32.4 us -> 28 us
    ppermute x6, waiting for transfers between devices: 11.1 us -> 3.79 us  [exchange(): lax.ppermute(ends, 'gz', pairs)]
    ppermute x6, starting transfers between devices: 5.64 us -> 11.3 us  [exchange(): lax.ppermute(ends, 'gz', pairs)]
    pallas_call x3, Pallas kernels: 19.3 us -> 15.8 us  [sweep(): pl.pallas_call(functools.partial(sweep_kernel, shape, with_flux, last), g...]
    ppermute x3, starting transfers between devices: 3.01 us -> 4.61 us  [xor_gather(): lax.ppermute(held[key], axis, swap)]
    ppermute x9, waiting for transfers between devices: 9.37 us -> 10.7 us  [exchange(): halos[face] = lax.ppermute(value, face[0], pairs)]
    pallas_call x1, Pallas kernels: 5.06 us -> 3.97 us  [first_faces(): pl.pallas_call(functools.partial(faces_kernel, shape, slots), in_specs=[W...]
  transfers between devices with their start and end apart: 18 -> 18, of which waited for: 10 -> 5; matrix products, arithmetic and copies ran while one was open for 0% -> 0% of each run, Pallas kernels for 6% -> 5%
where the time goes in v4:
time: 80 us; the launch traced here: 79.3 us
  Pallas kernels  28 us (35%)
  starting transfers between devices  21.8 us (27%)
  waiting for transfers between devices  14.5 us (18%)
  blocking collectives  14.1 us (18%)
    pallas_call x3, Pallas kernels, sweep(): pl.pallas_call(functools.partial(sweep_kernel, shape, with_flux, last), g...  15.8 us
    all_to_all x1, blocking collectives, per_device(): lax.all_to_all(sent, ('col', 'gz'), split_axis=0, concat_axis=0, tiled=True)  14.1 us
    ppermute x6, starting transfers between devices, exchange(): lax.ppermute(ends, 'gz', pairs)  11.3 us
    ppermute x9, waiting for transfers between devices, exchange(): halos[face] = lax.ppermute(value, face[0], pairs)  10.7 us
    pallas_call x1, Pallas kernels, traces(): pl.pallas_call(functools.partial(trace_kernel, stride, block), in_specs=[...  7.5 us
    ppermute x9, starting transfers between devices, exchange(): halos[face] = lax.ppermute(value, face[0], pairs)  5.92 us
    ppermute x3, starting transfers between devices, xor_gather(): lax.ppermute(held[key], axis, swap)  4.61 us
    pallas_call x1, Pallas kernels, first_faces(): pl.pallas_call(functools.partial(faces_kernel, shape, slots), in_specs=[W...  3.97 us
  transfers between devices with their start and end apart: 18, of which 5 were waited for; matrix products, arithmetic and copies ran while one was open for 0% of the time, Pallas kernels for 5%

profile of v4, /device:TPU:0, one launch (start us, length us, event | category | flops | bytes accessed | tf_op | source)
XLA Modules:
  0.0 79.3 jit_solution(9879737294512702178)
XLA Ops:
  0.6 7.5 %shard_map.77.refs_0_ = bf16[1024,128]{1,0:T(8,128)(2,1)} custom-call(bf16[128,64,128]{2,1,0:T(8,128)(2,1)} %bitcast.5, s32[1,1,1,1024]{3,2,1,0:T(1,128)} %cell_ref.1), custom_call_target="tpu_custom_call" | custom-call | flops 536870912 | bytes 2097152 | tf_op jit(solution)/shard_map/pallas_call | solution.py:90
  8.1 3.0 %collective-permute-start.1 = (bf16[1024,128]{1,0:T(8,128)(2,1)}, bf16[1024,128]{1,0:T(8,128)(2,1)S(1)}, u32[]{:S(2)}, u32[]{:S(2)}) collective-permute-start(bf16[1024,128]{1,0:T(8,128)(2,1)} %shard_map.77.refs_0_), channel_id=1, source_target_pairs={{0,16},{8,24},{16,0},{24,8},{1,17},{9,25},{17,1},{25,9},{2,18},{10... | collective-permute-start | bytes 786440 | tf_op jit(solution)/shard_map/ppermute | solution.py:498
  11.1 4.0 %shard_map.78 = (bf16[1024,128]{1,0:T(8,128)(2,1)S(1)}, bf16[1024,128]{1,0:T(8,128)(2,1)S(1)}, bf16[1024,128]{1,0:T(8,128)(2,1)S(1)}, bf16[128,128]{1,0:T(8,128)(2,1)S(1)}, bf16[4,256,1024]{2,1,0:T(8,128)(2,1)S(1)}) custom-call(bf16[8192,128]{1,0:T(8,128)(2,1)} %bitcast.6, bf16[256,16384]{1,0:T(8,128)(2,1)} %block_ref.1), custom_call_target="tpu_custom_call" | custom-call | flops 134217728 | bytes 4194304 | tf_op jit(solution)/shard_map/pallas_call | solution.py:302
  15.1 0.0 copy-start
  15.1 0.0 copy-start.3
  15.1 0.0 copy-start.4
  15.2 0.8 %collective-permute-start.7 = (bf16[128,128]{1,0:T(8,128)(2,1)S(1)}, bf16[128,128]{1,0:T(8,128)(2,1)S(1)}, u32[]{:S(2)}, u32[]{:S(2)}) collective-permute-start(bf16[128,128]{1,0:T(8,128)(2,1)S(1)} %get-tuple-element.32), channel_id=1, source_target_pairs={{0,0},{1,2},{2,1},{3,3},{4,4},{5,6},{6,5},{7,7},{8,8},{9,10},{10,9... | collective-permute-start | bytes 98312 | tf_op jit(solution)/shard_map/ppermute | solution.py:488
  16.0 4.5 %collective-permute-start.6 = (bf16[128,128]{1,0:T(8,128)(2,1)S(1)}, bf16[128,128]{1,0:T(8,128)(2,1)S(1)}, u32[]{:S(2)}, u32[]{:S(2)}) collective-permute-start(bf16[128,128]{1,0:T(8,128)(2,1)S(1)} %get-tuple-element.32), channel_id=1, source_target_pairs={{0,1},{1,0},{2,3},{3,2},{4,5},{5,4},{6,7},{7,6},{8,9},{9,8},{10,11... | collective-permute-start | bytes 98312 | tf_op jit(solution)/shard_map/ppermute | solution.py:488
  20.4 0.0 collective-permute-start
  20.4 0.5 collective-permute-start.3
  20.9 0.7 collective-permute-start.4
  21.6 1.6 %collective-permute-start.5 = (bf16[1024,128]{1,0:T(8,128)(2,1)S(1)}, bf16[1024,128]{1,0:T(8,128)(2,1)S(1)}, u32[]{:S(2)}, u32[]{:S(2)}) collective-permute-start(bf16[1024,128]{1,0:T(8,128)(2,1)S(1)} %get-tuple-element.31), channel_id=1, source_target_pairs={{0,4},{4,0},{1,5},{5,1},{2,6},{6,2},{3,7},{7,3},{8,12},{12,8},{9,1... | collective-permute-start | bytes 786440 | tf_op jit(solution)/shard_map/ppermute | solution.py:487
  23.2 1.6 %collective-permute-start.2 = (bf16[1024,128]{1,0:T(8,128)(2,1)S(1)}, bf16[1024,128]{1,0:T(8,128)(2,1)S(1)}, u32[]{:S(2)}, u32[]{:S(2)}) collective-permute-start(bf16[1024,128]{1,0:T(8,128)(2,1)S(1)} %collective-permute-done.1.refs_2_), channel_id=1, source_target_pairs={{0,8},{8,0},{16,24},{24,16},{1,9},{9,1},{17,25},{25,17},{2,10},{10... | collective-permute-start | bytes 786440 | tf_op jit(solution)/shard_map/ppermute | solution.py:498
  24.8 5.1 %collective-permute-done.5.refs_5_ = bf16[1024,128]{1,0:T(8,128)(2,1)S(1)} collective-permute-done((bf16[1024,128]{1,0:T(8,128)(2,1)S(1)}, bf16[1024,128]{1,0:T(8,128)(2,1)S(1)}, u32[]{:S(2)}, u32[]{:S(2)}) %collective-permute-start.5) | collective-permute-done | bytes 262176 | tf_op jit(solution)/shard_map/ppermute | solution.py:487
  30.0 0.8 shard_map.79
  30.7 14.1 %all_to_all.5.refs_8_ = f32[8,64,128]{2,1,0:T(8,128)S(1)} all-to-all(f32[8,64,128]{2,1,0:T(8,128)S(1)} %shard_map.79), channel_id=1, replica_groups=mesh['row'=4,'col'=2,'gz'=4] {'col','gz'}, dimensions={0} | all-to-all | bytes 524288 | tf_op jit(solution)/shard_map/all_to_all | solution.py:521
  44.9 6.5 %shard_map.80 = (bf16[8192,128]{1,0:T(8,128)(2,1)S(1)}, bf16[1024,128]{1,0:T(8,128)(2,1)S(1)}, bf16[1024,128]{1,0:T(8,128)(2,1)S(1)}, bf16[1024,128]{1,0:T(8,128...) custom-call(bf16[8192,128]{1,0:T(8,128)(2,1)S(1)} %bitcast.7, ...), custom_call_target="tpu_custom_call" | custom-call | flops 805306368 | bytes 8388608 | tf_op jit(solution)/shard_map/pallas_call | solution.py:468
  51.4 0.7 collective-permute-start.9
  52.1 0.6 collective-permute-start.10
  52.7 0.7 collective-permute-start.12
  53.4 2.4 %collective-permute-start.11 = (bf16[128,128]{1,0:T(8,128)(2,1)S(1)}, bf16[128,128]{1,0:T(8,128)(2,1)S(1)}, u32[]{:S(2)}, u32[]{:S(2)}) collective-permute-start(bf16[128,128]{1,0:T(8,128)(2,1)S(1)} %get-tuple-element.49), channel_id=1, source_target_pairs={{0,1},{1,0},{2,3},{3,2},{4,5},{5,4},{6,7},{7,6},{8,9},{9,8},{10,11... | collective-permute-start | bytes 98312 | tf_op jit(solution)/shard_map/ppermute | solution.py:488
  55.8 1.9 %collective-permute-done.11.refs_6_ = bf16[128,128]{1,0:T(8,128)(2,1)S(1)} collective-permute-done((bf16[128,128]{1,0:T(8,128)(2,1)S(1)}, bf16[128,128]{1,0:T(8,128)(2,1)S(1)}, u32[]{:S(2)}, u32[]{:S(2)}) %collective-permute-start.11) | collective-permute-done | bytes 32800 | tf_op jit(solution)/shard_map/ppermute | solution.py:488
  57.7 2.9 %collective-permute-done.10.refs_5_ = bf16[1024,128]{1,0:T(8,128)(2,1)S(1)} collective-permute-done((bf16[1024,128]{1,0:T(8,128)(2,1)S(1)}, bf16[1024,128]{1,0:T(8,128)(2,1)S(1)}, u32[]{:S(2)}, u32[]{:S(2)}) %collective-permute-start.10) | collective-permute-done | bytes 262176 | tf_op jit(solution)/shard_map/ppermute | solution.py:487
  60.6 5.7 %shard_map.81 = (bf16[8192,128]{1,0:T(8,128)(2,1)S(1)}, bf16[1024,128]{1,0:T(8,128)(2,1)S(1)}, bf16[1024,128]{1,0:T(8,128)(2,1)S(1)}, bf16[1024,128]{1,0:T(8,128)(2,1)S(1)}, bf16[128,128]{1,0:T(8,128)(2,1)S(1)}) custom-call(bf16[8192,128]{1,0:T(8,128)(2,1)S(1)} %get-tuple-element.44.refs_0_, bf16[8192,128]{1,0:T(8,128)(2,1)S(1)} %get-tuple-element.45.refs_1_, ...), custom_call_target="tpu_custom_call" | custom-call | flops 805306368 | bytes 8388608 | tf_op jit(solution)/shard_map/pallas_call | solution.py:468
  66.3 0.6 collective-permute-start.13
  66.9 0.7 collective-permute-start.14
  67.6 0.6 collective-permute-start.15
  68.2 0.7 collective-permute-start.17
  68.8 2.4 %collective-permute-start.16 = (bf16[128,128]{1,0:T(8,128)(2,1)S(1)}, bf16[128,128]{1,0:T(8,128)(2,1)S(1)}, u32[]{:S(2)}, u32[]{:S(2)}) collective-permute-start(bf16[128,128]{1,0:T(8,128)(2,1)S(1)} %get-tuple-element.54), channel_id=1, source_target_pairs={{0,1},{1,0},{2,3},{3,2},{4,5},{5,4},{6,7},{7,6},{8,9},{9,8},{10,11... | collective-permute-start | bytes 98312 | tf_op jit(solution)/shard_map/ppermute | solution.py:488
  71.2 1.9 %collective-permute-done.16.refs_6_ = bf16[128,128]{1,0:T(8,128)(2,1)S(1)} collective-permute-done((bf16[128,128]{1,0:T(8,128)(2,1)S(1)}, bf16[128,128]{1,0:T(8,128)(2,1)S(1)}, u32[]{:S(2)}, u32[]{:S(2)}) %collective-permute-start.16) | collective-permute-done | bytes 32800 | tf_op jit(solution)/shard_map/ppermute | solution.py:488
  73.1 2.6 %collective-permute-done.15.refs_5_ = bf16[1024,128]{1,0:T(8,128)(2,1)S(1)} collective-permute-done((bf16[1024,128]{1,0:T(8,128)(2,1)S(1)}, bf16[1024,128]{1,0:T(8,128)(2,1)S(1)}, u32[]{:S(2)}, u32[]{:S(2)}) %collective-permute-start.15) | collective-permute-done | bytes 262176 | tf_op jit(solution)/shard_map/ppermute | solution.py:487
  75.7 3.6 %shard_map.82 = bf16[8192,128]{1,0:T(8,128)(2,1)} custom-call(bf16[8192,128]{1,0:T(8,128)(2,1)S(1)} %get-tuple-element.50.refs_0_, bf16[8192,128]{1,0:T(8,128)(2,1)S(1)} %get-tuple-element.45.refs_1_, f32[64,128]{1,0:T(8,128)S(1)} %bitcast.11, bf16[1024,128]{1,0:T(8,128)(2,1)S(1)} %collective-permute-done.13.refs_3_, ...), custom_call_target="tpu_custom_call" | custom-call | flops 805306368 | bytes 8388608 | tf_op jit(solution)/shard_map/pallas_call | solution.py:468
  (21 shorter events, 0.1 us)
Async XLA Ops:
  8.1 12.8 %collective-permute-start.1 = (bf16[1024,128]{1,0:T(8,128)(2,1)}, bf16[1024,128]{1,0:T(8,128)(2,1)S(1)}, u32[]{:S(2)}, u32[]{:S(2)}) collective-permute-start(bf16[1024,128]{1,0:T(8,128)(2,1)} %shard_map.77.refs_0_), channel_id=1, source_target_pairs={{0,16},{8,24},{16,0},{24,8},{1,17},{9,25},{17,1},{25,9},{2,18},{10... | collective-permute-start | bytes 786440 | tf_op jit(solution)/shard_map/ppermute | solution.py:498
  11.1 9.3 %copy-start.2 = (bf16[1024,128]{1,0:T(8,128)(2,1)S(1)}, bf16[1024,128]{1,0:T(8,128)(2,1)}, u32[]{:S(2)}) copy-start(bf16[1024,128]{1,0:T(8,128)(2,1)} %shard_map.77.refs_0_) | copy-start | bytes 786436
  11.1 33.7 %copy-start.1 = (bf16[128,8,8,128]{3,2,1,0:T(8,128)(2,1)S(1)}, bf16[128,8,8,128]{3,2,1,0:T(8,128)(2,1)}, u32[]{:S(2)}) copy-start(bf16[128,8,8,128]{3,2,1,0:T(8,128)(2,1)} %param.7) | copy-start | bytes 6291460
  15.1 29.7 %copy-start = (bf16[128,8,8,128]{3,2,1,0:T(8,128)(2,1)S(1)}, bf16[128,8,8,128]{3,2,1,0:T(8,128)(2,1)}, u32[]{:S(2)}) copy-start(bf16[128,8,8,128]{3,2,1,0:T(8,128)(2,1)} %param.6) | copy-start | bytes 6291460
  15.1 29.7 %copy-start.3 = (f32[8,8,128]{2,1,0:T(8,128)S(1)}, f32[8,8,128]{2,1,0:T(8,128)}, u32[]{:S(2)}) copy-start(f32[8,8,128]{2,1,0:T(8,128)} %param.8) | copy-start | bytes 98308
  15.1 29.7 %copy-start.4 = (s32[1,1,1,32]{3,2,1,0:T(1,128)S(1)}, s32[1,1,1,32]{3,2,1,0:T(1,128)}, u32[]{:S(2)}) copy-start(s32[1,1,1,32]{3,2,1,0:T(1,128)} %refs_9_.1) | copy-start | bytes 388
  15.2 6.5 %collective-permute-start.7 = (bf16[128,128]{1,0:T(8,128)(2,1)S(1)}, bf16[128,128]{1,0:T(8,128)(2,1)S(1)}, u32[]{:S(2)}, u32[]{:S(2)}) collective-permute-start(bf16[128,128]{1,0:T(8,128)(2,1)S(1)} %get-tuple-element.32), channel_id=1, source_target_pairs={{0,0},{1,2},{2,1},{3,3},{4,4},{5,6},{6,5},{7,7},{8,8},{9,10},{10,9... | collective-permute-start | bytes 98312 | tf_op jit(solution)/shard_map/ppermute | solution.py:488
  16.0 7.3 %collective-permute-start.6 = (bf16[128,128]{1,0:T(8,128)(2,1)S(1)}, bf16[128,128]{1,0:T(8,128)(2,1)S(1)}, u32[]{:S(2)}, u32[]{:S(2)}) collective-permute-start(bf16[128,128]{1,0:T(8,128)(2,1)S(1)} %get-tuple-element.32), channel_id=1, source_target_pairs={{0,1},{1,0},{2,3},{3,2},{4,5},{5,4},{6,7},{7,6},{8,9},{9,8},{10,11... | collective-permute-start | bytes 98312 | tf_op jit(solution)/shard_map/ppermute | solution.py:488
  20.4 4.4 %collective-permute-start = (bf16[1024,128]{1,0:T(8,128)(2,1)S(1)}, bf16[1024,128]{1,0:T(8,128)(2,1)S(1)}, u32[]{:S(2)}, u32[]{:S(2)}) collective-permute-start(bf16[1024,128]{1,0:T(8,128)(2,1)S(1)} %copy-done.2), channel_id=1, source_target_pairs={{0,8},{8,0},{16,24},{24,16},{1,9},{9,1},{17,25},{25,17},{2,10},{10... | collective-permute-start | bytes 786440 | tf_op jit(solution)/shard_map/ppermute | solution.py:498
  20.4 4.4 %collective-permute-start.3 = (bf16[1024,128]{1,0:T(8,128)(2,1)S(1)}, bf16[1024,128]{1,0:T(8,128)(2,1)S(1)}, u32[]{:S(2)}, u32[]{:S(2)}) collective-permute-start(bf16[1024,128]{1,0:T(8,128)(2,1)S(1)} %get-tuple-element.29), channel_id=1, source_target_pairs={{0,8},{8,0},{16,24},{24,16},{1,9},{9,1},{17,25},{25,17},{2,10},{10... | collective-permute-start | bytes 786440 | tf_op jit(solution)/shard_map/ppermute | solution.py:487
  20.9 3.9 %collective-permute-start.4 = (bf16[1024,128]{1,0:T(8,128)(2,1)S(1)}, bf16[1024,128]{1,0:T(8,128)(2,1)S(1)}, u32[]{:S(2)}, u32[]{:S(2)}) collective-permute-start(bf16[1024,128]{1,0:T(8,128)(2,1)S(1)} %get-tuple-element.30), channel_id=1, source_target_pairs={{0,0},{8,16},{16,8},{24,24},{1,1},{9,17},{17,9},{25,25},{2,2},{10,... | collective-permute-start | bytes 786440 | tf_op jit(solution)/shard_map/ppermute | solution.py:487
  21.6 8.3 %collective-permute-start.5 = (bf16[1024,128]{1,0:T(8,128)(2,1)S(1)}, bf16[1024,128]{1,0:T(8,128)(2,1)S(1)}, u32[]{:S(2)}, u32[]{:S(2)}) collective-permute-start(bf16[1024,128]{1,0:T(8,128)(2,1)S(1)} %get-tuple-element.31), channel_id=1, source_target_pairs={{0,4},{4,0},{1,5},{5,1},{2,6},{6,2},{3,7},{7,3},{8,12},{12,8},{9,1... | collective-permute-start | bytes 786440 | tf_op jit(solution)/shard_map/ppermute | solution.py:487
  23.2 6.8 %collective-permute-start.2 = (bf16[1024,128]{1,0:T(8,128)(2,1)S(1)}, bf16[1024,128]{1,0:T(8,128)(2,1)S(1)}, u32[]{:S(2)}, u32[]{:S(2)}) collective-permute-start(bf16[1024,128]{1,0:T(8,128)(2,1)S(1)} %collective-permute-done.1.refs_2_), channel_id=1, source_target_pairs={{0,8},{8,0},{16,24},{24,16},{1,9},{9,1},{17,25},{25,17},{2,10},{10... | collective-permute-start | bytes 786440 | tf_op jit(solution)/shard_map/ppermute | solution.py:498
  51.4 6.2 %collective-permute-start.8 = (bf16[1024,128]{1,0:T(8,128)(2,1)S(1)}, bf16[1024,128]{1,0:T(8,128)(2,1)S(1)}, u32[]{:S(2)}, u32[]{:S(2)}) collective-permute-start(bf16[1024,128]{1,0:T(8,128)(2,1)S(1)} %get-tuple-element.46), channel_id=1, source_target_pairs={{0,8},{8,0},{16,24},{24,16},{1,9},{9,1},{17,25},{25,17},{2,10},{10... | collective-permute-start | bytes 786440 | tf_op jit(solution)/shard_map/ppermute | solution.py:487
  51.4 6.2 %collective-permute-start.9 = (bf16[1024,128]{1,0:T(8,128)(2,1)S(1)}, bf16[1024,128]{1,0:T(8,128)(2,1)S(1)}, u32[]{:S(2)}, u32[]{:S(2)}) collective-permute-start(bf16[1024,128]{1,0:T(8,128)(2,1)S(1)} %get-tuple-element.47), channel_id=1, source_target_pairs={{0,0},{8,16},{16,8},{24,24},{1,1},{9,17},{17,9},{25,25},{2,2},{10,... | collective-permute-start | bytes 786440 | tf_op jit(solution)/shard_map/ppermute | solution.py:487
  52.1 8.5 %collective-permute-start.10 = (bf16[1024,128]{1,0:T(8,128)(2,1)S(1)}, bf16[1024,128]{1,0:T(8,128)(2,1)S(1)}, u32[]{:S(2)}, u32[]{:S(2)}) collective-permute-start(bf16[1024,128]{1,0:T(8,128)(2,1)S(1)} %get-tuple-element.48), channel_id=1, source_target_pairs={{0,4},{4,0},{1,5},{5,1},{2,6},{6,2},{3,7},{7,3},{8,12},{12,8},{9,1... | collective-permute-start | bytes 786440 | tf_op jit(solution)/shard_map/ppermute | solution.py:487
  52.7 3.0 %collective-permute-start.12 = (bf16[128,128]{1,0:T(8,128)(2,1)S(1)}, bf16[128,128]{1,0:T(8,128)(2,1)S(1)}, u32[]{:S(2)}, u32[]{:S(2)}) collective-permute-start(bf16[128,128]{1,0:T(8,128)(2,1)S(1)} %get-tuple-element.49), channel_id=1, source_target_pairs={{0,0},{1,2},{2,1},{3,3},{4,4},{5,6},{6,5},{7,7},{8,8},{9,10},{10,9... | collective-permute-start | bytes 98312 | tf_op jit(solution)/shard_map/ppermute | solution.py:488
  53.4 4.3 %collective-permute-start.11 = (bf16[128,128]{1,0:T(8,128)(2,1)S(1)}, bf16[128,128]{1,0:T(8,128)(2,1)S(1)}, u32[]{:S(2)}, u32[]{:S(2)}) collective-permute-start(bf16[128,128]{1,0:T(8,128)(2,1)S(1)} %get-tuple-element.49), channel_id=1, source_target_pairs={{0,1},{1,0},{2,3},{3,2},{4,5},{5,4},{6,7},{7,6},{8,9},{9,8},{10,11... | collective-permute-start | bytes 98312 | tf_op jit(solution)/shard_map/ppermute | solution.py:488
  66.3 6.8 %collective-permute-start.13 = (bf16[1024,128]{1,0:T(8,128)(2,1)S(1)}, bf16[1024,128]{1,0:T(8,128)(2,1)S(1)}, u32[]{:S(2)}, u32[]{:S(2)}) collective-permute-start(bf16[1024,128]{1,0:T(8,128)(2,1)S(1)} %get-tuple-element.51), channel_id=1, source_target_pairs={{0,8},{8,0},{16,24},{24,16},{1,9},{9,1},{17,25},{25,17},{2,10},{10... | collective-permute-start | bytes 786440 | tf_op jit(solution)/shard_map/ppermute | solution.py:487
  66.9 6.2 %collective-permute-start.14 = (bf16[1024,128]{1,0:T(8,128)(2,1)S(1)}, bf16[1024,128]{1,0:T(8,128)(2,1)S(1)}, u32[]{:S(2)}, u32[]{:S(2)}) collective-permute-start(bf16[1024,128]{1,0:T(8,128)(2,1)S(1)} %get-tuple-element.52), channel_id=1, source_target_pairs={{0,0},{8,16},{16,8},{24,24},{1,1},{9,17},{17,9},{25,25},{2,2},{10,... | collective-permute-start | bytes 786440 | tf_op jit(solution)/shard_map/ppermute | solution.py:487
  67.6 8.1 %collective-permute-start.15 = (bf16[1024,128]{1,0:T(8,128)(2,1)S(1)}, bf16[1024,128]{1,0:T(8,128)(2,1)S(1)}, u32[]{:S(2)}, u32[]{:S(2)}) collective-permute-start(bf16[1024,128]{1,0:T(8,128)(2,1)S(1)} %get-tuple-element.53), channel_id=1, source_target_pairs={{0,4},{4,0},{1,5},{5,1},{2,6},{6,2},{3,7},{7,3},{8,12},{12,8},{9,1... | collective-permute-start | bytes 786440 | tf_op jit(solution)/shard_map/ppermute | solution.py:487
  68.2 3.0 %collective-permute-start.17 = (bf16[128,128]{1,0:T(8,128)(2,1)S(1)}, bf16[128,128]{1,0:T(8,128)(2,1)S(1)}, u32[]{:S(2)}, u32[]{:S(2)}) collective-permute-start(bf16[128,128]{1,0:T(8,128)(2,1)S(1)} %get-tuple-element.54), channel_id=1, source_target_pairs={{0,0},{1,2},{2,1},{3,3},{4,4},{5,6},{6,5},{7,7},{8,8},{9,10},{10,9... | collective-permute-start | bytes 98312 | tf_op jit(solution)/shard_map/ppermute | solution.py:488
  68.8 4.3 %collective-permute-start.16 = (bf16[128,128]{1,0:T(8,128)(2,1)S(1)}, bf16[128,128]{1,0:T(8,128)(2,1)S(1)}, u32[]{:S(2)}, u32[]{:S(2)}) collective-permute-start(bf16[128,128]{1,0:T(8,128)(2,1)S(1)} %get-tuple-element.54), channel_id=1, source_target_pairs={{0,1},{1,0},{2,3},{3,2},{4,5},{5,4},{6,7},{7,6},{8,9},{9,8},{10,11... | collective-permute-start | bytes 98312 | tf_op jit(solution)/shard_map/ppermute | solution.py:488

commit v5 on v4

--- a/solution.py
+++ b/solution.py
@@ -32,13 +32,12 @@
     return pltpu.CompilerParams(vmem_limit_bytes=mebibytes * 1024 * 1024)
 
 
-def trace_kernel(stride, block, field_ref, cell_ref, out_ref, field, cell_v, near, pick, rsum, sems):
+def trace_kernel(stride, block, field_ref, cell_ref, out_ref, field, cell_v, tall, near, place, picked, sems):
     sides, rows, lanes = field.shape
     slots = cell_ref.shape[3]
     per_row = lanes // stride
-    group = 16
-    width = group * per_row
-    parts = rows // group
+    width = near.shape[0]
+    parts = slots // width
     cell_copy = pltpu.make_async_copy(cell_ref, cell_v, sems.at[sides // block])
     cell_copy.start()
     copies = []
@@ -47,8 +46,6 @@
         copies.append(pltpu.make_async_copy(field_ref.at[span], field.at[span], sems.at[step]))
         copies[-1].start()
 
-    shape = (block, block * group)
-    rsum[...] = (iota(shape, 1) // group == iota(shape, 0)).astype(BF)
     cell_copy.wait()
     cell = cell_v[0, 0]
     run = cell // stride
@@ -58,26 +55,36 @@
     hit = iota((width, slots), 0) == run % width
     near[...] = hit.astype(BF)
     digits = jnp.sum(jnp.where(hit, digit.astype(F32), 0.0), axis=1, keepdims=True)
-    digits = digits.astype(jnp.int32)
+    digits = jnp.broadcast_to(digits, (width, 128)).T[0:8].astype(jnp.int32)
+    first = iota((8, width), 1) % per_row * stride
     for part in range(parts):
-        offset = digits // stride**part % stride
-        place = iota((width, lanes), 0) % per_row * stride + offset
-        pick[part] = (iota((width, lanes), 1) == place).astype(BF)
-
-    shape = (block * group, width)
-    own = iota(shape, 0) % group == iota(shape, 1) // per_row
-    picked = [[] for _ in range(parts)]
+        place[:, part * width : (part + 1) * width] = first + digits // stride**part % stride
+
+    together = 128 // per_row
+    group = iota((8, 128), 1) // per_row
     for step in range(sides // block):
         copies[step].wait()
-        for part in range(parts):
-            values = field[step * block : (step + 1) * block, part * group : (part + 1) * group, :]
-            spread = dot_nt(values.reshape(block * group, lanes), pick[part])
-            spread = jnp.where(own, spread, 0.0).astype(BF)
-            picked[part].append(dot(rsum[...], spread).astype(BF))
+        span = field[step * block : (step + 1) * block]
+        tall[...] = span.reshape(block * rows, lanes).astype(F32)
+
+        @pl.loop(0, block // 8)
+        def _(batch):
+            for tile in range(rows // together):
+                cols = slice(tile * 128, (tile + 1) * 128)
+                where = place[:, cols]
+                found = None
+                for row in range(together):
+                    start = batch * 8 * rows + tile * together + row
+                    line = tall[pl.ds(start, 8, stride=rows), :]
+                    line = jnp.take_along_axis(line, where, axis=1)
+                    found = line if found is None else jnp.where(group == row, line, found)
+                at = pl.multiple_of(step * block + batch * 8, 8)
+                picked[pl.ds(at, 8), cols] = found
+
     total = jnp.zeros((sides, slots), F32)
     for part in range(parts):
-        placed = dot(jnp.concatenate(picked[part], axis=0), near[...])
-        total = jnp.where(run // width == part, placed, total)
+        sorted_runs = picked[:, part * width : (part + 1) * width].astype(BF)
+        total = jnp.where(run // width == part, dot(sorted_runs, near[...]), total)
     out_ref[...] = total.T.astype(BF)
 
 
@@ -85,7 +92,7 @@
     sides, rows, lanes = field.shape
     slots = trace_cell.shape[3]
     stride = rows * lanes // slots
-    width = 16 * lanes // stride
+    width = min(slots, 256)
     hbm = pl.BlockSpec(memory_space=pltpu.HBM)
     return pl.pallas_call(
         functools.partial(trace_kernel, stride, block),
@@ -95,9 +102,10 @@
         scratch_shapes=[
             pltpu.VMEM(field.shape, BF),
             pltpu.VMEM(trace_cell.shape, jnp.int32),
+            pltpu.VMEM((block * rows, lanes), F32),
             pltpu.VMEM((width, slots), BF),
-            pltpu.VMEM((slots // width, width, lanes), BF),
-            pltpu.VMEM((block, block * 16), BF),
+            pltpu.VMEM((8, slots), jnp.int32),
+            pltpu.VMEM((sides, slots), F32),
             pltpu.SemaphoreType.DMA((sides // block + 1,)),
         ],
         compiler_params=params(62),
@@ -119,40 +127,37 @@
     return copies
 
 
-def surface_kernel(gzs, cols, *refs):
-    *parts, held, out_ref = refs
-    sides = parts[0].shape[1]
-    total = None
+def surface_kernel(direct, *refs):
+    *ins, total = refs
+    outs = ins[len(ins) - direct :]
+    *parts, held = ins[: len(ins) - direct]
+    value = None
     for key, part in enumerate(parts):
         term = dot(held[key], part[...])
-        total = term if total is None else total + term
-    turned = total.T
-    lines = total.shape[0]
-    if out_ref.shape[2] != sides or lines // cols != sides:
-        out_ref[...] = jnp.zeros_like(out_ref)
-    s_count, l_count, f_count = sides // gzs, lines // cols, lines // (cols * gzs)
-    for c in range(cols):
-        for g in range(gzs):
-            dest = c * gzs + g
-            out_ref[dest, :s_count, :l_count] = turned[
-                g * s_count : (g + 1) * s_count, c * l_count : (c + 1) * l_count
-            ].astype(out_ref.dtype)
-            out_ref[dest, s_count : s_count + f_count, :sides] = total[
-                dest * f_count : (dest + 1) * f_count
-            ].astype(out_ref.dtype)
-
-
-def surface(parts, held, dtype):
-    gzs, cols = lax.axis_size("gz"), lax.axis_size("col")
+        value = term if value is None else value + term
+    if direct == 1:
+        outs[0][...] = value
+        return
+    total[...] = value
+    count = outs[0].shape[0]
+    me = lax.axis_index("col") * lax.axis_size("gz") + lax.axis_index("gz")
+    for key, out in enumerate(outs):
+        start = pl.multiple_of(jnp.bitwise_xor(me, key) * count, 8)
+        out[...] = total[pl.ds(start, count), :]
+
+
+def surface(parts, held):
+    owners = lax.axis_size("gz") * lax.axis_size("col")
     sides = parts[0].shape[1]
     lines = held.shape[1]
-    depth = sides // gzs + lines // (cols * gzs)
-    shape = (cols * gzs, depth, max(sides, lines // cols))
+    few = owners <= 8 and owners & (owners - 1) == 0 and lines // owners % 8 == 0
+    count = owners if few else 1
     return pl.pallas_call(
-        functools.partial(surface_kernel, gzs, cols),
+        functools.partial(surface_kernel, count),
         in_specs=[WHOLE] * (len(parts) + 1),
-        out_specs=WHOLE,
-        out_shape=jax.ShapeDtypeStruct(shape, dtype),
+        out_specs=[WHOLE] * count,
+        out_shape=[jax.ShapeDtypeStruct((lines // count, sides), F32)] * count,
+        scratch_shapes=[pltpu.VMEM((lines, sides), F32)],
         compiler_params=params(),
         cost_estimate=pl.CostEstimate(
             flops=2 * sides * held.size, bytes_accessed=2 * held.size, transcendentals=0
@@ -160,20 +165,55 @@
     )(*parts, held)
 
 
-def swaps(peers):
-    turns = []
-    for turn in (0, 1):
-        partner = {i: i + 1 if i % 2 == turn else i - 1 for i in range(peers)}
-        pairs = [(i, j if 0 <= j < peers else i) for i, j in partner.items()]
-        if any(i != j for i, j in pairs):
-            turns.append(pairs)
-    return turns
+def send_to_owners(shares, late):
+    owners = lax.axis_size("gz") * lax.axis_size("col")
+    if len(shares) == 1:
+        share = shares[0]
+        share = share.reshape(owners, share.shape[0] // owners, share.shape[1])
+        return [lax.all_to_all(share, ("col", "gz"), split_axis=0, concat_axis=0, tiled=True)], late
+    got = [shares[0]]
+    order = sorted(range(1, owners), key=lambda key: -(key % lax.axis_size("gz")))
+    for place, key in enumerate(order):
+        if place == len(order) // 2:
+            held, late = lax.optimization_barrier(([shares[k] for k in order[place:]], late))
+            shares = [held[order.index(k) - place] if k in order[place:] else s for k, s in enumerate(shares)]
+        pairs = [(i, i ^ key) for i in range(owners)]
+        got.append(lax.ppermute(shares[key], ("col", "gz"), pairs))
+    return got, late
+
+
+def turns(axis):
+    return 1 if lax.axis_size(axis) == 2 else 2
+
+
+def partner(index, turn):
+    return jnp.where(index % 2 == turn, index + 1, index - 1)
 
 
 def has_neighbour(axis, turn):
-    index = lax.axis_index(axis)
-    other = jnp.where(index % 2 == turn, index + 1, index - 1)
+    other = partner(lax.axis_index(axis), turn)
     return (other >= 0) & (other < lax.axis_size(axis))
+
+
+def swap(value, axis, turn):
+    axes = ("row", "col", "gz")
+    sizes = [lax.axis_size(name) for name in axes]
+    along = axes.index(axis)
+    spare = 0 if axis == "gz" else 2
+    pairs = []
+    for r in range(sizes[0]):
+        for c in range(sizes[1]):
+            for g in range(sizes[2]):
+                here = [r, c, g]
+                there = [r, c, g]
+                there[along] += 1 if here[along] % 2 == turn else -1
+                if not 0 <= there[along] < sizes[along]:
+                    there[along] = here[along]
+                    if here[spare] ^ 1 < sizes[spare]:
+                        there[spare] ^= 1
+                flat = [(at[0] * sizes[1] + at[1]) * sizes[2] + at[2] for at in (here, there)]
+                pairs.append(tuple(flat))
+    return lax.ppermute(value, axes, pairs)
 
 
 class Shape:
@@ -185,9 +225,9 @@
         self.block = min(sides, 32)
         self.half = self.block // 2
         self.half_rows = self.half * self.cells
-        self.faces = [("row", i) for i in range(len(swaps(lax.axis_size("row"))))]
-        self.faces += [("col", i) for i in range(len(swaps(lax.axis_size("col"))))]
-        self.ends = len(swaps(lax.axis_size("gz")))
+        self.faces = [("col", i) for i in range(turns("col"))]
+        self.faces += [("row", i) for i in reversed(range(turns("row")))]
+        self.ends = turns("gz")
 
     def face_len(self, face):
         return self.y if face[0] == "row" else self.x
@@ -312,22 +352,29 @@
     )(field, block)
 
 
-def sweep_kernel(shape, with_flux, last, *refs):
+def sweep_kernel(shape, recvs, fluxes, by_xor, *refs):
+    with_flux, last = recvs > 0, fluxes > 0
     refs = list(refs)
     take = lambda count: [refs.pop(0) for _ in range(count)]
     field_ref, load_ref, coef_ref = take(3)
     halo_refs = take(len(shape.faces))
     end_refs = take(shape.ends)
     if with_flux:
-        recv_ref, cell_ref = take(2)
+        recv_refs = take(recvs)
+        (cell_ref,) = take(1)
+    flux_refs = take(fluxes)
     (out_ref,) = take(1)
-    if not last:
+    if last:
+        (flux_ref,) = take(1)
+    else:
         face_refs = take(len(shape.faces))
         (z_ref,) = take(1)
     if with_flux:
-        source_ref, flux_ref = take(2)
+        source_ref, owned_ref = take(2)
     weight, near_m, line_m, lines = take(4)
-    if not last:
+    if last:
+        window, turned = take(2)
+    else:
         tall, ends_m, rsum = take(3)
     if with_flux:
         phi, cell_m, placed = take(3)
@@ -351,16 +398,28 @@
         dims = (2 * cells, lanes)
         edge = jnp.where(iota(dims, 0) < cells, lanes - 1, 0)
         line_m[2 * lanes :, :] = twice((iota(dims, 1) == edge).astype(F32)).astype(BF)
-        if not last:
+        if last:
+            group = lax.axis_index("gz")
+            count = flux_refs[0].shape[0]
+            for key, ref in enumerate(flux_refs):
+                place = jnp.bitwise_xor(group, key) if by_xor else key
+                window[pl.ds(place * count, count), :] = ref[...]
+            turned[...] = window[...].T
+            count = flux_ref.shape[0]
+            flux_ref[...] = turned[pl.ds(pl.multiple_of(group * count, count), count), :]
+        else:
             build_out(shape, ends_m, rsum)
         if with_flux:
-            total = recv_ref[0].astype(F32)
-            for peer in range(1, recv_ref.shape[0]):
-                total = total + recv_ref[peer].astype(F32)
-            s_count, l_count = flux_ref.shape
             slots = cell_ref.shape[3]
-            flux_ref[...] = total[:s_count, :l_count]
-            owned = total[s_count : s_count + slots, : shape.sides]
+            if recvs == 1:
+                owned = recv_refs[0][0]
+                for peer in range(1, recv_refs[0].shape[0]):
+                    owned = owned + recv_refs[0][peer]
+            else:
+                owned = recv_refs[0][...]
+                for ref in recv_refs[1:]:
+                    owned = owned + ref[...]
+            owned_ref[...] = owned
             high = owned.astype(BF).astype(F32)
             both = jnp.concatenate([high, owned - high], axis=0)
             phi[...] = both.T
@@ -434,10 +493,9 @@
             emit_faces(shape, at, fresh, tall, face_refs, z_ref, ends_m, rsum)
 
 
-def sweep(shape, field, load, coef, halos, recv=None, flux_cell=None, last=False):
-    with_flux = recv is not None
+def sweep(shape, field, load, coef, halos, recv=(), flux_cell=None, flux=(), by_xor=True, last=False):
     lanes, cells = shape.lanes, shape.cells
-    operands = [field, load, coef, *halos]
+    operands = [field, load, coef, *halos, *recv]
     out_shapes = [jax.ShapeDtypeStruct(field.shape, BF)]
     scratch = [
         pltpu.VMEM(coef.shape, F32),
@@ -445,28 +503,40 @@
         pltpu.VMEM((2 * lanes + 4 * cells, 2 * lanes), BF),
         pltpu.VMEM((shape.half_rows, 2 * lanes), F32),
     ]
-    if not last:
+    if last:
+        operands += flux
+        gzs = len(flux)
+        slots = flux[0].shape[0]
+        flux_shape = (shape.sides // gzs, slots * gzs)
+        out_shapes.append(jax.ShapeDtypeStruct(flux_shape, F32))
+        scratch += [
+            pltpu.VMEM((slots * gzs, shape.sides), F32),
+            pltpu.VMEM((shape.sides, slots * gzs), F32),
+        ]
+    else:
         out_shapes += face_outputs(shape)
         scratch += face_scratch(shape)
-    if with_flux:
+    if recv:
         slots = flux_cell.shape[3]
-        gzs = lax.axis_size("gz")
-        operands += [recv, flux_cell]
+        operands.append(flux_cell)
         out_shapes += [
             jax.ShapeDtypeStruct(field.shape, BF),
-            jax.ShapeDtypeStruct((shape.sides // gzs, slots * gzs), F32),
+            jax.ShapeDtypeStruct((slots, shape.sides), F32),
         ]
         scratch += [
             pltpu.VMEM((shape.sides, 2 * slots), F32),
             pltpu.VMEM((2 * lanes, 4 * slots), BF),
             pltpu.VMEM((shape.half_rows, 2 * lanes), F32),
         ]
-    steps = max(1, shape.sides // (2 * shape.block)) if last else 1
+    steps = shape.sides // shape.block if last else 1
     out_specs = [WHOLE] * len(out_shapes)
     if last:
-        out_specs = [pl.BlockSpec((field.shape[0] // steps, lanes), lambda i: (i, 0))]
+        out_specs = [
+            pl.BlockSpec((field.shape[0] // steps, lanes), lambda i: (i, 0)),
+            pl.BlockSpec(flux_shape, lambda i: (0, 0)),
+        ]
     return pl.pallas_call(
-        functools.partial(sweep_kernel, shape, with_flux, last),
+        functools.partial(sweep_kernel, shape, len(recv), len(flux), by_xor),
         grid=(steps,),
         in_specs=[WHOLE] * len(operands),
         out_specs=out_specs,
@@ -481,26 +551,32 @@
 
 def exchange(shape, faces):
     *cut, ends = faces
-    halos = {}
-    for face, value in sorted(zip(shape.faces, cut), key=lambda item: item[0][0]):
-        pairs = swaps(lax.axis_size(face[0]))[face[1]]
-        halos[face] = lax.ppermute(value, face[0], pairs)
-    tips = [lax.ppermute(ends, "gz", pairs) for pairs in swaps(lax.axis_size("gz"))]
-    return [halos[face] for face in shape.faces] + tips
-
-
-def xor_gather(value, axis, hidden):
-    peers = lax.axis_size(axis)
-    held = {0: value}
+    halos = [swap(value, *face) for face, value in zip(shape.faces, cut)]
+    return halos + [swap(ends, "gz", turn) for turn in range(shape.ends)]
+
+
+def row_gather(trace, faces):
+    peers = lax.axis_size("row")
+    held = {0: trace}
     bit = peers // 2
     while bit:
-        swap = [(i, i ^ bit) for i in range(peers)]
-        fresh = {key ^ bit: lax.ppermute(held[key], axis, swap) for key in sorted(held, reverse=True)}
+        pairs = [(i, i ^ bit) for i in range(peers)]
+        fresh = {key ^ bit: lax.ppermute(held[key], "row", pairs) for key in sorted(held, reverse=True)}
+        if bit == peers // 2:
+            held, fresh, _ = lax.optimization_barrier((held, fresh, faces))
         held.update(fresh)
-        if bit == peers // 2:
-            held[bit], hidden = lax.optimization_barrier((held[bit], hidden))
         bit //= 2
-    return [held[key] for key in range(peers)], hidden
+    return [held[key] for key in range(peers)]
+
+
+def gz_gather(value):
+    peers = lax.axis_size("gz")
+    if peers & (peers - 1):
+        return list(lax.all_gather(value, "gz")), False
+    got = [value]
+    for key in range(1, peers):
+        got.append(lax.ppermute(value, "gz", [(i, i ^ key) for i in range(peers)]))
+    return got, True
 
 
 def per_device(volume_field, volume_load, coefficient, surface_block, trace_cell, flux_cell):
@@ -514,17 +590,20 @@
     slots = trace_cell.shape[3]
     trace = traces(volume_field.reshape(sides, cells, lanes), trace_cell, min(32, sides))
     *faces, held = first_faces(shape, field, surface_block, slots)
-    parts, _ = xor_gather(trace, "row", faces)
+    parts = row_gather(trace, faces)
     halos = exchange(shape, faces)
-    parts, halos = lax.optimization_barrier((parts, halos))
-    sent = surface(parts, held, F32)
-    recv = lax.all_to_all(sent, ("col", "gz"), split_axis=0, concat_axis=0, tiled=True)
-
-    current, *faces, source, surface_flux = sweep(
+    early = len([face for face in shape.faces if face[0] == "col"])
+    parts, halos[early:] = lax.optimization_barrier((parts, halos[early:]))
+    recv, halos[:early] = send_to_owners(surface(parts, held), halos[:early])
+
+    current, *faces, source, owned = sweep(
         shape, field, load, coef, halos, recv=recv, flux_cell=flux_cell
     )
     current, *faces = sweep(shape, current, source, coef, exchange(shape, faces))
-    (current,) = sweep(shape, current, source, coef, exchange(shape, faces), last=True)
+    flux, by_xor = gz_gather(owned)
+    current, surface_flux = sweep(
+        shape, current, source, coef, exchange(shape, faces), flux=flux, by_xor=by_xor, last=True
+    )
     return current.reshape(volume_field.shape), surface_flux
 
 

time: 80 us -> 82.4 us (1.030)
  blocking collectives: 14.1 us -> 0 us
  waiting for transfers between devices: 14.5 us -> 26.1 us
  starting transfers between devices: 21.8 us -> 29 us
  Pallas kernels: 28 us -> 26.4 us
    all_to_all x1 -> x0, blocking collectives: 14.1 us -> none  [per_device(): lax.all_to_all(sent, ('col', 'gz'), split_axis=0, concat_axis=0, tiled=True)]
    ppermute x18 -> x28, waiting for transfers between devices: 14.5 us -> 26.1 us  [the longest x15 12.5 us: swap(): return lax.ppermute(value, axes, pairs)]
    ppermute x18 -> x28, starting transfers between devices: 21.8 us -> 29 us  [the longest x7 11.1 us: send_to_owners(): got.append(lax.ppermute(shares[key], ('col', 'gz'), pairs))]
    pallas_call x1, Pallas kernels: 7.5 us -> 6.07 us  [traces(): pl.pallas_call(functools.partial(trace_kernel, stride, block), in_specs=[...]
  transfers between devices with their start and end apart: 18 -> 28, of which waited for: 5 -> 8; matrix products, arithmetic and copies ran while one was open for 0% -> 0% of each run, Pallas kernels for 5% -> 6%
where the time goes in v5:
time: 82.4 us; the launch traced here: 82.2 us
  starting transfers between devices  29 us (35%)
  Pallas kernels  26.4 us (32%)
  waiting for transfers between devices  26.1 us (32%)
    pallas_call x3, Pallas kernels, sweep(): pl.pallas_call(functools.partial(sweep_kernel, shape, len(recv), len(flux...  15.6 us
    ppermute x15, waiting for transfers between devices, swap(): return lax.ppermute(value, axes, pairs)  12.5 us
    ppermute x7, starting transfers between devices, send_to_owners(): got.append(lax.ppermute(shares[key], ('col', 'gz'), pairs))  11.1 us
    ppermute x15, starting transfers between devices, swap(): return lax.ppermute(value, axes, pairs)  10.6 us
    ppermute x3, waiting for transfers between devices, gz_gather(): got.append(lax.ppermute(value, 'gz', [(i, i ^ key) for i in range(peers)]))  8.69 us
    pallas_call x1, Pallas kernels, traces(): pl.pallas_call(functools.partial(trace_kernel, stride, block), in_specs=[...  6.07 us
    ppermute x7, waiting for transfers between devices, send_to_owners(): got.append(lax.ppermute(shares[key], ('col', 'gz'), pairs))  4.92 us
    pallas_call x1, Pallas kernels, first_faces(): pl.pallas_call(functools.partial(faces_kernel, shape, slots), in_specs=[W...  3.95 us
  transfers between devices with their start and end apart: 28, of which 8 were waited for; matrix products, arithmetic and copies ran while one was open for 0% of the time, Pallas kernels for 6%

profile of v5, /device:TPU:0, one launch (start us, length us, event | category | flops | bytes accessed | tf_op | source)
XLA Modules:
  0.0 82.2 jit_solution(4099300425469193700)
XLA Ops:
  0.6 6.1 %shard_map.77.refs_0_ = bf16[1024,128]{1,0:T(8,128)(2,1)} custom-call(bf16[128,64,128]{2,1,0:T(8,128)(2,1)} %bitcast.5, s32[1,1,1,1024]{3,2,1,0:T(1,128)} %cell_ref.1), custom_call_target="tpu_custom_call" | custom-call | flops 536870912 | bytes 2097152 | tf_op jit(solution)/shard_map/pallas_call | solution.py:97
  6.7 3.0 %collective-permute-start = (bf16[1024,128]{1,0:T(8,128)(2,1)}, bf16[1024,128]{1,0:T(8,128)(2,1)S(1)}, u32[]{:S(2)}, u32[]{:S(2)}) collective-permute-start(bf16[1024,128]{1,0:T(8,128)(2,1)} %shard_map.77.refs_0_), channel_id=1, source_target_pairs={{0,16},{8,24},{16,0},{24,8},{1,17},{9,25},{17,1},{25,9},{2,18},{10... | collective-permute-start | bytes 786440 | tf_op jit(solution)/shard_map/ppermute | solution.py:564
  9.7 4.0 %shard_map.78 = (bf16[1024,128]{1,0:T(8,128)(2,1)S(1)}, bf16[1024,128]{1,0:T(8,128)(2,1)S(1)}, bf16[1024,128]{1,0:T(8,128)(2,1)S(1)}, bf16[128,128]{1,0:T(8,128)(2,1)S(1)}, bf16[4,256,1024]{2,1,0:T(8,128)(2,1)S(1)}) custom-call(bf16[8192,128]{1,0:T(8,128)(2,1)} %bitcast.6, bf16[256,16384]{1,0:T(8,128)(2,1)} %block_ref.1), custom_call_target="tpu_custom_call" | custom-call | flops 134217728 | bytes 4194304 | tf_op jit(solution)/shard_map/pallas_call | solution.py:342
  13.7 1.6 %collective-permute-start.5 = (bf16[128,128]{1,0:T(8,128)(2,1)S(1)}, bf16[128,128]{1,0:T(8,128)(2,1)S(1)}, u32[]{:S(2)}, u32[]{:S(2)}) collective-permute-start(bf16[128,128]{1,0:T(8,128)(2,1)S(1)} %get-tuple-element.47), channel_id=1, source_target_pairs={{0,1},{1,0},{2,3},{3,2},{4,5},{5,4},{6,7},{7,6},{8,9},{9,8},{10,11... | collective-permute-start | bytes 98312 | tf_op jit(solution)/shard_map/ppermute | solution.py:216
  15.4 3.2 %collective-permute-start.3 = (bf16[1024,128]{1,0:T(8,128)(2,1)S(1)}, bf16[1024,128]{1,0:T(8,128)(2,1)S(1)}, u32[]{:S(2)}, u32[]{:S(2)}) collective-permute-start(bf16[1024,128]{1,0:T(8,128)(2,1)S(1)} %get-tuple-element.45), channel_id=1, source_target_pairs={{0,1},{1,0},{2,3},{3,2},{4,5},{5,4},{6,7},{7,6},{8,16},{9,17},{10,... | collective-permute-start | bytes 786440 | tf_op jit(solution)/shard_map/ppermute | solution.py:216
  18.5 0.5 collective-permute-start.1
  19.1 1.5 %collective-permute-start.7 = (bf16[1024,128]{1,0:T(8,128)(2,1)S(1)}, bf16[1024,128]{1,0:T(8,128)(2,1)S(1)}, u32[]{:S(2)}, u32[]{:S(2)}) collective-permute-start(bf16[1024,128]{1,0:T(8,128)(2,1)S(1)} %get-tuple-element.44), channel_id=1, source_target_pairs={{0,4},{1,5},{2,6},{3,7},{4,0},{5,1},{6,2},{7,3},{8,12},{9,13},{10,... | collective-permute-start | bytes 786440 | tf_op jit(solution)/shard_map/ppermute | solution.py:216
  20.6 2.2 %collective-permute-done.3.refs_4_ = bf16[1024,128]{1,0:T(8,128)(2,1)S(1)} collective-permute-done((bf16[1024,128]{1,0:T(8,128)(2,1)S(1)}, bf16[1024,128]{1,0:T(8,128)(2,1)S(1)}, u32[]{:S(2)}, u32[]{:S(2)}) %collective-permute-start.3) | collective-permute-done | bytes 262176 | tf_op jit(solution)/shard_map/ppermute | solution.py:216
  22.9 0.7 shard_map.79
  23.6 4.2 %collective-permute-done.7.refs_3_ = bf16[1024,128]{1,0:T(8,128)(2,1)S(1)} collective-permute-done((bf16[1024,128]{1,0:T(8,128)(2,1)S(1)}, bf16[1024,128]{1,0:T(8,128)(2,1)S(1)}, u32[]{:S(2)}, u32[]{:S(2)}) %collective-permute-start.7) | collective-permute-done | bytes 262176 | tf_op jit(solution)/shard_map/ppermute | solution.py:216
  27.8 2.2 %collective-permute-start.11 = (f32[32,128]{1,0:T(8,128)S(1)}, f32[32,128]{1,0:T(8,128)S(1)}, u32[]{:S(2)}, u32[]{:S(2)}) collective-permute-start(f32[32,128]{1,0:T(8,128)S(1)} %get-tuple-element.68), channel_id=1, source_target_pairs={{0,6},{1,7},{2,4},{3,5},{4,2},{5,3},{6,0},{7,1},{8,14},{9,15},{10,... | collective-permute-start | bytes 49160 | tf_op jit(solution)/shard_map/ppermute | solution.py:181
  30.0 1.6 %collective-permute-start.12 = (f32[32,128]{1,0:T(8,128)S(1)}, f32[32,128]{1,0:T(8,128)S(1)}, u32[]{:S(2)}, u32[]{:S(2)}) collective-permute-start(f32[32,128]{1,0:T(8,128)S(1)} %get-tuple-element.69), channel_id=1, source_target_pairs={{0,1},{1,0},{2,3},{3,2},{4,5},{5,4},{6,7},{7,6},{8,9},{9,8},{10,11... | collective-permute-start | bytes 49160 | tf_op jit(solution)/shard_map/ppermute | solution.py:181
  31.5 0.4 collective-permute-start.13
  31.9 1.5 %collective-permute-start.14 = (f32[32,128]{1,0:T(8,128)S(1)}, f32[32,128]{1,0:T(8,128)S(1)}, u32[]{:S(2)}, u32[]{:S(2)}) collective-permute-start(f32[32,128]{1,0:T(8,128)S(1)} %get-tuple-element.71), channel_id=1, source_target_pairs={{0,4},{1,5},{2,6},{3,7},{4,0},{5,1},{6,2},{7,3},{8,12},{9,13},{10,... | collective-permute-start | bytes 49160 | tf_op jit(solution)/shard_map/ppermute | solution.py:181
  33.5 1.7 %collective-permute-start.10 = (f32[32,128]{1,0:T(8,128)S(1)}, f32[32,128]{1,0:T(8,128)S(1)}, u32[]{:S(2)}, u32[]{:S(2)}) collective-permute-start(f32[32,128]{1,0:T(8,128)S(1)} %get-tuple-element.67), channel_id=1, source_target_pairs={{0,2},{1,3},{2,0},{3,1},{4,6},{5,7},{6,4},{7,5},{8,10},{9,11},{10,... | collective-permute-start | bytes 49160 | tf_op jit(solution)/shard_map/ppermute | solution.py:181
  35.1 2.3 %collective-permute-start.8 = (f32[32,128]{1,0:T(8,128)S(1)}, f32[32,128]{1,0:T(8,128)S(1)}, u32[]{:S(2)}, u32[]{:S(2)}) collective-permute-start(f32[32,128]{1,0:T(8,128)S(1)} %get-tuple-element.65), channel_id=1, source_target_pairs={{0,3},{1,2},{2,1},{3,0},{4,7},{5,6},{6,5},{7,4},{8,11},{9,10},{10,... | collective-permute-start | bytes 49160 | tf_op jit(solution)/shard_map/ppermute | solution.py:181
  37.4 1.5 %collective-permute-start.9 = (f32[32,128]{1,0:T(8,128)S(1)}, f32[32,128]{1,0:T(8,128)S(1)}, u32[]{:S(2)}, u32[]{:S(2)}) collective-permute-start(f32[32,128]{1,0:T(8,128)S(1)} %get-tuple-element.66), channel_id=1, source_target_pairs={{0,7},{1,6},{2,5},{3,4},{4,3},{5,2},{6,1},{7,0},{8,15},{9,14},{10,... | collective-permute-start | bytes 49160 | tf_op jit(solution)/shard_map/ppermute | solution.py:181
  38.9 1.8 %collective-permute-done.8.refs_9_ = f32[32,128]{1,0:T(8,128)S(1)} collective-permute-done((f32[32,128]{1,0:T(8,128)S(1)}, f32[32,128]{1,0:T(8,128)S(1)}, u32[]{:S(2)}, u32[]{:S(2)}) %collective-permute-start.8) | collective-permute-done | bytes 16416 | tf_op jit(solution)/shard_map/ppermute | solution.py:181
  40.7 3.2 %collective-permute-done.9.refs_10_ = f32[32,128]{1,0:T(8,128)S(1)} collective-permute-done((f32[32,128]{1,0:T(8,128)S(1)}, f32[32,128]{1,0:T(8,128)S(1)}, u32[]{:S(2)}, u32[]{:S(2)}) %collective-permute-start.9) | collective-permute-done | bytes 16416 | tf_op jit(solution)/shard_map/ppermute | solution.py:181
  43.9 6.4 %shard_map.80 = (bf16[8192,128]{1,0:T(8,128)(2,1)S(1)}, bf16[1024,128]{1,0:T(8,128)(2,1)S(1)}, bf16[1024,128]{1,0:T(8,128)(2,1)S(1)}, bf16[1024,128]{1,0:T(8,128...) custom-call(bf16[8192,128]{1,0:T(8,128)(2,1)S(1)} %bitcast.7, ...), custom_call_target="tpu_custom_call" | custom-call | flops 805306368 | bytes 8388608 | tf_op jit(solution)/shard_map/pallas_call | solution.py:538
  50.2 0.5 collective-permute-start.15
  50.8 1.0 %collective-permute-start.17 = (bf16[1024,128]{1,0:T(8,128)(2,1)S(1)}, bf16[1024,128]{1,0:T(8,128)(2,1)S(1)}, u32[]{:S(2)}, u32[]{:S(2)}) collective-permute-start(bf16[1024,128]{1,0:T(8,128)(2,1)S(1)} %get-tuple-element.76), channel_id=1, source_target_pairs={{0,8},{1,9},{2,10},{3,11},{4,12},{5,13},{6,14},{7,15},{8,0},{9,1},... | collective-permute-start | bytes 786440 | tf_op jit(solution)/shard_map/ppermute | solution.py:216
  51.7 1.0 %collective-permute-start.18 = (bf16[128,128]{1,0:T(8,128)(2,1)S(1)}, bf16[128,128]{1,0:T(8,128)(2,1)S(1)}, u32[]{:S(2)}, u32[]{:S(2)}) collective-permute-start(bf16[128,128]{1,0:T(8,128)(2,1)S(1)} %get-tuple-element.77), channel_id=1, source_target_pairs={{0,1},{1,0},{2,3},{3,2},{4,5},{5,4},{6,7},{7,6},{8,9},{9,8},{10,11... | collective-permute-start | bytes 98312 | tf_op jit(solution)/shard_map/ppermute | solution.py:216
  53.0 4.8 %collective-permute-done.18.refs_6_ = bf16[128,128]{1,0:T(8,128)(2,1)S(1)} collective-permute-done((bf16[128,128]{1,0:T(8,128)(2,1)S(1)}, bf16[128,128]{1,0:T(8,128)(2,1)S(1)}, u32[]{:S(2)}, u32[]{:S(2)}) %collective-permute-start.18) | collective-permute-done | bytes 32800 | tf_op jit(solution)/shard_map/ppermute | solution.py:216
  57.8 5.7 %shard_map.81 = (bf16[8192,128]{1,0:T(8,128)(2,1)S(1)}, bf16[1024,128]{1,0:T(8,128)(2,1)S(1)}, bf16[1024,128]{1,0:T(8,128)(2,1)S(1)}, bf16[1024,128]{1,0:T(8,128)(2,1)S(1)}, bf16[128,128]{1,0:T(8,128)(2,1)S(1)}) custom-call(bf16[8192,128]{1,0:T(8,128)(2,1)S(1)} %get-tuple-element.72.refs_0_, bf16[8192,128]{1,0:T(8,128)(2,1)S(1)} %get-tuple-element.73.refs_1_, ...), custom_call_target="tpu_custom_call" | custom-call | flops 805306368 | bytes 8388608 | tf_op jit(solution)/shard_map/pallas_call | solution.py:538
  63.5 1.5 %collective-permute-start.20 = (bf16[1024,128]{1,0:T(8,128)(2,1)S(1)}, bf16[1024,128]{1,0:T(8,128)(2,1)S(1)}, u32[]{:S(2)}, u32[]{:S(2)}) collective-permute-start(bf16[1024,128]{1,0:T(8,128)(2,1)S(1)} %get-tuple-element.79), channel_id=1, source_target_pairs={{0,4},{1,5},{2,6},{3,7},{4,0},{5,1},{6,2},{7,3},{8,12},{9,13},{10,... | collective-permute-start | bytes 786440 | tf_op jit(solution)/shard_map/ppermute | solution.py:216
  65.0 2.0 %collective-permute-start.25 = (f32[32,128]{1,0:T(8,128)S(1)}, f32[32,128]{1,0:T(8,128)S(1)}, u32[]{:S(2)}, u32[]{:S(2)}) collective-permute-start(f32[32,128]{1,0:T(8,128)S(1)} %get-tuple-element.83.refs_8_), channel_id=1, source_target_pairs={{0,1},{1,0},{2,3},{3,2},{4,5},{5,4},{6,7},{7,6},{8,9},{9,8},{10,11... | collective-permute-start | bytes 49160 | tf_op jit(solution)/shard_map/ppermute | solution.py:578
  67.2 4.6 %collective-permute-done.25.refs_9_ = f32[32,128]{1,0:T(8,128)S(1)} collective-permute-done((f32[32,128]{1,0:T(8,128)S(1)}, f32[32,128]{1,0:T(8,128)S(1)}, u32[]{:S(2)}, u32[]{:S(2)}) %collective-permute-start.25) | collective-permute-done | bytes 16416 | tf_op jit(solution)/shard_map/ppermute | solution.py:578
  71.8 1.6 %collective-permute-start.27 = (f32[32,128]{1,0:T(8,128)S(1)}, f32[32,128]{1,0:T(8,128)S(1)}, u32[]{:S(2)}, u32[]{:S(2)}) collective-permute-start(f32[32,128]{1,0:T(8,128)S(1)} %get-tuple-element.83.refs_8_), channel_id=1, source_target_pairs={{0,3},{1,2},{2,1},{3,0},{4,7},{5,6},{6,5},{7,4},{8,11},{9,10},{10,... | collective-permute-start | bytes 49160 | tf_op jit(solution)/shard_map/ppermute | solution.py:578
  73.3 4.1 %collective-permute-done.27.refs_11_ = f32[32,128]{1,0:T(8,128)S(1)} collective-permute-done((f32[32,128]{1,0:T(8,128)S(1)}, f32[32,128]{1,0:T(8,128)S(1)}, u32[]{:S(2)}, u32[]{:S(2)}) %collective-permute-start.27) | collective-permute-done | bytes 16416 | tf_op jit(solution)/shard_map/ppermute | solution.py:578
  77.4 1.2 %collective-permute-done.24.refs_7_ = bf16[128,128]{1,0:T(8,128)(2,1)S(1)} collective-permute-done((bf16[128,128]{1,0:T(8,128)(2,1)S(1)}, bf16[128,128]{1,0:T(8,128)(2,1)S(1)}, u32[]{:S(2)}, u32[]{:S(2)}) %collective-permute-start.24) | collective-permute-done | bytes 32800 | tf_op jit(solution)/shard_map/ppermute | solution.py:216
  78.6 3.6 %shard_map.82 = (bf16[8192,128]{1,0:T(8,128)(2,1)}, f32[32,128]{1,0:T(8,128)}) custom-call(bf16[8192,128]{1,0:T(8,128)(2,1)S(1)} %get-tuple-element.78.refs_0_, bf16[8192,128]{1,0:T(8,128)(2,1)S(1)} %get-tuple-element.73.refs_1_, f32[64,128]{1,0:T(8,128)S(1)} %bitcast.11, bf16[1024,128]{1,0:T(8,128)(2,1)S(1)} %collective-permute-done.20.refs_3_, ...), custom_call_target="tpu_custom_call" | custom-call | flops 805306368 | bytes 8388608 | tf_op jit(solution)/shard_map/pallas_call | solution.py:538
  (40 shorter events, 0.5 us)
Async XLA Ops:
  6.7 11.8 %collective-permute-start = (bf16[1024,128]{1,0:T(8,128)(2,1)}, bf16[1024,128]{1,0:T(8,128)(2,1)S(1)}, u32[]{:S(2)}, u32[]{:S(2)}) collective-permute-start(bf16[1024,128]{1,0:T(8,128)(2,1)} %shard_map.77.refs_0_), channel_id=1, source_target_pairs={{0,16},{8,24},{16,0},{24,8},{1,17},{9,25},{17,1},{25,9},{2,18},{10... | collective-permute-start | bytes 786440 | tf_op jit(solution)/shard_map/ppermute | solution.py:564
  9.7 34.1 %copy-start.1 = (bf16[128,8,8,128]{3,2,1,0:T(8,128)(2,1)S(1)}, bf16[128,8,8,128]{3,2,1,0:T(8,128)(2,1)}, u32[]{:S(2)}) copy-start(bf16[128,8,8,128]{3,2,1,0:T(8,128)(2,1)} %param.7) | copy-start | bytes 6291460
  13.7 30.2 %copy-start = (bf16[128,8,8,128]{3,2,1,0:T(8,128)(2,1)S(1)}, bf16[128,8,8,128]{3,2,1,0:T(8,128)(2,1)}, u32[]{:S(2)}) copy-start(bf16[128,8,8,128]{3,2,1,0:T(8,128)(2,1)} %param.6) | copy-start | bytes 6291460
  13.7 30.2 %copy-start.3 = (f32[8,8,128]{2,1,0:T(8,128)S(1)}, f32[8,8,128]{2,1,0:T(8,128)}, u32[]{:S(2)}) copy-start(f32[8,8,128]{2,1,0:T(8,128)} %param.8) | copy-start | bytes 98308
  13.7 30.1 %copy-start.4 = (s32[1,1,1,32]{3,2,1,0:T(1,128)S(1)}, s32[1,1,1,32]{3,2,1,0:T(1,128)}, u32[]{:S(2)}) copy-start(s32[1,1,1,32]{3,2,1,0:T(1,128)} %refs_16_.1) | copy-start | bytes 388
  13.7 5.3 %collective-permute-start.5 = (bf16[128,128]{1,0:T(8,128)(2,1)S(1)}, bf16[128,128]{1,0:T(8,128)(2,1)S(1)}, u32[]{:S(2)}, u32[]{:S(2)}) collective-permute-start(bf16[128,128]{1,0:T(8,128)(2,1)S(1)} %get-tuple-element.47), channel_id=1, source_target_pairs={{0,1},{1,0},{2,3},{3,2},{4,5},{5,4},{6,7},{7,6},{8,9},{9,8},{10,11... | collective-permute-start | bytes 98312 | tf_op jit(solution)/shard_map/ppermute | solution.py:216
  15.4 3.8 %collective-permute-start.6 = (bf16[128,128]{1,0:T(8,128)(2,1)S(1)}, bf16[128,128]{1,0:T(8,128)(2,1)S(1)}, u32[]{:S(2)}, u32[]{:S(2)}) collective-permute-start(bf16[128,128]{1,0:T(8,128)(2,1)S(1)} %get-tuple-element.47), channel_id=1, source_target_pairs={{0,8},{1,2},{2,1},{3,11},{4,12},{5,6},{6,5},{7,15},{8,0},{9,10},{1... | collective-permute-start | bytes 98312 | tf_op jit(solution)/shard_map/ppermute | solution.py:216
  15.4 7.5 %collective-permute-start.3 = (bf16[1024,128]{1,0:T(8,128)(2,1)S(1)}, bf16[1024,128]{1,0:T(8,128)(2,1)S(1)}, u32[]{:S(2)}, u32[]{:S(2)}) collective-permute-start(bf16[1024,128]{1,0:T(8,128)(2,1)S(1)} %get-tuple-element.45), channel_id=1, source_target_pairs={{0,1},{1,0},{2,3},{3,2},{4,5},{5,4},{6,7},{7,6},{8,16},{9,17},{10,... | collective-permute-start | bytes 786440 | tf_op jit(solution)/shard_map/ppermute | solution.py:216
  18.5 4.4 %collective-permute-start.4 = (bf16[1024,128]{1,0:T(8,128)(2,1)S(1)}, bf16[1024,128]{1,0:T(8,128)(2,1)S(1)}, u32[]{:S(2)}, u32[]{:S(2)}) collective-permute-start(bf16[1024,128]{1,0:T(8,128)(2,1)S(1)} %get-tuple-element.46), channel_id=1, source_target_pairs={{0,8},{1,9},{2,10},{3,11},{4,12},{5,13},{6,14},{7,15},{8,0},{9,1},... | collective-permute-start | bytes 786440 | tf_op jit(solution)/shard_map/ppermute | solution.py:216
  18.5 4.3 %collective-permute-start.1 = (bf16[1024,128]{1,0:T(8,128)(2,1)S(1)}, bf16[1024,128]{1,0:T(8,128)(2,1)S(1)}, u32[]{:S(2)}, u32[]{:S(2)}) collective-permute-start(bf16[1024,128]{1,0:T(8,128)(2,1)S(1)} %copy-done.2), channel_id=1, source_target_pairs={{0,8},{8,0},{16,24},{24,16},{1,9},{9,1},{17,25},{25,17},{2,10},{10... | collective-permute-start | bytes 786440 | tf_op jit(solution)/shard_map/ppermute | solution.py:564
  19.0 3.8 %collective-permute-start.2 = (bf16[1024,128]{1,0:T(8,128)(2,1)S(1)}, bf16[1024,128]{1,0:T(8,128)(2,1)S(1)}, u32[]{:S(2)}, u32[]{:S(2)}) collective-permute-start(bf16[1024,128]{1,0:T(8,128)(2,1)S(1)} %collective-permute-done.refs_2_), channel_id=1, source_target_pairs={{0,8},{8,0},{16,24},{24,16},{1,9},{9,1},{17,25},{25,17},{2,10},{10... | collective-permute-start | bytes 786440 | tf_op jit(solution)/shard_map/ppermute | solution.py:564
  19.1 8.7 %collective-permute-start.7 = (bf16[1024,128]{1,0:T(8,128)(2,1)S(1)}, bf16[1024,128]{1,0:T(8,128)(2,1)S(1)}, u32[]{:S(2)}, u32[]{:S(2)}) collective-permute-start(bf16[1024,128]{1,0:T(8,128)(2,1)S(1)} %get-tuple-element.44), channel_id=1, source_target_pairs={{0,4},{1,5},{2,6},{3,7},{4,0},{5,1},{6,2},{7,3},{8,12},{9,13},{10,... | collective-permute-start | bytes 786440 | tf_op jit(solution)/shard_map/ppermute | solution.py:216
  27.8 7.4 %collective-permute-start.11 = (f32[32,128]{1,0:T(8,128)S(1)}, f32[32,128]{1,0:T(8,128)S(1)}, u32[]{:S(2)}, u32[]{:S(2)}) collective-permute-start(f32[32,128]{1,0:T(8,128)S(1)} %get-tuple-element.68), channel_id=1, source_target_pairs={{0,6},{1,7},{2,4},{3,5},{4,2},{5,3},{6,0},{7,1},{8,14},{9,15},{10,... | collective-permute-start | bytes 49160 | tf_op jit(solution)/shard_map/ppermute | solution.py:181
  30.0 7.4 %collective-permute-start.12 = (f32[32,128]{1,0:T(8,128)S(1)}, f32[32,128]{1,0:T(8,128)S(1)}, u32[]{:S(2)}, u32[]{:S(2)}) collective-permute-start(f32[32,128]{1,0:T(8,128)S(1)} %get-tuple-element.69), channel_id=1, source_target_pairs={{0,1},{1,0},{2,3},{3,2},{4,5},{5,4},{6,7},{7,6},{8,9},{9,8},{10,11... | collective-permute-start | bytes 49160 | tf_op jit(solution)/shard_map/ppermute | solution.py:181
  31.5 7.4 %collective-permute-start.13 = (f32[32,128]{1,0:T(8,128)S(1)}, f32[32,128]{1,0:T(8,128)S(1)}, u32[]{:S(2)}, u32[]{:S(2)}) collective-permute-start(f32[32,128]{1,0:T(8,128)S(1)} %get-tuple-element.70), channel_id=1, source_target_pairs={{0,5},{1,4},{2,7},{3,6},{4,1},{5,0},{6,3},{7,2},{8,13},{9,12},{10,... | collective-permute-start | bytes 49160 | tf_op jit(solution)/shard_map/ppermute | solution.py:181
  31.9 7.0 %collective-permute-start.14 = (f32[32,128]{1,0:T(8,128)S(1)}, f32[32,128]{1,0:T(8,128)S(1)}, u32[]{:S(2)}, u32[]{:S(2)}) collective-permute-start(f32[32,128]{1,0:T(8,128)S(1)} %get-tuple-element.71), channel_id=1, source_target_pairs={{0,4},{1,5},{2,6},{3,7},{4,0},{5,1},{6,2},{7,3},{8,12},{9,13},{10,... | collective-permute-start | bytes 49160 | tf_op jit(solution)/shard_map/ppermute | solution.py:181
  33.5 5.5 %collective-permute-start.10 = (f32[32,128]{1,0:T(8,128)S(1)}, f32[32,128]{1,0:T(8,128)S(1)}, u32[]{:S(2)}, u32[]{:S(2)}) collective-permute-start(f32[32,128]{1,0:T(8,128)S(1)} %get-tuple-element.67), channel_id=1, source_target_pairs={{0,2},{1,3},{2,0},{3,1},{4,6},{5,7},{6,4},{7,5},{8,10},{9,11},{10,... | collective-permute-start | bytes 49160 | tf_op jit(solution)/shard_map/ppermute | solution.py:181
  35.1 5.5 %collective-permute-start.8 = (f32[32,128]{1,0:T(8,128)S(1)}, f32[32,128]{1,0:T(8,128)S(1)}, u32[]{:S(2)}, u32[]{:S(2)}) collective-permute-start(f32[32,128]{1,0:T(8,128)S(1)} %get-tuple-element.65), channel_id=1, source_target_pairs={{0,3},{1,2},{2,1},{3,0},{4,7},{5,6},{6,5},{7,4},{8,11},{9,10},{10,... | collective-permute-start | bytes 49160 | tf_op jit(solution)/shard_map/ppermute | solution.py:181
  37.4 6.4 %collective-permute-start.9 = (f32[32,128]{1,0:T(8,128)S(1)}, f32[32,128]{1,0:T(8,128)S(1)}, u32[]{:S(2)}, u32[]{:S(2)}) collective-permute-start(f32[32,128]{1,0:T(8,128)S(1)} %get-tuple-element.66), channel_id=1, source_target_pairs={{0,7},{1,6},{2,5},{3,4},{4,3},{5,2},{6,1},{7,0},{8,15},{9,14},{10,... | collective-permute-start | bytes 49160 | tf_op jit(solution)/shard_map/ppermute | solution.py:181
  50.2 7.6 %collective-permute-start.15 = (bf16[1024,128]{1,0:T(8,128)(2,1)S(1)}, bf16[1024,128]{1,0:T(8,128)(2,1)S(1)}, u32[]{:S(2)}, u32[]{:S(2)}) collective-permute-start(bf16[1024,128]{1,0:T(8,128)(2,1)S(1)} %get-tuple-element.74), channel_id=1, source_target_pairs={{0,4},{1,5},{2,6},{3,7},{4,0},{5,1},{6,2},{7,3},{8,12},{9,13},{10,... | collective-permute-start | bytes 786440 | tf_op jit(solution)/shard_map/ppermute | solution.py:216
  50.8 7.1 %collective-permute-start.16 = (bf16[1024,128]{1,0:T(8,128)(2,1)S(1)}, bf16[1024,128]{1,0:T(8,128)(2,1)S(1)}, u32[]{:S(2)}, u32[]{:S(2)}) collective-permute-start(bf16[1024,128]{1,0:T(8,128)(2,1)S(1)} %get-tuple-element.75), channel_id=1, source_target_pairs={{0,1},{1,0},{2,3},{3,2},{4,5},{5,4},{6,7},{7,6},{8,16},{9,17},{10,... | collective-permute-start | bytes 786440 | tf_op jit(solution)/shard_map/ppermute | solution.py:216
  50.8 7.1 %collective-permute-start.17 = (bf16[1024,128]{1,0:T(8,128)(2,1)S(1)}, bf16[1024,128]{1,0:T(8,128)(2,1)S(1)}, u32[]{:S(2)}, u32[]{:S(2)}) collective-permute-start(bf16[1024,128]{1,0:T(8,128)(2,1)S(1)} %get-tuple-element.76), channel_id=1, source_target_pairs={{0,8},{1,9},{2,10},{3,11},{4,12},{5,13},{6,14},{7,15},{8,0},{9,1},... | collective-permute-start | bytes 786440 | tf_op jit(solution)/shard_map/ppermute | solution.py:216
  51.7 6.1 %collective-permute-start.18 = (bf16[128,128]{1,0:T(8,128)(2,1)S(1)}, bf16[128,128]{1,0:T(8,128)(2,1)S(1)}, u32[]{:S(2)}, u32[]{:S(2)}) collective-permute-start(bf16[128,128]{1,0:T(8,128)(2,1)S(1)} %get-tuple-element.77), channel_id=1, source_target_pairs={{0,1},{1,0},{2,3},{3,2},{4,5},{5,4},{6,7},{7,6},{8,9},{9,8},{10,11... | collective-permute-start | bytes 98312 | tf_op jit(solution)/shard_map/ppermute | solution.py:216
  52.8 5.0 %collective-permute-start.19 = (bf16[128,128]{1,0:T(8,128)(2,1)S(1)}, bf16[128,128]{1,0:T(8,128)(2,1)S(1)}, u32[]{:S(2)}, u32[]{:S(2)}) collective-permute-start(bf16[128,128]{1,0:T(8,128)(2,1)S(1)} %get-tuple-element.77), channel_id=1, source_target_pairs={{0,8},{1,2},{2,1},{3,11},{4,12},{5,6},{6,5},{7,15},{8,0},{9,10},{1... | collective-permute-start | bytes 98312 | tf_op jit(solution)/shard_map/ppermute | solution.py:216
  63.5 15.1 %collective-permute-start.20 = (bf16[1024,128]{1,0:T(8,128)(2,1)S(1)}, bf16[1024,128]{1,0:T(8,128)(2,1)S(1)}, u32[]{:S(2)}, u32[]{:S(2)}) collective-permute-start(bf16[1024,128]{1,0:T(8,128)(2,1)S(1)} %get-tuple-element.79), channel_id=1, source_target_pairs={{0,4},{1,5},{2,6},{3,7},{4,0},{5,1},{6,2},{7,3},{8,12},{9,13},{10,... | collective-permute-start | bytes 786440 | tf_op jit(solution)/shard_map/ppermute | solution.py:216
  65.0 13.6 %collective-permute-start.21 = (bf16[1024,128]{1,0:T(8,128)(2,1)S(1)}, bf16[1024,128]{1,0:T(8,128)(2,1)S(1)}, u32[]{:S(2)}, u32[]{:S(2)}) collective-permute-start(bf16[1024,128]{1,0:T(8,128)(2,1)S(1)} %get-tuple-element.80), channel_id=1, source_target_pairs={{0,1},{1,0},{2,3},{3,2},{4,5},{5,4},{6,7},{7,6},{8,16},{9,17},{10,... | collective-permute-start | bytes 786440 | tf_op jit(solution)/shard_map/ppermute | solution.py:216
  65.0 13.6 %collective-permute-start.22 = (bf16[1024,128]{1,0:T(8,128)(2,1)S(1)}, bf16[1024,128]{1,0:T(8,128)(2,1)S(1)}, u32[]{:S(2)}, u32[]{:S(2)}) collective-permute-start(bf16[1024,128]{1,0:T(8,128)(2,1)S(1)} %get-tuple-element.81), channel_id=1, source_target_pairs={{0,8},{1,9},{2,10},{3,11},{4,12},{5,13},{6,14},{7,15},{8,0},{9,1},... | collective-permute-start | bytes 786440 | tf_op jit(solution)/shard_map/ppermute | solution.py:216
  65.0 6.7 %collective-permute-start.25 = (f32[32,128]{1,0:T(8,128)S(1)}, f32[32,128]{1,0:T(8,128)S(1)}, u32[]{:S(2)}, u32[]{:S(2)}) collective-permute-start(f32[32,128]{1,0:T(8,128)S(1)} %get-tuple-element.83.refs_8_), channel_id=1, source_target_pairs={{0,1},{1,0},{2,3},{3,2},{4,5},{5,4},{6,7},{7,6},{8,9},{9,8},{10,11... | collective-permute-start | bytes 49160 | tf_op jit(solution)/shard_map/ppermute | solution.py:578
  67.0 6.3 %collective-permute-start.26 = (f32[32,128]{1,0:T(8,128)S(1)}, f32[32,128]{1,0:T(8,128)S(1)}, u32[]{:S(2)}, u32[]{:S(2)}) collective-permute-start(f32[32,128]{1,0:T(8,128)S(1)} %get-tuple-element.83.refs_8_), channel_id=1, source_target_pairs={{0,2},{1,3},{2,0},{3,1},{4,6},{5,7},{6,4},{7,5},{8,10},{9,11},{10,... | collective-permute-start | bytes 49160 | tf_op jit(solution)/shard_map/ppermute | solution.py:578
  71.8 5.6 %collective-permute-start.27 = (f32[32,128]{1,0:T(8,128)S(1)}, f32[32,128]{1,0:T(8,128)S(1)}, u32[]{:S(2)}, u32[]{:S(2)}) collective-permute-start(f32[32,128]{1,0:T(8,128)S(1)} %get-tuple-element.83.refs_8_), channel_id=1, source_target_pairs={{0,3},{1,2},{2,1},{3,0},{4,7},{5,6},{6,5},{7,4},{8,11},{9,10},{10,... | collective-permute-start | bytes 49160 | tf_op jit(solution)/shard_map/ppermute | solution.py:578
  73.3 4.1 %collective-permute-start.23 = (bf16[128,128]{1,0:T(8,128)(2,1)S(1)}, bf16[128,128]{1,0:T(8,128)(2,1)S(1)}, u32[]{:S(2)}, u32[]{:S(2)}) collective-permute-start(bf16[128,128]{1,0:T(8,128)(2,1)S(1)} %get-tuple-element.82), channel_id=1, source_target_pairs={{0,1},{1,0},{2,3},{3,2},{4,5},{5,4},{6,7},{7,6},{8,9},{9,8},{10,11... | collective-permute-start | bytes 98312 | tf_op jit(solution)/shard_map/ppermute | solution.py:216
  77.4 1.2 %collective-permute-start.24 = (bf16[128,128]{1,0:T(8,128)(2,1)S(1)}, bf16[128,128]{1,0:T(8,128)(2,1)S(1)}, u32[]{:S(2)}, u32[]{:S(2)}) collective-permute-start(bf16[128,128]{1,0:T(8,128)(2,1)S(1)} %get-tuple-element.82), channel_id=1, source_target_pairs={{0,8},{1,2},{2,1},{3,11},{4,12},{5,6},{6,5},{7,15},{8,0},{9,10},{1... | collective-permute-start | bytes 98312 | tf_op jit(solution)/shard_map/ppermute | solution.py:216
  (1 other events, 8.8 us)

commit v6 on v5

--- a/solution.py
+++ b/solution.py
@@ -11,6 +11,10 @@
 BF = jnp.bfloat16
 F32 = jnp.float32
 WHOLE = pl.BlockSpec(memory_space=pltpu.VMEM)
+
+
+def aligned(start, unit):
+    return start if isinstance(start, int) else pl.multiple_of(start, unit)
 
 
 def iota(shape, dim):
@@ -127,36 +131,32 @@
     return copies
 
 
-def surface_kernel(direct, *refs):
-    *ins, total = refs
-    outs = ins[len(ins) - direct :]
-    *parts, held = ins[: len(ins) - direct]
+def surface_kernel(halves, *refs):
+    ins, total = refs[:-1], refs[-1]
+    outs = ins[len(ins) - halves :]
+    *parts, held = ins[: len(ins) - halves]
     value = None
     for key, part in enumerate(parts):
         term = dot(held[key], part[...])
         value = term if value is None else value + term
-    if direct == 1:
+    if halves == 1:
         outs[0][...] = value
         return
     total[...] = value
     count = outs[0].shape[0]
-    me = lax.axis_index("col") * lax.axis_size("gz") + lax.axis_index("gz")
+    mine = lax.axis_index("col")
     for key, out in enumerate(outs):
-        start = pl.multiple_of(jnp.bitwise_xor(me, key) * count, 8)
-        out[...] = total[pl.ds(start, count), :]
-
-
-def surface(parts, held):
-    owners = lax.axis_size("gz") * lax.axis_size("col")
+        out[...] = total[pl.ds(pl.multiple_of((mine ^ key) * count, 8), count), :]
+
+
+def surface(parts, held, halves):
     sides = parts[0].shape[1]
     lines = held.shape[1]
-    few = owners <= 8 and owners & (owners - 1) == 0 and lines // owners % 8 == 0
-    count = owners if few else 1
     return pl.pallas_call(
-        functools.partial(surface_kernel, count),
+        functools.partial(surface_kernel, halves),
         in_specs=[WHOLE] * (len(parts) + 1),
-        out_specs=[WHOLE] * count,
-        out_shape=[jax.ShapeDtypeStruct((lines // count, sides), F32)] * count,
+        out_specs=[WHOLE] * halves,
+        out_shape=[jax.ShapeDtypeStruct((lines // halves, sides), F32)] * halves,
         scratch_shapes=[pltpu.VMEM((lines, sides), F32)],
         compiler_params=params(),
         cost_estimate=pl.CostEstimate(
@@ -165,21 +165,55 @@
     )(*parts, held)
 
 
-def send_to_owners(shares, late):
-    owners = lax.axis_size("gz") * lax.axis_size("col")
-    if len(shares) == 1:
-        share = shares[0]
-        share = share.reshape(owners, share.shape[0] // owners, share.shape[1])
-        return [lax.all_to_all(share, ("col", "gz"), split_axis=0, concat_axis=0, tiled=True)], late
-    got = [shares[0]]
-    order = sorted(range(1, owners), key=lambda key: -(key % lax.axis_size("gz")))
-    for place, key in enumerate(order):
-        if place == len(order) // 2:
-            held, late = lax.optimization_barrier(([shares[k] for k in order[place:]], late))
-            shares = [held[order.index(k) - place] if k in order[place:] else s for k, s in enumerate(shares)]
-        pairs = [(i, i ^ key) for i in range(owners)]
-        got.append(lax.ppermute(shares[key], ("col", "gz"), pairs))
-    return got, late
+def share_kernel(peers, mine_ref, other_ref, *refs):
+    *outs, total, turned = refs
+    total[...] = mine_ref[...] + other_ref[...]
+    turned[...] = total[...].T
+    lines, sides = total.shape
+    group = lax.axis_index("gz")
+    for key, out in enumerate(outs):
+        peer = group ^ key
+        rows, some = lines // peers, sides // peers
+        out[:rows, :] = total[pl.ds(pl.multiple_of(peer * rows, 8), rows), :]
+        out[rows:, :] = turned[pl.ds(pl.multiple_of(peer * some, 8), some), :]
+
+
+def shares(mine, other):
+    peers = lax.axis_size("gz")
+    lines, sides = mine.shape
+    out = jax.ShapeDtypeStruct(((lines + sides) // peers, sides), F32)
+    return pl.pallas_call(
+        functools.partial(share_kernel, peers),
+        in_specs=[WHOLE] * 2,
+        out_specs=[WHOLE] * peers,
+        out_shape=[out] * peers,
+        scratch_shapes=[pltpu.VMEM((lines, sides), F32), pltpu.VMEM((sides, lines), F32)],
+        compiler_params=params(),
+        cost_estimate=pl.CostEstimate(
+            flops=lines * sides, bytes_accessed=16 * lines * sides, transcendentals=0
+        ),
+    )(mine, other)
+
+
+def flux_sums(parts, held, late):
+    cols, gzs = lax.axis_size("col"), lax.axis_size("gz")
+    sides = parts[0].shape[1]
+    lines = held.shape[1]
+    if cols == 2 and gzs & (gzs - 1) == 0 and lines // cols == sides and sides // gzs % 8 == 0:
+        mine, other = surface(parts, held, 2)
+        other = lax.ppermute(other, "col", [(0, 1), (1, 0)])
+        sent = shares(mine, other)
+        sent, late = lax.optimization_barrier((sent, late))
+        recv = [sent[0]]
+        for key in range(gzs - 1, 0, -1):
+            recv.append(lax.ppermute(sent[key], "gz", [(i, i ^ key) for i in range(gzs)]))
+        return recv, late
+    (total,) = surface(parts, held, 1)
+    rows = lax.psum_scatter(total, "col", scatter_dimension=0, tiled=True)
+    owned = lax.psum_scatter(rows, "gz", scatter_dimension=0, tiled=True)
+    flux = lax.psum_scatter(rows.T, "gz", scatter_dimension=0, tiled=True)
+    flux = jnp.pad(flux, ((0, 0), (0, sides - flux.shape[1])))
+    return [jnp.concatenate([owned, flux], axis=0)], late
 
 
 def turns(axis):
@@ -289,18 +323,18 @@
         for side in range(shape.block):
             start = side * shape.cells
             if face[0] == "row":
-                lines.append(tall[pl.ds(pl.multiple_of(start + edge * length, 8), length), :])
+                lines.append(tall[pl.ds(aligned(start + edge * length, 8), length), :])
             else:
                 lines.append(tall[pl.ds(start + edge, length, stride=shape.y), :])
         span = shape.block * length
-        ref[pl.ds(pl.multiple_of(at * length, span), span), :] = jnp.concatenate(
+        ref[pl.ds(aligned(at * length, span), span), :] = jnp.concatenate(
             lines, axis=0
         ).astype(BF)
     mask = jnp.concatenate([z_mask(shape, shape.half)] * 2, axis=1)
     tips = jnp.where(mask, dot(beside(values), ends_m[...]), 0.0).astype(BF)
     tips = dot(rsum[...], tips)[: shape.half]
     tips = jnp.concatenate([tips[:, : 2 * shape.cells], tips[:, 2 * shape.cells :]], axis=0)
-    z_ref[pl.ds(pl.multiple_of(at, shape.block), shape.block), :] = tips.astype(BF)
+    z_ref[pl.ds(aligned(at, shape.block), shape.block), :] = tips.astype(BF)
 
 
 def faces_kernel(shape, slots, field_ref, block_ref, *refs):
@@ -311,7 +345,7 @@
     @pl.loop(0, shape.sides // shape.block)
     def _(step):
         size = shape.block * shape.cells
-        values = field_ref[pl.ds(pl.multiple_of(step * size, size), size), :]
+        values = field_ref[pl.ds(aligned(step * size, size), size), :]
         tall[...] = values.astype(F32)
         emit_faces(shape, step * shape.block, values, tall, face_refs, z_ref, ends_m, rsum)
 
@@ -352,8 +386,8 @@
     )(field, block)
 
 
-def sweep_kernel(shape, recvs, fluxes, by_xor, *refs):
-    with_flux, last = recvs > 0, fluxes > 0
+def sweep_kernel(shape, recvs, last, *refs):
+    with_flux = recvs > 0
     refs = list(refs)
     take = lambda count: [refs.pop(0) for _ in range(count)]
     field_ref, load_ref, coef_ref = take(3)
@@ -362,19 +396,14 @@
     if with_flux:
         recv_refs = take(recvs)
         (cell_ref,) = take(1)
-    flux_refs = take(fluxes)
     (out_ref,) = take(1)
-    if last:
-        (flux_ref,) = take(1)
-    else:
+    if not last:
         face_refs = take(len(shape.faces))
         (z_ref,) = take(1)
     if with_flux:
-        source_ref, owned_ref = take(2)
+        source_ref, flux_ref = take(2)
     weight, near_m, line_m, lines = take(4)
-    if last:
-        window, turned = take(2)
-    else:
+    if not last:
         tall, ends_m, rsum = take(3)
     if with_flux:
         phi, cell_m, placed = take(3)
@@ -398,28 +427,15 @@
         dims = (2 * cells, lanes)
         edge = jnp.where(iota(dims, 0) < cells, lanes - 1, 0)
         line_m[2 * lanes :, :] = twice((iota(dims, 1) == edge).astype(F32)).astype(BF)
-        if last:
-            group = lax.axis_index("gz")
-            count = flux_refs[0].shape[0]
-            for key, ref in enumerate(flux_refs):
-                place = jnp.bitwise_xor(group, key) if by_xor else key
-                window[pl.ds(place * count, count), :] = ref[...]
-            turned[...] = window[...].T
-            count = flux_ref.shape[0]
-            flux_ref[...] = turned[pl.ds(pl.multiple_of(group * count, count), count), :]
-        else:
+        if not last:
             build_out(shape, ends_m, rsum)
         if with_flux:
             slots = cell_ref.shape[3]
-            if recvs == 1:
-                owned = recv_refs[0][0]
-                for peer in range(1, recv_refs[0].shape[0]):
-                    owned = owned + recv_refs[0][peer]
-            else:
-                owned = recv_refs[0][...]
-                for ref in recv_refs[1:]:
-                    owned = owned + ref[...]
-            owned_ref[...] = owned
+            owned = recv_refs[0][...]
+            for ref in recv_refs[1:]:
+                owned = owned + ref[...]
+            flux_ref[...] = owned[slots:, : flux_ref.shape[1]]
+            owned = owned[:slots]
             high = owned.astype(BF).astype(F32)
             both = jnp.concatenate([high, owned - high], axis=0)
             phi[...] = both.T
@@ -443,101 +459,100 @@
             rows.append(jnp.where(where, line, 0.0))
         return jnp.concatenate(rows, axis=0).astype(BF)
 
-    @pl.loop(0, out_sides // shape.block)
-    def _(step):
+    def work(step):
         local = step * shape.block
-        at = grid_step * out_sides + local
-        sides = pl.ds(pl.multiple_of(at, shape.block), shape.block)
+        at = local if out_sides == shape.sides else grid_step * out_sides + local
+        sides = pl.ds(aligned(at, shape.block), shape.block)
         size = shape.block * cells
         zs = 0.0
         for turn in range(shape.ends):
             wanted = (filled == (turn == 0)) & has_neighbour("gz", turn)
             zs = jnp.where(wanted, end_refs[turn][sides, :].astype(F32), zs)
-        values = field_ref[pl.ds(pl.multiple_of(at * cells, size), size), :]
+        values = field_ref[pl.ds(aligned(at * cells, size), size), :]
         left = [beside(values), expand(zs, mask, 0), expand(zs, mask, shape.half)]
-        lines[...] = dot(jnp.concatenate(left, axis=1), line_m[...])
+        lines[step] = dot(jnp.concatenate(left, axis=1), line_m[...])
         if with_flux:
             phis = phi[sides, :]
             left = [expand(phis, cell_mask, 0), expand(phis, cell_mask, shape.half)]
-            placed[...] = dot_nt(jnp.concatenate(left, axis=1), cell_m[...])
+            placed[step] = dot_nt(jnp.concatenate(left, axis=1), cell_m[...])
         for index in range(shape.half // shape.chunk):
             offset = index * shape.rows
             starts = (offset, offset + shape.half_rows)
             stacks = []
             for start in starts:
-                rows = pl.ds(pl.multiple_of(at * cells + start, shape.rows), shape.rows)
+                rows = pl.ds(aligned(at * cells + start, shape.rows), shape.rows)
                 stack = [field_ref[rows, :]]
                 for face, ref in zip(shape.faces, halo_refs):
                     length = shape.face_len(face)
                     count = shape.chunk * length
-                    first = pl.multiple_of(at * length + start // cells * length, count)
+                    first = aligned(at * length + start // cells * length, count)
                     stack.append(ref[pl.ds(first, count), :])
                 stacks.append(jnp.concatenate(stack, axis=0))
             near = dot(near_m[...], jnp.concatenate(stacks, axis=1))
-            near = near + lines[offset : offset + shape.rows, :]
+            near = near + lines[step, offset : offset + shape.rows, :]
             for part, start in enumerate(starts):
                 cols = slice(part * lanes, (part + 1) * lanes)
-                rows = pl.ds(pl.multiple_of(at * cells + start, shape.rows), shape.rows)
+                rows = pl.ds(aligned(at * cells + start, shape.rows), shape.rows)
                 source = load_ref[rows, :].astype(F32)
                 if with_flux:
-                    source = source + placed[offset : offset + shape.rows, cols]
+                    source = source + placed[step, offset : offset + shape.rows, cols]
                     source_ref[rows, :] = source.astype(BF)
                 centre = field_ref[rows, :].astype(F32)
                 fresh = (1.0 - OMEGA) * centre + weights * (source + near[:, cols])
-                to = pl.ds(pl.multiple_of(local * cells + start, shape.rows), shape.rows)
+                to = pl.ds(aligned(local * cells + start, shape.rows), shape.rows)
                 out_ref[to, :] = fresh.astype(BF)
                 if not last:
-                    tall[start : start + shape.rows, :] = fresh
-        if not last:
-            fresh = out_ref[pl.ds(pl.multiple_of(local * cells, size), size), :]
-            emit_faces(shape, at, fresh, tall, face_refs, z_ref, ends_m, rsum)
-
-
-def sweep(shape, field, load, coef, halos, recv=(), flux_cell=None, flux=(), by_xor=True, last=False):
+                    tall[step, start : start + shape.rows, :] = fresh
+
+    def emit(step):
+        at, size = step * shape.block, shape.block * cells
+        fresh = out_ref[at * cells : at * cells + size, :]
+        emit_faces(shape, at, fresh, tall.at[step], face_refs, z_ref, ends_m, rsum)
+
+    steps = out_sides // shape.block
+    for step in range(steps):
+        work(step)
+        if not last and step > 0:
+            emit(step - 1)
+    if not last:
+        emit(steps - 1)
+
+
+def sweep(shape, field, load, coef, halos, recv=(), flux_cell=None, last=False):
     lanes, cells = shape.lanes, shape.cells
+    steps = shape.sides // shape.block
+    grid = steps if last else 1
+    half = (steps // grid, shape.half_rows, 2 * lanes)
     operands = [field, load, coef, *halos, *recv]
     out_shapes = [jax.ShapeDtypeStruct(field.shape, BF)]
     scratch = [
         pltpu.VMEM(coef.shape, F32),
         pltpu.VMEM((shape.rows, shape.rows + shape.halo_rows()), BF),
         pltpu.VMEM((2 * lanes + 4 * cells, 2 * lanes), BF),
-        pltpu.VMEM((shape.half_rows, 2 * lanes), F32),
+        pltpu.VMEM(half, F32),
     ]
-    if last:
-        operands += flux
-        gzs = len(flux)
-        slots = flux[0].shape[0]
-        flux_shape = (shape.sides // gzs, slots * gzs)
-        out_shapes.append(jax.ShapeDtypeStruct(flux_shape, F32))
-        scratch += [
-            pltpu.VMEM((slots * gzs, shape.sides), F32),
-            pltpu.VMEM((shape.sides, slots * gzs), F32),
-        ]
-    else:
+    if not last:
         out_shapes += face_outputs(shape)
-        scratch += face_scratch(shape)
+        tall, *others = face_scratch(shape)
+        scratch += [pltpu.VMEM((steps, *tall.shape), F32), *others]
     if recv:
         slots = flux_cell.shape[3]
         operands.append(flux_cell)
         out_shapes += [
             jax.ShapeDtypeStruct(field.shape, BF),
-            jax.ShapeDtypeStruct((slots, shape.sides), F32),
+            jax.ShapeDtypeStruct((recv[0].shape[0] - slots, slots * lax.axis_size("gz")), F32),
         ]
         scratch += [
             pltpu.VMEM((shape.sides, 2 * slots), F32),
             pltpu.VMEM((2 * lanes, 4 * slots), BF),
-            pltpu.VMEM((shape.half_rows, 2 * lanes), F32),
+            pltpu.VMEM(half, F32),
         ]
-    steps = shape.sides // shape.block if last else 1
     out_specs = [WHOLE] * len(out_shapes)
     if last:
-        out_specs = [
-            pl.BlockSpec((field.shape[0] // steps, lanes), lambda i: (i, 0)),
-            pl.BlockSpec(flux_shape, lambda i: (0, 0)),
-        ]
+        out_specs = [pl.BlockSpec((field.shape[0] // grid, lanes), lambda i: (i, 0))]
     return pl.pallas_call(
-        functools.partial(sweep_kernel, shape, len(recv), len(flux), by_xor),
-        grid=(steps,),
+        functools.partial(sweep_kernel, shape, len(recv), last),
+        grid=(grid,),
         in_specs=[WHOLE] * len(operands),
         out_specs=out_specs,
         out_shape=out_shapes,
@@ -569,16 +584,6 @@
     return [held[key] for key in range(peers)]
 
 
-def gz_gather(value):
-    peers = lax.axis_size("gz")
-    if peers & (peers - 1):
-        return list(lax.all_gather(value, "gz")), False
-    got = [value]
-    for key in range(1, peers):
-        got.append(lax.ppermute(value, "gz", [(i, i ^ key) for i in range(peers)]))
-    return got, True
-
-
 def per_device(volume_field, volume_load, coefficient, surface_block, trace_cell, flux_cell):
     sides, first, second, lanes = volume_field.shape
     cells = first * second
@@ -593,17 +598,14 @@
     parts = row_gather(trace, faces)
     halos = exchange(shape, faces)
     early = len([face for face in shape.faces if face[0] == "col"])
-    parts, halos[early:] = lax.optimization_barrier((parts, halos[early:]))
-    recv, halos[:early] = send_to_owners(surface(parts, held), halos[:early])
-
-    current, *faces, source, owned = sweep(
+    parts, halos[:early] = lax.optimization_barrier((parts, halos[:early]))
+    recv, halos[early:] = flux_sums(parts, held, halos[early:])
+
+    current, *faces, source, surface_flux = sweep(
         shape, field, load, coef, halos, recv=recv, flux_cell=flux_cell
     )
     current, *faces = sweep(shape, current, source, coef, exchange(shape, faces))
-    flux, by_xor = gz_gather(owned)
-    current, surface_flux = sweep(
-        shape, current, source, coef, exchange(shape, faces), flux=flux, by_xor=by_xor, last=True
-    )
+    (current,) = sweep(shape, current, source, coef, exchange(shape, faces), last=True)
     return current.reshape(volume_field.shape), surface_flux
 
 

time: 82.4 us -> 65 us (0.79)
  waiting for transfers between devices: 26.1 us -> 17.7 us
  starting transfers between devices: 29 us -> 23.5 us
  Pallas kernels: 26.4 us -> 22.8 us
    ppermute x10 -> x4, waiting for transfers between devices: 13.6 us -> 3.25 us  [the longest x3 3.25 us: flux_sums(): lax.ppermute(sent[key], 'gz', [(i, i ^ key) for i in range(gzs)])]
    ppermute x10 -> x4, starting transfers between devices: 14.8 us -> 5.98 us  [the longest x3 4.39 us: flux_sums(): lax.ppermute(sent[key], 'gz', [(i, i ^ key) for i in range(gzs)])]
    pallas_call x4 -> x5, Pallas kernels: 16.3 us -> 12.8 us  [the longest x3 12 us: sweep(): pl.pallas_call(functools.partial(sweep_kernel, shape, len(recv), last), g...]
    ppermute x15, starting transfers between devices: 10.6 us -> 14 us  [swap(): return lax.ppermute(value, axes, pairs)]
    ppermute x15, waiting for transfers between devices: 12.5 us -> 13.5 us  [swap(): return lax.ppermute(value, axes, pairs)]
    ppermute x3, waiting for transfers between devices: 0.01 us -> 0.93 us  [row_gather(): lax.ppermute(held[key], 'row', pairs)]
  transfers between devices with their start and end apart: 28 -> 22, of which waited for: 8 -> 8; matrix products, arithmetic and copies ran while one was open for 0% -> 0% of each run, Pallas kernels for 6% -> 7%
where the time goes in v6:
time: 65 us; the launch traced here: 64.8 us
  starting transfers between devices  23.5 us (36%)
  Pallas kernels  22.8 us (35%)
  waiting for transfers between devices  17.7 us (27%)
  between operations  0.74 us (1%)
    ppermute x15, starting transfers between devices, swap(): return lax.ppermute(value, axes, pairs)  14 us
    ppermute x15, waiting for transfers between devices, swap(): return lax.ppermute(value, axes, pairs)  13.5 us
    pallas_call x3, Pallas kernels, sweep(): pl.pallas_call(functools.partial(sweep_kernel, shape, len(recv), last), g...  12 us
    pallas_call x1, Pallas kernels, traces(): pl.pallas_call(functools.partial(trace_kernel, stride, block), in_specs=[...  6.07 us
    ppermute x3, starting transfers between devices, flux_sums(): lax.ppermute(sent[key], 'gz', [(i, i ^ key) for i in range(gzs)])  4.39 us
    pallas_call x1, Pallas kernels, first_faces(): pl.pallas_call(functools.partial(faces_kernel, shape, slots), in_specs=[W...  3.95 us
    ppermute x3, starting transfers between devices, row_gather(): lax.ppermute(held[key], 'row', pairs)  3.52 us
    ppermute x3, waiting for transfers between devices, flux_sums(): lax.ppermute(sent[key], 'gz', [(i, i ^ key) for i in range(gzs)])  3.25 us
  transfers between devices with their start and end apart: 22, of which 8 were waited for; matrix products, arithmetic and copies ran while one was open for 0% of the time, Pallas kernels for 7%

profile of v6, /device:TPU:0, one launch (start us, length us, event | category | flops | bytes accessed | tf_op | source)
XLA Modules:
  0.0 64.8 jit_solution(1510838592966169030)
XLA Ops:
  0.6 6.1 %shard_map.77.refs_0_ = bf16[1024,128]{1,0:T(8,128)(2,1)} custom-call(bf16[128,64,128]{2,1,0:T(8,128)(2,1)} %bitcast.5, s32[1,1,1,1024]{3,2,1,0:T(1,128)} %cell_ref.1), custom_call_target="tpu_custom_call" | custom-call | flops 536870912 | bytes 2097152 | tf_op jit(solution)/shard_map/pallas_call | solution.py:101
  6.7 3.0 %collective-permute-start = (bf16[1024,128]{1,0:T(8,128)(2,1)}, bf16[1024,128]{1,0:T(8,128)(2,1)S(1)}, u32[]{:S(2)}, u32[]{:S(2)}) collective-permute-start(bf16[1024,128]{1,0:T(8,128)(2,1)} %shard_map.77.refs_0_), channel_id=1, source_target_pairs={{0,16},{8,24},{16,0},{24,8},{1,17},{9,25},{17,1},{25,9},{2,18},{10... | collective-permute-start | bytes 786440 | tf_op jit(solution)/shard_map/ppermute | solution.py:579
  9.7 4.0 %shard_map.78 = (bf16[1024,128]{1,0:T(8,128)(2,1)S(1)}, bf16[1024,128]{1,0:T(8,128)(2,1)S(1)}, bf16[1024,128]{1,0:T(8,128)(2,1)S(1)}, bf16[128,128]{1,0:T(8,128)(2,1)S(1)}, bf16[4,256,1024]{2,1,0:T(8,128)(2,1)S(1)}) custom-call(bf16[8192,128]{1,0:T(8,128)(2,1)} %bitcast.6, bf16[256,16384]{1,0:T(8,128)(2,1)} %block_ref.1), custom_call_target="tpu_custom_call" | custom-call | flops 134217728 | bytes 4194304 | tf_op jit(solution)/shard_map/pallas_call | solution.py:376
  13.7 1.6 %collective-permute-start.3 = (bf16[1024,128]{1,0:T(8,128)(2,1)S(1)}, bf16[1024,128]{1,0:T(8,128)(2,1)S(1)}, u32[]{:S(2)}, u32[]{:S(2)}) collective-permute-start(bf16[1024,128]{1,0:T(8,128)(2,1)S(1)} %get-tuple-element.40), channel_id=1, source_target_pairs={{0,4},{1,5},{2,6},{3,7},{4,0},{5,1},{6,2},{7,3},{8,12},{9,13},{10,... | collective-permute-start | bytes 786440 | tf_op jit(solution)/shard_map/ppermute | solution.py:250
  15.3 0.9 %collective-permute-done.refs_2_ = bf16[1024,128]{1,0:T(8,128)(2,1)S(1)} collective-permute-done((bf16[1024,128]{1,0:T(8,128)(2,1)}, bf16[1024,128]{1,0:T(8,128)(2,1)S(1)}, u32[]{:S(2)}, u32[]{:S(2)}) %collective-permute-start) | collective-permute-done | bytes 262176 | tf_op jit(solution)/shard_map/ppermute | solution.py:579
  16.2 0.5 collective-permute-start.2
  16.7 1.8 %collective-permute-start.5 = (bf16[1024,128]{1,0:T(8,128)(2,1)S(1)}, bf16[1024,128]{1,0:T(8,128)(2,1)S(1)}, u32[]{:S(2)}, u32[]{:S(2)}) collective-permute-start(bf16[1024,128]{1,0:T(8,128)(2,1)S(1)} %get-tuple-element.41), channel_id=1, source_target_pairs={{0,1},{1,0},{2,3},{3,2},{4,5},{5,4},{6,7},{7,6},{8,16},{9,17},{10,... | collective-permute-start | bytes 786440 | tf_op jit(solution)/shard_map/ppermute | solution.py:250
  18.6 3.0 %collective-permute-done.3.refs_3_ = bf16[1024,128]{1,0:T(8,128)(2,1)S(1)} collective-permute-done((bf16[1024,128]{1,0:T(8,128)(2,1)S(1)}, bf16[1024,128]{1,0:T(8,128)(2,1)S(1)}, u32[]{:S(2)}, u32[]{:S(2)}) %collective-permute-start.3) | collective-permute-done | bytes 262176 | tf_op jit(solution)/shard_map/ppermute | solution.py:250
  21.6 0.7 %shard_map.79 = (f32[128,128]{1,0:T(8,128)S(1)}, f32[128,128]{1,0:T(8,128)S(1)}) custom-call(bf16[1024,128]{1,0:T(8,128)(2,1)S(1)} %copy-done.2, bf16[1024,128]{1,0:T(8,128)(2,1)S(1)} %collective-permute-done.1.refs_1_, bf16[1024,128]{1,0:T(8,128)(2,1)S(1)} %collective-permute-done.refs_2_, bf16[1024,128]{1,0:T(8,128)(2,1)S(1)} %collective-permute-done.2.refs_3_, ...), custom_call_target="tpu_custom_call" | custom-call | flops 268435456 | bytes 2097152 | tf_op jit(solution)/shard_map/pallas_call | solution.py:155
  22.3 1.6 %collective-permute-start.4 = (f32[128,128]{1,0:T(8,128)S(1)}, f32[128,128]{1,0:T(8,128)S(1)}, u32[]{:S(2)}, u32[]{:S(2)}) collective-permute-start(f32[128,128]{1,0:T(8,128)S(1)} %get-tuple-element.53), channel_id=1, source_target_pairs={{0,4},{4,0},{1,5},{5,1},{2,6},{6,2},{3,7},{7,3},{8,12},{12,8},{9,1... | collective-permute-start | bytes 196616 | tf_op jit(solution)/shard_map/ppermute | solution.py:204
  23.9 3.1 %collective-permute-start.7 = (bf16[128,128]{1,0:T(8,128)(2,1)S(1)}, bf16[128,128]{1,0:T(8,128)(2,1)S(1)}, u32[]{:S(2)}, u32[]{:S(2)}) collective-permute-start(bf16[128,128]{1,0:T(8,128)(2,1)S(1)} %get-tuple-element.43), channel_id=1, source_target_pairs={{0,1},{1,0},{2,3},{3,2},{4,5},{5,4},{6,7},{7,6},{8,9},{9,8},{10,11... | collective-permute-start | bytes 98312 | tf_op jit(solution)/shard_map/ppermute | solution.py:250
  27.0 0.1 shard_map.80
  27.2 1.8 %collective-permute-done.7.refs_6_ = bf16[128,128]{1,0:T(8,128)(2,1)S(1)} collective-permute-done((bf16[128,128]{1,0:T(8,128)(2,1)S(1)}, bf16[128,128]{1,0:T(8,128)(2,1)S(1)}, u32[]{:S(2)}, u32[]{:S(2)}) %collective-permute-start.7) | collective-permute-done | bytes 32800 | tf_op jit(solution)/shard_map/ppermute | solution.py:250
  28.9 2.5 %collective-permute-start.9 = (f32[64,128]{1,0:T(8,128)S(1)}, f32[64,128]{1,0:T(8,128)S(1)}, u32[]{:S(2)}, u32[]{:S(2)}) collective-permute-start(f32[64,128]{1,0:T(8,128)S(1)} %get-tuple-element.63), channel_id=1, source_target_pairs={{0,3},{1,2},{2,1},{3,0},{4,7},{5,6},{6,5},{7,4},{8,11},{9,10},{10,... | collective-permute-start | bytes 98312 | tf_op jit(solution)/shard_map/ppermute | solution.py:209
  31.4 1.0 %collective-permute-start.10 = (f32[64,128]{1,0:T(8,128)S(1)}, f32[64,128]{1,0:T(8,128)S(1)}, u32[]{:S(2)}, u32[]{:S(2)}) collective-permute-start(f32[64,128]{1,0:T(8,128)S(1)} %get-tuple-element.64), channel_id=1, source_target_pairs={{0,2},{1,3},{2,0},{3,1},{4,6},{5,7},{6,4},{7,5},{8,10},{9,11},{10,... | collective-permute-start | bytes 98312 | tf_op jit(solution)/shard_map/ppermute | solution.py:209
  32.4 0.9 %collective-permute-start.11 = (f32[64,128]{1,0:T(8,128)S(1)}, f32[64,128]{1,0:T(8,128)S(1)}, u32[]{:S(2)}, u32[]{:S(2)}) collective-permute-start(f32[64,128]{1,0:T(8,128)S(1)} %get-tuple-element.65), channel_id=1, source_target_pairs={{0,1},{1,0},{2,3},{3,2},{4,5},{5,4},{6,7},{7,6},{8,9},{9,8},{10,11... | collective-permute-start | bytes 98312 | tf_op jit(solution)/shard_map/ppermute | solution.py:209
  33.3 1.4 %collective-permute-done.9.refs_9_ = f32[64,128]{1,0:T(8,128)S(1)} collective-permute-done((f32[64,128]{1,0:T(8,128)S(1)}, f32[64,128]{1,0:T(8,128)S(1)}, u32[]{:S(2)}, u32[]{:S(2)}) %collective-permute-start.9) | collective-permute-done | bytes 32800 | tf_op jit(solution)/shard_map/ppermute | solution.py:209
  34.7 1.5 %collective-permute-done.10.refs_10_ = f32[64,128]{1,0:T(8,128)S(1)} collective-permute-done((f32[64,128]{1,0:T(8,128)S(1)}, f32[64,128]{1,0:T(8,128)S(1)}, u32[]{:S(2)}, u32[]{:S(2)}) %collective-permute-start.10) | collective-permute-done | bytes 32800 | tf_op jit(solution)/shard_map/ppermute | solution.py:209
  36.2 0.3 collective-permute-done.11.refs_11_
  36.6 4.7 %shard_map.81 = (bf16[8192,128]{1,0:T(8,128)(2,1)S(1)}, bf16[1024,128]{1,0:T(8,128)(2,1)S(1)}, bf16[1024,128]{1,0:T(8,128)(2,1)S(1)}, bf16[1024,128]{1,0:T(8,128...) custom-call(bf16[8192,128]{1,0:T(8,128)(2,1)S(1)} %bitcast.7, ...), custom_call_target="tpu_custom_call" | custom-call | flops 805306368 | bytes 8388608 | tf_op jit(solution)/shard_map/pallas_call | solution.py:553
  41.3 0.6 collective-permute-start.12
  41.9 0.6 collective-permute-start.13
  42.5 0.5 collective-permute-start.16
  43.0 1.8 %collective-permute-start.15 = (bf16[128,128]{1,0:T(8,128)(2,1)S(1)}, bf16[128,128]{1,0:T(8,128)(2,1)S(1)}, u32[]{:S(2)}, u32[]{:S(2)}) collective-permute-start(bf16[128,128]{1,0:T(8,128)(2,1)S(1)} %get-tuple-element.71), channel_id=1, source_target_pairs={{0,1},{1,0},{2,3},{3,2},{4,5},{5,4},{6,7},{7,6},{8,9},{9,8},{10,11... | collective-permute-start | bytes 98312 | tf_op jit(solution)/shard_map/ppermute | solution.py:250
  44.8 4.2 %collective-permute-done.15.refs_6_ = bf16[128,128]{1,0:T(8,128)(2,1)S(1)} collective-permute-done((bf16[128,128]{1,0:T(8,128)(2,1)S(1)}, bf16[128,128]{1,0:T(8,128)(2,1)S(1)}, u32[]{:S(2)}, u32[]{:S(2)}) %collective-permute-start.15) | collective-permute-done | bytes 32800 | tf_op jit(solution)/shard_map/ppermute | solution.py:250
  48.9 3.7 %shard_map.82 = (bf16[8192,128]{1,0:T(8,128)(2,1)S(1)}, bf16[1024,128]{1,0:T(8,128)(2,1)S(1)}, bf16[1024,128]{1,0:T(8,128)(2,1)S(1)}, bf16[1024,128]{1,0:T(8,128)(2,1)S(1)}, bf16[128,128]{1,0:T(8,128)(2,1)S(1)}) custom-call(bf16[8192,128]{1,0:T(8,128)(2,1)S(1)} %get-tuple-element.66.refs_0_, bf16[8192,128]{1,0:T(8,128)(2,1)S(1)} %get-tuple-element.67.refs_1_, ...), custom_call_target="tpu_custom_call" | custom-call | flops 805306368 | bytes 8388608 | tf_op jit(solution)/shard_map/pallas_call | solution.py:553
  52.7 1.5 %collective-permute-start.17 = (bf16[1024,128]{1,0:T(8,128)(2,1)S(1)}, bf16[1024,128]{1,0:T(8,128)(2,1)S(1)}, u32[]{:S(2)}, u32[]{:S(2)}) collective-permute-start(bf16[1024,128]{1,0:T(8,128)(2,1)S(1)} %get-tuple-element.73), channel_id=1, source_target_pairs={{0,4},{1,5},{2,6},{3,7},{4,0},{5,1},{6,2},{7,3},{8,12},{9,13},{10,... | collective-permute-start | bytes 786440 | tf_op jit(solution)/shard_map/ppermute | solution.py:250
  54.1 0.7 %collective-permute-start.18 = (bf16[1024,128]{1,0:T(8,128)(2,1)S(1)}, bf16[1024,128]{1,0:T(8,128)(2,1)S(1)}, u32[]{:S(2)}, u32[]{:S(2)}) collective-permute-start(bf16[1024,128]{1,0:T(8,128)(2,1)S(1)} %get-tuple-element.74), channel_id=1, source_target_pairs={{0,1},{1,0},{2,3},{3,2},{4,5},{5,4},{6,7},{7,6},{8,16},{9,17},{10,... | collective-permute-start | bytes 786440 | tf_op jit(solution)/shard_map/ppermute | solution.py:250
  54.8 0.5 collective-permute-start.21
  55.3 1.3 %collective-permute-start.20 = (bf16[128,128]{1,0:T(8,128)(2,1)S(1)}, bf16[128,128]{1,0:T(8,128)(2,1)S(1)}, u32[]{:S(2)}, u32[]{:S(2)}) collective-permute-start(bf16[128,128]{1,0:T(8,128)(2,1)S(1)} %get-tuple-element.76), channel_id=1, source_target_pairs={{0,1},{1,0},{2,3},{3,2},{4,5},{5,4},{6,7},{7,6},{8,9},{9,8},{10,11... | collective-permute-start | bytes 98312 | tf_op jit(solution)/shard_map/ppermute | solution.py:250
  56.6 4.6 %collective-permute-done.20.refs_6_ = bf16[128,128]{1,0:T(8,128)(2,1)S(1)} collective-permute-done((bf16[128,128]{1,0:T(8,128)(2,1)S(1)}, bf16[128,128]{1,0:T(8,128)(2,1)S(1)}, u32[]{:S(2)}, u32[]{:S(2)}) %collective-permute-start.20) | collective-permute-done | bytes 32800 | tf_op jit(solution)/shard_map/ppermute | solution.py:250
  61.2 3.5 %shard_map.83 = bf16[8192,128]{1,0:T(8,128)(2,1)} custom-call(bf16[8192,128]{1,0:T(8,128)(2,1)S(1)} %get-tuple-element.72.refs_0_, bf16[8192,128]{1,0:T(8,128)(2,1)S(1)} %get-tuple-element.67.refs_1_, f32[64,128]{1,0:T(8,128)S(1)} %bitcast.11, bf16[1024,128]{1,0:T(8,128)(2,1)S(1)} %collective-permute-done.17.refs_3_, ...), custom_call_target="tpu_custom_call" | custom-call | flops 805306368 | bytes 8388608 | tf_op jit(solution)/shard_map/pallas_call | solution.py:553
  (29 shorter events, 0.1 us)
Async XLA Ops:
  6.7 9.5 %collective-permute-start = (bf16[1024,128]{1,0:T(8,128)(2,1)}, bf16[1024,128]{1,0:T(8,128)(2,1)S(1)}, u32[]{:S(2)}, u32[]{:S(2)}) collective-permute-start(bf16[1024,128]{1,0:T(8,128)(2,1)} %shard_map.77.refs_0_), channel_id=1, source_target_pairs={{0,16},{8,24},{16,0},{24,8},{1,17},{9,25},{17,1},{25,9},{2,18},{10... | collective-permute-start | bytes 786440 | tf_op jit(solution)/shard_map/ppermute | solution.py:579
  9.7 6.5 %copy-start.2 = (bf16[1024,128]{1,0:T(8,128)(2,1)S(1)}, bf16[1024,128]{1,0:T(8,128)(2,1)}, u32[]{:S(2)}) copy-start(bf16[1024,128]{1,0:T(8,128)(2,1)} %shard_map.77.refs_0_) | copy-start | bytes 786436
  9.7 26.9 %copy-start.1 = (bf16[128,8,8,128]{3,2,1,0:T(8,128)(2,1)S(1)}, bf16[128,8,8,128]{3,2,1,0:T(8,128)(2,1)}, u32[]{:S(2)}) copy-start(bf16[128,8,8,128]{3,2,1,0:T(8,128)(2,1)} %param.7) | copy-start | bytes 6291460
  13.7 22.9 %copy-start = (bf16[128,8,8,128]{3,2,1,0:T(8,128)(2,1)S(1)}, bf16[128,8,8,128]{3,2,1,0:T(8,128)(2,1)}, u32[]{:S(2)}) copy-start(bf16[128,8,8,128]{3,2,1,0:T(8,128)(2,1)} %param.6) | copy-start | bytes 6291460
  13.7 22.9 %copy-start.3 = (f32[8,8,128]{2,1,0:T(8,128)S(1)}, f32[8,8,128]{2,1,0:T(8,128)}, u32[]{:S(2)}) copy-start(f32[8,8,128]{2,1,0:T(8,128)} %param.8) | copy-start | bytes 98308
  13.7 22.9 %copy-start.4 = (s32[1,1,1,32]{3,2,1,0:T(1,128)S(1)}, s32[1,1,1,32]{3,2,1,0:T(1,128)}, u32[]{:S(2)}) copy-start(s32[1,1,1,32]{3,2,1,0:T(1,128)} %refs_12_.1) | copy-start | bytes 388
  13.7 7.8 %collective-permute-start.3 = (bf16[1024,128]{1,0:T(8,128)(2,1)S(1)}, bf16[1024,128]{1,0:T(8,128)(2,1)S(1)}, u32[]{:S(2)}, u32[]{:S(2)}) collective-permute-start(bf16[1024,128]{1,0:T(8,128)(2,1)S(1)} %get-tuple-element.40), channel_id=1, source_target_pairs={{0,4},{1,5},{2,6},{3,7},{4,0},{5,1},{6,2},{7,3},{8,12},{9,13},{10,... | collective-permute-start | bytes 786440 | tf_op jit(solution)/shard_map/ppermute | solution.py:250
  16.2 5.3 %collective-permute-start.1 = (bf16[1024,128]{1,0:T(8,128)(2,1)S(1)}, bf16[1024,128]{1,0:T(8,128)(2,1)S(1)}, u32[]{:S(2)}, u32[]{:S(2)}) collective-permute-start(bf16[1024,128]{1,0:T(8,128)(2,1)S(1)} %copy-done.2), channel_id=1, source_target_pairs={{0,8},{8,0},{16,24},{24,16},{1,9},{9,1},{17,25},{25,17},{2,10},{10... | collective-permute-start | bytes 786440 | tf_op jit(solution)/shard_map/ppermute | solution.py:579
  16.2 5.3 %collective-permute-start.2 = (bf16[1024,128]{1,0:T(8,128)(2,1)S(1)}, bf16[1024,128]{1,0:T(8,128)(2,1)S(1)}, u32[]{:S(2)}, u32[]{:S(2)}) collective-permute-start(bf16[1024,128]{1,0:T(8,128)(2,1)S(1)} %collective-permute-done.refs_2_), channel_id=1, source_target_pairs={{0,8},{8,0},{16,24},{24,16},{1,9},{9,1},{17,25},{25,17},{2,10},{10... | collective-permute-start | bytes 786440 | tf_op jit(solution)/shard_map/ppermute | solution.py:579
  16.7 12.2 %collective-permute-start.5 = (bf16[1024,128]{1,0:T(8,128)(2,1)S(1)}, bf16[1024,128]{1,0:T(8,128)(2,1)S(1)}, u32[]{:S(2)}, u32[]{:S(2)}) collective-permute-start(bf16[1024,128]{1,0:T(8,128)(2,1)S(1)} %get-tuple-element.41), channel_id=1, source_target_pairs={{0,1},{1,0},{2,3},{3,2},{4,5},{5,4},{6,7},{7,6},{8,16},{9,17},{10,... | collective-permute-start | bytes 786440 | tf_op jit(solution)/shard_map/ppermute | solution.py:250
  18.6 10.4 %collective-permute-start.6 = (bf16[1024,128]{1,0:T(8,128)(2,1)S(1)}, bf16[1024,128]{1,0:T(8,128)(2,1)S(1)}, u32[]{:S(2)}, u32[]{:S(2)}) collective-permute-start(bf16[1024,128]{1,0:T(8,128)(2,1)S(1)} %get-tuple-element.42), channel_id=1, source_target_pairs={{0,8},{1,9},{2,10},{3,11},{4,12},{5,13},{6,14},{7,15},{8,0},{9,1},... | collective-permute-start | bytes 786440 | tf_op jit(solution)/shard_map/ppermute | solution.py:250
  22.3 4.7 %collective-permute-start.4 = (f32[128,128]{1,0:T(8,128)S(1)}, f32[128,128]{1,0:T(8,128)S(1)}, u32[]{:S(2)}, u32[]{:S(2)}) collective-permute-start(f32[128,128]{1,0:T(8,128)S(1)} %get-tuple-element.53), channel_id=1, source_target_pairs={{0,4},{4,0},{1,5},{5,1},{2,6},{6,2},{3,7},{7,3},{8,12},{12,8},{9,1... | collective-permute-start | bytes 196616 | tf_op jit(solution)/shard_map/ppermute | solution.py:204
  23.9 3.3 %collective-permute-start.8 = (bf16[128,128]{1,0:T(8,128)(2,1)S(1)}, bf16[128,128]{1,0:T(8,128)(2,1)S(1)}, u32[]{:S(2)}, u32[]{:S(2)}) collective-permute-start(bf16[128,128]{1,0:T(8,128)(2,1)S(1)} %get-tuple-element.43), channel_id=1, source_target_pairs={{0,8},{1,2},{2,1},{3,11},{4,12},{5,6},{6,5},{7,15},{8,0},{9,10},{1... | collective-permute-start | bytes 98312 | tf_op jit(solution)/shard_map/ppermute | solution.py:250
  23.9 5.0 %collective-permute-start.7 = (bf16[128,128]{1,0:T(8,128)(2,1)S(1)}, bf16[128,128]{1,0:T(8,128)(2,1)S(1)}, u32[]{:S(2)}, u32[]{:S(2)}) collective-permute-start(bf16[128,128]{1,0:T(8,128)(2,1)S(1)} %get-tuple-element.43), channel_id=1, source_target_pairs={{0,1},{1,0},{2,3},{3,2},{4,5},{5,4},{6,7},{7,6},{8,9},{9,8},{10,11... | collective-permute-start | bytes 98312 | tf_op jit(solution)/shard_map/ppermute | solution.py:250
  28.9 5.8 %collective-permute-start.9 = (f32[64,128]{1,0:T(8,128)S(1)}, f32[64,128]{1,0:T(8,128)S(1)}, u32[]{:S(2)}, u32[]{:S(2)}) collective-permute-start(f32[64,128]{1,0:T(8,128)S(1)} %get-tuple-element.63), channel_id=1, source_target_pairs={{0,3},{1,2},{2,1},{3,0},{4,7},{5,6},{6,5},{7,4},{8,11},{9,10},{10,... | collective-permute-start | bytes 98312 | tf_op jit(solution)/shard_map/ppermute | solution.py:209
  31.4 4.8 %collective-permute-start.10 = (f32[64,128]{1,0:T(8,128)S(1)}, f32[64,128]{1,0:T(8,128)S(1)}, u32[]{:S(2)}, u32[]{:S(2)}) collective-permute-start(f32[64,128]{1,0:T(8,128)S(1)} %get-tuple-element.64), channel_id=1, source_target_pairs={{0,2},{1,3},{2,0},{3,1},{4,6},{5,7},{6,4},{7,5},{8,10},{9,11},{10,... | collective-permute-start | bytes 98312 | tf_op jit(solution)/shard_map/ppermute | solution.py:209
  32.4 4.2 %collective-permute-start.11 = (f32[64,128]{1,0:T(8,128)S(1)}, f32[64,128]{1,0:T(8,128)S(1)}, u32[]{:S(2)}, u32[]{:S(2)}) collective-permute-start(f32[64,128]{1,0:T(8,128)S(1)} %get-tuple-element.65), channel_id=1, source_target_pairs={{0,1},{1,0},{2,3},{3,2},{4,5},{5,4},{6,7},{7,6},{8,9},{9,8},{10,11... | collective-permute-start | bytes 98312 | tf_op jit(solution)/shard_map/ppermute | solution.py:209
  41.3 7.6 %collective-permute-start.12 = (bf16[1024,128]{1,0:T(8,128)(2,1)S(1)}, bf16[1024,128]{1,0:T(8,128)(2,1)S(1)}, u32[]{:S(2)}, u32[]{:S(2)}) collective-permute-start(bf16[1024,128]{1,0:T(8,128)(2,1)S(1)} %get-tuple-element.68), channel_id=1, source_target_pairs={{0,4},{1,5},{2,6},{3,7},{4,0},{5,1},{6,2},{7,3},{8,12},{9,13},{10,... | collective-permute-start | bytes 786440 | tf_op jit(solution)/shard_map/ppermute | solution.py:250
  41.9 7.1 %collective-permute-start.13 = (bf16[1024,128]{1,0:T(8,128)(2,1)S(1)}, bf16[1024,128]{1,0:T(8,128)(2,1)S(1)}, u32[]{:S(2)}, u32[]{:S(2)}) collective-permute-start(bf16[1024,128]{1,0:T(8,128)(2,1)S(1)} %get-tuple-element.69), channel_id=1, source_target_pairs={{0,1},{1,0},{2,3},{3,2},{4,5},{5,4},{6,7},{7,6},{8,16},{9,17},{10,... | collective-permute-start | bytes 786440 | tf_op jit(solution)/shard_map/ppermute | solution.py:250
  42.5 6.5 %collective-permute-start.14 = (bf16[1024,128]{1,0:T(8,128)(2,1)S(1)}, bf16[1024,128]{1,0:T(8,128)(2,1)S(1)}, u32[]{:S(2)}, u32[]{:S(2)}) collective-permute-start(bf16[1024,128]{1,0:T(8,128)(2,1)S(1)} %get-tuple-element.70), channel_id=1, source_target_pairs={{0,8},{1,9},{2,10},{3,11},{4,12},{5,13},{6,14},{7,15},{8,0},{9,1},... | collective-permute-start | bytes 786440 | tf_op jit(solution)/shard_map/ppermute | solution.py:250
  42.5 2.2 %collective-permute-start.16 = (bf16[128,128]{1,0:T(8,128)(2,1)S(1)}, bf16[128,128]{1,0:T(8,128)(2,1)S(1)}, u32[]{:S(2)}, u32[]{:S(2)}) collective-permute-start(bf16[128,128]{1,0:T(8,128)(2,1)S(1)} %get-tuple-element.71), channel_id=1, source_target_pairs={{0,8},{1,2},{2,1},{3,11},{4,12},{5,6},{6,5},{7,15},{8,0},{9,10},{1... | collective-permute-start | bytes 98312 | tf_op jit(solution)/shard_map/ppermute | solution.py:250
  43.0 6.0 %collective-permute-start.15 = (bf16[128,128]{1,0:T(8,128)(2,1)S(1)}, bf16[128,128]{1,0:T(8,128)(2,1)S(1)}, u32[]{:S(2)}, u32[]{:S(2)}) collective-permute-start(bf16[128,128]{1,0:T(8,128)(2,1)S(1)} %get-tuple-element.71), channel_id=1, source_target_pairs={{0,1},{1,0},{2,3},{3,2},{4,5},{5,4},{6,7},{7,6},{8,9},{9,8},{10,11... | collective-permute-start | bytes 98312 | tf_op jit(solution)/shard_map/ppermute | solution.py:250
  52.7 8.5 %collective-permute-start.17 = (bf16[1024,128]{1,0:T(8,128)(2,1)S(1)}, bf16[1024,128]{1,0:T(8,128)(2,1)S(1)}, u32[]{:S(2)}, u32[]{:S(2)}) collective-permute-start(bf16[1024,128]{1,0:T(8,128)(2,1)S(1)} %get-tuple-element.73), channel_id=1, source_target_pairs={{0,4},{1,5},{2,6},{3,7},{4,0},{5,1},{6,2},{7,3},{8,12},{9,13},{10,... | collective-permute-start | bytes 786440 | tf_op jit(solution)/shard_map/ppermute | solution.py:250
  54.1 7.1 %collective-permute-start.18 = (bf16[1024,128]{1,0:T(8,128)(2,1)S(1)}, bf16[1024,128]{1,0:T(8,128)(2,1)S(1)}, u32[]{:S(2)}, u32[]{:S(2)}) collective-permute-start(bf16[1024,128]{1,0:T(8,128)(2,1)S(1)} %get-tuple-element.74), channel_id=1, source_target_pairs={{0,1},{1,0},{2,3},{3,2},{4,5},{5,4},{6,7},{7,6},{8,16},{9,17},{10,... | collective-permute-start | bytes 786440 | tf_op jit(solution)/shard_map/ppermute | solution.py:250
  54.8 6.4 %collective-permute-start.19 = (bf16[1024,128]{1,0:T(8,128)(2,1)S(1)}, bf16[1024,128]{1,0:T(8,128)(2,1)S(1)}, u32[]{:S(2)}, u32[]{:S(2)}) collective-permute-start(bf16[1024,128]{1,0:T(8,128)(2,1)S(1)} %get-tuple-element.75), channel_id=1, source_target_pairs={{0,8},{1,9},{2,10},{3,11},{4,12},{5,13},{6,14},{7,15},{8,0},{9,1},... | collective-permute-start | bytes 786440 | tf_op jit(solution)/shard_map/ppermute | solution.py:250
  54.8 1.8 %collective-permute-start.21 = (bf16[128,128]{1,0:T(8,128)(2,1)S(1)}, bf16[128,128]{1,0:T(8,128)(2,1)S(1)}, u32[]{:S(2)}, u32[]{:S(2)}) collective-permute-start(bf16[128,128]{1,0:T(8,128)(2,1)S(1)} %get-tuple-element.76), channel_id=1, source_target_pairs={{0,8},{1,2},{2,1},{3,11},{4,12},{5,6},{6,5},{7,15},{8,0},{9,10},{1... | collective-permute-start | bytes 98312 | tf_op jit(solution)/shard_map/ppermute | solution.py:250
  55.3 5.9 %collective-permute-start.20 = (bf16[128,128]{1,0:T(8,128)(2,1)S(1)}, bf16[128,128]{1,0:T(8,128)(2,1)S(1)}, u32[]{:S(2)}, u32[]{:S(2)}) collective-permute-start(bf16[128,128]{1,0:T(8,128)(2,1)S(1)} %get-tuple-element.76), channel_id=1, source_target_pairs={{0,1},{1,0},{2,3},{3,2},{4,5},{5,4},{6,7},{7,6},{8,9},{9,8},{10,11... | collective-permute-start | bytes 98312 | tf_op jit(solution)/shard_map/ppermute | solution.py:250

commit v7 on v6

--- a/solution.py
+++ b/solution.py
@@ -69,21 +69,20 @@
     for step in range(sides // block):
         copies[step].wait()
         span = field[step * block : (step + 1) * block]
-        tall[...] = span.reshape(block * rows, lanes).astype(F32)
-
-        @pl.loop(0, block // 8)
-        def _(batch):
+        tall[step] = span.reshape(block * rows, lanes).astype(F32)
+
+        for batch in range(block // 8):
             for tile in range(rows // together):
                 cols = slice(tile * 128, (tile + 1) * 128)
                 where = place[:, cols]
                 found = None
                 for row in range(together):
                     start = batch * 8 * rows + tile * together + row
-                    line = tall[pl.ds(start, 8, stride=rows), :]
+                    line = tall[step, pl.ds(start, 8, stride=rows), :]
                     line = jnp.take_along_axis(line, where, axis=1)
                     found = line if found is None else jnp.where(group == row, line, found)
-                at = pl.multiple_of(step * block + batch * 8, 8)
-                picked[pl.ds(at, 8), cols] = found
+                at = step * block + batch * 8
+                picked[at : at + 8, cols] = found
 
     total = jnp.zeros((sides, slots), F32)
     for part in range(parts):
@@ -106,7 +105,7 @@
         scratch_shapes=[
             pltpu.VMEM(field.shape, BF),
             pltpu.VMEM(trace_cell.shape, jnp.int32),
-            pltpu.VMEM((block * rows, lanes), F32),
+            pltpu.VMEM((sides // block, block * rows, lanes), F32),
             pltpu.VMEM((width, slots), BF),
             pltpu.VMEM((8, slots), jnp.int32),
             pltpu.VMEM((sides, slots), F32),
@@ -338,18 +337,24 @@
 
 
 def faces_kernel(shape, slots, field_ref, block_ref, *refs):
-    *face_refs, z_ref, held, tall, ends_m, rsum, sems = refs
-    copies = fetch_columns(block_ref, held, sems, slots)
+    *face_refs, z_ref, held, field, tall, ends_m, rsum, sems, field_sems = refs
+    size = shape.block * shape.cells
+    steps = shape.sides // shape.block
+    copies = []
+    for step in range(steps):
+        span = pl.ds(step * size, size)
+        copies.append(
+            pltpu.make_async_copy(field_ref.at[span], field.at[span], field_sems.at[step])
+        )
+        copies[-1].start()
+    columns = fetch_columns(block_ref, held, sems, slots)
     build_out(shape, ends_m, rsum)
-
-    @pl.loop(0, shape.sides // shape.block)
-    def _(step):
-        size = shape.block * shape.cells
-        values = field_ref[pl.ds(aligned(step * size, size), size), :]
-        tall[...] = values.astype(F32)
-        emit_faces(shape, step * shape.block, values, tall, face_refs, z_ref, ends_m, rsum)
-
-    for copy in copies:
+    for step in range(steps):
+        copies[step].wait()
+        values = field[step * size : (step + 1) * size, :]
+        tall[step] = values.astype(F32)
+        emit_faces(shape, step * shape.block, values, tall.at[step], face_refs, z_ref, ends_m, rsum)
+    for copy in columns:
         copy.wait()
 
 
@@ -371,14 +376,22 @@
 
 def first_faces(shape, field, block, slots):
     peers = lax.axis_size("row")
+    steps = shape.sides // shape.block
     shapes = face_outputs(shape)
     shapes.append(jax.ShapeDtypeStruct((peers, block.shape[0], slots), BF))
+    tall, *others = face_scratch(shape)
     return pl.pallas_call(
         functools.partial(faces_kernel, shape, slots),
-        in_specs=[WHOLE, pl.BlockSpec(memory_space=pltpu.HBM)],
+        in_specs=[pl.BlockSpec(memory_space=pltpu.HBM)] * 2,
         out_specs=[WHOLE] * len(shapes),
         out_shape=shapes,
-        scratch_shapes=face_scratch(shape) + [pltpu.SemaphoreType.DMA((peers,))],
+        scratch_shapes=[
+            pltpu.VMEM(field.shape, BF),
+            pltpu.VMEM((steps, *tall.shape), F32),
+            *others,
+            pltpu.SemaphoreType.DMA((peers,)),
+            pltpu.SemaphoreType.DMA((steps,)),
+        ],
         compiler_params=params(FACES_MIB),
         cost_estimate=pl.CostEstimate(
             flops=field.size * 128, bytes_accessed=4 * field.size, transcendentals=0
@@ -403,16 +416,17 @@
     if with_flux:
         source_ref, flux_ref = take(2)
     weight, near_m, line_m, lines = take(4)
-    if not last:
+    if last:
+        result_ref = out_ref
+        out_ref, out_sems = take(2)
+    else:
         tall, ends_m, rsum = take(3)
     if with_flux:
         phi, cell_m, placed = take(3)
 
-    grid_step = pl.program_id(0)
     cells, lanes = shape.cells, shape.lanes
 
-    @pl.when(grid_step == 0)
-    def _():
+    def prepare():
         weight[...] = OMEGA / (6.0 + coef_ref[...])
         dims = (shape.rows, shape.rows)
         row, col = iota(dims, 0), iota(dims, 1)
@@ -442,6 +456,7 @@
             cell = jnp.concatenate([cell_ref[0, 0]] * 2, axis=1)
             cell_m[...] = twice((iota((lanes, 2 * slots), 0) == cell % lanes).astype(F32)).astype(BF)
 
+    prepare()
     mask = z_mask(shape, 1)
     even = lax.axis_index("gz") % 2 == 0
     filled = (iota((shape.block, 2 * cells), 1) < cells) == even
@@ -450,7 +465,6 @@
         cell = jnp.concatenate([cell_ref[0, 0]] * 2, axis=1)
         cell_mask = iota((cells, 2 * slots), 0) == cell // lanes
     weights = jnp.concatenate([weight[...]] * shape.chunk, axis=0)
-    out_sides = out_ref.shape[0] // cells
 
     def expand(lines, where, first):
         rows = []
@@ -460,8 +474,7 @@
         return jnp.concatenate(rows, axis=0).astype(BF)
 
     def work(step):
-        local = step * shape.block
-        at = local if out_sides == shape.sides else grid_step * out_sides + local
+        at = step * shape.block
         sides = pl.ds(aligned(at, shape.block), shape.block)
         size = shape.block * cells
         zs = 0.0
@@ -499,8 +512,7 @@
                     source_ref[rows, :] = source.astype(BF)
                 centre = field_ref[rows, :].astype(F32)
                 fresh = (1.0 - OMEGA) * centre + weights * (source + near[:, cols])
-                to = pl.ds(aligned(local * cells + start, shape.rows), shape.rows)
-                out_ref[to, :] = fresh.astype(BF)
+                out_ref[rows, :] = fresh.astype(BF)
                 if not last:
                     tall[step, start : start + shape.rows, :] = fresh
 
@@ -509,11 +521,20 @@
         fresh = out_ref[at * cells : at * cells + size, :]
         emit_faces(shape, at, fresh, tall.at[step], face_refs, z_ref, ends_m, rsum)
 
-    steps = out_sides // shape.block
+    steps = shape.sides // shape.block
+    copies = []
     for step in range(steps):
         work(step)
-        if not last and step > 0:
+        if last:
+            span = pl.ds(step * shape.block * cells, shape.block * cells)
+            copies.append(
+                pltpu.make_async_copy(out_ref.at[span], result_ref.at[span], out_sems.at[step])
+            )
+            copies[-1].start()
+        elif step > 0:
             emit(step - 1)
+    for copy in copies:
+        copy.wait()
     if not last:
         emit(steps - 1)
 
@@ -521,8 +542,7 @@
 def sweep(shape, field, load, coef, halos, recv=(), flux_cell=None, last=False):
     lanes, cells = shape.lanes, shape.cells
     steps = shape.sides // shape.block
-    grid = steps if last else 1
-    half = (steps // grid, shape.half_rows, 2 * lanes)
+    half = (steps, shape.half_rows, 2 * lanes)
     operands = [field, load, coef, *halos, *recv]
     out_shapes = [jax.ShapeDtypeStruct(field.shape, BF)]
     scratch = [
@@ -531,7 +551,9 @@
         pltpu.VMEM((2 * lanes + 4 * cells, 2 * lanes), BF),
         pltpu.VMEM(half, F32),
     ]
-    if not last:
+    if last:
+        scratch += [pltpu.VMEM(field.shape, BF), pltpu.SemaphoreType.DMA((steps,))]
+    else:
         out_shapes += face_outputs(shape)
         tall, *others = face_scratch(shape)
         scratch += [pltpu.VMEM((steps, *tall.shape), F32), *others]
@@ -549,10 +571,9 @@
         ]
     out_specs = [WHOLE] * len(out_shapes)
     if last:
-        out_specs = [pl.BlockSpec((field.shape[0] // grid, lanes), lambda i: (i, 0))]
+        out_specs = [pl.BlockSpec(memory_space=pltpu.HBM)]
     return pl.pallas_call(
         functools.partial(sweep_kernel, shape, len(recv), last),
-        grid=(grid,),
         in_specs=[WHOLE] * len(operands),
         out_specs=out_specs,
         out_shape=out_shapes,
@@ -597,9 +618,11 @@
     *faces, held = first_faces(shape, field, surface_block, slots)
     parts = row_gather(trace, faces)
     halos = exchange(shape, faces)
-    early = len([face for face in shape.faces if face[0] == "col"])
-    parts, halos[:early] = lax.optimization_barrier((parts, halos[:early]))
-    recv, halos[early:] = flux_sums(parts, held, halos[early:])
+    late = shape.faces.index(("row", 1)) if ("row", 1) in shape.faces else 0
+    rest = [halo for place, halo in enumerate(halos) if place != late]
+    parts, rest = lax.optimization_barrier((parts, rest))
+    recv, halo = flux_sums(parts, held, halos[late])
+    halos = rest[:late] + [halo] + rest[late:]
 
     current, *faces, source, surface_flux = sweep(
         shape, field, load, coef, halos, recv=recv, flux_cell=flux_cell

time: 65 us -> 66.5 us (1.023)
  starting transfers between devices: 23.5 us -> 25.6 us
  Pallas kernels: 22.8 us -> 21.3 us
  waiting for transfers between devices: 17.7 us -> 18.4 us
    ppermute x1, waiting for transfers between devices: 0.01 us -> 2.74 us  [flux_sums(): other = lax.ppermute(other, 'col', [(0, 1), (1, 0)])]
    ppermute x15, waiting for transfers between devices: 13.5 us -> 11.4 us  [swap(): return lax.ppermute(value, axes, pairs)]
    ppermute x15, starting transfers between devices: 14 us -> 16.1 us  [swap(): return lax.ppermute(value, axes, pairs)]
    pallas_call x1, Pallas kernels: 6.07 us -> 5.08 us  [traces(): pl.pallas_call(functools.partial(trace_kernel, stride, block), in_specs=[...]
  transfers between devices with their start and end apart: 22 -> 22, of which waited for: 8 -> 8; matrix products, arithmetic and copies ran while one was open for 0% -> 0% of each run, Pallas kernels for 7% -> 6%
where the time goes in v7:
time: 66.5 us; the launch traced here: 66.3 us
  starting transfers between devices  25.6 us (38%)
  Pallas kernels  21.3 us (32%)
  waiting for transfers between devices  18.4 us (28%)
  between operations  0.91 us (1%)
    ppermute x15, starting transfers between devices, swap(): return lax.ppermute(value, axes, pairs)  16.1 us
    pallas_call x3, Pallas kernels, sweep(): pl.pallas_call(functools.partial(sweep_kernel, shape, len(recv), last), i...  11.9 us
    ppermute x15, waiting for transfers between devices, swap(): return lax.ppermute(value, axes, pairs)  11.4 us
    pallas_call x1, Pallas kernels, traces(): pl.pallas_call(functools.partial(trace_kernel, stride, block), in_specs=[...  5.08 us
    ppermute x3, starting transfers between devices, flux_sums(): lax.ppermute(sent[key], 'gz', [(i, i ^ key) for i in range(gzs)])  4.45 us
    ppermute x3, starting transfers between devices, row_gather(): lax.ppermute(held[key], 'row', pairs)  3.51 us
    pallas_call x1, Pallas kernels, first_faces(): pl.pallas_call(functools.partial(faces_kernel, shape, slots), in_specs=[p...  3.46 us
    ppermute x3, waiting for transfers between devices, flux_sums(): lax.ppermute(sent[key], 'gz', [(i, i ^ key) for i in range(gzs)])  2.91 us
  transfers between devices with their start and end apart: 22, of which 8 were waited for; matrix products, arithmetic and copies ran while one was open for 0% of the time, Pallas kernels for 6%

profile of v7, /device:TPU:0, one launch (start us, length us, event | category | flops | bytes accessed | tf_op | source)
XLA Modules:
  0.0 66.3 jit_solution(12963930341837634467)
XLA Ops:
  0.6 5.1 %shard_map.77.refs_0_ = bf16[1024,128]{1,0:T(8,128)(2,1)} custom-call(bf16[128,64,128]{2,1,0:T(8,128)(2,1)} %bitcast.5, s32[1,1,1,1024]{3,2,1,0:T(1,128)} %cell_ref.1), custom_call_target="tpu_custom_call" | custom-call | flops 536870912 | bytes 2097152 | tf_op jit(solution)/shard_map/pallas_call | solution.py:100
  5.7 3.0 %collective-permute-start = (bf16[1024,128]{1,0:T(8,128)(2,1)}, bf16[1024,128]{1,0:T(8,128)(2,1)S(1)}, u32[]{:S(2)}, u32[]{:S(2)}) collective-permute-start(bf16[1024,128]{1,0:T(8,128)(2,1)} %shard_map.77.refs_0_), channel_id=1, source_target_pairs={{0,16},{8,24},{16,0},{24,8},{1,17},{9,25},{17,1},{25,9},{2,18},{10... | collective-permute-start | bytes 786440 | tf_op jit(solution)/shard_map/ppermute | solution.py:600
  8.7 3.5 %shard_map.78 = (bf16[1024,128]{1,0:T(8,128)(2,1)S(1)}, bf16[1024,128]{1,0:T(8,128)(2,1)S(1)}, bf16[1024,128]{1,0:T(8,128)(2,1)S(1)}, bf16[128,128]{1,0:T(8,128)(2,1)S(1)}, bf16[4,256,1024]{2,1,0:T(8,128)(2,1)S(1)}) custom-call(bf16[8192,128]{1,0:T(8,128)(2,1)} %bitcast.6, bf16[256,16384]{1,0:T(8,128)(2,1)} %block_ref.1), custom_call_target="tpu_custom_call" | custom-call | flops 134217728 | bytes 4194304 | tf_op jit(solution)/shard_map/pallas_call | solution.py:383
  12.2 1.6 %collective-permute-start.3 = (bf16[1024,128]{1,0:T(8,128)(2,1)S(1)}, bf16[1024,128]{1,0:T(8,128)(2,1)S(1)}, u32[]{:S(2)}, u32[]{:S(2)}) collective-permute-start(bf16[1024,128]{1,0:T(8,128)(2,1)S(1)} %get-tuple-element.40), channel_id=1, source_target_pairs={{0,4},{1,5},{2,6},{3,7},{4,0},{5,1},{6,2},{7,3},{8,12},{9,13},{10,... | collective-permute-start | bytes 786440 | tf_op jit(solution)/shard_map/ppermute | solution.py:249
  13.8 1.4 %collective-permute-done.refs_2_ = bf16[1024,128]{1,0:T(8,128)(2,1)S(1)} collective-permute-done((bf16[1024,128]{1,0:T(8,128)(2,1)}, bf16[1024,128]{1,0:T(8,128)(2,1)S(1)}, u32[]{:S(2)}, u32[]{:S(2)}) %collective-permute-start) | collective-permute-done | bytes 262176 | tf_op jit(solution)/shard_map/ppermute | solution.py:600
  15.2 0.5 collective-permute-start.2
  15.8 1.4 %collective-permute-done.6.refs_7_ = bf16[128,128]{1,0:T(8,128)(2,1)S(1)} collective-permute-done((bf16[128,128]{1,0:T(8,128)(2,1)S(1)}, bf16[128,128]{1,0:T(8,128)(2,1)S(1)}, u32[]{:S(2)}, u32[]{:S(2)}) %collective-permute-start.6) | collective-permute-done | bytes 32800 | tf_op jit(solution)/shard_map/ppermute | solution.py:249
  17.2 4.3 %collective-permute-start.5 = (bf16[128,128]{1,0:T(8,128)(2,1)S(1)}, bf16[128,128]{1,0:T(8,128)(2,1)S(1)}, u32[]{:S(2)}, u32[]{:S(2)}) collective-permute-start(bf16[128,128]{1,0:T(8,128)(2,1)S(1)} %get-tuple-element.43), channel_id=1, source_target_pairs={{0,1},{1,0},{2,3},{3,2},{4,5},{5,4},{6,7},{7,6},{8,9},{9,8},{10,11... | collective-permute-start | bytes 98312 | tf_op jit(solution)/shard_map/ppermute | solution.py:249
  21.5 1.9 %collective-permute-done.5.refs_6_ = bf16[128,128]{1,0:T(8,128)(2,1)S(1)} collective-permute-done((bf16[128,128]{1,0:T(8,128)(2,1)S(1)}, bf16[128,128]{1,0:T(8,128)(2,1)S(1)}, u32[]{:S(2)}, u32[]{:S(2)}) %collective-permute-start.5) | collective-permute-done | bytes 32800 | tf_op jit(solution)/shard_map/ppermute | solution.py:249
  23.4 2.0 %collective-permute-start.8 = (bf16[1024,128]{1,0:T(8,128)(2,1)S(1)}, bf16[1024,128]{1,0:T(8,128)(2,1)S(1)}, u32[]{:S(2)}, u32[]{:S(2)}) collective-permute-start(bf16[1024,128]{1,0:T(8,128)(2,1)S(1)} %get-tuple-element.41), channel_id=1, source_target_pairs={{0,1},{1,0},{2,3},{3,2},{4,5},{5,4},{6,7},{7,6},{8,16},{9,17},{10,... | collective-permute-start | bytes 786440 | tf_op jit(solution)/shard_map/ppermute | solution.py:249
  25.4 0.7 %shard_map.79 = (f32[128,128]{1,0:T(8,128)S(1)}, f32[128,128]{1,0:T(8,128)S(1)}) custom-call(bf16[1024,128]{1,0:T(8,128)(2,1)S(1)} %copy-done.2, bf16[1024,128]{1,0:T(8,128)(2,1)S(1)} %collective-permute-done.1.refs_1_, bf16[1024,128]{1,0:T(8,128)(2,1)S(1)} %collective-permute-done.refs_2_, bf16[1024,128]{1,0:T(8,128)(2,1)S(1)} %collective-permute-done.2.refs_3_, ...), custom_call_target="tpu_custom_call" | custom-call | flops 268435456 | bytes 2097152 | tf_op jit(solution)/shard_map/pallas_call | solution.py:154
  26.1 1.6 %collective-permute-start.7 = (f32[128,128]{1,0:T(8,128)S(1)}, f32[128,128]{1,0:T(8,128)S(1)}, u32[]{:S(2)}, u32[]{:S(2)}) collective-permute-start(f32[128,128]{1,0:T(8,128)S(1)} %get-tuple-element.53), channel_id=1, source_target_pairs={{0,4},{4,0},{1,5},{5,1},{2,6},{6,2},{3,7},{7,3},{8,12},{12,8},{9,1... | collective-permute-start | bytes 196616 | tf_op jit(solution)/shard_map/ppermute | solution.py:203
  27.7 2.7 %collective-permute-done.7.other_ref = f32[128,128]{1,0:T(8,128)S(1)} collective-permute-done((f32[128,128]{1,0:T(8,128)S(1)}, f32[128,128]{1,0:T(8,128)S(1)}, u32[]{:S(2)}, u32[]{:S(2)}) %collective-permute-start.7) | collective-permute-done | bytes 65568 | tf_op jit(solution)/shard_map/ppermute | solution.py:203
  30.5 0.1 shard_map.80
  30.6 2.5 %collective-permute-start.9 = (f32[64,128]{1,0:T(8,128)S(1)}, f32[64,128]{1,0:T(8,128)S(1)}, u32[]{:S(2)}, u32[]{:S(2)}) collective-permute-start(f32[64,128]{1,0:T(8,128)S(1)} %get-tuple-element.63), channel_id=1, source_target_pairs={{0,3},{1,2},{2,1},{3,0},{4,7},{5,6},{6,5},{7,4},{8,11},{9,10},{10,... | collective-permute-start | bytes 98312 | tf_op jit(solution)/shard_map/ppermute | solution.py:208
  33.1 0.1 collective-permute-start.10
  33.2 1.8 %collective-permute-start.11 = (f32[64,128]{1,0:T(8,128)S(1)}, f32[64,128]{1,0:T(8,128)S(1)}, u32[]{:S(2)}, u32[]{:S(2)}) collective-permute-start(f32[64,128]{1,0:T(8,128)S(1)} %get-tuple-element.65), channel_id=1, source_target_pairs={{0,1},{1,0},{2,3},{3,2},{4,5},{5,4},{6,7},{7,6},{8,9},{9,8},{10,11... | collective-permute-start | bytes 98312 | tf_op jit(solution)/shard_map/ppermute | solution.py:208
  35.1 1.5 %collective-permute-done.9.refs_9_ = f32[64,128]{1,0:T(8,128)S(1)} collective-permute-done((f32[64,128]{1,0:T(8,128)S(1)}, f32[64,128]{1,0:T(8,128)S(1)}, u32[]{:S(2)}, u32[]{:S(2)}) %collective-permute-start.9) | collective-permute-done | bytes 32800 | tf_op jit(solution)/shard_map/ppermute | solution.py:208
  36.6 1.4 %collective-permute-done.10.refs_10_ = f32[64,128]{1,0:T(8,128)S(1)} collective-permute-done((f32[64,128]{1,0:T(8,128)S(1)}, f32[64,128]{1,0:T(8,128)S(1)}, u32[]{:S(2)}, u32[]{:S(2)}) %collective-permute-start.10) | collective-permute-done | bytes 32800 | tf_op jit(solution)/shard_map/ppermute | solution.py:208
  38.0 4.7 %shard_map.81 = (bf16[8192,128]{1,0:T(8,128)(2,1)S(1)}, bf16[1024,128]{1,0:T(8,128)(2,1)S(1)}, bf16[1024,128]{1,0:T(8,128)(2,1)S(1)}, bf16[1024,128]{1,0:T(8,128...) custom-call(bf16[8192,128]{1,0:T(8,128)(2,1)S(1)} %bitcast.7, ...), custom_call_target="tpu_custom_call" | custom-call | flops 805306368 | bytes 8388608 | tf_op jit(solution)/shard_map/pallas_call | solution.py:575
  42.7 1.5 %collective-permute-start.12 = (bf16[1024,128]{1,0:T(8,128)(2,1)S(1)}, bf16[1024,128]{1,0:T(8,128)(2,1)S(1)}, u32[]{:S(2)}, u32[]{:S(2)}) collective-permute-start(bf16[1024,128]{1,0:T(8,128)(2,1)S(1)} %get-tuple-element.68), channel_id=1, source_target_pairs={{0,4},{1,5},{2,6},{3,7},{4,0},{5,1},{6,2},{7,3},{8,12},{9,13},{10,... | collective-permute-start | bytes 786440 | tf_op jit(solution)/shard_map/ppermute | solution.py:249
  44.2 1.0 %collective-permute-start.13 = (bf16[1024,128]{1,0:T(8,128)(2,1)S(1)}, bf16[1024,128]{1,0:T(8,128)(2,1)S(1)}, u32[]{:S(2)}, u32[]{:S(2)}) collective-permute-start(bf16[1024,128]{1,0:T(8,128)(2,1)S(1)} %get-tuple-element.69), channel_id=1, source_target_pairs={{0,1},{1,0},{2,3},{3,2},{4,5},{5,4},{6,7},{7,6},{8,16},{9,17},{10,... | collective-permute-start | bytes 786440 | tf_op jit(solution)/shard_map/ppermute | solution.py:249
  45.2 0.5 collective-permute-start.16
  45.7 1.6 %collective-permute-start.15 = (bf16[128,128]{1,0:T(8,128)(2,1)S(1)}, bf16[128,128]{1,0:T(8,128)(2,1)S(1)}, u32[]{:S(2)}, u32[]{:S(2)}) collective-permute-start(bf16[128,128]{1,0:T(8,128)(2,1)S(1)} %get-tuple-element.71), channel_id=1, source_target_pairs={{0,1},{1,0},{2,3},{3,2},{4,5},{5,4},{6,7},{7,6},{8,9},{9,8},{10,11... | collective-permute-start | bytes 98312 | tf_op jit(solution)/shard_map/ppermute | solution.py:249
  47.3 4.0 %collective-permute-done.15.refs_6_ = bf16[128,128]{1,0:T(8,128)(2,1)S(1)} collective-permute-done((bf16[128,128]{1,0:T(8,128)(2,1)S(1)}, bf16[128,128]{1,0:T(8,128)(2,1)S(1)}, u32[]{:S(2)}, u32[]{:S(2)}) %collective-permute-start.15) | collective-permute-done | bytes 32800 | tf_op jit(solution)/shard_map/ppermute | solution.py:249
  51.3 3.9 %shard_map.82 = (bf16[8192,128]{1,0:T(8,128)(2,1)S(1)}, bf16[1024,128]{1,0:T(8,128)(2,1)S(1)}, bf16[1024,128]{1,0:T(8,128)(2,1)S(1)}, bf16[1024,128]{1,0:T(8,128)(2,1)S(1)}, bf16[128,128]{1,0:T(8,128)(2,1)S(1)}) custom-call(bf16[8192,128]{1,0:T(8,128)(2,1)S(1)} %get-tuple-element.66.refs_0_, bf16[8192,128]{1,0:T(8,128)(2,1)S(1)} %get-tuple-element.67.refs_1_, ...), custom_call_target="tpu_custom_call" | custom-call | flops 805306368 | bytes 8388608 | tf_op jit(solution)/shard_map/pallas_call | solution.py:575
  55.2 0.5 collective-permute-start.17
  55.7 1.0 %collective-permute-start.18 = (bf16[1024,128]{1,0:T(8,128)(2,1)S(1)}, bf16[1024,128]{1,0:T(8,128)(2,1)S(1)}, u32[]{:S(2)}, u32[]{:S(2)}) collective-permute-start(bf16[1024,128]{1,0:T(8,128)(2,1)S(1)} %get-tuple-element.74), channel_id=1, source_target_pairs={{0,1},{1,0},{2,3},{3,2},{4,5},{5,4},{6,7},{7,6},{8,16},{9,17},{10,... | collective-permute-start | bytes 786440 | tf_op jit(solution)/shard_map/ppermute | solution.py:249
  56.7 0.5 collective-permute-start.21
  57.2 1.6 %collective-permute-start.20 = (bf16[128,128]{1,0:T(8,128)(2,1)S(1)}, bf16[128,128]{1,0:T(8,128)(2,1)S(1)}, u32[]{:S(2)}, u32[]{:S(2)}) collective-permute-start(bf16[128,128]{1,0:T(8,128)(2,1)S(1)} %get-tuple-element.76), channel_id=1, source_target_pairs={{0,1},{1,0},{2,3},{3,2},{4,5},{5,4},{6,7},{7,6},{8,9},{9,8},{10,11... | collective-permute-start | bytes 98312 | tf_op jit(solution)/shard_map/ppermute | solution.py:249
  58.8 4.0 %collective-permute-done.20.refs_6_ = bf16[128,128]{1,0:T(8,128)(2,1)S(1)} collective-permute-done((bf16[128,128]{1,0:T(8,128)(2,1)S(1)}, bf16[128,128]{1,0:T(8,128)(2,1)S(1)}, u32[]{:S(2)}, u32[]{:S(2)}) %collective-permute-start.20) | collective-permute-done | bytes 32800 | tf_op jit(solution)/shard_map/ppermute | solution.py:249
  62.8 3.3 %shard_map.83 = bf16[8192,128]{1,0:T(8,128)(2,1)} custom-call(bf16[8192,128]{1,0:T(8,128)(2,1)S(1)} %get-tuple-element.72.refs_0_, bf16[8192,128]{1,0:T(8,128)(2,1)S(1)} %get-tuple-element.67.refs_1_, f32[64,128]{1,0:T(8,128)S(1)} %bitcast.11, bf16[1024,128]{1,0:T(8,128)(2,1)S(1)} %collective-permute-done.17.refs_3_, ...), custom_call_target="tpu_custom_call" | custom-call | flops 805306368 | bytes 8388608 | tf_op jit(solution)/shard_map/pallas_call | solution.py:575
  (29 shorter events, 0.1 us)
Async XLA Ops:
  5.7 9.5 %collective-permute-start = (bf16[1024,128]{1,0:T(8,128)(2,1)}, bf16[1024,128]{1,0:T(8,128)(2,1)S(1)}, u32[]{:S(2)}, u32[]{:S(2)}) collective-permute-start(bf16[1024,128]{1,0:T(8,128)(2,1)} %shard_map.77.refs_0_), channel_id=1, source_target_pairs={{0,16},{8,24},{16,0},{24,8},{1,17},{9,25},{17,1},{25,9},{2,18},{10... | collective-permute-start | bytes 786440 | tf_op jit(solution)/shard_map/ppermute | solution.py:600
  8.7 6.5 %copy-start.2 = (bf16[1024,128]{1,0:T(8,128)(2,1)S(1)}, bf16[1024,128]{1,0:T(8,128)(2,1)}, u32[]{:S(2)}) copy-start(bf16[1024,128]{1,0:T(8,128)(2,1)} %shard_map.77.refs_0_) | copy-start | bytes 786436
  8.7 29.2 %copy-start.1 = (bf16[128,8,8,128]{3,2,1,0:T(8,128)(2,1)S(1)}, bf16[128,8,8,128]{3,2,1,0:T(8,128)(2,1)}, u32[]{:S(2)}) copy-start(bf16[128,8,8,128]{3,2,1,0:T(8,128)(2,1)} %param.7) | copy-start | bytes 6291460
  12.2 25.8 %copy-start = (bf16[128,8,8,128]{3,2,1,0:T(8,128)(2,1)S(1)}, bf16[128,8,8,128]{3,2,1,0:T(8,128)(2,1)}, u32[]{:S(2)}) copy-start(bf16[128,8,8,128]{3,2,1,0:T(8,128)(2,1)} %param.6) | copy-start | bytes 6291460
  12.2 25.8 %copy-start.3 = (f32[8,8,128]{2,1,0:T(8,128)S(1)}, f32[8,8,128]{2,1,0:T(8,128)}, u32[]{:S(2)}) copy-start(f32[8,8,128]{2,1,0:T(8,128)} %param.8) | copy-start | bytes 98308
  12.2 25.8 %copy-start.4 = (s32[1,1,1,32]{3,2,1,0:T(1,128)S(1)}, s32[1,1,1,32]{3,2,1,0:T(1,128)}, u32[]{:S(2)}) copy-start(s32[1,1,1,32]{3,2,1,0:T(1,128)} %refs_12_.1) | copy-start | bytes 388
  12.2 13.2 %collective-permute-start.3 = (bf16[1024,128]{1,0:T(8,128)(2,1)S(1)}, bf16[1024,128]{1,0:T(8,128)(2,1)S(1)}, u32[]{:S(2)}, u32[]{:S(2)}) collective-permute-start(bf16[1024,128]{1,0:T(8,128)(2,1)S(1)} %get-tuple-element.40), channel_id=1, source_target_pairs={{0,4},{1,5},{2,6},{3,7},{4,0},{5,1},{6,2},{7,3},{8,12},{9,13},{10,... | collective-permute-start | bytes 786440 | tf_op jit(solution)/shard_map/ppermute | solution.py:249
  13.8 11.6 %collective-permute-start.4 = (bf16[1024,128]{1,0:T(8,128)(2,1)S(1)}, bf16[1024,128]{1,0:T(8,128)(2,1)S(1)}, u32[]{:S(2)}, u32[]{:S(2)}) collective-permute-start(bf16[1024,128]{1,0:T(8,128)(2,1)S(1)} %get-tuple-element.42), channel_id=1, source_target_pairs={{0,8},{1,9},{2,10},{3,11},{4,12},{5,13},{6,14},{7,15},{8,0},{9,1},... | collective-permute-start | bytes 786440 | tf_op jit(solution)/shard_map/ppermute | solution.py:249
  15.2 10.2 %collective-permute-start.1 = (bf16[1024,128]{1,0:T(8,128)(2,1)S(1)}, bf16[1024,128]{1,0:T(8,128)(2,1)S(1)}, u32[]{:S(2)}, u32[]{:S(2)}) collective-permute-start(bf16[1024,128]{1,0:T(8,128)(2,1)S(1)} %copy-done.2), channel_id=1, source_target_pairs={{0,8},{8,0},{16,24},{24,16},{1,9},{9,1},{17,25},{25,17},{2,10},{10... | collective-permute-start | bytes 786440 | tf_op jit(solution)/shard_map/ppermute | solution.py:600
  15.2 10.2 %collective-permute-start.2 = (bf16[1024,128]{1,0:T(8,128)(2,1)S(1)}, bf16[1024,128]{1,0:T(8,128)(2,1)S(1)}, u32[]{:S(2)}, u32[]{:S(2)}) collective-permute-start(bf16[1024,128]{1,0:T(8,128)(2,1)S(1)} %collective-permute-done.refs_2_), channel_id=1, source_target_pairs={{0,8},{8,0},{16,24},{24,16},{1,9},{9,1},{17,25},{25,17},{2,10},{10... | collective-permute-start | bytes 786440 | tf_op jit(solution)/shard_map/ppermute | solution.py:600
  15.8 1.4 %collective-permute-start.6 = (bf16[128,128]{1,0:T(8,128)(2,1)S(1)}, bf16[128,128]{1,0:T(8,128)(2,1)S(1)}, u32[]{:S(2)}, u32[]{:S(2)}) collective-permute-start(bf16[128,128]{1,0:T(8,128)(2,1)S(1)} %get-tuple-element.43), channel_id=1, source_target_pairs={{0,8},{1,2},{2,1},{3,11},{4,12},{5,6},{6,5},{7,15},{8,0},{9,10},{1... | collective-permute-start | bytes 98312 | tf_op jit(solution)/shard_map/ppermute | solution.py:249
  17.2 6.2 %collective-permute-start.5 = (bf16[128,128]{1,0:T(8,128)(2,1)S(1)}, bf16[128,128]{1,0:T(8,128)(2,1)S(1)}, u32[]{:S(2)}, u32[]{:S(2)}) collective-permute-start(bf16[128,128]{1,0:T(8,128)(2,1)S(1)} %get-tuple-element.43), channel_id=1, source_target_pairs={{0,1},{1,0},{2,3},{3,2},{4,5},{5,4},{6,7},{7,6},{8,9},{9,8},{10,11... | collective-permute-start | bytes 98312 | tf_op jit(solution)/shard_map/ppermute | solution.py:249
  23.4 7.2 %collective-permute-start.8 = (bf16[1024,128]{1,0:T(8,128)(2,1)S(1)}, bf16[1024,128]{1,0:T(8,128)(2,1)S(1)}, u32[]{:S(2)}, u32[]{:S(2)}) collective-permute-start(bf16[1024,128]{1,0:T(8,128)(2,1)S(1)} %get-tuple-element.41), channel_id=1, source_target_pairs={{0,1},{1,0},{2,3},{3,2},{4,5},{5,4},{6,7},{7,6},{8,16},{9,17},{10,... | collective-permute-start | bytes 786440 | tf_op jit(solution)/shard_map/ppermute | solution.py:249
  26.1 4.3 %collective-permute-start.7 = (f32[128,128]{1,0:T(8,128)S(1)}, f32[128,128]{1,0:T(8,128)S(1)}, u32[]{:S(2)}, u32[]{:S(2)}) collective-permute-start(f32[128,128]{1,0:T(8,128)S(1)} %get-tuple-element.53), channel_id=1, source_target_pairs={{0,4},{4,0},{1,5},{5,1},{2,6},{6,2},{3,7},{7,3},{8,12},{12,8},{9,1... | collective-permute-start | bytes 196616 | tf_op jit(solution)/shard_map/ppermute | solution.py:203
  30.6 6.0 %collective-permute-start.9 = (f32[64,128]{1,0:T(8,128)S(1)}, f32[64,128]{1,0:T(8,128)S(1)}, u32[]{:S(2)}, u32[]{:S(2)}) collective-permute-start(f32[64,128]{1,0:T(8,128)S(1)} %get-tuple-element.63), channel_id=1, source_target_pairs={{0,3},{1,2},{2,1},{3,0},{4,7},{5,6},{6,5},{7,4},{8,11},{9,10},{10,... | collective-permute-start | bytes 98312 | tf_op jit(solution)/shard_map/ppermute | solution.py:208
  33.1 4.8 %collective-permute-start.10 = (f32[64,128]{1,0:T(8,128)S(1)}, f32[64,128]{1,0:T(8,128)S(1)}, u32[]{:S(2)}, u32[]{:S(2)}) collective-permute-start(f32[64,128]{1,0:T(8,128)S(1)} %get-tuple-element.64), channel_id=1, source_target_pairs={{0,2},{1,3},{2,0},{3,1},{4,6},{5,7},{6,4},{7,5},{8,10},{9,11},{10,... | collective-permute-start | bytes 98312 | tf_op jit(solution)/shard_map/ppermute | solution.py:208
  33.2 4.7 %collective-permute-start.11 = (f32[64,128]{1,0:T(8,128)S(1)}, f32[64,128]{1,0:T(8,128)S(1)}, u32[]{:S(2)}, u32[]{:S(2)}) collective-permute-start(f32[64,128]{1,0:T(8,128)S(1)} %get-tuple-element.65), channel_id=1, source_target_pairs={{0,1},{1,0},{2,3},{3,2},{4,5},{5,4},{6,7},{7,6},{8,9},{9,8},{10,11... | collective-permute-start | bytes 98312 | tf_op jit(solution)/shard_map/ppermute | solution.py:208
  42.7 8.6 %collective-permute-start.12 = (bf16[1024,128]{1,0:T(8,128)(2,1)S(1)}, bf16[1024,128]{1,0:T(8,128)(2,1)S(1)}, u32[]{:S(2)}, u32[]{:S(2)}) collective-permute-start(bf16[1024,128]{1,0:T(8,128)(2,1)S(1)} %get-tuple-element.68), channel_id=1, source_target_pairs={{0,4},{1,5},{2,6},{3,7},{4,0},{5,1},{6,2},{7,3},{8,12},{9,13},{10,... | collective-permute-start | bytes 786440 | tf_op jit(solution)/shard_map/ppermute | solution.py:249
  44.2 7.1 %collective-permute-start.13 = (bf16[1024,128]{1,0:T(8,128)(2,1)S(1)}, bf16[1024,128]{1,0:T(8,128)(2,1)S(1)}, u32[]{:S(2)}, u32[]{:S(2)}) collective-permute-start(bf16[1024,128]{1,0:T(8,128)(2,1)S(1)} %get-tuple-element.69), channel_id=1, source_target_pairs={{0,1},{1,0},{2,3},{3,2},{4,5},{5,4},{6,7},{7,6},{8,16},{9,17},{10,... | collective-permute-start | bytes 786440 | tf_op jit(solution)/shard_map/ppermute | solution.py:249
  45.2 6.1 %collective-permute-start.14 = (bf16[1024,128]{1,0:T(8,128)(2,1)S(1)}, bf16[1024,128]{1,0:T(8,128)(2,1)S(1)}, u32[]{:S(2)}, u32[]{:S(2)}) collective-permute-start(bf16[1024,128]{1,0:T(8,128)(2,1)S(1)} %get-tuple-element.70), channel_id=1, source_target_pairs={{0,8},{1,9},{2,10},{3,11},{4,12},{5,13},{6,14},{7,15},{8,0},{9,1},... | collective-permute-start | bytes 786440 | tf_op jit(solution)/shard_map/ppermute | solution.py:249
  45.2 2.1 %collective-permute-start.16 = (bf16[128,128]{1,0:T(8,128)(2,1)S(1)}, bf16[128,128]{1,0:T(8,128)(2,1)S(1)}, u32[]{:S(2)}, u32[]{:S(2)}) collective-permute-start(bf16[128,128]{1,0:T(8,128)(2,1)S(1)} %get-tuple-element.71), channel_id=1, source_target_pairs={{0,8},{1,2},{2,1},{3,11},{4,12},{5,6},{6,5},{7,15},{8,0},{9,10},{1... | collective-permute-start | bytes 98312 | tf_op jit(solution)/shard_map/ppermute | solution.py:249
  45.7 5.6 %collective-permute-start.15 = (bf16[128,128]{1,0:T(8,128)(2,1)S(1)}, bf16[128,128]{1,0:T(8,128)(2,1)S(1)}, u32[]{:S(2)}, u32[]{:S(2)}) collective-permute-start(bf16[128,128]{1,0:T(8,128)(2,1)S(1)} %get-tuple-element.71), channel_id=1, source_target_pairs={{0,1},{1,0},{2,3},{3,2},{4,5},{5,4},{6,7},{7,6},{8,9},{9,8},{10,11... | collective-permute-start | bytes 98312 | tf_op jit(solution)/shard_map/ppermute | solution.py:249
  55.2 7.6 %collective-permute-start.17 = (bf16[1024,128]{1,0:T(8,128)(2,1)S(1)}, bf16[1024,128]{1,0:T(8,128)(2,1)S(1)}, u32[]{:S(2)}, u32[]{:S(2)}) collective-permute-start(bf16[1024,128]{1,0:T(8,128)(2,1)S(1)} %get-tuple-element.73), channel_id=1, source_target_pairs={{0,4},{1,5},{2,6},{3,7},{4,0},{5,1},{6,2},{7,3},{8,12},{9,13},{10,... | collective-permute-start | bytes 786440 | tf_op jit(solution)/shard_map/ppermute | solution.py:249
  55.7 7.1 %collective-permute-start.18 = (bf16[1024,128]{1,0:T(8,128)(2,1)S(1)}, bf16[1024,128]{1,0:T(8,128)(2,1)S(1)}, u32[]{:S(2)}, u32[]{:S(2)}) collective-permute-start(bf16[1024,128]{1,0:T(8,128)(2,1)S(1)} %get-tuple-element.74), channel_id=1, source_target_pairs={{0,1},{1,0},{2,3},{3,2},{4,5},{5,4},{6,7},{7,6},{8,16},{9,17},{10,... | collective-permute-start | bytes 786440 | tf_op jit(solution)/shard_map/ppermute | solution.py:249
  56.7 6.1 %collective-permute-start.19 = (bf16[1024,128]{1,0:T(8,128)(2,1)S(1)}, bf16[1024,128]{1,0:T(8,128)(2,1)S(1)}, u32[]{:S(2)}, u32[]{:S(2)}) collective-permute-start(bf16[1024,128]{1,0:T(8,128)(2,1)S(1)} %get-tuple-element.75), channel_id=1, source_target_pairs={{0,8},{1,9},{2,10},{3,11},{4,12},{5,13},{6,14},{7,15},{8,0},{9,1},... | collective-permute-start | bytes 786440 | tf_op jit(solution)/shard_map/ppermute | solution.py:249
  56.7 2.1 %collective-permute-start.21 = (bf16[128,128]{1,0:T(8,128)(2,1)S(1)}, bf16[128,128]{1,0:T(8,128)(2,1)S(1)}, u32[]{:S(2)}, u32[]{:S(2)}) collective-permute-start(bf16[128,128]{1,0:T(8,128)(2,1)S(1)} %get-tuple-element.76), channel_id=1, source_target_pairs={{0,8},{1,2},{2,1},{3,11},{4,12},{5,6},{6,5},{7,15},{8,0},{9,10},{1... | collective-permute-start | bytes 98312 | tf_op jit(solution)/shard_map/ppermute | solution.py:249
  57.2 5.6 %collective-permute-start.20 = (bf16[128,128]{1,0:T(8,128)(2,1)S(1)}, bf16[128,128]{1,0:T(8,128)(2,1)S(1)}, u32[]{:S(2)}, u32[]{:S(2)}) collective-permute-start(bf16[128,128]{1,0:T(8,128)(2,1)S(1)} %get-tuple-element.76), channel_id=1, source_target_pairs={{0,1},{1,0},{2,3},{3,2},{4,5},{5,4},{6,7},{7,6},{8,9},{9,8},{10,11... | collective-permute-start | bytes 98312 | tf_op jit(solution)/shard_map/ppermute | solution.py:249

commit v8 on v7

--- a/solution.py
+++ b/solution.py
@@ -201,8 +201,8 @@
     if cols == 2 and gzs & (gzs - 1) == 0 and lines // cols == sides and sides // gzs % 8 == 0:
         mine, other = surface(parts, held, 2)
         other = lax.ppermute(other, "col", [(0, 1), (1, 0)])
+        other, late = lax.optimization_barrier((other, late))
         sent = shares(mine, other)
-        sent, late = lax.optimization_barrier((sent, late))
         recv = [sent[0]]
         for key in range(gzs - 1, 0, -1):
             recv.append(lax.ppermute(sent[key], "gz", [(i, i ^ key) for i in range(gzs)]))
@@ -591,7 +591,7 @@
     return halos + [swap(ends, "gz", turn) for turn in range(shape.ends)]
 
 
-def row_gather(trace, faces):
+def row_gather(trace, hidden):
     peers = lax.axis_size("row")
     held = {0: trace}
     bit = peers // 2
@@ -599,10 +599,10 @@
         pairs = [(i, i ^ bit) for i in range(peers)]
         fresh = {key ^ bit: lax.ppermute(held[key], "row", pairs) for key in sorted(held, reverse=True)}
         if bit == peers // 2:
-            held, fresh, _ = lax.optimization_barrier((held, fresh, faces))
+            held, fresh, hidden = lax.optimization_barrier((held, fresh, hidden))
         held.update(fresh)
         bit //= 2
-    return [held[key] for key in range(peers)]
+    return [held[key] for key in range(peers)], hidden
 
 
 def per_device(volume_field, volume_load, coefficient, surface_block, trace_cell, flux_cell):
@@ -616,13 +616,13 @@
     slots = trace_cell.shape[3]
     trace = traces(volume_field.reshape(sides, cells, lanes), trace_cell, min(32, sides))
     *faces, held = first_faces(shape, field, surface_block, slots)
-    parts = row_gather(trace, faces)
     halos = exchange(shape, faces)
-    late = shape.faces.index(("row", 1)) if ("row", 1) in shape.faces else 0
-    rest = [halo for place, halo in enumerate(halos) if place != late]
-    parts, rest = lax.optimization_barrier((parts, rest))
-    recv, halo = flux_sums(parts, held, halos[late])
-    halos = rest[:late] + [halo] + rest[late:]
+    layers = len(shape.faces)
+    parts, (_, ends) = row_gather(trace, (faces, halos[layers:]))
+    early = len([face for face in shape.faces if face[0] == "col"])
+    parts, along_col = lax.optimization_barrier((parts, halos[:early]))
+    recv, along_row = flux_sums(parts, held, halos[early:layers])
+    halos = along_col + along_row + ends
 
     current, *faces, source, surface_flux = sweep(
         shape, field, load, coef, halos, recv=recv, flux_cell=flux_cell

time: 66.5 us -> 63.2 us (0.950)
  waiting for transfers between devices: 18.4 us -> 15.6 us
    ppermute x3, waiting for transfers between devices: 1.42 us -> 0.01 us  [row_gather(): lax.ppermute(held[key], 'row', pairs)]
    ppermute x15, waiting for transfers between devices: 11.4 us -> 10.4 us  [swap(): return lax.ppermute(value, axes, pairs)]
  transfers between devices with their start and end apart: 22 -> 22, of which waited for: 8 -> 7; matrix products, arithmetic and copies ran while one was open for 0% -> 0% of each run, Pallas kernels for 6% -> 7%
where the time goes in v8:
time: 63.2 us; the launch traced here: 63 us
  starting transfers between devices  25.2 us (40%)
  Pallas kernels  21.3 us (34%)
  waiting for transfers between devices  15.6 us (25%)
  between operations  0.91 us (1%)
    ppermute x15, starting transfers between devices, swap(): return lax.ppermute(value, axes, pairs)  15.6 us
    pallas_call x3, Pallas kernels, sweep(): pl.pallas_call(functools.partial(sweep_kernel, shape, len(recv), last), i...  11.9 us
    ppermute x15, waiting for transfers between devices, swap(): return lax.ppermute(value, axes, pairs)  10.4 us
    pallas_call x1, Pallas kernels, traces(): pl.pallas_call(functools.partial(trace_kernel, stride, block), in_specs=[...  5.08 us
    ppermute x3, starting transfers between devices, flux_sums(): lax.ppermute(sent[key], 'gz', [(i, i ^ key) for i in range(gzs)])  4.45 us
    ppermute x3, starting transfers between devices, row_gather(): lax.ppermute(held[key], 'row', pairs)  3.51 us
    pallas_call x1, Pallas kernels, first_faces(): pl.pallas_call(functools.partial(faces_kernel, shape, slots), in_specs=[p...  3.46 us
    ppermute x1, waiting for transfers between devices, flux_sums(): other = lax.ppermute(other, 'col', [(0, 1), (1, 0)])  2.73 us
  transfers between devices with their start and end apart: 22, of which 7 were waited for; matrix products, arithmetic and copies ran while one was open for 0% of the time, Pallas kernels for 7%

profile of v8, /device:TPU:0, one launch (start us, length us, event | category | flops | bytes accessed | tf_op | source)
XLA Modules:
  0.0 63.0 jit_solution(4830068958848734118)
XLA Ops:
  0.6 5.1 %shard_map.77.refs_0_ = bf16[1024,128]{1,0:T(8,128)(2,1)} custom-call(bf16[128,64,128]{2,1,0:T(8,128)(2,1)} %bitcast.5, s32[1,1,1,1024]{3,2,1,0:T(1,128)} %cell_ref.1), custom_call_target="tpu_custom_call" | custom-call | flops 536870912 | bytes 2097152 | tf_op jit(solution)/shard_map/pallas_call | solution.py:100
  5.7 3.0 %collective-permute-start = (bf16[1024,128]{1,0:T(8,128)(2,1)}, bf16[1024,128]{1,0:T(8,128)(2,1)S(1)}, u32[]{:S(2)}, u32[]{:S(2)}) collective-permute-start(bf16[1024,128]{1,0:T(8,128)(2,1)} %shard_map.77.refs_0_), channel_id=1, source_target_pairs={{0,16},{8,24},{16,0},{24,8},{1,17},{9,25},{17,1},{25,9},{2,18},{10... | collective-permute-start | bytes 786440 | tf_op jit(solution)/shard_map/ppermute | solution.py:600
  8.7 3.5 %shard_map.78 = (bf16[1024,128]{1,0:T(8,128)(2,1)S(1)}, bf16[1024,128]{1,0:T(8,128)(2,1)S(1)}, bf16[1024,128]{1,0:T(8,128)(2,1)S(1)}, bf16[128,128]{1,0:T(8,128)(2,1)S(1)}, bf16[4,256,1024]{2,1,0:T(8,128)(2,1)S(1)}) custom-call(bf16[8192,128]{1,0:T(8,128)(2,1)} %bitcast.6, bf16[256,16384]{1,0:T(8,128)(2,1)} %block_ref.1), custom_call_target="tpu_custom_call" | custom-call | flops 134217728 | bytes 4194304 | tf_op jit(solution)/shard_map/pallas_call | solution.py:383
  12.2 0.1 collective-permute-start.2
  12.3 3.1 %collective-permute-start.1 = (bf16[128,128]{1,0:T(8,128)(2,1)S(1)}, bf16[128,128]{1,0:T(8,128)(2,1)S(1)}, u32[]{:S(2)}, u32[]{:S(2)}) collective-permute-start(bf16[128,128]{1,0:T(8,128)(2,1)S(1)} %get-tuple-element.40), channel_id=1, source_target_pairs={{0,1},{1,0},{2,3},{3,2},{4,5},{5,4},{6,7},{7,6},{8,9},{9,8},{10,11... | collective-permute-start | bytes 98312 | tf_op jit(solution)/shard_map/ppermute | solution.py:249
  15.4 1.5 %collective-permute-start.5 = (bf16[1024,128]{1,0:T(8,128)(2,1)S(1)}, bf16[1024,128]{1,0:T(8,128)(2,1)S(1)}, u32[]{:S(2)}, u32[]{:S(2)}) collective-permute-start(bf16[1024,128]{1,0:T(8,128)(2,1)S(1)} %get-tuple-element.37), channel_id=1, source_target_pairs={{0,4},{1,5},{2,6},{3,7},{4,0},{5,1},{6,2},{7,3},{8,12},{9,13},{10,... | collective-permute-start | bytes 786440 | tf_op jit(solution)/shard_map/ppermute | solution.py:249
  17.0 0.4 collective-permute-done.1.refs_6_
  17.4 0.5 collective-permute-start.4
  17.9 2.0 %collective-permute-start.7 = (bf16[1024,128]{1,0:T(8,128)(2,1)S(1)}, bf16[1024,128]{1,0:T(8,128)(2,1)S(1)}, u32[]{:S(2)}, u32[]{:S(2)}) collective-permute-start(bf16[1024,128]{1,0:T(8,128)(2,1)S(1)} %get-tuple-element.38), channel_id=1, source_target_pairs={{0,1},{1,0},{2,3},{3,2},{4,5},{5,4},{6,7},{7,6},{8,16},{9,17},{10,... | collective-permute-start | bytes 786440 | tf_op jit(solution)/shard_map/ppermute | solution.py:249
  19.9 2.8 %collective-permute-done.5.refs_3_ = bf16[1024,128]{1,0:T(8,128)(2,1)S(1)} collective-permute-done((bf16[1024,128]{1,0:T(8,128)(2,1)S(1)}, bf16[1024,128]{1,0:T(8,128)(2,1)S(1)}, u32[]{:S(2)}, u32[]{:S(2)}) %collective-permute-start.5) | collective-permute-done | bytes 262176 | tf_op jit(solution)/shard_map/ppermute | solution.py:249
  22.7 0.7 %shard_map.79 = (f32[128,128]{1,0:T(8,128)S(1)}, f32[128,128]{1,0:T(8,128)S(1)}) custom-call(bf16[1024,128]{1,0:T(8,128)(2,1)S(1)} %copy-done.2, bf16[1024,128]{1,0:T(8,128)(2,1)S(1)} %collective-permute-done.3.refs_1_, bf16[1024,128]{1,0:T(8,128)(2,1)S(1)} %collective-permute-done.refs_2_, bf16[1024,128]{1,0:T(8,128)(2,1)S(1)} %collective-permute-done.4.refs_3_, ...), custom_call_target="tpu_custom_call" | custom-call | flops 268435456 | bytes 2097152 | tf_op jit(solution)/shard_map/pallas_call | solution.py:154
  23.4 1.6 %collective-permute-start.6 = (f32[128,128]{1,0:T(8,128)S(1)}, f32[128,128]{1,0:T(8,128)S(1)}, u32[]{:S(2)}, u32[]{:S(2)}) collective-permute-start(f32[128,128]{1,0:T(8,128)S(1)} %get-tuple-element.49), channel_id=1, source_target_pairs={{0,4},{4,0},{1,5},{5,1},{2,6},{6,2},{3,7},{7,3},{8,12},{12,8},{9,1... | collective-permute-start | bytes 196616 | tf_op jit(solution)/shard_map/ppermute | solution.py:203
  25.0 2.7 %collective-permute-done.6.other_ref = f32[128,128]{1,0:T(8,128)S(1)} collective-permute-done((f32[128,128]{1,0:T(8,128)S(1)}, f32[128,128]{1,0:T(8,128)S(1)}, u32[]{:S(2)}, u32[]{:S(2)}) %collective-permute-start.6) | collective-permute-done | bytes 65568 | tf_op jit(solution)/shard_map/ppermute | solution.py:203
  27.7 0.1 shard_map.80
  27.8 2.0 %collective-permute-start.9 = (f32[64,128]{1,0:T(8,128)S(1)}, f32[64,128]{1,0:T(8,128)S(1)}, u32[]{:S(2)}, u32[]{:S(2)}) collective-permute-start(f32[64,128]{1,0:T(8,128)S(1)} %get-tuple-element.57), channel_id=1, source_target_pairs={{0,3},{1,2},{2,1},{3,0},{4,7},{5,6},{6,5},{7,4},{8,11},{9,10},{10,... | collective-permute-start | bytes 98312 | tf_op jit(solution)/shard_map/ppermute | solution.py:208
  29.8 0.4 collective-permute-start.10
  30.2 2.0 %collective-permute-start.11 = (f32[64,128]{1,0:T(8,128)S(1)}, f32[64,128]{1,0:T(8,128)S(1)}, u32[]{:S(2)}, u32[]{:S(2)}) collective-permute-start(f32[64,128]{1,0:T(8,128)S(1)} %get-tuple-element.59), channel_id=1, source_target_pairs={{0,1},{1,0},{2,3},{3,2},{4,5},{5,4},{6,7},{7,6},{8,9},{9,8},{10,11... | collective-permute-start | bytes 98312 | tf_op jit(solution)/shard_map/ppermute | solution.py:208
  32.3 1.3 %collective-permute-done.9.refs_9_ = f32[64,128]{1,0:T(8,128)S(1)} collective-permute-done((f32[64,128]{1,0:T(8,128)S(1)}, f32[64,128]{1,0:T(8,128)S(1)}, u32[]{:S(2)}, u32[]{:S(2)}) %collective-permute-start.9) | collective-permute-done | bytes 32800 | tf_op jit(solution)/shard_map/ppermute | solution.py:208
  33.6 1.1 %collective-permute-done.10.refs_10_ = f32[64,128]{1,0:T(8,128)S(1)} collective-permute-done((f32[64,128]{1,0:T(8,128)S(1)}, f32[64,128]{1,0:T(8,128)S(1)}, u32[]{:S(2)}, u32[]{:S(2)}) %collective-permute-start.10) | collective-permute-done | bytes 32800 | tf_op jit(solution)/shard_map/ppermute | solution.py:208
  34.7 4.7 %shard_map.81 = (bf16[8192,128]{1,0:T(8,128)(2,1)S(1)}, bf16[1024,128]{1,0:T(8,128)(2,1)S(1)}, bf16[1024,128]{1,0:T(8,128)(2,1)S(1)}, bf16[1024,128]{1,0:T(8,128...) custom-call(bf16[8192,128]{1,0:T(8,128)(2,1)S(1)} %bitcast.7, ...), custom_call_target="tpu_custom_call" | custom-call | flops 805306368 | bytes 8388608 | tf_op jit(solution)/shard_map/pallas_call | solution.py:575
  39.4 1.5 %collective-permute-start.12 = (bf16[1024,128]{1,0:T(8,128)(2,1)S(1)}, bf16[1024,128]{1,0:T(8,128)(2,1)S(1)}, u32[]{:S(2)}, u32[]{:S(2)}) collective-permute-start(bf16[1024,128]{1,0:T(8,128)(2,1)S(1)} %get-tuple-element.62), channel_id=1, source_target_pairs={{0,4},{1,5},{2,6},{3,7},{4,0},{5,1},{6,2},{7,3},{8,12},{9,13},{10,... | collective-permute-start | bytes 786440 | tf_op jit(solution)/shard_map/ppermute | solution.py:249
  40.9 1.5 %collective-permute-start.13 = (bf16[1024,128]{1,0:T(8,128)(2,1)S(1)}, bf16[1024,128]{1,0:T(8,128)(2,1)S(1)}, u32[]{:S(2)}, u32[]{:S(2)}) collective-permute-start(bf16[1024,128]{1,0:T(8,128)(2,1)S(1)} %get-tuple-element.63), channel_id=1, source_target_pairs={{0,1},{1,0},{2,3},{3,2},{4,5},{5,4},{6,7},{7,6},{8,16},{9,17},{10,... | collective-permute-start | bytes 786440 | tf_op jit(solution)/shard_map/ppermute | solution.py:249
  42.4 0.5 collective-permute-start.16
  42.9 1.4 %collective-permute-start.15 = (bf16[128,128]{1,0:T(8,128)(2,1)S(1)}, bf16[128,128]{1,0:T(8,128)(2,1)S(1)}, u32[]{:S(2)}, u32[]{:S(2)}) collective-permute-start(bf16[128,128]{1,0:T(8,128)(2,1)S(1)} %get-tuple-element.65), channel_id=1, source_target_pairs={{0,1},{1,0},{2,3},{3,2},{4,5},{5,4},{6,7},{7,6},{8,9},{9,8},{10,11... | collective-permute-start | bytes 98312 | tf_op jit(solution)/shard_map/ppermute | solution.py:249
  44.4 3.6 %collective-permute-done.15.refs_6_ = bf16[128,128]{1,0:T(8,128)(2,1)S(1)} collective-permute-done((bf16[128,128]{1,0:T(8,128)(2,1)S(1)}, bf16[128,128]{1,0:T(8,128)(2,1)S(1)}, u32[]{:S(2)}, u32[]{:S(2)}) %collective-permute-start.15) | collective-permute-done | bytes 32800 | tf_op jit(solution)/shard_map/ppermute | solution.py:249
  48.0 3.9 %shard_map.82 = (bf16[8192,128]{1,0:T(8,128)(2,1)S(1)}, bf16[1024,128]{1,0:T(8,128)(2,1)S(1)}, bf16[1024,128]{1,0:T(8,128)(2,1)S(1)}, bf16[1024,128]{1,0:T(8,128)(2,1)S(1)}, bf16[128,128]{1,0:T(8,128)(2,1)S(1)}) custom-call(bf16[8192,128]{1,0:T(8,128)(2,1)S(1)} %get-tuple-element.60.refs_0_, bf16[8192,128]{1,0:T(8,128)(2,1)S(1)} %get-tuple-element.61.refs_1_, ...), custom_call_target="tpu_custom_call" | custom-call | flops 805306368 | bytes 8388608 | tf_op jit(solution)/shard_map/pallas_call | solution.py:575
  51.9 0.5 collective-permute-start.17
  52.4 1.5 %collective-permute-start.18 = (bf16[1024,128]{1,0:T(8,128)(2,1)S(1)}, bf16[1024,128]{1,0:T(8,128)(2,1)S(1)}, u32[]{:S(2)}, u32[]{:S(2)}) collective-permute-start(bf16[1024,128]{1,0:T(8,128)(2,1)S(1)} %get-tuple-element.68), channel_id=1, source_target_pairs={{0,1},{1,0},{2,3},{3,2},{4,5},{5,4},{6,7},{7,6},{8,16},{9,17},{10,... | collective-permute-start | bytes 786440 | tf_op jit(solution)/shard_map/ppermute | solution.py:249
  53.9 0.5 collective-permute-start.21
  54.5 1.4 %collective-permute-start.20 = (bf16[128,128]{1,0:T(8,128)(2,1)S(1)}, bf16[128,128]{1,0:T(8,128)(2,1)S(1)}, u32[]{:S(2)}, u32[]{:S(2)}) collective-permute-start(bf16[128,128]{1,0:T(8,128)(2,1)S(1)} %get-tuple-element.70), channel_id=1, source_target_pairs={{0,1},{1,0},{2,3},{3,2},{4,5},{5,4},{6,7},{7,6},{8,9},{9,8},{10,11... | collective-permute-start | bytes 98312 | tf_op jit(solution)/shard_map/ppermute | solution.py:249
  55.9 3.6 %collective-permute-done.20.refs_6_ = bf16[128,128]{1,0:T(8,128)(2,1)S(1)} collective-permute-done((bf16[128,128]{1,0:T(8,128)(2,1)S(1)}, bf16[128,128]{1,0:T(8,128)(2,1)S(1)}, u32[]{:S(2)}, u32[]{:S(2)}) %collective-permute-start.20) | collective-permute-done | bytes 32800 | tf_op jit(solution)/shard_map/ppermute | solution.py:249
  59.5 3.3 %shard_map.83 = bf16[8192,128]{1,0:T(8,128)(2,1)} custom-call(bf16[8192,128]{1,0:T(8,128)(2,1)S(1)} %get-tuple-element.66.refs_0_, bf16[8192,128]{1,0:T(8,128)(2,1)S(1)} %get-tuple-element.61.refs_1_, f32[64,128]{1,0:T(8,128)S(1)} %bitcast.11, bf16[1024,128]{1,0:T(8,128)(2,1)S(1)} %collective-permute-done.17.refs_3_, ...), custom_call_target="tpu_custom_call" | custom-call | flops 805306368 | bytes 8388608 | tf_op jit(solution)/shard_map/pallas_call | solution.py:575
  (29 shorter events, 0.1 us)
Async XLA Ops:
  5.7 11.6 %collective-permute-start = (bf16[1024,128]{1,0:T(8,128)(2,1)}, bf16[1024,128]{1,0:T(8,128)(2,1)S(1)}, u32[]{:S(2)}, u32[]{:S(2)}) collective-permute-start(bf16[1024,128]{1,0:T(8,128)(2,1)} %shard_map.77.refs_0_), channel_id=1, source_target_pairs={{0,16},{8,24},{16,0},{24,8},{1,17},{9,25},{17,1},{25,9},{2,18},{10... | collective-permute-start | bytes 786440 | tf_op jit(solution)/shard_map/ppermute | solution.py:600
  8.7 8.6 %copy-start.2 = (bf16[1024,128]{1,0:T(8,128)(2,1)S(1)}, bf16[1024,128]{1,0:T(8,128)(2,1)}, u32[]{:S(2)}) copy-start(bf16[1024,128]{1,0:T(8,128)(2,1)} %shard_map.77.refs_0_) | copy-start | bytes 786436
  8.7 26.0 %copy-start.1 = (bf16[128,8,8,128]{3,2,1,0:T(8,128)(2,1)S(1)}, bf16[128,8,8,128]{3,2,1,0:T(8,128)(2,1)}, u32[]{:S(2)}) copy-start(bf16[128,8,8,128]{3,2,1,0:T(8,128)(2,1)} %param.7) | copy-start | bytes 6291460
  12.2 22.5 %copy-start = (bf16[128,8,8,128]{3,2,1,0:T(8,128)(2,1)S(1)}, bf16[128,8,8,128]{3,2,1,0:T(8,128)(2,1)}, u32[]{:S(2)}) copy-start(bf16[128,8,8,128]{3,2,1,0:T(8,128)(2,1)} %param.6) | copy-start | bytes 6291460
  12.2 22.5 %copy-start.3 = (f32[8,8,128]{2,1,0:T(8,128)S(1)}, f32[8,8,128]{2,1,0:T(8,128)}, u32[]{:S(2)}) copy-start(f32[8,8,128]{2,1,0:T(8,128)} %param.8) | copy-start | bytes 98308
  12.2 22.5 %copy-start.4 = (s32[1,1,1,32]{3,2,1,0:T(1,128)S(1)}, s32[1,1,1,32]{3,2,1,0:T(1,128)}, u32[]{:S(2)}) copy-start(s32[1,1,1,32]{3,2,1,0:T(1,128)} %refs_12_.1) | copy-start | bytes 388
  12.2 4.7 %collective-permute-start.2 = (bf16[128,128]{1,0:T(8,128)(2,1)S(1)}, bf16[128,128]{1,0:T(8,128)(2,1)S(1)}, u32[]{:S(2)}, u32[]{:S(2)}) collective-permute-start(bf16[128,128]{1,0:T(8,128)(2,1)S(1)} %get-tuple-element.40), channel_id=1, source_target_pairs={{0,8},{1,2},{2,1},{3,11},{4,12},{5,6},{6,5},{7,15},{8,0},{9,10},{1... | collective-permute-start | bytes 98312 | tf_op jit(solution)/shard_map/ppermute | solution.py:249
  12.3 5.0 %collective-permute-start.1 = (bf16[128,128]{1,0:T(8,128)(2,1)S(1)}, bf16[128,128]{1,0:T(8,128)(2,1)S(1)}, u32[]{:S(2)}, u32[]{:S(2)}) collective-permute-start(bf16[128,128]{1,0:T(8,128)(2,1)S(1)} %get-tuple-element.40), channel_id=1, source_target_pairs={{0,1},{1,0},{2,3},{3,2},{4,5},{5,4},{6,7},{7,6},{8,9},{9,8},{10,11... | collective-permute-start | bytes 98312 | tf_op jit(solution)/shard_map/ppermute | solution.py:249
  15.4 7.2 %collective-permute-start.5 = (bf16[1024,128]{1,0:T(8,128)(2,1)S(1)}, bf16[1024,128]{1,0:T(8,128)(2,1)S(1)}, u32[]{:S(2)}, u32[]{:S(2)}) collective-permute-start(bf16[1024,128]{1,0:T(8,128)(2,1)S(1)} %get-tuple-element.37), channel_id=1, source_target_pairs={{0,4},{1,5},{2,6},{3,7},{4,0},{5,1},{6,2},{7,3},{8,12},{9,13},{10,... | collective-permute-start | bytes 786440 | tf_op jit(solution)/shard_map/ppermute | solution.py:249
  17.3 5.3 %collective-permute-start.3 = (bf16[1024,128]{1,0:T(8,128)(2,1)S(1)}, bf16[1024,128]{1,0:T(8,128)(2,1)S(1)}, u32[]{:S(2)}, u32[]{:S(2)}) collective-permute-start(bf16[1024,128]{1,0:T(8,128)(2,1)S(1)} %copy-done.2), channel_id=1, source_target_pairs={{0,8},{8,0},{16,24},{24,16},{1,9},{9,1},{17,25},{25,17},{2,10},{10... | collective-permute-start | bytes 786440 | tf_op jit(solution)/shard_map/ppermute | solution.py:600
  17.4 5.3 %collective-permute-start.4 = (bf16[1024,128]{1,0:T(8,128)(2,1)S(1)}, bf16[1024,128]{1,0:T(8,128)(2,1)S(1)}, u32[]{:S(2)}, u32[]{:S(2)}) collective-permute-start(bf16[1024,128]{1,0:T(8,128)(2,1)S(1)} %collective-permute-done.refs_2_), channel_id=1, source_target_pairs={{0,8},{8,0},{16,24},{24,16},{1,9},{9,1},{17,25},{25,17},{2,10},{10... | collective-permute-start | bytes 786440 | tf_op jit(solution)/shard_map/ppermute | solution.py:600
  17.9 7.1 %collective-permute-start.7 = (bf16[1024,128]{1,0:T(8,128)(2,1)S(1)}, bf16[1024,128]{1,0:T(8,128)(2,1)S(1)}, u32[]{:S(2)}, u32[]{:S(2)}) collective-permute-start(bf16[1024,128]{1,0:T(8,128)(2,1)S(1)} %get-tuple-element.38), channel_id=1, source_target_pairs={{0,1},{1,0},{2,3},{3,2},{4,5},{5,4},{6,7},{7,6},{8,16},{9,17},{10,... | collective-permute-start | bytes 786440 | tf_op jit(solution)/shard_map/ppermute | solution.py:249
  19.9 5.1 %collective-permute-start.8 = (bf16[1024,128]{1,0:T(8,128)(2,1)S(1)}, bf16[1024,128]{1,0:T(8,128)(2,1)S(1)}, u32[]{:S(2)}, u32[]{:S(2)}) collective-permute-start(bf16[1024,128]{1,0:T(8,128)(2,1)S(1)} %get-tuple-element.39), channel_id=1, source_target_pairs={{0,8},{1,9},{2,10},{3,11},{4,12},{5,13},{6,14},{7,15},{8,0},{9,1},... | collective-permute-start | bytes 786440 | tf_op jit(solution)/shard_map/ppermute | solution.py:249
  23.4 4.3 %collective-permute-start.6 = (f32[128,128]{1,0:T(8,128)S(1)}, f32[128,128]{1,0:T(8,128)S(1)}, u32[]{:S(2)}, u32[]{:S(2)}) collective-permute-start(f32[128,128]{1,0:T(8,128)S(1)} %get-tuple-element.49), channel_id=1, source_target_pairs={{0,4},{4,0},{1,5},{5,1},{2,6},{6,2},{3,7},{7,3},{8,12},{12,8},{9,1... | collective-permute-start | bytes 196616 | tf_op jit(solution)/shard_map/ppermute | solution.py:203
  27.8 5.8 %collective-permute-start.9 = (f32[64,128]{1,0:T(8,128)S(1)}, f32[64,128]{1,0:T(8,128)S(1)}, u32[]{:S(2)}, u32[]{:S(2)}) collective-permute-start(f32[64,128]{1,0:T(8,128)S(1)} %get-tuple-element.57), channel_id=1, source_target_pairs={{0,3},{1,2},{2,1},{3,0},{4,7},{5,6},{6,5},{7,4},{8,11},{9,10},{10,... | collective-permute-start | bytes 98312 | tf_op jit(solution)/shard_map/ppermute | solution.py:208
  29.8 4.8 %collective-permute-start.10 = (f32[64,128]{1,0:T(8,128)S(1)}, f32[64,128]{1,0:T(8,128)S(1)}, u32[]{:S(2)}, u32[]{:S(2)}) collective-permute-start(f32[64,128]{1,0:T(8,128)S(1)} %get-tuple-element.58), channel_id=1, source_target_pairs={{0,2},{1,3},{2,0},{3,1},{4,6},{5,7},{6,4},{7,5},{8,10},{9,11},{10,... | collective-permute-start | bytes 98312 | tf_op jit(solution)/shard_map/ppermute | solution.py:208
  30.2 4.5 %collective-permute-start.11 = (f32[64,128]{1,0:T(8,128)S(1)}, f32[64,128]{1,0:T(8,128)S(1)}, u32[]{:S(2)}, u32[]{:S(2)}) collective-permute-start(f32[64,128]{1,0:T(8,128)S(1)} %get-tuple-element.59), channel_id=1, source_target_pairs={{0,1},{1,0},{2,3},{3,2},{4,5},{5,4},{6,7},{7,6},{8,9},{9,8},{10,11... | collective-permute-start | bytes 98312 | tf_op jit(solution)/shard_map/ppermute | solution.py:208
  39.4 8.6 %collective-permute-start.12 = (bf16[1024,128]{1,0:T(8,128)(2,1)S(1)}, bf16[1024,128]{1,0:T(8,128)(2,1)S(1)}, u32[]{:S(2)}, u32[]{:S(2)}) collective-permute-start(bf16[1024,128]{1,0:T(8,128)(2,1)S(1)} %get-tuple-element.62), channel_id=1, source_target_pairs={{0,4},{1,5},{2,6},{3,7},{4,0},{5,1},{6,2},{7,3},{8,12},{9,13},{10,... | collective-permute-start | bytes 786440 | tf_op jit(solution)/shard_map/ppermute | solution.py:249
  40.9 7.1 %collective-permute-start.13 = (bf16[1024,128]{1,0:T(8,128)(2,1)S(1)}, bf16[1024,128]{1,0:T(8,128)(2,1)S(1)}, u32[]{:S(2)}, u32[]{:S(2)}) collective-permute-start(bf16[1024,128]{1,0:T(8,128)(2,1)S(1)} %get-tuple-element.63), channel_id=1, source_target_pairs={{0,1},{1,0},{2,3},{3,2},{4,5},{5,4},{6,7},{7,6},{8,16},{9,17},{10,... | collective-permute-start | bytes 786440 | tf_op jit(solution)/shard_map/ppermute | solution.py:249
  42.4 5.6 %collective-permute-start.14 = (bf16[1024,128]{1,0:T(8,128)(2,1)S(1)}, bf16[1024,128]{1,0:T(8,128)(2,1)S(1)}, u32[]{:S(2)}, u32[]{:S(2)}) collective-permute-start(bf16[1024,128]{1,0:T(8,128)(2,1)S(1)} %get-tuple-element.64), channel_id=1, source_target_pairs={{0,8},{1,9},{2,10},{3,11},{4,12},{5,13},{6,14},{7,15},{8,0},{9,1},... | collective-permute-start | bytes 786440 | tf_op jit(solution)/shard_map/ppermute | solution.py:249
  42.4 1.9 %collective-permute-start.16 = (bf16[128,128]{1,0:T(8,128)(2,1)S(1)}, bf16[128,128]{1,0:T(8,128)(2,1)S(1)}, u32[]{:S(2)}, u32[]{:S(2)}) collective-permute-start(bf16[128,128]{1,0:T(8,128)(2,1)S(1)} %get-tuple-element.65), channel_id=1, source_target_pairs={{0,8},{1,2},{2,1},{3,11},{4,12},{5,6},{6,5},{7,15},{8,0},{9,10},{1... | collective-permute-start | bytes 98312 | tf_op jit(solution)/shard_map/ppermute | solution.py:249
  42.9 5.1 %collective-permute-start.15 = (bf16[128,128]{1,0:T(8,128)(2,1)S(1)}, bf16[128,128]{1,0:T(8,128)(2,1)S(1)}, u32[]{:S(2)}, u32[]{:S(2)}) collective-permute-start(bf16[128,128]{1,0:T(8,128)(2,1)S(1)} %get-tuple-element.65), channel_id=1, source_target_pairs={{0,1},{1,0},{2,3},{3,2},{4,5},{5,4},{6,7},{7,6},{8,9},{9,8},{10,11... | collective-permute-start | bytes 98312 | tf_op jit(solution)/shard_map/ppermute | solution.py:249
  51.9 7.6 %collective-permute-start.17 = (bf16[1024,128]{1,0:T(8,128)(2,1)S(1)}, bf16[1024,128]{1,0:T(8,128)(2,1)S(1)}, u32[]{:S(2)}, u32[]{:S(2)}) collective-permute-start(bf16[1024,128]{1,0:T(8,128)(2,1)S(1)} %get-tuple-element.67), channel_id=1, source_target_pairs={{0,4},{1,5},{2,6},{3,7},{4,0},{5,1},{6,2},{7,3},{8,12},{9,13},{10,... | collective-permute-start | bytes 786440 | tf_op jit(solution)/shard_map/ppermute | solution.py:249
  52.4 7.1 %collective-permute-start.18 = (bf16[1024,128]{1,0:T(8,128)(2,1)S(1)}, bf16[1024,128]{1,0:T(8,128)(2,1)S(1)}, u32[]{:S(2)}, u32[]{:S(2)}) collective-permute-start(bf16[1024,128]{1,0:T(8,128)(2,1)S(1)} %get-tuple-element.68), channel_id=1, source_target_pairs={{0,1},{1,0},{2,3},{3,2},{4,5},{5,4},{6,7},{7,6},{8,16},{9,17},{10,... | collective-permute-start | bytes 786440 | tf_op jit(solution)/shard_map/ppermute | solution.py:249
  53.9 5.6 %collective-permute-start.19 = (bf16[1024,128]{1,0:T(8,128)(2,1)S(1)}, bf16[1024,128]{1,0:T(8,128)(2,1)S(1)}, u32[]{:S(2)}, u32[]{:S(2)}) collective-permute-start(bf16[1024,128]{1,0:T(8,128)(2,1)S(1)} %get-tuple-element.69), channel_id=1, source_target_pairs={{0,8},{1,9},{2,10},{3,11},{4,12},{5,13},{6,14},{7,15},{8,0},{9,1},... | collective-permute-start | bytes 786440 | tf_op jit(solution)/shard_map/ppermute | solution.py:249
  53.9 1.9 %collective-permute-start.21 = (bf16[128,128]{1,0:T(8,128)(2,1)S(1)}, bf16[128,128]{1,0:T(8,128)(2,1)S(1)}, u32[]{:S(2)}, u32[]{:S(2)}) collective-permute-start(bf16[128,128]{1,0:T(8,128)(2,1)S(1)} %get-tuple-element.70), channel_id=1, source_target_pairs={{0,8},{1,2},{2,1},{3,11},{4,12},{5,6},{6,5},{7,15},{8,0},{9,10},{1... | collective-permute-start | bytes 98312 | tf_op jit(solution)/shard_map/ppermute | solution.py:249
  54.5 5.1 %collective-permute-start.20 = (bf16[128,128]{1,0:T(8,128)(2,1)S(1)}, bf16[128,128]{1,0:T(8,128)(2,1)S(1)}, u32[]{:S(2)}, u32[]{:S(2)}) collective-permute-start(bf16[128,128]{1,0:T(8,128)(2,1)S(1)} %get-tuple-element.70), channel_id=1, source_target_pairs={{0,1},{1,0},{2,3},{3,2},{4,5},{5,4},{6,7},{7,6},{8,9},{9,8},{10,11... | collective-permute-start | bytes 98312 | tf_op jit(solution)/shard_map/ppermute | solution.py:249

commit v9 on v8

--- a/solution.py
+++ b/solution.py
@@ -36,7 +36,8 @@
     return pltpu.CompilerParams(vmem_limit_bytes=mebibytes * 1024 * 1024)
 
 
-def trace_kernel(stride, block, field_ref, cell_ref, out_ref, field, cell_v, tall, near, place, picked, sems):
+def trace_kernel(shape, stride, block, field_ref, cell_ref, out_ref, *refs):
+    *face_refs, field, cell_v, tall, near, place, picked, sems = refs
     sides, rows, lanes = field.shape
     slots = cell_ref.shape[3]
     per_row = lanes // stride
@@ -70,6 +71,7 @@
         copies[step].wait()
         span = field[step * block : (step + 1) * block]
         tall[step] = span.reshape(block * rows, lanes).astype(F32)
+        cut_faces(shape, shape.outer, step * block, block, tall.at[step], face_refs)
 
         for batch in range(block // 8):
             for tile in range(rows // together):
@@ -91,17 +93,17 @@
     out_ref[...] = total.T.astype(BF)
 
 
-def traces(field, trace_cell, block):
+def traces(shape, field, trace_cell, block):
     sides, rows, lanes = field.shape
     slots = trace_cell.shape[3]
     stride = rows * lanes // slots
     width = min(slots, 256)
     hbm = pl.BlockSpec(memory_space=pltpu.HBM)
     return pl.pallas_call(
-        functools.partial(trace_kernel, stride, block),
+        functools.partial(trace_kernel, shape, stride, block),
         in_specs=[hbm, hbm],
-        out_specs=WHOLE,
-        out_shape=jax.ShapeDtypeStruct((slots, sides), BF),
+        out_specs=[WHOLE] * (1 + len(shape.outer)),
+        out_shape=[jax.ShapeDtypeStruct((slots, sides), BF)] + face_shapes(shape, shape.outer),
         scratch_shapes=[
             pltpu.VMEM(field.shape, BF),
             pltpu.VMEM(trace_cell.shape, jnp.int32),
@@ -258,8 +260,9 @@
         self.block = min(sides, 32)
         self.half = self.block // 2
         self.half_rows = self.half * self.cells
-        self.faces = [("col", i) for i in range(turns("col"))]
-        self.faces += [("row", i) for i in reversed(range(turns("row")))]
+        self.outer = [("col", i) for i in range(turns("col"))]
+        self.inner = [("row", i) for i in reversed(range(turns("row")))]
+        self.faces = self.outer + self.inner
         self.ends = turns("gz")
 
     def face_len(self, face):
@@ -315,29 +318,62 @@
     rsum[...] = (iota(dims, 1) // shape.cells == iota(dims, 0)).astype(BF)
 
 
-def emit_faces(shape, at, values, tall, face_refs, z_ref, ends_m, rsum):
-    for face, ref in zip(shape.faces, face_refs):
+def cut_faces(shape, faces, at, block, tall, face_refs):
+    for face, ref in zip(faces, face_refs):
         length, edge = shape.face_len(face), shape.edge(face)
         lines = []
-        for side in range(shape.block):
+        for side in range(block):
             start = side * shape.cells
             if face[0] == "row":
                 lines.append(tall[pl.ds(aligned(start + edge * length, 8), length), :])
             else:
                 lines.append(tall[pl.ds(start + edge, length, stride=shape.y), :])
-        span = shape.block * length
-        ref[pl.ds(aligned(at * length, span), span), :] = jnp.concatenate(
-            lines, axis=0
-        ).astype(BF)
+        span = slice(at * length, (at + block) * length)
+        ref[span, :] = jnp.concatenate(lines, axis=0).astype(BF)
+
+
+def cut_ends(shape, at, values, z_ref, ends_m, rsum):
     mask = jnp.concatenate([z_mask(shape, shape.half)] * 2, axis=1)
     tips = jnp.where(mask, dot(beside(values), ends_m[...]), 0.0).astype(BF)
     tips = dot(rsum[...], tips)[: shape.half]
     tips = jnp.concatenate([tips[:, : 2 * shape.cells], tips[:, 2 * shape.cells :]], axis=0)
-    z_ref[pl.ds(aligned(at, shape.block), shape.block), :] = tips.astype(BF)
-
-
-def faces_kernel(shape, slots, field_ref, block_ref, *refs):
-    *face_refs, z_ref, held, field, tall, ends_m, rsum, sems, field_sems = refs
+    z_ref[at : at + shape.block, :] = tips.astype(BF)
+
+
+def build_tables(shape, coef_ref, weight, near_m, line_m, ends_m, rsum):
+    cells, lanes = shape.cells, shape.lanes
+    weight[...] = jnp.concatenate([OMEGA / (6.0 + coef_ref[...])] * shape.chunk, axis=0)
+    dims = (shape.rows, shape.rows)
+    row, col = iota(dims, 0), iota(dims, 1)
+    x, y = row % cells // shape.y, row % shape.y
+    x2, y2 = col % cells // shape.y, col % shape.y
+    near = ((x == x2) & (jnp.abs(y - y2) == 1)) | ((y == y2) & (jnp.abs(x - x2) == 1))
+    near_m[:, : shape.rows] = (near & (row // cells == col // cells)).astype(BF)
+    near_m[:, shape.rows :] = halo_place(shape)
+    dims = (lanes, lanes)
+    line = (jnp.abs(iota(dims, 0) - iota(dims, 1)) == 1).astype(F32)
+    line_m[: 2 * lanes, :] = twice(line).astype(BF)
+    dims = (2 * cells, lanes)
+    edge = jnp.where(iota(dims, 0) < cells, lanes - 1, 0)
+    line_m[2 * lanes :, :] = twice((iota(dims, 1) == edge).astype(F32)).astype(BF)
+    build_out(shape, ends_m, rsum)
+
+
+def table_shapes(shape):
+    lanes, cells = shape.lanes, shape.cells
+    return [
+        jax.ShapeDtypeStruct((shape.rows, lanes), F32),
+        jax.ShapeDtypeStruct((shape.rows, shape.rows + shape.halo_rows()), BF),
+        jax.ShapeDtypeStruct((2 * lanes + 4 * cells, 2 * lanes), BF),
+        jax.ShapeDtypeStruct((2 * lanes, 4 * cells), BF),
+        jax.ShapeDtypeStruct((max(8, shape.half), shape.half_rows), BF),
+    ]
+
+
+def faces_kernel(shape, slots, field_ref, block_ref, coef_ref, *refs):
+    refs = list(refs)
+    face_refs = [refs.pop(0) for _ in shape.inner]
+    z_ref, held, *tables, field, tall, sems, field_sems = refs
     size = shape.block * shape.cells
     steps = shape.sides // shape.block
     copies = []
@@ -348,47 +384,41 @@
         )
         copies[-1].start()
     columns = fetch_columns(block_ref, held, sems, slots)
-    build_out(shape, ends_m, rsum)
+    build_tables(shape, coef_ref, *tables)
+    ends_m, rsum = tables[-2:]
     for step in range(steps):
         copies[step].wait()
         values = field[step * size : (step + 1) * size, :]
         tall[step] = values.astype(F32)
-        emit_faces(shape, step * shape.block, values, tall.at[step], face_refs, z_ref, ends_m, rsum)
+        cut_faces(shape, shape.inner, step * shape.block, shape.block, tall.at[step], face_refs)
+        cut_ends(shape, step * shape.block, values, z_ref, ends_m, rsum)
     for copy in columns:
         copy.wait()
 
 
-def face_outputs(shape):
-    shapes = [
+def face_shapes(shape, faces):
+    return [
         jax.ShapeDtypeStruct((shape.sides * shape.face_len(face), shape.lanes), BF)
-        for face in shape.faces
+        for face in faces
     ]
-    return shapes + [jax.ShapeDtypeStruct((shape.sides, 2 * shape.cells), BF)]
-
-
-def face_scratch(shape):
-    return [
-        pltpu.VMEM((shape.block * shape.cells, shape.lanes), F32),
-        pltpu.VMEM((2 * shape.lanes, 4 * shape.cells), BF),
-        pltpu.VMEM((max(8, shape.half), shape.half_rows), BF),
-    ]
-
-
-def first_faces(shape, field, block, slots):
+
+
+def first_faces(shape, field, block, coef, slots):
     peers = lax.axis_size("row")
     steps = shape.sides // shape.block
-    shapes = face_outputs(shape)
+    shapes = face_shapes(shape, shape.inner)
+    shapes.append(jax.ShapeDtypeStruct((shape.sides, 2 * shape.cells), BF))
     shapes.append(jax.ShapeDtypeStruct((peers, block.shape[0], slots), BF))
-    tall, *others = face_scratch(shape)
+    shapes += table_shapes(shape)
+    hbm = pl.BlockSpec(memory_space=pltpu.HBM)
     return pl.pallas_call(
         functools.partial(faces_kernel, shape, slots),
-        in_specs=[pl.BlockSpec(memory_space=pltpu.HBM)] * 2,
+        in_specs=[hbm, hbm, WHOLE],
         out_specs=[WHOLE] * len(shapes),
         out_shape=shapes,
         scratch_shapes=[
             pltpu.VMEM(field.shape, BF),
-            pltpu.VMEM((steps, *tall.shape), F32),
-            *others,
+            pltpu.VMEM((steps, shape.block * shape.cells, shape.lanes), F32),
             pltpu.SemaphoreType.DMA((peers,)),
             pltpu.SemaphoreType.DMA((steps,)),
         ],
@@ -396,14 +426,14 @@
         cost_estimate=pl.CostEstimate(
             flops=field.size * 128, bytes_accessed=4 * field.size, transcendentals=0
         ),
-    )(field, block)
+    )(field, block, coef)
 
 
 def sweep_kernel(shape, recvs, last, *refs):
     with_flux = recvs > 0
     refs = list(refs)
     take = lambda count: [refs.pop(0) for _ in range(count)]
-    field_ref, load_ref, coef_ref = take(3)
+    field_ref, load_ref, weight, near_m, line_m, ends_m, rsum = take(7)
     halo_refs = take(len(shape.faces))
     end_refs = take(shape.ends)
     if with_flux:
@@ -415,48 +445,30 @@
         (z_ref,) = take(1)
     if with_flux:
         source_ref, flux_ref = take(2)
-    weight, near_m, line_m, lines = take(4)
+    (lines,) = take(1)
     if last:
         result_ref = out_ref
         out_ref, out_sems = take(2)
     else:
-        tall, ends_m, rsum = take(3)
+        (tall,) = take(1)
     if with_flux:
         phi, cell_m, placed = take(3)
 
     cells, lanes = shape.cells, shape.lanes
 
-    def prepare():
-        weight[...] = OMEGA / (6.0 + coef_ref[...])
-        dims = (shape.rows, shape.rows)
-        row, col = iota(dims, 0), iota(dims, 1)
-        x, y = row % cells // shape.y, row % shape.y
-        x2, y2 = col % cells // shape.y, col % shape.y
-        near = ((x == x2) & (jnp.abs(y - y2) == 1)) | ((y == y2) & (jnp.abs(x - x2) == 1))
-        near_m[:, : shape.rows] = (near & (row // cells == col // cells)).astype(BF)
-        near_m[:, shape.rows :] = halo_place(shape)
-        dims = (lanes, lanes)
-        line = (jnp.abs(iota(dims, 0) - iota(dims, 1)) == 1).astype(F32)
-        line_m[: 2 * lanes, :] = twice(line).astype(BF)
-        dims = (2 * cells, lanes)
-        edge = jnp.where(iota(dims, 0) < cells, lanes - 1, 0)
-        line_m[2 * lanes :, :] = twice((iota(dims, 1) == edge).astype(F32)).astype(BF)
-        if not last:
-            build_out(shape, ends_m, rsum)
-        if with_flux:
-            slots = cell_ref.shape[3]
-            owned = recv_refs[0][...]
-            for ref in recv_refs[1:]:
-                owned = owned + ref[...]
-            flux_ref[...] = owned[slots:, : flux_ref.shape[1]]
-            owned = owned[:slots]
-            high = owned.astype(BF).astype(F32)
-            both = jnp.concatenate([high, owned - high], axis=0)
-            phi[...] = both.T
-            cell = jnp.concatenate([cell_ref[0, 0]] * 2, axis=1)
-            cell_m[...] = twice((iota((lanes, 2 * slots), 0) == cell % lanes).astype(F32)).astype(BF)
-
-    prepare()
+    if with_flux:
+        slots = cell_ref.shape[3]
+        owned = recv_refs[0][...]
+        for ref in recv_refs[1:]:
+            owned = owned + ref[...]
+        flux_ref[...] = owned[slots:, : flux_ref.shape[1]]
+        owned = owned[:slots]
+        high = owned.astype(BF).astype(F32)
+        both = jnp.concatenate([high, owned - high], axis=0)
+        phi[...] = both.T
+        cell = jnp.concatenate([cell_ref[0, 0]] * 2, axis=1)
+        cell_m[...] = twice((iota((lanes, 2 * slots), 0) == cell % lanes).astype(F32)).astype(BF)
+
     mask = z_mask(shape, 1)
     even = lax.axis_index("gz") % 2 == 0
     filled = (iota((shape.block, 2 * cells), 1) < cells) == even
@@ -464,7 +476,7 @@
         slots = cell_ref.shape[3]
         cell = jnp.concatenate([cell_ref[0, 0]] * 2, axis=1)
         cell_mask = iota((cells, 2 * slots), 0) == cell // lanes
-    weights = jnp.concatenate([weight[...]] * shape.chunk, axis=0)
+    weights = weight[...]
 
     def expand(lines, where, first):
         rows = []
@@ -519,7 +531,8 @@
     def emit(step):
         at, size = step * shape.block, shape.block * cells
         fresh = out_ref[at * cells : at * cells + size, :]
-        emit_faces(shape, at, fresh, tall.at[step], face_refs, z_ref, ends_m, rsum)
+        cut_faces(shape, shape.faces, at, shape.block, tall.at[step], face_refs)
+        cut_ends(shape, at, fresh, z_ref, ends_m, rsum)
 
     steps = shape.sides // shape.block
     copies = []
@@ -539,24 +552,19 @@
         emit(steps - 1)
 
 
-def sweep(shape, field, load, coef, halos, recv=(), flux_cell=None, last=False):
+def sweep(shape, field, load, tables, halos, recv=(), flux_cell=None, last=False):
     lanes, cells = shape.lanes, shape.cells
     steps = shape.sides // shape.block
     half = (steps, shape.half_rows, 2 * lanes)
-    operands = [field, load, coef, *halos, *recv]
+    operands = [field, load, *tables, *halos, *recv]
     out_shapes = [jax.ShapeDtypeStruct(field.shape, BF)]
-    scratch = [
-        pltpu.VMEM(coef.shape, F32),
-        pltpu.VMEM((shape.rows, shape.rows + shape.halo_rows()), BF),
-        pltpu.VMEM((2 * lanes + 4 * cells, 2 * lanes), BF),
-        pltpu.VMEM(half, F32),
-    ]
+    scratch = [pltpu.VMEM(half, F32)]
     if last:
         scratch += [pltpu.VMEM(field.shape, BF), pltpu.SemaphoreType.DMA((steps,))]
     else:
-        out_shapes += face_outputs(shape)
-        tall, *others = face_scratch(shape)
-        scratch += [pltpu.VMEM((steps, *tall.shape), F32), *others]
+        out_shapes += face_shapes(shape, shape.faces)
+        out_shapes.append(jax.ShapeDtypeStruct((shape.sides, 2 * cells), BF))
+        scratch.append(pltpu.VMEM((steps, shape.block * cells, lanes), F32))
     if recv:
         slots = flux_cell.shape[3]
         operands.append(flux_cell)
@@ -614,21 +622,24 @@
     coef = coefficient.reshape(cells, lanes)
 
     slots = trace_cell.shape[3]
-    trace = traces(volume_field.reshape(sides, cells, lanes), trace_cell, min(32, sides))
-    *faces, held = first_faces(shape, field, surface_block, slots)
-    halos = exchange(shape, faces)
+    trace, *outer = traces(
+        shape, volume_field.reshape(sides, cells, lanes), trace_cell, min(32, sides)
+    )
+    firsts = first_faces(shape, field, surface_block, coef, slots)
     layers = len(shape.faces)
-    parts, (_, ends) = row_gather(trace, (faces, halos[layers:]))
-    early = len([face for face in shape.faces if face[0] == "col"])
-    parts, along_col = lax.optimization_barrier((parts, halos[:early]))
+    count = len(shape.inner) + 1
+    inner, held, tables = firsts[:count], firsts[count], firsts[count + 1 :]
+    halos = exchange(shape, [*outer, *inner])
+    early = len(shape.outer)
+    parts, (_, along_col, ends) = row_gather(trace, (inner, halos[:early], halos[layers:]))
     recv, along_row = flux_sums(parts, held, halos[early:layers])
     halos = along_col + along_row + ends
 
     current, *faces, source, surface_flux = sweep(
-        shape, field, load, coef, halos, recv=recv, flux_cell=flux_cell
+        shape, field, load, tables, halos, recv=recv, flux_cell=flux_cell
     )
-    current, *faces = sweep(shape, current, source, coef, exchange(shape, faces))
-    (current,) = sweep(shape, current, source, coef, exchange(shape, faces), last=True)
+    current, *faces = sweep(shape, current, source, tables, exchange(shape, faces))
+    (current,) = sweep(shape, current, source, tables, exchange(shape, faces), last=True)
     return current.reshape(volume_field.shape), surface_flux
 
 

time: 63.2 us -> 62.1 us (0.983)
  starting transfers between devices: 25.2 us -> 23.6 us
  waiting for transfers between devices: 15.6 us -> 16.3 us
    ppermute x15, waiting for transfers between devices: 10.4 us -> 12.9 us  [swap(): return lax.ppermute(value, axes, pairs)]
    ppermute x1, waiting for transfers between devices: 2.73 us -> 0.95 us  [flux_sums(): other = lax.ppermute(other, 'col', [(0, 1), (1, 0)])]
    ppermute x3, starting transfers between devices: 3.51 us -> 2.06 us  [row_gather(): lax.ppermute(held[key], 'row', pairs)]
    ppermute x1, starting transfers between devices: 1.59 us -> 0.6 us  [flux_sums(): other = lax.ppermute(other, 'col', [(0, 1), (1, 0)])]
    ppermute x15, starting transfers between devices: 15.6 us -> 16.5 us  [swap(): return lax.ppermute(value, axes, pairs)]
  transfers between devices with their start and end apart: 22 -> 22, of which waited for: 7 -> 8; matrix products, arithmetic and copies ran while one was open for 0% -> 0% of each run, Pallas kernels for 7% -> 7%
where the time goes in v9:
time: 62.1 us; the launch traced here: 62 us
  starting transfers between devices  23.6 us (38%)
  Pallas kernels  21.1 us (34%)
  waiting for transfers between devices  16.3 us (26%)
  between operations  0.9 us (1%)
    ppermute x15, starting transfers between devices, swap(): return lax.ppermute(value, axes, pairs)  16.5 us
    ppermute x15, waiting for transfers between devices, swap(): return lax.ppermute(value, axes, pairs)  12.9 us
    pallas_call x3, Pallas kernels, sweep(): pl.pallas_call(functools.partial(sweep_kernel, shape, len(recv), last), i...  11.7 us
    pallas_call x1, Pallas kernels, traces(): pl.pallas_call(functools.partial(trace_kernel, shape, stride, block), in_...  5.21 us
    ppermute x3, starting transfers between devices, flux_sums(): lax.ppermute(sent[key], 'gz', [(i, i ^ key) for i in range(gzs)])  4.45 us
    pallas_call x1, Pallas kernels, first_faces(): pl.pallas_call(functools.partial(faces_kernel, shape, slots), in_specs=[h...  3.46 us
    ppermute x3, waiting for transfers between devices, flux_sums(): lax.ppermute(sent[key], 'gz', [(i, i ^ key) for i in range(gzs)])  2.47 us
    ppermute x3, starting transfers between devices, row_gather(): lax.ppermute(held[key], 'row', pairs)  2.06 us
  transfers between devices with their start and end apart: 22, of which 8 were waited for; matrix products, arithmetic and copies ran while one was open for 0% of the time, Pallas kernels for 7%

profile of v9, /device:TPU:0, one launch (start us, length us, event | category | flops | bytes accessed | tf_op | source)
XLA Modules:
  0.0 62.0 jit_solution(2162058086841521331)
XLA Ops:
  0.6 5.2 %shard_map.78 = (bf16[1024,128]{1,0:T(8,128)(2,1)}, bf16[1024,128]{1,0:T(8,128)(2,1)}) custom-call(bf16[128,64,128]{2,1,0:T(8,128)(2,1)} %bitcast.5, s32[1,1,1,1024]{3,2,1,0:T(1,128)} %cell_ref.1), custom_call_target="tpu_custom_call" | custom-call | flops 536870912 | bytes 2097152 | tf_op jit(solution)/shard_map/pallas_call | solution.py:102
  5.9 3.0 %collective-permute-start.1 = (bf16[1024,128]{1,0:T(8,128)(2,1)}, bf16[1024,128]{1,0:T(8,128)(2,1)S(1)}, u32[]{:S(2)}, u32[]{:S(2)}) collective-permute-start(bf16[1024,128]{1,0:T(8,128)(2,1)} %get-tuple-element.48), channel_id=1, source_target_pairs={{0,4},{1,5},{2,6},{3,7},{4,0},{5,1},{6,2},{7,3},{8,12},{9,13},{10,... | collective-permute-start | bytes 786440 | tf_op jit(solution)/shard_map/ppermute | solution.py:251
  8.9 1.5 %collective-permute-start = (bf16[1024,128]{1,0:T(8,128)(2,1)}, bf16[1024,128]{1,0:T(8,128)(2,1)S(1)}, u32[]{:S(2)}, u32[]{:S(2)}) collective-permute-start(bf16[1024,128]{1,0:T(8,128)(2,1)} %get-tuple-element.50.refs_0_), channel_id=1, source_target_pairs={{0,16},{8,24},{16,0},{24,8},{1,17},{9,25},{17,1},{25,9},{2,18},{10... | collective-permute-start | bytes 786440 | tf_op jit(solution)/shard_map/ppermute | solution.py:608
  10.4 3.5 %shard_map.77 = (bf16[1024,128]{1,0:T(8,128)(2,1)S(1)}, bf16[1024,128]{1,0:T(8,128)(2,1)S(1)}, bf16[128,128]{1,0:T(8,128)(2,1)S(1)}, bf16[4,256,1024]{2,1,0:T(8,...) custom-call(bf16[8192,128]{1,0:T(8,128)(2,1)} %bitcast.6, ...), custom_call_target="tpu_custom_call" | custom-call | flops 134217728 | bytes 4194304 | tf_op jit(solution)/shard_map/pallas_call | solution.py:414
  13.9 3.1 %collective-permute-start.2 = (bf16[128,128]{1,0:T(8,128)(2,1)S(1)}, bf16[128,128]{1,0:T(8,128)(2,1)S(1)}, u32[]{:S(2)}, u32[]{:S(2)}) collective-permute-start(bf16[128,128]{1,0:T(8,128)(2,1)S(1)} %get-tuple-element.47), channel_id=1, source_target_pairs={{0,1},{1,0},{2,3},{3,2},{4,5},{5,4},{6,7},{7,6},{8,9},{9,8},{10,11... | collective-permute-start | bytes 98312 | tf_op jit(solution)/shard_map/ppermute | solution.py:251
  17.1 1.9 %collective-permute-done.2.refs_10_ = bf16[128,128]{1,0:T(8,128)(2,1)S(1)} collective-permute-done((bf16[128,128]{1,0:T(8,128)(2,1)S(1)}, bf16[128,128]{1,0:T(8,128)(2,1)S(1)}, u32[]{:S(2)}, u32[]{:S(2)}) %collective-permute-start.2) | collective-permute-done | bytes 32800 | tf_op jit(solution)/shard_map/ppermute | solution.py:251
  19.1 0.5 collective-permute-start.5
  19.6 2.0 %collective-permute-start.7 = (bf16[1024,128]{1,0:T(8,128)(2,1)S(1)}, bf16[1024,128]{1,0:T(8,128)(2,1)S(1)}, u32[]{:S(2)}, u32[]{:S(2)}) collective-permute-start(bf16[1024,128]{1,0:T(8,128)(2,1)S(1)} %get-tuple-element.45), channel_id=1, source_target_pairs={{0,1},{1,0},{2,3},{3,2},{4,5},{5,4},{6,7},{7,6},{8,16},{9,17},{10,... | collective-permute-start | bytes 786440 | tf_op jit(solution)/shard_map/ppermute | solution.py:251
  21.6 0.7 %shard_map.79 = (f32[128,128]{1,0:T(8,128)S(1)}, f32[128,128]{1,0:T(8,128)S(1)}) custom-call(bf16[1024,128]{1,0:T(8,128)(2,1)S(1)} %copy-done.2, bf16[1024,128]{1,0:T(8,128)(2,1)S(1)} %collective-permute-done.4.refs_1_, bf16[1024,128]{1,0:T(8,128)(2,1)S(1)} %collective-permute-done.refs_2_, bf16[1024,128]{1,0:T(8,128)(2,1)S(1)} %collective-permute-done.5.refs_3_, ...), custom_call_target="tpu_custom_call" | custom-call | flops 268435456 | bytes 2097152 | tf_op jit(solution)/shard_map/pallas_call | solution.py:156
  22.3 0.6 collective-permute-start.6
  22.9 3.0 %collective-permute-done.7.refs_8_ = bf16[1024,128]{1,0:T(8,128)(2,1)S(1)} collective-permute-done((bf16[1024,128]{1,0:T(8,128)(2,1)S(1)}, bf16[1024,128]{1,0:T(8,128)(2,1)S(1)}, u32[]{:S(2)}, u32[]{:S(2)}) %collective-permute-start.7) | collective-permute-done | bytes 262176 | tf_op jit(solution)/shard_map/ppermute | solution.py:251
  25.9 0.9 %collective-permute-done.6.other_ref = f32[128,128]{1,0:T(8,128)S(1)} collective-permute-done((f32[128,128]{1,0:T(8,128)S(1)}, f32[128,128]{1,0:T(8,128)S(1)}, u32[]{:S(2)}, u32[]{:S(2)}) %collective-permute-start.6) | collective-permute-done | bytes 65568 | tf_op jit(solution)/shard_map/ppermute | solution.py:205
  26.9 0.1 shard_map.80
  27.0 1.7 %collective-permute-start.9 = (f32[64,128]{1,0:T(8,128)S(1)}, f32[64,128]{1,0:T(8,128)S(1)}, u32[]{:S(2)}, u32[]{:S(2)}) collective-permute-start(f32[64,128]{1,0:T(8,128)S(1)} %get-tuple-element.61), channel_id=1, source_target_pairs={{0,3},{1,2},{2,1},{3,0},{4,7},{5,6},{6,5},{7,4},{8,11},{9,10},{10,... | collective-permute-start | bytes 98312 | tf_op jit(solution)/shard_map/ppermute | solution.py:210
  28.7 0.9 %collective-permute-start.10 = (f32[64,128]{1,0:T(8,128)S(1)}, f32[64,128]{1,0:T(8,128)S(1)}, u32[]{:S(2)}, u32[]{:S(2)}) collective-permute-start(f32[64,128]{1,0:T(8,128)S(1)} %get-tuple-element.62), channel_id=1, source_target_pairs={{0,2},{1,3},{2,0},{3,1},{4,6},{5,7},{6,4},{7,5},{8,10},{9,11},{10,... | collective-permute-start | bytes 98312 | tf_op jit(solution)/shard_map/ppermute | solution.py:210
  29.7 1.8 %collective-permute-start.11 = (f32[64,128]{1,0:T(8,128)S(1)}, f32[64,128]{1,0:T(8,128)S(1)}, u32[]{:S(2)}, u32[]{:S(2)}) collective-permute-start(f32[64,128]{1,0:T(8,128)S(1)} %get-tuple-element.63), channel_id=1, source_target_pairs={{0,1},{1,0},{2,3},{3,2},{4,5},{5,4},{6,7},{7,6},{8,9},{9,8},{10,11... | collective-permute-start | bytes 98312 | tf_op jit(solution)/shard_map/ppermute | solution.py:210
  31.4 1.4 %collective-permute-done.9.refs_13_ = f32[64,128]{1,0:T(8,128)S(1)} collective-permute-done((f32[64,128]{1,0:T(8,128)S(1)}, f32[64,128]{1,0:T(8,128)S(1)}, u32[]{:S(2)}, u32[]{:S(2)}) %collective-permute-start.9) | collective-permute-done | bytes 32800 | tf_op jit(solution)/shard_map/ppermute | solution.py:210
  32.9 0.8 %collective-permute-done.10.refs_14_ = f32[64,128]{1,0:T(8,128)S(1)} collective-permute-done((f32[64,128]{1,0:T(8,128)S(1)}, f32[64,128]{1,0:T(8,128)S(1)}, u32[]{:S(2)}, u32[]{:S(2)}) %collective-permute-start.10) | collective-permute-done | bytes 32800 | tf_op jit(solution)/shard_map/ppermute | solution.py:210
  33.7 0.2 collective-permute-done.11.refs_15_
  33.9 4.8 %shard_map.81 = (bf16[8192,128]{1,0:T(8,128)(2,1)S(1)}, bf16[1024,128]{1,0:T(8,128)(2,1)S(1)}, bf16[1024,128]{1,0:T(8,128)(2,1)S(1)}, bf16[1024,128]{1,0:T(8,128...) custom-call(bf16[8192,128]{1,0:T(8,128)(2,1)S(1)} %bitcast.7, ...), custom_call_target="tpu_custom_call" | custom-call | flops 805306368 | bytes 8388608 | tf_op jit(solution)/shard_map/pallas_call | solution.py:583
  38.7 0.5 collective-permute-start.12
  39.2 1.4 %collective-permute-start.13 = (bf16[1024,128]{1,0:T(8,128)(2,1)S(1)}, bf16[1024,128]{1,0:T(8,128)(2,1)S(1)}, u32[]{:S(2)}, u32[]{:S(2)}) collective-permute-start(bf16[1024,128]{1,0:T(8,128)(2,1)S(1)} %get-tuple-element.67), channel_id=1, source_target_pairs={{0,1},{1,0},{2,3},{3,2},{4,5},{5,4},{6,7},{7,6},{8,16},{9,17},{10,... | collective-permute-start | bytes 786440 | tf_op jit(solution)/shard_map/ppermute | solution.py:251
  40.7 0.5 collective-permute-start.16
  41.2 1.2 %collective-permute-start.15 = (bf16[128,128]{1,0:T(8,128)(2,1)S(1)}, bf16[128,128]{1,0:T(8,128)(2,1)S(1)}, u32[]{:S(2)}, u32[]{:S(2)}) collective-permute-start(bf16[128,128]{1,0:T(8,128)(2,1)S(1)} %get-tuple-element.69), channel_id=1, source_target_pairs={{0,1},{1,0},{2,3},{3,2},{4,5},{5,4},{6,7},{7,6},{8,9},{9,8},{10,11... | collective-permute-start | bytes 98312 | tf_op jit(solution)/shard_map/ppermute | solution.py:251
  42.3 4.0 %collective-permute-done.15.refs_10_ = bf16[128,128]{1,0:T(8,128)(2,1)S(1)} collective-permute-done((bf16[128,128]{1,0:T(8,128)(2,1)S(1)}, bf16[128,128]{1,0:T(8,128)(2,1)S(1)}, u32[]{:S(2)}, u32[]{:S(2)}) %collective-permute-start.15) | collective-permute-done | bytes 32800 | tf_op jit(solution)/shard_map/ppermute | solution.py:251
  46.3 3.8 %shard_map.82 = (bf16[8192,128]{1,0:T(8,128)(2,1)S(1)}, bf16[1024,128]{1,0:T(8,128)(2,1)S(1)}, bf16[1024,128]{1,0:T(8,128)(2,1)S(1)}, bf16[1024,128]{1,0:T(8,128)(2,1)S(1)}, bf16[128,128]{1,0:T(8,128)(2,1)S(1)}) custom-call(bf16[8192,128]{1,0:T(8,128)(2,1)S(1)} %get-tuple-element.64.refs_0_, bf16[8192,128]{1,0:T(8,128)(2,1)S(1)} %get-tuple-element.65.refs_1_, ...), custom_call_target="tpu_custom_call" | custom-call | flops 805306368 | bytes 8388608 | tf_op jit(solution)/shard_map/pallas_call | solution.py:583
  50.1 1.5 %collective-permute-start.17 = (bf16[1024,128]{1,0:T(8,128)(2,1)S(1)}, bf16[1024,128]{1,0:T(8,128)(2,1)S(1)}, u32[]{:S(2)}, u32[]{:S(2)}) collective-permute-start(bf16[1024,128]{1,0:T(8,128)(2,1)S(1)} %get-tuple-element.71), channel_id=1, source_target_pairs={{0,4},{1,5},{2,6},{3,7},{4,0},{5,1},{6,2},{7,3},{8,12},{9,13},{10,... | collective-permute-start | bytes 786440 | tf_op jit(solution)/shard_map/ppermute | solution.py:251
  51.6 1.4 %collective-permute-start.18 = (bf16[1024,128]{1,0:T(8,128)(2,1)S(1)}, bf16[1024,128]{1,0:T(8,128)(2,1)S(1)}, u32[]{:S(2)}, u32[]{:S(2)}) collective-permute-start(bf16[1024,128]{1,0:T(8,128)(2,1)S(1)} %get-tuple-element.72), channel_id=1, source_target_pairs={{0,1},{1,0},{2,3},{3,2},{4,5},{5,4},{6,7},{7,6},{8,16},{9,17},{10,... | collective-permute-start | bytes 786440 | tf_op jit(solution)/shard_map/ppermute | solution.py:251
  53.0 0.5 collective-permute-start.21
  53.5 1.2 %collective-permute-start.20 = (bf16[128,128]{1,0:T(8,128)(2,1)S(1)}, bf16[128,128]{1,0:T(8,128)(2,1)S(1)}, u32[]{:S(2)}, u32[]{:S(2)}) collective-permute-start(bf16[128,128]{1,0:T(8,128)(2,1)S(1)} %get-tuple-element.74), channel_id=1, source_target_pairs={{0,1},{1,0},{2,3},{3,2},{4,5},{5,4},{6,7},{7,6},{8,9},{9,8},{10,11... | collective-permute-start | bytes 98312 | tf_op jit(solution)/shard_map/ppermute | solution.py:251
  54.7 4.0 %collective-permute-done.20.refs_10_ = bf16[128,128]{1,0:T(8,128)(2,1)S(1)} collective-permute-done((bf16[128,128]{1,0:T(8,128)(2,1)S(1)}, bf16[128,128]{1,0:T(8,128)(2,1)S(1)}, u32[]{:S(2)}, u32[]{:S(2)}) %collective-permute-start.20) | collective-permute-done | bytes 32800 | tf_op jit(solution)/shard_map/ppermute | solution.py:251
  58.7 3.1 %shard_map.83 = bf16[8192,128]{1,0:T(8,128)(2,1)} custom-call(bf16[8192,128]{1,0:T(8,128)(2,1)S(1)} %get-tuple-element.70.refs_0_, bf16[8192,128]{1,0:T(8,128)(2,1)S(1)} %get-tuple-element.65.refs_1_, f32[128,128]{1,0:T(8,128)S(1)} %get-tuple-element.39.refs_2_, bf16[128,176]{1,0:T(8,128)(2,1)S(1)} %get-tuple-element.40.refs_3_, ...), custom_call_target="tpu_custom_call" | custom-call | flops 805306368 | bytes 8388608 | tf_op jit(solution)/shard_map/pallas_call | solution.py:583
  (29 shorter events, 0.2 us)
Async XLA Ops:
  0.6 9.7 %copy-start.3 = (f32[8,8,128]{2,1,0:T(8,128)S(1)}, f32[8,8,128]{2,1,0:T(8,128)}, u32[]{:S(2)}) copy-start(f32[8,8,128]{2,1,0:T(8,128)} %param.8) | copy-start | bytes 98308
  5.9 13.1 %collective-permute-start.1 = (bf16[1024,128]{1,0:T(8,128)(2,1)}, bf16[1024,128]{1,0:T(8,128)(2,1)S(1)}, u32[]{:S(2)}, u32[]{:S(2)}) collective-permute-start(bf16[1024,128]{1,0:T(8,128)(2,1)} %get-tuple-element.48), channel_id=1, source_target_pairs={{0,4},{1,5},{2,6},{3,7},{4,0},{5,1},{6,2},{7,3},{8,12},{9,13},{10,... | collective-permute-start | bytes 786440 | tf_op jit(solution)/shard_map/ppermute | solution.py:251
  8.9 10.1 %collective-permute-start = (bf16[1024,128]{1,0:T(8,128)(2,1)}, bf16[1024,128]{1,0:T(8,128)(2,1)S(1)}, u32[]{:S(2)}, u32[]{:S(2)}) collective-permute-start(bf16[1024,128]{1,0:T(8,128)(2,1)} %get-tuple-element.50.refs_0_), channel_id=1, source_target_pairs={{0,16},{8,24},{16,0},{24,8},{1,17},{9,25},{17,1},{25,9},{2,18},{10... | collective-permute-start | bytes 786440 | tf_op jit(solution)/shard_map/ppermute | solution.py:608
  10.4 8.6 %copy-start.2 = (bf16[1024,128]{1,0:T(8,128)(2,1)S(1)}, bf16[1024,128]{1,0:T(8,128)(2,1)}, u32[]{:S(2)}) copy-start(bf16[1024,128]{1,0:T(8,128)(2,1)} %get-tuple-element.50.refs_0_) | copy-start | bytes 786436
  10.4 23.5 %copy-start.1 = (bf16[128,8,8,128]{3,2,1,0:T(8,128)(2,1)S(1)}, bf16[128,8,8,128]{3,2,1,0:T(8,128)(2,1)}, u32[]{:S(2)}) copy-start(bf16[128,8,8,128]{3,2,1,0:T(8,128)(2,1)} %param.7) | copy-start | bytes 6291460
  13.8 20.1 %copy-start = (bf16[128,8,8,128]{3,2,1,0:T(8,128)(2,1)S(1)}, bf16[128,8,8,128]{3,2,1,0:T(8,128)(2,1)}, u32[]{:S(2)}) copy-start(bf16[128,8,8,128]{3,2,1,0:T(8,128)(2,1)} %param.6) | copy-start | bytes 6291460
  13.8 20.1 %copy-start.4 = (s32[1,1,1,32]{3,2,1,0:T(1,128)S(1)}, s32[1,1,1,32]{3,2,1,0:T(1,128)}, u32[]{:S(2)}) copy-start(s32[1,1,1,32]{3,2,1,0:T(1,128)} %refs_16_.1) | copy-start | bytes 388
  13.9 3.2 %collective-permute-start.3 = (bf16[128,128]{1,0:T(8,128)(2,1)S(1)}, bf16[128,128]{1,0:T(8,128)(2,1)S(1)}, u32[]{:S(2)}, u32[]{:S(2)}) collective-permute-start(bf16[128,128]{1,0:T(8,128)(2,1)S(1)} %get-tuple-element.47), channel_id=1, source_target_pairs={{0,8},{1,2},{2,1},{3,11},{4,12},{5,6},{6,5},{7,15},{8,0},{9,10},{1... | collective-permute-start | bytes 98312 | tf_op jit(solution)/shard_map/ppermute | solution.py:251
  13.9 5.0 %collective-permute-start.2 = (bf16[128,128]{1,0:T(8,128)(2,1)S(1)}, bf16[128,128]{1,0:T(8,128)(2,1)S(1)}, u32[]{:S(2)}, u32[]{:S(2)}) collective-permute-start(bf16[128,128]{1,0:T(8,128)(2,1)S(1)} %get-tuple-element.47), channel_id=1, source_target_pairs={{0,1},{1,0},{2,3},{3,2},{4,5},{5,4},{6,7},{7,6},{8,9},{9,8},{10,11... | collective-permute-start | bytes 98312 | tf_op jit(solution)/shard_map/ppermute | solution.py:251
  19.0 2.6 %collective-permute-start.4 = (bf16[1024,128]{1,0:T(8,128)(2,1)S(1)}, bf16[1024,128]{1,0:T(8,128)(2,1)S(1)}, u32[]{:S(2)}, u32[]{:S(2)}) collective-permute-start(bf16[1024,128]{1,0:T(8,128)(2,1)S(1)} %copy-done.2), channel_id=1, source_target_pairs={{0,8},{8,0},{16,24},{24,16},{1,9},{9,1},{17,25},{25,17},{2,10},{10... | collective-permute-start | bytes 786440 | tf_op jit(solution)/shard_map/ppermute | solution.py:608
  19.1 2.5 %collective-permute-start.5 = (bf16[1024,128]{1,0:T(8,128)(2,1)S(1)}, bf16[1024,128]{1,0:T(8,128)(2,1)S(1)}, u32[]{:S(2)}, u32[]{:S(2)}) collective-permute-start(bf16[1024,128]{1,0:T(8,128)(2,1)S(1)} %collective-permute-done.refs_2_), channel_id=1, source_target_pairs={{0,8},{8,0},{16,24},{24,16},{1,9},{9,1},{17,25},{25,17},{2,10},{10... | collective-permute-start | bytes 786440 | tf_op jit(solution)/shard_map/ppermute | solution.py:608
  19.6 6.4 %collective-permute-start.7 = (bf16[1024,128]{1,0:T(8,128)(2,1)S(1)}, bf16[1024,128]{1,0:T(8,128)(2,1)S(1)}, u32[]{:S(2)}, u32[]{:S(2)}) collective-permute-start(bf16[1024,128]{1,0:T(8,128)(2,1)S(1)} %get-tuple-element.45), channel_id=1, source_target_pairs={{0,1},{1,0},{2,3},{3,2},{4,5},{5,4},{6,7},{7,6},{8,16},{9,17},{10,... | collective-permute-start | bytes 786440 | tf_op jit(solution)/shard_map/ppermute | solution.py:251
  21.6 4.4 %collective-permute-start.8 = (bf16[1024,128]{1,0:T(8,128)(2,1)S(1)}, bf16[1024,128]{1,0:T(8,128)(2,1)S(1)}, u32[]{:S(2)}, u32[]{:S(2)}) collective-permute-start(bf16[1024,128]{1,0:T(8,128)(2,1)S(1)} %get-tuple-element.46), channel_id=1, source_target_pairs={{0,8},{1,9},{2,10},{3,11},{4,12},{5,13},{6,14},{7,15},{8,0},{9,1},... | collective-permute-start | bytes 786440 | tf_op jit(solution)/shard_map/ppermute | solution.py:251
  22.3 4.6 %collective-permute-start.6 = (f32[128,128]{1,0:T(8,128)S(1)}, f32[128,128]{1,0:T(8,128)S(1)}, u32[]{:S(2)}, u32[]{:S(2)}) collective-permute-start(f32[128,128]{1,0:T(8,128)S(1)} %get-tuple-element.53), channel_id=1, source_target_pairs={{0,4},{4,0},{1,5},{5,1},{2,6},{6,2},{3,7},{7,3},{8,12},{12,8},{9,1... | collective-permute-start | bytes 196616 | tf_op jit(solution)/shard_map/ppermute | solution.py:205
  27.0 5.9 %collective-permute-start.9 = (f32[64,128]{1,0:T(8,128)S(1)}, f32[64,128]{1,0:T(8,128)S(1)}, u32[]{:S(2)}, u32[]{:S(2)}) collective-permute-start(f32[64,128]{1,0:T(8,128)S(1)} %get-tuple-element.61), channel_id=1, source_target_pairs={{0,3},{1,2},{2,1},{3,0},{4,7},{5,6},{6,5},{7,4},{8,11},{9,10},{10,... | collective-permute-start | bytes 98312 | tf_op jit(solution)/shard_map/ppermute | solution.py:210
  28.7 5.0 %collective-permute-start.10 = (f32[64,128]{1,0:T(8,128)S(1)}, f32[64,128]{1,0:T(8,128)S(1)}, u32[]{:S(2)}, u32[]{:S(2)}) collective-permute-start(f32[64,128]{1,0:T(8,128)S(1)} %get-tuple-element.62), channel_id=1, source_target_pairs={{0,2},{1,3},{2,0},{3,1},{4,6},{5,7},{6,4},{7,5},{8,10},{9,11},{10,... | collective-permute-start | bytes 98312 | tf_op jit(solution)/shard_map/ppermute | solution.py:210
  29.7 4.2 %collective-permute-start.11 = (f32[64,128]{1,0:T(8,128)S(1)}, f32[64,128]{1,0:T(8,128)S(1)}, u32[]{:S(2)}, u32[]{:S(2)}) collective-permute-start(f32[64,128]{1,0:T(8,128)S(1)} %get-tuple-element.63), channel_id=1, source_target_pairs={{0,1},{1,0},{2,3},{3,2},{4,5},{5,4},{6,7},{7,6},{8,9},{9,8},{10,11... | collective-permute-start | bytes 98312 | tf_op jit(solution)/shard_map/ppermute | solution.py:210
  38.7 7.6 %collective-permute-start.12 = (bf16[1024,128]{1,0:T(8,128)(2,1)S(1)}, bf16[1024,128]{1,0:T(8,128)(2,1)S(1)}, u32[]{:S(2)}, u32[]{:S(2)}) collective-permute-start(bf16[1024,128]{1,0:T(8,128)(2,1)S(1)} %get-tuple-element.66), channel_id=1, source_target_pairs={{0,4},{1,5},{2,6},{3,7},{4,0},{5,1},{6,2},{7,3},{8,12},{9,13},{10,... | collective-permute-start | bytes 786440 | tf_op jit(solution)/shard_map/ppermute | solution.py:251
  39.2 7.1 %collective-permute-start.13 = (bf16[1024,128]{1,0:T(8,128)(2,1)S(1)}, bf16[1024,128]{1,0:T(8,128)(2,1)S(1)}, u32[]{:S(2)}, u32[]{:S(2)}) collective-permute-start(bf16[1024,128]{1,0:T(8,128)(2,1)S(1)} %get-tuple-element.67), channel_id=1, source_target_pairs={{0,1},{1,0},{2,3},{3,2},{4,5},{5,4},{6,7},{7,6},{8,16},{9,17},{10,... | collective-permute-start | bytes 786440 | tf_op jit(solution)/shard_map/ppermute | solution.py:251
  40.6 5.6 %collective-permute-start.14 = (bf16[1024,128]{1,0:T(8,128)(2,1)S(1)}, bf16[1024,128]{1,0:T(8,128)(2,1)S(1)}, u32[]{:S(2)}, u32[]{:S(2)}) collective-permute-start(bf16[1024,128]{1,0:T(8,128)(2,1)S(1)} %get-tuple-element.68), channel_id=1, source_target_pairs={{0,8},{1,9},{2,10},{3,11},{4,12},{5,13},{6,14},{7,15},{8,0},{9,1},... | collective-permute-start | bytes 786440 | tf_op jit(solution)/shard_map/ppermute | solution.py:251
  40.7 1.7 %collective-permute-start.16 = (bf16[128,128]{1,0:T(8,128)(2,1)S(1)}, bf16[128,128]{1,0:T(8,128)(2,1)S(1)}, u32[]{:S(2)}, u32[]{:S(2)}) collective-permute-start(bf16[128,128]{1,0:T(8,128)(2,1)S(1)} %get-tuple-element.69), channel_id=1, source_target_pairs={{0,8},{1,2},{2,1},{3,11},{4,12},{5,6},{6,5},{7,15},{8,0},{9,10},{1... | collective-permute-start | bytes 98312 | tf_op jit(solution)/shard_map/ppermute | solution.py:251
  41.2 5.1 %collective-permute-start.15 = (bf16[128,128]{1,0:T(8,128)(2,1)S(1)}, bf16[128,128]{1,0:T(8,128)(2,1)S(1)}, u32[]{:S(2)}, u32[]{:S(2)}) collective-permute-start(bf16[128,128]{1,0:T(8,128)(2,1)S(1)} %get-tuple-element.69), channel_id=1, source_target_pairs={{0,1},{1,0},{2,3},{3,2},{4,5},{5,4},{6,7},{7,6},{8,9},{9,8},{10,11... | collective-permute-start | bytes 98312 | tf_op jit(solution)/shard_map/ppermute | solution.py:251
  50.1 8.6 %collective-permute-start.17 = (bf16[1024,128]{1,0:T(8,128)(2,1)S(1)}, bf16[1024,128]{1,0:T(8,128)(2,1)S(1)}, u32[]{:S(2)}, u32[]{:S(2)}) collective-permute-start(bf16[1024,128]{1,0:T(8,128)(2,1)S(1)} %get-tuple-element.71), channel_id=1, source_target_pairs={{0,4},{1,5},{2,6},{3,7},{4,0},{5,1},{6,2},{7,3},{8,12},{9,13},{10,... | collective-permute-start | bytes 786440 | tf_op jit(solution)/shard_map/ppermute | solution.py:251
  51.6 7.1 %collective-permute-start.18 = (bf16[1024,128]{1,0:T(8,128)(2,1)S(1)}, bf16[1024,128]{1,0:T(8,128)(2,1)S(1)}, u32[]{:S(2)}, u32[]{:S(2)}) collective-permute-start(bf16[1024,128]{1,0:T(8,128)(2,1)S(1)} %get-tuple-element.72), channel_id=1, source_target_pairs={{0,1},{1,0},{2,3},{3,2},{4,5},{5,4},{6,7},{7,6},{8,16},{9,17},{10,... | collective-permute-start | bytes 786440 | tf_op jit(solution)/shard_map/ppermute | solution.py:251
  53.0 5.6 %collective-permute-start.19 = (bf16[1024,128]{1,0:T(8,128)(2,1)S(1)}, bf16[1024,128]{1,0:T(8,128)(2,1)S(1)}, u32[]{:S(2)}, u32[]{:S(2)}) collective-permute-start(bf16[1024,128]{1,0:T(8,128)(2,1)S(1)} %get-tuple-element.73), channel_id=1, source_target_pairs={{0,8},{1,9},{2,10},{3,11},{4,12},{5,13},{6,14},{7,15},{8,0},{9,1},... | collective-permute-start | bytes 786440 | tf_op jit(solution)/shard_map/ppermute | solution.py:251
  53.0 1.7 %collective-permute-start.21 = (bf16[128,128]{1,0:T(8,128)(2,1)S(1)}, bf16[128,128]{1,0:T(8,128)(2,1)S(1)}, u32[]{:S(2)}, u32[]{:S(2)}) collective-permute-start(bf16[128,128]{1,0:T(8,128)(2,1)S(1)} %get-tuple-element.74), channel_id=1, source_target_pairs={{0,8},{1,2},{2,1},{3,11},{4,12},{5,6},{6,5},{7,15},{8,0},{9,10},{1... | collective-permute-start | bytes 98312 | tf_op jit(solution)/shard_map/ppermute | solution.py:251
  53.5 5.1 %collective-permute-start.20 = (bf16[128,128]{1,0:T(8,128)(2,1)S(1)}, bf16[128,128]{1,0:T(8,128)(2,1)S(1)}, u32[]{:S(2)}, u32[]{:S(2)}) collective-permute-start(bf16[128,128]{1,0:T(8,128)(2,1)S(1)} %get-tuple-element.74), channel_id=1, source_target_pairs={{0,1},{1,0},{2,3},{3,2},{4,5},{5,4},{6,7},{7,6},{8,9},{9,8},{10,11... | collective-permute-start | bytes 98312 | tf_op jit(solution)/shard_map/ppermute | solution.py:251

commit v10 on v9

--- a/solution.py
+++ b/solution.py
@@ -196,25 +196,26 @@
     )(mine, other)
 
 
-def flux_sums(parts, held, late):
+def flux_sums(parts, held, late, after):
     cols, gzs = lax.axis_size("col"), lax.axis_size("gz")
     sides = parts[0].shape[1]
     lines = held.shape[1]
     if cols == 2 and gzs & (gzs - 1) == 0 and lines // cols == sides and sides // gzs % 8 == 0:
         mine, other = surface(parts, held, 2)
+        mine, other, after = lax.optimization_barrier((mine, other, after))
         other = lax.ppermute(other, "col", [(0, 1), (1, 0)])
         other, late = lax.optimization_barrier((other, late))
         sent = shares(mine, other)
         recv = [sent[0]]
         for key in range(gzs - 1, 0, -1):
             recv.append(lax.ppermute(sent[key], "gz", [(i, i ^ key) for i in range(gzs)]))
-        return recv, late
+        return recv, after
     (total,) = surface(parts, held, 1)
     rows = lax.psum_scatter(total, "col", scatter_dimension=0, tiled=True)
     owned = lax.psum_scatter(rows, "gz", scatter_dimension=0, tiled=True)
     flux = lax.psum_scatter(rows.T, "gz", scatter_dimension=0, tiled=True)
     flux = jnp.pad(flux, ((0, 0), (0, sides - flux.shape[1])))
-    return [jnp.concatenate([owned, flux], axis=0)], late
+    return [jnp.concatenate([owned, flux], axis=0)], after
 
 
 def turns(axis):
@@ -593,10 +594,17 @@
     )(*operands)
 
 
+def swap_faces(faces, values):
+    return [swap(value, *face) for face, value in zip(faces, values)]
+
+
+def swap_ends(shape, ends):
+    return [swap(ends, "gz", turn) for turn in range(shape.ends)]
+
+
 def exchange(shape, faces):
     *cut, ends = faces
-    halos = [swap(value, *face) for face, value in zip(shape.faces, cut)]
-    return halos + [swap(ends, "gz", turn) for turn in range(shape.ends)]
+    return swap_faces(shape.faces, cut) + swap_ends(shape, ends)
 
 
 def row_gather(trace, hidden):
@@ -629,11 +637,12 @@
     layers = len(shape.faces)
     count = len(shape.inner) + 1
     inner, held, tables = firsts[:count], firsts[count], firsts[count + 1 :]
-    halos = exchange(shape, [*outer, *inner])
-    early = len(shape.outer)
-    parts, (_, along_col, ends) = row_gather(trace, (inner, halos[:early], halos[layers:]))
-    recv, along_row = flux_sums(parts, held, halos[early:layers])
-    halos = along_col + along_row + ends
+    *inner, ends = inner
+    along_col = swap_faces(shape.outer, outer)
+    parts, (inner, along_col) = row_gather(trace, (inner, along_col))
+    along_row = swap_faces(shape.inner, inner)
+    recv, ends = flux_sums(parts, held, along_row, ends)
+    halos = along_col + along_row + swap_ends(shape, ends)
 
     current, *faces, source, surface_flux = sweep(
         shape, field, load, tables, halos, recv=recv, flux_cell=flux_cell

time: 62.1 us -> 60.8 us (0.979)
  waiting for transfers between devices: 16.3 us -> 15.1 us
    ppermute x15, waiting for transfers between devices: 12.9 us -> 9.34 us  [swap(): return lax.ppermute(value, axes, pairs)]
    ppermute x3, waiting for transfers between devices: 0.01 us -> 1.47 us  [row_gather(): lax.ppermute(held[key], 'row', pairs)]
    ppermute x3, waiting for transfers between devices: 2.47 us -> 3.81 us  [flux_sums(): lax.ppermute(sent[key], 'gz', [(i, i ^ key) for i in range(gzs)])]
where the time goes in v10:
time: 60.8 us; the launch traced here: 60.7 us
  starting transfers between devices  23.5 us (39%)
  Pallas kernels  21.2 us (35%)
  waiting for transfers between devices  15.1 us (25%)
  between operations  0.89 us (1%)
    ppermute x15, starting transfers between devices, swap(): return lax.ppermute(value, axes, pairs)  16.4 us
    pallas_call x3, Pallas kernels, sweep(): pl.pallas_call(functools.partial(sweep_kernel, shape, len(recv), last), i...  11.7 us
    ppermute x15, waiting for transfers between devices, swap(): return lax.ppermute(value, axes, pairs)  9.34 us
    pallas_call x1, Pallas kernels, traces(): pl.pallas_call(functools.partial(trace_kernel, shape, stride, block), in_...  5.21 us
    ppermute x3, starting transfers between devices, flux_sums(): lax.ppermute(sent[key], 'gz', [(i, i ^ key) for i in range(gzs)])  4.45 us
    ppermute x3, waiting for transfers between devices, flux_sums(): lax.ppermute(sent[key], 'gz', [(i, i ^ key) for i in range(gzs)])  3.81 us
    pallas_call x1, Pallas kernels, first_faces(): pl.pallas_call(functools.partial(faces_kernel, shape, slots), in_specs=[h...  3.46 us
    ppermute x3, starting transfers between devices, row_gather(): lax.ppermute(held[key], 'row', pairs)  2 us
  transfers between devices with their start and end apart: 22, of which 8 were waited for; matrix products, arithmetic and copies ran while one was open for 0% of the time, Pallas kernels for 7%

profile of v10, /device:TPU:0, one launch (start us, length us, event | category | flops | bytes accessed | tf_op | source)
XLA Modules:
  0.0 60.7 jit_solution(1310070606396199847)
XLA Ops:
  0.6 5.2 %shard_map.78 = (bf16[1024,128]{1,0:T(8,128)(2,1)}, bf16[1024,128]{1,0:T(8,128)(2,1)}) custom-call(bf16[128,64,128]{2,1,0:T(8,128)(2,1)} %bitcast.5, s32[1,1,1,1024]{3,2,1,0:T(1,128)} %cell_ref.1), custom_call_target="tpu_custom_call" | custom-call | flops 536870912 | bytes 2097152 | tf_op jit(solution)/shard_map/pallas_call | solution.py:102
  5.9 3.0 %collective-permute-start.1 = (bf16[1024,128]{1,0:T(8,128)(2,1)}, bf16[1024,128]{1,0:T(8,128)(2,1)S(1)}, u32[]{:S(2)}, u32[]{:S(2)}) collective-permute-start(bf16[1024,128]{1,0:T(8,128)(2,1)} %get-tuple-element.48), channel_id=1, source_target_pairs={{0,4},{1,5},{2,6},{3,7},{4,0},{5,1},{6,2},{7,3},{8,12},{9,13},{10,... | collective-permute-start | bytes 786440 | tf_op jit(solution)/shard_map/ppermute | solution.py:252
  8.9 1.5 %collective-permute-start = (bf16[1024,128]{1,0:T(8,128)(2,1)}, bf16[1024,128]{1,0:T(8,128)(2,1)S(1)}, u32[]{:S(2)}, u32[]{:S(2)}) collective-permute-start(bf16[1024,128]{1,0:T(8,128)(2,1)} %get-tuple-element.52.refs_0_), channel_id=1, source_target_pairs={{0,16},{8,24},{16,0},{24,8},{1,17},{9,25},{17,1},{25,9},{2,18},{10... | collective-permute-start | bytes 786440 | tf_op jit(solution)/shard_map/ppermute | solution.py:616
  10.4 3.5 %shard_map.77 = (bf16[1024,128]{1,0:T(8,128)(2,1)S(1)}, bf16[1024,128]{1,0:T(8,128)(2,1)S(1)}, bf16[128,128]{1,0:T(8,128)(2,1)S(1)}, bf16[4,256,1024]{2,1,0:T(8,...) custom-call(bf16[8192,128]{1,0:T(8,128)(2,1)} %bitcast.6, ...), custom_call_target="tpu_custom_call" | custom-call | flops 134217728 | bytes 4194304 | tf_op jit(solution)/shard_map/pallas_call | solution.py:415
  13.9 1.5 %collective-permute-done.1.refs_7_ = bf16[1024,128]{1,0:T(8,128)(2,1)S(1)} collective-permute-done((bf16[1024,128]{1,0:T(8,128)(2,1)}, bf16[1024,128]{1,0:T(8,128)(2,1)S(1)}, u32[]{:S(2)}, u32[]{:S(2)}) %collective-permute-start.1) | collective-permute-done | bytes 262176 | tf_op jit(solution)/shard_map/ppermute | solution.py:252
  15.4 1.5 %collective-permute-done.refs_2_ = bf16[1024,128]{1,0:T(8,128)(2,1)S(1)} collective-permute-done((bf16[1024,128]{1,0:T(8,128)(2,1)}, bf16[1024,128]{1,0:T(8,128)(2,1)S(1)}, u32[]{:S(2)}, u32[]{:S(2)}) %collective-permute-start) | collective-permute-done | bytes 262176 | tf_op jit(solution)/shard_map/ppermute | solution.py:616
  16.9 0.5 collective-permute-start.5
  17.4 1.6 %collective-permute-start.2 = (bf16[1024,128]{1,0:T(8,128)(2,1)S(1)}, bf16[1024,128]{1,0:T(8,128)(2,1)S(1)}, u32[]{:S(2)}, u32[]{:S(2)}) collective-permute-start(bf16[1024,128]{1,0:T(8,128)(2,1)S(1)} %get-tuple-element.50), channel_id=1, source_target_pairs={{0,1},{1,0},{2,3},{3,2},{4,5},{5,4},{6,7},{7,6},{8,16},{9,17},{10,... | collective-permute-start | bytes 786440 | tf_op jit(solution)/shard_map/ppermute | solution.py:252
  19.0 0.7 %shard_map.79 = (f32[128,128]{1,0:T(8,128)S(1)}, f32[128,128]{1,0:T(8,128)S(1)}) custom-call(bf16[1024,128]{1,0:T(8,128)(2,1)S(1)} %copy-done.2, bf16[1024,128]{1,0:T(8,128)(2,1)S(1)} %collective-permute-done.4.refs_1_, bf16[1024,128]{1,0:T(8,128)(2,1)S(1)} %collective-permute-done.refs_2_, bf16[1024,128]{1,0:T(8,128)(2,1)S(1)} %collective-permute-done.5.refs_3_, ...), custom_call_target="tpu_custom_call" | custom-call | flops 268435456 | bytes 2097152 | tf_op jit(solution)/shard_map/pallas_call | solution.py:156
  19.7 0.6 collective-permute-start.8
  20.3 0.2 collective-permute-start.7
  20.5 3.0 %collective-permute-start.6 = (bf16[128,128]{1,0:T(8,128)(2,1)S(1)}, bf16[128,128]{1,0:T(8,128)(2,1)S(1)}, u32[]{:S(2)}, u32[]{:S(2)}) collective-permute-start(bf16[128,128]{1,0:T(8,128)(2,1)S(1)} %get-tuple-element.58), channel_id=1, source_target_pairs={{0,1},{1,0},{2,3},{3,2},{4,5},{5,4},{6,7},{7,6},{8,9},{9,8},{10,11... | collective-permute-start | bytes 98312 | tf_op jit(solution)/shard_map/ppermute | solution.py:252
  23.4 0.3 collective-permute-done.2.refs_8_
  23.7 0.5 collective-permute-done.8.other_ref
  24.2 0.1 shard_map.80
  24.4 3.5 %collective-permute-start.9 = (f32[64,128]{1,0:T(8,128)S(1)}, f32[64,128]{1,0:T(8,128)S(1)}, u32[]{:S(2)}, u32[]{:S(2)}) collective-permute-start(f32[64,128]{1,0:T(8,128)S(1)} %get-tuple-element.63), channel_id=1, source_target_pairs={{0,3},{1,2},{2,1},{3,0},{4,7},{5,6},{6,5},{7,4},{8,11},{9,10},{10,... | collective-permute-start | bytes 98312 | tf_op jit(solution)/shard_map/ppermute | solution.py:211
  27.8 1.0 %collective-permute-start.11 = (f32[64,128]{1,0:T(8,128)S(1)}, f32[64,128]{1,0:T(8,128)S(1)}, u32[]{:S(2)}, u32[]{:S(2)}) collective-permute-start(f32[64,128]{1,0:T(8,128)S(1)} %get-tuple-element.65), channel_id=1, source_target_pairs={{0,1},{1,0},{2,3},{3,2},{4,5},{5,4},{6,7},{7,6},{8,9},{9,8},{10,11... | collective-permute-start | bytes 98312 | tf_op jit(solution)/shard_map/ppermute | solution.py:211
  28.8 1.5 %collective-permute-done.9.refs_13_ = f32[64,128]{1,0:T(8,128)S(1)} collective-permute-done((f32[64,128]{1,0:T(8,128)S(1)}, f32[64,128]{1,0:T(8,128)S(1)}, u32[]{:S(2)}, u32[]{:S(2)}) %collective-permute-start.9) | collective-permute-done | bytes 32800 | tf_op jit(solution)/shard_map/ppermute | solution.py:211
  30.3 2.3 %collective-permute-done.10.refs_14_ = f32[64,128]{1,0:T(8,128)S(1)} collective-permute-done((f32[64,128]{1,0:T(8,128)S(1)}, f32[64,128]{1,0:T(8,128)S(1)}, u32[]{:S(2)}, u32[]{:S(2)}) %collective-permute-start.10) | collective-permute-done | bytes 32800 | tf_op jit(solution)/shard_map/ppermute | solution.py:211
  32.6 4.8 %shard_map.81 = (bf16[8192,128]{1,0:T(8,128)(2,1)S(1)}, bf16[1024,128]{1,0:T(8,128)(2,1)S(1)}, bf16[1024,128]{1,0:T(8,128)(2,1)S(1)}, bf16[1024,128]{1,0:T(8,128...) custom-call(bf16[8192,128]{1,0:T(8,128)(2,1)S(1)} %bitcast.7, ...), custom_call_target="tpu_custom_call" | custom-call | flops 805306368 | bytes 8388608 | tf_op jit(solution)/shard_map/pallas_call | solution.py:584
  37.4 0.5 collective-permute-start.12
  37.9 0.3 collective-permute-start.13
  38.2 1.1 %collective-permute-start.14 = (bf16[1024,128]{1,0:T(8,128)(2,1)S(1)}, bf16[1024,128]{1,0:T(8,128)(2,1)S(1)}, u32[]{:S(2)}, u32[]{:S(2)}) collective-permute-start(bf16[1024,128]{1,0:T(8,128)(2,1)S(1)} %get-tuple-element.70), channel_id=1, source_target_pairs={{0,8},{1,9},{2,10},{3,11},{4,12},{5,13},{6,14},{7,15},{8,0},{9,1},... | collective-permute-start | bytes 786440 | tf_op jit(solution)/shard_map/ppermute | solution.py:252
  39.3 2.6 %collective-permute-start.15 = (bf16[128,128]{1,0:T(8,128)(2,1)S(1)}, bf16[128,128]{1,0:T(8,128)(2,1)S(1)}, u32[]{:S(2)}, u32[]{:S(2)}) collective-permute-start(bf16[128,128]{1,0:T(8,128)(2,1)S(1)} %get-tuple-element.71), channel_id=1, source_target_pairs={{0,1},{1,0},{2,3},{3,2},{4,5},{5,4},{6,7},{7,6},{8,9},{9,8},{10,11... | collective-permute-start | bytes 98312 | tf_op jit(solution)/shard_map/ppermute | solution.py:252
  41.9 3.1 %collective-permute-done.15.refs_10_ = bf16[128,128]{1,0:T(8,128)(2,1)S(1)} collective-permute-done((bf16[128,128]{1,0:T(8,128)(2,1)S(1)}, bf16[128,128]{1,0:T(8,128)(2,1)S(1)}, u32[]{:S(2)}, u32[]{:S(2)}) %collective-permute-start.15) | collective-permute-done | bytes 32800 | tf_op jit(solution)/shard_map/ppermute | solution.py:252
  45.0 3.8 %shard_map.82 = (bf16[8192,128]{1,0:T(8,128)(2,1)S(1)}, bf16[1024,128]{1,0:T(8,128)(2,1)S(1)}, bf16[1024,128]{1,0:T(8,128)(2,1)S(1)}, bf16[1024,128]{1,0:T(8,128)(2,1)S(1)}, bf16[128,128]{1,0:T(8,128)(2,1)S(1)}) custom-call(bf16[8192,128]{1,0:T(8,128)(2,1)S(1)} %get-tuple-element.66.refs_0_, bf16[8192,128]{1,0:T(8,128)(2,1)S(1)} %get-tuple-element.67.refs_1_, ...), custom_call_target="tpu_custom_call" | custom-call | flops 805306368 | bytes 8388608 | tf_op jit(solution)/shard_map/pallas_call | solution.py:584
  48.8 1.5 %collective-permute-start.17 = (bf16[1024,128]{1,0:T(8,128)(2,1)S(1)}, bf16[1024,128]{1,0:T(8,128)(2,1)S(1)}, u32[]{:S(2)}, u32[]{:S(2)}) collective-permute-start(bf16[1024,128]{1,0:T(8,128)(2,1)S(1)} %get-tuple-element.73), channel_id=1, source_target_pairs={{0,4},{1,5},{2,6},{3,7},{4,0},{5,1},{6,2},{7,3},{8,12},{9,13},{10,... | collective-permute-start | bytes 786440 | tf_op jit(solution)/shard_map/ppermute | solution.py:252
  50.3 0.8 %collective-permute-start.18 = (bf16[1024,128]{1,0:T(8,128)(2,1)S(1)}, bf16[1024,128]{1,0:T(8,128)(2,1)S(1)}, u32[]{:S(2)}, u32[]{:S(2)}) collective-permute-start(bf16[1024,128]{1,0:T(8,128)(2,1)S(1)} %get-tuple-element.74), channel_id=1, source_target_pairs={{0,1},{1,0},{2,3},{3,2},{4,5},{5,4},{6,7},{7,6},{8,16},{9,17},{10,... | collective-permute-start | bytes 786440 | tf_op jit(solution)/shard_map/ppermute | solution.py:252
  51.1 0.5 collective-permute-start.21
  51.6 1.4 %collective-permute-start.20 = (bf16[128,128]{1,0:T(8,128)(2,1)S(1)}, bf16[128,128]{1,0:T(8,128)(2,1)S(1)}, u32[]{:S(2)}, u32[]{:S(2)}) collective-permute-start(bf16[128,128]{1,0:T(8,128)(2,1)S(1)} %get-tuple-element.76), channel_id=1, source_target_pairs={{0,1},{1,0},{2,3},{3,2},{4,5},{5,4},{6,7},{7,6},{8,9},{9,8},{10,11... | collective-permute-start | bytes 98312 | tf_op jit(solution)/shard_map/ppermute | solution.py:252
  53.0 4.4 %collective-permute-done.20.refs_10_ = bf16[128,128]{1,0:T(8,128)(2,1)S(1)} collective-permute-done((bf16[128,128]{1,0:T(8,128)(2,1)S(1)}, bf16[128,128]{1,0:T(8,128)(2,1)S(1)}, u32[]{:S(2)}, u32[]{:S(2)}) %collective-permute-start.20) | collective-permute-done | bytes 32800 | tf_op jit(solution)/shard_map/ppermute | solution.py:252
  57.4 3.1 %shard_map.83 = bf16[8192,128]{1,0:T(8,128)(2,1)} custom-call(bf16[8192,128]{1,0:T(8,128)(2,1)S(1)} %get-tuple-element.72.refs_0_, bf16[8192,128]{1,0:T(8,128)(2,1)S(1)} %get-tuple-element.67.refs_1_, f32[128,128]{1,0:T(8,128)S(1)} %get-tuple-element.40.refs_2_, bf16[128,176]{1,0:T(8,128)(2,1)S(1)} %get-tuple-element.41.refs_3_, ...), custom_call_target="tpu_custom_call" | custom-call | flops 805306368 | bytes 8388608 | tf_op jit(solution)/shard_map/pallas_call | solution.py:584
  (29 shorter events, 0.1 us)
Async XLA Ops:
  0.6 9.7 %copy-start.3 = (f32[8,8,128]{2,1,0:T(8,128)S(1)}, f32[8,8,128]{2,1,0:T(8,128)}, u32[]{:S(2)}) copy-start(f32[8,8,128]{2,1,0:T(8,128)} %param.8) | copy-start | bytes 98308
  5.9 9.5 %collective-permute-start.1 = (bf16[1024,128]{1,0:T(8,128)(2,1)}, bf16[1024,128]{1,0:T(8,128)(2,1)S(1)}, u32[]{:S(2)}, u32[]{:S(2)}) collective-permute-start(bf16[1024,128]{1,0:T(8,128)(2,1)} %get-tuple-element.48), channel_id=1, source_target_pairs={{0,4},{1,5},{2,6},{3,7},{4,0},{5,1},{6,2},{7,3},{8,12},{9,13},{10,... | collective-permute-start | bytes 786440 | tf_op jit(solution)/shard_map/ppermute | solution.py:252
  8.9 8.0 %collective-permute-start = (bf16[1024,128]{1,0:T(8,128)(2,1)}, bf16[1024,128]{1,0:T(8,128)(2,1)S(1)}, u32[]{:S(2)}, u32[]{:S(2)}) collective-permute-start(bf16[1024,128]{1,0:T(8,128)(2,1)} %get-tuple-element.52.refs_0_), channel_id=1, source_target_pairs={{0,16},{8,24},{16,0},{24,8},{1,17},{9,25},{17,1},{25,9},{2,18},{10... | collective-permute-start | bytes 786440 | tf_op jit(solution)/shard_map/ppermute | solution.py:616
  10.4 6.5 %copy-start.2 = (bf16[1024,128]{1,0:T(8,128)(2,1)S(1)}, bf16[1024,128]{1,0:T(8,128)(2,1)}, u32[]{:S(2)}) copy-start(bf16[1024,128]{1,0:T(8,128)(2,1)} %get-tuple-element.52.refs_0_) | copy-start | bytes 786436
  10.4 22.3 %copy-start.1 = (bf16[128,8,8,128]{3,2,1,0:T(8,128)(2,1)S(1)}, bf16[128,8,8,128]{3,2,1,0:T(8,128)(2,1)}, u32[]{:S(2)}) copy-start(bf16[128,8,8,128]{3,2,1,0:T(8,128)(2,1)} %param.7) | copy-start | bytes 6291460
  13.8 18.8 %copy-start = (bf16[128,8,8,128]{3,2,1,0:T(8,128)(2,1)S(1)}, bf16[128,8,8,128]{3,2,1,0:T(8,128)(2,1)}, u32[]{:S(2)}) copy-start(bf16[128,8,8,128]{3,2,1,0:T(8,128)(2,1)} %param.6) | copy-start | bytes 6291460
  13.8 18.8 %copy-start.4 = (s32[1,1,1,32]{3,2,1,0:T(1,128)S(1)}, s32[1,1,1,32]{3,2,1,0:T(1,128)}, u32[]{:S(2)}) copy-start(s32[1,1,1,32]{3,2,1,0:T(1,128)} %refs_16_.1) | copy-start | bytes 388
  16.9 2.1 %collective-permute-start.4 = (bf16[1024,128]{1,0:T(8,128)(2,1)S(1)}, bf16[1024,128]{1,0:T(8,128)(2,1)S(1)}, u32[]{:S(2)}, u32[]{:S(2)}) collective-permute-start(bf16[1024,128]{1,0:T(8,128)(2,1)S(1)} %copy-done.2), channel_id=1, source_target_pairs={{0,8},{8,0},{16,24},{24,16},{1,9},{9,1},{17,25},{25,17},{2,10},{10... | collective-permute-start | bytes 786440 | tf_op jit(solution)/shard_map/ppermute | solution.py:616
  16.9 2.1 %collective-permute-start.5 = (bf16[1024,128]{1,0:T(8,128)(2,1)S(1)}, bf16[1024,128]{1,0:T(8,128)(2,1)S(1)}, u32[]{:S(2)}, u32[]{:S(2)}) collective-permute-start(bf16[1024,128]{1,0:T(8,128)(2,1)S(1)} %collective-permute-done.refs_2_), channel_id=1, source_target_pairs={{0,8},{8,0},{16,24},{24,16},{1,9},{9,1},{17,25},{25,17},{2,10},{10... | collective-permute-start | bytes 786440 | tf_op jit(solution)/shard_map/ppermute | solution.py:616
  17.4 6.4 %collective-permute-start.2 = (bf16[1024,128]{1,0:T(8,128)(2,1)S(1)}, bf16[1024,128]{1,0:T(8,128)(2,1)S(1)}, u32[]{:S(2)}, u32[]{:S(2)}) collective-permute-start(bf16[1024,128]{1,0:T(8,128)(2,1)S(1)} %get-tuple-element.50), channel_id=1, source_target_pairs={{0,1},{1,0},{2,3},{3,2},{4,5},{5,4},{6,7},{7,6},{8,16},{9,17},{10,... | collective-permute-start | bytes 786440 | tf_op jit(solution)/shard_map/ppermute | solution.py:252
  18.9 4.8 %collective-permute-start.3 = (bf16[1024,128]{1,0:T(8,128)(2,1)S(1)}, bf16[1024,128]{1,0:T(8,128)(2,1)S(1)}, u32[]{:S(2)}, u32[]{:S(2)}) collective-permute-start(bf16[1024,128]{1,0:T(8,128)(2,1)S(1)} %get-tuple-element.51), channel_id=1, source_target_pairs={{0,8},{1,9},{2,10},{3,11},{4,12},{5,13},{6,14},{7,15},{8,0},{9,1},... | collective-permute-start | bytes 786440 | tf_op jit(solution)/shard_map/ppermute | solution.py:252
  19.7 4.5 %collective-permute-start.8 = (f32[128,128]{1,0:T(8,128)S(1)}, f32[128,128]{1,0:T(8,128)S(1)}, u32[]{:S(2)}, u32[]{:S(2)}) collective-permute-start(f32[128,128]{1,0:T(8,128)S(1)} %get-tuple-element.60), channel_id=1, source_target_pairs={{0,4},{4,0},{1,5},{5,1},{2,6},{6,2},{3,7},{7,3},{8,12},{12,8},{9,1... | collective-permute-start | bytes 196616 | tf_op jit(solution)/shard_map/ppermute | solution.py:206
  20.3 8.5 %collective-permute-start.7 = (bf16[128,128]{1,0:T(8,128)(2,1)S(1)}, bf16[128,128]{1,0:T(8,128)(2,1)S(1)}, u32[]{:S(2)}, u32[]{:S(2)}) collective-permute-start(bf16[128,128]{1,0:T(8,128)(2,1)S(1)} %get-tuple-element.58), channel_id=1, source_target_pairs={{0,8},{1,2},{2,1},{3,11},{4,12},{5,6},{6,5},{7,15},{8,0},{9,10},{1... | collective-permute-start | bytes 98312 | tf_op jit(solution)/shard_map/ppermute | solution.py:252
  20.5 8.3 %collective-permute-start.6 = (bf16[128,128]{1,0:T(8,128)(2,1)S(1)}, bf16[128,128]{1,0:T(8,128)(2,1)S(1)}, u32[]{:S(2)}, u32[]{:S(2)}) collective-permute-start(bf16[128,128]{1,0:T(8,128)(2,1)S(1)} %get-tuple-element.58), channel_id=1, source_target_pairs={{0,1},{1,0},{2,3},{3,2},{4,5},{5,4},{6,7},{7,6},{8,9},{9,8},{10,11... | collective-permute-start | bytes 98312 | tf_op jit(solution)/shard_map/ppermute | solution.py:252
  24.4 6.0 %collective-permute-start.9 = (f32[64,128]{1,0:T(8,128)S(1)}, f32[64,128]{1,0:T(8,128)S(1)}, u32[]{:S(2)}, u32[]{:S(2)}) collective-permute-start(f32[64,128]{1,0:T(8,128)S(1)} %get-tuple-element.63), channel_id=1, source_target_pairs={{0,3},{1,2},{2,1},{3,0},{4,7},{5,6},{6,5},{7,4},{8,11},{9,10},{10,... | collective-permute-start | bytes 98312 | tf_op jit(solution)/shard_map/ppermute | solution.py:211
  27.8 4.8 %collective-permute-start.10 = (f32[64,128]{1,0:T(8,128)S(1)}, f32[64,128]{1,0:T(8,128)S(1)}, u32[]{:S(2)}, u32[]{:S(2)}) collective-permute-start(f32[64,128]{1,0:T(8,128)S(1)} %get-tuple-element.64), channel_id=1, source_target_pairs={{0,2},{1,3},{2,0},{3,1},{4,6},{5,7},{6,4},{7,5},{8,10},{9,11},{10,... | collective-permute-start | bytes 98312 | tf_op jit(solution)/shard_map/ppermute | solution.py:211
  27.8 4.8 %collective-permute-start.11 = (f32[64,128]{1,0:T(8,128)S(1)}, f32[64,128]{1,0:T(8,128)S(1)}, u32[]{:S(2)}, u32[]{:S(2)}) collective-permute-start(f32[64,128]{1,0:T(8,128)S(1)} %get-tuple-element.65), channel_id=1, source_target_pairs={{0,1},{1,0},{2,3},{3,2},{4,5},{5,4},{6,7},{7,6},{8,9},{9,8},{10,11... | collective-permute-start | bytes 98312 | tf_op jit(solution)/shard_map/ppermute | solution.py:211
  37.4 7.6 %collective-permute-start.12 = (bf16[1024,128]{1,0:T(8,128)(2,1)S(1)}, bf16[1024,128]{1,0:T(8,128)(2,1)S(1)}, u32[]{:S(2)}, u32[]{:S(2)}) collective-permute-start(bf16[1024,128]{1,0:T(8,128)(2,1)S(1)} %get-tuple-element.68), channel_id=1, source_target_pairs={{0,4},{1,5},{2,6},{3,7},{4,0},{5,1},{6,2},{7,3},{8,12},{9,13},{10,... | collective-permute-start | bytes 786440 | tf_op jit(solution)/shard_map/ppermute | solution.py:252
  37.9 7.1 %collective-permute-start.13 = (bf16[1024,128]{1,0:T(8,128)(2,1)S(1)}, bf16[1024,128]{1,0:T(8,128)(2,1)S(1)}, u32[]{:S(2)}, u32[]{:S(2)}) collective-permute-start(bf16[1024,128]{1,0:T(8,128)(2,1)S(1)} %get-tuple-element.69), channel_id=1, source_target_pairs={{0,1},{1,0},{2,3},{3,2},{4,5},{5,4},{6,7},{7,6},{8,16},{9,17},{10,... | collective-permute-start | bytes 786440 | tf_op jit(solution)/shard_map/ppermute | solution.py:252
  38.2 6.8 %collective-permute-start.14 = (bf16[1024,128]{1,0:T(8,128)(2,1)S(1)}, bf16[1024,128]{1,0:T(8,128)(2,1)S(1)}, u32[]{:S(2)}, u32[]{:S(2)}) collective-permute-start(bf16[1024,128]{1,0:T(8,128)(2,1)S(1)} %get-tuple-element.70), channel_id=1, source_target_pairs={{0,8},{1,9},{2,10},{3,11},{4,12},{5,13},{6,14},{7,15},{8,0},{9,1},... | collective-permute-start | bytes 786440 | tf_op jit(solution)/shard_map/ppermute | solution.py:252
  39.3 2.6 %collective-permute-start.16 = (bf16[128,128]{1,0:T(8,128)(2,1)S(1)}, bf16[128,128]{1,0:T(8,128)(2,1)S(1)}, u32[]{:S(2)}, u32[]{:S(2)}) collective-permute-start(bf16[128,128]{1,0:T(8,128)(2,1)S(1)} %get-tuple-element.71), channel_id=1, source_target_pairs={{0,8},{1,2},{2,1},{3,11},{4,12},{5,6},{6,5},{7,15},{8,0},{9,10},{1... | collective-permute-start | bytes 98312 | tf_op jit(solution)/shard_map/ppermute | solution.py:252
  39.3 5.7 %collective-permute-start.15 = (bf16[128,128]{1,0:T(8,128)(2,1)S(1)}, bf16[128,128]{1,0:T(8,128)(2,1)S(1)}, u32[]{:S(2)}, u32[]{:S(2)}) collective-permute-start(bf16[128,128]{1,0:T(8,128)(2,1)S(1)} %get-tuple-element.71), channel_id=1, source_target_pairs={{0,1},{1,0},{2,3},{3,2},{4,5},{5,4},{6,7},{7,6},{8,9},{9,8},{10,11... | collective-permute-start | bytes 98312 | tf_op jit(solution)/shard_map/ppermute | solution.py:252
  48.8 8.6 %collective-permute-start.17 = (bf16[1024,128]{1,0:T(8,128)(2,1)S(1)}, bf16[1024,128]{1,0:T(8,128)(2,1)S(1)}, u32[]{:S(2)}, u32[]{:S(2)}) collective-permute-start(bf16[1024,128]{1,0:T(8,128)(2,1)S(1)} %get-tuple-element.73), channel_id=1, source_target_pairs={{0,4},{1,5},{2,6},{3,7},{4,0},{5,1},{6,2},{7,3},{8,12},{9,13},{10,... | collective-permute-start | bytes 786440 | tf_op jit(solution)/shard_map/ppermute | solution.py:252
  50.3 7.1 %collective-permute-start.18 = (bf16[1024,128]{1,0:T(8,128)(2,1)S(1)}, bf16[1024,128]{1,0:T(8,128)(2,1)S(1)}, u32[]{:S(2)}, u32[]{:S(2)}) collective-permute-start(bf16[1024,128]{1,0:T(8,128)(2,1)S(1)} %get-tuple-element.74), channel_id=1, source_target_pairs={{0,1},{1,0},{2,3},{3,2},{4,5},{5,4},{6,7},{7,6},{8,16},{9,17},{10,... | collective-permute-start | bytes 786440 | tf_op jit(solution)/shard_map/ppermute | solution.py:252
  51.1 6.3 %collective-permute-start.19 = (bf16[1024,128]{1,0:T(8,128)(2,1)S(1)}, bf16[1024,128]{1,0:T(8,128)(2,1)S(1)}, u32[]{:S(2)}, u32[]{:S(2)}) collective-permute-start(bf16[1024,128]{1,0:T(8,128)(2,1)S(1)} %get-tuple-element.75), channel_id=1, source_target_pairs={{0,8},{1,9},{2,10},{3,11},{4,12},{5,13},{6,14},{7,15},{8,0},{9,1},... | collective-permute-start | bytes 786440 | tf_op jit(solution)/shard_map/ppermute | solution.py:252
  51.1 1.9 %collective-permute-start.21 = (bf16[128,128]{1,0:T(8,128)(2,1)S(1)}, bf16[128,128]{1,0:T(8,128)(2,1)S(1)}, u32[]{:S(2)}, u32[]{:S(2)}) collective-permute-start(bf16[128,128]{1,0:T(8,128)(2,1)S(1)} %get-tuple-element.76), channel_id=1, source_target_pairs={{0,8},{1,2},{2,1},{3,11},{4,12},{5,6},{6,5},{7,15},{8,0},{9,10},{1... | collective-permute-start | bytes 98312 | tf_op jit(solution)/shard_map/ppermute | solution.py:252
  51.6 5.8 %collective-permute-start.20 = (bf16[128,128]{1,0:T(8,128)(2,1)S(1)}, bf16[128,128]{1,0:T(8,128)(2,1)S(1)}, u32[]{:S(2)}, u32[]{:S(2)}) collective-permute-start(bf16[128,128]{1,0:T(8,128)(2,1)S(1)} %get-tuple-element.76), channel_id=1, source_target_pairs={{0,1},{1,0},{2,3},{3,2},{4,5},{5,4},{6,7},{7,6},{8,9},{9,8},{10,11... | collective-permute-start | bytes 98312 | tf_op jit(solution)/shard_map/ppermute | solution.py:252

commit v11 on v10

--- a/solution.py
+++ b/solution.py
@@ -166,28 +166,30 @@
     )(*parts, held)
 
 
-def share_kernel(peers, mine_ref, other_ref, *refs):
-    *outs, total, turned = refs
+def share_kernel(peers, mine_ref, other_ref, keep_ref, send_ref, total, turned):
     total[...] = mine_ref[...] + other_ref[...]
     turned[...] = total[...].T
     lines, sides = total.shape
+    rows, some = lines // peers, sides // peers
     group = lax.axis_index("gz")
-    for key, out in enumerate(outs):
+    for key in range(peers):
         peer = group ^ key
-        rows, some = lines // peers, sides // peers
-        out[:rows, :] = total[pl.ds(pl.multiple_of(peer * rows, 8), rows), :]
-        out[rows:, :] = turned[pl.ds(pl.multiple_of(peer * some, 8), some), :]
+        out = send_ref if key % 2 else keep_ref
+        base = key // 2 * (rows + some)
+        out[base : base + rows, :] = total[pl.ds(pl.multiple_of(peer * rows, 8), rows), :]
+        base += rows
+        out[base : base + some, :] = turned[pl.ds(pl.multiple_of(peer * some, 8), some), :]
 
 
 def shares(mine, other):
     peers = lax.axis_size("gz")
     lines, sides = mine.shape
-    out = jax.ShapeDtypeStruct(((lines + sides) // peers, sides), F32)
+    out = jax.ShapeDtypeStruct(((lines + sides) // 2, sides), F32)
     return pl.pallas_call(
         functools.partial(share_kernel, peers),
         in_specs=[WHOLE] * 2,
-        out_specs=[WHOLE] * peers,
-        out_shape=[out] * peers,
+        out_specs=[WHOLE] * 2,
+        out_shape=[out] * 2,
         scratch_shapes=[pltpu.VMEM((lines, sides), F32), pltpu.VMEM((sides, lines), F32)],
         compiler_params=params(),
         cost_estimate=pl.CostEstimate(
@@ -196,26 +198,47 @@
     )(mine, other)
 
 
-def flux_sums(parts, held, late, after):
+def halve_kernel(kept_ref, got_ref, keep_ref, send_ref):
+    half = keep_ref.shape[0]
+    keep_ref[...] = kept_ref[:half, :] + got_ref[:half, :]
+    send_ref[...] = kept_ref[half:, :] + got_ref[half:, :]
+
+
+def halve(kept, got):
+    out = jax.ShapeDtypeStruct((kept.shape[0] // 2, kept.shape[1]), F32)
+    return pl.pallas_call(
+        halve_kernel,
+        in_specs=[WHOLE] * 2,
+        out_specs=[WHOLE] * 2,
+        out_shape=[out] * 2,
+        compiler_params=params(),
+        cost_estimate=pl.CostEstimate(
+            flops=kept.size, bytes_accessed=16 * kept.size, transcendentals=0
+        ),
+    )(kept, got)
+
+
+def flux_sums(parts, held, late, swap_z, ends):
     cols, gzs = lax.axis_size("col"), lax.axis_size("gz")
     sides = parts[0].shape[1]
     lines = held.shape[1]
-    if cols == 2 and gzs & (gzs - 1) == 0 and lines // cols == sides and sides // gzs % 8 == 0:
+    if cols == 2 and gzs == 4 and lines // cols == sides and sides // gzs % 8 == 0:
         mine, other = surface(parts, held, 2)
-        mine, other, after = lax.optimization_barrier((mine, other, after))
+        mine, other, late, ends = lax.optimization_barrier((mine, other, late, ends))
         other = lax.ppermute(other, "col", [(0, 1), (1, 0)])
-        other, late = lax.optimization_barrier((other, late))
-        sent = shares(mine, other)
-        recv = [sent[0]]
-        for key in range(gzs - 1, 0, -1):
-            recv.append(lax.ppermute(sent[key], "gz", [(i, i ^ key) for i in range(gzs)]))
-        return recv, after
+        other, tips = lax.optimization_barrier((other, swap_z(ends)))
+        keep, send = shares(mine, other)
+        for bit in (1, 2):
+            got = lax.ppermute(send, "gz", [(i, i ^ bit) for i in range(gzs)])
+            if bit == 1:
+                keep, send = halve(keep, got)
+        return [keep, got], late, tips
     (total,) = surface(parts, held, 1)
     rows = lax.psum_scatter(total, "col", scatter_dimension=0, tiled=True)
     owned = lax.psum_scatter(rows, "gz", scatter_dimension=0, tiled=True)
     flux = lax.psum_scatter(rows.T, "gz", scatter_dimension=0, tiled=True)
     flux = jnp.pad(flux, ((0, 0), (0, sides - flux.shape[1])))
-    return [jnp.concatenate([owned, flux], axis=0)], after
+    return [jnp.concatenate([owned, flux], axis=0)], late, swap_z(ends)
 
 
 def turns(axis):
@@ -639,10 +662,12 @@
     inner, held, tables = firsts[:count], firsts[count], firsts[count + 1 :]
     *inner, ends = inner
     along_col = swap_faces(shape.outer, outer)
-    parts, (inner, along_col) = row_gather(trace, (inner, along_col))
     along_row = swap_faces(shape.inner, inner)
-    recv, ends = flux_sums(parts, held, along_row, ends)
-    halos = along_col + along_row + swap_ends(shape, ends)
+    parts, (_, along_col) = row_gather(trace, (inner, along_col))
+    parts, along_row = lax.optimization_barrier((parts, along_row))
+    swap_z = functools.partial(swap_ends, shape)
+    recv, along_row, tips = flux_sums(parts, held, along_row, swap_z, ends)
+    halos = along_col + along_row + tips
 
     current, *faces, source, surface_flux = sweep(
         shape, field, load, tables, halos, recv=recv, flux_cell=flux_cell

time: 60.8 us -> 64.2 us (1.056)
  waiting for transfers between devices: 15.1 us -> 18.3 us
    ppermute x15, waiting for transfers between devices: 9.34 us -> 11.8 us  [swap(): return lax.ppermute(value, axes, pairs)]
    ppermute x3 -> x2, waiting for transfers between devices: 3.81 us -> 5.15 us  [flux_sums(): got = lax.ppermute(send, 'gz', [(i, i ^ bit) for i in range(gzs)])]
    ppermute x3 -> x2, starting transfers between devices: 4.45 us -> 4.06 us  [flux_sums(): got = lax.ppermute(send, 'gz', [(i, i ^ bit) for i in range(gzs)])]
  transfers between devices with their start and end apart: 22 -> 21, of which waited for: 8 -> 7; matrix products, arithmetic and copies ran while one was open for 0% -> 0% of each run, Pallas kernels for 7% -> 5%
where the time goes in v11:
time: 64.2 us; the launch traced here: 64 us
  starting transfers between devices  23.7 us (37%)
  Pallas kernels  21.1 us (33%)
  waiting for transfers between devices  18.3 us (29%)
  between operations  0.89 us (1%)
    ppermute x15, starting transfers between devices, swap(): return lax.ppermute(value, axes, pairs)  17.1 us
    ppermute x15, waiting for transfers between devices, swap(): return lax.ppermute(value, axes, pairs)  11.8 us
    pallas_call x3, Pallas kernels, sweep(): pl.pallas_call(functools.partial(sweep_kernel, shape, len(recv), last), i...  11.6 us
    pallas_call x1, Pallas kernels, traces(): pl.pallas_call(functools.partial(trace_kernel, shape, stride, block), in_...  5.21 us
    ppermute x2, waiting for transfers between devices, flux_sums(): got = lax.ppermute(send, 'gz', [(i, i ^ bit) for i in range(gzs)])  5.15 us
    ppermute x2, starting transfers between devices, flux_sums(): got = lax.ppermute(send, 'gz', [(i, i ^ bit) for i in range(gzs)])  4.06 us
    pallas_call x1, Pallas kernels, first_faces(): pl.pallas_call(functools.partial(faces_kernel, shape, slots), in_specs=[h...  3.46 us
    ppermute x3, starting transfers between devices, row_gather(): lax.ppermute(held[key], 'row', pairs)  2 us
  transfers between devices with their start and end apart: 21, of which 7 were waited for; matrix products, arithmetic and copies ran while one was open for 0% of the time, Pallas kernels for 5%

profile of v11, /device:TPU:0, one launch (start us, length us, event | category | flops | bytes accessed | tf_op | source)
XLA Modules:
  0.0 64.0 jit_solution(14063469359124014425)
XLA Ops:
  0.6 5.2 %shard_map.78 = (bf16[1024,128]{1,0:T(8,128)(2,1)}, bf16[1024,128]{1,0:T(8,128)(2,1)}) custom-call(bf16[128,64,128]{2,1,0:T(8,128)(2,1)} %bitcast.5, s32[1,1,1,1024]{3,2,1,0:T(1,128)} %cell_ref.1), custom_call_target="tpu_custom_call" | custom-call | flops 536870912 | bytes 2097152 | tf_op jit(solution)/shard_map/pallas_call | solution.py:102
  5.9 3.0 %collective-permute-start.1 = (bf16[1024,128]{1,0:T(8,128)(2,1)}, bf16[1024,128]{1,0:T(8,128)(2,1)S(1)}, u32[]{:S(2)}, u32[]{:S(2)}) collective-permute-start(bf16[1024,128]{1,0:T(8,128)(2,1)} %get-tuple-element.56), channel_id=1, source_target_pairs={{0,4},{1,5},{2,6},{3,7},{4,0},{5,1},{6,2},{7,3},{8,12},{9,13},{10,... | collective-permute-start | bytes 786440 | tf_op jit(solution)/shard_map/ppermute | solution.py:275
  8.9 1.5 %collective-permute-start = (bf16[1024,128]{1,0:T(8,128)(2,1)}, bf16[1024,128]{1,0:T(8,128)(2,1)S(1)}, u32[]{:S(2)}, u32[]{:S(2)}) collective-permute-start(bf16[1024,128]{1,0:T(8,128)(2,1)} %get-tuple-element.60.refs_0_), channel_id=1, source_target_pairs={{0,16},{8,24},{16,0},{24,8},{1,17},{9,25},{17,1},{25,9},{2,18},{10... | collective-permute-start | bytes 786440 | tf_op jit(solution)/shard_map/ppermute | solution.py:639
  10.4 3.5 %shard_map.77 = (bf16[1024,128]{1,0:T(8,128)(2,1)S(1)}, bf16[1024,128]{1,0:T(8,128)(2,1)S(1)}, bf16[128,128]{1,0:T(8,128)(2,1)S(1)}, bf16[4,256,1024]{2,1,0:T(8,...) custom-call(bf16[8192,128]{1,0:T(8,128)(2,1)} %bitcast.6, ...), custom_call_target="tpu_custom_call" | custom-call | flops 134217728 | bytes 4194304 | tf_op jit(solution)/shard_map/pallas_call | solution.py:438
  13.8 0.0 copy-start
  13.8 0.0 copy-start.4
  13.9 1.6 %collective-permute-start.4 = (bf16[1024,128]{1,0:T(8,128)(2,1)S(1)}, bf16[1024,128]{1,0:T(8,128)(2,1)S(1)}, u32[]{:S(2)}, u32[]{:S(2)}) collective-permute-start(bf16[1024,128]{1,0:T(8,128)(2,1)S(1)} %get-tuple-element.54), channel_id=1, source_target_pairs={{0,1},{1,0},{2,3},{3,2},{4,5},{5,4},{6,7},{7,6},{8,16},{9,17},{10,... | collective-permute-start | bytes 786440 | tf_op jit(solution)/shard_map/ppermute | solution.py:275
  15.5 1.3 %collective-permute-done.refs_2_ = bf16[1024,128]{1,0:T(8,128)(2,1)S(1)} collective-permute-done((bf16[1024,128]{1,0:T(8,128)(2,1)}, bf16[1024,128]{1,0:T(8,128)(2,1)S(1)}, u32[]{:S(2)}, u32[]{:S(2)}) %collective-permute-start) | collective-permute-done | bytes 262176 | tf_op jit(solution)/shard_map/ppermute | solution.py:639
  16.9 0.5 collective-permute-start.3
  17.4 2.9 %collective-permute-done.4.refs_8_ = bf16[1024,128]{1,0:T(8,128)(2,1)S(1)} collective-permute-done((bf16[1024,128]{1,0:T(8,128)(2,1)S(1)}, bf16[1024,128]{1,0:T(8,128)(2,1)S(1)}, u32[]{:S(2)}, u32[]{:S(2)}) %collective-permute-start.4) | collective-permute-done | bytes 262176 | tf_op jit(solution)/shard_map/ppermute | solution.py:275
  20.3 0.7 %shard_map.79 = (f32[128,128]{1,0:T(8,128)S(1)}, f32[128,128]{1,0:T(8,128)S(1)}) custom-call(bf16[1024,128]{1,0:T(8,128)(2,1)S(1)} %copy-done.2, bf16[1024,128]{1,0:T(8,128)(2,1)S(1)} %collective-permute-done.2.refs_1_, bf16[1024,128]{1,0:T(8,128)(2,1)S(1)} %collective-permute-done.refs_2_, bf16[1024,128]{1,0:T(8,128)(2,1)S(1)} %collective-permute-done.3.refs_3_, ...), custom_call_target="tpu_custom_call" | custom-call | flops 268435456 | bytes 2097152 | tf_op jit(solution)/shard_map/pallas_call | solution.py:156
  21.0 0.6 collective-permute-start.6
  21.6 3.2 %collective-permute-start.7 = (bf16[128,128]{1,0:T(8,128)(2,1)S(1)}, bf16[128,128]{1,0:T(8,128)(2,1)S(1)}, u32[]{:S(2)}, u32[]{:S(2)}) collective-permute-start(bf16[128,128]{1,0:T(8,128)(2,1)S(1)} %get-tuple-element.73), channel_id=1, source_target_pairs={{0,1},{1,0},{2,3},{3,2},{4,5},{5,4},{6,7},{7,6},{8,9},{9,8},{10,11... | collective-permute-start | bytes 98312 | tf_op jit(solution)/shard_map/ppermute | solution.py:275
  24.8 1.9 %collective-permute-done.7.refs_10_ = bf16[128,128]{1,0:T(8,128)(2,1)S(1)} collective-permute-done((bf16[128,128]{1,0:T(8,128)(2,1)S(1)}, bf16[128,128]{1,0:T(8,128)(2,1)S(1)}, u32[]{:S(2)}, u32[]{:S(2)}) %collective-permute-start.7) | collective-permute-done | bytes 32800 | tf_op jit(solution)/shard_map/ppermute | solution.py:275
  26.7 0.1 shard_map.80
  26.8 2.1 %collective-permute-start.9 = (f32[128,128]{1,0:T(8,128)S(1)}, f32[128,128]{1,0:T(8,128)S(1)}, u32[]{:S(2)}, u32[]{:S(2)}) collective-permute-start(f32[128,128]{1,0:T(8,128)S(1)} %get-tuple-element.79), channel_id=1, source_target_pairs={{0,1},{1,0},{2,3},{3,2},{4,5},{5,4},{6,7},{7,6},{8,9},{9,8},{10,11... | collective-permute-start | bytes 196616 | tf_op jit(solution)/shard_map/ppermute | solution.py:232
  28.9 2.2 %collective-permute-done.9.got_ref = f32[128,128]{1,0:T(8,128)S(1)} collective-permute-done((f32[128,128]{1,0:T(8,128)S(1)}, f32[128,128]{1,0:T(8,128)S(1)}, u32[]{:S(2)}, u32[]{:S(2)}) %collective-permute-start.9) | collective-permute-done | bytes 65568 | tf_op jit(solution)/shard_map/ppermute | solution.py:232
  31.1 2.0 %collective-permute-start.10 = (f32[64,128]{1,0:T(8,128)S(1)}, f32[64,128]{1,0:T(8,128)S(1)}, u32[]{:S(2)}, u32[]{:S(2)}) collective-permute-start(f32[64,128]{1,0:T(8,128)S(1)} %get-tuple-element.81), channel_id=1, source_target_pairs={{0,2},{1,3},{2,0},{3,1},{4,6},{5,7},{6,4},{7,5},{8,10},{9,11},{10,... | collective-permute-start | bytes 98312 | tf_op jit(solution)/shard_map/ppermute | solution.py:232
  33.1 2.9 %collective-permute-done.10.refs_13_ = f32[64,128]{1,0:T(8,128)S(1)} collective-permute-done((f32[64,128]{1,0:T(8,128)S(1)}, f32[64,128]{1,0:T(8,128)S(1)}, u32[]{:S(2)}, u32[]{:S(2)}) %collective-permute-start.10) | collective-permute-done | bytes 32800 | tf_op jit(solution)/shard_map/ppermute | solution.py:232
  36.0 4.7 %shard_map.82 = (bf16[8192,128]{1,0:T(8,128)(2,1)S(1)}, bf16[1024,128]{1,0:T(8,128)(2,1)S(1)}, bf16[1024,128]{1,0:T(8,128)(2,1)S(1)}, bf16[1024,128]{1,0:T(8,128...) custom-call(bf16[8192,128]{1,0:T(8,128)(2,1)S(1)} %bitcast.7, ...), custom_call_target="tpu_custom_call" | custom-call | flops 805306368 | bytes 8388608 | tf_op jit(solution)/shard_map/pallas_call | solution.py:607
  40.8 1.5 %collective-permute-start.11 = (bf16[1024,128]{1,0:T(8,128)(2,1)S(1)}, bf16[1024,128]{1,0:T(8,128)(2,1)S(1)}, u32[]{:S(2)}, u32[]{:S(2)}) collective-permute-start(bf16[1024,128]{1,0:T(8,128)(2,1)S(1)} %get-tuple-element.84), channel_id=1, source_target_pairs={{0,4},{1,5},{2,6},{3,7},{4,0},{5,1},{6,2},{7,3},{8,12},{9,13},{10,... | collective-permute-start | bytes 786440 | tf_op jit(solution)/shard_map/ppermute | solution.py:275
  42.2 2.0 %collective-permute-start.12 = (bf16[1024,128]{1,0:T(8,128)(2,1)S(1)}, bf16[1024,128]{1,0:T(8,128)(2,1)S(1)}, u32[]{:S(2)}, u32[]{:S(2)}) collective-permute-start(bf16[1024,128]{1,0:T(8,128)(2,1)S(1)} %get-tuple-element.85), channel_id=1, source_target_pairs={{0,1},{1,0},{2,3},{3,2},{4,5},{5,4},{6,7},{7,6},{8,16},{9,17},{10,... | collective-permute-start | bytes 786440 | tf_op jit(solution)/shard_map/ppermute | solution.py:275
  44.3 0.5 collective-permute-start.15
  44.8 1.1 %collective-permute-start.14 = (bf16[128,128]{1,0:T(8,128)(2,1)S(1)}, bf16[128,128]{1,0:T(8,128)(2,1)S(1)}, u32[]{:S(2)}, u32[]{:S(2)}) collective-permute-start(bf16[128,128]{1,0:T(8,128)(2,1)S(1)} %get-tuple-element.87), channel_id=1, source_target_pairs={{0,1},{1,0},{2,3},{3,2},{4,5},{5,4},{6,7},{7,6},{8,9},{9,8},{10,11... | collective-permute-start | bytes 98312 | tf_op jit(solution)/shard_map/ppermute | solution.py:275
  45.9 3.5 %collective-permute-done.14.refs_10_ = bf16[128,128]{1,0:T(8,128)(2,1)S(1)} collective-permute-done((bf16[128,128]{1,0:T(8,128)(2,1)S(1)}, bf16[128,128]{1,0:T(8,128)(2,1)S(1)}, u32[]{:S(2)}, u32[]{:S(2)}) %collective-permute-start.14) | collective-permute-done | bytes 32800 | tf_op jit(solution)/shard_map/ppermute | solution.py:275
  49.3 3.8 %shard_map.83 = (bf16[8192,128]{1,0:T(8,128)(2,1)S(1)}, bf16[1024,128]{1,0:T(8,128)(2,1)S(1)}, bf16[1024,128]{1,0:T(8,128)(2,1)S(1)}, bf16[1024,128]{1,0:T(8,128)(2,1)S(1)}, bf16[128,128]{1,0:T(8,128)(2,1)S(1)}) custom-call(bf16[8192,128]{1,0:T(8,128)(2,1)S(1)} %get-tuple-element.82.refs_0_, bf16[8192,128]{1,0:T(8,128)(2,1)S(1)} %get-tuple-element.83.refs_1_, ...), custom_call_target="tpu_custom_call" | custom-call | flops 805306368 | bytes 8388608 | tf_op jit(solution)/shard_map/pallas_call | solution.py:607
  53.1 0.6 collective-permute-start.16
  53.7 2.0 %collective-permute-start.17 = (bf16[1024,128]{1,0:T(8,128)(2,1)S(1)}, bf16[1024,128]{1,0:T(8,128)(2,1)S(1)}, u32[]{:S(2)}, u32[]{:S(2)}) collective-permute-start(bf16[1024,128]{1,0:T(8,128)(2,1)S(1)} %get-tuple-element.90), channel_id=1, source_target_pairs={{0,1},{1,0},{2,3},{3,2},{4,5},{5,4},{6,7},{7,6},{8,16},{9,17},{10,... | collective-permute-start | bytes 786440 | tf_op jit(solution)/shard_map/ppermute | solution.py:275
  55.7 0.5 collective-permute-start.20
  56.2 1.1 %collective-permute-start.19 = (bf16[128,128]{1,0:T(8,128)(2,1)S(1)}, bf16[128,128]{1,0:T(8,128)(2,1)S(1)}, u32[]{:S(2)}, u32[]{:S(2)}) collective-permute-start(bf16[128,128]{1,0:T(8,128)(2,1)S(1)} %get-tuple-element.92), channel_id=1, source_target_pairs={{0,1},{1,0},{2,3},{3,2},{4,5},{5,4},{6,7},{7,6},{8,9},{9,8},{10,11... | collective-permute-start | bytes 98312 | tf_op jit(solution)/shard_map/ppermute | solution.py:275
  57.3 3.5 %collective-permute-done.19.refs_10_ = bf16[128,128]{1,0:T(8,128)(2,1)S(1)} collective-permute-done((bf16[128,128]{1,0:T(8,128)(2,1)S(1)}, bf16[128,128]{1,0:T(8,128)(2,1)S(1)}, u32[]{:S(2)}, u32[]{:S(2)}) %collective-permute-start.19) | collective-permute-done | bytes 32800 | tf_op jit(solution)/shard_map/ppermute | solution.py:275
  60.8 3.1 %shard_map.84 = bf16[8192,128]{1,0:T(8,128)(2,1)} custom-call(bf16[8192,128]{1,0:T(8,128)(2,1)S(1)} %get-tuple-element.88.refs_0_, bf16[8192,128]{1,0:T(8,128)(2,1)S(1)} %get-tuple-element.83.refs_1_, f32[128,128]{1,0:T(8,128)S(1)} %get-tuple-element.48.refs_2_, bf16[128,176]{1,0:T(8,128)(2,1)S(1)} %get-tuple-element.49.refs_3_, ...), custom_call_target="tpu_custom_call" | custom-call | flops 805306368 | bytes 8388608 | tf_op jit(solution)/shard_map/pallas_call | solution.py:607
  (28 shorter events, 0.1 us)
Async XLA Ops:
  0.6 9.7 %copy-start.3 = (f32[8,8,128]{2,1,0:T(8,128)S(1)}, f32[8,8,128]{2,1,0:T(8,128)}, u32[]{:S(2)}) copy-start(f32[8,8,128]{2,1,0:T(8,128)} %param.8) | copy-start | bytes 98308
  5.9 9.6 %collective-permute-start.1 = (bf16[1024,128]{1,0:T(8,128)(2,1)}, bf16[1024,128]{1,0:T(8,128)(2,1)S(1)}, u32[]{:S(2)}, u32[]{:S(2)}) collective-permute-start(bf16[1024,128]{1,0:T(8,128)(2,1)} %get-tuple-element.56), channel_id=1, source_target_pairs={{0,4},{1,5},{2,6},{3,7},{4,0},{5,1},{6,2},{7,3},{8,12},{9,13},{10,... | collective-permute-start | bytes 786440 | tf_op jit(solution)/shard_map/ppermute | solution.py:275
  8.9 8.0 %collective-permute-start = (bf16[1024,128]{1,0:T(8,128)(2,1)}, bf16[1024,128]{1,0:T(8,128)(2,1)S(1)}, u32[]{:S(2)}, u32[]{:S(2)}) collective-permute-start(bf16[1024,128]{1,0:T(8,128)(2,1)} %get-tuple-element.60.refs_0_), channel_id=1, source_target_pairs={{0,16},{8,24},{16,0},{24,8},{1,17},{9,25},{17,1},{25,9},{2,18},{10... | collective-permute-start | bytes 786440 | tf_op jit(solution)/shard_map/ppermute | solution.py:639
  10.4 6.5 %copy-start.2 = (bf16[1024,128]{1,0:T(8,128)(2,1)S(1)}, bf16[1024,128]{1,0:T(8,128)(2,1)}, u32[]{:S(2)}) copy-start(bf16[1024,128]{1,0:T(8,128)(2,1)} %get-tuple-element.60.refs_0_) | copy-start | bytes 786436
  10.4 25.6 %copy-start.1 = (bf16[128,8,8,128]{3,2,1,0:T(8,128)(2,1)S(1)}, bf16[128,8,8,128]{3,2,1,0:T(8,128)(2,1)}, u32[]{:S(2)}) copy-start(bf16[128,8,8,128]{3,2,1,0:T(8,128)(2,1)} %param.7) | copy-start | bytes 6291460
  13.8 22.2 %copy-start = (bf16[128,8,8,128]{3,2,1,0:T(8,128)(2,1)S(1)}, bf16[128,8,8,128]{3,2,1,0:T(8,128)(2,1)}, u32[]{:S(2)}) copy-start(bf16[128,8,8,128]{3,2,1,0:T(8,128)(2,1)} %param.6) | copy-start | bytes 6291460
  13.8 22.2 %copy-start.4 = (s32[1,1,1,32]{3,2,1,0:T(1,128)S(1)}, s32[1,1,1,32]{3,2,1,0:T(1,128)}, u32[]{:S(2)}) copy-start(s32[1,1,1,32]{3,2,1,0:T(1,128)} %refs_14_.1) | copy-start | bytes 388
  13.9 6.4 %collective-permute-start.4 = (bf16[1024,128]{1,0:T(8,128)(2,1)S(1)}, bf16[1024,128]{1,0:T(8,128)(2,1)S(1)}, u32[]{:S(2)}, u32[]{:S(2)}) collective-permute-start(bf16[1024,128]{1,0:T(8,128)(2,1)S(1)} %get-tuple-element.54), channel_id=1, source_target_pairs={{0,1},{1,0},{2,3},{3,2},{4,5},{5,4},{6,7},{7,6},{8,16},{9,17},{10,... | collective-permute-start | bytes 786440 | tf_op jit(solution)/shard_map/ppermute | solution.py:275
  15.5 4.8 %collective-permute-start.5 = (bf16[1024,128]{1,0:T(8,128)(2,1)S(1)}, bf16[1024,128]{1,0:T(8,128)(2,1)S(1)}, u32[]{:S(2)}, u32[]{:S(2)}) collective-permute-start(bf16[1024,128]{1,0:T(8,128)(2,1)S(1)} %get-tuple-element.55), channel_id=1, source_target_pairs={{0,8},{1,9},{2,10},{3,11},{4,12},{5,13},{6,14},{7,15},{8,0},{9,1},... | collective-permute-start | bytes 786440 | tf_op jit(solution)/shard_map/ppermute | solution.py:275
  16.9 3.5 %collective-permute-start.2 = (bf16[1024,128]{1,0:T(8,128)(2,1)S(1)}, bf16[1024,128]{1,0:T(8,128)(2,1)S(1)}, u32[]{:S(2)}, u32[]{:S(2)}) collective-permute-start(bf16[1024,128]{1,0:T(8,128)(2,1)S(1)} %copy-done.2), channel_id=1, source_target_pairs={{0,8},{8,0},{16,24},{24,16},{1,9},{9,1},{17,25},{25,17},{2,10},{10... | collective-permute-start | bytes 786440 | tf_op jit(solution)/shard_map/ppermute | solution.py:639
  16.9 3.5 %collective-permute-start.3 = (bf16[1024,128]{1,0:T(8,128)(2,1)S(1)}, bf16[1024,128]{1,0:T(8,128)(2,1)S(1)}, u32[]{:S(2)}, u32[]{:S(2)}) collective-permute-start(bf16[1024,128]{1,0:T(8,128)(2,1)S(1)} %collective-permute-done.refs_2_), channel_id=1, source_target_pairs={{0,8},{8,0},{16,24},{24,16},{1,9},{9,1},{17,25},{25,17},{2,10},{10... | collective-permute-start | bytes 786440 | tf_op jit(solution)/shard_map/ppermute | solution.py:639
  21.0 5.6 %collective-permute-start.6 = (f32[128,128]{1,0:T(8,128)S(1)}, f32[128,128]{1,0:T(8,128)S(1)}, u32[]{:S(2)}, u32[]{:S(2)}) collective-permute-start(f32[128,128]{1,0:T(8,128)S(1)} %get-tuple-element.72), channel_id=1, source_target_pairs={{0,4},{4,0},{1,5},{5,1},{2,6},{6,2},{3,7},{7,3},{8,12},{12,8},{9,1... | collective-permute-start | bytes 196616 | tf_op jit(solution)/shard_map/ppermute | solution.py:228
  21.6 3.2 %collective-permute-start.8 = (bf16[128,128]{1,0:T(8,128)(2,1)S(1)}, bf16[128,128]{1,0:T(8,128)(2,1)S(1)}, u32[]{:S(2)}, u32[]{:S(2)}) collective-permute-start(bf16[128,128]{1,0:T(8,128)(2,1)S(1)} %get-tuple-element.73), channel_id=1, source_target_pairs={{0,8},{1,2},{2,1},{3,11},{4,12},{5,6},{6,5},{7,15},{8,0},{9,10},{1... | collective-permute-start | bytes 98312 | tf_op jit(solution)/shard_map/ppermute | solution.py:275
  21.6 5.0 %collective-permute-start.7 = (bf16[128,128]{1,0:T(8,128)(2,1)S(1)}, bf16[128,128]{1,0:T(8,128)(2,1)S(1)}, u32[]{:S(2)}, u32[]{:S(2)}) collective-permute-start(bf16[128,128]{1,0:T(8,128)(2,1)S(1)} %get-tuple-element.73), channel_id=1, source_target_pairs={{0,1},{1,0},{2,3},{3,2},{4,5},{5,4},{6,7},{7,6},{8,9},{9,8},{10,11... | collective-permute-start | bytes 98312 | tf_op jit(solution)/shard_map/ppermute | solution.py:275
  26.8 4.3 %collective-permute-start.9 = (f32[128,128]{1,0:T(8,128)S(1)}, f32[128,128]{1,0:T(8,128)S(1)}, u32[]{:S(2)}, u32[]{:S(2)}) collective-permute-start(f32[128,128]{1,0:T(8,128)S(1)} %get-tuple-element.79), channel_id=1, source_target_pairs={{0,1},{1,0},{2,3},{3,2},{4,5},{5,4},{6,7},{7,6},{8,9},{9,8},{10,11... | collective-permute-start | bytes 196616 | tf_op jit(solution)/shard_map/ppermute | solution.py:232
  31.1 4.9 %collective-permute-start.10 = (f32[64,128]{1,0:T(8,128)S(1)}, f32[64,128]{1,0:T(8,128)S(1)}, u32[]{:S(2)}, u32[]{:S(2)}) collective-permute-start(f32[64,128]{1,0:T(8,128)S(1)} %get-tuple-element.81), channel_id=1, source_target_pairs={{0,2},{1,3},{2,0},{3,1},{4,6},{5,7},{6,4},{7,5},{8,10},{9,11},{10,... | collective-permute-start | bytes 98312 | tf_op jit(solution)/shard_map/ppermute | solution.py:232
  40.8 8.6 %collective-permute-start.11 = (bf16[1024,128]{1,0:T(8,128)(2,1)S(1)}, bf16[1024,128]{1,0:T(8,128)(2,1)S(1)}, u32[]{:S(2)}, u32[]{:S(2)}) collective-permute-start(bf16[1024,128]{1,0:T(8,128)(2,1)S(1)} %get-tuple-element.84), channel_id=1, source_target_pairs={{0,4},{1,5},{2,6},{3,7},{4,0},{5,1},{6,2},{7,3},{8,12},{9,13},{10,... | collective-permute-start | bytes 786440 | tf_op jit(solution)/shard_map/ppermute | solution.py:275
  42.2 7.1 %collective-permute-start.12 = (bf16[1024,128]{1,0:T(8,128)(2,1)S(1)}, bf16[1024,128]{1,0:T(8,128)(2,1)S(1)}, u32[]{:S(2)}, u32[]{:S(2)}) collective-permute-start(bf16[1024,128]{1,0:T(8,128)(2,1)S(1)} %get-tuple-element.85), channel_id=1, source_target_pairs={{0,1},{1,0},{2,3},{3,2},{4,5},{5,4},{6,7},{7,6},{8,16},{9,17},{10,... | collective-permute-start | bytes 786440 | tf_op jit(solution)/shard_map/ppermute | solution.py:275
  44.3 5.1 %collective-permute-start.13 = (bf16[1024,128]{1,0:T(8,128)(2,1)S(1)}, bf16[1024,128]{1,0:T(8,128)(2,1)S(1)}, u32[]{:S(2)}, u32[]{:S(2)}) collective-permute-start(bf16[1024,128]{1,0:T(8,128)(2,1)S(1)} %get-tuple-element.86), channel_id=1, source_target_pairs={{0,8},{1,9},{2,10},{3,11},{4,12},{5,13},{6,14},{7,15},{8,0},{9,1},... | collective-permute-start | bytes 786440 | tf_op jit(solution)/shard_map/ppermute | solution.py:275
  44.3 1.6 %collective-permute-start.15 = (bf16[128,128]{1,0:T(8,128)(2,1)S(1)}, bf16[128,128]{1,0:T(8,128)(2,1)S(1)}, u32[]{:S(2)}, u32[]{:S(2)}) collective-permute-start(bf16[128,128]{1,0:T(8,128)(2,1)S(1)} %get-tuple-element.87), channel_id=1, source_target_pairs={{0,8},{1,2},{2,1},{3,11},{4,12},{5,6},{6,5},{7,15},{8,0},{9,10},{1... | collective-permute-start | bytes 98312 | tf_op jit(solution)/shard_map/ppermute | solution.py:275
  44.8 4.5 %collective-permute-start.14 = (bf16[128,128]{1,0:T(8,128)(2,1)S(1)}, bf16[128,128]{1,0:T(8,128)(2,1)S(1)}, u32[]{:S(2)}, u32[]{:S(2)}) collective-permute-start(bf16[128,128]{1,0:T(8,128)(2,1)S(1)} %get-tuple-element.87), channel_id=1, source_target_pairs={{0,1},{1,0},{2,3},{3,2},{4,5},{5,4},{6,7},{7,6},{8,9},{9,8},{10,11... | collective-permute-start | bytes 98312 | tf_op jit(solution)/shard_map/ppermute | solution.py:275
  53.1 7.6 %collective-permute-start.16 = (bf16[1024,128]{1,0:T(8,128)(2,1)S(1)}, bf16[1024,128]{1,0:T(8,128)(2,1)S(1)}, u32[]{:S(2)}, u32[]{:S(2)}) collective-permute-start(bf16[1024,128]{1,0:T(8,128)(2,1)S(1)} %get-tuple-element.89), channel_id=1, source_target_pairs={{0,4},{1,5},{2,6},{3,7},{4,0},{5,1},{6,2},{7,3},{8,12},{9,13},{10,... | collective-permute-start | bytes 786440 | tf_op jit(solution)/shard_map/ppermute | solution.py:275
  53.7 7.1 %collective-permute-start.17 = (bf16[1024,128]{1,0:T(8,128)(2,1)S(1)}, bf16[1024,128]{1,0:T(8,128)(2,1)S(1)}, u32[]{:S(2)}, u32[]{:S(2)}) collective-permute-start(bf16[1024,128]{1,0:T(8,128)(2,1)S(1)} %get-tuple-element.90), channel_id=1, source_target_pairs={{0,1},{1,0},{2,3},{3,2},{4,5},{5,4},{6,7},{7,6},{8,16},{9,17},{10,... | collective-permute-start | bytes 786440 | tf_op jit(solution)/shard_map/ppermute | solution.py:275
  55.7 5.1 %collective-permute-start.18 = (bf16[1024,128]{1,0:T(8,128)(2,1)S(1)}, bf16[1024,128]{1,0:T(8,128)(2,1)S(1)}, u32[]{:S(2)}, u32[]{:S(2)}) collective-permute-start(bf16[1024,128]{1,0:T(8,128)(2,1)S(1)} %get-tuple-element.91), channel_id=1, source_target_pairs={{0,8},{1,9},{2,10},{3,11},{4,12},{5,13},{6,14},{7,15},{8,0},{9,1},... | collective-permute-start | bytes 786440 | tf_op jit(solution)/shard_map/ppermute | solution.py:275
  55.7 1.6 %collective-permute-start.20 = (bf16[128,128]{1,0:T(8,128)(2,1)S(1)}, bf16[128,128]{1,0:T(8,128)(2,1)S(1)}, u32[]{:S(2)}, u32[]{:S(2)}) collective-permute-start(bf16[128,128]{1,0:T(8,128)(2,1)S(1)} %get-tuple-element.92), channel_id=1, source_target_pairs={{0,8},{1,2},{2,1},{3,11},{4,12},{5,6},{6,5},{7,15},{8,0},{9,10},{1... | collective-permute-start | bytes 98312 | tf_op jit(solution)/shard_map/ppermute | solution.py:275
  56.2 4.5 %collective-permute-start.19 = (bf16[128,128]{1,0:T(8,128)(2,1)S(1)}, bf16[128,128]{1,0:T(8,128)(2,1)S(1)}, u32[]{:S(2)}, u32[]{:S(2)}) collective-permute-start(bf16[128,128]{1,0:T(8,128)(2,1)S(1)} %get-tuple-element.92), channel_id=1, source_target_pairs={{0,1},{1,0},{2,3},{3,2},{4,5},{5,4},{6,7},{7,6},{8,9},{9,8},{10,11... | collective-permute-start | bytes 98312 | tf_op jit(solution)/shard_map/ppermute | solution.py:275

commit v12 on v10

--- a/solution.py
+++ b/solution.py
@@ -430,16 +430,53 @@
     )(field, block, coef)
 
 
-def sweep_kernel(shape, recvs, last, *refs):
+def base_kernel(shape, field_ref, load_ref, weight, near_m, line_m, base_ref, lines):
+    cells, lanes = shape.cells, shape.lanes
+    weights = weight[...]
+    for step in range(shape.sides // shape.block):
+        at = step * shape.block * cells
+        values = field_ref[at : at + shape.block * cells, :]
+        lines[step] = dot(beside(values), line_m[: 2 * lanes, :])
+        for index in range(shape.half // shape.chunk):
+            offset = index * shape.rows
+            spans = [
+                slice(at + start, at + start + shape.rows)
+                for start in (offset, offset + shape.half_rows)
+            ]
+            stack = jnp.concatenate([field_ref[span, :] for span in spans], axis=1)
+            near = dot(near_m[:, : shape.rows], stack) + lines[step, offset : offset + shape.rows, :]
+            for part, span in enumerate(spans):
+                source = load_ref[span, :].astype(F32)
+                centre = field_ref[span, :].astype(F32)
+                near_part = near[:, part * lanes : (part + 1) * lanes]
+                base_ref[span, :] = (1.0 - OMEGA) * centre + weights * (source + near_part)
+
+
+def sweep_base(shape, field, load, tables):
+    steps = shape.sides // shape.block
+    return pl.pallas_call(
+        functools.partial(base_kernel, shape),
+        in_specs=[WHOLE] * 5,
+        out_specs=WHOLE,
+        out_shape=jax.ShapeDtypeStruct(field.shape, F32),
+        scratch_shapes=[pltpu.VMEM((steps, shape.half_rows, 2 * shape.lanes), F32)],
+        compiler_params=params(),
+        cost_estimate=pl.CostEstimate(
+            flops=6 * field.size * 128, bytes_accessed=8 * field.size, transcendentals=0
+        ),
+    )(field, load, *tables[:3])
+
+
+def finish_kernel(shape, recvs, last, *refs):
     with_flux = recvs > 0
     refs = list(refs)
     take = lambda count: [refs.pop(0) for _ in range(count)]
-    field_ref, load_ref, weight, near_m, line_m, ends_m, rsum = take(7)
+    base_ref, weight, near_m, line_m, ends_m, rsum = take(6)
     halo_refs = take(len(shape.faces))
     end_refs = take(shape.ends)
     if with_flux:
+        load_ref, cell_ref = take(2)
         recv_refs = take(recvs)
-        (cell_ref,) = take(1)
     (out_ref,) = take(1)
     if not last:
         face_refs = take(len(shape.faces))
@@ -469,62 +506,52 @@
         phi[...] = both.T
         cell = jnp.concatenate([cell_ref[0, 0]] * 2, axis=1)
         cell_m[...] = twice((iota((lanes, 2 * slots), 0) == cell % lanes).astype(F32)).astype(BF)
+        cell_mask = iota((cells, 2 * slots), 0) == cell // lanes
 
     mask = z_mask(shape, 1)
     even = lax.axis_index("gz") % 2 == 0
     filled = (iota((shape.block, 2 * cells), 1) < cells) == even
-    if with_flux:
-        slots = cell_ref.shape[3]
-        cell = jnp.concatenate([cell_ref[0, 0]] * 2, axis=1)
-        cell_mask = iota((cells, 2 * slots), 0) == cell // lanes
     weights = weight[...]
 
-    def expand(lines, where, first):
+    def expand(lines, where):
         rows = []
-        for side in range(first, first + shape.half):
+        for side in range(shape.block):
             line = jnp.broadcast_to(lines[side : side + 1], where.shape)
             rows.append(jnp.where(where, line, 0.0))
-        return jnp.concatenate(rows, axis=0).astype(BF)
+        return beside(jnp.concatenate(rows, axis=0).astype(BF))
 
     def work(step):
         at = step * shape.block
-        sides = pl.ds(aligned(at, shape.block), shape.block)
-        size = shape.block * cells
+        sides = slice(at, at + shape.block)
         zs = 0.0
         for turn in range(shape.ends):
             wanted = (filled == (turn == 0)) & has_neighbour("gz", turn)
             zs = jnp.where(wanted, end_refs[turn][sides, :].astype(F32), zs)
-        values = field_ref[pl.ds(aligned(at * cells, size), size), :]
-        left = [beside(values), expand(zs, mask, 0), expand(zs, mask, shape.half)]
-        lines[step] = dot(jnp.concatenate(left, axis=1), line_m[...])
+        lines[step] = dot(expand(zs, mask), line_m[2 * lanes :, :])
         if with_flux:
-            phis = phi[sides, :]
-            left = [expand(phis, cell_mask, 0), expand(phis, cell_mask, shape.half)]
-            placed[step] = dot_nt(jnp.concatenate(left, axis=1), cell_m[...])
+            placed[step] = dot_nt(expand(phi[sides, :], cell_mask), cell_m[...])
         for index in range(shape.half // shape.chunk):
             offset = index * shape.rows
             starts = (offset, offset + shape.half_rows)
             stacks = []
             for start in starts:
-                rows = pl.ds(aligned(at * cells + start, shape.rows), shape.rows)
-                stack = [field_ref[rows, :]]
+                stack = []
                 for face, ref in zip(shape.faces, halo_refs):
                     length = shape.face_len(face)
-                    count = shape.chunk * length
-                    first = aligned(at * length + start // cells * length, count)
-                    stack.append(ref[pl.ds(first, count), :])
+                    first = at * length + start // cells * length
+                    stack.append(ref[first : first + shape.chunk * length, :])
                 stacks.append(jnp.concatenate(stack, axis=0))
-            near = dot(near_m[...], jnp.concatenate(stacks, axis=1))
+            near = dot(near_m[:, shape.rows :], jnp.concatenate(stacks, axis=1))
             near = near + lines[step, offset : offset + shape.rows, :]
+            if with_flux:
+                near = near + placed[step, offset : offset + shape.rows, :]
             for part, start in enumerate(starts):
                 cols = slice(part * lanes, (part + 1) * lanes)
-                rows = pl.ds(aligned(at * cells + start, shape.rows), shape.rows)
-                source = load_ref[rows, :].astype(F32)
+                rows = slice(at * cells + start, at * cells + start + shape.rows)
                 if with_flux:
-                    source = source + placed[step, offset : offset + shape.rows, cols]
-                    source_ref[rows, :] = source.astype(BF)
-                centre = field_ref[rows, :].astype(F32)
-                fresh = (1.0 - OMEGA) * centre + weights * (source + near[:, cols])
+                    flux = placed[step, offset : offset + shape.rows, cols]
+                    source_ref[rows, :] = (load_ref[rows, :].astype(F32) + flux).astype(BF)
+                fresh = base_ref[rows, :] + weights * near[:, cols]
                 out_ref[rows, :] = fresh.astype(BF)
                 if not last:
                     tall[step, start : start + shape.rows, :] = fresh
@@ -553,24 +580,24 @@
         emit(steps - 1)
 
 
-def sweep(shape, field, load, tables, halos, recv=(), flux_cell=None, last=False):
+def sweep_finish(shape, base, tables, halos, load=None, flux_cell=None, recv=(), last=False):
     lanes, cells = shape.lanes, shape.cells
     steps = shape.sides // shape.block
     half = (steps, shape.half_rows, 2 * lanes)
-    operands = [field, load, *tables, *halos, *recv]
-    out_shapes = [jax.ShapeDtypeStruct(field.shape, BF)]
+    operands = [base, *tables, *halos]
+    out_shapes = [jax.ShapeDtypeStruct(base.shape, BF)]
     scratch = [pltpu.VMEM(half, F32)]
     if last:
-        scratch += [pltpu.VMEM(field.shape, BF), pltpu.SemaphoreType.DMA((steps,))]
+        scratch += [pltpu.VMEM(base.shape, BF), pltpu.SemaphoreType.DMA((steps,))]
     else:
         out_shapes += face_shapes(shape, shape.faces)
         out_shapes.append(jax.ShapeDtypeStruct((shape.sides, 2 * cells), BF))
         scratch.append(pltpu.VMEM((steps, shape.block * cells, lanes), F32))
     if recv:
         slots = flux_cell.shape[3]
-        operands.append(flux_cell)
+        operands += [load, flux_cell, *recv]
         out_shapes += [
-            jax.ShapeDtypeStruct(field.shape, BF),
+            jax.ShapeDtypeStruct(base.shape, BF),
             jax.ShapeDtypeStruct((recv[0].shape[0] - slots, slots * lax.axis_size("gz")), F32),
         ]
         scratch += [
@@ -582,14 +609,14 @@
     if last:
         out_specs = [pl.BlockSpec(memory_space=pltpu.HBM)]
     return pl.pallas_call(
-        functools.partial(sweep_kernel, shape, len(recv), last),
+        functools.partial(finish_kernel, shape, len(recv), last),
         in_specs=[WHOLE] * len(operands),
         out_specs=out_specs,
         out_shape=out_shapes,
         scratch_shapes=scratch,
         compiler_params=params(),
         cost_estimate=pl.CostEstimate(
-            flops=6 * field.size * 128, bytes_accessed=8 * field.size, transcendentals=0
+            flops=4 * base.size * 128, bytes_accessed=8 * base.size, transcendentals=0
         ),
     )(*operands)
 
@@ -644,11 +671,14 @@
     recv, ends = flux_sums(parts, held, along_row, ends)
     halos = along_col + along_row + swap_ends(shape, ends)
 
-    current, *faces, source, surface_flux = sweep(
-        shape, field, load, tables, halos, recv=recv, flux_cell=flux_cell
+    base = sweep_base(shape, field, load, tables)
+    current, *faces, source, surface_flux = sweep_finish(
+        shape, base, tables, halos, load=load, flux_cell=flux_cell, recv=recv
     )
-    current, *faces = sweep(shape, current, source, tables, exchange(shape, faces))
-    (current,) = sweep(shape, current, source, tables, exchange(shape, faces), last=True)
+    for last in (False, True):
+        halos = exchange(shape, faces)
+        base = sweep_base(shape, current, source, tables)
+        current, *faces = sweep_finish(shape, base, tables, halos, last=last)
     return current.reshape(volume_field.shape), surface_flux
 
 

time: 60.8 us -> 58.2 us (0.957)
  waiting for transfers between devices: 15.1 us -> 10.4 us
  Pallas kernels: 21.2 us -> 23.2 us
    ppermute x15, waiting for transfers between devices: 9.34 us -> 6.12 us  [swap(): return lax.ppermute(value, axes, pairs)]
    pallas_call x3 -> x6, Pallas kernels: 11.7 us -> 13.7 us  [the longest x3 9.09 us: sweep_finish(): pl.pallas_call(functools.partial(finish_kernel, shape, len(recv), last),...]
    ppermute x3, waiting for transfers between devices: 3.81 us -> 2.34 us  [flux_sums(): lax.ppermute(sent[key], 'gz', [(i, i ^ key) for i in range(gzs)])]
  transfers between devices with their start and end apart: 22 -> 22, of which waited for: 8 -> 8; matrix products, arithmetic and copies ran while one was open for 0% -> 0% of each run, Pallas kernels for 7% -> 15%
where the time goes in v12:
time: 58.2 us; the launch traced here: 58.1 us
  starting transfers between devices  23.5 us (40%)
  Pallas kernels  23.2 us (40%)
  waiting for transfers between devices  10.4 us (18%)
  between operations  0.92 us (2%)
    ppermute x15, starting transfers between devices, swap(): return lax.ppermute(value, axes, pairs)  16.5 us
    pallas_call x3, Pallas kernels, sweep_finish(): pl.pallas_call(functools.partial(finish_kernel, shape, len(recv), last),...  9.09 us
    ppermute x15, waiting for transfers between devices, swap(): return lax.ppermute(value, axes, pairs)  6.12 us
    pallas_call x1, Pallas kernels, traces(): pl.pallas_call(functools.partial(trace_kernel, shape, stride, block), in_...  5.21 us
    pallas_call x3, Pallas kernels, sweep_base(): pl.pallas_call(functools.partial(base_kernel, shape), in_specs=[WHOLE] *...  4.64 us
    ppermute x3, starting transfers between devices, flux_sums(): lax.ppermute(sent[key], 'gz', [(i, i ^ key) for i in range(gzs)])  4.45 us
    pallas_call x1, Pallas kernels, first_faces(): pl.pallas_call(functools.partial(faces_kernel, shape, slots), in_specs=[h...  3.46 us
    ppermute x3, waiting for transfers between devices, flux_sums(): lax.ppermute(sent[key], 'gz', [(i, i ^ key) for i in range(gzs)])  2.34 us
  transfers between devices with their start and end apart: 22, of which 8 were waited for; matrix products, arithmetic and copies ran while one was open for 0% of the time, Pallas kernels for 15%

profile of v12, /device:TPU:0, one launch (start us, length us, event | category | flops | bytes accessed | tf_op | source)
XLA Modules:
  0.0 58.1 jit_solution(8605879314468690947)
XLA Ops:
  0.6 5.2 %shard_map.79 = (bf16[1024,128]{1,0:T(8,128)(2,1)}, bf16[1024,128]{1,0:T(8,128)(2,1)}) custom-call(bf16[128,64,128]{2,1,0:T(8,128)(2,1)} %bitcast.5, s32[1,1,1,1024]{3,2,1,0:T(1,128)} %cell_ref.1), custom_call_target="tpu_custom_call" | custom-call | flops 536870912 | bytes 2097152 | tf_op jit(solution)/shard_map/pallas_call | solution.py:102
  5.9 3.0 %collective-permute-start.1 = (bf16[1024,128]{1,0:T(8,128)(2,1)}, bf16[1024,128]{1,0:T(8,128)(2,1)S(1)}, u32[]{:S(2)}, u32[]{:S(2)}) collective-permute-start(bf16[1024,128]{1,0:T(8,128)(2,1)} %get-tuple-element.48), channel_id=1, source_target_pairs={{0,4},{1,5},{2,6},{3,7},{4,0},{5,1},{6,2},{7,3},{8,12},{9,13},{10,... | collective-permute-start | bytes 786440 | tf_op jit(solution)/shard_map/ppermute | solution.py:252
  8.9 1.5 %collective-permute-start = (bf16[1024,128]{1,0:T(8,128)(2,1)}, bf16[1024,128]{1,0:T(8,128)(2,1)S(1)}, u32[]{:S(2)}, u32[]{:S(2)}) collective-permute-start(bf16[1024,128]{1,0:T(8,128)(2,1)} %get-tuple-element.52.refs_0_), channel_id=1, source_target_pairs={{0,16},{8,24},{16,0},{24,8},{1,17},{9,25},{17,1},{25,9},{2,18},{10... | collective-permute-start | bytes 786440 | tf_op jit(solution)/shard_map/ppermute | solution.py:643
  10.4 3.5 %shard_map.77 = (bf16[1024,128]{1,0:T(8,128)(2,1)S(1)}, bf16[1024,128]{1,0:T(8,128)(2,1)S(1)}, bf16[128,128]{1,0:T(8,128)(2,1)S(1)}, bf16[4,256,1024]{2,1,0:T(8,...) custom-call(bf16[8192,128]{1,0:T(8,128)(2,1)} %bitcast.6, ...), custom_call_target="tpu_custom_call" | custom-call | flops 134217728 | bytes 4194304 | tf_op jit(solution)/shard_map/pallas_call | solution.py:415
  13.8 1.5 %collective-permute-done.1.refs_6_ = bf16[1024,128]{1,0:T(8,128)(2,1)S(1)} collective-permute-done((bf16[1024,128]{1,0:T(8,128)(2,1)}, bf16[1024,128]{1,0:T(8,128)(2,1)S(1)}, u32[]{:S(2)}, u32[]{:S(2)}) %collective-permute-start.1) | collective-permute-done | bytes 262176 | tf_op jit(solution)/shard_map/ppermute | solution.py:252
  15.4 1.5 %collective-permute-done.refs_2_ = bf16[1024,128]{1,0:T(8,128)(2,1)S(1)} collective-permute-done((bf16[1024,128]{1,0:T(8,128)(2,1)}, bf16[1024,128]{1,0:T(8,128)(2,1)S(1)}, u32[]{:S(2)}, u32[]{:S(2)}) %collective-permute-start) | collective-permute-done | bytes 262176 | tf_op jit(solution)/shard_map/ppermute | solution.py:643
  16.9 0.5 collective-permute-start.5
  17.4 1.6 %collective-permute-start.2 = (bf16[1024,128]{1,0:T(8,128)(2,1)S(1)}, bf16[1024,128]{1,0:T(8,128)(2,1)S(1)}, u32[]{:S(2)}, u32[]{:S(2)}) collective-permute-start(bf16[1024,128]{1,0:T(8,128)(2,1)S(1)} %get-tuple-element.50), channel_id=1, source_target_pairs={{0,1},{1,0},{2,3},{3,2},{4,5},{5,4},{6,7},{7,6},{8,16},{9,17},{10,... | collective-permute-start | bytes 786440 | tf_op jit(solution)/shard_map/ppermute | solution.py:252
  19.0 0.7 %shard_map.80 = (f32[128,128]{1,0:T(8,128)S(1)}, f32[128,128]{1,0:T(8,128)S(1)}) custom-call(bf16[1024,128]{1,0:T(8,128)(2,1)S(1)} %copy-done.2, bf16[1024,128]{1,0:T(8,128)(2,1)S(1)} %collective-permute-done.4.refs_1_, bf16[1024,128]{1,0:T(8,128)(2,1)S(1)} %collective-permute-done.refs_2_, bf16[1024,128]{1,0:T(8,128)(2,1)S(1)} %collective-permute-done.5.refs_3_, ...), custom_call_target="tpu_custom_call" | custom-call | flops 268435456 | bytes 2097152 | tf_op jit(solution)/shard_map/pallas_call | solution.py:156
  19.7 0.6 %collective-permute-start.8 = (f32[128,128]{1,0:T(8,128)S(1)}, f32[128,128]{1,0:T(8,128)S(1)}, u32[]{:S(2)}, u32[]{:S(2)}) collective-permute-start(f32[128,128]{1,0:T(8,128)S(1)} %get-tuple-element.60), channel_id=1, source_target_pairs={{0,4},{4,0},{1,5},{5,1},{2,6},{6,2},{3,7},{7,3},{8,12},{12,8},{9,1... | collective-permute-start | bytes 196616 | tf_op jit(solution)/shard_map/ppermute | solution.py:206
  20.5 3.0 %collective-permute-start.6 = (bf16[128,128]{1,0:T(8,128)(2,1)S(1)}, bf16[128,128]{1,0:T(8,128)(2,1)S(1)}, u32[]{:S(2)}, u32[]{:S(2)}) collective-permute-start(bf16[128,128]{1,0:T(8,128)(2,1)S(1)} %get-tuple-element.58), channel_id=1, source_target_pairs={{0,1},{1,0},{2,3},{3,2},{4,5},{5,4},{6,7},{7,6},{8,9},{9,8},{10,11... | collective-permute-start | bytes 98312 | tf_op jit(solution)/shard_map/ppermute | solution.py:252
  23.4 0.3 collective-permute-done.2.refs_7_
  23.7 0.5 collective-permute-done.8.other_ref
  24.4 3.5 %collective-permute-start.9 = (f32[64,128]{1,0:T(8,128)S(1)}, f32[64,128]{1,0:T(8,128)S(1)}, u32[]{:S(2)}, u32[]{:S(2)}) collective-permute-start(f32[64,128]{1,0:T(8,128)S(1)} %get-tuple-element.63), channel_id=1, source_target_pairs={{0,3},{1,2},{2,1},{3,0},{4,7},{5,6},{6,5},{7,4},{8,11},{9,10},{10,... | collective-permute-start | bytes 98312 | tf_op jit(solution)/shard_map/ppermute | solution.py:211
  27.8 1.0 %collective-permute-start.11 = (f32[64,128]{1,0:T(8,128)S(1)}, f32[64,128]{1,0:T(8,128)S(1)}, u32[]{:S(2)}, u32[]{:S(2)}) collective-permute-start(f32[64,128]{1,0:T(8,128)S(1)} %get-tuple-element.65), channel_id=1, source_target_pairs={{0,1},{1,0},{2,3},{3,2},{4,5},{5,4},{6,7},{7,6},{8,9},{9,8},{10,11... | collective-permute-start | bytes 98312 | tf_op jit(solution)/shard_map/ppermute | solution.py:211
  28.8 1.4 %shard_map.78.refs_0_ = f32[8192,128]{1,0:T(8,128)S(1)} custom-call(bf16[8192,128]{1,0:T(8,128)(2,1)S(1)} %bitcast.7, bf16[8192,128]{1,0:T(8,128)(2,1)S(1)} %bitcast.8, f32[128,128]{1,0:T(8,128)S(1)} %get-tuple-element.40.weight.refs_1_, bf16[128,176]{1,0:T(8,128)(2,1)S(1)} %get-tuple-element.41.near_m.refs_2_, ...), custom_call_target="tpu_custom_call" | custom-call | flops 805306368 | bytes 8388608 | tf_op jit(solution)/shard_map/pallas_call | solution.py:457
  30.3 2.3 %collective-permute-done.10.refs_15_ = f32[64,128]{1,0:T(8,128)S(1)} collective-permute-done((f32[64,128]{1,0:T(8,128)S(1)}, f32[64,128]{1,0:T(8,128)S(1)}, u32[]{:S(2)}, u32[]{:S(2)}) %collective-permute-start.10) | collective-permute-done | bytes 32800 | tf_op jit(solution)/shard_map/ppermute | solution.py:211
  32.6 4.0 %shard_map.82 = (bf16[8192,128]{1,0:T(8,128)(2,1)S(1)}, bf16[1024,128]{1,0:T(8,128)(2,1)S(1)}, bf16[1024,128]{1,0:T(8,128)(2,1)S(1)}, bf16[1024,128]{1,0:T(8,128...) custom-call(f32[8192,128]{1,0:T(8,128)S(1)} %shard_map.78.refs_0_, ...), custom_call_target="tpu_custom_call" | custom-call | flops 536870912 | bytes 8388608 | tf_op jit(solution)/shard_map/pallas_call | solution.py:611
  36.6 0.5 collective-permute-start.12
  37.1 0.3 collective-permute-start.13
  37.4 1.1 %collective-permute-start.14 = (bf16[1024,128]{1,0:T(8,128)(2,1)S(1)}, bf16[1024,128]{1,0:T(8,128)(2,1)S(1)}, u32[]{:S(2)}, u32[]{:S(2)}) collective-permute-start(bf16[1024,128]{1,0:T(8,128)(2,1)S(1)} %get-tuple-element.70), channel_id=1, source_target_pairs={{0,8},{1,9},{2,10},{3,11},{4,12},{5,13},{6,14},{7,15},{8,0},{9,1},... | collective-permute-start | bytes 786440 | tf_op jit(solution)/shard_map/ppermute | solution.py:252
  38.5 2.6 %collective-permute-start.15 = (bf16[128,128]{1,0:T(8,128)(2,1)S(1)}, bf16[128,128]{1,0:T(8,128)(2,1)S(1)}, u32[]{:S(2)}, u32[]{:S(2)}) collective-permute-start(bf16[128,128]{1,0:T(8,128)(2,1)S(1)} %get-tuple-element.71), channel_id=1, source_target_pairs={{0,1},{1,0},{2,3},{3,2},{4,5},{5,4},{6,7},{7,6},{8,9},{9,8},{10,11... | collective-permute-start | bytes 98312 | tf_op jit(solution)/shard_map/ppermute | solution.py:252
  41.1 1.7 %shard_map.83.refs_0_ = f32[8192,128]{1,0:T(8,128)S(1)} custom-call(bf16[8192,128]{1,0:T(8,128)(2,1)S(1)} %get-tuple-element.66.field_ref, bf16[8192,128]{1,0:T(8,128)(2,1)S(1)} %get-tuple-element.67.load_ref, f32[128,128]{1,0:T(8,128)S(1)} %get-tuple-element.40.weight.refs_1_, bf16[128,176]{1,0:T(8,128)(2,1)S(1)} %get-tuple-element.41.near_m.refs_2_, ...), custom_call_target="tpu_custom_call" | custom-call | flops 805306368 | bytes 8388608 | tf_op jit(solution)/shard_map/pallas_call | solution.py:457
  42.8 1.4 %collective-permute-done.15.refs_9_ = bf16[128,128]{1,0:T(8,128)(2,1)S(1)} collective-permute-done((bf16[128,128]{1,0:T(8,128)(2,1)S(1)}, bf16[128,128]{1,0:T(8,128)(2,1)S(1)}, u32[]{:S(2)}, u32[]{:S(2)}) %collective-permute-start.15) | collective-permute-done | bytes 32800 | tf_op jit(solution)/shard_map/ppermute | solution.py:252
  44.2 2.8 %shard_map.84 = (bf16[8192,128]{1,0:T(8,128)(2,1)S(1)}, bf16[1024,128]{1,0:T(8,128)(2,1)S(1)}, bf16[1024,128]{1,0:T(8,128)(2,1)S(1)}, bf16[1024,128]{1,0:T(8,128)(2,1)S(1)}, bf16[128,128]{1,0:T(8,128)(2,1)S(1)}) custom-call(f32[8192,128]{1,0:T(8,128)S(1)} %shard_map.83.refs_0_, f32[128,128]{1,0:T(8,128)S(1)} %get-tuple-element.40.weight.refs_1_, ...), custom_call_target="tpu_custom_call" | custom-call | flops 536870912 | bytes 8388608 | tf_op jit(solution)/shard_map/pallas_call | solution.py:611
  47.0 1.5 %collective-permute-start.17 = (bf16[1024,128]{1,0:T(8,128)(2,1)S(1)}, bf16[1024,128]{1,0:T(8,128)(2,1)S(1)}, u32[]{:S(2)}, u32[]{:S(2)}) collective-permute-start(bf16[1024,128]{1,0:T(8,128)(2,1)S(1)} %get-tuple-element.73), channel_id=1, source_target_pairs={{0,4},{1,5},{2,6},{3,7},{4,0},{5,1},{6,2},{7,3},{8,12},{9,13},{10,... | collective-permute-start | bytes 786440 | tf_op jit(solution)/shard_map/ppermute | solution.py:252
  48.5 0.8 %collective-permute-start.18 = (bf16[1024,128]{1,0:T(8,128)(2,1)S(1)}, bf16[1024,128]{1,0:T(8,128)(2,1)S(1)}, u32[]{:S(2)}, u32[]{:S(2)}) collective-permute-start(bf16[1024,128]{1,0:T(8,128)(2,1)S(1)} %get-tuple-element.74), channel_id=1, source_target_pairs={{0,1},{1,0},{2,3},{3,2},{4,5},{5,4},{6,7},{7,6},{8,16},{9,17},{10,... | collective-permute-start | bytes 786440 | tf_op jit(solution)/shard_map/ppermute | solution.py:252
  49.3 0.5 collective-permute-start.21
  49.8 1.4 %collective-permute-start.20 = (bf16[128,128]{1,0:T(8,128)(2,1)S(1)}, bf16[128,128]{1,0:T(8,128)(2,1)S(1)}, u32[]{:S(2)}, u32[]{:S(2)}) collective-permute-start(bf16[128,128]{1,0:T(8,128)(2,1)S(1)} %get-tuple-element.76), channel_id=1, source_target_pairs={{0,1},{1,0},{2,3},{3,2},{4,5},{5,4},{6,7},{7,6},{8,9},{9,8},{10,11... | collective-permute-start | bytes 98312 | tf_op jit(solution)/shard_map/ppermute | solution.py:252
  51.2 1.5 %shard_map.85.refs_0_ = f32[8192,128]{1,0:T(8,128)S(1)} custom-call(bf16[8192,128]{1,0:T(8,128)(2,1)S(1)} %get-tuple-element.72.field_ref, bf16[8192,128]{1,0:T(8,128)(2,1)S(1)} %get-tuple-element.67.load_ref, f32[128,128]{1,0:T(8,128)S(1)} %get-tuple-element.40.weight.refs_1_, bf16[128,176]{1,0:T(8,128)(2,1)S(1)} %get-tuple-element.41.near_m.refs_2_, ...), custom_call_target="tpu_custom_call" | custom-call | flops 805306368 | bytes 8388608 | tf_op jit(solution)/shard_map/pallas_call | solution.py:457
  52.7 2.9 %collective-permute-done.20.refs_9_ = bf16[128,128]{1,0:T(8,128)(2,1)S(1)} collective-permute-done((bf16[128,128]{1,0:T(8,128)(2,1)S(1)}, bf16[128,128]{1,0:T(8,128)(2,1)S(1)}, u32[]{:S(2)}, u32[]{:S(2)}) %collective-permute-start.20) | collective-permute-done | bytes 32800 | tf_op jit(solution)/shard_map/ppermute | solution.py:252
  55.6 2.3 %shard_map.86 = bf16[8192,128]{1,0:T(8,128)(2,1)} custom-call(f32[8192,128]{1,0:T(8,128)S(1)} %shard_map.85.refs_0_, f32[128,128]{1,0:T(8,128)S(1)} %get-tuple-element.40.weight.refs_1_, bf16[128,176]{1,0:T(8,128)(2,1)S(1)} %get-tuple-element.41.near_m.refs_2_, bf16[512,256]{1,0:T(8,128)(2,1)S(1)} %get-tuple-element.42.line_m.refs_3_, ...), custom_call_target="tpu_custom_call" | custom-call | flops 536870912 | bytes 8388608 | tf_op jit(solution)/shard_map/pallas_call | solution.py:611
  (32 shorter events, 0.5 us)
Async XLA Ops:
  0.6 9.7 %copy-start.3 = (f32[8,8,128]{2,1,0:T(8,128)S(1)}, f32[8,8,128]{2,1,0:T(8,128)}, u32[]{:S(2)}) copy-start(f32[8,8,128]{2,1,0:T(8,128)} %param.8) | copy-start | bytes 98308
  5.9 9.5 %collective-permute-start.1 = (bf16[1024,128]{1,0:T(8,128)(2,1)}, bf16[1024,128]{1,0:T(8,128)(2,1)S(1)}, u32[]{:S(2)}, u32[]{:S(2)}) collective-permute-start(bf16[1024,128]{1,0:T(8,128)(2,1)} %get-tuple-element.48), channel_id=1, source_target_pairs={{0,4},{1,5},{2,6},{3,7},{4,0},{5,1},{6,2},{7,3},{8,12},{9,13},{10,... | collective-permute-start | bytes 786440 | tf_op jit(solution)/shard_map/ppermute | solution.py:252
  8.9 8.0 %collective-permute-start = (bf16[1024,128]{1,0:T(8,128)(2,1)}, bf16[1024,128]{1,0:T(8,128)(2,1)S(1)}, u32[]{:S(2)}, u32[]{:S(2)}) collective-permute-start(bf16[1024,128]{1,0:T(8,128)(2,1)} %get-tuple-element.52.refs_0_), channel_id=1, source_target_pairs={{0,16},{8,24},{16,0},{24,8},{1,17},{9,25},{17,1},{25,9},{2,18},{10... | collective-permute-start | bytes 786440 | tf_op jit(solution)/shard_map/ppermute | solution.py:643
  10.4 6.5 %copy-start.2 = (bf16[1024,128]{1,0:T(8,128)(2,1)S(1)}, bf16[1024,128]{1,0:T(8,128)(2,1)}, u32[]{:S(2)}) copy-start(bf16[1024,128]{1,0:T(8,128)(2,1)} %get-tuple-element.52.refs_0_) | copy-start | bytes 786436
  10.4 18.4 %copy-start.1 = (bf16[128,8,8,128]{3,2,1,0:T(8,128)(2,1)S(1)}, bf16[128,8,8,128]{3,2,1,0:T(8,128)(2,1)}, u32[]{:S(2)}) copy-start(bf16[128,8,8,128]{3,2,1,0:T(8,128)(2,1)} %param.7) | copy-start | bytes 6291460
  13.8 15.0 %copy-start = (bf16[128,8,8,128]{3,2,1,0:T(8,128)(2,1)S(1)}, bf16[128,8,8,128]{3,2,1,0:T(8,128)(2,1)}, u32[]{:S(2)}) copy-start(bf16[128,8,8,128]{3,2,1,0:T(8,128)(2,1)} %param.6) | copy-start | bytes 6291460
  16.9 2.1 %collective-permute-start.4 = (bf16[1024,128]{1,0:T(8,128)(2,1)S(1)}, bf16[1024,128]{1,0:T(8,128)(2,1)S(1)}, u32[]{:S(2)}, u32[]{:S(2)}) collective-permute-start(bf16[1024,128]{1,0:T(8,128)(2,1)S(1)} %copy-done.2), channel_id=1, source_target_pairs={{0,8},{8,0},{16,24},{24,16},{1,9},{9,1},{17,25},{25,17},{2,10},{10... | collective-permute-start | bytes 786440 | tf_op jit(solution)/shard_map/ppermute | solution.py:643
  16.9 2.1 %collective-permute-start.5 = (bf16[1024,128]{1,0:T(8,128)(2,1)S(1)}, bf16[1024,128]{1,0:T(8,128)(2,1)S(1)}, u32[]{:S(2)}, u32[]{:S(2)}) collective-permute-start(bf16[1024,128]{1,0:T(8,128)(2,1)S(1)} %collective-permute-done.refs_2_), channel_id=1, source_target_pairs={{0,8},{8,0},{16,24},{24,16},{1,9},{9,1},{17,25},{25,17},{2,10},{10... | collective-permute-start | bytes 786440 | tf_op jit(solution)/shard_map/ppermute | solution.py:643
  17.4 6.4 %collective-permute-start.2 = (bf16[1024,128]{1,0:T(8,128)(2,1)S(1)}, bf16[1024,128]{1,0:T(8,128)(2,1)S(1)}, u32[]{:S(2)}, u32[]{:S(2)}) collective-permute-start(bf16[1024,128]{1,0:T(8,128)(2,1)S(1)} %get-tuple-element.50), channel_id=1, source_target_pairs={{0,1},{1,0},{2,3},{3,2},{4,5},{5,4},{6,7},{7,6},{8,16},{9,17},{10,... | collective-permute-start | bytes 786440 | tf_op jit(solution)/shard_map/ppermute | solution.py:252
  18.9 4.8 %collective-permute-start.3 = (bf16[1024,128]{1,0:T(8,128)(2,1)S(1)}, bf16[1024,128]{1,0:T(8,128)(2,1)S(1)}, u32[]{:S(2)}, u32[]{:S(2)}) collective-permute-start(bf16[1024,128]{1,0:T(8,128)(2,1)S(1)} %get-tuple-element.51), channel_id=1, source_target_pairs={{0,8},{1,9},{2,10},{3,11},{4,12},{5,13},{6,14},{7,15},{8,0},{9,1},... | collective-permute-start | bytes 786440 | tf_op jit(solution)/shard_map/ppermute | solution.py:252
  19.7 4.5 %collective-permute-start.8 = (f32[128,128]{1,0:T(8,128)S(1)}, f32[128,128]{1,0:T(8,128)S(1)}, u32[]{:S(2)}, u32[]{:S(2)}) collective-permute-start(f32[128,128]{1,0:T(8,128)S(1)} %get-tuple-element.60), channel_id=1, source_target_pairs={{0,4},{4,0},{1,5},{5,1},{2,6},{6,2},{3,7},{7,3},{8,12},{12,8},{9,1... | collective-permute-start | bytes 196616 | tf_op jit(solution)/shard_map/ppermute | solution.py:206
  20.3 10.0 %collective-permute-start.7 = (bf16[128,128]{1,0:T(8,128)(2,1)S(1)}, bf16[128,128]{1,0:T(8,128)(2,1)S(1)}, u32[]{:S(2)}, u32[]{:S(2)}) collective-permute-start(bf16[128,128]{1,0:T(8,128)(2,1)S(1)} %get-tuple-element.58), channel_id=1, source_target_pairs={{0,8},{1,2},{2,1},{3,11},{4,12},{5,6},{6,5},{7,15},{8,0},{9,10},{1... | collective-permute-start | bytes 98312 | tf_op jit(solution)/shard_map/ppermute | solution.py:252
  20.5 9.8 %collective-permute-start.6 = (bf16[128,128]{1,0:T(8,128)(2,1)S(1)}, bf16[128,128]{1,0:T(8,128)(2,1)S(1)}, u32[]{:S(2)}, u32[]{:S(2)}) collective-permute-start(bf16[128,128]{1,0:T(8,128)(2,1)S(1)} %get-tuple-element.58), channel_id=1, source_target_pairs={{0,1},{1,0},{2,3},{3,2},{4,5},{5,4},{6,7},{7,6},{8,9},{9,8},{10,11... | collective-permute-start | bytes 98312 | tf_op jit(solution)/shard_map/ppermute | solution.py:252
  24.4 6.0 %collective-permute-start.9 = (f32[64,128]{1,0:T(8,128)S(1)}, f32[64,128]{1,0:T(8,128)S(1)}, u32[]{:S(2)}, u32[]{:S(2)}) collective-permute-start(f32[64,128]{1,0:T(8,128)S(1)} %get-tuple-element.63), channel_id=1, source_target_pairs={{0,3},{1,2},{2,1},{3,0},{4,7},{5,6},{6,5},{7,4},{8,11},{9,10},{10,... | collective-permute-start | bytes 98312 | tf_op jit(solution)/shard_map/ppermute | solution.py:211
  27.8 4.8 %collective-permute-start.10 = (f32[64,128]{1,0:T(8,128)S(1)}, f32[64,128]{1,0:T(8,128)S(1)}, u32[]{:S(2)}, u32[]{:S(2)}) collective-permute-start(f32[64,128]{1,0:T(8,128)S(1)} %get-tuple-element.64), channel_id=1, source_target_pairs={{0,2},{1,3},{2,0},{3,1},{4,6},{5,7},{6,4},{7,5},{8,10},{9,11},{10,... | collective-permute-start | bytes 98312 | tf_op jit(solution)/shard_map/ppermute | solution.py:211
  27.8 4.8 %collective-permute-start.11 = (f32[64,128]{1,0:T(8,128)S(1)}, f32[64,128]{1,0:T(8,128)S(1)}, u32[]{:S(2)}, u32[]{:S(2)}) collective-permute-start(f32[64,128]{1,0:T(8,128)S(1)} %get-tuple-element.65), channel_id=1, source_target_pairs={{0,1},{1,0},{2,3},{3,2},{4,5},{5,4},{6,7},{7,6},{8,9},{9,8},{10,11... | collective-permute-start | bytes 98312 | tf_op jit(solution)/shard_map/ppermute | solution.py:211
  28.8 3.8 %copy-start.4 = (s32[1,1,1,32]{3,2,1,0:T(1,128)S(1)}, s32[1,1,1,32]{3,2,1,0:T(1,128)}, u32[]{:S(2)}) copy-start(s32[1,1,1,32]{3,2,1,0:T(1,128)} %refs_12_.1) | copy-start | bytes 388
  36.6 7.6 %collective-permute-start.12 = (bf16[1024,128]{1,0:T(8,128)(2,1)S(1)}, bf16[1024,128]{1,0:T(8,128)(2,1)S(1)}, u32[]{:S(2)}, u32[]{:S(2)}) collective-permute-start(bf16[1024,128]{1,0:T(8,128)(2,1)S(1)} %get-tuple-element.68), channel_id=1, source_target_pairs={{0,4},{1,5},{2,6},{3,7},{4,0},{5,1},{6,2},{7,3},{8,12},{9,13},{10,... | collective-permute-start | bytes 786440 | tf_op jit(solution)/shard_map/ppermute | solution.py:252
  37.1 7.1 %collective-permute-start.13 = (bf16[1024,128]{1,0:T(8,128)(2,1)S(1)}, bf16[1024,128]{1,0:T(8,128)(2,1)S(1)}, u32[]{:S(2)}, u32[]{:S(2)}) collective-permute-start(bf16[1024,128]{1,0:T(8,128)(2,1)S(1)} %get-tuple-element.69), channel_id=1, source_target_pairs={{0,1},{1,0},{2,3},{3,2},{4,5},{5,4},{6,7},{7,6},{8,16},{9,17},{10,... | collective-permute-start | bytes 786440 | tf_op jit(solution)/shard_map/ppermute | solution.py:252
  37.4 6.8 %collective-permute-start.14 = (bf16[1024,128]{1,0:T(8,128)(2,1)S(1)}, bf16[1024,128]{1,0:T(8,128)(2,1)S(1)}, u32[]{:S(2)}, u32[]{:S(2)}) collective-permute-start(bf16[1024,128]{1,0:T(8,128)(2,1)S(1)} %get-tuple-element.70), channel_id=1, source_target_pairs={{0,8},{1,9},{2,10},{3,11},{4,12},{5,13},{6,14},{7,15},{8,0},{9,1},... | collective-permute-start | bytes 786440 | tf_op jit(solution)/shard_map/ppermute | solution.py:252
  38.5 4.3 %collective-permute-start.16 = (bf16[128,128]{1,0:T(8,128)(2,1)S(1)}, bf16[128,128]{1,0:T(8,128)(2,1)S(1)}, u32[]{:S(2)}, u32[]{:S(2)}) collective-permute-start(bf16[128,128]{1,0:T(8,128)(2,1)S(1)} %get-tuple-element.71), channel_id=1, source_target_pairs={{0,8},{1,2},{2,1},{3,11},{4,12},{5,6},{6,5},{7,15},{8,0},{9,10},{1... | collective-permute-start | bytes 98312 | tf_op jit(solution)/shard_map/ppermute | solution.py:252
  38.5 5.7 %collective-permute-start.15 = (bf16[128,128]{1,0:T(8,128)(2,1)S(1)}, bf16[128,128]{1,0:T(8,128)(2,1)S(1)}, u32[]{:S(2)}, u32[]{:S(2)}) collective-permute-start(bf16[128,128]{1,0:T(8,128)(2,1)S(1)} %get-tuple-element.71), channel_id=1, source_target_pairs={{0,1},{1,0},{2,3},{3,2},{4,5},{5,4},{6,7},{7,6},{8,9},{9,8},{10,11... | collective-permute-start | bytes 98312 | tf_op jit(solution)/shard_map/ppermute | solution.py:252
  47.0 8.6 %collective-permute-start.17 = (bf16[1024,128]{1,0:T(8,128)(2,1)S(1)}, bf16[1024,128]{1,0:T(8,128)(2,1)S(1)}, u32[]{:S(2)}, u32[]{:S(2)}) collective-permute-start(bf16[1024,128]{1,0:T(8,128)(2,1)S(1)} %get-tuple-element.73), channel_id=1, source_target_pairs={{0,4},{1,5},{2,6},{3,7},{4,0},{5,1},{6,2},{7,3},{8,12},{9,13},{10,... | collective-permute-start | bytes 786440 | tf_op jit(solution)/shard_map/ppermute | solution.py:252
  48.5 7.1 %collective-permute-start.18 = (bf16[1024,128]{1,0:T(8,128)(2,1)S(1)}, bf16[1024,128]{1,0:T(8,128)(2,1)S(1)}, u32[]{:S(2)}, u32[]{:S(2)}) collective-permute-start(bf16[1024,128]{1,0:T(8,128)(2,1)S(1)} %get-tuple-element.74), channel_id=1, source_target_pairs={{0,1},{1,0},{2,3},{3,2},{4,5},{5,4},{6,7},{7,6},{8,16},{9,17},{10,... | collective-permute-start | bytes 786440 | tf_op jit(solution)/shard_map/ppermute | solution.py:252
  49.3 6.3 %collective-permute-start.19 = (bf16[1024,128]{1,0:T(8,128)(2,1)S(1)}, bf16[1024,128]{1,0:T(8,128)(2,1)S(1)}, u32[]{:S(2)}, u32[]{:S(2)}) collective-permute-start(bf16[1024,128]{1,0:T(8,128)(2,1)S(1)} %get-tuple-element.75), channel_id=1, source_target_pairs={{0,8},{1,9},{2,10},{3,11},{4,12},{5,13},{6,14},{7,15},{8,0},{9,1},... | collective-permute-start | bytes 786440 | tf_op jit(solution)/shard_map/ppermute | solution.py:252
  49.3 3.4 %collective-permute-start.21 = (bf16[128,128]{1,0:T(8,128)(2,1)S(1)}, bf16[128,128]{1,0:T(8,128)(2,1)S(1)}, u32[]{:S(2)}, u32[]{:S(2)}) collective-permute-start(bf16[128,128]{1,0:T(8,128)(2,1)S(1)} %get-tuple-element.76), channel_id=1, source_target_pairs={{0,8},{1,2},{2,1},{3,11},{4,12},{5,6},{6,5},{7,15},{8,0},{9,10},{1... | collective-permute-start | bytes 98312 | tf_op jit(solution)/shard_map/ppermute | solution.py:252
  49.8 5.8 %collective-permute-start.20 = (bf16[128,128]{1,0:T(8,128)(2,1)S(1)}, bf16[128,128]{1,0:T(8,128)(2,1)S(1)}, u32[]{:S(2)}, u32[]{:S(2)}) collective-permute-start(bf16[128,128]{1,0:T(8,128)(2,1)S(1)} %get-tuple-element.76), channel_id=1, source_target_pairs={{0,1},{1,0},{2,3},{3,2},{4,5},{5,4},{6,7},{7,6},{8,9},{9,8},{10,11... | collective-permute-start | bytes 98312 | tf_op jit(solution)/shard_map/ppermute | solution.py:252

commit v13 on v12

--- a/solution.py
+++ b/solution.py
@@ -430,106 +430,140 @@
     )(field, block, coef)
 
 
-def base_kernel(shape, field_ref, load_ref, weight, near_m, line_m, base_ref, lines):
+def expand(shape, lines, where):
+    rows = []
+    for side in range(shape.block):
+        line = jnp.broadcast_to(lines[side : side + 1], where.shape)
+        rows.append(jnp.where(where, line, 0.0))
+    return beside(jnp.concatenate(rows, axis=0).astype(BF))
+
+
+def build_cells(shape, cell_ref, cell_m):
+    slots = cell_ref.shape[3]
+    cell = jnp.concatenate([cell_ref[0, 0]] * 2, axis=1)
+    place = (iota((shape.lanes, 2 * slots), 0) == cell % shape.lanes).astype(F32)
+    cell_m[...] = twice(place).astype(BF)
+    return iota((shape.cells, 2 * slots), 0) == cell // shape.lanes
+
+
+def base_kernel(shape, with_flux, *refs):
+    refs = list(refs)
+    take = lambda count: [refs.pop(0) for _ in range(count)]
+    field_ref, load_ref, weight, near_m, line_m = take(5)
+    end_refs = take(shape.ends)
+    if with_flux:
+        phi, cell_ref = take(2)
+    (base_ref,) = take(1)
+    if with_flux:
+        (source_ref,) = take(1)
+    (lines,) = take(1)
+    if with_flux:
+        cell_m, placed = take(2)
+        cell_mask = build_cells(shape, cell_ref, cell_m)
+
     cells, lanes = shape.cells, shape.lanes
     weights = weight[...]
+    mask = z_mask(shape, 1)
+    even = lax.axis_index("gz") % 2 == 0
+    filled = (iota((shape.block, 2 * cells), 1) < cells) == even
     for step in range(shape.sides // shape.block):
+        sides = slice(step * shape.block, (step + 1) * shape.block)
         at = step * shape.block * cells
+        zs = 0.0
+        for turn in range(shape.ends):
+            wanted = (filled == (turn == 0)) & has_neighbour("gz", turn)
+            zs = jnp.where(wanted, end_refs[turn][sides, :].astype(F32), zs)
         values = field_ref[at : at + shape.block * cells, :]
-        lines[step] = dot(beside(values), line_m[: 2 * lanes, :])
+        left = jnp.concatenate([beside(values), expand(shape, zs, mask)], axis=1)
+        lines[step] = dot(left, line_m[...])
+        if with_flux:
+            placed[step] = dot_nt(expand(shape, phi[sides, :], cell_mask), cell_m[...])
         for index in range(shape.half // shape.chunk):
             offset = index * shape.rows
+            here = slice(offset, offset + shape.rows)
             spans = [
                 slice(at + start, at + start + shape.rows)
                 for start in (offset, offset + shape.half_rows)
             ]
             stack = jnp.concatenate([field_ref[span, :] for span in spans], axis=1)
-            near = dot(near_m[:, : shape.rows], stack) + lines[step, offset : offset + shape.rows, :]
+            near = dot(near_m[:, : shape.rows], stack) + lines[step, here, :]
             for part, span in enumerate(spans):
+                cols = slice(part * lanes, (part + 1) * lanes)
                 source = load_ref[span, :].astype(F32)
+                if with_flux:
+                    source = source + placed[step, here, cols]
+                    source_ref[span, :] = source.astype(BF)
                 centre = field_ref[span, :].astype(F32)
-                near_part = near[:, part * lanes : (part + 1) * lanes]
-                base_ref[span, :] = (1.0 - OMEGA) * centre + weights * (source + near_part)
-
-
-def sweep_base(shape, field, load, tables):
+                base_ref[span, :] = (1.0 - OMEGA) * centre + weights * (source + near[:, cols])
+
+
+def sweep_base(shape, field, load, tables, ends, phi=None, flux_cell=None):
     steps = shape.sides // shape.block
+    half = (steps, shape.half_rows, 2 * shape.lanes)
+    operands = [field, load, *tables[:3], *ends]
+    shapes = [jax.ShapeDtypeStruct(field.shape, F32)]
+    scratch = [pltpu.VMEM(half, F32)]
+    if phi is not None:
+        operands += [phi, flux_cell]
+        shapes.append(jax.ShapeDtypeStruct(field.shape, BF))
+        scratch.append(pltpu.VMEM((2 * shape.lanes, 2 * phi.shape[1]), BF))
+        scratch.append(pltpu.VMEM(half, F32))
     return pl.pallas_call(
-        functools.partial(base_kernel, shape),
-        in_specs=[WHOLE] * 5,
-        out_specs=WHOLE,
-        out_shape=jax.ShapeDtypeStruct(field.shape, F32),
-        scratch_shapes=[pltpu.VMEM((steps, shape.half_rows, 2 * shape.lanes), F32)],
+        functools.partial(base_kernel, shape, phi is not None),
+        in_specs=[WHOLE] * len(operands),
+        out_specs=[WHOLE] * len(shapes),
+        out_shape=shapes,
+        scratch_shapes=scratch,
         compiler_params=params(),
         cost_estimate=pl.CostEstimate(
             flops=6 * field.size * 128, bytes_accessed=8 * field.size, transcendentals=0
         ),
-    )(field, load, *tables[:3])
+    )(*operands)
 
 
 def finish_kernel(shape, recvs, last, *refs):
     with_flux = recvs > 0
     refs = list(refs)
     take = lambda count: [refs.pop(0) for _ in range(count)]
-    base_ref, weight, near_m, line_m, ends_m, rsum = take(6)
+    base_ref, weight, near_m, ends_m, rsum = take(5)
     halo_refs = take(len(shape.faces))
-    end_refs = take(shape.ends)
     if with_flux:
-        load_ref, cell_ref = take(2)
+        (cell_ref,) = take(1)
         recv_refs = take(recvs)
     (out_ref,) = take(1)
     if not last:
         face_refs = take(len(shape.faces))
         (z_ref,) = take(1)
     if with_flux:
-        source_ref, flux_ref = take(2)
-    (lines,) = take(1)
+        phi, flux_ref = take(2)
     if last:
         result_ref = out_ref
         out_ref, out_sems = take(2)
     else:
         (tall,) = take(1)
     if with_flux:
-        phi, cell_m, placed = take(3)
+        cell_m, placed = take(2)
 
     cells, lanes = shape.cells, shape.lanes
 
     if with_flux:
         slots = cell_ref.shape[3]
+        cell_mask = build_cells(shape, cell_ref, cell_m)
         owned = recv_refs[0][...]
         for ref in recv_refs[1:]:
             owned = owned + ref[...]
         flux_ref[...] = owned[slots:, : flux_ref.shape[1]]
         owned = owned[:slots]
         high = owned.astype(BF).astype(F32)
-        both = jnp.concatenate([high, owned - high], axis=0)
-        phi[...] = both.T
-        cell = jnp.concatenate([cell_ref[0, 0]] * 2, axis=1)
-        cell_m[...] = twice((iota((lanes, 2 * slots), 0) == cell % lanes).astype(F32)).astype(BF)
-        cell_mask = iota((cells, 2 * slots), 0) == cell // lanes
-
-    mask = z_mask(shape, 1)
-    even = lax.axis_index("gz") % 2 == 0
-    filled = (iota((shape.block, 2 * cells), 1) < cells) == even
+        phi[...] = jnp.concatenate([high, owned - high], axis=0).T
+
     weights = weight[...]
-
-    def expand(lines, where):
-        rows = []
-        for side in range(shape.block):
-            line = jnp.broadcast_to(lines[side : side + 1], where.shape)
-            rows.append(jnp.where(where, line, 0.0))
-        return beside(jnp.concatenate(rows, axis=0).astype(BF))
 
     def work(step):
         at = step * shape.block
-        sides = slice(at, at + shape.block)
-        zs = 0.0
-        for turn in range(shape.ends):
-            wanted = (filled == (turn == 0)) & has_neighbour("gz", turn)
-            zs = jnp.where(wanted, end_refs[turn][sides, :].astype(F32), zs)
-        lines[step] = dot(expand(zs, mask), line_m[2 * lanes :, :])
         if with_flux:
-            placed[step] = dot_nt(expand(phi[sides, :], cell_mask), cell_m[...])
+            sides = slice(at, at + shape.block)
+            placed[step] = dot_nt(expand(shape, phi[sides, :], cell_mask), cell_m[...])
         for index in range(shape.half // shape.chunk):
             offset = index * shape.rows
             starts = (offset, offset + shape.half_rows)
@@ -542,16 +576,11 @@
                     stack.append(ref[first : first + shape.chunk * length, :])
                 stacks.append(jnp.concatenate(stack, axis=0))
             near = dot(near_m[:, shape.rows :], jnp.concatenate(stacks, axis=1))
-            near = near + lines[step, offset : offset + shape.rows, :]
             if with_flux:
                 near = near + placed[step, offset : offset + shape.rows, :]
             for part, start in enumerate(starts):
-                cols = slice(part * lanes, (part + 1) * lanes)
                 rows = slice(at * cells + start, at * cells + start + shape.rows)
-                if with_flux:
-                    flux = placed[step, offset : offset + shape.rows, cols]
-                    source_ref[rows, :] = (load_ref[rows, :].astype(F32) + flux).astype(BF)
-                fresh = base_ref[rows, :] + weights * near[:, cols]
+                fresh = base_ref[rows, :] + weights * near[:, part * lanes : (part + 1) * lanes]
                 out_ref[rows, :] = fresh.astype(BF)
                 if not last:
                     tall[step, start : start + shape.rows, :] = fresh
@@ -580,30 +609,28 @@
         emit(steps - 1)
 
 
-def sweep_finish(shape, base, tables, halos, load=None, flux_cell=None, recv=(), last=False):
+def sweep_finish(shape, base, tables, halos, flux_cell=None, recv=(), last=False):
     lanes, cells = shape.lanes, shape.cells
     steps = shape.sides // shape.block
-    half = (steps, shape.half_rows, 2 * lanes)
-    operands = [base, *tables, *halos]
+    weight, near_m, _, ends_m, rsum = tables
+    operands = [base, weight, near_m, ends_m, rsum, *halos]
     out_shapes = [jax.ShapeDtypeStruct(base.shape, BF)]
-    scratch = [pltpu.VMEM(half, F32)]
     if last:
-        scratch += [pltpu.VMEM(base.shape, BF), pltpu.SemaphoreType.DMA((steps,))]
+        scratch = [pltpu.VMEM(base.shape, BF), pltpu.SemaphoreType.DMA((steps,))]
     else:
         out_shapes += face_shapes(shape, shape.faces)
         out_shapes.append(jax.ShapeDtypeStruct((shape.sides, 2 * cells), BF))
-        scratch.append(pltpu.VMEM((steps, shape.block * cells, lanes), F32))
+        scratch = [pltpu.VMEM((steps, shape.block * cells, lanes), F32)]
     if recv:
         slots = flux_cell.shape[3]
-        operands += [load, flux_cell, *recv]
+        operands += [flux_cell, *recv]
         out_shapes += [
-            jax.ShapeDtypeStruct(base.shape, BF),
+            jax.ShapeDtypeStruct((shape.sides, 2 * slots), F32),
             jax.ShapeDtypeStruct((recv[0].shape[0] - slots, slots * lax.axis_size("gz")), F32),
         ]
         scratch += [
-            pltpu.VMEM((shape.sides, 2 * slots), F32),
             pltpu.VMEM((2 * lanes, 4 * slots), BF),
-            pltpu.VMEM(half, F32),
+            pltpu.VMEM((steps, shape.half_rows, 2 * lanes), F32),
         ]
     out_specs = [WHOLE] * len(out_shapes)
     if last:
@@ -629,9 +656,12 @@
     return [swap(ends, "gz", turn) for turn in range(shape.ends)]
 
 
-def exchange(shape, faces):
-    *cut, ends = faces
-    return swap_faces(shape.faces, cut) + swap_ends(shape, ends)
+def exchange(shape, faces, ends):
+    count = len(shape.outer)
+    tips = swap_ends(shape, ends)
+    along_col = swap_faces(shape.outer, faces[:count])
+    inner, tips[0] = lax.optimization_barrier((faces[count:], tips[0]))
+    return along_col + swap_faces(shape.inner, inner), tips
 
 
 def row_gather(trace, hidden):
@@ -669,16 +699,18 @@
     parts, (inner, along_col) = row_gather(trace, (inner, along_col))
     along_row = swap_faces(shape.inner, inner)
     recv, ends = flux_sums(parts, held, along_row, ends)
-    halos = along_col + along_row + swap_ends(shape, ends)
-
-    base = sweep_base(shape, field, load, tables)
-    current, *faces, source, surface_flux = sweep_finish(
-        shape, base, tables, halos, load=load, flux_cell=flux_cell, recv=recv
+    tips = swap_ends(shape, ends)
+
+    (base,) = sweep_base(shape, field, load, tables, tips)
+    current, *faces, ends, phi, surface_flux = sweep_finish(
+        shape, base, tables, along_col + along_row, flux_cell=flux_cell, recv=recv
     )
-    for last in (False, True):
-        halos = exchange(shape, faces)
-        base = sweep_base(shape, current, source, tables)
-        current, *faces = sweep_finish(shape, base, tables, halos, last=last)
+    halos, tips = exchange(shape, faces, ends)
+    base, source = sweep_base(shape, current, load, tables, tips, phi, flux_cell)
+    current, *faces, ends = sweep_finish(shape, base, tables, halos)
+    halos, tips = exchange(shape, faces, ends)
+    (base,) = sweep_base(shape, current, source, tables, tips)
+    (current,) = sweep_finish(shape, base, tables, halos, last=True)
     return current.reshape(volume_field.shape), surface_flux
 
 

time: 58.2 us -> 62 us (1.065)
  waiting for transfers between devices: 10.4 us -> 13.7 us
  Pallas kernels: 23.2 us -> 24.1 us
    ppermute x15, waiting for transfers between devices: 6.12 us -> 9.97 us  [swap(): return lax.ppermute(value, axes, pairs)]
    pallas_call x3, Pallas kernels: 4.64 us -> 6.76 us  [sweep_base(): pl.pallas_call(functools.partial(base_kernel, shape, phi is not None), in...]
    pallas_call x3, Pallas kernels: 9.09 us -> 7.81 us  [sweep_finish(): pl.pallas_call(functools.partial(finish_kernel, shape, len(recv), last),...]
  transfers between devices with their start and end apart: 22 -> 22, of which waited for: 8 -> 11; matrix products, arithmetic and copies ran while one was open for 0% -> 0% of each run, Pallas kernels for 15% -> 18%
where the time goes in v13:
time: 62 us; the launch traced here: 61.8 us
  Pallas kernels  24.1 us (39%)
  starting transfers between devices  23.1 us (37%)
  waiting for transfers between devices  13.7 us (22%)
  between operations  0.93 us (2%)
    ppermute x15, starting transfers between devices, swap(): return lax.ppermute(value, axes, pairs)  16 us
    ppermute x15, waiting for transfers between devices, swap(): return lax.ppermute(value, axes, pairs)  9.97 us
    pallas_call x3, Pallas kernels, sweep_finish(): pl.pallas_call(functools.partial(finish_kernel, shape, len(recv), last),...  7.81 us
    pallas_call x3, Pallas kernels, sweep_base(): pl.pallas_call(functools.partial(base_kernel, shape, phi is not None), in...  6.76 us
    pallas_call x1, Pallas kernels, traces(): pl.pallas_call(functools.partial(trace_kernel, shape, stride, block), in_...  5.21 us
    ppermute x3, starting transfers between devices, flux_sums(): lax.ppermute(sent[key], 'gz', [(i, i ^ key) for i in range(gzs)])  4.45 us
    pallas_call x1, Pallas kernels, first_faces(): pl.pallas_call(functools.partial(faces_kernel, shape, slots), in_specs=[h...  3.46 us
    ppermute x3, starting transfers between devices, row_gather(): lax.ppermute(held[key], 'row', pairs)  2 us
  transfers between devices with their start and end apart: 22, of which 11 were waited for; matrix products, arithmetic and copies ran while one was open for 0% of the time, Pallas kernels for 18%

profile of v13, /device:TPU:0, one launch (start us, length us, event | category | flops | bytes accessed | tf_op | source)
XLA Modules:
  0.0 61.8 jit_solution(14008691067636912695)
XLA Ops:
  0.6 5.2 %shard_map.78 = (bf16[1024,128]{1,0:T(8,128)(2,1)}, bf16[1024,128]{1,0:T(8,128)(2,1)}) custom-call(bf16[128,64,128]{2,1,0:T(8,128)(2,1)} %bitcast.5, s32[1,1,1,1024]{3,2,1,0:T(1,128)} %cell_ref.1), custom_call_target="tpu_custom_call" | custom-call | flops 536870912 | bytes 2097152 | tf_op jit(solution)/shard_map/pallas_call | solution.py:102
  5.9 3.0 %collective-permute-start.1 = (bf16[1024,128]{1,0:T(8,128)(2,1)}, bf16[1024,128]{1,0:T(8,128)(2,1)S(1)}, u32[]{:S(2)}, u32[]{:S(2)}) collective-permute-start(bf16[1024,128]{1,0:T(8,128)(2,1)} %get-tuple-element.54), channel_id=1, source_target_pairs={{0,4},{1,5},{2,6},{3,7},{4,0},{5,1},{6,2},{7,3},{8,12},{9,13},{10,... | collective-permute-start | bytes 786440 | tf_op jit(solution)/shard_map/ppermute | solution.py:252
  8.9 1.5 %collective-permute-start = (bf16[1024,128]{1,0:T(8,128)(2,1)}, bf16[1024,128]{1,0:T(8,128)(2,1)S(1)}, u32[]{:S(2)}, u32[]{:S(2)}) collective-permute-start(bf16[1024,128]{1,0:T(8,128)(2,1)} %get-tuple-element.55.refs_0_), channel_id=1, source_target_pairs={{0,16},{8,24},{16,0},{24,8},{1,17},{9,25},{17,1},{25,9},{2,18},{10... | collective-permute-start | bytes 786440 | tf_op jit(solution)/shard_map/ppermute | solution.py:673
  10.4 3.5 %shard_map.77 = (bf16[1024,128]{1,0:T(8,128)(2,1)S(1)}, bf16[1024,128]{1,0:T(8,128)(2,1)S(1)}, bf16[128,128]{1,0:T(8,128)(2,1)S(1)}, bf16[4,256,1024]{2,1,0:T(8,...) custom-call(bf16[8192,128]{1,0:T(8,128)(2,1)} %bitcast.6, ...), custom_call_target="tpu_custom_call" | custom-call | flops 134217728 | bytes 4194304 | tf_op jit(solution)/shard_map/pallas_call | solution.py:415
  13.8 1.5 %collective-permute-done.1.refs_5_ = bf16[1024,128]{1,0:T(8,128)(2,1)S(1)} collective-permute-done((bf16[1024,128]{1,0:T(8,128)(2,1)}, bf16[1024,128]{1,0:T(8,128)(2,1)S(1)}, u32[]{:S(2)}, u32[]{:S(2)}) %collective-permute-start.1) | collective-permute-done | bytes 262176 | tf_op jit(solution)/shard_map/ppermute | solution.py:252
  15.4 1.5 %collective-permute-done.refs_2_ = bf16[1024,128]{1,0:T(8,128)(2,1)S(1)} collective-permute-done((bf16[1024,128]{1,0:T(8,128)(2,1)}, bf16[1024,128]{1,0:T(8,128)(2,1)S(1)}, u32[]{:S(2)}, u32[]{:S(2)}) %collective-permute-start) | collective-permute-done | bytes 262176 | tf_op jit(solution)/shard_map/ppermute | solution.py:673
  16.9 0.5 collective-permute-start.3
  17.4 1.6 %collective-permute-start.6 = (bf16[1024,128]{1,0:T(8,128)(2,1)S(1)}, bf16[1024,128]{1,0:T(8,128)(2,1)S(1)}, u32[]{:S(2)}, u32[]{:S(2)}) collective-permute-start(bf16[1024,128]{1,0:T(8,128)(2,1)S(1)} %get-tuple-element.65), channel_id=1, source_target_pairs={{0,1},{1,0},{2,3},{3,2},{4,5},{5,4},{6,7},{7,6},{8,16},{9,17},{10,... | collective-permute-start | bytes 786440 | tf_op jit(solution)/shard_map/ppermute | solution.py:252
  19.0 0.7 %shard_map.79 = (f32[128,128]{1,0:T(8,128)S(1)}, f32[128,128]{1,0:T(8,128)S(1)}) custom-call(bf16[1024,128]{1,0:T(8,128)(2,1)S(1)} %copy-done.2, bf16[1024,128]{1,0:T(8,128)(2,1)S(1)} %collective-permute-done.2.refs_1_, bf16[1024,128]{1,0:T(8,128)(2,1)S(1)} %collective-permute-done.refs_2_, bf16[1024,128]{1,0:T(8,128)(2,1)S(1)} %collective-permute-done.3.refs_3_, ...), custom_call_target="tpu_custom_call" | custom-call | flops 268435456 | bytes 2097152 | tf_op jit(solution)/shard_map/pallas_call | solution.py:156
  19.7 0.6 collective-permute-start.8
  20.5 3.0 %collective-permute-start.4 = (bf16[128,128]{1,0:T(8,128)(2,1)S(1)}, bf16[128,128]{1,0:T(8,128)(2,1)S(1)}, u32[]{:S(2)}, u32[]{:S(2)}) collective-permute-start(bf16[128,128]{1,0:T(8,128)(2,1)S(1)} %get-tuple-element.61), channel_id=1, source_target_pairs={{0,1},{1,0},{2,3},{3,2},{4,5},{5,4},{6,7},{7,6},{8,9},{9,8},{10,11... | collective-permute-start | bytes 98312 | tf_op jit(solution)/shard_map/ppermute | solution.py:252
  24.4 3.5 %collective-permute-start.9 = (f32[64,128]{1,0:T(8,128)S(1)}, f32[64,128]{1,0:T(8,128)S(1)}, u32[]{:S(2)}, u32[]{:S(2)}) collective-permute-start(f32[64,128]{1,0:T(8,128)S(1)} %get-tuple-element.71), channel_id=1, source_target_pairs={{0,3},{1,2},{2,1},{3,0},{4,7},{5,6},{6,5},{7,4},{8,11},{9,10},{10,... | collective-permute-start | bytes 98312 | tf_op jit(solution)/shard_map/ppermute | solution.py:211
  27.8 1.0 %collective-permute-start.11 = (f32[64,128]{1,0:T(8,128)S(1)}, f32[64,128]{1,0:T(8,128)S(1)}, u32[]{:S(2)}, u32[]{:S(2)}) collective-permute-start(f32[64,128]{1,0:T(8,128)S(1)} %get-tuple-element.73), channel_id=1, source_target_pairs={{0,1},{1,0},{2,3},{3,2},{4,5},{5,4},{6,7},{7,6},{8,9},{9,8},{10,11... | collective-permute-start | bytes 98312 | tf_op jit(solution)/shard_map/ppermute | solution.py:211
  28.8 2.0 %shard_map.80.refs_0_ = f32[8192,128]{1,0:T(8,128)S(1)} custom-call(bf16[8192,128]{1,0:T(8,128)(2,1)S(1)} %bitcast.7, bf16[8192,128]{1,0:T(8,128)(2,1)S(1)} %bitcast.8, f32[128,128]{1,0:T(8,128)S(1)} %get-tuple-element.48.refs_2_.refs_1_, bf16[128,176]{1,0:T(8,128)(2,1)S(1)} %get-tuple-element.49.refs_3_.refs_2_, ...), custom_call_target="tpu_custom_call" | custom-call | flops 805306368 | bytes 8388608 | tf_op jit(solution)/shard_map/pallas_call | solution.py:511
  30.8 1.8 %collective-permute-done.10.refs_11_ = f32[64,128]{1,0:T(8,128)S(1)} collective-permute-done((f32[64,128]{1,0:T(8,128)S(1)}, f32[64,128]{1,0:T(8,128)S(1)}, u32[]{:S(2)}, u32[]{:S(2)}) %collective-permute-start.10) | collective-permute-done | bytes 32800 | tf_op jit(solution)/shard_map/ppermute | solution.py:211
  32.6 3.5 %shard_map.82 = (bf16[8192,128]{1,0:T(8,128)(2,1)S(1)}, bf16[1024,128]{1,0:T(8,128)(2,1)S(1)}, bf16[1024,128]{1,0:T(8,128)(2,1)S(1)}, bf16[1024,128]{1,0:T(8,128...) custom-call(f32[8192,128]{1,0:T(8,128)S(1)} %shard_map.80.refs_0_, ...), custom_call_target="tpu_custom_call" | custom-call | flops 536870912 | bytes 8388608 | tf_op jit(solution)/shard_map/pallas_call | solution.py:638
  36.3 0.7 %collective-permute-start.14 = (bf16[1024,128]{1,0:T(8,128)(2,1)S(1)}, bf16[1024,128]{1,0:T(8,128)(2,1)S(1)}, u32[]{:S(2)}, u32[]{:S(2)}) collective-permute-start(bf16[1024,128]{1,0:T(8,128)(2,1)S(1)} %get-tuple-element.81), channel_id=1, source_target_pairs={{0,4},{1,5},{2,6},{3,7},{4,0},{5,1},{6,2},{7,3},{8,12},{9,13},{10,... | collective-permute-start | bytes 786440 | tf_op jit(solution)/shard_map/ppermute | solution.py:252
  37.0 3.1 %collective-permute-done.12.refs_5_ = bf16[128,128]{1,0:T(8,128)(2,1)S(1)} collective-permute-done((bf16[128,128]{1,0:T(8,128)(2,1)S(1)}, bf16[128,128]{1,0:T(8,128)(2,1)S(1)}, u32[]{:S(2)}, u32[]{:S(2)}) %collective-permute-start.12) | collective-permute-done | bytes 32800 | tf_op jit(solution)/shard_map/ppermute | solution.py:252
  40.2 1.6 %collective-permute-start.16 = (bf16[1024,128]{1,0:T(8,128)(2,1)S(1)}, bf16[1024,128]{1,0:T(8,128)(2,1)S(1)}, u32[]{:S(2)}, u32[]{:S(2)}) collective-permute-start(bf16[1024,128]{1,0:T(8,128)(2,1)S(1)} %get-tuple-element.83), channel_id=1, source_target_pairs={{0,8},{1,9},{2,10},{3,11},{4,12},{5,13},{6,14},{7,15},{8,0},{9,1},... | collective-permute-start | bytes 786440 | tf_op jit(solution)/shard_map/ppermute | solution.py:252
  41.8 1.2 %collective-permute-done.13.refs_6_ = bf16[128,128]{1,0:T(8,128)(2,1)S(1)} collective-permute-done((bf16[128,128]{1,0:T(8,128)(2,1)S(1)}, bf16[128,128]{1,0:T(8,128)(2,1)S(1)}, u32[]{:S(2)}, u32[]{:S(2)}) %collective-permute-start.13) | collective-permute-done | bytes 32800 | tf_op jit(solution)/shard_map/ppermute | solution.py:252
  43.0 2.8 %shard_map.83 = (f32[8192,128]{1,0:T(8,128)S(1)}, bf16[8192,128]{1,0:T(8,128)(2,1)S(1)}) custom-call(bf16[8192,128]{1,0:T(8,128)(2,1)S(1)} %get-tuple-element.74.refs_0_, bf16[8192,128]{1,0:T(8,128)(2,1)S(1)} %bitcast.9, f32[128,128]{1,0:T(8,128)S(1)} %get-tuple-element.48.refs_2_.refs_1_, bf16[128,176]{1,0:T(8,128)(2,1)S(1)} %get-tuple-element.49.refs_3_.refs_2_, ...), custom_call_target="tpu_custom_call" | custom-call | flops 805306368 | bytes 8388608 | tf_op jit(solution)/shard_map/pallas_call | solution.py:511
  45.9 0.6 collective-permute-done.15.refs_6_
  46.5 2.7 %shard_map.84 = (bf16[8192,128]{1,0:T(8,128)(2,1)S(1)}, bf16[1024,128]{1,0:T(8,128)(2,1)S(1)}, bf16[1024,128]{1,0:T(8,128)(2,1)S(1)}, bf16[1024,128]{1,0:T(8,128)(2,1)S(1)}, bf16[128,128]{1,0:T(8,128)(2,1)S(1)}) custom-call(f32[8192,128]{1,0:T(8,128)S(1)} %get-tuple-element.80.refs_0_, f32[128,128]{1,0:T(8,128)S(1)} %get-tuple-element.48.refs_2_.refs_1_, ...), custom_call_target="tpu_custom_call" | custom-call | flops 536870912 | bytes 8388608 | tf_op jit(solution)/shard_map/pallas_call | solution.py:638
  49.1 2.7 %collective-permute-start.17 = (bf16[128,128]{1,0:T(8,128)(2,1)S(1)}, bf16[128,128]{1,0:T(8,128)(2,1)S(1)}, u32[]{:S(2)}, u32[]{:S(2)}) collective-permute-start(bf16[128,128]{1,0:T(8,128)(2,1)S(1)} %get-tuple-element.88), channel_id=1, source_target_pairs={{0,1},{1,0},{2,3},{3,2},{4,5},{5,4},{6,7},{7,6},{8,9},{9,8},{10,11... | collective-permute-start | bytes 98312 | tf_op jit(solution)/shard_map/ppermute | solution.py:252
  51.8 0.5 collective-permute-start.19
  52.3 1.4 %collective-permute-done.17.refs_5_ = bf16[128,128]{1,0:T(8,128)(2,1)S(1)} collective-permute-done((bf16[128,128]{1,0:T(8,128)(2,1)S(1)}, bf16[128,128]{1,0:T(8,128)(2,1)S(1)}, u32[]{:S(2)}, u32[]{:S(2)}) %collective-permute-start.17) | collective-permute-done | bytes 32800 | tf_op jit(solution)/shard_map/ppermute | solution.py:252
  53.7 2.0 %collective-permute-start.20 = (bf16[1024,128]{1,0:T(8,128)(2,1)S(1)}, bf16[1024,128]{1,0:T(8,128)(2,1)S(1)}, u32[]{:S(2)}, u32[]{:S(2)}) collective-permute-start(bf16[1024,128]{1,0:T(8,128)(2,1)S(1)} %get-tuple-element.91), channel_id=1, source_target_pairs={{0,1},{1,0},{2,3},{3,2},{4,5},{5,4},{6,7},{7,6},{8,16},{9,17},{10,... | collective-permute-start | bytes 786440 | tf_op jit(solution)/shard_map/ppermute | solution.py:252
  55.7 0.5 collective-permute-start.18
  56.2 1.1 %collective-permute-done.18.refs_6_ = bf16[128,128]{1,0:T(8,128)(2,1)S(1)} collective-permute-done((bf16[128,128]{1,0:T(8,128)(2,1)S(1)}, bf16[128,128]{1,0:T(8,128)(2,1)S(1)}, u32[]{:S(2)}, u32[]{:S(2)}) %collective-permute-start.18) | collective-permute-done | bytes 32800 | tf_op jit(solution)/shard_map/ppermute | solution.py:252
  57.3 2.0 %shard_map.85.refs_0_ = f32[8192,128]{1,0:T(8,128)S(1)} custom-call(bf16[8192,128]{1,0:T(8,128)(2,1)S(1)} %get-tuple-element.84.refs_0_, bf16[8192,128]{1,0:T(8,128)(2,1)S(1)} %get-tuple-element.85.refs_1_, f32[128,128]{1,0:T(8,128)S(1)} %get-tuple-element.48.refs_2_.refs_1_, bf16[128,176]{1,0:T(8,128)(2,1)S(1)} %get-tuple-element.49.refs_3_.refs_2_, ...), custom_call_target="tpu_custom_call" | custom-call | flops 805306368 | bytes 8388608 | tf_op jit(solution)/shard_map/pallas_call | solution.py:511
  59.3 0.8 %collective-permute-done.20.refs_6_ = bf16[1024,128]{1,0:T(8,128)(2,1)S(1)} collective-permute-done((bf16[1024,128]{1,0:T(8,128)(2,1)S(1)}, bf16[1024,128]{1,0:T(8,128)(2,1)S(1)}, u32[]{:S(2)}, u32[]{:S(2)}) %collective-permute-start.20) | collective-permute-done | bytes 262176 | tf_op jit(solution)/shard_map/ppermute | solution.py:252
  60.0 1.6 %shard_map.86 = bf16[8192,128]{1,0:T(8,128)(2,1)} custom-call(f32[8192,128]{1,0:T(8,128)S(1)} %shard_map.85.refs_0_, f32[128,128]{1,0:T(8,128)S(1)} %get-tuple-element.48.refs_2_.refs_1_, bf16[128,176]{1,0:T(8,128)(2,1)S(1)} %get-tuple-element.49.refs_3_.refs_2_, bf16[256,256]{1,0:T(8,128)(2,1)S(1)} %get-tuple-element.62.refs_3_, ...), custom_call_target="tpu_custom_call" | custom-call | flops 536870912 | bytes 8388608 | tf_op jit(solution)/shard_map/pallas_call | solution.py:638
  (32 shorter events, 1.4 us)
Async XLA Ops:
  0.6 9.7 %copy-start.3 = (f32[8,8,128]{2,1,0:T(8,128)S(1)}, f32[8,8,128]{2,1,0:T(8,128)}, u32[]{:S(2)}) copy-start(f32[8,8,128]{2,1,0:T(8,128)} %param.8) | copy-start | bytes 98308
  5.9 9.5 %collective-permute-start.1 = (bf16[1024,128]{1,0:T(8,128)(2,1)}, bf16[1024,128]{1,0:T(8,128)(2,1)S(1)}, u32[]{:S(2)}, u32[]{:S(2)}) collective-permute-start(bf16[1024,128]{1,0:T(8,128)(2,1)} %get-tuple-element.54), channel_id=1, source_target_pairs={{0,4},{1,5},{2,6},{3,7},{4,0},{5,1},{6,2},{7,3},{8,12},{9,13},{10,... | collective-permute-start | bytes 786440 | tf_op jit(solution)/shard_map/ppermute | solution.py:252
  8.9 8.0 %collective-permute-start = (bf16[1024,128]{1,0:T(8,128)(2,1)}, bf16[1024,128]{1,0:T(8,128)(2,1)S(1)}, u32[]{:S(2)}, u32[]{:S(2)}) collective-permute-start(bf16[1024,128]{1,0:T(8,128)(2,1)} %get-tuple-element.55.refs_0_), channel_id=1, source_target_pairs={{0,16},{8,24},{16,0},{24,8},{1,17},{9,25},{17,1},{25,9},{2,18},{10... | collective-permute-start | bytes 786440 | tf_op jit(solution)/shard_map/ppermute | solution.py:673
  10.4 6.5 %copy-start.2 = (bf16[1024,128]{1,0:T(8,128)(2,1)S(1)}, bf16[1024,128]{1,0:T(8,128)(2,1)}, u32[]{:S(2)}) copy-start(bf16[1024,128]{1,0:T(8,128)(2,1)} %get-tuple-element.55.refs_0_) | copy-start | bytes 786436
  10.4 18.4 %copy-start.1 = (bf16[128,8,8,128]{3,2,1,0:T(8,128)(2,1)S(1)}, bf16[128,8,8,128]{3,2,1,0:T(8,128)(2,1)}, u32[]{:S(2)}) copy-start(bf16[128,8,8,128]{3,2,1,0:T(8,128)(2,1)} %param.7) | copy-start | bytes 6291460
  13.8 15.0 %copy-start = (bf16[128,8,8,128]{3,2,1,0:T(8,128)(2,1)S(1)}, bf16[128,8,8,128]{3,2,1,0:T(8,128)(2,1)}, u32[]{:S(2)}) copy-start(bf16[128,8,8,128]{3,2,1,0:T(8,128)(2,1)} %param.6) | copy-start | bytes 6291460
  16.9 2.1 %collective-permute-start.2 = (bf16[1024,128]{1,0:T(8,128)(2,1)S(1)}, bf16[1024,128]{1,0:T(8,128)(2,1)S(1)}, u32[]{:S(2)}, u32[]{:S(2)}) collective-permute-start(bf16[1024,128]{1,0:T(8,128)(2,1)S(1)} %copy-done.2), channel_id=1, source_target_pairs={{0,8},{8,0},{16,24},{24,16},{1,9},{9,1},{17,25},{25,17},{2,10},{10... | collective-permute-start | bytes 786440 | tf_op jit(solution)/shard_map/ppermute | solution.py:673
  16.9 2.1 %collective-permute-start.3 = (bf16[1024,128]{1,0:T(8,128)(2,1)S(1)}, bf16[1024,128]{1,0:T(8,128)(2,1)S(1)}, u32[]{:S(2)}, u32[]{:S(2)}) collective-permute-start(bf16[1024,128]{1,0:T(8,128)(2,1)S(1)} %collective-permute-done.refs_2_), channel_id=1, source_target_pairs={{0,8},{8,0},{16,24},{24,16},{1,9},{9,1},{17,25},{25,17},{2,10},{10... | collective-permute-start | bytes 786440 | tf_op jit(solution)/shard_map/ppermute | solution.py:673
  17.4 6.4 %collective-permute-start.6 = (bf16[1024,128]{1,0:T(8,128)(2,1)S(1)}, bf16[1024,128]{1,0:T(8,128)(2,1)S(1)}, u32[]{:S(2)}, u32[]{:S(2)}) collective-permute-start(bf16[1024,128]{1,0:T(8,128)(2,1)S(1)} %get-tuple-element.65), channel_id=1, source_target_pairs={{0,1},{1,0},{2,3},{3,2},{4,5},{5,4},{6,7},{7,6},{8,16},{9,17},{10,... | collective-permute-start | bytes 786440 | tf_op jit(solution)/shard_map/ppermute | solution.py:252
  18.9 4.8 %collective-permute-start.7 = (bf16[1024,128]{1,0:T(8,128)(2,1)S(1)}, bf16[1024,128]{1,0:T(8,128)(2,1)S(1)}, u32[]{:S(2)}, u32[]{:S(2)}) collective-permute-start(bf16[1024,128]{1,0:T(8,128)(2,1)S(1)} %get-tuple-element.66), channel_id=1, source_target_pairs={{0,8},{1,9},{2,10},{3,11},{4,12},{5,13},{6,14},{7,15},{8,0},{9,1},... | collective-permute-start | bytes 786440 | tf_op jit(solution)/shard_map/ppermute | solution.py:252
  19.7 4.5 %collective-permute-start.8 = (f32[128,128]{1,0:T(8,128)S(1)}, f32[128,128]{1,0:T(8,128)S(1)}, u32[]{:S(2)}, u32[]{:S(2)}) collective-permute-start(f32[128,128]{1,0:T(8,128)S(1)} %get-tuple-element.68), channel_id=1, source_target_pairs={{0,4},{4,0},{1,5},{5,1},{2,6},{6,2},{3,7},{7,3},{8,12},{12,8},{9,1... | collective-permute-start | bytes 196616 | tf_op jit(solution)/shard_map/ppermute | solution.py:206
  20.3 8.5 %collective-permute-start.5 = (bf16[128,128]{1,0:T(8,128)(2,1)S(1)}, bf16[128,128]{1,0:T(8,128)(2,1)S(1)}, u32[]{:S(2)}, u32[]{:S(2)}) collective-permute-start(bf16[128,128]{1,0:T(8,128)(2,1)S(1)} %get-tuple-element.61), channel_id=1, source_target_pairs={{0,8},{1,2},{2,1},{3,11},{4,12},{5,6},{6,5},{7,15},{8,0},{9,10},{1... | collective-permute-start | bytes 98312 | tf_op jit(solution)/shard_map/ppermute | solution.py:252
  20.5 8.3 %collective-permute-start.4 = (bf16[128,128]{1,0:T(8,128)(2,1)S(1)}, bf16[128,128]{1,0:T(8,128)(2,1)S(1)}, u32[]{:S(2)}, u32[]{:S(2)}) collective-permute-start(bf16[128,128]{1,0:T(8,128)(2,1)S(1)} %get-tuple-element.61), channel_id=1, source_target_pairs={{0,1},{1,0},{2,3},{3,2},{4,5},{5,4},{6,7},{7,6},{8,9},{9,8},{10,11... | collective-permute-start | bytes 98312 | tf_op jit(solution)/shard_map/ppermute | solution.py:252
  24.4 6.5 %collective-permute-start.9 = (f32[64,128]{1,0:T(8,128)S(1)}, f32[64,128]{1,0:T(8,128)S(1)}, u32[]{:S(2)}, u32[]{:S(2)}) collective-permute-start(f32[64,128]{1,0:T(8,128)S(1)} %get-tuple-element.71), channel_id=1, source_target_pairs={{0,3},{1,2},{2,1},{3,0},{4,7},{5,6},{6,5},{7,4},{8,11},{9,10},{10,... | collective-permute-start | bytes 98312 | tf_op jit(solution)/shard_map/ppermute | solution.py:211
  27.8 4.8 %collective-permute-start.10 = (f32[64,128]{1,0:T(8,128)S(1)}, f32[64,128]{1,0:T(8,128)S(1)}, u32[]{:S(2)}, u32[]{:S(2)}) collective-permute-start(f32[64,128]{1,0:T(8,128)S(1)} %get-tuple-element.72), channel_id=1, source_target_pairs={{0,2},{1,3},{2,0},{3,1},{4,6},{5,7},{6,4},{7,5},{8,10},{9,11},{10,... | collective-permute-start | bytes 98312 | tf_op jit(solution)/shard_map/ppermute | solution.py:211
  27.8 4.8 %collective-permute-start.11 = (f32[64,128]{1,0:T(8,128)S(1)}, f32[64,128]{1,0:T(8,128)S(1)}, u32[]{:S(2)}, u32[]{:S(2)}) collective-permute-start(f32[64,128]{1,0:T(8,128)S(1)} %get-tuple-element.73), channel_id=1, source_target_pairs={{0,1},{1,0},{2,3},{3,2},{4,5},{5,4},{6,7},{7,6},{8,9},{9,8},{10,11... | collective-permute-start | bytes 98312 | tf_op jit(solution)/shard_map/ppermute | solution.py:211
  28.8 3.8 %copy-start.4 = (s32[1,1,1,32]{3,2,1,0:T(1,128)S(1)}, s32[1,1,1,32]{3,2,1,0:T(1,128)}, u32[]{:S(2)}) copy-start(s32[1,1,1,32]{3,2,1,0:T(1,128)} %refs_8_.3) | copy-start | bytes 388
  36.2 3.9 %collective-permute-start.12 = (bf16[128,128]{1,0:T(8,128)(2,1)S(1)}, bf16[128,128]{1,0:T(8,128)(2,1)S(1)}, u32[]{:S(2)}, u32[]{:S(2)}) collective-permute-start(bf16[128,128]{1,0:T(8,128)(2,1)S(1)} %get-tuple-element.77), channel_id=1, source_target_pairs={{0,1},{1,0},{2,3},{3,2},{4,5},{5,4},{6,7},{7,6},{8,9},{9,8},{10,11... | collective-permute-start | bytes 98312 | tf_op jit(solution)/shard_map/ppermute | solution.py:252
  36.3 9.6 %collective-permute-start.14 = (bf16[1024,128]{1,0:T(8,128)(2,1)S(1)}, bf16[1024,128]{1,0:T(8,128)(2,1)S(1)}, u32[]{:S(2)}, u32[]{:S(2)}) collective-permute-start(bf16[1024,128]{1,0:T(8,128)(2,1)S(1)} %get-tuple-element.81), channel_id=1, source_target_pairs={{0,4},{1,5},{2,6},{3,7},{4,0},{5,1},{6,2},{7,3},{8,12},{9,13},{10,... | collective-permute-start | bytes 786440 | tf_op jit(solution)/shard_map/ppermute | solution.py:252
  40.1 6.4 %collective-permute-start.15 = (bf16[1024,128]{1,0:T(8,128)(2,1)S(1)}, bf16[1024,128]{1,0:T(8,128)(2,1)S(1)}, u32[]{:S(2)}, u32[]{:S(2)}) collective-permute-start(bf16[1024,128]{1,0:T(8,128)(2,1)S(1)} %get-tuple-element.82), channel_id=1, source_target_pairs={{0,1},{1,0},{2,3},{3,2},{4,5},{5,4},{6,7},{7,6},{8,16},{9,17},{10,... | collective-permute-start | bytes 786440 | tf_op jit(solution)/shard_map/ppermute | solution.py:252
  40.2 6.3 %collective-permute-start.16 = (bf16[1024,128]{1,0:T(8,128)(2,1)S(1)}, bf16[1024,128]{1,0:T(8,128)(2,1)S(1)}, u32[]{:S(2)}, u32[]{:S(2)}) collective-permute-start(bf16[1024,128]{1,0:T(8,128)(2,1)S(1)} %get-tuple-element.83), channel_id=1, source_target_pairs={{0,8},{1,9},{2,10},{3,11},{4,12},{5,13},{6,14},{7,15},{8,0},{9,1},... | collective-permute-start | bytes 786440 | tf_op jit(solution)/shard_map/ppermute | solution.py:252
  41.8 1.2 %collective-permute-start.13 = (bf16[128,128]{1,0:T(8,128)(2,1)S(1)}, bf16[128,128]{1,0:T(8,128)(2,1)S(1)}, u32[]{:S(2)}, u32[]{:S(2)}) collective-permute-start(bf16[128,128]{1,0:T(8,128)(2,1)S(1)} %get-tuple-element.77), channel_id=1, source_target_pairs={{0,8},{1,2},{2,1},{3,11},{4,12},{5,6},{6,5},{7,15},{8,0},{9,10},{1... | collective-permute-start | bytes 98312 | tf_op jit(solution)/shard_map/ppermute | solution.py:252
  49.1 4.6 %collective-permute-start.17 = (bf16[128,128]{1,0:T(8,128)(2,1)S(1)}, bf16[128,128]{1,0:T(8,128)(2,1)S(1)}, u32[]{:S(2)}, u32[]{:S(2)}) collective-permute-start(bf16[128,128]{1,0:T(8,128)(2,1)S(1)} %get-tuple-element.88), channel_id=1, source_target_pairs={{0,1},{1,0},{2,3},{3,2},{4,5},{5,4},{6,7},{7,6},{8,9},{9,8},{10,11... | collective-permute-start | bytes 98312 | tf_op jit(solution)/shard_map/ppermute | solution.py:252
  51.8 7.5 %collective-permute-start.19 = (bf16[1024,128]{1,0:T(8,128)(2,1)S(1)}, bf16[1024,128]{1,0:T(8,128)(2,1)S(1)}, u32[]{:S(2)}, u32[]{:S(2)}) collective-permute-start(bf16[1024,128]{1,0:T(8,128)(2,1)S(1)} %get-tuple-element.90), channel_id=1, source_target_pairs={{0,4},{1,5},{2,6},{3,7},{4,0},{5,1},{6,2},{7,3},{8,12},{9,13},{10,... | collective-permute-start | bytes 786440 | tf_op jit(solution)/shard_map/ppermute | solution.py:252
  53.7 6.4 %collective-permute-start.20 = (bf16[1024,128]{1,0:T(8,128)(2,1)S(1)}, bf16[1024,128]{1,0:T(8,128)(2,1)S(1)}, u32[]{:S(2)}, u32[]{:S(2)}) collective-permute-start(bf16[1024,128]{1,0:T(8,128)(2,1)S(1)} %get-tuple-element.91), channel_id=1, source_target_pairs={{0,1},{1,0},{2,3},{3,2},{4,5},{5,4},{6,7},{7,6},{8,16},{9,17},{10,... | collective-permute-start | bytes 786440 | tf_op jit(solution)/shard_map/ppermute | solution.py:252
  55.7 4.4 %collective-permute-start.21 = (bf16[1024,128]{1,0:T(8,128)(2,1)S(1)}, bf16[1024,128]{1,0:T(8,128)(2,1)S(1)}, u32[]{:S(2)}, u32[]{:S(2)}) collective-permute-start(bf16[1024,128]{1,0:T(8,128)(2,1)S(1)} %get-tuple-element.92), channel_id=1, source_target_pairs={{0,8},{1,9},{2,10},{3,11},{4,12},{5,13},{6,14},{7,15},{8,0},{9,1},... | collective-permute-start | bytes 786440 | tf_op jit(solution)/shard_map/ppermute | solution.py:252
  55.7 1.6 %collective-permute-start.18 = (bf16[128,128]{1,0:T(8,128)(2,1)S(1)}, bf16[128,128]{1,0:T(8,128)(2,1)S(1)}, u32[]{:S(2)}, u32[]{:S(2)}) collective-permute-start(bf16[128,128]{1,0:T(8,128)(2,1)S(1)} %get-tuple-element.88), channel_id=1, source_target_pairs={{0,8},{1,2},{2,1},{3,11},{4,12},{5,6},{6,5},{7,15},{8,0},{9,10},{1... | collective-permute-start | bytes 98312 | tf_op jit(solution)/shard_map/ppermute | solution.py:252

commit v14 on v13

--- a/solution.py
+++ b/solution.py
@@ -438,6 +438,16 @@
     return beside(jnp.concatenate(rows, axis=0).astype(BF))
 
 
+def halo_ends(shape, end_refs, sides):
+    even = lax.axis_index("gz") % 2 == 0
+    filled = (iota((shape.block, 2 * shape.cells), 1) < shape.cells) == even
+    zs = 0.0
+    for turn in range(shape.ends):
+        wanted = (filled == (turn == 0)) & has_neighbour("gz", turn)
+        zs = jnp.where(wanted, end_refs[turn][sides, :].astype(F32), zs)
+    return expand(shape, zs, z_mask(shape, 1))
+
+
 def build_cells(shape, cell_ref, cell_m):
     slots = cell_ref.shape[3]
     cell = jnp.concatenate([cell_ref[0, 0]] * 2, axis=1)
@@ -446,11 +456,11 @@
     return iota((shape.cells, 2 * slots), 0) == cell // shape.lanes
 
 
-def base_kernel(shape, with_flux, *refs):
+def base_kernel(shape, ends, with_flux, *refs):
     refs = list(refs)
     take = lambda count: [refs.pop(0) for _ in range(count)]
     field_ref, load_ref, weight, near_m, line_m = take(5)
-    end_refs = take(shape.ends)
+    end_refs = take(ends)
     if with_flux:
         phi, cell_ref = take(2)
     (base_ref,) = take(1)
@@ -463,19 +473,13 @@
 
     cells, lanes = shape.cells, shape.lanes
     weights = weight[...]
-    mask = z_mask(shape, 1)
-    even = lax.axis_index("gz") % 2 == 0
-    filled = (iota((shape.block, 2 * cells), 1) < cells) == even
     for step in range(shape.sides // shape.block):
         sides = slice(step * shape.block, (step + 1) * shape.block)
         at = step * shape.block * cells
-        zs = 0.0
-        for turn in range(shape.ends):
-            wanted = (filled == (turn == 0)) & has_neighbour("gz", turn)
-            zs = jnp.where(wanted, end_refs[turn][sides, :].astype(F32), zs)
-        values = field_ref[at : at + shape.block * cells, :]
-        left = jnp.concatenate([beside(values), expand(shape, zs, mask)], axis=1)
-        lines[step] = dot(left, line_m[...])
+        left = beside(field_ref[at : at + shape.block * cells, :])
+        if ends:
+            left = jnp.concatenate([left, halo_ends(shape, end_refs, sides)], axis=1)
+        lines[step] = dot(left, line_m[: left.shape[1], :])
         if with_flux:
             placed[step] = dot_nt(expand(shape, phi[sides, :], cell_mask), cell_m[...])
         for index in range(shape.half // shape.chunk):
@@ -497,7 +501,7 @@
                 base_ref[span, :] = (1.0 - OMEGA) * centre + weights * (source + near[:, cols])
 
 
-def sweep_base(shape, field, load, tables, ends, phi=None, flux_cell=None):
+def sweep_base(shape, field, load, tables, ends=(), phi=None, flux_cell=None):
     steps = shape.sides // shape.block
     half = (steps, shape.half_rows, 2 * shape.lanes)
     operands = [field, load, *tables[:3], *ends]
@@ -509,7 +513,7 @@
         scratch.append(pltpu.VMEM((2 * shape.lanes, 2 * phi.shape[1]), BF))
         scratch.append(pltpu.VMEM(half, F32))
     return pl.pallas_call(
-        functools.partial(base_kernel, shape, phi is not None),
+        functools.partial(base_kernel, shape, len(ends), phi is not None),
         in_specs=[WHOLE] * len(operands),
         out_specs=[WHOLE] * len(shapes),
         out_shape=shapes,
@@ -521,12 +525,13 @@
     )(*operands)
 
 
-def finish_kernel(shape, recvs, last, *refs):
+def finish_kernel(shape, ends, recvs, last, *refs):
     with_flux = recvs > 0
     refs = list(refs)
     take = lambda count: [refs.pop(0) for _ in range(count)]
-    base_ref, weight, near_m, ends_m, rsum = take(5)
+    base_ref, weight, near_m, line_m, ends_m, rsum = take(6)
     halo_refs = take(len(shape.faces))
+    end_refs = take(ends)
     if with_flux:
         (cell_ref,) = take(1)
         recv_refs = take(recvs)
@@ -541,6 +546,8 @@
         out_ref, out_sems = take(2)
     else:
         (tall,) = take(1)
+    if ends:
+        (lines,) = take(1)
     if with_flux:
         cell_m, placed = take(2)
 
@@ -561,8 +568,10 @@
 
     def work(step):
         at = step * shape.block
+        sides = slice(at, at + shape.block)
+        if ends:
+            lines[step] = dot(halo_ends(shape, end_refs, sides), line_m[2 * lanes :, :])
         if with_flux:
-            sides = slice(at, at + shape.block)
             placed[step] = dot_nt(expand(shape, phi[sides, :], cell_mask), cell_m[...])
         for index in range(shape.half // shape.chunk):
             offset = index * shape.rows
@@ -576,6 +585,8 @@
                     stack.append(ref[first : first + shape.chunk * length, :])
                 stacks.append(jnp.concatenate(stack, axis=0))
             near = dot(near_m[:, shape.rows :], jnp.concatenate(stacks, axis=1))
+            if ends:
+                near = near + lines[step, offset : offset + shape.rows, :]
             if with_flux:
                 near = near + placed[step, offset : offset + shape.rows, :]
             for part, start in enumerate(starts):
@@ -609,11 +620,11 @@
         emit(steps - 1)
 
 
-def sweep_finish(shape, base, tables, halos, flux_cell=None, recv=(), last=False):
+def sweep_finish(shape, base, tables, halos, ends=(), flux_cell=None, recv=(), last=False):
     lanes, cells = shape.lanes, shape.cells
     steps = shape.sides // shape.block
-    weight, near_m, _, ends_m, rsum = tables
-    operands = [base, weight, near_m, ends_m, rsum, *halos]
+    half = (steps, shape.half_rows, 2 * lanes)
+    operands = [base, *tables, *halos, *ends]
     out_shapes = [jax.ShapeDtypeStruct(base.shape, BF)]
     if last:
         scratch = [pltpu.VMEM(base.shape, BF), pltpu.SemaphoreType.DMA((steps,))]
@@ -621,6 +632,8 @@
         out_shapes += face_shapes(shape, shape.faces)
         out_shapes.append(jax.ShapeDtypeStruct((shape.sides, 2 * cells), BF))
         scratch = [pltpu.VMEM((steps, shape.block * cells, lanes), F32)]
+    if ends:
+        scratch.append(pltpu.VMEM(half, F32))
     if recv:
         slots = flux_cell.shape[3]
         operands += [flux_cell, *recv]
@@ -630,13 +643,13 @@
         ]
         scratch += [
             pltpu.VMEM((2 * lanes, 4 * slots), BF),
-            pltpu.VMEM((steps, shape.half_rows, 2 * lanes), F32),
+            pltpu.VMEM(half, F32),
         ]
     out_specs = [WHOLE] * len(out_shapes)
     if last:
         out_specs = [pl.BlockSpec(memory_space=pltpu.HBM)]
     return pl.pallas_call(
-        functools.partial(finish_kernel, shape, len(recv), last),
+        functools.partial(finish_kernel, shape, len(ends), len(recv), last),
         in_specs=[WHOLE] * len(operands),
         out_specs=out_specs,
         out_shape=out_shapes,
@@ -656,15 +669,7 @@
     return [swap(ends, "gz", turn) for turn in range(shape.ends)]
 
 
-def exchange(shape, faces, ends):
-    count = len(shape.outer)
-    tips = swap_ends(shape, ends)
-    along_col = swap_faces(shape.outer, faces[:count])
-    inner, tips[0] = lax.optimization_barrier((faces[count:], tips[0]))
-    return along_col + swap_faces(shape.inner, inner), tips
-
-
-def row_gather(trace, hidden):
+def row_gather(trace, hidden, late):
     peers = lax.axis_size("row")
     held = {0: trace}
     bit = peers // 2
@@ -672,10 +677,11 @@
         pairs = [(i, i ^ bit) for i in range(peers)]
         fresh = {key ^ bit: lax.ppermute(held[key], "row", pairs) for key in sorted(held, reverse=True)}
         if bit == peers // 2:
-            held, fresh, hidden = lax.optimization_barrier((held, fresh, hidden))
+            fresh, hidden = lax.optimization_barrier((fresh, hidden))
+            fresh, late = lax.optimization_barrier((fresh, late))
         held.update(fresh)
         bit //= 2
-    return [held[key] for key in range(peers)], hidden
+    return [held[key] for key in range(peers)], hidden, late
 
 
 def per_device(volume_field, volume_load, coefficient, surface_block, trace_cell, flux_cell):
@@ -696,7 +702,7 @@
     inner, held, tables = firsts[:count], firsts[count], firsts[count + 1 :]
     *inner, ends = inner
     along_col = swap_faces(shape.outer, outer)
-    parts, (inner, along_col) = row_gather(trace, (inner, along_col))
+    parts, inner, along_col = row_gather(trace, inner, along_col)
     along_row = swap_faces(shape.inner, inner)
     recv, ends = flux_sums(parts, held, along_row, ends)
     tips = swap_ends(shape, ends)
@@ -705,12 +711,12 @@
     current, *faces, ends, phi, surface_flux = sweep_finish(
         shape, base, tables, along_col + along_row, flux_cell=flux_cell, recv=recv
     )
-    halos, tips = exchange(shape, faces, ends)
-    base, source = sweep_base(shape, current, load, tables, tips, phi, flux_cell)
-    current, *faces, ends = sweep_finish(shape, base, tables, halos)
-    halos, tips = exchange(shape, faces, ends)
-    (base,) = sweep_base(shape, current, source, tables, tips)
-    (current,) = sweep_finish(shape, base, tables, halos, last=True)
+    halos, tips = swap_faces(shape.faces, faces), swap_ends(shape, ends)
+    base, source = sweep_base(shape, current, load, tables, phi=phi, flux_cell=flux_cell)
+    current, *faces, ends = sweep_finish(shape, base, tables, halos, tips)
+    halos, tips = swap_faces(shape.faces, faces), swap_ends(shape, ends)
+    (base,) = sweep_base(shape, current, source, tables)
+    (current,) = sweep_finish(shape, base, tables, halos, tips, last=True)
     return current.reshape(volume_field.shape), surface_flux
 
 

time: 62 us -> 57.2 us (0.923)
  waiting for transfers between devices: 13.7 us -> 8.67 us
    ppermute x15, waiting for transfers between devices: 9.97 us -> 5.61 us  [swap(): return lax.ppermute(value, axes, pairs)]
    ppermute x15, starting transfers between devices: 16 us -> 14.4 us  [swap(): return lax.ppermute(value, axes, pairs)]
    ppermute x3, starting transfers between devices: 2 us -> 3.01 us  [row_gather(): lax.ppermute(held[key], 'row', pairs)]
    ppermute x1, starting transfers between devices: 0.6 us -> 1.57 us  [flux_sums(): other = lax.ppermute(other, 'col', [(0, 1), (1, 0)])]
  transfers between devices with their start and end apart: 22 -> 22, of which waited for: 11 -> 5; matrix products, arithmetic and copies ran while one was open for 0% -> 0% of each run, Pallas kernels for 18% -> 18%
where the time goes in v14:
time: 57.2 us; the launch traced here: 57.1 us
  Pallas kernels  24 us (42%)
  starting transfers between devices  23.5 us (41%)
  waiting for transfers between devices  8.67 us (15%)
  between operations  0.95 us (2%)
    ppermute x15, starting transfers between devices, swap(): return lax.ppermute(value, axes, pairs)  14.4 us
    pallas_call x3, Pallas kernels, sweep_finish(): pl.pallas_call(functools.partial(finish_kernel, shape, len(ends), len(rec...  8.69 us
    pallas_call x3, Pallas kernels, sweep_base(): pl.pallas_call(functools.partial(base_kernel, shape, len(ends), phi is no...  5.79 us
    ppermute x15, waiting for transfers between devices, swap(): return lax.ppermute(value, axes, pairs)  5.61 us
    pallas_call x1, Pallas kernels, traces(): pl.pallas_call(functools.partial(trace_kernel, shape, stride, block), in_...  5.21 us
    ppermute x3, starting transfers between devices, flux_sums(): lax.ppermute(sent[key], 'gz', [(i, i ^ key) for i in range(gzs)])  4.45 us
    pallas_call x1, Pallas kernels, first_faces(): pl.pallas_call(functools.partial(faces_kernel, shape, slots), in_specs=[h...  3.46 us
    ppermute x3, starting transfers between devices, row_gather(): lax.ppermute(held[key], 'row', pairs)  3.01 us
  transfers between devices with their start and end apart: 22, of which 5 were waited for; matrix products, arithmetic and copies ran while one was open for 0% of the time, Pallas kernels for 18%

profile of v14, /device:TPU:0, one launch (start us, length us, event | category | flops | bytes accessed | tf_op | source)
XLA Modules:
  0.0 57.1 jit_solution(1734031996752518614)
XLA Ops:
  0.6 5.2 %shard_map.78 = (bf16[1024,128]{1,0:T(8,128)(2,1)}, bf16[1024,128]{1,0:T(8,128)(2,1)}) custom-call(bf16[128,64,128]{2,1,0:T(8,128)(2,1)} %bitcast.5, s32[1,1,1,1024]{3,2,1,0:T(1,128)} %cell_ref.1), custom_call_target="tpu_custom_call" | custom-call | flops 536870912 | bytes 2097152 | tf_op jit(solution)/shard_map/pallas_call | solution.py:102
  5.9 3.0 %collective-permute-start.1 = (bf16[1024,128]{1,0:T(8,128)(2,1)}, bf16[1024,128]{1,0:T(8,128)(2,1)S(1)}, u32[]{:S(2)}, u32[]{:S(2)}) collective-permute-start(bf16[1024,128]{1,0:T(8,128)(2,1)} %get-tuple-element.45.refs_0_), channel_id=1, source_target_pairs={{0,16},{8,24},{16,0},{24,8},{1,17},{9,25},{17,1},{25,9},{2,18},{10... | collective-permute-start | bytes 786440 | tf_op jit(solution)/shard_map/ppermute | solution.py:678
  8.9 1.5 %collective-permute-start.2 = (bf16[1024,128]{1,0:T(8,128)(2,1)}, bf16[1024,128]{1,0:T(8,128)(2,1)S(1)}, u32[]{:S(2)}, u32[]{:S(2)}) collective-permute-start(bf16[1024,128]{1,0:T(8,128)(2,1)} %get-tuple-element.49), channel_id=1, source_target_pairs={{0,4},{1,5},{2,6},{3,7},{4,0},{5,1},{6,2},{7,3},{8,12},{9,13},{10,... | collective-permute-start | bytes 786440 | tf_op jit(solution)/shard_map/ppermute | solution.py:252
  10.4 3.5 %shard_map.77 = (bf16[1024,128]{1,0:T(8,128)(2,1)S(1)}, bf16[1024,128]{1,0:T(8,128)(2,1)S(1)}, bf16[128,128]{1,0:T(8,128)(2,1)S(1)}, bf16[4,256,1024]{2,1,0:T(8,...) custom-call(bf16[8192,128]{1,0:T(8,128)(2,1)} %bitcast.6, ...), custom_call_target="tpu_custom_call" | custom-call | flops 134217728 | bytes 4194304 | tf_op jit(solution)/shard_map/pallas_call | solution.py:415
  13.8 0.0 copy-start
  13.9 1.5 %collective-permute-done.1.refs_2_ = bf16[1024,128]{1,0:T(8,128)(2,1)S(1)} collective-permute-done((bf16[1024,128]{1,0:T(8,128)(2,1)}, bf16[1024,128]{1,0:T(8,128)(2,1)S(1)}, u32[]{:S(2)}, u32[]{:S(2)}) %collective-permute-start.1) | collective-permute-done | bytes 262176 | tf_op jit(solution)/shard_map/ppermute | solution.py:678
  15.4 1.5 %collective-permute-done.2.refs_6_ = bf16[1024,128]{1,0:T(8,128)(2,1)S(1)} collective-permute-done((bf16[1024,128]{1,0:T(8,128)(2,1)}, bf16[1024,128]{1,0:T(8,128)(2,1)S(1)}, u32[]{:S(2)}, u32[]{:S(2)}) %collective-permute-start.2) | collective-permute-done | bytes 262176 | tf_op jit(solution)/shard_map/ppermute | solution.py:252
  16.8 1.6 %collective-permute-start.6 = (bf16[1024,128]{1,0:T(8,128)(2,1)S(1)}, bf16[1024,128]{1,0:T(8,128)(2,1)S(1)}, u32[]{:S(2)}, u32[]{:S(2)}) collective-permute-start(bf16[1024,128]{1,0:T(8,128)(2,1)S(1)} %get-tuple-element.59), channel_id=1, source_target_pairs={{0,1},{1,0},{2,3},{3,2},{4,5},{5,4},{6,7},{7,6},{8,16},{9,17},{10,... | collective-permute-start | bytes 786440 | tf_op jit(solution)/shard_map/ppermute | solution.py:252
  18.4 0.7 %shard_map.79 = (f32[128,128]{1,0:T(8,128)S(1)}, f32[128,128]{1,0:T(8,128)S(1)}) custom-call(bf16[1024,128]{1,0:T(8,128)(2,1)S(1)} %copy-done.2, bf16[1024,128]{1,0:T(8,128)(2,1)S(1)} %collective-permute-done.refs_1_, bf16[1024,128]{1,0:T(8,128)(2,1)S(1)} %collective-permute-done.1.refs_2_, bf16[1024,128]{1,0:T(8,128)(2,1)S(1)} %collective-permute-done.3.refs_3_, ...), custom_call_target="tpu_custom_call" | custom-call | flops 268435456 | bytes 2097152 | tf_op jit(solution)/shard_map/pallas_call | solution.py:156
  19.2 1.6 %collective-permute-start.8 = (f32[128,128]{1,0:T(8,128)S(1)}, f32[128,128]{1,0:T(8,128)S(1)}, u32[]{:S(2)}, u32[]{:S(2)}) collective-permute-start(f32[128,128]{1,0:T(8,128)S(1)} %get-tuple-element.62), channel_id=1, source_target_pairs={{0,4},{4,0},{1,5},{5,1},{2,6},{6,2},{3,7},{7,3},{8,12},{12,8},{9,1... | collective-permute-start | bytes 196616 | tf_op jit(solution)/shard_map/ppermute | solution.py:206
  20.7 0.2 collective-permute-start.5
  21.0 2.9 %collective-permute-start.4 = (bf16[128,128]{1,0:T(8,128)(2,1)S(1)}, bf16[128,128]{1,0:T(8,128)(2,1)S(1)}, u32[]{:S(2)}, u32[]{:S(2)}) collective-permute-start(bf16[128,128]{1,0:T(8,128)(2,1)S(1)} %get-tuple-element.55), channel_id=1, source_target_pairs={{0,1},{1,0},{2,3},{3,2},{4,5},{5,4},{6,7},{7,6},{8,9},{9,8},{10,11... | collective-permute-start | bytes 98312 | tf_op jit(solution)/shard_map/ppermute | solution.py:252
  23.9 0.1 shard_map.81
  24.0 3.2 %collective-permute-start.9 = (f32[64,128]{1,0:T(8,128)S(1)}, f32[64,128]{1,0:T(8,128)S(1)}, u32[]{:S(2)}, u32[]{:S(2)}) collective-permute-start(f32[64,128]{1,0:T(8,128)S(1)} %get-tuple-element.65), channel_id=1, source_target_pairs={{0,3},{1,2},{2,1},{3,0},{4,7},{5,6},{6,5},{7,4},{8,11},{9,10},{10,... | collective-permute-start | bytes 98312 | tf_op jit(solution)/shard_map/ppermute | solution.py:211
  27.2 1.3 %collective-permute-start.11 = (f32[64,128]{1,0:T(8,128)S(1)}, f32[64,128]{1,0:T(8,128)S(1)}, u32[]{:S(2)}, u32[]{:S(2)}) collective-permute-start(f32[64,128]{1,0:T(8,128)S(1)} %get-tuple-element.67), channel_id=1, source_target_pairs={{0,1},{1,0},{2,3},{3,2},{4,5},{5,4},{6,7},{7,6},{8,9},{9,8},{10,11... | collective-permute-start | bytes 98312 | tf_op jit(solution)/shard_map/ppermute | solution.py:211
  28.5 2.0 %shard_map.80.refs_0_ = f32[8192,128]{1,0:T(8,128)S(1)} custom-call(bf16[8192,128]{1,0:T(8,128)(2,1)S(1)} %bitcast.7, bf16[8192,128]{1,0:T(8,128)(2,1)S(1)} %bitcast.8, f32[128,128]{1,0:T(8,128)S(1)} %get-tuple-element.42.refs_2_.refs_1_, bf16[128,176]{1,0:T(8,128)(2,1)S(1)} %get-tuple-element.43.refs_3_.refs_2_, ...), custom_call_target="tpu_custom_call" | custom-call | flops 805306368 | bytes 8388608 | tf_op jit(solution)/shard_map/pallas_call | solution.py:515
  30.5 1.5 %collective-permute-done.10.refs_12_ = f32[64,128]{1,0:T(8,128)S(1)} collective-permute-done((f32[64,128]{1,0:T(8,128)S(1)}, f32[64,128]{1,0:T(8,128)S(1)}, u32[]{:S(2)}, u32[]{:S(2)}) %collective-permute-start.10) | collective-permute-done | bytes 32800 | tf_op jit(solution)/shard_map/ppermute | solution.py:211
  32.0 3.5 %shard_map.82 = (bf16[8192,128]{1,0:T(8,128)(2,1)S(1)}, bf16[1024,128]{1,0:T(8,128)(2,1)S(1)}, bf16[1024,128]{1,0:T(8,128)(2,1)S(1)}, bf16[1024,128]{1,0:T(8,128...) custom-call(f32[8192,128]{1,0:T(8,128)S(1)} %shard_map.80.refs_0_, ...), custom_call_target="tpu_custom_call" | custom-call | flops 536870912 | bytes 8388608 | tf_op jit(solution)/shard_map/pallas_call | solution.py:651
  35.6 1.7 %collective-permute-start.12 = (bf16[1024,128]{1,0:T(8,128)(2,1)S(1)}, bf16[1024,128]{1,0:T(8,128)(2,1)S(1)}, u32[]{:S(2)}, u32[]{:S(2)}) collective-permute-start(bf16[1024,128]{1,0:T(8,128)(2,1)S(1)} %get-tuple-element.71), channel_id=1, source_target_pairs={{0,4},{1,5},{2,6},{3,7},{4,0},{5,1},{6,2},{7,3},{8,12},{9,13},{10,... | collective-permute-start | bytes 786440 | tf_op jit(solution)/shard_map/ppermute | solution.py:252
  37.2 0.0 collective-permute-start.13
  37.2 0.8 %collective-permute-start.14 = (bf16[1024,128]{1,0:T(8,128)(2,1)S(1)}, bf16[1024,128]{1,0:T(8,128)(2,1)S(1)}, u32[]{:S(2)}, u32[]{:S(2)}) collective-permute-start(bf16[1024,128]{1,0:T(8,128)(2,1)S(1)} %get-tuple-element.73), channel_id=1, source_target_pairs={{0,8},{1,9},{2,10},{3,11},{4,12},{5,13},{6,14},{7,15},{8,0},{9,1},... | collective-permute-start | bytes 786440 | tf_op jit(solution)/shard_map/ppermute | solution.py:252
  38.0 2.6 %collective-permute-start.15 = (bf16[128,128]{1,0:T(8,128)(2,1)S(1)}, bf16[128,128]{1,0:T(8,128)(2,1)S(1)}, u32[]{:S(2)}, u32[]{:S(2)}) collective-permute-start(bf16[128,128]{1,0:T(8,128)(2,1)S(1)} %get-tuple-element.74), channel_id=1, source_target_pairs={{0,1},{1,0},{2,3},{3,2},{4,5},{5,4},{6,7},{7,6},{8,9},{9,8},{10,11... | collective-permute-start | bytes 98312 | tf_op jit(solution)/shard_map/ppermute | solution.py:252
  40.6 2.3 %shard_map.83 = (f32[8192,128]{1,0:T(8,128)S(1)}, bf16[8192,128]{1,0:T(8,128)(2,1)S(1)}) custom-call(bf16[8192,128]{1,0:T(8,128)(2,1)S(1)} %get-tuple-element.68.refs_0_, bf16[8192,128]{1,0:T(8,128)(2,1)S(1)} %bitcast.9, f32[128,128]{1,0:T(8,128)S(1)} %get-tuple-element.42.refs_2_.refs_1_, bf16[128,176]{1,0:T(8,128)(2,1)S(1)} %get-tuple-element.43.refs_3_.refs_2_, ...), custom_call_target="tpu_custom_call" | custom-call | flops 805306368 | bytes 8388608 | tf_op jit(solution)/shard_map/pallas_call | solution.py:515
  43.0 1.3 %collective-permute-done.15.refs_9_ = bf16[128,128]{1,0:T(8,128)(2,1)S(1)} collective-permute-done((bf16[128,128]{1,0:T(8,128)(2,1)S(1)}, bf16[128,128]{1,0:T(8,128)(2,1)S(1)}, u32[]{:S(2)}, u32[]{:S(2)}) %collective-permute-start.15) | collective-permute-done | bytes 32800 | tf_op jit(solution)/shard_map/ppermute | solution.py:252
  44.3 2.8 %shard_map.84 = (bf16[8192,128]{1,0:T(8,128)(2,1)S(1)}, bf16[1024,128]{1,0:T(8,128)(2,1)S(1)}, bf16[1024,128]{1,0:T(8,128)(2,1)S(1)}, bf16[1024,128]{1,0:T(8,128)(2,1)S(1)}, bf16[128,128]{1,0:T(8,128)(2,1)S(1)}) custom-call(f32[8192,128]{1,0:T(8,128)S(1)} %get-tuple-element.70.refs_0_, f32[128,128]{1,0:T(8,128)S(1)} %get-tuple-element.42.refs_2_.refs_1_, ...), custom_call_target="tpu_custom_call" | custom-call | flops 536870912 | bytes 8388608 | tf_op jit(solution)/shard_map/pallas_call | solution.py:651
  47.1 0.4 collective-permute-start.17
  47.5 0.4 collective-permute-start.18
  47.9 0.5 collective-permute-start.21
  48.4 1.8 %collective-permute-start.20 = (bf16[128,128]{1,0:T(8,128)(2,1)S(1)}, bf16[128,128]{1,0:T(8,128)(2,1)S(1)}, u32[]{:S(2)}, u32[]{:S(2)}) collective-permute-start(bf16[128,128]{1,0:T(8,128)(2,1)S(1)} %get-tuple-element.80), channel_id=1, source_target_pairs={{0,1},{1,0},{2,3},{3,2},{4,5},{5,4},{6,7},{7,6},{8,9},{9,8},{10,11... | collective-permute-start | bytes 98312 | tf_op jit(solution)/shard_map/ppermute | solution.py:252
  50.3 1.5 %shard_map.85.refs_0_ = f32[8192,128]{1,0:T(8,128)S(1)} custom-call(bf16[8192,128]{1,0:T(8,128)(2,1)S(1)} %get-tuple-element.75.refs_0_, bf16[8192,128]{1,0:T(8,128)(2,1)S(1)} %get-tuple-element.76.refs_1_, f32[128,128]{1,0:T(8,128)S(1)} %get-tuple-element.42.refs_2_.refs_1_, bf16[128,176]{1,0:T(8,128)(2,1)S(1)} %get-tuple-element.43.refs_3_.refs_2_, ...), custom_call_target="tpu_custom_call" | custom-call | flops 805306368 | bytes 8388608 | tf_op jit(solution)/shard_map/pallas_call | solution.py:515
  51.8 2.8 %collective-permute-done.20.refs_9_ = bf16[128,128]{1,0:T(8,128)(2,1)S(1)} collective-permute-done((bf16[128,128]{1,0:T(8,128)(2,1)S(1)}, bf16[128,128]{1,0:T(8,128)(2,1)S(1)}, u32[]{:S(2)}, u32[]{:S(2)}) %collective-permute-start.20) | collective-permute-done | bytes 32800 | tf_op jit(solution)/shard_map/ppermute | solution.py:252
  54.6 2.3 %shard_map.86 = bf16[8192,128]{1,0:T(8,128)(2,1)} custom-call(f32[8192,128]{1,0:T(8,128)S(1)} %shard_map.85.refs_0_, f32[128,128]{1,0:T(8,128)S(1)} %get-tuple-element.42.refs_2_.refs_1_, bf16[128,176]{1,0:T(8,128)(2,1)S(1)} %get-tuple-element.43.refs_3_.refs_2_, bf16[512,256]{1,0:T(8,128)(2,1)S(1)} %get-tuple-element.44.refs_4_.refs_3_, ...), custom_call_target="tpu_custom_call" | custom-call | flops 536870912 | bytes 8388608 | tf_op jit(solution)/shard_map/pallas_call | solution.py:651
  (32 shorter events, 0.1 us)
Async XLA Ops:
  0.6 9.7 %copy-start.3 = (f32[8,8,128]{2,1,0:T(8,128)S(1)}, f32[8,8,128]{2,1,0:T(8,128)}, u32[]{:S(2)}) copy-start(f32[8,8,128]{2,1,0:T(8,128)} %param.8) | copy-start | bytes 98308
  5.9 9.5 %collective-permute-start.1 = (bf16[1024,128]{1,0:T(8,128)(2,1)}, bf16[1024,128]{1,0:T(8,128)(2,1)S(1)}, u32[]{:S(2)}, u32[]{:S(2)}) collective-permute-start(bf16[1024,128]{1,0:T(8,128)(2,1)} %get-tuple-element.45.refs_0_), channel_id=1, source_target_pairs={{0,16},{8,24},{16,0},{24,8},{1,17},{9,25},{17,1},{25,9},{2,18},{10... | collective-permute-start | bytes 786440 | tf_op jit(solution)/shard_map/ppermute | solution.py:678
  8.9 8.0 %collective-permute-start.2 = (bf16[1024,128]{1,0:T(8,128)(2,1)}, bf16[1024,128]{1,0:T(8,128)(2,1)S(1)}, u32[]{:S(2)}, u32[]{:S(2)}) collective-permute-start(bf16[1024,128]{1,0:T(8,128)(2,1)} %get-tuple-element.49), channel_id=1, source_target_pairs={{0,4},{1,5},{2,6},{3,7},{4,0},{5,1},{6,2},{7,3},{8,12},{9,13},{10,... | collective-permute-start | bytes 786440 | tf_op jit(solution)/shard_map/ppermute | solution.py:252
  10.4 8.1 %collective-permute-start = (bf16[1024,128]{1,0:T(8,128)(2,1)}, bf16[1024,128]{1,0:T(8,128)(2,1)S(1)}, u32[]{:S(2)}, u32[]{:S(2)}) collective-permute-start(bf16[1024,128]{1,0:T(8,128)(2,1)} %get-tuple-element.45.refs_0_), channel_id=1, source_target_pairs={{0,8},{8,0},{16,24},{24,16},{1,9},{9,1},{17,25},{25,17},{2,10},{10... | collective-permute-start | bytes 786440 | tf_op jit(solution)/shard_map/ppermute | solution.py:678
  10.4 8.1 %copy-start.2 = (bf16[1024,128]{1,0:T(8,128)(2,1)S(1)}, bf16[1024,128]{1,0:T(8,128)(2,1)}, u32[]{:S(2)}) copy-start(bf16[1024,128]{1,0:T(8,128)(2,1)} %get-tuple-element.45.refs_0_) | copy-start | bytes 786436
  10.4 18.1 %copy-start.1 = (bf16[128,8,8,128]{3,2,1,0:T(8,128)(2,1)S(1)}, bf16[128,8,8,128]{3,2,1,0:T(8,128)(2,1)}, u32[]{:S(2)}) copy-start(bf16[128,8,8,128]{3,2,1,0:T(8,128)(2,1)} %param.7) | copy-start | bytes 6291460
  13.8 14.6 %copy-start = (bf16[128,8,8,128]{3,2,1,0:T(8,128)(2,1)S(1)}, bf16[128,8,8,128]{3,2,1,0:T(8,128)(2,1)}, u32[]{:S(2)}) copy-start(bf16[128,8,8,128]{3,2,1,0:T(8,128)(2,1)} %param.6) | copy-start | bytes 6291460
  16.8 1.6 %collective-permute-start.3 = (bf16[1024,128]{1,0:T(8,128)(2,1)S(1)}, bf16[1024,128]{1,0:T(8,128)(2,1)S(1)}, u32[]{:S(2)}, u32[]{:S(2)}) collective-permute-start(bf16[1024,128]{1,0:T(8,128)(2,1)S(1)} %collective-permute-done.1.refs_2_), channel_id=1, source_target_pairs={{0,8},{8,0},{16,24},{24,16},{1,9},{9,1},{17,25},{25,17},{2,10},{10... | collective-permute-start | bytes 786440 | tf_op jit(solution)/shard_map/ppermute | solution.py:678
  16.8 7.0 %collective-permute-start.6 = (bf16[1024,128]{1,0:T(8,128)(2,1)S(1)}, bf16[1024,128]{1,0:T(8,128)(2,1)S(1)}, u32[]{:S(2)}, u32[]{:S(2)}) collective-permute-start(bf16[1024,128]{1,0:T(8,128)(2,1)S(1)} %get-tuple-element.59), channel_id=1, source_target_pairs={{0,1},{1,0},{2,3},{3,2},{4,5},{5,4},{6,7},{7,6},{8,16},{9,17},{10,... | collective-permute-start | bytes 786440 | tf_op jit(solution)/shard_map/ppermute | solution.py:252
  18.4 5.5 %collective-permute-start.7 = (bf16[1024,128]{1,0:T(8,128)(2,1)S(1)}, bf16[1024,128]{1,0:T(8,128)(2,1)S(1)}, u32[]{:S(2)}, u32[]{:S(2)}) collective-permute-start(bf16[1024,128]{1,0:T(8,128)(2,1)S(1)} %get-tuple-element.60), channel_id=1, source_target_pairs={{0,8},{1,9},{2,10},{3,11},{4,12},{5,13},{6,14},{7,15},{8,0},{9,1},... | collective-permute-start | bytes 786440 | tf_op jit(solution)/shard_map/ppermute | solution.py:252
  19.2 4.7 %collective-permute-start.8 = (f32[128,128]{1,0:T(8,128)S(1)}, f32[128,128]{1,0:T(8,128)S(1)}, u32[]{:S(2)}, u32[]{:S(2)}) collective-permute-start(f32[128,128]{1,0:T(8,128)S(1)} %get-tuple-element.62), channel_id=1, source_target_pairs={{0,4},{4,0},{1,5},{5,1},{2,6},{6,2},{3,7},{7,3},{8,12},{12,8},{9,1... | collective-permute-start | bytes 196616 | tf_op jit(solution)/shard_map/ppermute | solution.py:206
  20.7 7.7 %collective-permute-start.5 = (bf16[128,128]{1,0:T(8,128)(2,1)S(1)}, bf16[128,128]{1,0:T(8,128)(2,1)S(1)}, u32[]{:S(2)}, u32[]{:S(2)}) collective-permute-start(bf16[128,128]{1,0:T(8,128)(2,1)S(1)} %get-tuple-element.55), channel_id=1, source_target_pairs={{0,8},{1,2},{2,1},{3,11},{4,12},{5,6},{6,5},{7,15},{8,0},{9,10},{1... | collective-permute-start | bytes 98312 | tf_op jit(solution)/shard_map/ppermute | solution.py:252
  21.0 7.5 %collective-permute-start.4 = (bf16[128,128]{1,0:T(8,128)(2,1)S(1)}, bf16[128,128]{1,0:T(8,128)(2,1)S(1)}, u32[]{:S(2)}, u32[]{:S(2)}) collective-permute-start(bf16[128,128]{1,0:T(8,128)(2,1)S(1)} %get-tuple-element.55), channel_id=1, source_target_pairs={{0,1},{1,0},{2,3},{3,2},{4,5},{5,4},{6,7},{7,6},{8,9},{9,8},{10,11... | collective-permute-start | bytes 98312 | tf_op jit(solution)/shard_map/ppermute | solution.py:252
  24.0 6.5 %collective-permute-start.9 = (f32[64,128]{1,0:T(8,128)S(1)}, f32[64,128]{1,0:T(8,128)S(1)}, u32[]{:S(2)}, u32[]{:S(2)}) collective-permute-start(f32[64,128]{1,0:T(8,128)S(1)} %get-tuple-element.65), channel_id=1, source_target_pairs={{0,3},{1,2},{2,1},{3,0},{4,7},{5,6},{6,5},{7,4},{8,11},{9,10},{10,... | collective-permute-start | bytes 98312 | tf_op jit(solution)/shard_map/ppermute | solution.py:211
  27.2 4.8 %collective-permute-start.10 = (f32[64,128]{1,0:T(8,128)S(1)}, f32[64,128]{1,0:T(8,128)S(1)}, u32[]{:S(2)}, u32[]{:S(2)}) collective-permute-start(f32[64,128]{1,0:T(8,128)S(1)} %get-tuple-element.66), channel_id=1, source_target_pairs={{0,2},{1,3},{2,0},{3,1},{4,6},{5,7},{6,4},{7,5},{8,10},{9,11},{10,... | collective-permute-start | bytes 98312 | tf_op jit(solution)/shard_map/ppermute | solution.py:211
  27.2 4.8 %collective-permute-start.11 = (f32[64,128]{1,0:T(8,128)S(1)}, f32[64,128]{1,0:T(8,128)S(1)}, u32[]{:S(2)}, u32[]{:S(2)}) collective-permute-start(f32[64,128]{1,0:T(8,128)S(1)} %get-tuple-element.67), channel_id=1, source_target_pairs={{0,1},{1,0},{2,3},{3,2},{4,5},{5,4},{6,7},{7,6},{8,9},{9,8},{10,11... | collective-permute-start | bytes 98312 | tf_op jit(solution)/shard_map/ppermute | solution.py:211
  28.5 3.5 %copy-start.4 = (s32[1,1,1,32]{3,2,1,0:T(1,128)S(1)}, s32[1,1,1,32]{3,2,1,0:T(1,128)}, u32[]{:S(2)}) copy-start(s32[1,1,1,32]{3,2,1,0:T(1,128)} %refs_6_.1) | copy-start | bytes 388
  35.6 8.7 %collective-permute-start.12 = (bf16[1024,128]{1,0:T(8,128)(2,1)S(1)}, bf16[1024,128]{1,0:T(8,128)(2,1)S(1)}, u32[]{:S(2)}, u32[]{:S(2)}) collective-permute-start(bf16[1024,128]{1,0:T(8,128)(2,1)S(1)} %get-tuple-element.71), channel_id=1, source_target_pairs={{0,4},{1,5},{2,6},{3,7},{4,0},{5,1},{6,2},{7,3},{8,12},{9,13},{10,... | collective-permute-start | bytes 786440 | tf_op jit(solution)/shard_map/ppermute | solution.py:252
  37.2 7.1 %collective-permute-start.13 = (bf16[1024,128]{1,0:T(8,128)(2,1)S(1)}, bf16[1024,128]{1,0:T(8,128)(2,1)S(1)}, u32[]{:S(2)}, u32[]{:S(2)}) collective-permute-start(bf16[1024,128]{1,0:T(8,128)(2,1)S(1)} %get-tuple-element.72), channel_id=1, source_target_pairs={{0,1},{1,0},{2,3},{3,2},{4,5},{5,4},{6,7},{7,6},{8,16},{9,17},{10,... | collective-permute-start | bytes 786440 | tf_op jit(solution)/shard_map/ppermute | solution.py:252
  37.2 7.0 %collective-permute-start.14 = (bf16[1024,128]{1,0:T(8,128)(2,1)S(1)}, bf16[1024,128]{1,0:T(8,128)(2,1)S(1)}, u32[]{:S(2)}, u32[]{:S(2)}) collective-permute-start(bf16[1024,128]{1,0:T(8,128)(2,1)S(1)} %get-tuple-element.73), channel_id=1, source_target_pairs={{0,8},{1,9},{2,10},{3,11},{4,12},{5,13},{6,14},{7,15},{8,0},{9,1},... | collective-permute-start | bytes 786440 | tf_op jit(solution)/shard_map/ppermute | solution.py:252
  38.0 4.9 %collective-permute-start.16 = (bf16[128,128]{1,0:T(8,128)(2,1)S(1)}, bf16[128,128]{1,0:T(8,128)(2,1)S(1)}, u32[]{:S(2)}, u32[]{:S(2)}) collective-permute-start(bf16[128,128]{1,0:T(8,128)(2,1)S(1)} %get-tuple-element.74), channel_id=1, source_target_pairs={{0,8},{1,2},{2,1},{3,11},{4,12},{5,6},{6,5},{7,15},{8,0},{9,10},{1... | collective-permute-start | bytes 98312 | tf_op jit(solution)/shard_map/ppermute | solution.py:252
  38.0 6.2 %collective-permute-start.15 = (bf16[128,128]{1,0:T(8,128)(2,1)S(1)}, bf16[128,128]{1,0:T(8,128)(2,1)S(1)}, u32[]{:S(2)}, u32[]{:S(2)}) collective-permute-start(bf16[128,128]{1,0:T(8,128)(2,1)S(1)} %get-tuple-element.74), channel_id=1, source_target_pairs={{0,1},{1,0},{2,3},{3,2},{4,5},{5,4},{6,7},{7,6},{8,9},{9,8},{10,11... | collective-permute-start | bytes 98312 | tf_op jit(solution)/shard_map/ppermute | solution.py:252
  47.1 7.5 %collective-permute-start.17 = (bf16[1024,128]{1,0:T(8,128)(2,1)S(1)}, bf16[1024,128]{1,0:T(8,128)(2,1)S(1)}, u32[]{:S(2)}, u32[]{:S(2)}) collective-permute-start(bf16[1024,128]{1,0:T(8,128)(2,1)S(1)} %get-tuple-element.77), channel_id=1, source_target_pairs={{0,4},{1,5},{2,6},{3,7},{4,0},{5,1},{6,2},{7,3},{8,12},{9,13},{10,... | collective-permute-start | bytes 786440 | tf_op jit(solution)/shard_map/ppermute | solution.py:252
  47.5 7.1 %collective-permute-start.18 = (bf16[1024,128]{1,0:T(8,128)(2,1)S(1)}, bf16[1024,128]{1,0:T(8,128)(2,1)S(1)}, u32[]{:S(2)}, u32[]{:S(2)}) collective-permute-start(bf16[1024,128]{1,0:T(8,128)(2,1)S(1)} %get-tuple-element.78), channel_id=1, source_target_pairs={{0,1},{1,0},{2,3},{3,2},{4,5},{5,4},{6,7},{7,6},{8,16},{9,17},{10,... | collective-permute-start | bytes 786440 | tf_op jit(solution)/shard_map/ppermute | solution.py:252
  47.9 6.7 %collective-permute-start.19 = (bf16[1024,128]{1,0:T(8,128)(2,1)S(1)}, bf16[1024,128]{1,0:T(8,128)(2,1)S(1)}, u32[]{:S(2)}, u32[]{:S(2)}) collective-permute-start(bf16[1024,128]{1,0:T(8,128)(2,1)S(1)} %get-tuple-element.79), channel_id=1, source_target_pairs={{0,8},{1,9},{2,10},{3,11},{4,12},{5,13},{6,14},{7,15},{8,0},{9,1},... | collective-permute-start | bytes 786440 | tf_op jit(solution)/shard_map/ppermute | solution.py:252
  47.9 3.9 %collective-permute-start.21 = (bf16[128,128]{1,0:T(8,128)(2,1)S(1)}, bf16[128,128]{1,0:T(8,128)(2,1)S(1)}, u32[]{:S(2)}, u32[]{:S(2)}) collective-permute-start(bf16[128,128]{1,0:T(8,128)(2,1)S(1)} %get-tuple-element.80), channel_id=1, source_target_pairs={{0,8},{1,2},{2,1},{3,11},{4,12},{5,6},{6,5},{7,15},{8,0},{9,10},{1... | collective-permute-start | bytes 98312 | tf_op jit(solution)/shard_map/ppermute | solution.py:252
  48.4 6.2 %collective-permute-start.20 = (bf16[128,128]{1,0:T(8,128)(2,1)S(1)}, bf16[128,128]{1,0:T(8,128)(2,1)S(1)}, u32[]{:S(2)}, u32[]{:S(2)}) collective-permute-start(bf16[128,128]{1,0:T(8,128)(2,1)S(1)} %get-tuple-element.80), channel_id=1, source_target_pairs={{0,1},{1,0},{2,3},{3,2},{4,5},{5,4},{6,7},{7,6},{8,9},{9,8},{10,11... | collective-permute-start | bytes 98312 | tf_op jit(solution)/shard_map/ppermute | solution.py:252

commit v15 on v14

--- a/solution.py
+++ b/solution.py
@@ -444,7 +444,7 @@
     zs = 0.0
     for turn in range(shape.ends):
         wanted = (filled == (turn == 0)) & has_neighbour("gz", turn)
-        zs = jnp.where(wanted, end_refs[turn][sides, :].astype(F32), zs)
+        zs = jnp.where(wanted, end_refs[-1 - turn][sides, :].astype(F32), zs)
     return expand(shape, zs, z_mask(shape, 1))
 
 
@@ -666,7 +666,7 @@
 
 
 def swap_ends(shape, ends):
-    return [swap(ends, "gz", turn) for turn in range(shape.ends)]
+    return [swap(ends, "gz", turn) for turn in reversed(range(shape.ends))]
 
 
 def row_gather(trace, hidden, late):
@@ -678,10 +678,10 @@
         fresh = {key ^ bit: lax.ppermute(held[key], "row", pairs) for key in sorted(held, reverse=True)}
         if bit == peers // 2:
             fresh, hidden = lax.optimization_barrier((fresh, hidden))
-            fresh, late = lax.optimization_barrier((fresh, late))
         held.update(fresh)
         bit //= 2
-    return [held[key] for key in range(peers)], hidden, late
+    parts, late = lax.optimization_barrier(([held[key] for key in range(peers)], late))
+    return parts, hidden, late
 
 
 def per_device(volume_field, volume_load, coefficient, surface_block, trace_cell, flux_cell):

time: 57.2 us -> 56.5 us (0.988)
  starting transfers between devices: 23.5 us -> 20.5 us
  waiting for transfers between devices: 8.67 us -> 10.9 us
    ppermute x15, starting transfers between devices: 14.4 us -> 11.5 us  [swap(): return lax.ppermute(value, axes, pairs)]
    ppermute x1, waiting for transfers between devices: 0.01 us -> 1.1 us  [flux_sums(): other = lax.ppermute(other, 'col', [(0, 1), (1, 0)])]
    ppermute x15, waiting for transfers between devices: 5.61 us -> 6.27 us  [swap(): return lax.ppermute(value, axes, pairs)]
  transfers between devices with their start and end apart: 22 -> 22, of which waited for: 5 -> 7; matrix products, arithmetic and copies ran while one was open for 0% -> 0% of each run, Pallas kernels for 18% -> 18%
where the time goes in v15:
time: 56.5 us; the launch traced here: 56.3 us
  Pallas kernels  24 us (42%)
  starting transfers between devices  20.5 us (36%)
  waiting for transfers between devices  10.9 us (19%)
  between operations  0.94 us (2%)
    ppermute x15, starting transfers between devices, swap(): return lax.ppermute(value, axes, pairs)  11.5 us
    pallas_call x3, Pallas kernels, sweep_finish(): pl.pallas_call(functools.partial(finish_kernel, shape, len(ends), len(rec...  8.68 us
    ppermute x15, waiting for transfers between devices, swap(): return lax.ppermute(value, axes, pairs)  6.27 us
    pallas_call x3, Pallas kernels, sweep_base(): pl.pallas_call(functools.partial(base_kernel, shape, len(ends), phi is no...  5.8 us
    pallas_call x1, Pallas kernels, traces(): pl.pallas_call(functools.partial(trace_kernel, shape, stride, block), in_...  5.21 us
    ppermute x3, starting transfers between devices, flux_sums(): lax.ppermute(sent[key], 'gz', [(i, i ^ key) for i in range(gzs)])  4.45 us
    pallas_call x1, Pallas kernels, first_faces(): pl.pallas_call(functools.partial(faces_kernel, shape, slots), in_specs=[h...  3.46 us
    ppermute x3, starting transfers between devices, row_gather(): lax.ppermute(held[key], 'row', pairs)  3.01 us
  transfers between devices with their start and end apart: 22, of which 7 were waited for; matrix products, arithmetic and copies ran while one was open for 0% of the time, Pallas kernels for 18%

profile of v15, /device:TPU:0, one launch (start us, length us, event | category | flops | bytes accessed | tf_op | source)
XLA Modules:
  0.0 56.3 jit_solution(3758596706373602730)
XLA Ops:
  0.6 5.2 %shard_map.78 = (bf16[1024,128]{1,0:T(8,128)(2,1)}, bf16[1024,128]{1,0:T(8,128)(2,1)}) custom-call(bf16[128,64,128]{2,1,0:T(8,128)(2,1)} %bitcast.5, s32[1,1,1,1024]{3,2,1,0:T(1,128)} %cell_ref.1), custom_call_target="tpu_custom_call" | custom-call | flops 536870912 | bytes 2097152 | tf_op jit(solution)/shard_map/pallas_call | solution.py:102
  5.9 3.0 %collective-permute-start.1 = (bf16[1024,128]{1,0:T(8,128)(2,1)}, bf16[1024,128]{1,0:T(8,128)(2,1)S(1)}, u32[]{:S(2)}, u32[]{:S(2)}) collective-permute-start(bf16[1024,128]{1,0:T(8,128)(2,1)} %get-tuple-element.53.refs_0_), channel_id=1, source_target_pairs={{0,16},{8,24},{16,0},{24,8},{1,17},{9,25},{17,1},{25,9},{2,18},{10... | collective-permute-start | bytes 786440 | tf_op jit(solution)/shard_map/ppermute | solution.py:678
  8.9 1.5 %collective-permute-start.3 = (bf16[1024,128]{1,0:T(8,128)(2,1)}, bf16[1024,128]{1,0:T(8,128)(2,1)S(1)}, u32[]{:S(2)}, u32[]{:S(2)}) collective-permute-start(bf16[1024,128]{1,0:T(8,128)(2,1)} %get-tuple-element.52), channel_id=1, source_target_pairs={{0,4},{1,5},{2,6},{3,7},{4,0},{5,1},{6,2},{7,3},{8,12},{9,13},{10,... | collective-permute-start | bytes 786440 | tf_op jit(solution)/shard_map/ppermute | solution.py:252
  10.4 3.5 %shard_map.77 = (bf16[1024,128]{1,0:T(8,128)(2,1)S(1)}, bf16[1024,128]{1,0:T(8,128)(2,1)S(1)}, bf16[128,128]{1,0:T(8,128)(2,1)S(1)}, bf16[4,256,1024]{2,1,0:T(8,...) custom-call(bf16[8192,128]{1,0:T(8,128)(2,1)} %bitcast.6, ...), custom_call_target="tpu_custom_call" | custom-call | flops 134217728 | bytes 4194304 | tf_op jit(solution)/shard_map/pallas_call | solution.py:415
  13.9 1.5 %collective-permute-done.1.refs_2_ = bf16[1024,128]{1,0:T(8,128)(2,1)S(1)} collective-permute-done((bf16[1024,128]{1,0:T(8,128)(2,1)}, bf16[1024,128]{1,0:T(8,128)(2,1)S(1)}, u32[]{:S(2)}, u32[]{:S(2)}) %collective-permute-start.1) | collective-permute-done | bytes 262176 | tf_op jit(solution)/shard_map/ppermute | solution.py:678
  15.4 1.8 %collective-permute-start.6 = (bf16[1024,128]{1,0:T(8,128)(2,1)S(1)}, bf16[1024,128]{1,0:T(8,128)(2,1)S(1)}, u32[]{:S(2)}, u32[]{:S(2)}) collective-permute-start(bf16[1024,128]{1,0:T(8,128)(2,1)S(1)} %get-tuple-element.65), channel_id=1, source_target_pairs={{0,1},{1,0},{2,3},{3,2},{4,5},{5,4},{6,7},{7,6},{8,16},{9,17},{10,... | collective-permute-start | bytes 786440 | tf_op jit(solution)/shard_map/ppermute | solution.py:252
  17.2 0.0 collective-permute-start.7
  17.2 0.6 collective-permute-done.3.refs_6_
  17.8 0.7 %shard_map.79 = (f32[128,128]{1,0:T(8,128)S(1)}, f32[128,128]{1,0:T(8,128)S(1)}) custom-call(bf16[1024,128]{1,0:T(8,128)(2,1)S(1)} %copy-done.2, bf16[1024,128]{1,0:T(8,128)(2,1)S(1)} %collective-permute-done.refs_1_, bf16[1024,128]{1,0:T(8,128)(2,1)S(1)} %collective-permute-done.1.refs_2_, bf16[1024,128]{1,0:T(8,128)(2,1)S(1)} %collective-permute-done.2.refs_3_, ...), custom_call_target="tpu_custom_call" | custom-call | flops 268435456 | bytes 2097152 | tf_op jit(solution)/shard_map/pallas_call | solution.py:156
  18.5 1.6 %collective-permute-start.8 = (f32[128,128]{1,0:T(8,128)S(1)}, f32[128,128]{1,0:T(8,128)S(1)}, u32[]{:S(2)}, u32[]{:S(2)}) collective-permute-start(f32[128,128]{1,0:T(8,128)S(1)} %get-tuple-element.68), channel_id=1, source_target_pairs={{0,4},{4,0},{1,5},{5,1},{2,6},{6,2},{3,7},{7,3},{8,12},{12,8},{9,1... | collective-permute-start | bytes 196616 | tf_op jit(solution)/shard_map/ppermute | solution.py:206
  20.1 1.6 %collective-permute-start.5 = (bf16[128,128]{1,0:T(8,128)(2,1)S(1)}, bf16[128,128]{1,0:T(8,128)(2,1)S(1)}, u32[]{:S(2)}, u32[]{:S(2)}) collective-permute-start(bf16[128,128]{1,0:T(8,128)(2,1)S(1)} %get-tuple-element.61), channel_id=1, source_target_pairs={{0,1},{1,0},{2,3},{3,2},{4,5},{5,4},{6,7},{7,6},{8,9},{9,8},{10,11... | collective-permute-start | bytes 98312 | tf_op jit(solution)/shard_map/ppermute | solution.py:252
  21.7 0.1 collective-permute-done.6.refs_7_
  21.8 1.1 %collective-permute-done.8.other_ref = f32[128,128]{1,0:T(8,128)S(1)} collective-permute-done((f32[128,128]{1,0:T(8,128)S(1)}, f32[128,128]{1,0:T(8,128)S(1)}, u32[]{:S(2)}, u32[]{:S(2)}) %collective-permute-start.8) | collective-permute-done | bytes 65568 | tf_op jit(solution)/shard_map/ppermute | solution.py:206
  22.9 0.1 shard_map.81
  23.0 3.7 %collective-permute-start.9 = (f32[64,128]{1,0:T(8,128)S(1)}, f32[64,128]{1,0:T(8,128)S(1)}, u32[]{:S(2)}, u32[]{:S(2)}) collective-permute-start(f32[64,128]{1,0:T(8,128)S(1)} %get-tuple-element.71), channel_id=1, source_target_pairs={{0,3},{1,2},{2,1},{3,0},{4,7},{5,6},{6,5},{7,4},{8,11},{9,10},{10,... | collective-permute-start | bytes 98312 | tf_op jit(solution)/shard_map/ppermute | solution.py:211
  26.6 0.8 %collective-permute-start.11 = (f32[64,128]{1,0:T(8,128)S(1)}, f32[64,128]{1,0:T(8,128)S(1)}, u32[]{:S(2)}, u32[]{:S(2)}) collective-permute-start(f32[64,128]{1,0:T(8,128)S(1)} %get-tuple-element.73), channel_id=1, source_target_pairs={{0,1},{1,0},{2,3},{3,2},{4,5},{5,4},{6,7},{7,6},{8,9},{9,8},{10,11... | collective-permute-start | bytes 98312 | tf_op jit(solution)/shard_map/ppermute | solution.py:211
  27.5 2.0 %shard_map.80.refs_0_ = f32[8192,128]{1,0:T(8,128)S(1)} custom-call(bf16[8192,128]{1,0:T(8,128)(2,1)S(1)} %bitcast.7, bf16[8192,128]{1,0:T(8,128)(2,1)S(1)} %bitcast.8, f32[128,128]{1,0:T(8,128)S(1)} %get-tuple-element.45.refs_2_.refs_1_, bf16[128,176]{1,0:T(8,128)(2,1)S(1)} %get-tuple-element.46.refs_3_.refs_2_, ...), custom_call_target="tpu_custom_call" | custom-call | flops 805306368 | bytes 8388608 | tf_op jit(solution)/shard_map/pallas_call | solution.py:515
  29.4 2.0 %collective-permute-done.10.refs_12_ = f32[64,128]{1,0:T(8,128)S(1)} collective-permute-done((f32[64,128]{1,0:T(8,128)S(1)}, f32[64,128]{1,0:T(8,128)S(1)}, u32[]{:S(2)}, u32[]{:S(2)}) %collective-permute-start.10) | collective-permute-done | bytes 32800 | tf_op jit(solution)/shard_map/ppermute | solution.py:211
  31.5 3.5 %shard_map.82 = (bf16[8192,128]{1,0:T(8,128)(2,1)S(1)}, bf16[1024,128]{1,0:T(8,128)(2,1)S(1)}, bf16[1024,128]{1,0:T(8,128)(2,1)S(1)}, bf16[1024,128]{1,0:T(8,128...) custom-call(f32[8192,128]{1,0:T(8,128)S(1)} %shard_map.80.refs_0_, ...), custom_call_target="tpu_custom_call" | custom-call | flops 536870912 | bytes 8388608 | tf_op jit(solution)/shard_map/pallas_call | solution.py:651
  35.0 1.5 %collective-permute-start.12 = (bf16[1024,128]{1,0:T(8,128)(2,1)S(1)}, bf16[1024,128]{1,0:T(8,128)(2,1)S(1)}, u32[]{:S(2)}, u32[]{:S(2)}) collective-permute-start(bf16[1024,128]{1,0:T(8,128)(2,1)S(1)} %get-tuple-element.77), channel_id=1, source_target_pairs={{0,4},{1,5},{2,6},{3,7},{4,0},{5,1},{6,2},{7,3},{8,12},{9,13},{10,... | collective-permute-start | bytes 786440 | tf_op jit(solution)/shard_map/ppermute | solution.py:252
  36.5 1.0 %collective-permute-start.14 = (bf16[1024,128]{1,0:T(8,128)(2,1)S(1)}, bf16[1024,128]{1,0:T(8,128)(2,1)S(1)}, u32[]{:S(2)}, u32[]{:S(2)}) collective-permute-start(bf16[1024,128]{1,0:T(8,128)(2,1)S(1)} %get-tuple-element.79), channel_id=1, source_target_pairs={{0,8},{1,9},{2,10},{3,11},{4,12},{5,13},{6,14},{7,15},{8,0},{9,1},... | collective-permute-start | bytes 786440 | tf_op jit(solution)/shard_map/ppermute | solution.py:252
  37.5 1.1 %collective-permute-start.16 = (bf16[128,128]{1,0:T(8,128)(2,1)S(1)}, bf16[128,128]{1,0:T(8,128)(2,1)S(1)}, u32[]{:S(2)}, u32[]{:S(2)}) collective-permute-start(bf16[128,128]{1,0:T(8,128)(2,1)S(1)} %get-tuple-element.80), channel_id=1, source_target_pairs={{0,1},{1,0},{2,3},{3,2},{4,5},{5,4},{6,7},{7,6},{8,9},{9,8},{10,11... | collective-permute-start | bytes 98312 | tf_op jit(solution)/shard_map/ppermute | solution.py:252
  38.5 0.2 collective-permute-start.15
  38.7 2.3 %shard_map.83 = (f32[8192,128]{1,0:T(8,128)S(1)}, bf16[8192,128]{1,0:T(8,128)(2,1)S(1)}) custom-call(bf16[8192,128]{1,0:T(8,128)(2,1)S(1)} %get-tuple-element.74.refs_0_, bf16[8192,128]{1,0:T(8,128)(2,1)S(1)} %bitcast.9, f32[128,128]{1,0:T(8,128)S(1)} %get-tuple-element.45.refs_2_.refs_1_, bf16[128,176]{1,0:T(8,128)(2,1)S(1)} %get-tuple-element.46.refs_3_.refs_2_, ...), custom_call_target="tpu_custom_call" | custom-call | flops 805306368 | bytes 8388608 | tf_op jit(solution)/shard_map/pallas_call | solution.py:515
  41.1 2.5 %collective-permute-done.16.refs_10_ = bf16[128,128]{1,0:T(8,128)(2,1)S(1)} collective-permute-done((bf16[128,128]{1,0:T(8,128)(2,1)S(1)}, bf16[128,128]{1,0:T(8,128)(2,1)S(1)}, u32[]{:S(2)}, u32[]{:S(2)}) %collective-permute-start.16) | collective-permute-done | bytes 32800 | tf_op jit(solution)/shard_map/ppermute | solution.py:252
  43.6 2.8 %shard_map.84 = (bf16[8192,128]{1,0:T(8,128)(2,1)S(1)}, bf16[1024,128]{1,0:T(8,128)(2,1)S(1)}, bf16[1024,128]{1,0:T(8,128)(2,1)S(1)}, bf16[1024,128]{1,0:T(8,128)(2,1)S(1)}, bf16[128,128]{1,0:T(8,128)(2,1)S(1)}) custom-call(f32[8192,128]{1,0:T(8,128)S(1)} %get-tuple-element.76.refs_0_, f32[128,128]{1,0:T(8,128)S(1)} %get-tuple-element.45.refs_2_.refs_1_, ...), custom_call_target="tpu_custom_call" | custom-call | flops 536870912 | bytes 8388608 | tf_op jit(solution)/shard_map/pallas_call | solution.py:651
  46.4 0.5 collective-permute-start.17
  47.0 2.0 %collective-permute-start.21 = (bf16[128,128]{1,0:T(8,128)(2,1)S(1)}, bf16[128,128]{1,0:T(8,128)(2,1)S(1)}, u32[]{:S(2)}, u32[]{:S(2)}) collective-permute-start(bf16[128,128]{1,0:T(8,128)(2,1)S(1)} %get-tuple-element.86), channel_id=1, source_target_pairs={{0,1},{1,0},{2,3},{3,2},{4,5},{5,4},{6,7},{7,6},{8,9},{9,8},{10,11... | collective-permute-start | bytes 98312 | tf_op jit(solution)/shard_map/ppermute | solution.py:252
  49.0 0.2 collective-permute-start.20
  49.2 1.5 %shard_map.85.refs_0_ = f32[8192,128]{1,0:T(8,128)S(1)} custom-call(bf16[8192,128]{1,0:T(8,128)(2,1)S(1)} %get-tuple-element.81.refs_0_, bf16[8192,128]{1,0:T(8,128)(2,1)S(1)} %get-tuple-element.82.refs_1_, f32[128,128]{1,0:T(8,128)S(1)} %get-tuple-element.45.refs_2_.refs_1_, bf16[128,176]{1,0:T(8,128)(2,1)S(1)} %get-tuple-element.46.refs_3_.refs_2_, ...), custom_call_target="tpu_custom_call" | custom-call | flops 805306368 | bytes 8388608 | tf_op jit(solution)/shard_map/pallas_call | solution.py:515
  50.7 3.1 %collective-permute-done.21.refs_10_ = bf16[128,128]{1,0:T(8,128)(2,1)S(1)} collective-permute-done((bf16[128,128]{1,0:T(8,128)(2,1)S(1)}, bf16[128,128]{1,0:T(8,128)(2,1)S(1)}, u32[]{:S(2)}, u32[]{:S(2)}) %collective-permute-start.21) | collective-permute-done | bytes 32800 | tf_op jit(solution)/shard_map/ppermute | solution.py:252
  53.9 2.3 %shard_map.86 = bf16[8192,128]{1,0:T(8,128)(2,1)} custom-call(f32[8192,128]{1,0:T(8,128)S(1)} %shard_map.85.refs_0_, f32[128,128]{1,0:T(8,128)S(1)} %get-tuple-element.45.refs_2_.refs_1_, bf16[128,176]{1,0:T(8,128)(2,1)S(1)} %get-tuple-element.46.refs_3_.refs_2_, bf16[512,256]{1,0:T(8,128)(2,1)S(1)} %get-tuple-element.47.refs_4_.refs_3_, ...), custom_call_target="tpu_custom_call" | custom-call | flops 536870912 | bytes 8388608 | tf_op jit(solution)/shard_map/pallas_call | solution.py:651
  (32 shorter events, 0.1 us)
Async XLA Ops:
  0.6 9.7 %copy-start.3 = (f32[8,8,128]{2,1,0:T(8,128)S(1)}, f32[8,8,128]{2,1,0:T(8,128)}, u32[]{:S(2)}) copy-start(f32[8,8,128]{2,1,0:T(8,128)} %param.8) | copy-start | bytes 98308
  5.9 9.5 %collective-permute-start.1 = (bf16[1024,128]{1,0:T(8,128)(2,1)}, bf16[1024,128]{1,0:T(8,128)(2,1)S(1)}, u32[]{:S(2)}, u32[]{:S(2)}) collective-permute-start(bf16[1024,128]{1,0:T(8,128)(2,1)} %get-tuple-element.53.refs_0_), channel_id=1, source_target_pairs={{0,16},{8,24},{16,0},{24,8},{1,17},{9,25},{17,1},{25,9},{2,18},{10... | collective-permute-start | bytes 786440 | tf_op jit(solution)/shard_map/ppermute | solution.py:678
  8.9 8.9 %collective-permute-start = (bf16[1024,128]{1,0:T(8,128)(2,1)}, bf16[1024,128]{1,0:T(8,128)(2,1)S(1)}, u32[]{:S(2)}, u32[]{:S(2)}) collective-permute-start(bf16[1024,128]{1,0:T(8,128)(2,1)} %get-tuple-element.53.refs_0_), channel_id=1, source_target_pairs={{0,8},{8,0},{16,24},{24,16},{1,9},{9,1},{17,25},{25,17},{2,10},{10... | collective-permute-start | bytes 786440 | tf_op jit(solution)/shard_map/ppermute | solution.py:678
  8.9 8.9 %collective-permute-start.3 = (bf16[1024,128]{1,0:T(8,128)(2,1)}, bf16[1024,128]{1,0:T(8,128)(2,1)S(1)}, u32[]{:S(2)}, u32[]{:S(2)}) collective-permute-start(bf16[1024,128]{1,0:T(8,128)(2,1)} %get-tuple-element.52), channel_id=1, source_target_pairs={{0,4},{1,5},{2,6},{3,7},{4,0},{5,1},{6,2},{7,3},{8,12},{9,13},{10,... | collective-permute-start | bytes 786440 | tf_op jit(solution)/shard_map/ppermute | solution.py:252
  10.4 7.4 %copy-start.2 = (bf16[1024,128]{1,0:T(8,128)(2,1)S(1)}, bf16[1024,128]{1,0:T(8,128)(2,1)}, u32[]{:S(2)}) copy-start(bf16[1024,128]{1,0:T(8,128)(2,1)} %get-tuple-element.53.refs_0_) | copy-start | bytes 786436
  10.4 17.1 %copy-start.1 = (bf16[128,8,8,128]{3,2,1,0:T(8,128)(2,1)S(1)}, bf16[128,8,8,128]{3,2,1,0:T(8,128)(2,1)}, u32[]{:S(2)}) copy-start(bf16[128,8,8,128]{3,2,1,0:T(8,128)(2,1)} %param.7) | copy-start | bytes 6291460
  13.8 13.6 %copy-start = (bf16[128,8,8,128]{3,2,1,0:T(8,128)(2,1)S(1)}, bf16[128,8,8,128]{3,2,1,0:T(8,128)(2,1)}, u32[]{:S(2)}) copy-start(bf16[128,8,8,128]{3,2,1,0:T(8,128)(2,1)} %param.6) | copy-start | bytes 6291460
  15.4 2.4 %collective-permute-start.2 = (bf16[1024,128]{1,0:T(8,128)(2,1)S(1)}, bf16[1024,128]{1,0:T(8,128)(2,1)S(1)}, u32[]{:S(2)}, u32[]{:S(2)}) collective-permute-start(bf16[1024,128]{1,0:T(8,128)(2,1)S(1)} %collective-permute-done.1.refs_2_), channel_id=1, source_target_pairs={{0,8},{8,0},{16,24},{24,16},{1,9},{9,1},{17,25},{25,17},{2,10},{10... | collective-permute-start | bytes 786440 | tf_op jit(solution)/shard_map/ppermute | solution.py:678
  15.4 6.4 %collective-permute-start.6 = (bf16[1024,128]{1,0:T(8,128)(2,1)S(1)}, bf16[1024,128]{1,0:T(8,128)(2,1)S(1)}, u32[]{:S(2)}, u32[]{:S(2)}) collective-permute-start(bf16[1024,128]{1,0:T(8,128)(2,1)S(1)} %get-tuple-element.65), channel_id=1, source_target_pairs={{0,1},{1,0},{2,3},{3,2},{4,5},{5,4},{6,7},{7,6},{8,16},{9,17},{10,... | collective-permute-start | bytes 786440 | tf_op jit(solution)/shard_map/ppermute | solution.py:252
  17.2 4.5 %collective-permute-start.7 = (bf16[1024,128]{1,0:T(8,128)(2,1)S(1)}, bf16[1024,128]{1,0:T(8,128)(2,1)S(1)}, u32[]{:S(2)}, u32[]{:S(2)}) collective-permute-start(bf16[1024,128]{1,0:T(8,128)(2,1)S(1)} %get-tuple-element.66), channel_id=1, source_target_pairs={{0,8},{1,9},{2,10},{3,11},{4,12},{5,13},{6,14},{7,15},{8,0},{9,1},... | collective-permute-start | bytes 786440 | tf_op jit(solution)/shard_map/ppermute | solution.py:252
  18.5 4.3 %collective-permute-start.8 = (f32[128,128]{1,0:T(8,128)S(1)}, f32[128,128]{1,0:T(8,128)S(1)}, u32[]{:S(2)}, u32[]{:S(2)}) collective-permute-start(f32[128,128]{1,0:T(8,128)S(1)} %get-tuple-element.68), channel_id=1, source_target_pairs={{0,4},{4,0},{1,5},{5,1},{2,6},{6,2},{3,7},{7,3},{8,12},{12,8},{9,1... | collective-permute-start | bytes 196616 | tf_op jit(solution)/shard_map/ppermute | solution.py:206
  20.1 7.3 %collective-permute-start.5 = (bf16[128,128]{1,0:T(8,128)(2,1)S(1)}, bf16[128,128]{1,0:T(8,128)(2,1)S(1)}, u32[]{:S(2)}, u32[]{:S(2)}) collective-permute-start(bf16[128,128]{1,0:T(8,128)(2,1)S(1)} %get-tuple-element.61), channel_id=1, source_target_pairs={{0,1},{1,0},{2,3},{3,2},{4,5},{5,4},{6,7},{7,6},{8,9},{9,8},{10,11... | collective-permute-start | bytes 98312 | tf_op jit(solution)/shard_map/ppermute | solution.py:252
  21.7 5.7 %collective-permute-start.4 = (bf16[128,128]{1,0:T(8,128)(2,1)S(1)}, bf16[128,128]{1,0:T(8,128)(2,1)S(1)}, u32[]{:S(2)}, u32[]{:S(2)}) collective-permute-start(bf16[128,128]{1,0:T(8,128)(2,1)S(1)} %get-tuple-element.61), channel_id=1, source_target_pairs={{0,8},{1,2},{2,1},{3,11},{4,12},{5,6},{6,5},{7,15},{8,0},{9,10},{1... | collective-permute-start | bytes 98312 | tf_op jit(solution)/shard_map/ppermute | solution.py:252
  23.0 6.5 %collective-permute-start.9 = (f32[64,128]{1,0:T(8,128)S(1)}, f32[64,128]{1,0:T(8,128)S(1)}, u32[]{:S(2)}, u32[]{:S(2)}) collective-permute-start(f32[64,128]{1,0:T(8,128)S(1)} %get-tuple-element.71), channel_id=1, source_target_pairs={{0,3},{1,2},{2,1},{3,0},{4,7},{5,6},{6,5},{7,4},{8,11},{9,10},{10,... | collective-permute-start | bytes 98312 | tf_op jit(solution)/shard_map/ppermute | solution.py:211
  26.6 4.8 %collective-permute-start.10 = (f32[64,128]{1,0:T(8,128)S(1)}, f32[64,128]{1,0:T(8,128)S(1)}, u32[]{:S(2)}, u32[]{:S(2)}) collective-permute-start(f32[64,128]{1,0:T(8,128)S(1)} %get-tuple-element.72), channel_id=1, source_target_pairs={{0,2},{1,3},{2,0},{3,1},{4,6},{5,7},{6,4},{7,5},{8,10},{9,11},{10,... | collective-permute-start | bytes 98312 | tf_op jit(solution)/shard_map/ppermute | solution.py:211
  26.6 4.8 %collective-permute-start.11 = (f32[64,128]{1,0:T(8,128)S(1)}, f32[64,128]{1,0:T(8,128)S(1)}, u32[]{:S(2)}, u32[]{:S(2)}) collective-permute-start(f32[64,128]{1,0:T(8,128)S(1)} %get-tuple-element.73), channel_id=1, source_target_pairs={{0,1},{1,0},{2,3},{3,2},{4,5},{5,4},{6,7},{7,6},{8,9},{9,8},{10,11... | collective-permute-start | bytes 98312 | tf_op jit(solution)/shard_map/ppermute | solution.py:211
  27.4 4.0 %copy-start.4 = (s32[1,1,1,32]{3,2,1,0:T(1,128)S(1)}, s32[1,1,1,32]{3,2,1,0:T(1,128)}, u32[]{:S(2)}) copy-start(s32[1,1,1,32]{3,2,1,0:T(1,128)} %refs_6_.1) | copy-start | bytes 388
  35.0 8.6 %collective-permute-start.12 = (bf16[1024,128]{1,0:T(8,128)(2,1)S(1)}, bf16[1024,128]{1,0:T(8,128)(2,1)S(1)}, u32[]{:S(2)}, u32[]{:S(2)}) collective-permute-start(bf16[1024,128]{1,0:T(8,128)(2,1)S(1)} %get-tuple-element.77), channel_id=1, source_target_pairs={{0,4},{1,5},{2,6},{3,7},{4,0},{5,1},{6,2},{7,3},{8,12},{9,13},{10,... | collective-permute-start | bytes 786440 | tf_op jit(solution)/shard_map/ppermute | solution.py:252
  36.5 7.1 %collective-permute-start.13 = (bf16[1024,128]{1,0:T(8,128)(2,1)S(1)}, bf16[1024,128]{1,0:T(8,128)(2,1)S(1)}, u32[]{:S(2)}, u32[]{:S(2)}) collective-permute-start(bf16[1024,128]{1,0:T(8,128)(2,1)S(1)} %get-tuple-element.78), channel_id=1, source_target_pairs={{0,1},{1,0},{2,3},{3,2},{4,5},{5,4},{6,7},{7,6},{8,16},{9,17},{10,... | collective-permute-start | bytes 786440 | tf_op jit(solution)/shard_map/ppermute | solution.py:252
  36.5 7.1 %collective-permute-start.14 = (bf16[1024,128]{1,0:T(8,128)(2,1)S(1)}, bf16[1024,128]{1,0:T(8,128)(2,1)S(1)}, u32[]{:S(2)}, u32[]{:S(2)}) collective-permute-start(bf16[1024,128]{1,0:T(8,128)(2,1)S(1)} %get-tuple-element.79), channel_id=1, source_target_pairs={{0,8},{1,9},{2,10},{3,11},{4,12},{5,13},{6,14},{7,15},{8,0},{9,1},... | collective-permute-start | bytes 786440 | tf_op jit(solution)/shard_map/ppermute | solution.py:252
  37.5 6.1 %collective-permute-start.16 = (bf16[128,128]{1,0:T(8,128)(2,1)S(1)}, bf16[128,128]{1,0:T(8,128)(2,1)S(1)}, u32[]{:S(2)}, u32[]{:S(2)}) collective-permute-start(bf16[128,128]{1,0:T(8,128)(2,1)S(1)} %get-tuple-element.80), channel_id=1, source_target_pairs={{0,1},{1,0},{2,3},{3,2},{4,5},{5,4},{6,7},{7,6},{8,9},{9,8},{10,11... | collective-permute-start | bytes 98312 | tf_op jit(solution)/shard_map/ppermute | solution.py:252
  38.5 5.0 %collective-permute-start.15 = (bf16[128,128]{1,0:T(8,128)(2,1)S(1)}, bf16[128,128]{1,0:T(8,128)(2,1)S(1)}, u32[]{:S(2)}, u32[]{:S(2)}) collective-permute-start(bf16[128,128]{1,0:T(8,128)(2,1)S(1)} %get-tuple-element.80), channel_id=1, source_target_pairs={{0,8},{1,2},{2,1},{3,11},{4,12},{5,6},{6,5},{7,15},{8,0},{9,10},{1... | collective-permute-start | bytes 98312 | tf_op jit(solution)/shard_map/ppermute | solution.py:252
  46.4 7.4 %collective-permute-start.17 = (bf16[1024,128]{1,0:T(8,128)(2,1)S(1)}, bf16[1024,128]{1,0:T(8,128)(2,1)S(1)}, u32[]{:S(2)}, u32[]{:S(2)}) collective-permute-start(bf16[1024,128]{1,0:T(8,128)(2,1)S(1)} %get-tuple-element.83), channel_id=1, source_target_pairs={{0,4},{1,5},{2,6},{3,7},{4,0},{5,1},{6,2},{7,3},{8,12},{9,13},{10,... | collective-permute-start | bytes 786440 | tf_op jit(solution)/shard_map/ppermute | solution.py:252
  47.0 6.9 %collective-permute-start.18 = (bf16[1024,128]{1,0:T(8,128)(2,1)S(1)}, bf16[1024,128]{1,0:T(8,128)(2,1)S(1)}, u32[]{:S(2)}, u32[]{:S(2)}) collective-permute-start(bf16[1024,128]{1,0:T(8,128)(2,1)S(1)} %get-tuple-element.84), channel_id=1, source_target_pairs={{0,1},{1,0},{2,3},{3,2},{4,5},{5,4},{6,7},{7,6},{8,16},{9,17},{10,... | collective-permute-start | bytes 786440 | tf_op jit(solution)/shard_map/ppermute | solution.py:252
  47.0 6.9 %collective-permute-start.19 = (bf16[1024,128]{1,0:T(8,128)(2,1)S(1)}, bf16[1024,128]{1,0:T(8,128)(2,1)S(1)}, u32[]{:S(2)}, u32[]{:S(2)}) collective-permute-start(bf16[1024,128]{1,0:T(8,128)(2,1)S(1)} %get-tuple-element.85), channel_id=1, source_target_pairs={{0,8},{1,9},{2,10},{3,11},{4,12},{5,13},{6,14},{7,15},{8,0},{9,1},... | collective-permute-start | bytes 786440 | tf_op jit(solution)/shard_map/ppermute | solution.py:252
  47.0 6.9 %collective-permute-start.21 = (bf16[128,128]{1,0:T(8,128)(2,1)S(1)}, bf16[128,128]{1,0:T(8,128)(2,1)S(1)}, u32[]{:S(2)}, u32[]{:S(2)}) collective-permute-start(bf16[128,128]{1,0:T(8,128)(2,1)S(1)} %get-tuple-element.86), channel_id=1, source_target_pairs={{0,1},{1,0},{2,3},{3,2},{4,5},{5,4},{6,7},{7,6},{8,9},{9,8},{10,11... | collective-permute-start | bytes 98312 | tf_op jit(solution)/shard_map/ppermute | solution.py:252
  49.0 4.9 %collective-permute-start.20 = (bf16[128,128]{1,0:T(8,128)(2,1)S(1)}, bf16[128,128]{1,0:T(8,128)(2,1)S(1)}, u32[]{:S(2)}, u32[]{:S(2)}) collective-permute-start(bf16[128,128]{1,0:T(8,128)(2,1)S(1)} %get-tuple-element.86), channel_id=1, source_target_pairs={{0,8},{1,2},{2,1},{3,11},{4,12},{5,6},{6,5},{7,15},{8,0},{9,10},{1... | collective-permute-start | bytes 98312 | tf_op jit(solution)/shard_map/ppermute | solution.py:252

commit v16 on v15

--- a/solution.py
+++ b/solution.py
@@ -30,6 +30,7 @@
 
 
 FACES_MIB = 50
+TRACE_MIB = 52
 
 
 def params(mebibytes=24):
@@ -113,7 +114,7 @@
             pltpu.VMEM((sides, slots), F32),
             pltpu.SemaphoreType.DMA((sides // block + 1,)),
         ],
-        compiler_params=params(62),
+        compiler_params=params(TRACE_MIB),
         cost_estimate=pl.CostEstimate(
             flops=4 * sides * rows * lanes * 128, bytes_accessed=field.size * 2, transcendentals=0
         ),
@@ -448,12 +449,19 @@
     return expand(shape, zs, z_mask(shape, 1))
 
 
+def flux_width(slots):
+    return (2 * slots + 127) // 128 * 128
+
+
 def build_cells(shape, cell_ref, cell_m):
     slots = cell_ref.shape[3]
-    cell = jnp.concatenate([cell_ref[0, 0]] * 2, axis=1)
-    place = (iota((shape.lanes, 2 * slots), 0) == cell % shape.lanes).astype(F32)
+    width = flux_width(slots)
+    cell = cell_ref[0, 0]
+    none = jnp.full((1, width - 2 * slots), -shape.lanes, jnp.int32)
+    cell = jnp.concatenate([cell, cell, none], axis=1)
+    place = (iota((shape.lanes, width), 0) == cell % shape.lanes).astype(F32)
     cell_m[...] = twice(place).astype(BF)
-    return iota((shape.cells, 2 * slots), 0) == cell // shape.lanes
+    return iota((shape.cells, width), 0) == cell // shape.lanes
 
 
 def base_kernel(shape, ends, with_flux, *refs):
@@ -562,7 +570,8 @@
         flux_ref[...] = owned[slots:, : flux_ref.shape[1]]
         owned = owned[:slots]
         high = owned.astype(BF).astype(F32)
-        phi[...] = jnp.concatenate([high, owned - high], axis=0).T
+        none = jnp.zeros((phi.shape[1] - 2 * slots, phi.shape[0]), F32)
+        phi[...] = jnp.concatenate([high, owned - high, none], axis=0).T
 
     weights = weight[...]
 
@@ -638,11 +647,11 @@
         slots = flux_cell.shape[3]
         operands += [flux_cell, *recv]
         out_shapes += [
-            jax.ShapeDtypeStruct((shape.sides, 2 * slots), F32),
+            jax.ShapeDtypeStruct((shape.sides, flux_width(slots)), F32),
             jax.ShapeDtypeStruct((recv[0].shape[0] - slots, slots * lax.axis_size("gz")), F32),
         ]
         scratch += [
-            pltpu.VMEM((2 * lanes, 4 * slots), BF),
+            pltpu.VMEM((2 * lanes, 2 * flux_width(slots)), BF),
             pltpu.VMEM(half, F32),
         ]
     out_specs = [WHOLE] * len(out_shapes)

time: 56.5 us -> 56.2 us (level)
  Pallas kernels: 24 us -> 23.1 us
  local copies, waits for them, and re-layouts: 0.02 us -> 0.71 us
    pallas_call x1, Pallas kernels: 5.21 us -> 4.48 us  [traces(): pl.pallas_call(functools.partial(trace_kernel, shape, stride, block), in_...]
    unnamed x10, local copies, waits for them, and re-layouts: 0.02 us -> 0.71 us
where the time goes in v16:
time: 56.2 us; the launch traced here: 56 us
  Pallas kernels  23.1 us (41%)
  starting transfers between devices  20.5 us (36%)
  waiting for transfers between devices  10.8 us (19%)
  between operations  0.94 us (2%)
  local copies, waits for them, and re-layouts  0.71 us (1%)
    ppermute x15, starting transfers between devices, swap(): return lax.ppermute(value, axes, pairs)  11.5 us
    pallas_call x3, Pallas kernels, sweep_finish(): pl.pallas_call(functools.partial(finish_kernel, shape, len(ends), len(rec...  8.61 us
    ppermute x15, waiting for transfers between devices, swap(): return lax.ppermute(value, axes, pairs)  6.35 us
    pallas_call x3, Pallas kernels, sweep_base(): pl.pallas_call(functools.partial(base_kernel, shape, len(ends), phi is no...  5.72 us
    pallas_call x1, Pallas kernels, traces(): pl.pallas_call(functools.partial(trace_kernel, shape, stride, block), in_...  4.48 us
    ppermute x3, starting transfers between devices, flux_sums(): lax.ppermute(sent[key], 'gz', [(i, i ^ key) for i in range(gzs)])  4.45 us
    pallas_call x1, Pallas kernels, first_faces(): pl.pallas_call(functools.partial(faces_kernel, shape, slots), in_specs=[h...  3.45 us
    ppermute x3, starting transfers between devices, row_gather(): lax.ppermute(held[key], 'row', pairs)  3.01 us
  transfers between devices with their start and end apart: 22, of which 7 were waited for; matrix products, arithmetic and copies ran while one was open for 0% of the time, Pallas kernels for 18%

profile of v16, /device:TPU:0, one launch (start us, length us, event | category | flops | bytes accessed | tf_op | source)
XLA Modules:
  0.0 56.0 jit_solution(7409815126580053383)
XLA Ops:
  0.6 0.7 %copy-done.3 = s32[1,1,1,1024]{3,2,1,0:T(1,128)S(1)} copy-done((s32[1,1,1,1024]{3,2,1,0:T(1,128)S(1)}, s32[1,1,1,1024]{3,2,1,0:T(1,128)}, u32[]{:S(2)}) %copy-start.3) | copy-done | bytes 4120
  1.3 4.5 %shard_map.78 = (bf16[1024,128]{1,0:T(8,128)(2,1)S(1)}, bf16[1024,128]{1,0:T(8,128)(2,1)S(1)}) custom-call(bf16[128,64,128]{2,1,0:T(8,128)(2,1)} %bitcast.5, s32[1,1,1,1024]{3,2,1,0:T(1,128)S(1)} %copy-done.3), custom_call_target="tpu_custom_call" | custom-call | flops 536870912 | bytes 2097152 | tf_op jit(solution)/shard_map/pallas_call | solution.py:103
  5.8 3.0 %collective-permute-start.1 = (bf16[1024,128]{1,0:T(8,128)(2,1)S(1)}, bf16[1024,128]{1,0:T(8,128)(2,1)S(1)}, u32[]{:S(2)}, u32[]{:S(2)}) collective-permute-start(bf16[1024,128]{1,0:T(8,128)(2,1)S(1)} %get-tuple-element.53.refs_0_), channel_id=1, source_target_pairs={{0,16},{8,24},{16,0},{24,8},{1,17},{9,25},{17,1},{25,9},{2,18},{10... | collective-permute-start | bytes 786440 | tf_op jit(solution)/shard_map/ppermute | solution.py:687
  8.8 1.5 %collective-permute-start.3 = (bf16[1024,128]{1,0:T(8,128)(2,1)S(1)}, bf16[1024,128]{1,0:T(8,128)(2,1)S(1)}, u32[]{:S(2)}, u32[]{:S(2)}) collective-permute-start(bf16[1024,128]{1,0:T(8,128)(2,1)S(1)} %get-tuple-element.52), channel_id=1, source_target_pairs={{0,4},{1,5},{2,6},{3,7},{4,0},{5,1},{6,2},{7,3},{8,12},{9,13},{10,... | collective-permute-start | bytes 786440 | tf_op jit(solution)/shard_map/ppermute | solution.py:253
  10.3 3.5 %shard_map.77 = (bf16[1024,128]{1,0:T(8,128)(2,1)S(1)}, bf16[1024,128]{1,0:T(8,128)(2,1)S(1)}, bf16[128,128]{1,0:T(8,128)(2,1)S(1)}, bf16[4,256,1024]{2,1,0:T(8,...) custom-call(bf16[8192,128]{1,0:T(8,128)(2,1)} %bitcast.6, ...), custom_call_target="tpu_custom_call" | custom-call | flops 134217728 | bytes 4194304 | tf_op jit(solution)/shard_map/pallas_call | solution.py:416
  13.8 1.3 %collective-permute-done.1.refs_2_ = bf16[1024,128]{1,0:T(8,128)(2,1)S(1)} collective-permute-done((bf16[1024,128]{1,0:T(8,128)(2,1)S(1)}, bf16[1024,128]{1,0:T(8,128)(2,1)S(1)}, u32[]{:S(2)}, u32[]{:S(2)}) %collective-permute-start.1) | collective-permute-done | bytes 262176 | tf_op jit(solution)/shard_map/ppermute | solution.py:687
  15.1 1.8 %collective-permute-start.6 = (bf16[1024,128]{1,0:T(8,128)(2,1)S(1)}, bf16[1024,128]{1,0:T(8,128)(2,1)S(1)}, u32[]{:S(2)}, u32[]{:S(2)}) collective-permute-start(bf16[1024,128]{1,0:T(8,128)(2,1)S(1)} %get-tuple-element.65), channel_id=1, source_target_pairs={{0,1},{1,0},{2,3},{3,2},{4,5},{5,4},{6,7},{7,6},{8,16},{9,17},{10,... | collective-permute-start | bytes 786440 | tf_op jit(solution)/shard_map/ppermute | solution.py:253
  17.0 0.6 collective-permute-done.3.refs_6_
  17.6 0.7 %shard_map.79 = (f32[128,128]{1,0:T(8,128)S(1)}, f32[128,128]{1,0:T(8,128)S(1)}) custom-call(bf16[1024,128]{1,0:T(8,128)(2,1)S(1)} %get-tuple-element.53.refs_0_, bf16[1024,128]{1,0:T(8,128)(2,1)S(1)} %collective-permute-done.refs_1_, bf16[1024,128]{1,0:T(8,128)(2,1)S(1)} %collective-permute-done.1.refs_2_, ...), custom_call_target="tpu_custom_call" | custom-call | flops 268435456 | bytes 2097152 | tf_op jit(solution)/shard_map/pallas_call | solution.py:157
  18.3 1.6 %collective-permute-start.8 = (f32[128,128]{1,0:T(8,128)S(1)}, f32[128,128]{1,0:T(8,128)S(1)}, u32[]{:S(2)}, u32[]{:S(2)}) collective-permute-start(f32[128,128]{1,0:T(8,128)S(1)} %get-tuple-element.68), channel_id=1, source_target_pairs={{0,4},{4,0},{1,5},{5,1},{2,6},{6,2},{3,7},{7,3},{8,12},{12,8},{9,1... | collective-permute-start | bytes 196616 | tf_op jit(solution)/shard_map/ppermute | solution.py:207
  19.8 1.6 %collective-permute-start.5 = (bf16[128,128]{1,0:T(8,128)(2,1)S(1)}, bf16[128,128]{1,0:T(8,128)(2,1)S(1)}, u32[]{:S(2)}, u32[]{:S(2)}) collective-permute-start(bf16[128,128]{1,0:T(8,128)(2,1)S(1)} %get-tuple-element.61), channel_id=1, source_target_pairs={{0,1},{1,0},{2,3},{3,2},{4,5},{5,4},{6,7},{7,6},{8,9},{9,8},{10,11... | collective-permute-start | bytes 98312 | tf_op jit(solution)/shard_map/ppermute | solution.py:253
  21.4 0.1 collective-permute-done.6.refs_7_
  21.5 1.1 %collective-permute-done.8.other_ref = f32[128,128]{1,0:T(8,128)S(1)} collective-permute-done((f32[128,128]{1,0:T(8,128)S(1)}, f32[128,128]{1,0:T(8,128)S(1)}, u32[]{:S(2)}, u32[]{:S(2)}) %collective-permute-start.8) | collective-permute-done | bytes 65568 | tf_op jit(solution)/shard_map/ppermute | solution.py:207
  22.6 0.1 shard_map.81
  22.7 3.7 %collective-permute-start.9 = (f32[64,128]{1,0:T(8,128)S(1)}, f32[64,128]{1,0:T(8,128)S(1)}, u32[]{:S(2)}, u32[]{:S(2)}) collective-permute-start(f32[64,128]{1,0:T(8,128)S(1)} %get-tuple-element.71), channel_id=1, source_target_pairs={{0,3},{1,2},{2,1},{3,0},{4,7},{5,6},{6,5},{7,4},{8,11},{9,10},{10,... | collective-permute-start | bytes 98312 | tf_op jit(solution)/shard_map/ppermute | solution.py:212
  26.4 0.8 %collective-permute-start.11 = (f32[64,128]{1,0:T(8,128)S(1)}, f32[64,128]{1,0:T(8,128)S(1)}, u32[]{:S(2)}, u32[]{:S(2)}) collective-permute-start(f32[64,128]{1,0:T(8,128)S(1)} %get-tuple-element.73), channel_id=1, source_target_pairs={{0,1},{1,0},{2,3},{3,2},{4,5},{5,4},{6,7},{7,6},{8,9},{9,8},{10,11... | collective-permute-start | bytes 98312 | tf_op jit(solution)/shard_map/ppermute | solution.py:212
  27.2 2.0 %shard_map.80.refs_0_ = f32[8192,128]{1,0:T(8,128)S(1)} custom-call(bf16[8192,128]{1,0:T(8,128)(2,1)S(1)} %bitcast.7, bf16[8192,128]{1,0:T(8,128)(2,1)S(1)} %bitcast.8, f32[128,128]{1,0:T(8,128)S(1)} %get-tuple-element.45.refs_2_.refs_1_, bf16[128,176]{1,0:T(8,128)(2,1)S(1)} %get-tuple-element.46.refs_3_.refs_2_, ...), custom_call_target="tpu_custom_call" | custom-call | flops 805306368 | bytes 8388608 | tf_op jit(solution)/shard_map/pallas_call | solution.py:523
  29.2 2.0 %collective-permute-done.10.refs_12_ = f32[64,128]{1,0:T(8,128)S(1)} collective-permute-done((f32[64,128]{1,0:T(8,128)S(1)}, f32[64,128]{1,0:T(8,128)S(1)}, u32[]{:S(2)}, u32[]{:S(2)}) %collective-permute-start.10) | collective-permute-done | bytes 32800 | tf_op jit(solution)/shard_map/ppermute | solution.py:212
  31.2 3.5 %shard_map.82 = (bf16[8192,128]{1,0:T(8,128)(2,1)S(1)}, bf16[1024,128]{1,0:T(8,128)(2,1)S(1)}, bf16[1024,128]{1,0:T(8,128)(2,1)S(1)}, bf16[1024,128]{1,0:T(8,128...) custom-call(f32[8192,128]{1,0:T(8,128)S(1)} %shard_map.80.refs_0_, ...), custom_call_target="tpu_custom_call" | custom-call | flops 536870912 | bytes 8388608 | tf_op jit(solution)/shard_map/pallas_call | solution.py:660
  34.7 1.5 %collective-permute-start.12 = (bf16[1024,128]{1,0:T(8,128)(2,1)S(1)}, bf16[1024,128]{1,0:T(8,128)(2,1)S(1)}, u32[]{:S(2)}, u32[]{:S(2)}) collective-permute-start(bf16[1024,128]{1,0:T(8,128)(2,1)S(1)} %get-tuple-element.77), channel_id=1, source_target_pairs={{0,4},{1,5},{2,6},{3,7},{4,0},{5,1},{6,2},{7,3},{8,12},{9,13},{10,... | collective-permute-start | bytes 786440 | tf_op jit(solution)/shard_map/ppermute | solution.py:253
  36.2 1.0 %collective-permute-start.14 = (bf16[1024,128]{1,0:T(8,128)(2,1)S(1)}, bf16[1024,128]{1,0:T(8,128)(2,1)S(1)}, u32[]{:S(2)}, u32[]{:S(2)}) collective-permute-start(bf16[1024,128]{1,0:T(8,128)(2,1)S(1)} %get-tuple-element.79), channel_id=1, source_target_pairs={{0,8},{1,9},{2,10},{3,11},{4,12},{5,13},{6,14},{7,15},{8,0},{9,1},... | collective-permute-start | bytes 786440 | tf_op jit(solution)/shard_map/ppermute | solution.py:253
  37.2 1.1 %collective-permute-start.16 = (bf16[128,128]{1,0:T(8,128)(2,1)S(1)}, bf16[128,128]{1,0:T(8,128)(2,1)S(1)}, u32[]{:S(2)}, u32[]{:S(2)}) collective-permute-start(bf16[128,128]{1,0:T(8,128)(2,1)S(1)} %get-tuple-element.80), channel_id=1, source_target_pairs={{0,1},{1,0},{2,3},{3,2},{4,5},{5,4},{6,7},{7,6},{8,9},{9,8},{10,11... | collective-permute-start | bytes 98312 | tf_op jit(solution)/shard_map/ppermute | solution.py:253
  38.2 0.2 collective-permute-start.15
  38.5 2.2 %shard_map.83 = (f32[8192,128]{1,0:T(8,128)S(1)}, bf16[8192,128]{1,0:T(8,128)(2,1)S(1)}) custom-call(bf16[8192,128]{1,0:T(8,128)(2,1)S(1)} %get-tuple-element.74.refs_0_, bf16[8192,128]{1,0:T(8,128)(2,1)S(1)} %bitcast.9, f32[128,128]{1,0:T(8,128)S(1)} %get-tuple-element.45.refs_2_.refs_1_, bf16[128,176]{1,0:T(8,128)(2,1)S(1)} %get-tuple-element.46.refs_3_.refs_2_, ...), custom_call_target="tpu_custom_call" | custom-call | flops 805306368 | bytes 8388608 | tf_op jit(solution)/shard_map/pallas_call | solution.py:523
  40.7 2.6 %collective-permute-done.16.refs_10_ = bf16[128,128]{1,0:T(8,128)(2,1)S(1)} collective-permute-done((bf16[128,128]{1,0:T(8,128)(2,1)S(1)}, bf16[128,128]{1,0:T(8,128)(2,1)S(1)}, u32[]{:S(2)}, u32[]{:S(2)}) %collective-permute-start.16) | collective-permute-done | bytes 32800 | tf_op jit(solution)/shard_map/ppermute | solution.py:253
  43.3 2.8 %shard_map.84 = (bf16[8192,128]{1,0:T(8,128)(2,1)S(1)}, bf16[1024,128]{1,0:T(8,128)(2,1)S(1)}, bf16[1024,128]{1,0:T(8,128)(2,1)S(1)}, bf16[1024,128]{1,0:T(8,128)(2,1)S(1)}, bf16[128,128]{1,0:T(8,128)(2,1)S(1)}) custom-call(f32[8192,128]{1,0:T(8,128)S(1)} %get-tuple-element.76.refs_0_, f32[128,128]{1,0:T(8,128)S(1)} %get-tuple-element.45.refs_2_.refs_1_, ...), custom_call_target="tpu_custom_call" | custom-call | flops 536870912 | bytes 8388608 | tf_op jit(solution)/shard_map/pallas_call | solution.py:660
  46.1 0.5 collective-permute-start.17
  46.6 2.0 %collective-permute-start.21 = (bf16[128,128]{1,0:T(8,128)(2,1)S(1)}, bf16[128,128]{1,0:T(8,128)(2,1)S(1)}, u32[]{:S(2)}, u32[]{:S(2)}) collective-permute-start(bf16[128,128]{1,0:T(8,128)(2,1)S(1)} %get-tuple-element.86), channel_id=1, source_target_pairs={{0,1},{1,0},{2,3},{3,2},{4,5},{5,4},{6,7},{7,6},{8,9},{9,8},{10,11... | collective-permute-start | bytes 98312 | tf_op jit(solution)/shard_map/ppermute | solution.py:253
  48.7 0.2 collective-permute-start.20
  48.9 1.5 %shard_map.85.refs_0_ = f32[8192,128]{1,0:T(8,128)S(1)} custom-call(bf16[8192,128]{1,0:T(8,128)(2,1)S(1)} %get-tuple-element.81.refs_0_, bf16[8192,128]{1,0:T(8,128)(2,1)S(1)} %get-tuple-element.82.refs_1_, f32[128,128]{1,0:T(8,128)S(1)} %get-tuple-element.45.refs_2_.refs_1_, bf16[128,176]{1,0:T(8,128)(2,1)S(1)} %get-tuple-element.46.refs_3_.refs_2_, ...), custom_call_target="tpu_custom_call" | custom-call | flops 805306368 | bytes 8388608 | tf_op jit(solution)/shard_map/pallas_call | solution.py:523
  50.4 3.1 %collective-permute-done.21.refs_10_ = bf16[128,128]{1,0:T(8,128)(2,1)S(1)} collective-permute-done((bf16[128,128]{1,0:T(8,128)(2,1)S(1)}, bf16[128,128]{1,0:T(8,128)(2,1)S(1)}, u32[]{:S(2)}, u32[]{:S(2)}) %collective-permute-start.21) | collective-permute-done | bytes 32800 | tf_op jit(solution)/shard_map/ppermute | solution.py:253
  53.6 2.3 %shard_map.86 = bf16[8192,128]{1,0:T(8,128)(2,1)} custom-call(f32[8192,128]{1,0:T(8,128)S(1)} %shard_map.85.refs_0_, f32[128,128]{1,0:T(8,128)S(1)} %get-tuple-element.45.refs_2_.refs_1_, bf16[128,176]{1,0:T(8,128)(2,1)S(1)} %get-tuple-element.46.refs_3_.refs_2_, bf16[512,256]{1,0:T(8,128)(2,1)S(1)} %get-tuple-element.47.refs_4_.refs_3_, ...), custom_call_target="tpu_custom_call" | custom-call | flops 536870912 | bytes 8388608 | tf_op jit(solution)/shard_map/pallas_call | solution.py:660
  (32 shorter events, 0.1 us)
Async XLA Ops:
  0.6 9.7 %copy-start.2 = (f32[8,8,128]{2,1,0:T(8,128)S(1)}, f32[8,8,128]{2,1,0:T(8,128)}, u32[]{:S(2)}) copy-start(f32[8,8,128]{2,1,0:T(8,128)} %param.8) | copy-start | bytes 98308
  0.6 0.7 %copy-start.3 = (s32[1,1,1,1024]{3,2,1,0:T(1,128)S(1)}, s32[1,1,1,1024]{3,2,1,0:T(1,128)}, u32[]{:S(2)}) copy-start(s32[1,1,1,1024]{3,2,1,0:T(1,128)} %cell_ref.1) | copy-start | bytes 12292
  5.8 9.3 %collective-permute-start.1 = (bf16[1024,128]{1,0:T(8,128)(2,1)S(1)}, bf16[1024,128]{1,0:T(8,128)(2,1)S(1)}, u32[]{:S(2)}, u32[]{:S(2)}) collective-permute-start(bf16[1024,128]{1,0:T(8,128)(2,1)S(1)} %get-tuple-element.53.refs_0_), channel_id=1, source_target_pairs={{0,16},{8,24},{16,0},{24,8},{1,17},{9,25},{17,1},{25,9},{2,18},{10... | collective-permute-start | bytes 786440 | tf_op jit(solution)/shard_map/ppermute | solution.py:687
  8.8 8.7 %collective-permute-start = (bf16[1024,128]{1,0:T(8,128)(2,1)S(1)}, bf16[1024,128]{1,0:T(8,128)(2,1)S(1)}, u32[]{:S(2)}, u32[]{:S(2)}) collective-permute-start(bf16[1024,128]{1,0:T(8,128)(2,1)S(1)} %get-tuple-element.53.refs_0_), channel_id=1, source_target_pairs={{0,8},{8,0},{16,24},{24,16},{1,9},{9,1},{17,25},{25,17},{2,10},{10... | collective-permute-start | bytes 786440 | tf_op jit(solution)/shard_map/ppermute | solution.py:687
  8.8 8.7 %collective-permute-start.3 = (bf16[1024,128]{1,0:T(8,128)(2,1)S(1)}, bf16[1024,128]{1,0:T(8,128)(2,1)S(1)}, u32[]{:S(2)}, u32[]{:S(2)}) collective-permute-start(bf16[1024,128]{1,0:T(8,128)(2,1)S(1)} %get-tuple-element.52), channel_id=1, source_target_pairs={{0,4},{1,5},{2,6},{3,7},{4,0},{5,1},{6,2},{7,3},{8,12},{9,13},{10,... | collective-permute-start | bytes 786440 | tf_op jit(solution)/shard_map/ppermute | solution.py:253
  10.3 16.8 %copy-start.1 = (bf16[128,8,8,128]{3,2,1,0:T(8,128)(2,1)S(1)}, bf16[128,8,8,128]{3,2,1,0:T(8,128)(2,1)}, u32[]{:S(2)}) copy-start(bf16[128,8,8,128]{3,2,1,0:T(8,128)(2,1)} %param.7) | copy-start | bytes 6291460
  13.8 13.4 %copy-start = (bf16[128,8,8,128]{3,2,1,0:T(8,128)(2,1)S(1)}, bf16[128,8,8,128]{3,2,1,0:T(8,128)(2,1)}, u32[]{:S(2)}) copy-start(bf16[128,8,8,128]{3,2,1,0:T(8,128)(2,1)} %param.6) | copy-start | bytes 6291460
  15.1 2.4 %collective-permute-start.2 = (bf16[1024,128]{1,0:T(8,128)(2,1)S(1)}, bf16[1024,128]{1,0:T(8,128)(2,1)S(1)}, u32[]{:S(2)}, u32[]{:S(2)}) collective-permute-start(bf16[1024,128]{1,0:T(8,128)(2,1)S(1)} %collective-permute-done.1.refs_2_), channel_id=1, source_target_pairs={{0,8},{8,0},{16,24},{24,16},{1,9},{9,1},{17,25},{25,17},{2,10},{10... | collective-permute-start | bytes 786440 | tf_op jit(solution)/shard_map/ppermute | solution.py:687
  15.1 6.4 %collective-permute-start.6 = (bf16[1024,128]{1,0:T(8,128)(2,1)S(1)}, bf16[1024,128]{1,0:T(8,128)(2,1)S(1)}, u32[]{:S(2)}, u32[]{:S(2)}) collective-permute-start(bf16[1024,128]{1,0:T(8,128)(2,1)S(1)} %get-tuple-element.65), channel_id=1, source_target_pairs={{0,1},{1,0},{2,3},{3,2},{4,5},{5,4},{6,7},{7,6},{8,16},{9,17},{10,... | collective-permute-start | bytes 786440 | tf_op jit(solution)/shard_map/ppermute | solution.py:253
  17.0 4.6 %collective-permute-start.7 = (bf16[1024,128]{1,0:T(8,128)(2,1)S(1)}, bf16[1024,128]{1,0:T(8,128)(2,1)S(1)}, u32[]{:S(2)}, u32[]{:S(2)}) collective-permute-start(bf16[1024,128]{1,0:T(8,128)(2,1)S(1)} %get-tuple-element.66), channel_id=1, source_target_pairs={{0,8},{1,9},{2,10},{3,11},{4,12},{5,13},{6,14},{7,15},{8,0},{9,1},... | collective-permute-start | bytes 786440 | tf_op jit(solution)/shard_map/ppermute | solution.py:253
  18.3 4.3 %collective-permute-start.8 = (f32[128,128]{1,0:T(8,128)S(1)}, f32[128,128]{1,0:T(8,128)S(1)}, u32[]{:S(2)}, u32[]{:S(2)}) collective-permute-start(f32[128,128]{1,0:T(8,128)S(1)} %get-tuple-element.68), channel_id=1, source_target_pairs={{0,4},{4,0},{1,5},{5,1},{2,6},{6,2},{3,7},{7,3},{8,12},{12,8},{9,1... | collective-permute-start | bytes 196616 | tf_op jit(solution)/shard_map/ppermute | solution.py:207
  19.8 7.3 %collective-permute-start.5 = (bf16[128,128]{1,0:T(8,128)(2,1)S(1)}, bf16[128,128]{1,0:T(8,128)(2,1)S(1)}, u32[]{:S(2)}, u32[]{:S(2)}) collective-permute-start(bf16[128,128]{1,0:T(8,128)(2,1)S(1)} %get-tuple-element.61), channel_id=1, source_target_pairs={{0,1},{1,0},{2,3},{3,2},{4,5},{5,4},{6,7},{7,6},{8,9},{9,8},{10,11... | collective-permute-start | bytes 98312 | tf_op jit(solution)/shard_map/ppermute | solution.py:253
  21.4 5.7 %collective-permute-start.4 = (bf16[128,128]{1,0:T(8,128)(2,1)S(1)}, bf16[128,128]{1,0:T(8,128)(2,1)S(1)}, u32[]{:S(2)}, u32[]{:S(2)}) collective-permute-start(bf16[128,128]{1,0:T(8,128)(2,1)S(1)} %get-tuple-element.61), channel_id=1, source_target_pairs={{0,8},{1,2},{2,1},{3,11},{4,12},{5,6},{6,5},{7,15},{8,0},{9,10},{1... | collective-permute-start | bytes 98312 | tf_op jit(solution)/shard_map/ppermute | solution.py:253
  22.7 6.5 %collective-permute-start.9 = (f32[64,128]{1,0:T(8,128)S(1)}, f32[64,128]{1,0:T(8,128)S(1)}, u32[]{:S(2)}, u32[]{:S(2)}) collective-permute-start(f32[64,128]{1,0:T(8,128)S(1)} %get-tuple-element.71), channel_id=1, source_target_pairs={{0,3},{1,2},{2,1},{3,0},{4,7},{5,6},{6,5},{7,4},{8,11},{9,10},{10,... | collective-permute-start | bytes 98312 | tf_op jit(solution)/shard_map/ppermute | solution.py:212
  26.4 4.8 %collective-permute-start.10 = (f32[64,128]{1,0:T(8,128)S(1)}, f32[64,128]{1,0:T(8,128)S(1)}, u32[]{:S(2)}, u32[]{:S(2)}) collective-permute-start(f32[64,128]{1,0:T(8,128)S(1)} %get-tuple-element.72), channel_id=1, source_target_pairs={{0,2},{1,3},{2,0},{3,1},{4,6},{5,7},{6,4},{7,5},{8,10},{9,11},{10,... | collective-permute-start | bytes 98312 | tf_op jit(solution)/shard_map/ppermute | solution.py:212
  26.4 4.8 %collective-permute-start.11 = (f32[64,128]{1,0:T(8,128)S(1)}, f32[64,128]{1,0:T(8,128)S(1)}, u32[]{:S(2)}, u32[]{:S(2)}) collective-permute-start(f32[64,128]{1,0:T(8,128)S(1)} %get-tuple-element.73), channel_id=1, source_target_pairs={{0,1},{1,0},{2,3},{3,2},{4,5},{5,4},{6,7},{7,6},{8,9},{9,8},{10,11... | collective-permute-start | bytes 98312 | tf_op jit(solution)/shard_map/ppermute | solution.py:212
  27.2 4.0 %copy-start.4 = (s32[1,1,1,32]{3,2,1,0:T(1,128)S(1)}, s32[1,1,1,32]{3,2,1,0:T(1,128)}, u32[]{:S(2)}) copy-start(s32[1,1,1,32]{3,2,1,0:T(1,128)} %refs_6_.1) | copy-start | bytes 388
  34.7 8.6 %collective-permute-start.12 = (bf16[1024,128]{1,0:T(8,128)(2,1)S(1)}, bf16[1024,128]{1,0:T(8,128)(2,1)S(1)}, u32[]{:S(2)}, u32[]{:S(2)}) collective-permute-start(bf16[1024,128]{1,0:T(8,128)(2,1)S(1)} %get-tuple-element.77), channel_id=1, source_target_pairs={{0,4},{1,5},{2,6},{3,7},{4,0},{5,1},{6,2},{7,3},{8,12},{9,13},{10,... | collective-permute-start | bytes 786440 | tf_op jit(solution)/shard_map/ppermute | solution.py:253
  36.2 7.1 %collective-permute-start.13 = (bf16[1024,128]{1,0:T(8,128)(2,1)S(1)}, bf16[1024,128]{1,0:T(8,128)(2,1)S(1)}, u32[]{:S(2)}, u32[]{:S(2)}) collective-permute-start(bf16[1024,128]{1,0:T(8,128)(2,1)S(1)} %get-tuple-element.78), channel_id=1, source_target_pairs={{0,1},{1,0},{2,3},{3,2},{4,5},{5,4},{6,7},{7,6},{8,16},{9,17},{10,... | collective-permute-start | bytes 786440 | tf_op jit(solution)/shard_map/ppermute | solution.py:253
  36.2 7.1 %collective-permute-start.14 = (bf16[1024,128]{1,0:T(8,128)(2,1)S(1)}, bf16[1024,128]{1,0:T(8,128)(2,1)S(1)}, u32[]{:S(2)}, u32[]{:S(2)}) collective-permute-start(bf16[1024,128]{1,0:T(8,128)(2,1)S(1)} %get-tuple-element.79), channel_id=1, source_target_pairs={{0,8},{1,9},{2,10},{3,11},{4,12},{5,13},{6,14},{7,15},{8,0},{9,1},... | collective-permute-start | bytes 786440 | tf_op jit(solution)/shard_map/ppermute | solution.py:253
  37.2 6.1 %collective-permute-start.16 = (bf16[128,128]{1,0:T(8,128)(2,1)S(1)}, bf16[128,128]{1,0:T(8,128)(2,1)S(1)}, u32[]{:S(2)}, u32[]{:S(2)}) collective-permute-start(bf16[128,128]{1,0:T(8,128)(2,1)S(1)} %get-tuple-element.80), channel_id=1, source_target_pairs={{0,1},{1,0},{2,3},{3,2},{4,5},{5,4},{6,7},{7,6},{8,9},{9,8},{10,11... | collective-permute-start | bytes 98312 | tf_op jit(solution)/shard_map/ppermute | solution.py:253
  38.2 5.0 %collective-permute-start.15 = (bf16[128,128]{1,0:T(8,128)(2,1)S(1)}, bf16[128,128]{1,0:T(8,128)(2,1)S(1)}, u32[]{:S(2)}, u32[]{:S(2)}) collective-permute-start(bf16[128,128]{1,0:T(8,128)(2,1)S(1)} %get-tuple-element.80), channel_id=1, source_target_pairs={{0,8},{1,2},{2,1},{3,11},{4,12},{5,6},{6,5},{7,15},{8,0},{9,10},{1... | collective-permute-start | bytes 98312 | tf_op jit(solution)/shard_map/ppermute | solution.py:253
  46.1 7.4 %collective-permute-start.17 = (bf16[1024,128]{1,0:T(8,128)(2,1)S(1)}, bf16[1024,128]{1,0:T(8,128)(2,1)S(1)}, u32[]{:S(2)}, u32[]{:S(2)}) collective-permute-start(bf16[1024,128]{1,0:T(8,128)(2,1)S(1)} %get-tuple-element.83), channel_id=1, source_target_pairs={{0,4},{1,5},{2,6},{3,7},{4,0},{5,1},{6,2},{7,3},{8,12},{9,13},{10,... | collective-permute-start | bytes 786440 | tf_op jit(solution)/shard_map/ppermute | solution.py:253
  46.6 6.9 %collective-permute-start.18 = (bf16[1024,128]{1,0:T(8,128)(2,1)S(1)}, bf16[1024,128]{1,0:T(8,128)(2,1)S(1)}, u32[]{:S(2)}, u32[]{:S(2)}) collective-permute-start(bf16[1024,128]{1,0:T(8,128)(2,1)S(1)} %get-tuple-element.84), channel_id=1, source_target_pairs={{0,1},{1,0},{2,3},{3,2},{4,5},{5,4},{6,7},{7,6},{8,16},{9,17},{10,... | collective-permute-start | bytes 786440 | tf_op jit(solution)/shard_map/ppermute | solution.py:253
  46.6 6.9 %collective-permute-start.19 = (bf16[1024,128]{1,0:T(8,128)(2,1)S(1)}, bf16[1024,128]{1,0:T(8,128)(2,1)S(1)}, u32[]{:S(2)}, u32[]{:S(2)}) collective-permute-start(bf16[1024,128]{1,0:T(8,128)(2,1)S(1)} %get-tuple-element.85), channel_id=1, source_target_pairs={{0,8},{1,9},{2,10},{3,11},{4,12},{5,13},{6,14},{7,15},{8,0},{9,1},... | collective-permute-start | bytes 786440 | tf_op jit(solution)/shard_map/ppermute | solution.py:253
  46.6 6.9 %collective-permute-start.21 = (bf16[128,128]{1,0:T(8,128)(2,1)S(1)}, bf16[128,128]{1,0:T(8,128)(2,1)S(1)}, u32[]{:S(2)}, u32[]{:S(2)}) collective-permute-start(bf16[128,128]{1,0:T(8,128)(2,1)S(1)} %get-tuple-element.86), channel_id=1, source_target_pairs={{0,1},{1,0},{2,3},{3,2},{4,5},{5,4},{6,7},{7,6},{8,9},{9,8},{10,11... | collective-permute-start | bytes 98312 | tf_op jit(solution)/shard_map/ppermute | solution.py:253
  48.7 4.9 %collective-permute-start.20 = (bf16[128,128]{1,0:T(8,128)(2,1)S(1)}, bf16[128,128]{1,0:T(8,128)(2,1)S(1)}, u32[]{:S(2)}, u32[]{:S(2)}) collective-permute-start(bf16[128,128]{1,0:T(8,128)(2,1)S(1)} %get-tuple-element.86), channel_id=1, source_target_pairs={{0,8},{1,2},{2,1},{3,11},{4,12},{5,6},{6,5},{7,15},{8,0},{9,10},{1... | collective-permute-start | bytes 98312 | tf_op jit(solution)/shard_map/ppermute | solution.py:253

commit v17 on v16

--- a/solution.py
+++ b/solution.py
@@ -66,13 +66,16 @@
     for part in range(parts):
         place[:, part * width : (part + 1) * width] = first + digits // stride**part % stride
 
+    pitch = rows + 1
     together = 128 // per_row
     group = iota((8, 128), 1) // per_row
     for step in range(sides // block):
         copies[step].wait()
         span = field[step * block : (step + 1) * block]
-        tall[step] = span.reshape(block * rows, lanes).astype(F32)
-        cut_faces(shape, shape.outer, step * block, block, tall.at[step], face_refs)
+        for side in range(block):
+            start = side * pitch
+            tall[step, start : start + rows, :] = span[side].astype(F32)
+        cut_faces(shape, shape.outer, step * block, block, tall.at[step], face_refs, pitch)
 
         for batch in range(block // 8):
             for tile in range(rows // together):
@@ -80,8 +83,8 @@
                 where = place[:, cols]
                 found = None
                 for row in range(together):
-                    start = batch * 8 * rows + tile * together + row
-                    line = tall[step, pl.ds(start, 8, stride=rows), :]
+                    start = batch * 8 * pitch + tile * together + row
+                    line = tall[step, pl.ds(start, 8, stride=pitch), :]
                     line = jnp.take_along_axis(line, where, axis=1)
                     found = line if found is None else jnp.where(group == row, line, found)
                 at = step * block + batch * 8
@@ -108,7 +111,7 @@
         scratch_shapes=[
             pltpu.VMEM(field.shape, BF),
             pltpu.VMEM(trace_cell.shape, jnp.int32),
-            pltpu.VMEM((sides // block, block * rows, lanes), F32),
+            pltpu.VMEM((sides // block, block * (rows + 1), lanes), F32),
             pltpu.VMEM((width, slots), BF),
             pltpu.VMEM((8, slots), jnp.int32),
             pltpu.VMEM((sides, slots), F32),
@@ -320,12 +323,12 @@
     rsum[...] = (iota(dims, 1) // shape.cells == iota(dims, 0)).astype(BF)
 
 
-def cut_faces(shape, faces, at, block, tall, face_refs):
+def cut_faces(shape, faces, at, block, tall, face_refs, pitch=None):
     for face, ref in zip(faces, face_refs):
         length, edge = shape.face_len(face), shape.edge(face)
         lines = []
         for side in range(block):
-            start = side * shape.cells
+            start = side * (pitch or shape.cells)
             if face[0] == "row":
                 lines.append(tall[pl.ds(aligned(start + edge * length, 8), length), :])
             else:

time: 56.2 us -> 55 us (0.979)
  Pallas kernels: 23.1 us -> 21.6 us
    pallas_call x1, Pallas kernels: 4.48 us -> 3.03 us  [traces(): pl.pallas_call(functools.partial(trace_kernel, shape, stride, block), in_...]
where the time goes in v17:
time: 55 us; the launch traced here: 54.8 us
  Pallas kernels  21.6 us (39%)
  starting transfers between devices  20.5 us (37%)
  waiting for transfers between devices  10.9 us (20%)
  between operations  0.94 us (2%)
  local copies, waits for them, and re-layouts  0.71 us (1%)
    ppermute x15, starting transfers between devices, swap(): return lax.ppermute(value, axes, pairs)  11.5 us
    pallas_call x3, Pallas kernels, sweep_finish(): pl.pallas_call(functools.partial(finish_kernel, shape, len(ends), len(rec...  8.8 us
    ppermute x15, waiting for transfers between devices, swap(): return lax.ppermute(value, axes, pairs)  6.53 us
    pallas_call x3, Pallas kernels, sweep_base(): pl.pallas_call(functools.partial(base_kernel, shape, len(ends), phi is no...  5.53 us
    ppermute x3, starting transfers between devices, flux_sums(): lax.ppermute(sent[key], 'gz', [(i, i ^ key) for i in range(gzs)])  4.45 us
    pallas_call x1, Pallas kernels, first_faces(): pl.pallas_call(functools.partial(faces_kernel, shape, slots), in_specs=[h...  3.45 us
    pallas_call x1, Pallas kernels, traces(): pl.pallas_call(functools.partial(trace_kernel, shape, stride, block), in_...  3.03 us
    ppermute x3, starting transfers between devices, row_gather(): lax.ppermute(held[key], 'row', pairs)  3.01 us
  transfers between devices with their start and end apart: 22, of which 7 were waited for; matrix products, arithmetic and copies ran while one was open for 0% of the time, Pallas kernels for 18%

profile of v17, /device:TPU:0, one launch (start us, length us, event | category | flops | bytes accessed | tf_op | source)
XLA Modules:
  0.0 54.8 jit_solution(14826549891033600625)
XLA Ops:
  0.6 0.7 %copy-done.3 = s32[1,1,1,1024]{3,2,1,0:T(1,128)S(1)} copy-done((s32[1,1,1,1024]{3,2,1,0:T(1,128)S(1)}, s32[1,1,1,1024]{3,2,1,0:T(1,128)}, u32[]{:S(2)}) %copy-start.3) | copy-done | bytes 4120
  1.3 3.0 %shard_map.78 = (bf16[1024,128]{1,0:T(8,128)(2,1)S(1)}, bf16[1024,128]{1,0:T(8,128)(2,1)S(1)}) custom-call(bf16[128,64,128]{2,1,0:T(8,128)(2,1)} %bitcast.5, s32[1,1,1,1024]{3,2,1,0:T(1,128)S(1)} %copy-done.3), custom_call_target="tpu_custom_call" | custom-call | flops 536870912 | bytes 2097152 | tf_op jit(solution)/shard_map/pallas_call | solution.py:106
  4.4 3.0 %collective-permute-start.1 = (bf16[1024,128]{1,0:T(8,128)(2,1)S(1)}, bf16[1024,128]{1,0:T(8,128)(2,1)S(1)}, u32[]{:S(2)}, u32[]{:S(2)}) collective-permute-start(bf16[1024,128]{1,0:T(8,128)(2,1)S(1)} %get-tuple-element.53.refs_0_), channel_id=1, source_target_pairs={{0,16},{8,24},{16,0},{24,8},{1,17},{9,25},{17,1},{25,9},{2,18},{10... | collective-permute-start | bytes 786440 | tf_op jit(solution)/shard_map/ppermute | solution.py:690
  7.4 1.5 %collective-permute-start.3 = (bf16[1024,128]{1,0:T(8,128)(2,1)S(1)}, bf16[1024,128]{1,0:T(8,128)(2,1)S(1)}, u32[]{:S(2)}, u32[]{:S(2)}) collective-permute-start(bf16[1024,128]{1,0:T(8,128)(2,1)S(1)} %get-tuple-element.52), channel_id=1, source_target_pairs={{0,4},{1,5},{2,6},{3,7},{4,0},{5,1},{6,2},{7,3},{8,12},{9,13},{10,... | collective-permute-start | bytes 786440 | tf_op jit(solution)/shard_map/ppermute | solution.py:256
  8.9 3.5 %shard_map.77 = (bf16[1024,128]{1,0:T(8,128)(2,1)S(1)}, bf16[1024,128]{1,0:T(8,128)(2,1)S(1)}, bf16[128,128]{1,0:T(8,128)(2,1)S(1)}, bf16[4,256,1024]{2,1,0:T(8,...) custom-call(bf16[8192,128]{1,0:T(8,128)(2,1)} %bitcast.6, ...), custom_call_target="tpu_custom_call" | custom-call | flops 134217728 | bytes 4194304 | tf_op jit(solution)/shard_map/pallas_call | solution.py:419
  12.4 1.3 %collective-permute-done.1.refs_2_ = bf16[1024,128]{1,0:T(8,128)(2,1)S(1)} collective-permute-done((bf16[1024,128]{1,0:T(8,128)(2,1)S(1)}, bf16[1024,128]{1,0:T(8,128)(2,1)S(1)}, u32[]{:S(2)}, u32[]{:S(2)}) %collective-permute-start.1) | collective-permute-done | bytes 262176 | tf_op jit(solution)/shard_map/ppermute | solution.py:690
  13.7 1.8 %collective-permute-start.6 = (bf16[1024,128]{1,0:T(8,128)(2,1)S(1)}, bf16[1024,128]{1,0:T(8,128)(2,1)S(1)}, u32[]{:S(2)}, u32[]{:S(2)}) collective-permute-start(bf16[1024,128]{1,0:T(8,128)(2,1)S(1)} %get-tuple-element.65), channel_id=1, source_target_pairs={{0,1},{1,0},{2,3},{3,2},{4,5},{5,4},{6,7},{7,6},{8,16},{9,17},{10,... | collective-permute-start | bytes 786440 | tf_op jit(solution)/shard_map/ppermute | solution.py:256
  15.5 0.6 %collective-permute-done.3.refs_6_ = bf16[1024,128]{1,0:T(8,128)(2,1)S(1)} collective-permute-done((bf16[1024,128]{1,0:T(8,128)(2,1)S(1)}, bf16[1024,128]{1,0:T(8,128)(2,1)S(1)}, u32[]{:S(2)}, u32[]{:S(2)}) %collective-permute-start.3) | collective-permute-done | bytes 262176 | tf_op jit(solution)/shard_map/ppermute | solution.py:256
  16.1 0.7 %shard_map.79 = (f32[128,128]{1,0:T(8,128)S(1)}, f32[128,128]{1,0:T(8,128)S(1)}) custom-call(bf16[1024,128]{1,0:T(8,128)(2,1)S(1)} %get-tuple-element.53.refs_0_, bf16[1024,128]{1,0:T(8,128)(2,1)S(1)} %collective-permute-done.refs_1_, bf16[1024,128]{1,0:T(8,128)(2,1)S(1)} %collective-permute-done.1.refs_2_, ...), custom_call_target="tpu_custom_call" | custom-call | flops 268435456 | bytes 2097152 | tf_op jit(solution)/shard_map/pallas_call | solution.py:160
  16.8 1.6 %collective-permute-start.8 = (f32[128,128]{1,0:T(8,128)S(1)}, f32[128,128]{1,0:T(8,128)S(1)}, u32[]{:S(2)}, u32[]{:S(2)}) collective-permute-start(f32[128,128]{1,0:T(8,128)S(1)} %get-tuple-element.68), channel_id=1, source_target_pairs={{0,4},{4,0},{1,5},{5,1},{2,6},{6,2},{3,7},{7,3},{8,12},{12,8},{9,1... | collective-permute-start | bytes 196616 | tf_op jit(solution)/shard_map/ppermute | solution.py:210
  18.4 1.6 %collective-permute-start.5 = (bf16[128,128]{1,0:T(8,128)(2,1)S(1)}, bf16[128,128]{1,0:T(8,128)(2,1)S(1)}, u32[]{:S(2)}, u32[]{:S(2)}) collective-permute-start(bf16[128,128]{1,0:T(8,128)(2,1)S(1)} %get-tuple-element.61), channel_id=1, source_target_pairs={{0,1},{1,0},{2,3},{3,2},{4,5},{5,4},{6,7},{7,6},{8,9},{9,8},{10,11... | collective-permute-start | bytes 98312 | tf_op jit(solution)/shard_map/ppermute | solution.py:256
  20.0 0.1 collective-permute-done.6.refs_7_
  20.1 1.1 %collective-permute-done.8.other_ref = f32[128,128]{1,0:T(8,128)S(1)} collective-permute-done((f32[128,128]{1,0:T(8,128)S(1)}, f32[128,128]{1,0:T(8,128)S(1)}, u32[]{:S(2)}, u32[]{:S(2)}) %collective-permute-start.8) | collective-permute-done | bytes 65568 | tf_op jit(solution)/shard_map/ppermute | solution.py:210
  21.2 0.1 shard_map.81
  21.3 3.7 %collective-permute-start.9 = (f32[64,128]{1,0:T(8,128)S(1)}, f32[64,128]{1,0:T(8,128)S(1)}, u32[]{:S(2)}, u32[]{:S(2)}) collective-permute-start(f32[64,128]{1,0:T(8,128)S(1)} %get-tuple-element.71), channel_id=1, source_target_pairs={{0,3},{1,2},{2,1},{3,0},{4,7},{5,6},{6,5},{7,4},{8,11},{9,10},{10,... | collective-permute-start | bytes 98312 | tf_op jit(solution)/shard_map/ppermute | solution.py:215
  24.9 0.8 %collective-permute-start.11 = (f32[64,128]{1,0:T(8,128)S(1)}, f32[64,128]{1,0:T(8,128)S(1)}, u32[]{:S(2)}, u32[]{:S(2)}) collective-permute-start(f32[64,128]{1,0:T(8,128)S(1)} %get-tuple-element.73), channel_id=1, source_target_pairs={{0,1},{1,0},{2,3},{3,2},{4,5},{5,4},{6,7},{7,6},{8,9},{9,8},{10,11... | collective-permute-start | bytes 98312 | tf_op jit(solution)/shard_map/ppermute | solution.py:215
  25.8 2.0 %shard_map.80.refs_0_ = f32[8192,128]{1,0:T(8,128)S(1)} custom-call(bf16[8192,128]{1,0:T(8,128)(2,1)S(1)} %bitcast.7, bf16[8192,128]{1,0:T(8,128)(2,1)S(1)} %bitcast.8, f32[128,128]{1,0:T(8,128)S(1)} %get-tuple-element.45.refs_2_.refs_1_, bf16[128,176]{1,0:T(8,128)(2,1)S(1)} %get-tuple-element.46.refs_3_.refs_2_, ...), custom_call_target="tpu_custom_call" | custom-call | flops 805306368 | bytes 8388608 | tf_op jit(solution)/shard_map/pallas_call | solution.py:526
  27.7 2.0 %collective-permute-done.10.refs_12_ = f32[64,128]{1,0:T(8,128)S(1)} collective-permute-done((f32[64,128]{1,0:T(8,128)S(1)}, f32[64,128]{1,0:T(8,128)S(1)}, u32[]{:S(2)}, u32[]{:S(2)}) %collective-permute-start.10) | collective-permute-done | bytes 32800 | tf_op jit(solution)/shard_map/ppermute | solution.py:215
  29.8 3.5 %shard_map.82 = (bf16[8192,128]{1,0:T(8,128)(2,1)S(1)}, bf16[1024,128]{1,0:T(8,128)(2,1)S(1)}, bf16[1024,128]{1,0:T(8,128)(2,1)S(1)}, bf16[1024,128]{1,0:T(8,128...) custom-call(f32[8192,128]{1,0:T(8,128)S(1)} %shard_map.80.refs_0_, ...), custom_call_target="tpu_custom_call" | custom-call | flops 536870912 | bytes 8388608 | tf_op jit(solution)/shard_map/pallas_call | solution.py:663
  33.2 1.5 %collective-permute-start.12 = (bf16[1024,128]{1,0:T(8,128)(2,1)S(1)}, bf16[1024,128]{1,0:T(8,128)(2,1)S(1)}, u32[]{:S(2)}, u32[]{:S(2)}) collective-permute-start(bf16[1024,128]{1,0:T(8,128)(2,1)S(1)} %get-tuple-element.77), channel_id=1, source_target_pairs={{0,4},{1,5},{2,6},{3,7},{4,0},{5,1},{6,2},{7,3},{8,12},{9,13},{10,... | collective-permute-start | bytes 786440 | tf_op jit(solution)/shard_map/ppermute | solution.py:256
  34.7 1.0 %collective-permute-start.14 = (bf16[1024,128]{1,0:T(8,128)(2,1)S(1)}, bf16[1024,128]{1,0:T(8,128)(2,1)S(1)}, u32[]{:S(2)}, u32[]{:S(2)}) collective-permute-start(bf16[1024,128]{1,0:T(8,128)(2,1)S(1)} %get-tuple-element.79), channel_id=1, source_target_pairs={{0,8},{1,9},{2,10},{3,11},{4,12},{5,13},{6,14},{7,15},{8,0},{9,1},... | collective-permute-start | bytes 786440 | tf_op jit(solution)/shard_map/ppermute | solution.py:256
  35.7 1.1 %collective-permute-start.16 = (bf16[128,128]{1,0:T(8,128)(2,1)S(1)}, bf16[128,128]{1,0:T(8,128)(2,1)S(1)}, u32[]{:S(2)}, u32[]{:S(2)}) collective-permute-start(bf16[128,128]{1,0:T(8,128)(2,1)S(1)} %get-tuple-element.80), channel_id=1, source_target_pairs={{0,1},{1,0},{2,3},{3,2},{4,5},{5,4},{6,7},{7,6},{8,9},{9,8},{10,11... | collective-permute-start | bytes 98312 | tf_op jit(solution)/shard_map/ppermute | solution.py:256
  36.8 0.2 collective-permute-start.15
  37.0 2.0 %shard_map.83 = (f32[8192,128]{1,0:T(8,128)S(1)}, bf16[8192,128]{1,0:T(8,128)(2,1)S(1)}) custom-call(bf16[8192,128]{1,0:T(8,128)(2,1)S(1)} %get-tuple-element.74.refs_0_, bf16[8192,128]{1,0:T(8,128)(2,1)S(1)} %bitcast.9, f32[128,128]{1,0:T(8,128)S(1)} %get-tuple-element.45.refs_2_.refs_1_, bf16[128,176]{1,0:T(8,128)(2,1)S(1)} %get-tuple-element.46.refs_3_.refs_2_, ...), custom_call_target="tpu_custom_call" | custom-call | flops 805306368 | bytes 8388608 | tf_op jit(solution)/shard_map/pallas_call | solution.py:526
  39.1 2.8 %collective-permute-done.16.refs_10_ = bf16[128,128]{1,0:T(8,128)(2,1)S(1)} collective-permute-done((bf16[128,128]{1,0:T(8,128)(2,1)S(1)}, bf16[128,128]{1,0:T(8,128)(2,1)S(1)}, u32[]{:S(2)}, u32[]{:S(2)}) %collective-permute-start.16) | collective-permute-done | bytes 32800 | tf_op jit(solution)/shard_map/ppermute | solution.py:256
  41.8 3.0 %shard_map.84 = (bf16[8192,128]{1,0:T(8,128)(2,1)S(1)}, bf16[1024,128]{1,0:T(8,128)(2,1)S(1)}, bf16[1024,128]{1,0:T(8,128)(2,1)S(1)}, bf16[1024,128]{1,0:T(8,128)(2,1)S(1)}, bf16[128,128]{1,0:T(8,128)(2,1)S(1)}) custom-call(f32[8192,128]{1,0:T(8,128)S(1)} %get-tuple-element.76.refs_0_, f32[128,128]{1,0:T(8,128)S(1)} %get-tuple-element.45.refs_2_.refs_1_, ...), custom_call_target="tpu_custom_call" | custom-call | flops 536870912 | bytes 8388608 | tf_op jit(solution)/shard_map/pallas_call | solution.py:663
  44.9 0.5 collective-permute-start.17
  45.4 2.0 %collective-permute-start.21 = (bf16[128,128]{1,0:T(8,128)(2,1)S(1)}, bf16[128,128]{1,0:T(8,128)(2,1)S(1)}, u32[]{:S(2)}, u32[]{:S(2)}) collective-permute-start(bf16[128,128]{1,0:T(8,128)(2,1)S(1)} %get-tuple-element.86), channel_id=1, source_target_pairs={{0,1},{1,0},{2,3},{3,2},{4,5},{5,4},{6,7},{7,6},{8,9},{9,8},{10,11... | collective-permute-start | bytes 98312 | tf_op jit(solution)/shard_map/ppermute | solution.py:256
  47.4 0.2 collective-permute-start.20
  47.6 1.5 %shard_map.85.refs_0_ = f32[8192,128]{1,0:T(8,128)S(1)} custom-call(bf16[8192,128]{1,0:T(8,128)(2,1)S(1)} %get-tuple-element.81.refs_0_, bf16[8192,128]{1,0:T(8,128)(2,1)S(1)} %get-tuple-element.82.refs_1_, f32[128,128]{1,0:T(8,128)S(1)} %get-tuple-element.45.refs_2_.refs_1_, bf16[128,176]{1,0:T(8,128)(2,1)S(1)} %get-tuple-element.46.refs_3_.refs_2_, ...), custom_call_target="tpu_custom_call" | custom-call | flops 805306368 | bytes 8388608 | tf_op jit(solution)/shard_map/pallas_call | solution.py:526
  49.2 3.1 %collective-permute-done.21.refs_10_ = bf16[128,128]{1,0:T(8,128)(2,1)S(1)} collective-permute-done((bf16[128,128]{1,0:T(8,128)(2,1)S(1)}, bf16[128,128]{1,0:T(8,128)(2,1)S(1)}, u32[]{:S(2)}, u32[]{:S(2)}) %collective-permute-start.21) | collective-permute-done | bytes 32800 | tf_op jit(solution)/shard_map/ppermute | solution.py:256
  52.3 2.3 %shard_map.86 = bf16[8192,128]{1,0:T(8,128)(2,1)} custom-call(f32[8192,128]{1,0:T(8,128)S(1)} %shard_map.85.refs_0_, f32[128,128]{1,0:T(8,128)S(1)} %get-tuple-element.45.refs_2_.refs_1_, bf16[128,176]{1,0:T(8,128)(2,1)S(1)} %get-tuple-element.46.refs_3_.refs_2_, bf16[512,256]{1,0:T(8,128)(2,1)S(1)} %get-tuple-element.47.refs_4_.refs_3_, ...), custom_call_target="tpu_custom_call" | custom-call | flops 536870912 | bytes 8388608 | tf_op jit(solution)/shard_map/pallas_call | solution.py:663
  (32 shorter events, 0.1 us)
Async XLA Ops:
  0.6 8.3 %copy-start.2 = (f32[8,8,128]{2,1,0:T(8,128)S(1)}, f32[8,8,128]{2,1,0:T(8,128)}, u32[]{:S(2)}) copy-start(f32[8,8,128]{2,1,0:T(8,128)} %param.8) | copy-start | bytes 98308
  0.6 0.7 %copy-start.3 = (s32[1,1,1,1024]{3,2,1,0:T(1,128)S(1)}, s32[1,1,1,1024]{3,2,1,0:T(1,128)}, u32[]{:S(2)}) copy-start(s32[1,1,1,1024]{3,2,1,0:T(1,128)} %cell_ref.1) | copy-start | bytes 12292
  4.4 9.3 %collective-permute-start.1 = (bf16[1024,128]{1,0:T(8,128)(2,1)S(1)}, bf16[1024,128]{1,0:T(8,128)(2,1)S(1)}, u32[]{:S(2)}, u32[]{:S(2)}) collective-permute-start(bf16[1024,128]{1,0:T(8,128)(2,1)S(1)} %get-tuple-element.53.refs_0_), channel_id=1, source_target_pairs={{0,16},{8,24},{16,0},{24,8},{1,17},{9,25},{17,1},{25,9},{2,18},{10... | collective-permute-start | bytes 786440 | tf_op jit(solution)/shard_map/ppermute | solution.py:690
  7.4 8.7 %collective-permute-start = (bf16[1024,128]{1,0:T(8,128)(2,1)S(1)}, bf16[1024,128]{1,0:T(8,128)(2,1)S(1)}, u32[]{:S(2)}, u32[]{:S(2)}) collective-permute-start(bf16[1024,128]{1,0:T(8,128)(2,1)S(1)} %get-tuple-element.53.refs_0_), channel_id=1, source_target_pairs={{0,8},{8,0},{16,24},{24,16},{1,9},{9,1},{17,25},{25,17},{2,10},{10... | collective-permute-start | bytes 786440 | tf_op jit(solution)/shard_map/ppermute | solution.py:690
  7.4 8.7 %collective-permute-start.3 = (bf16[1024,128]{1,0:T(8,128)(2,1)S(1)}, bf16[1024,128]{1,0:T(8,128)(2,1)S(1)}, u32[]{:S(2)}, u32[]{:S(2)}) collective-permute-start(bf16[1024,128]{1,0:T(8,128)(2,1)S(1)} %get-tuple-element.52), channel_id=1, source_target_pairs={{0,4},{1,5},{2,6},{3,7},{4,0},{5,1},{6,2},{7,3},{8,12},{9,13},{10,... | collective-permute-start | bytes 786440 | tf_op jit(solution)/shard_map/ppermute | solution.py:256
  8.9 16.8 %copy-start.1 = (bf16[128,8,8,128]{3,2,1,0:T(8,128)(2,1)S(1)}, bf16[128,8,8,128]{3,2,1,0:T(8,128)(2,1)}, u32[]{:S(2)}) copy-start(bf16[128,8,8,128]{3,2,1,0:T(8,128)(2,1)} %param.7) | copy-start | bytes 6291460
  12.4 13.4 %copy-start = (bf16[128,8,8,128]{3,2,1,0:T(8,128)(2,1)S(1)}, bf16[128,8,8,128]{3,2,1,0:T(8,128)(2,1)}, u32[]{:S(2)}) copy-start(bf16[128,8,8,128]{3,2,1,0:T(8,128)(2,1)} %param.6) | copy-start | bytes 6291460
  13.7 2.4 %collective-permute-start.2 = (bf16[1024,128]{1,0:T(8,128)(2,1)S(1)}, bf16[1024,128]{1,0:T(8,128)(2,1)S(1)}, u32[]{:S(2)}, u32[]{:S(2)}) collective-permute-start(bf16[1024,128]{1,0:T(8,128)(2,1)S(1)} %collective-permute-done.1.refs_2_), channel_id=1, source_target_pairs={{0,8},{8,0},{16,24},{24,16},{1,9},{9,1},{17,25},{25,17},{2,10},{10... | collective-permute-start | bytes 786440 | tf_op jit(solution)/shard_map/ppermute | solution.py:690
  13.7 6.4 %collective-permute-start.6 = (bf16[1024,128]{1,0:T(8,128)(2,1)S(1)}, bf16[1024,128]{1,0:T(8,128)(2,1)S(1)}, u32[]{:S(2)}, u32[]{:S(2)}) collective-permute-start(bf16[1024,128]{1,0:T(8,128)(2,1)S(1)} %get-tuple-element.65), channel_id=1, source_target_pairs={{0,1},{1,0},{2,3},{3,2},{4,5},{5,4},{6,7},{7,6},{8,16},{9,17},{10,... | collective-permute-start | bytes 786440 | tf_op jit(solution)/shard_map/ppermute | solution.py:256
  15.5 4.5 %collective-permute-start.7 = (bf16[1024,128]{1,0:T(8,128)(2,1)S(1)}, bf16[1024,128]{1,0:T(8,128)(2,1)S(1)}, u32[]{:S(2)}, u32[]{:S(2)}) collective-permute-start(bf16[1024,128]{1,0:T(8,128)(2,1)S(1)} %get-tuple-element.66), channel_id=1, source_target_pairs={{0,8},{1,9},{2,10},{3,11},{4,12},{5,13},{6,14},{7,15},{8,0},{9,1},... | collective-permute-start | bytes 786440 | tf_op jit(solution)/shard_map/ppermute | solution.py:256
  16.8 4.3 %collective-permute-start.8 = (f32[128,128]{1,0:T(8,128)S(1)}, f32[128,128]{1,0:T(8,128)S(1)}, u32[]{:S(2)}, u32[]{:S(2)}) collective-permute-start(f32[128,128]{1,0:T(8,128)S(1)} %get-tuple-element.68), channel_id=1, source_target_pairs={{0,4},{4,0},{1,5},{5,1},{2,6},{6,2},{3,7},{7,3},{8,12},{12,8},{9,1... | collective-permute-start | bytes 196616 | tf_op jit(solution)/shard_map/ppermute | solution.py:210
  18.4 7.3 %collective-permute-start.5 = (bf16[128,128]{1,0:T(8,128)(2,1)S(1)}, bf16[128,128]{1,0:T(8,128)(2,1)S(1)}, u32[]{:S(2)}, u32[]{:S(2)}) collective-permute-start(bf16[128,128]{1,0:T(8,128)(2,1)S(1)} %get-tuple-element.61), channel_id=1, source_target_pairs={{0,1},{1,0},{2,3},{3,2},{4,5},{5,4},{6,7},{7,6},{8,9},{9,8},{10,11... | collective-permute-start | bytes 98312 | tf_op jit(solution)/shard_map/ppermute | solution.py:256
  20.0 5.7 %collective-permute-start.4 = (bf16[128,128]{1,0:T(8,128)(2,1)S(1)}, bf16[128,128]{1,0:T(8,128)(2,1)S(1)}, u32[]{:S(2)}, u32[]{:S(2)}) collective-permute-start(bf16[128,128]{1,0:T(8,128)(2,1)S(1)} %get-tuple-element.61), channel_id=1, source_target_pairs={{0,8},{1,2},{2,1},{3,11},{4,12},{5,6},{6,5},{7,15},{8,0},{9,10},{1... | collective-permute-start | bytes 98312 | tf_op jit(solution)/shard_map/ppermute | solution.py:256
  21.3 6.5 %collective-permute-start.9 = (f32[64,128]{1,0:T(8,128)S(1)}, f32[64,128]{1,0:T(8,128)S(1)}, u32[]{:S(2)}, u32[]{:S(2)}) collective-permute-start(f32[64,128]{1,0:T(8,128)S(1)} %get-tuple-element.71), channel_id=1, source_target_pairs={{0,3},{1,2},{2,1},{3,0},{4,7},{5,6},{6,5},{7,4},{8,11},{9,10},{10,... | collective-permute-start | bytes 98312 | tf_op jit(solution)/shard_map/ppermute | solution.py:215
  24.9 4.8 %collective-permute-start.10 = (f32[64,128]{1,0:T(8,128)S(1)}, f32[64,128]{1,0:T(8,128)S(1)}, u32[]{:S(2)}, u32[]{:S(2)}) collective-permute-start(f32[64,128]{1,0:T(8,128)S(1)} %get-tuple-element.72), channel_id=1, source_target_pairs={{0,2},{1,3},{2,0},{3,1},{4,6},{5,7},{6,4},{7,5},{8,10},{9,11},{10,... | collective-permute-start | bytes 98312 | tf_op jit(solution)/shard_map/ppermute | solution.py:215
  24.9 4.8 %collective-permute-start.11 = (f32[64,128]{1,0:T(8,128)S(1)}, f32[64,128]{1,0:T(8,128)S(1)}, u32[]{:S(2)}, u32[]{:S(2)}) collective-permute-start(f32[64,128]{1,0:T(8,128)S(1)} %get-tuple-element.73), channel_id=1, source_target_pairs={{0,1},{1,0},{2,3},{3,2},{4,5},{5,4},{6,7},{7,6},{8,9},{9,8},{10,11... | collective-permute-start | bytes 98312 | tf_op jit(solution)/shard_map/ppermute | solution.py:215
  25.7 4.0 %copy-start.4 = (s32[1,1,1,32]{3,2,1,0:T(1,128)S(1)}, s32[1,1,1,32]{3,2,1,0:T(1,128)}, u32[]{:S(2)}) copy-start(s32[1,1,1,32]{3,2,1,0:T(1,128)} %refs_6_.1) | copy-start | bytes 388
  33.2 8.6 %collective-permute-start.12 = (bf16[1024,128]{1,0:T(8,128)(2,1)S(1)}, bf16[1024,128]{1,0:T(8,128)(2,1)S(1)}, u32[]{:S(2)}, u32[]{:S(2)}) collective-permute-start(bf16[1024,128]{1,0:T(8,128)(2,1)S(1)} %get-tuple-element.77), channel_id=1, source_target_pairs={{0,4},{1,5},{2,6},{3,7},{4,0},{5,1},{6,2},{7,3},{8,12},{9,13},{10,... | collective-permute-start | bytes 786440 | tf_op jit(solution)/shard_map/ppermute | solution.py:256
  34.7 7.1 %collective-permute-start.13 = (bf16[1024,128]{1,0:T(8,128)(2,1)S(1)}, bf16[1024,128]{1,0:T(8,128)(2,1)S(1)}, u32[]{:S(2)}, u32[]{:S(2)}) collective-permute-start(bf16[1024,128]{1,0:T(8,128)(2,1)S(1)} %get-tuple-element.78), channel_id=1, source_target_pairs={{0,1},{1,0},{2,3},{3,2},{4,5},{5,4},{6,7},{7,6},{8,16},{9,17},{10,... | collective-permute-start | bytes 786440 | tf_op jit(solution)/shard_map/ppermute | solution.py:256
  34.7 7.1 %collective-permute-start.14 = (bf16[1024,128]{1,0:T(8,128)(2,1)S(1)}, bf16[1024,128]{1,0:T(8,128)(2,1)S(1)}, u32[]{:S(2)}, u32[]{:S(2)}) collective-permute-start(bf16[1024,128]{1,0:T(8,128)(2,1)S(1)} %get-tuple-element.79), channel_id=1, source_target_pairs={{0,8},{1,9},{2,10},{3,11},{4,12},{5,13},{6,14},{7,15},{8,0},{9,1},... | collective-permute-start | bytes 786440 | tf_op jit(solution)/shard_map/ppermute | solution.py:256
  35.7 6.1 %collective-permute-start.16 = (bf16[128,128]{1,0:T(8,128)(2,1)S(1)}, bf16[128,128]{1,0:T(8,128)(2,1)S(1)}, u32[]{:S(2)}, u32[]{:S(2)}) collective-permute-start(bf16[128,128]{1,0:T(8,128)(2,1)S(1)} %get-tuple-element.80), channel_id=1, source_target_pairs={{0,1},{1,0},{2,3},{3,2},{4,5},{5,4},{6,7},{7,6},{8,9},{9,8},{10,11... | collective-permute-start | bytes 98312 | tf_op jit(solution)/shard_map/ppermute | solution.py:256
  36.8 5.0 %collective-permute-start.15 = (bf16[128,128]{1,0:T(8,128)(2,1)S(1)}, bf16[128,128]{1,0:T(8,128)(2,1)S(1)}, u32[]{:S(2)}, u32[]{:S(2)}) collective-permute-start(bf16[128,128]{1,0:T(8,128)(2,1)S(1)} %get-tuple-element.80), channel_id=1, source_target_pairs={{0,8},{1,2},{2,1},{3,11},{4,12},{5,6},{6,5},{7,15},{8,0},{9,10},{1... | collective-permute-start | bytes 98312 | tf_op jit(solution)/shard_map/ppermute | solution.py:256
  44.9 7.4 %collective-permute-start.17 = (bf16[1024,128]{1,0:T(8,128)(2,1)S(1)}, bf16[1024,128]{1,0:T(8,128)(2,1)S(1)}, u32[]{:S(2)}, u32[]{:S(2)}) collective-permute-start(bf16[1024,128]{1,0:T(8,128)(2,1)S(1)} %get-tuple-element.83), channel_id=1, source_target_pairs={{0,4},{1,5},{2,6},{3,7},{4,0},{5,1},{6,2},{7,3},{8,12},{9,13},{10,... | collective-permute-start | bytes 786440 | tf_op jit(solution)/shard_map/ppermute | solution.py:256
  45.4 6.9 %collective-permute-start.18 = (bf16[1024,128]{1,0:T(8,128)(2,1)S(1)}, bf16[1024,128]{1,0:T(8,128)(2,1)S(1)}, u32[]{:S(2)}, u32[]{:S(2)}) collective-permute-start(bf16[1024,128]{1,0:T(8,128)(2,1)S(1)} %get-tuple-element.84), channel_id=1, source_target_pairs={{0,1},{1,0},{2,3},{3,2},{4,5},{5,4},{6,7},{7,6},{8,16},{9,17},{10,... | collective-permute-start | bytes 786440 | tf_op jit(solution)/shard_map/ppermute | solution.py:256
  45.4 6.9 %collective-permute-start.19 = (bf16[1024,128]{1,0:T(8,128)(2,1)S(1)}, bf16[1024,128]{1,0:T(8,128)(2,1)S(1)}, u32[]{:S(2)}, u32[]{:S(2)}) collective-permute-start(bf16[1024,128]{1,0:T(8,128)(2,1)S(1)} %get-tuple-element.85), channel_id=1, source_target_pairs={{0,8},{1,9},{2,10},{3,11},{4,12},{5,13},{6,14},{7,15},{8,0},{9,1},... | collective-permute-start | bytes 786440 | tf_op jit(solution)/shard_map/ppermute | solution.py:256
  45.4 6.9 %collective-permute-start.21 = (bf16[128,128]{1,0:T(8,128)(2,1)S(1)}, bf16[128,128]{1,0:T(8,128)(2,1)S(1)}, u32[]{:S(2)}, u32[]{:S(2)}) collective-permute-start(bf16[128,128]{1,0:T(8,128)(2,1)S(1)} %get-tuple-element.86), channel_id=1, source_target_pairs={{0,1},{1,0},{2,3},{3,2},{4,5},{5,4},{6,7},{7,6},{8,9},{9,8},{10,11... | collective-permute-start | bytes 98312 | tf_op jit(solution)/shard_map/ppermute | solution.py:256
  47.4 4.9 %collective-permute-start.20 = (bf16[128,128]{1,0:T(8,128)(2,1)S(1)}, bf16[128,128]{1,0:T(8,128)(2,1)S(1)}, u32[]{:S(2)}, u32[]{:S(2)}) collective-permute-start(bf16[128,128]{1,0:T(8,128)(2,1)S(1)} %get-tuple-element.86), channel_id=1, source_target_pairs={{0,8},{1,2},{2,1},{3,11},{4,12},{5,6},{6,5},{7,15},{8,0},{9,10},{1... | collective-permute-start | bytes 98312 | tf_op jit(solution)/shard_map/ppermute | solution.py:256

commit v18 on v17

--- a/solution.py
+++ b/solution.py
@@ -239,7 +239,6 @@
     axes = ("row", "col", "gz")
     sizes = [lax.axis_size(name) for name in axes]
     along = axes.index(axis)
-    spare = 0 if axis == "gz" else 2
     pairs = []
     for r in range(sizes[0]):
         for c in range(sizes[1]):
@@ -249,8 +248,8 @@
                 there[along] += 1 if here[along] % 2 == turn else -1
                 if not 0 <= there[along] < sizes[along]:
                     there[along] = here[along]
-                    if here[spare] ^ 1 < sizes[spare]:
-                        there[spare] ^= 1
+                    if axis != "row" and r ^ 1 < sizes[0]:
+                        there[0] ^= 1
                 flat = [(at[0] * sizes[1] + at[1]) * sizes[2] + at[2] for at in (here, there)]
                 pairs.append(tuple(flat))
     return lax.ppermute(value, axes, pairs)

time: 55 us -> 57 us (1.036)
  starting transfers between devices: 20.5 us -> 25.3 us
  waiting for transfers between devices: 10.9 us -> 8.42 us
    ppermute x15, starting transfers between devices: 11.5 us -> 16.2 us  [swap(): return lax.ppermute(value, axes, pairs)]
    ppermute x15, waiting for transfers between devices: 6.53 us -> 3.94 us  [swap(): return lax.ppermute(value, axes, pairs)]
  transfers between devices with their start and end apart: 22 -> 22, of which waited for: 7 -> 6; matrix products, arithmetic and copies ran while one was open for 0% -> 0% of each run, Pallas kernels for 18% -> 17%
where the time goes in v18:
time: 57 us; the launch traced here: 56.8 us
  starting transfers between devices  25.3 us (44%)
  Pallas kernels  21.4 us (38%)
  waiting for transfers between devices  8.42 us (15%)
  between operations  0.96 us (2%)
  local copies, waits for them, and re-layouts  0.71 us (1%)
    ppermute x15, starting transfers between devices, swap(): return lax.ppermute(value, axes, pairs)  16.2 us
    pallas_call x3, Pallas kernels, sweep_finish(): pl.pallas_call(functools.partial(finish_kernel, shape, len(ends), len(rec...  8.62 us
    pallas_call x3, Pallas kernels, sweep_base(): pl.pallas_call(functools.partial(base_kernel, shape, len(ends), phi is no...  5.53 us
    ppermute x3, starting transfers between devices, flux_sums(): lax.ppermute(sent[key], 'gz', [(i, i ^ key) for i in range(gzs)])  4.45 us
    ppermute x15, waiting for transfers between devices, swap(): return lax.ppermute(value, axes, pairs)  3.94 us
    pallas_call x1, Pallas kernels, first_faces(): pl.pallas_call(functools.partial(faces_kernel, shape, slots), in_specs=[h...  3.45 us
    pallas_call x1, Pallas kernels, traces(): pl.pallas_call(functools.partial(trace_kernel, shape, stride, block), in_...  3.03 us
    ppermute x3, starting transfers between devices, row_gather(): lax.ppermute(held[key], 'row', pairs)  3.01 us
  transfers between devices with their start and end apart: 22, of which 6 were waited for; matrix products, arithmetic and copies ran while one was open for 0% of the time, Pallas kernels for 17%

profile of v18, /device:TPU:0, one launch (start us, length us, event | category | flops | bytes accessed | tf_op | source)
XLA Modules:
  0.0 56.8 jit_solution(17970893573982600027)
XLA Ops:
  0.6 0.7 %copy-done.3 = s32[1,1,1,1024]{3,2,1,0:T(1,128)S(1)} copy-done((s32[1,1,1,1024]{3,2,1,0:T(1,128)S(1)}, s32[1,1,1,1024]{3,2,1,0:T(1,128)}, u32[]{:S(2)}) %copy-start.3) | copy-done | bytes 4120
  1.3 3.0 %shard_map.78 = (bf16[1024,128]{1,0:T(8,128)(2,1)S(1)}, bf16[1024,128]{1,0:T(8,128)(2,1)S(1)}) custom-call(bf16[128,64,128]{2,1,0:T(8,128)(2,1)} %bitcast.5, s32[1,1,1,1024]{3,2,1,0:T(1,128)S(1)} %copy-done.3), custom_call_target="tpu_custom_call" | custom-call | flops 536870912 | bytes 2097152 | tf_op jit(solution)/shard_map/pallas_call | solution.py:106
  4.4 3.0 %collective-permute-start.1 = (bf16[1024,128]{1,0:T(8,128)(2,1)S(1)}, bf16[1024,128]{1,0:T(8,128)(2,1)S(1)}, u32[]{:S(2)}, u32[]{:S(2)}) collective-permute-start(bf16[1024,128]{1,0:T(8,128)(2,1)S(1)} %get-tuple-element.53.refs_0_), channel_id=1, source_target_pairs={{0,16},{8,24},{16,0},{24,8},{1,17},{9,25},{17,1},{25,9},{2,18},{10... | collective-permute-start | bytes 786440 | tf_op jit(solution)/shard_map/ppermute | solution.py:689
  7.4 1.5 %collective-permute-start.3 = (bf16[1024,128]{1,0:T(8,128)(2,1)S(1)}, bf16[1024,128]{1,0:T(8,128)(2,1)S(1)}, u32[]{:S(2)}, u32[]{:S(2)}) collective-permute-start(bf16[1024,128]{1,0:T(8,128)(2,1)S(1)} %get-tuple-element.52), channel_id=1, source_target_pairs={{0,4},{1,5},{2,6},{3,7},{4,0},{5,1},{6,2},{7,3},{8,12},{9,13},{10,... | collective-permute-start | bytes 786440 | tf_op jit(solution)/shard_map/ppermute | solution.py:255
  8.9 3.5 %shard_map.77 = (bf16[1024,128]{1,0:T(8,128)(2,1)S(1)}, bf16[1024,128]{1,0:T(8,128)(2,1)S(1)}, bf16[128,128]{1,0:T(8,128)(2,1)S(1)}, bf16[4,256,1024]{2,1,0:T(8,...) custom-call(bf16[8192,128]{1,0:T(8,128)(2,1)} %bitcast.6, ...), custom_call_target="tpu_custom_call" | custom-call | flops 134217728 | bytes 4194304 | tf_op jit(solution)/shard_map/pallas_call | solution.py:418
  12.4 1.3 %collective-permute-done.1.refs_2_ = bf16[1024,128]{1,0:T(8,128)(2,1)S(1)} collective-permute-done((bf16[1024,128]{1,0:T(8,128)(2,1)S(1)}, bf16[1024,128]{1,0:T(8,128)(2,1)S(1)}, u32[]{:S(2)}, u32[]{:S(2)}) %collective-permute-start.1) | collective-permute-done | bytes 262176 | tf_op jit(solution)/shard_map/ppermute | solution.py:689
  13.7 0.7 %collective-permute-start.6 = (bf16[1024,128]{1,0:T(8,128)(2,1)S(1)}, bf16[1024,128]{1,0:T(8,128)(2,1)S(1)}, u32[]{:S(2)}, u32[]{:S(2)}) collective-permute-start(bf16[1024,128]{1,0:T(8,128)(2,1)S(1)} %get-tuple-element.65), channel_id=1, source_target_pairs={{0,0},{1,1},{2,2},{3,3},{4,4},{5,5},{6,6},{7,7},{8,16},{9,17},{10,... | collective-permute-start | bytes 786440 | tf_op jit(solution)/shard_map/ppermute | solution.py:255
  14.4 3.2 %collective-permute-start.7 = (bf16[1024,128]{1,0:T(8,128)(2,1)S(1)}, bf16[1024,128]{1,0:T(8,128)(2,1)S(1)}, u32[]{:S(2)}, u32[]{:S(2)}) collective-permute-start(bf16[1024,128]{1,0:T(8,128)(2,1)S(1)} %get-tuple-element.66), channel_id=1, source_target_pairs={{0,8},{1,9},{2,10},{3,11},{4,12},{5,13},{6,14},{7,15},{8,0},{9,1},... | collective-permute-start | bytes 786440 | tf_op jit(solution)/shard_map/ppermute | solution.py:255
  17.5 0.7 %shard_map.79 = (f32[128,128]{1,0:T(8,128)S(1)}, f32[128,128]{1,0:T(8,128)S(1)}) custom-call(bf16[1024,128]{1,0:T(8,128)(2,1)S(1)} %get-tuple-element.53.refs_0_, bf16[1024,128]{1,0:T(8,128)(2,1)S(1)} %collective-permute-done.refs_1_, bf16[1024,128]{1,0:T(8,128)(2,1)S(1)} %collective-permute-done.1.refs_2_, ...), custom_call_target="tpu_custom_call" | custom-call | flops 268435456 | bytes 2097152 | tf_op jit(solution)/shard_map/pallas_call | solution.py:160
  18.2 1.6 %collective-permute-start.8 = (f32[128,128]{1,0:T(8,128)S(1)}, f32[128,128]{1,0:T(8,128)S(1)}, u32[]{:S(2)}, u32[]{:S(2)}) collective-permute-start(f32[128,128]{1,0:T(8,128)S(1)} %get-tuple-element.68), channel_id=1, source_target_pairs={{0,4},{4,0},{1,5},{5,1},{2,6},{6,2},{3,7},{7,3},{8,12},{12,8},{9,1... | collective-permute-start | bytes 196616 | tf_op jit(solution)/shard_map/ppermute | solution.py:210
  19.8 1.6 %collective-permute-start.5 = (bf16[128,128]{1,0:T(8,128)(2,1)S(1)}, bf16[128,128]{1,0:T(8,128)(2,1)S(1)}, u32[]{:S(2)}, u32[]{:S(2)}) collective-permute-start(bf16[128,128]{1,0:T(8,128)(2,1)S(1)} %get-tuple-element.61), channel_id=1, source_target_pairs={{0,1},{1,0},{2,3},{3,2},{4,5},{5,4},{6,7},{7,6},{8,9},{9,8},{10,11... | collective-permute-start | bytes 98312 | tf_op jit(solution)/shard_map/ppermute | solution.py:255
  21.4 1.2 %collective-permute-done.8.other_ref = f32[128,128]{1,0:T(8,128)S(1)} collective-permute-done((f32[128,128]{1,0:T(8,128)S(1)}, f32[128,128]{1,0:T(8,128)S(1)}, u32[]{:S(2)}, u32[]{:S(2)}) %collective-permute-start.8) | collective-permute-done | bytes 65568 | tf_op jit(solution)/shard_map/ppermute | solution.py:210
  22.7 3.7 %collective-permute-start.9 = (f32[64,128]{1,0:T(8,128)S(1)}, f32[64,128]{1,0:T(8,128)S(1)}, u32[]{:S(2)}, u32[]{:S(2)}) collective-permute-start(f32[64,128]{1,0:T(8,128)S(1)} %get-tuple-element.71), channel_id=1, source_target_pairs={{0,3},{1,2},{2,1},{3,0},{4,7},{5,6},{6,5},{7,4},{8,11},{9,10},{10,... | collective-permute-start | bytes 98312 | tf_op jit(solution)/shard_map/ppermute | solution.py:215
  26.4 0.8 %collective-permute-start.11 = (f32[64,128]{1,0:T(8,128)S(1)}, f32[64,128]{1,0:T(8,128)S(1)}, u32[]{:S(2)}, u32[]{:S(2)}) collective-permute-start(f32[64,128]{1,0:T(8,128)S(1)} %get-tuple-element.73), channel_id=1, source_target_pairs={{0,1},{1,0},{2,3},{3,2},{4,5},{5,4},{6,7},{7,6},{8,9},{9,8},{10,11... | collective-permute-start | bytes 98312 | tf_op jit(solution)/shard_map/ppermute | solution.py:215
  27.2 2.0 %shard_map.80.refs_0_ = f32[8192,128]{1,0:T(8,128)S(1)} custom-call(bf16[8192,128]{1,0:T(8,128)(2,1)S(1)} %bitcast.7, bf16[8192,128]{1,0:T(8,128)(2,1)S(1)} %bitcast.8, f32[128,128]{1,0:T(8,128)S(1)} %get-tuple-element.45.refs_2_.refs_1_, bf16[128,176]{1,0:T(8,128)(2,1)S(1)} %get-tuple-element.46.refs_3_.refs_2_, ...), custom_call_target="tpu_custom_call" | custom-call | flops 805306368 | bytes 8388608 | tf_op jit(solution)/shard_map/pallas_call | solution.py:525
  29.2 2.0 %collective-permute-done.10.refs_12_ = f32[64,128]{1,0:T(8,128)S(1)} collective-permute-done((f32[64,128]{1,0:T(8,128)S(1)}, f32[64,128]{1,0:T(8,128)S(1)}, u32[]{:S(2)}, u32[]{:S(2)}) %collective-permute-start.10) | collective-permute-done | bytes 32800 | tf_op jit(solution)/shard_map/ppermute | solution.py:215
  31.2 3.5 %shard_map.82 = (bf16[8192,128]{1,0:T(8,128)(2,1)S(1)}, bf16[1024,128]{1,0:T(8,128)(2,1)S(1)}, bf16[1024,128]{1,0:T(8,128)(2,1)S(1)}, bf16[1024,128]{1,0:T(8,128...) custom-call(f32[8192,128]{1,0:T(8,128)S(1)} %shard_map.80.refs_0_, ...), custom_call_target="tpu_custom_call" | custom-call | flops 536870912 | bytes 8388608 | tf_op jit(solution)/shard_map/pallas_call | solution.py:662
  34.6 1.5 %collective-permute-start.12 = (bf16[1024,128]{1,0:T(8,128)(2,1)S(1)}, bf16[1024,128]{1,0:T(8,128)(2,1)S(1)}, u32[]{:S(2)}, u32[]{:S(2)}) collective-permute-start(bf16[1024,128]{1,0:T(8,128)(2,1)S(1)} %get-tuple-element.77), channel_id=1, source_target_pairs={{0,4},{1,5},{2,6},{3,7},{4,0},{5,1},{6,2},{7,3},{8,12},{9,13},{10,... | collective-permute-start | bytes 786440 | tf_op jit(solution)/shard_map/ppermute | solution.py:255
  36.2 0.8 %collective-permute-start.13 = (bf16[1024,128]{1,0:T(8,128)(2,1)S(1)}, bf16[1024,128]{1,0:T(8,128)(2,1)S(1)}, u32[]{:S(2)}, u32[]{:S(2)}) collective-permute-start(bf16[1024,128]{1,0:T(8,128)(2,1)S(1)} %get-tuple-element.78), channel_id=1, source_target_pairs={{0,0},{1,1},{2,2},{3,3},{4,4},{5,5},{6,6},{7,7},{8,16},{9,17},{10,... | collective-permute-start | bytes 786440 | tf_op jit(solution)/shard_map/ppermute | solution.py:255
  37.0 2.2 %collective-permute-start.14 = (bf16[1024,128]{1,0:T(8,128)(2,1)S(1)}, bf16[1024,128]{1,0:T(8,128)(2,1)S(1)}, u32[]{:S(2)}, u32[]{:S(2)}) collective-permute-start(bf16[1024,128]{1,0:T(8,128)(2,1)S(1)} %get-tuple-element.79), channel_id=1, source_target_pairs={{0,8},{1,9},{2,10},{3,11},{4,12},{5,13},{6,14},{7,15},{8,0},{9,1},... | collective-permute-start | bytes 786440 | tf_op jit(solution)/shard_map/ppermute | solution.py:255
  39.2 0.2 collective-permute-start.15
  39.4 2.0 %shard_map.83 = (f32[8192,128]{1,0:T(8,128)S(1)}, bf16[8192,128]{1,0:T(8,128)(2,1)S(1)}) custom-call(bf16[8192,128]{1,0:T(8,128)(2,1)S(1)} %get-tuple-element.74.refs_0_, bf16[8192,128]{1,0:T(8,128)(2,1)S(1)} %bitcast.9, f32[128,128]{1,0:T(8,128)S(1)} %get-tuple-element.45.refs_2_.refs_1_, bf16[128,176]{1,0:T(8,128)(2,1)S(1)} %get-tuple-element.46.refs_3_.refs_2_, ...), custom_call_target="tpu_custom_call" | custom-call | flops 805306368 | bytes 8388608 | tf_op jit(solution)/shard_map/pallas_call | solution.py:525
  41.4 1.7 %collective-permute-done.16.refs_10_ = bf16[128,128]{1,0:T(8,128)(2,1)S(1)} collective-permute-done((bf16[128,128]{1,0:T(8,128)(2,1)S(1)}, bf16[128,128]{1,0:T(8,128)(2,1)S(1)}, u32[]{:S(2)}, u32[]{:S(2)}) %collective-permute-start.16) | collective-permute-done | bytes 32800 | tf_op jit(solution)/shard_map/ppermute | solution.py:255
  43.2 2.8 %shard_map.84 = (bf16[8192,128]{1,0:T(8,128)(2,1)S(1)}, bf16[1024,128]{1,0:T(8,128)(2,1)S(1)}, bf16[1024,128]{1,0:T(8,128)(2,1)S(1)}, bf16[1024,128]{1,0:T(8,128)(2,1)S(1)}, bf16[128,128]{1,0:T(8,128)(2,1)S(1)}) custom-call(f32[8192,128]{1,0:T(8,128)S(1)} %get-tuple-element.76.refs_0_, f32[128,128]{1,0:T(8,128)S(1)} %get-tuple-element.45.refs_2_.refs_1_, ...), custom_call_target="tpu_custom_call" | custom-call | flops 536870912 | bytes 8388608 | tf_op jit(solution)/shard_map/pallas_call | solution.py:662
  46.0 0.5 collective-permute-start.17
  46.5 0.7 %collective-permute-start.18 = (bf16[1024,128]{1,0:T(8,128)(2,1)S(1)}, bf16[1024,128]{1,0:T(8,128)(2,1)S(1)}, u32[]{:S(2)}, u32[]{:S(2)}) collective-permute-start(bf16[1024,128]{1,0:T(8,128)(2,1)S(1)} %get-tuple-element.84), channel_id=1, source_target_pairs={{0,0},{1,1},{2,2},{3,3},{4,4},{5,5},{6,6},{7,7},{8,16},{9,17},{10,... | collective-permute-start | bytes 786440 | tf_op jit(solution)/shard_map/ppermute | solution.py:255
  47.2 2.9 %collective-permute-start.19 = (bf16[1024,128]{1,0:T(8,128)(2,1)S(1)}, bf16[1024,128]{1,0:T(8,128)(2,1)S(1)}, u32[]{:S(2)}, u32[]{:S(2)}) collective-permute-start(bf16[1024,128]{1,0:T(8,128)(2,1)S(1)} %get-tuple-element.85), channel_id=1, source_target_pairs={{0,8},{1,9},{2,10},{3,11},{4,12},{5,13},{6,14},{7,15},{8,0},{9,1},... | collective-permute-start | bytes 786440 | tf_op jit(solution)/shard_map/ppermute | solution.py:255
  50.1 0.5 collective-permute-start.21
  50.6 1.5 %shard_map.85.refs_0_ = f32[8192,128]{1,0:T(8,128)S(1)} custom-call(bf16[8192,128]{1,0:T(8,128)(2,1)S(1)} %get-tuple-element.81.refs_0_, bf16[8192,128]{1,0:T(8,128)(2,1)S(1)} %get-tuple-element.82.refs_1_, f32[128,128]{1,0:T(8,128)S(1)} %get-tuple-element.45.refs_2_.refs_1_, bf16[128,176]{1,0:T(8,128)(2,1)S(1)} %get-tuple-element.46.refs_3_.refs_2_, ...), custom_call_target="tpu_custom_call" | custom-call | flops 805306368 | bytes 8388608 | tf_op jit(solution)/shard_map/pallas_call | solution.py:525
  52.1 1.9 %collective-permute-done.21.refs_10_ = bf16[128,128]{1,0:T(8,128)(2,1)S(1)} collective-permute-done((bf16[128,128]{1,0:T(8,128)(2,1)S(1)}, bf16[128,128]{1,0:T(8,128)(2,1)S(1)}, u32[]{:S(2)}, u32[]{:S(2)}) %collective-permute-start.21) | collective-permute-done | bytes 32800 | tf_op jit(solution)/shard_map/ppermute | solution.py:255
  54.0 0.3 collective-permute-done.17.refs_6_
  54.3 2.3 %shard_map.86 = bf16[8192,128]{1,0:T(8,128)(2,1)} custom-call(f32[8192,128]{1,0:T(8,128)S(1)} %shard_map.85.refs_0_, f32[128,128]{1,0:T(8,128)S(1)} %get-tuple-element.45.refs_2_.refs_1_, bf16[128,176]{1,0:T(8,128)(2,1)S(1)} %get-tuple-element.46.refs_3_.refs_2_, bf16[512,256]{1,0:T(8,128)(2,1)S(1)} %get-tuple-element.47.refs_4_.refs_3_, ...), custom_call_target="tpu_custom_call" | custom-call | flops 536870912 | bytes 8388608 | tf_op jit(solution)/shard_map/pallas_call | solution.py:662
  (32 shorter events, 0.2 us)
Async XLA Ops:
  0.6 8.3 %copy-start.2 = (f32[8,8,128]{2,1,0:T(8,128)S(1)}, f32[8,8,128]{2,1,0:T(8,128)}, u32[]{:S(2)}) copy-start(f32[8,8,128]{2,1,0:T(8,128)} %param.8) | copy-start | bytes 98308
  0.6 0.7 %copy-start.3 = (s32[1,1,1,1024]{3,2,1,0:T(1,128)S(1)}, s32[1,1,1,1024]{3,2,1,0:T(1,128)}, u32[]{:S(2)}) copy-start(s32[1,1,1,1024]{3,2,1,0:T(1,128)} %cell_ref.1) | copy-start | bytes 12292
  4.4 9.3 %collective-permute-start.1 = (bf16[1024,128]{1,0:T(8,128)(2,1)S(1)}, bf16[1024,128]{1,0:T(8,128)(2,1)S(1)}, u32[]{:S(2)}, u32[]{:S(2)}) collective-permute-start(bf16[1024,128]{1,0:T(8,128)(2,1)S(1)} %get-tuple-element.53.refs_0_), channel_id=1, source_target_pairs={{0,16},{8,24},{16,0},{24,8},{1,17},{9,25},{17,1},{25,9},{2,18},{10... | collective-permute-start | bytes 786440 | tf_op jit(solution)/shard_map/ppermute | solution.py:689
  7.4 10.1 %collective-permute-start = (bf16[1024,128]{1,0:T(8,128)(2,1)S(1)}, bf16[1024,128]{1,0:T(8,128)(2,1)S(1)}, u32[]{:S(2)}, u32[]{:S(2)}) collective-permute-start(bf16[1024,128]{1,0:T(8,128)(2,1)S(1)} %get-tuple-element.53.refs_0_), channel_id=1, source_target_pairs={{0,8},{8,0},{16,24},{24,16},{1,9},{9,1},{17,25},{25,17},{2,10},{10... | collective-permute-start | bytes 786440 | tf_op jit(solution)/shard_map/ppermute | solution.py:689
  7.4 10.1 %collective-permute-start.3 = (bf16[1024,128]{1,0:T(8,128)(2,1)S(1)}, bf16[1024,128]{1,0:T(8,128)(2,1)S(1)}, u32[]{:S(2)}, u32[]{:S(2)}) collective-permute-start(bf16[1024,128]{1,0:T(8,128)(2,1)S(1)} %get-tuple-element.52), channel_id=1, source_target_pairs={{0,4},{1,5},{2,6},{3,7},{4,0},{5,1},{6,2},{7,3},{8,12},{9,13},{10,... | collective-permute-start | bytes 786440 | tf_op jit(solution)/shard_map/ppermute | solution.py:255
  8.9 18.2 %copy-start.1 = (bf16[128,8,8,128]{3,2,1,0:T(8,128)(2,1)S(1)}, bf16[128,8,8,128]{3,2,1,0:T(8,128)(2,1)}, u32[]{:S(2)}) copy-start(bf16[128,8,8,128]{3,2,1,0:T(8,128)(2,1)} %param.7) | copy-start | bytes 6291460
  12.4 14.8 %copy-start = (bf16[128,8,8,128]{3,2,1,0:T(8,128)(2,1)S(1)}, bf16[128,8,8,128]{3,2,1,0:T(8,128)(2,1)}, u32[]{:S(2)}) copy-start(bf16[128,8,8,128]{3,2,1,0:T(8,128)(2,1)} %param.6) | copy-start | bytes 6291460
  13.7 3.8 %collective-permute-start.2 = (bf16[1024,128]{1,0:T(8,128)(2,1)S(1)}, bf16[1024,128]{1,0:T(8,128)(2,1)S(1)}, u32[]{:S(2)}, u32[]{:S(2)}) collective-permute-start(bf16[1024,128]{1,0:T(8,128)(2,1)S(1)} %collective-permute-done.1.refs_2_), channel_id=1, source_target_pairs={{0,8},{8,0},{16,24},{24,16},{1,9},{9,1},{17,25},{25,17},{2,10},{10... | collective-permute-start | bytes 786440 | tf_op jit(solution)/shard_map/ppermute | solution.py:689
  13.7 7.7 %collective-permute-start.6 = (bf16[1024,128]{1,0:T(8,128)(2,1)S(1)}, bf16[1024,128]{1,0:T(8,128)(2,1)S(1)}, u32[]{:S(2)}, u32[]{:S(2)}) collective-permute-start(bf16[1024,128]{1,0:T(8,128)(2,1)S(1)} %get-tuple-element.65), channel_id=1, source_target_pairs={{0,0},{1,1},{2,2},{3,3},{4,4},{5,5},{6,6},{7,7},{8,16},{9,17},{10,... | collective-permute-start | bytes 786440 | tf_op jit(solution)/shard_map/ppermute | solution.py:255
  14.4 7.1 %collective-permute-start.7 = (bf16[1024,128]{1,0:T(8,128)(2,1)S(1)}, bf16[1024,128]{1,0:T(8,128)(2,1)S(1)}, u32[]{:S(2)}, u32[]{:S(2)}) collective-permute-start(bf16[1024,128]{1,0:T(8,128)(2,1)S(1)} %get-tuple-element.66), channel_id=1, source_target_pairs={{0,8},{1,9},{2,10},{3,11},{4,12},{5,13},{6,14},{7,15},{8,0},{9,1},... | collective-permute-start | bytes 786440 | tf_op jit(solution)/shard_map/ppermute | solution.py:255
  18.2 4.3 %collective-permute-start.8 = (f32[128,128]{1,0:T(8,128)S(1)}, f32[128,128]{1,0:T(8,128)S(1)}, u32[]{:S(2)}, u32[]{:S(2)}) collective-permute-start(f32[128,128]{1,0:T(8,128)S(1)} %get-tuple-element.68), channel_id=1, source_target_pairs={{0,4},{4,0},{1,5},{5,1},{2,6},{6,2},{3,7},{7,3},{8,12},{12,8},{9,1... | collective-permute-start | bytes 196616 | tf_op jit(solution)/shard_map/ppermute | solution.py:210
  19.8 7.3 %collective-permute-start.5 = (bf16[128,128]{1,0:T(8,128)(2,1)S(1)}, bf16[128,128]{1,0:T(8,128)(2,1)S(1)}, u32[]{:S(2)}, u32[]{:S(2)}) collective-permute-start(bf16[128,128]{1,0:T(8,128)(2,1)S(1)} %get-tuple-element.61), channel_id=1, source_target_pairs={{0,1},{1,0},{2,3},{3,2},{4,5},{5,4},{6,7},{7,6},{8,9},{9,8},{10,11... | collective-permute-start | bytes 98312 | tf_op jit(solution)/shard_map/ppermute | solution.py:255
  21.4 5.7 %collective-permute-start.4 = (bf16[128,128]{1,0:T(8,128)(2,1)S(1)}, bf16[128,128]{1,0:T(8,128)(2,1)S(1)}, u32[]{:S(2)}, u32[]{:S(2)}) collective-permute-start(bf16[128,128]{1,0:T(8,128)(2,1)S(1)} %get-tuple-element.61), channel_id=1, source_target_pairs={{0,8},{1,2},{2,1},{3,11},{4,12},{5,6},{6,5},{7,15},{8,0},{9,10},{1... | collective-permute-start | bytes 98312 | tf_op jit(solution)/shard_map/ppermute | solution.py:255
  22.7 6.5 %collective-permute-start.9 = (f32[64,128]{1,0:T(8,128)S(1)}, f32[64,128]{1,0:T(8,128)S(1)}, u32[]{:S(2)}, u32[]{:S(2)}) collective-permute-start(f32[64,128]{1,0:T(8,128)S(1)} %get-tuple-element.71), channel_id=1, source_target_pairs={{0,3},{1,2},{2,1},{3,0},{4,7},{5,6},{6,5},{7,4},{8,11},{9,10},{10,... | collective-permute-start | bytes 98312 | tf_op jit(solution)/shard_map/ppermute | solution.py:215
  26.4 4.8 %collective-permute-start.10 = (f32[64,128]{1,0:T(8,128)S(1)}, f32[64,128]{1,0:T(8,128)S(1)}, u32[]{:S(2)}, u32[]{:S(2)}) collective-permute-start(f32[64,128]{1,0:T(8,128)S(1)} %get-tuple-element.72), channel_id=1, source_target_pairs={{0,2},{1,3},{2,0},{3,1},{4,6},{5,7},{6,4},{7,5},{8,10},{9,11},{10,... | collective-permute-start | bytes 98312 | tf_op jit(solution)/shard_map/ppermute | solution.py:215
  26.4 4.8 %collective-permute-start.11 = (f32[64,128]{1,0:T(8,128)S(1)}, f32[64,128]{1,0:T(8,128)S(1)}, u32[]{:S(2)}, u32[]{:S(2)}) collective-permute-start(f32[64,128]{1,0:T(8,128)S(1)} %get-tuple-element.73), channel_id=1, source_target_pairs={{0,1},{1,0},{2,3},{3,2},{4,5},{5,4},{6,7},{7,6},{8,9},{9,8},{10,11... | collective-permute-start | bytes 98312 | tf_op jit(solution)/shard_map/ppermute | solution.py:215
  27.2 4.0 %copy-start.4 = (s32[1,1,1,32]{3,2,1,0:T(1,128)S(1)}, s32[1,1,1,32]{3,2,1,0:T(1,128)}, u32[]{:S(2)}) copy-start(s32[1,1,1,32]{3,2,1,0:T(1,128)} %refs_6_.1) | copy-start | bytes 388
  34.6 8.5 %collective-permute-start.12 = (bf16[1024,128]{1,0:T(8,128)(2,1)S(1)}, bf16[1024,128]{1,0:T(8,128)(2,1)S(1)}, u32[]{:S(2)}, u32[]{:S(2)}) collective-permute-start(bf16[1024,128]{1,0:T(8,128)(2,1)S(1)} %get-tuple-element.77), channel_id=1, source_target_pairs={{0,4},{1,5},{2,6},{3,7},{4,0},{5,1},{6,2},{7,3},{8,12},{9,13},{10,... | collective-permute-start | bytes 786440 | tf_op jit(solution)/shard_map/ppermute | solution.py:255
  36.2 7.0 %collective-permute-start.13 = (bf16[1024,128]{1,0:T(8,128)(2,1)S(1)}, bf16[1024,128]{1,0:T(8,128)(2,1)S(1)}, u32[]{:S(2)}, u32[]{:S(2)}) collective-permute-start(bf16[1024,128]{1,0:T(8,128)(2,1)S(1)} %get-tuple-element.78), channel_id=1, source_target_pairs={{0,0},{1,1},{2,2},{3,3},{4,4},{5,5},{6,6},{7,7},{8,16},{9,17},{10,... | collective-permute-start | bytes 786440 | tf_op jit(solution)/shard_map/ppermute | solution.py:255
  37.0 6.1 %collective-permute-start.14 = (bf16[1024,128]{1,0:T(8,128)(2,1)S(1)}, bf16[1024,128]{1,0:T(8,128)(2,1)S(1)}, u32[]{:S(2)}, u32[]{:S(2)}) collective-permute-start(bf16[1024,128]{1,0:T(8,128)(2,1)S(1)} %get-tuple-element.79), channel_id=1, source_target_pairs={{0,8},{1,9},{2,10},{3,11},{4,12},{5,13},{6,14},{7,15},{8,0},{9,1},... | collective-permute-start | bytes 786440 | tf_op jit(solution)/shard_map/ppermute | solution.py:255
  39.2 3.9 %collective-permute-start.16 = (bf16[128,128]{1,0:T(8,128)(2,1)S(1)}, bf16[128,128]{1,0:T(8,128)(2,1)S(1)}, u32[]{:S(2)}, u32[]{:S(2)}) collective-permute-start(bf16[128,128]{1,0:T(8,128)(2,1)S(1)} %get-tuple-element.80), channel_id=1, source_target_pairs={{0,1},{1,0},{2,3},{3,2},{4,5},{5,4},{6,7},{7,6},{8,9},{9,8},{10,11... | collective-permute-start | bytes 98312 | tf_op jit(solution)/shard_map/ppermute | solution.py:255
  39.2 3.9 %collective-permute-start.15 = (bf16[128,128]{1,0:T(8,128)(2,1)S(1)}, bf16[128,128]{1,0:T(8,128)(2,1)S(1)}, u32[]{:S(2)}, u32[]{:S(2)}) collective-permute-start(bf16[128,128]{1,0:T(8,128)(2,1)S(1)} %get-tuple-element.80), channel_id=1, source_target_pairs={{0,8},{1,2},{2,1},{3,11},{4,12},{5,6},{6,5},{7,15},{8,0},{9,10},{1... | collective-permute-start | bytes 98312 | tf_op jit(solution)/shard_map/ppermute | solution.py:255
  46.0 8.3 %collective-permute-start.17 = (bf16[1024,128]{1,0:T(8,128)(2,1)S(1)}, bf16[1024,128]{1,0:T(8,128)(2,1)S(1)}, u32[]{:S(2)}, u32[]{:S(2)}) collective-permute-start(bf16[1024,128]{1,0:T(8,128)(2,1)S(1)} %get-tuple-element.83), channel_id=1, source_target_pairs={{0,4},{1,5},{2,6},{3,7},{4,0},{5,1},{6,2},{7,3},{8,12},{9,13},{10,... | collective-permute-start | bytes 786440 | tf_op jit(solution)/shard_map/ppermute | solution.py:255
  46.5 7.8 %collective-permute-start.18 = (bf16[1024,128]{1,0:T(8,128)(2,1)S(1)}, bf16[1024,128]{1,0:T(8,128)(2,1)S(1)}, u32[]{:S(2)}, u32[]{:S(2)}) collective-permute-start(bf16[1024,128]{1,0:T(8,128)(2,1)S(1)} %get-tuple-element.84), channel_id=1, source_target_pairs={{0,0},{1,1},{2,2},{3,3},{4,4},{5,5},{6,6},{7,7},{8,16},{9,17},{10,... | collective-permute-start | bytes 786440 | tf_op jit(solution)/shard_map/ppermute | solution.py:255
  47.2 7.2 %collective-permute-start.19 = (bf16[1024,128]{1,0:T(8,128)(2,1)S(1)}, bf16[1024,128]{1,0:T(8,128)(2,1)S(1)}, u32[]{:S(2)}, u32[]{:S(2)}) collective-permute-start(bf16[1024,128]{1,0:T(8,128)(2,1)S(1)} %get-tuple-element.85), channel_id=1, source_target_pairs={{0,8},{1,9},{2,10},{3,11},{4,12},{5,13},{6,14},{7,15},{8,0},{9,1},... | collective-permute-start | bytes 786440 | tf_op jit(solution)/shard_map/ppermute | solution.py:255
  50.1 3.9 %collective-permute-start.21 = (bf16[128,128]{1,0:T(8,128)(2,1)S(1)}, bf16[128,128]{1,0:T(8,128)(2,1)S(1)}, u32[]{:S(2)}, u32[]{:S(2)}) collective-permute-start(bf16[128,128]{1,0:T(8,128)(2,1)S(1)} %get-tuple-element.86), channel_id=1, source_target_pairs={{0,1},{1,0},{2,3},{3,2},{4,5},{5,4},{6,7},{7,6},{8,9},{9,8},{10,11... | collective-permute-start | bytes 98312 | tf_op jit(solution)/shard_map/ppermute | solution.py:255
  50.6 3.4 %collective-permute-start.20 = (bf16[128,128]{1,0:T(8,128)(2,1)S(1)}, bf16[128,128]{1,0:T(8,128)(2,1)S(1)}, u32[]{:S(2)}, u32[]{:S(2)}) collective-permute-start(bf16[128,128]{1,0:T(8,128)(2,1)S(1)} %get-tuple-element.86), channel_id=1, source_target_pairs={{0,8},{1,2},{2,1},{3,11},{4,12},{5,6},{6,5},{7,15},{8,0},{9,10},{1... | collective-permute-start | bytes 98312 | tf_op jit(solution)/shard_map/ppermute | solution.py:255

commit v19 on v18

--- a/solution.py
+++ b/solution.py
@@ -265,7 +265,7 @@
         self.half = self.block // 2
         self.half_rows = self.half * self.cells
         self.outer = [("col", i) for i in range(turns("col"))]
-        self.inner = [("row", i) for i in reversed(range(turns("row")))]
+        self.inner = [("row", i) for i in range(turns("row"))]
         self.faces = self.outer + self.inner
         self.ends = turns("gz")
 

time: 57 us -> 56.6 us (level)
  waiting for transfers between devices: 8.42 us -> 6.6 us
  starting transfers between devices: 25.3 us -> 26.4 us
    ppermute x1, waiting for transfers between devices: 1.15 us -> 0.01 us  [flux_sums(): other = lax.ppermute(other, 'col', [(0, 1), (1, 0)])]
    ppermute x15, starting transfers between devices: 16.2 us -> 17.3 us  [swap(): return lax.ppermute(value, axes, pairs)]
    ppermute x15, waiting for transfers between devices: 3.94 us -> 3.11 us  [swap(): return lax.ppermute(value, axes, pairs)]
  transfers between devices with their start and end apart: 22 -> 22, of which waited for: 6 -> 5; matrix products, arithmetic and copies ran while one was open for 0% -> 0% of each run, Pallas kernels for 17% -> 17%
where the time goes in v19:
time: 56.6 us; the launch traced here: 56.1 us
  starting transfers between devices  26.4 us (47%)
  Pallas kernels  21.4 us (38%)
  waiting for transfers between devices  6.6 us (12%)
  between operations  0.98 us (2%)
  local copies, waits for them, and re-layouts  0.71 us (1%)
    ppermute x15, starting transfers between devices, swap(): return lax.ppermute(value, axes, pairs)  17.3 us
    pallas_call x3, Pallas kernels, sweep_finish(): pl.pallas_call(functools.partial(finish_kernel, shape, len(ends), len(rec...  8.63 us
    pallas_call x3, Pallas kernels, sweep_base(): pl.pallas_call(functools.partial(base_kernel, shape, len(ends), phi is no...  5.52 us
    ppermute x3, starting transfers between devices, flux_sums(): lax.ppermute(sent[key], 'gz', [(i, i ^ key) for i in range(gzs)])  4.45 us
    pallas_call x1, Pallas kernels, first_faces(): pl.pallas_call(functools.partial(faces_kernel, shape, slots), in_specs=[h...  3.45 us
    ppermute x15, waiting for transfers between devices, swap(): return lax.ppermute(value, axes, pairs)  3.11 us
    pallas_call x1, Pallas kernels, traces(): pl.pallas_call(functools.partial(trace_kernel, shape, stride, block), in_...  3.03 us
    ppermute x3, starting transfers between devices, row_gather(): lax.ppermute(held[key], 'row', pairs)  3.01 us
  transfers between devices with their start and end apart: 22, of which 5 were waited for; matrix products, arithmetic and copies ran while one was open for 0% of the time, Pallas kernels for 17%

profile of v19, /device:TPU:0, one launch (start us, length us, event | category | flops | bytes accessed | tf_op | source)
XLA Modules:
  0.0 56.1 jit_solution(8666015184857800704)
XLA Ops:
  0.6 0.7 %copy-done.3 = s32[1,1,1,1024]{3,2,1,0:T(1,128)S(1)} copy-done((s32[1,1,1,1024]{3,2,1,0:T(1,128)S(1)}, s32[1,1,1,1024]{3,2,1,0:T(1,128)}, u32[]{:S(2)}) %copy-start.3) | copy-done | bytes 4120
  1.3 3.0 %shard_map.78 = (bf16[1024,128]{1,0:T(8,128)(2,1)S(1)}, bf16[1024,128]{1,0:T(8,128)(2,1)S(1)}) custom-call(bf16[128,64,128]{2,1,0:T(8,128)(2,1)} %bitcast.5, s32[1,1,1,1024]{3,2,1,0:T(1,128)S(1)} %copy-done.3), custom_call_target="tpu_custom_call" | custom-call | flops 536870912 | bytes 2097152 | tf_op jit(solution)/shard_map/pallas_call | solution.py:106
  4.4 3.0 %collective-permute-start.1 = (bf16[1024,128]{1,0:T(8,128)(2,1)S(1)}, bf16[1024,128]{1,0:T(8,128)(2,1)S(1)}, u32[]{:S(2)}, u32[]{:S(2)}) collective-permute-start(bf16[1024,128]{1,0:T(8,128)(2,1)S(1)} %get-tuple-element.53.refs_0_), channel_id=1, source_target_pairs={{0,16},{8,24},{16,0},{24,8},{1,17},{9,25},{17,1},{25,9},{2,18},{10... | collective-permute-start | bytes 786440 | tf_op jit(solution)/shard_map/ppermute | solution.py:689
  7.4 1.5 %collective-permute-start.3 = (bf16[1024,128]{1,0:T(8,128)(2,1)S(1)}, bf16[1024,128]{1,0:T(8,128)(2,1)S(1)}, u32[]{:S(2)}, u32[]{:S(2)}) collective-permute-start(bf16[1024,128]{1,0:T(8,128)(2,1)S(1)} %get-tuple-element.52), channel_id=1, source_target_pairs={{0,4},{1,5},{2,6},{3,7},{4,0},{5,1},{6,2},{7,3},{8,12},{9,13},{10,... | collective-permute-start | bytes 786440 | tf_op jit(solution)/shard_map/ppermute | solution.py:255
  8.9 3.5 %shard_map.77 = (bf16[1024,128]{1,0:T(8,128)(2,1)S(1)}, bf16[1024,128]{1,0:T(8,128)(2,1)S(1)}, bf16[128,128]{1,0:T(8,128)(2,1)S(1)}, bf16[4,256,1024]{2,1,0:T(8,...) custom-call(bf16[8192,128]{1,0:T(8,128)(2,1)} %bitcast.6, ...), custom_call_target="tpu_custom_call" | custom-call | flops 134217728 | bytes 4194304 | tf_op jit(solution)/shard_map/pallas_call | solution.py:418
  12.4 1.3 %collective-permute-done.1.refs_2_ = bf16[1024,128]{1,0:T(8,128)(2,1)S(1)} collective-permute-done((bf16[1024,128]{1,0:T(8,128)(2,1)S(1)}, bf16[1024,128]{1,0:T(8,128)(2,1)S(1)}, u32[]{:S(2)}, u32[]{:S(2)}) %collective-permute-start.1) | collective-permute-done | bytes 262176 | tf_op jit(solution)/shard_map/ppermute | solution.py:689
  13.7 0.5 collective-permute-start.6
  14.2 0.7 %collective-permute-start.7 = (bf16[1024,128]{1,0:T(8,128)(2,1)S(1)}, bf16[1024,128]{1,0:T(8,128)(2,1)S(1)}, u32[]{:S(2)}, u32[]{:S(2)}) collective-permute-start(bf16[1024,128]{1,0:T(8,128)(2,1)S(1)} %get-tuple-element.66), channel_id=1, source_target_pairs={{0,0},{1,1},{2,2},{3,3},{4,4},{5,5},{6,6},{7,7},{8,16},{9,17},{10,... | collective-permute-start | bytes 786440 | tf_op jit(solution)/shard_map/ppermute | solution.py:255
  14.9 1.2 %collective-permute-done.3.refs_6_ = bf16[1024,128]{1,0:T(8,128)(2,1)S(1)} collective-permute-done((bf16[1024,128]{1,0:T(8,128)(2,1)S(1)}, bf16[1024,128]{1,0:T(8,128)(2,1)S(1)}, u32[]{:S(2)}, u32[]{:S(2)}) %collective-permute-start.3) | collective-permute-done | bytes 262176 | tf_op jit(solution)/shard_map/ppermute | solution.py:255
  16.1 0.7 %shard_map.79 = (f32[128,128]{1,0:T(8,128)S(1)}, f32[128,128]{1,0:T(8,128)S(1)}) custom-call(bf16[1024,128]{1,0:T(8,128)(2,1)S(1)} %get-tuple-element.53.refs_0_, bf16[1024,128]{1,0:T(8,128)(2,1)S(1)} %collective-permute-done.refs_1_, bf16[1024,128]{1,0:T(8,128)(2,1)S(1)} %collective-permute-done.1.refs_2_, ...), custom_call_target="tpu_custom_call" | custom-call | flops 268435456 | bytes 2097152 | tf_op jit(solution)/shard_map/pallas_call | solution.py:160
  16.8 1.6 %collective-permute-start.8 = (f32[128,128]{1,0:T(8,128)S(1)}, f32[128,128]{1,0:T(8,128)S(1)}, u32[]{:S(2)}, u32[]{:S(2)}) collective-permute-start(f32[128,128]{1,0:T(8,128)S(1)} %get-tuple-element.68), channel_id=1, source_target_pairs={{0,4},{4,0},{1,5},{5,1},{2,6},{6,2},{3,7},{7,3},{8,12},{12,8},{9,1... | collective-permute-start | bytes 196616 | tf_op jit(solution)/shard_map/ppermute | solution.py:210
  18.4 1.6 %collective-permute-start.5 = (bf16[128,128]{1,0:T(8,128)(2,1)S(1)}, bf16[128,128]{1,0:T(8,128)(2,1)S(1)}, u32[]{:S(2)}, u32[]{:S(2)}) collective-permute-start(bf16[128,128]{1,0:T(8,128)(2,1)S(1)} %get-tuple-element.61), channel_id=1, source_target_pairs={{0,1},{1,0},{2,3},{3,2},{4,5},{5,4},{6,7},{7,6},{8,9},{9,8},{10,11... | collective-permute-start | bytes 98312 | tf_op jit(solution)/shard_map/ppermute | solution.py:255
  20.0 1.3 %collective-permute-start.4 = (bf16[128,128]{1,0:T(8,128)(2,1)S(1)}, bf16[128,128]{1,0:T(8,128)(2,1)S(1)}, u32[]{:S(2)}, u32[]{:S(2)}) collective-permute-start(bf16[128,128]{1,0:T(8,128)(2,1)S(1)} %get-tuple-element.61), channel_id=1, source_target_pairs={{0,8},{1,2},{2,1},{3,11},{4,12},{5,6},{6,5},{7,15},{8,0},{9,10},{1... | collective-permute-start | bytes 98312 | tf_op jit(solution)/shard_map/ppermute | solution.py:255
  21.4 3.5 %collective-permute-start.9 = (f32[64,128]{1,0:T(8,128)S(1)}, f32[64,128]{1,0:T(8,128)S(1)}, u32[]{:S(2)}, u32[]{:S(2)}) collective-permute-start(f32[64,128]{1,0:T(8,128)S(1)} %get-tuple-element.71), channel_id=1, source_target_pairs={{0,3},{1,2},{2,1},{3,0},{4,7},{5,6},{6,5},{7,4},{8,11},{9,10},{10,... | collective-permute-start | bytes 98312 | tf_op jit(solution)/shard_map/ppermute | solution.py:215
  24.9 1.0 %collective-permute-start.11 = (f32[64,128]{1,0:T(8,128)S(1)}, f32[64,128]{1,0:T(8,128)S(1)}, u32[]{:S(2)}, u32[]{:S(2)}) collective-permute-start(f32[64,128]{1,0:T(8,128)S(1)} %get-tuple-element.73), channel_id=1, source_target_pairs={{0,1},{1,0},{2,3},{3,2},{4,5},{5,4},{6,7},{7,6},{8,9},{9,8},{10,11... | collective-permute-start | bytes 98312 | tf_op jit(solution)/shard_map/ppermute | solution.py:215
  25.9 2.0 %shard_map.80.refs_0_ = f32[8192,128]{1,0:T(8,128)S(1)} custom-call(bf16[8192,128]{1,0:T(8,128)(2,1)S(1)} %bitcast.7, bf16[8192,128]{1,0:T(8,128)(2,1)S(1)} %bitcast.8, f32[128,128]{1,0:T(8,128)S(1)} %get-tuple-element.45.refs_2_.refs_1_, bf16[128,176]{1,0:T(8,128)(2,1)S(1)} %get-tuple-element.46.refs_3_.refs_2_, ...), custom_call_target="tpu_custom_call" | custom-call | flops 805306368 | bytes 8388608 | tf_op jit(solution)/shard_map/pallas_call | solution.py:525
  27.9 2.2 %collective-permute-done.10.refs_12_ = f32[64,128]{1,0:T(8,128)S(1)} collective-permute-done((f32[64,128]{1,0:T(8,128)S(1)}, f32[64,128]{1,0:T(8,128)S(1)}, u32[]{:S(2)}, u32[]{:S(2)}) %collective-permute-start.10) | collective-permute-done | bytes 32800 | tf_op jit(solution)/shard_map/ppermute | solution.py:215
  30.1 3.5 %shard_map.82 = (bf16[8192,128]{1,0:T(8,128)(2,1)S(1)}, bf16[1024,128]{1,0:T(8,128)(2,1)S(1)}, bf16[1024,128]{1,0:T(8,128)(2,1)S(1)}, bf16[1024,128]{1,0:T(8,128...) custom-call(f32[8192,128]{1,0:T(8,128)S(1)} %shard_map.80.refs_0_, ...), custom_call_target="tpu_custom_call" | custom-call | flops 536870912 | bytes 8388608 | tf_op jit(solution)/shard_map/pallas_call | solution.py:662
  33.6 1.3 %collective-permute-start.12 = (bf16[1024,128]{1,0:T(8,128)(2,1)S(1)}, bf16[1024,128]{1,0:T(8,128)(2,1)S(1)}, u32[]{:S(2)}, u32[]{:S(2)}) collective-permute-start(bf16[1024,128]{1,0:T(8,128)(2,1)S(1)} %get-tuple-element.77), channel_id=1, source_target_pairs={{0,4},{1,5},{2,6},{3,7},{4,0},{5,1},{6,2},{7,3},{8,12},{9,13},{10,... | collective-permute-start | bytes 786440 | tf_op jit(solution)/shard_map/ppermute | solution.py:255
  34.8 0.8 %collective-permute-start.14 = (bf16[1024,128]{1,0:T(8,128)(2,1)S(1)}, bf16[1024,128]{1,0:T(8,128)(2,1)S(1)}, u32[]{:S(2)}, u32[]{:S(2)}) collective-permute-start(bf16[1024,128]{1,0:T(8,128)(2,1)S(1)} %get-tuple-element.79), channel_id=1, source_target_pairs={{0,0},{1,1},{2,2},{3,3},{4,4},{5,5},{6,6},{7,7},{8,16},{9,17},{10,... | collective-permute-start | bytes 786440 | tf_op jit(solution)/shard_map/ppermute | solution.py:255
  35.7 0.9 %collective-permute-start.16 = (bf16[128,128]{1,0:T(8,128)(2,1)S(1)}, bf16[128,128]{1,0:T(8,128)(2,1)S(1)}, u32[]{:S(2)}, u32[]{:S(2)}) collective-permute-start(bf16[128,128]{1,0:T(8,128)(2,1)S(1)} %get-tuple-element.80), channel_id=1, source_target_pairs={{0,1},{1,0},{2,3},{3,2},{4,5},{5,4},{6,7},{7,6},{8,9},{9,8},{10,11... | collective-permute-start | bytes 98312 | tf_op jit(solution)/shard_map/ppermute | solution.py:255
  36.5 3.0 %collective-permute-start.15 = (bf16[128,128]{1,0:T(8,128)(2,1)S(1)}, bf16[128,128]{1,0:T(8,128)(2,1)S(1)}, u32[]{:S(2)}, u32[]{:S(2)}) collective-permute-start(bf16[128,128]{1,0:T(8,128)(2,1)S(1)} %get-tuple-element.80), channel_id=1, source_target_pairs={{0,8},{1,2},{2,1},{3,11},{4,12},{5,6},{6,5},{7,15},{8,0},{9,10},{1... | collective-permute-start | bytes 98312 | tf_op jit(solution)/shard_map/ppermute | solution.py:255
  39.6 2.0 %shard_map.83 = (f32[8192,128]{1,0:T(8,128)S(1)}, bf16[8192,128]{1,0:T(8,128)(2,1)S(1)}) custom-call(bf16[8192,128]{1,0:T(8,128)(2,1)S(1)} %get-tuple-element.74.refs_0_, bf16[8192,128]{1,0:T(8,128)(2,1)S(1)} %bitcast.9, f32[128,128]{1,0:T(8,128)S(1)} %get-tuple-element.45.refs_2_.refs_1_, bf16[128,176]{1,0:T(8,128)(2,1)S(1)} %get-tuple-element.46.refs_3_.refs_2_, ...), custom_call_target="tpu_custom_call" | custom-call | flops 805306368 | bytes 8388608 | tf_op jit(solution)/shard_map/pallas_call | solution.py:525
  41.9 2.9 %shard_map.84 = (bf16[8192,128]{1,0:T(8,128)(2,1)S(1)}, bf16[1024,128]{1,0:T(8,128)(2,1)S(1)}, bf16[1024,128]{1,0:T(8,128)(2,1)S(1)}, bf16[1024,128]{1,0:T(8,128)(2,1)S(1)}, bf16[128,128]{1,0:T(8,128)(2,1)S(1)}) custom-call(f32[8192,128]{1,0:T(8,128)S(1)} %get-tuple-element.76.refs_0_, f32[128,128]{1,0:T(8,128)S(1)} %get-tuple-element.45.refs_2_.refs_1_, ...), custom_call_target="tpu_custom_call" | custom-call | flops 536870912 | bytes 8388608 | tf_op jit(solution)/shard_map/pallas_call | solution.py:662
  44.7 1.0 %collective-permute-start.17 = (bf16[1024,128]{1,0:T(8,128)(2,1)S(1)}, bf16[1024,128]{1,0:T(8,128)(2,1)S(1)}, u32[]{:S(2)}, u32[]{:S(2)}) collective-permute-start(bf16[1024,128]{1,0:T(8,128)(2,1)S(1)} %get-tuple-element.83), channel_id=1, source_target_pairs={{0,4},{1,5},{2,6},{3,7},{4,0},{5,1},{6,2},{7,3},{8,12},{9,13},{10,... | collective-permute-start | bytes 786440 | tf_op jit(solution)/shard_map/ppermute | solution.py:255
  45.7 0.6 %collective-permute-start.18 = (bf16[1024,128]{1,0:T(8,128)(2,1)S(1)}, bf16[1024,128]{1,0:T(8,128)(2,1)S(1)}, u32[]{:S(2)}, u32[]{:S(2)}) collective-permute-start(bf16[1024,128]{1,0:T(8,128)(2,1)S(1)} %get-tuple-element.84), channel_id=1, source_target_pairs={{0,8},{1,9},{2,10},{3,11},{4,12},{5,13},{6,14},{7,15},{8,0},{9,1},... | collective-permute-start | bytes 786440 | tf_op jit(solution)/shard_map/ppermute | solution.py:255
  46.3 0.7 %collective-permute-start.19 = (bf16[1024,128]{1,0:T(8,128)(2,1)S(1)}, bf16[1024,128]{1,0:T(8,128)(2,1)S(1)}, u32[]{:S(2)}, u32[]{:S(2)}) collective-permute-start(bf16[1024,128]{1,0:T(8,128)(2,1)S(1)} %get-tuple-element.85), channel_id=1, source_target_pairs={{0,0},{1,1},{2,2},{3,3},{4,4},{5,5},{6,6},{7,7},{8,16},{9,17},{10,... | collective-permute-start | bytes 786440 | tf_op jit(solution)/shard_map/ppermute | solution.py:255
  47.0 0.8 %collective-permute-start.21 = (bf16[128,128]{1,0:T(8,128)(2,1)S(1)}, bf16[128,128]{1,0:T(8,128)(2,1)S(1)}, u32[]{:S(2)}, u32[]{:S(2)}) collective-permute-start(bf16[128,128]{1,0:T(8,128)(2,1)S(1)} %get-tuple-element.86), channel_id=1, source_target_pairs={{0,1},{1,0},{2,3},{3,2},{4,5},{5,4},{6,7},{7,6},{8,9},{9,8},{10,11... | collective-permute-start | bytes 98312 | tf_op jit(solution)/shard_map/ppermute | solution.py:255
  47.8 2.7 %collective-permute-start.20 = (bf16[128,128]{1,0:T(8,128)(2,1)S(1)}, bf16[128,128]{1,0:T(8,128)(2,1)S(1)}, u32[]{:S(2)}, u32[]{:S(2)}) collective-permute-start(bf16[128,128]{1,0:T(8,128)(2,1)S(1)} %get-tuple-element.86), channel_id=1, source_target_pairs={{0,8},{1,2},{2,1},{3,11},{4,12},{5,6},{6,5},{7,15},{8,0},{9,10},{1... | collective-permute-start | bytes 98312 | tf_op jit(solution)/shard_map/ppermute | solution.py:255
  50.5 1.5 %shard_map.85.refs_0_ = f32[8192,128]{1,0:T(8,128)S(1)} custom-call(bf16[8192,128]{1,0:T(8,128)(2,1)S(1)} %get-tuple-element.81.refs_0_, bf16[8192,128]{1,0:T(8,128)(2,1)S(1)} %get-tuple-element.82.refs_1_, f32[128,128]{1,0:T(8,128)S(1)} %get-tuple-element.45.refs_2_.refs_1_, bf16[128,176]{1,0:T(8,128)(2,1)S(1)} %get-tuple-element.46.refs_3_.refs_2_, ...), custom_call_target="tpu_custom_call" | custom-call | flops 805306368 | bytes 8388608 | tf_op jit(solution)/shard_map/pallas_call | solution.py:525
  52.0 1.6 %collective-permute-done.17.refs_6_ = bf16[1024,128]{1,0:T(8,128)(2,1)S(1)} collective-permute-done((bf16[1024,128]{1,0:T(8,128)(2,1)S(1)}, bf16[1024,128]{1,0:T(8,128)(2,1)S(1)}, u32[]{:S(2)}, u32[]{:S(2)}) %collective-permute-start.17) | collective-permute-done | bytes 262176 | tf_op jit(solution)/shard_map/ppermute | solution.py:255
  53.6 2.3 %shard_map.86 = bf16[8192,128]{1,0:T(8,128)(2,1)} custom-call(f32[8192,128]{1,0:T(8,128)S(1)} %shard_map.85.refs_0_, f32[128,128]{1,0:T(8,128)S(1)} %get-tuple-element.45.refs_2_.refs_1_, bf16[128,176]{1,0:T(8,128)(2,1)S(1)} %get-tuple-element.46.refs_3_.refs_2_, bf16[512,256]{1,0:T(8,128)(2,1)S(1)} %get-tuple-element.47.refs_4_.refs_3_, ...), custom_call_target="tpu_custom_call" | custom-call | flops 536870912 | bytes 8388608 | tf_op jit(solution)/shard_map/pallas_call | solution.py:662
  (32 shorter events, 0.4 us)
Async XLA Ops:
  0.6 8.3 %copy-start.2 = (f32[8,8,128]{2,1,0:T(8,128)S(1)}, f32[8,8,128]{2,1,0:T(8,128)}, u32[]{:S(2)}) copy-start(f32[8,8,128]{2,1,0:T(8,128)} %param.8) | copy-start | bytes 98308
  0.6 0.7 %copy-start.3 = (s32[1,1,1,1024]{3,2,1,0:T(1,128)S(1)}, s32[1,1,1,1024]{3,2,1,0:T(1,128)}, u32[]{:S(2)}) copy-start(s32[1,1,1,1024]{3,2,1,0:T(1,128)} %cell_ref.1) | copy-start | bytes 12292
  4.4 9.3 %collective-permute-start.1 = (bf16[1024,128]{1,0:T(8,128)(2,1)S(1)}, bf16[1024,128]{1,0:T(8,128)(2,1)S(1)}, u32[]{:S(2)}, u32[]{:S(2)}) collective-permute-start(bf16[1024,128]{1,0:T(8,128)(2,1)S(1)} %get-tuple-element.53.refs_0_), channel_id=1, source_target_pairs={{0,16},{8,24},{16,0},{24,8},{1,17},{9,25},{17,1},{25,9},{2,18},{10... | collective-permute-start | bytes 786440 | tf_op jit(solution)/shard_map/ppermute | solution.py:689
  7.4 8.7 %collective-permute-start = (bf16[1024,128]{1,0:T(8,128)(2,1)S(1)}, bf16[1024,128]{1,0:T(8,128)(2,1)S(1)}, u32[]{:S(2)}, u32[]{:S(2)}) collective-permute-start(bf16[1024,128]{1,0:T(8,128)(2,1)S(1)} %get-tuple-element.53.refs_0_), channel_id=1, source_target_pairs={{0,8},{8,0},{16,24},{24,16},{1,9},{9,1},{17,25},{25,17},{2,10},{10... | collective-permute-start | bytes 786440 | tf_op jit(solution)/shard_map/ppermute | solution.py:689
  7.4 8.7 %collective-permute-start.3 = (bf16[1024,128]{1,0:T(8,128)(2,1)S(1)}, bf16[1024,128]{1,0:T(8,128)(2,1)S(1)}, u32[]{:S(2)}, u32[]{:S(2)}) collective-permute-start(bf16[1024,128]{1,0:T(8,128)(2,1)S(1)} %get-tuple-element.52), channel_id=1, source_target_pairs={{0,4},{1,5},{2,6},{3,7},{4,0},{5,1},{6,2},{7,3},{8,12},{9,13},{10,... | collective-permute-start | bytes 786440 | tf_op jit(solution)/shard_map/ppermute | solution.py:255
  8.9 17.0 %copy-start.1 = (bf16[128,8,8,128]{3,2,1,0:T(8,128)(2,1)S(1)}, bf16[128,8,8,128]{3,2,1,0:T(8,128)(2,1)}, u32[]{:S(2)}) copy-start(bf16[128,8,8,128]{3,2,1,0:T(8,128)(2,1)} %param.7) | copy-start | bytes 6291460
  12.4 13.5 %copy-start = (bf16[128,8,8,128]{3,2,1,0:T(8,128)(2,1)S(1)}, bf16[128,8,8,128]{3,2,1,0:T(8,128)(2,1)}, u32[]{:S(2)}) copy-start(bf16[128,8,8,128]{3,2,1,0:T(8,128)(2,1)} %param.6) | copy-start | bytes 6291460
  13.7 2.4 %collective-permute-start.2 = (bf16[1024,128]{1,0:T(8,128)(2,1)S(1)}, bf16[1024,128]{1,0:T(8,128)(2,1)S(1)}, u32[]{:S(2)}, u32[]{:S(2)}) collective-permute-start(bf16[1024,128]{1,0:T(8,128)(2,1)S(1)} %collective-permute-done.1.refs_2_), channel_id=1, source_target_pairs={{0,8},{8,0},{16,24},{24,16},{1,9},{9,1},{17,25},{25,17},{2,10},{10... | collective-permute-start | bytes 786440 | tf_op jit(solution)/shard_map/ppermute | solution.py:689
  13.7 7.6 %collective-permute-start.6 = (bf16[1024,128]{1,0:T(8,128)(2,1)S(1)}, bf16[1024,128]{1,0:T(8,128)(2,1)S(1)}, u32[]{:S(2)}, u32[]{:S(2)}) collective-permute-start(bf16[1024,128]{1,0:T(8,128)(2,1)S(1)} %get-tuple-element.65), channel_id=1, source_target_pairs={{0,8},{1,9},{2,10},{3,11},{4,12},{5,13},{6,14},{7,15},{8,0},{9,1},... | collective-permute-start | bytes 786440 | tf_op jit(solution)/shard_map/ppermute | solution.py:255
  14.2 7.1 %collective-permute-start.7 = (bf16[1024,128]{1,0:T(8,128)(2,1)S(1)}, bf16[1024,128]{1,0:T(8,128)(2,1)S(1)}, u32[]{:S(2)}, u32[]{:S(2)}) collective-permute-start(bf16[1024,128]{1,0:T(8,128)(2,1)S(1)} %get-tuple-element.66), channel_id=1, source_target_pairs={{0,0},{1,1},{2,2},{3,3},{4,4},{5,5},{6,6},{7,7},{8,16},{9,17},{10,... | collective-permute-start | bytes 786440 | tf_op jit(solution)/shard_map/ppermute | solution.py:255
  16.8 4.5 %collective-permute-start.8 = (f32[128,128]{1,0:T(8,128)S(1)}, f32[128,128]{1,0:T(8,128)S(1)}, u32[]{:S(2)}, u32[]{:S(2)}) collective-permute-start(f32[128,128]{1,0:T(8,128)S(1)} %get-tuple-element.68), channel_id=1, source_target_pairs={{0,4},{4,0},{1,5},{5,1},{2,6},{6,2},{3,7},{7,3},{8,12},{12,8},{9,1... | collective-permute-start | bytes 196616 | tf_op jit(solution)/shard_map/ppermute | solution.py:210
  18.4 7.5 %collective-permute-start.5 = (bf16[128,128]{1,0:T(8,128)(2,1)S(1)}, bf16[128,128]{1,0:T(8,128)(2,1)S(1)}, u32[]{:S(2)}, u32[]{:S(2)}) collective-permute-start(bf16[128,128]{1,0:T(8,128)(2,1)S(1)} %get-tuple-element.61), channel_id=1, source_target_pairs={{0,1},{1,0},{2,3},{3,2},{4,5},{5,4},{6,7},{7,6},{8,9},{9,8},{10,11... | collective-permute-start | bytes 98312 | tf_op jit(solution)/shard_map/ppermute | solution.py:255
  20.0 5.9 %collective-permute-start.4 = (bf16[128,128]{1,0:T(8,128)(2,1)S(1)}, bf16[128,128]{1,0:T(8,128)(2,1)S(1)}, u32[]{:S(2)}, u32[]{:S(2)}) collective-permute-start(bf16[128,128]{1,0:T(8,128)(2,1)S(1)} %get-tuple-element.61), channel_id=1, source_target_pairs={{0,8},{1,2},{2,1},{3,11},{4,12},{5,6},{6,5},{7,15},{8,0},{9,10},{1... | collective-permute-start | bytes 98312 | tf_op jit(solution)/shard_map/ppermute | solution.py:255
  21.4 6.5 %collective-permute-start.9 = (f32[64,128]{1,0:T(8,128)S(1)}, f32[64,128]{1,0:T(8,128)S(1)}, u32[]{:S(2)}, u32[]{:S(2)}) collective-permute-start(f32[64,128]{1,0:T(8,128)S(1)} %get-tuple-element.71), channel_id=1, source_target_pairs={{0,3},{1,2},{2,1},{3,0},{4,7},{5,6},{6,5},{7,4},{8,11},{9,10},{10,... | collective-permute-start | bytes 98312 | tf_op jit(solution)/shard_map/ppermute | solution.py:215
  24.9 5.1 %collective-permute-start.10 = (f32[64,128]{1,0:T(8,128)S(1)}, f32[64,128]{1,0:T(8,128)S(1)}, u32[]{:S(2)}, u32[]{:S(2)}) collective-permute-start(f32[64,128]{1,0:T(8,128)S(1)} %get-tuple-element.72), channel_id=1, source_target_pairs={{0,2},{1,3},{2,0},{3,1},{4,6},{5,7},{6,4},{7,5},{8,10},{9,11},{10,... | collective-permute-start | bytes 98312 | tf_op jit(solution)/shard_map/ppermute | solution.py:215
  24.9 5.1 %collective-permute-start.11 = (f32[64,128]{1,0:T(8,128)S(1)}, f32[64,128]{1,0:T(8,128)S(1)}, u32[]{:S(2)}, u32[]{:S(2)}) collective-permute-start(f32[64,128]{1,0:T(8,128)S(1)} %get-tuple-element.73), channel_id=1, source_target_pairs={{0,1},{1,0},{2,3},{3,2},{4,5},{5,4},{6,7},{7,6},{8,9},{9,8},{10,11... | collective-permute-start | bytes 98312 | tf_op jit(solution)/shard_map/ppermute | solution.py:215
  25.9 4.2 %copy-start.4 = (s32[1,1,1,32]{3,2,1,0:T(1,128)S(1)}, s32[1,1,1,32]{3,2,1,0:T(1,128)}, u32[]{:S(2)}) copy-start(s32[1,1,1,32]{3,2,1,0:T(1,128)} %refs_6_.1) | copy-start | bytes 388
  33.6 8.3 %collective-permute-start.12 = (bf16[1024,128]{1,0:T(8,128)(2,1)S(1)}, bf16[1024,128]{1,0:T(8,128)(2,1)S(1)}, u32[]{:S(2)}, u32[]{:S(2)}) collective-permute-start(bf16[1024,128]{1,0:T(8,128)(2,1)S(1)} %get-tuple-element.77), channel_id=1, source_target_pairs={{0,4},{1,5},{2,6},{3,7},{4,0},{5,1},{6,2},{7,3},{8,12},{9,13},{10,... | collective-permute-start | bytes 786440 | tf_op jit(solution)/shard_map/ppermute | solution.py:255
  34.8 7.1 %collective-permute-start.13 = (bf16[1024,128]{1,0:T(8,128)(2,1)S(1)}, bf16[1024,128]{1,0:T(8,128)(2,1)S(1)}, u32[]{:S(2)}, u32[]{:S(2)}) collective-permute-start(bf16[1024,128]{1,0:T(8,128)(2,1)S(1)} %get-tuple-element.78), channel_id=1, source_target_pairs={{0,8},{1,9},{2,10},{3,11},{4,12},{5,13},{6,14},{7,15},{8,0},{9,1},... | collective-permute-start | bytes 786440 | tf_op jit(solution)/shard_map/ppermute | solution.py:255
  34.8 7.1 %collective-permute-start.14 = (bf16[1024,128]{1,0:T(8,128)(2,1)S(1)}, bf16[1024,128]{1,0:T(8,128)(2,1)S(1)}, u32[]{:S(2)}, u32[]{:S(2)}) collective-permute-start(bf16[1024,128]{1,0:T(8,128)(2,1)S(1)} %get-tuple-element.79), channel_id=1, source_target_pairs={{0,0},{1,1},{2,2},{3,3},{4,4},{5,5},{6,6},{7,7},{8,16},{9,17},{10,... | collective-permute-start | bytes 786440 | tf_op jit(solution)/shard_map/ppermute | solution.py:255
  35.7 5.9 %collective-permute-start.16 = (bf16[128,128]{1,0:T(8,128)(2,1)S(1)}, bf16[128,128]{1,0:T(8,128)(2,1)S(1)}, u32[]{:S(2)}, u32[]{:S(2)}) collective-permute-start(bf16[128,128]{1,0:T(8,128)(2,1)S(1)} %get-tuple-element.80), channel_id=1, source_target_pairs={{0,1},{1,0},{2,3},{3,2},{4,5},{5,4},{6,7},{7,6},{8,9},{9,8},{10,11... | collective-permute-start | bytes 98312 | tf_op jit(solution)/shard_map/ppermute | solution.py:255
  36.5 5.1 %collective-permute-start.15 = (bf16[128,128]{1,0:T(8,128)(2,1)S(1)}, bf16[128,128]{1,0:T(8,128)(2,1)S(1)}, u32[]{:S(2)}, u32[]{:S(2)}) collective-permute-start(bf16[128,128]{1,0:T(8,128)(2,1)S(1)} %get-tuple-element.80), channel_id=1, source_target_pairs={{0,8},{1,2},{2,1},{3,11},{4,12},{5,6},{6,5},{7,15},{8,0},{9,10},{1... | collective-permute-start | bytes 98312 | tf_op jit(solution)/shard_map/ppermute | solution.py:255
  44.7 8.9 %collective-permute-start.17 = (bf16[1024,128]{1,0:T(8,128)(2,1)S(1)}, bf16[1024,128]{1,0:T(8,128)(2,1)S(1)}, u32[]{:S(2)}, u32[]{:S(2)}) collective-permute-start(bf16[1024,128]{1,0:T(8,128)(2,1)S(1)} %get-tuple-element.83), channel_id=1, source_target_pairs={{0,4},{1,5},{2,6},{3,7},{4,0},{5,1},{6,2},{7,3},{8,12},{9,13},{10,... | collective-permute-start | bytes 786440 | tf_op jit(solution)/shard_map/ppermute | solution.py:255
  45.7 7.9 %collective-permute-start.18 = (bf16[1024,128]{1,0:T(8,128)(2,1)S(1)}, bf16[1024,128]{1,0:T(8,128)(2,1)S(1)}, u32[]{:S(2)}, u32[]{:S(2)}) collective-permute-start(bf16[1024,128]{1,0:T(8,128)(2,1)S(1)} %get-tuple-element.84), channel_id=1, source_target_pairs={{0,8},{1,9},{2,10},{3,11},{4,12},{5,13},{6,14},{7,15},{8,0},{9,1},... | collective-permute-start | bytes 786440 | tf_op jit(solution)/shard_map/ppermute | solution.py:255
  46.3 7.3 %collective-permute-start.19 = (bf16[1024,128]{1,0:T(8,128)(2,1)S(1)}, bf16[1024,128]{1,0:T(8,128)(2,1)S(1)}, u32[]{:S(2)}, u32[]{:S(2)}) collective-permute-start(bf16[1024,128]{1,0:T(8,128)(2,1)S(1)} %get-tuple-element.85), channel_id=1, source_target_pairs={{0,0},{1,1},{2,2},{3,3},{4,4},{5,5},{6,6},{7,7},{8,16},{9,17},{10,... | collective-permute-start | bytes 786440 | tf_op jit(solution)/shard_map/ppermute | solution.py:255
  47.0 5.0 %collective-permute-start.21 = (bf16[128,128]{1,0:T(8,128)(2,1)S(1)}, bf16[128,128]{1,0:T(8,128)(2,1)S(1)}, u32[]{:S(2)}, u32[]{:S(2)}) collective-permute-start(bf16[128,128]{1,0:T(8,128)(2,1)S(1)} %get-tuple-element.86), channel_id=1, source_target_pairs={{0,1},{1,0},{2,3},{3,2},{4,5},{5,4},{6,7},{7,6},{8,9},{9,8},{10,11... | collective-permute-start | bytes 98312 | tf_op jit(solution)/shard_map/ppermute | solution.py:255
  47.8 4.2 %collective-permute-start.20 = (bf16[128,128]{1,0:T(8,128)(2,1)S(1)}, bf16[128,128]{1,0:T(8,128)(2,1)S(1)}, u32[]{:S(2)}, u32[]{:S(2)}) collective-permute-start(bf16[128,128]{1,0:T(8,128)(2,1)S(1)} %get-tuple-element.86), channel_id=1, source_target_pairs={{0,8},{1,2},{2,1},{3,11},{4,12},{5,6},{6,5},{7,15},{8,0},{9,10},{1... | collective-permute-start | bytes 98312 | tf_op jit(solution)/shard_map/ppermute | solution.py:255

commit v20 on v18

--- a/solution.py
+++ b/solution.py
@@ -248,7 +248,9 @@
                 there[along] += 1 if here[along] % 2 == turn else -1
                 if not 0 <= there[along] < sizes[along]:
                     there[along] = here[along]
-                    if axis != "row" and r ^ 1 < sizes[0]:
+                    if axis == "row" and sizes[0] % 2 == 0:
+                        there[0] = sizes[0] - 1 - r
+                    elif axis != "row" and r ^ 1 < sizes[0]:
                         there[0] ^= 1
                 flat = [(at[0] * sizes[1] + at[1]) * sizes[2] + at[2] for at in (here, there)]
                 pairs.append(tuple(flat))

time: 57 us -> 58.9 us (1.033)
  waiting for transfers between devices: 8.42 us -> 16 us
  starting transfers between devices: 25.3 us -> 19.4 us
    ppermute x15, waiting for transfers between devices: 3.94 us -> 12.7 us  [swap(): return lax.ppermute(value, axes, pairs)]
    ppermute x15, starting transfers between devices: 16.2 us -> 10.3 us  [swap(): return lax.ppermute(value, axes, pairs)]
    ppermute x1, waiting for transfers between devices: 1.15 us -> 0.01 us  [flux_sums(): other = lax.ppermute(other, 'col', [(0, 1), (1, 0)])]
  transfers between devices with their start and end apart: 22 -> 22, of which waited for: 6 -> 10; matrix products, arithmetic and copies ran while one was open for 0% -> 0% of each run, Pallas kernels for 17% -> 17%
where the time goes in v20:
time: 58.9 us; the launch traced here: 58.7 us
  Pallas kernels  21.6 us (37%)
  starting transfers between devices  19.4 us (33%)
  waiting for transfers between devices  16 us (27%)
  between operations  0.92 us (2%)
  local copies, waits for them, and re-layouts  0.71 us (1%)
    ppermute x15, waiting for transfers between devices, swap(): return lax.ppermute(value, axes, pairs)  12.7 us
    ppermute x15, starting transfers between devices, swap(): return lax.ppermute(value, axes, pairs)  10.3 us
    pallas_call x3, Pallas kernels, sweep_finish(): pl.pallas_call(functools.partial(finish_kernel, shape, len(ends), len(rec...  8.81 us
    pallas_call x3, Pallas kernels, sweep_base(): pl.pallas_call(functools.partial(base_kernel, shape, len(ends), phi is no...  5.53 us
    ppermute x3, starting transfers between devices, flux_sums(): lax.ppermute(sent[key], 'gz', [(i, i ^ key) for i in range(gzs)])  4.45 us
    pallas_call x1, Pallas kernels, first_faces(): pl.pallas_call(functools.partial(faces_kernel, shape, slots), in_specs=[h...  3.45 us
    pallas_call x1, Pallas kernels, traces(): pl.pallas_call(functools.partial(trace_kernel, shape, stride, block), in_...  3.03 us
    ppermute x3, starting transfers between devices, row_gather(): lax.ppermute(held[key], 'row', pairs)  3.01 us
  transfers between devices with their start and end apart: 22, of which 10 were waited for; matrix products, arithmetic and copies ran while one was open for 0% of the time, Pallas kernels for 17%

profile of v20, /device:TPU:0, one launch (start us, length us, event | category | flops | bytes accessed | tf_op | source)
XLA Modules:
  0.0 58.7 jit_solution(13404033857252543172)
XLA Ops:
  0.6 0.7 %copy-done.3 = s32[1,1,1,1024]{3,2,1,0:T(1,128)S(1)} copy-done((s32[1,1,1,1024]{3,2,1,0:T(1,128)S(1)}, s32[1,1,1,1024]{3,2,1,0:T(1,128)}, u32[]{:S(2)}) %copy-start.3) | copy-done | bytes 4120
  1.3 3.0 %shard_map.78 = (bf16[1024,128]{1,0:T(8,128)(2,1)S(1)}, bf16[1024,128]{1,0:T(8,128)(2,1)S(1)}) custom-call(bf16[128,64,128]{2,1,0:T(8,128)(2,1)} %bitcast.5, s32[1,1,1,1024]{3,2,1,0:T(1,128)S(1)} %copy-done.3), custom_call_target="tpu_custom_call" | custom-call | flops 536870912 | bytes 2097152 | tf_op jit(solution)/shard_map/pallas_call | solution.py:106
  4.4 3.0 %collective-permute-start.1 = (bf16[1024,128]{1,0:T(8,128)(2,1)S(1)}, bf16[1024,128]{1,0:T(8,128)(2,1)S(1)}, u32[]{:S(2)}, u32[]{:S(2)}) collective-permute-start(bf16[1024,128]{1,0:T(8,128)(2,1)S(1)} %get-tuple-element.53.refs_0_), channel_id=1, source_target_pairs={{0,16},{8,24},{16,0},{24,8},{1,17},{9,25},{17,1},{25,9},{2,18},{10... | collective-permute-start | bytes 786440 | tf_op jit(solution)/shard_map/ppermute | solution.py:691
  7.4 1.5 %collective-permute-start.3 = (bf16[1024,128]{1,0:T(8,128)(2,1)S(1)}, bf16[1024,128]{1,0:T(8,128)(2,1)S(1)}, u32[]{:S(2)}, u32[]{:S(2)}) collective-permute-start(bf16[1024,128]{1,0:T(8,128)(2,1)S(1)} %get-tuple-element.52), channel_id=1, source_target_pairs={{0,4},{1,5},{2,6},{3,7},{4,0},{5,1},{6,2},{7,3},{8,12},{9,13},{10,... | collective-permute-start | bytes 786440 | tf_op jit(solution)/shard_map/ppermute | solution.py:257
  8.9 3.5 %shard_map.77 = (bf16[1024,128]{1,0:T(8,128)(2,1)S(1)}, bf16[1024,128]{1,0:T(8,128)(2,1)S(1)}, bf16[128,128]{1,0:T(8,128)(2,1)S(1)}, bf16[4,256,1024]{2,1,0:T(8,...) custom-call(bf16[8192,128]{1,0:T(8,128)(2,1)} %bitcast.6, ...), custom_call_target="tpu_custom_call" | custom-call | flops 134217728 | bytes 4194304 | tf_op jit(solution)/shard_map/pallas_call | solution.py:420
  12.4 1.3 %collective-permute-done.1.refs_2_ = bf16[1024,128]{1,0:T(8,128)(2,1)S(1)} collective-permute-done((bf16[1024,128]{1,0:T(8,128)(2,1)S(1)}, bf16[1024,128]{1,0:T(8,128)(2,1)S(1)}, u32[]{:S(2)}, u32[]{:S(2)}) %collective-permute-start.1) | collective-permute-done | bytes 262176 | tf_op jit(solution)/shard_map/ppermute | solution.py:691
  13.7 1.9 %collective-permute-start.6 = (bf16[1024,128]{1,0:T(8,128)(2,1)S(1)}, bf16[1024,128]{1,0:T(8,128)(2,1)S(1)}, u32[]{:S(2)}, u32[]{:S(2)}) collective-permute-start(bf16[1024,128]{1,0:T(8,128)(2,1)S(1)} %get-tuple-element.65), channel_id=1, source_target_pairs={{0,24},{1,25},{2,26},{3,27},{4,28},{5,29},{6,30},{7,31},{8,16},{9,... | collective-permute-start | bytes 786440 | tf_op jit(solution)/shard_map/ppermute | solution.py:257
  15.5 0.6 collective-permute-done.3.refs_6_
  16.1 0.7 %shard_map.79 = (f32[128,128]{1,0:T(8,128)S(1)}, f32[128,128]{1,0:T(8,128)S(1)}) custom-call(bf16[1024,128]{1,0:T(8,128)(2,1)S(1)} %get-tuple-element.53.refs_0_, bf16[1024,128]{1,0:T(8,128)(2,1)S(1)} %collective-permute-done.refs_1_, bf16[1024,128]{1,0:T(8,128)(2,1)S(1)} %collective-permute-done.1.refs_2_, ...), custom_call_target="tpu_custom_call" | custom-call | flops 268435456 | bytes 2097152 | tf_op jit(solution)/shard_map/pallas_call | solution.py:160
  16.8 1.6 %collective-permute-start.8 = (f32[128,128]{1,0:T(8,128)S(1)}, f32[128,128]{1,0:T(8,128)S(1)}, u32[]{:S(2)}, u32[]{:S(2)}) collective-permute-start(f32[128,128]{1,0:T(8,128)S(1)} %get-tuple-element.68), channel_id=1, source_target_pairs={{0,4},{4,0},{1,5},{5,1},{2,6},{6,2},{3,7},{7,3},{8,12},{12,8},{9,1... | collective-permute-start | bytes 196616 | tf_op jit(solution)/shard_map/ppermute | solution.py:210
  18.4 1.6 %collective-permute-start.5 = (bf16[128,128]{1,0:T(8,128)(2,1)S(1)}, bf16[128,128]{1,0:T(8,128)(2,1)S(1)}, u32[]{:S(2)}, u32[]{:S(2)}) collective-permute-start(bf16[128,128]{1,0:T(8,128)(2,1)S(1)} %get-tuple-element.61), channel_id=1, source_target_pairs={{0,1},{1,0},{2,3},{3,2},{4,5},{5,4},{6,7},{7,6},{8,9},{9,8},{10,11... | collective-permute-start | bytes 98312 | tf_op jit(solution)/shard_map/ppermute | solution.py:257
  20.0 1.9 %collective-permute-done.6.refs_7_ = bf16[1024,128]{1,0:T(8,128)(2,1)S(1)} collective-permute-done((bf16[1024,128]{1,0:T(8,128)(2,1)S(1)}, bf16[1024,128]{1,0:T(8,128)(2,1)S(1)}, u32[]{:S(2)}, u32[]{:S(2)}) %collective-permute-start.6) | collective-permute-done | bytes 262176 | tf_op jit(solution)/shard_map/ppermute | solution.py:257
  22.0 3.7 %collective-permute-start.9 = (f32[64,128]{1,0:T(8,128)S(1)}, f32[64,128]{1,0:T(8,128)S(1)}, u32[]{:S(2)}, u32[]{:S(2)}) collective-permute-start(f32[64,128]{1,0:T(8,128)S(1)} %get-tuple-element.71), channel_id=1, source_target_pairs={{0,3},{1,2},{2,1},{3,0},{4,7},{5,6},{6,5},{7,4},{8,11},{9,10},{10,... | collective-permute-start | bytes 98312 | tf_op jit(solution)/shard_map/ppermute | solution.py:215
  25.7 0.8 %collective-permute-start.11 = (f32[64,128]{1,0:T(8,128)S(1)}, f32[64,128]{1,0:T(8,128)S(1)}, u32[]{:S(2)}, u32[]{:S(2)}) collective-permute-start(f32[64,128]{1,0:T(8,128)S(1)} %get-tuple-element.73), channel_id=1, source_target_pairs={{0,1},{1,0},{2,3},{3,2},{4,5},{5,4},{6,7},{7,6},{8,9},{9,8},{10,11... | collective-permute-start | bytes 98312 | tf_op jit(solution)/shard_map/ppermute | solution.py:215
  26.5 2.0 %shard_map.80.refs_0_ = f32[8192,128]{1,0:T(8,128)S(1)} custom-call(bf16[8192,128]{1,0:T(8,128)(2,1)S(1)} %bitcast.7, bf16[8192,128]{1,0:T(8,128)(2,1)S(1)} %bitcast.8, f32[128,128]{1,0:T(8,128)S(1)} %get-tuple-element.45.refs_2_.refs_1_, bf16[128,176]{1,0:T(8,128)(2,1)S(1)} %get-tuple-element.46.refs_3_.refs_2_, ...), custom_call_target="tpu_custom_call" | custom-call | flops 805306368 | bytes 8388608 | tf_op jit(solution)/shard_map/pallas_call | solution.py:527
  28.5 2.0 %collective-permute-done.10.refs_12_ = f32[64,128]{1,0:T(8,128)S(1)} collective-permute-done((f32[64,128]{1,0:T(8,128)S(1)}, f32[64,128]{1,0:T(8,128)S(1)}, u32[]{:S(2)}, u32[]{:S(2)}) %collective-permute-start.10) | collective-permute-done | bytes 32800 | tf_op jit(solution)/shard_map/ppermute | solution.py:215
  30.5 3.5 %shard_map.82 = (bf16[8192,128]{1,0:T(8,128)(2,1)S(1)}, bf16[1024,128]{1,0:T(8,128)(2,1)S(1)}, bf16[1024,128]{1,0:T(8,128)(2,1)S(1)}, bf16[1024,128]{1,0:T(8,128...) custom-call(f32[8192,128]{1,0:T(8,128)S(1)} %shard_map.80.refs_0_, ...), custom_call_target="tpu_custom_call" | custom-call | flops 536870912 | bytes 8388608 | tf_op jit(solution)/shard_map/pallas_call | solution.py:664
  34.0 1.5 %collective-permute-start.12 = (bf16[1024,128]{1,0:T(8,128)(2,1)S(1)}, bf16[1024,128]{1,0:T(8,128)(2,1)S(1)}, u32[]{:S(2)}, u32[]{:S(2)}) collective-permute-start(bf16[1024,128]{1,0:T(8,128)(2,1)S(1)} %get-tuple-element.77), channel_id=1, source_target_pairs={{0,4},{1,5},{2,6},{3,7},{4,0},{5,1},{6,2},{7,3},{8,12},{9,13},{10,... | collective-permute-start | bytes 786440 | tf_op jit(solution)/shard_map/ppermute | solution.py:257
  35.6 1.5 %collective-permute-start.14 = (bf16[1024,128]{1,0:T(8,128)(2,1)S(1)}, bf16[1024,128]{1,0:T(8,128)(2,1)S(1)}, u32[]{:S(2)}, u32[]{:S(2)}) collective-permute-start(bf16[1024,128]{1,0:T(8,128)(2,1)S(1)} %get-tuple-element.79), channel_id=1, source_target_pairs={{0,8},{1,9},{2,10},{3,11},{4,12},{5,13},{6,14},{7,15},{8,0},{9,1},... | collective-permute-start | bytes 786440 | tf_op jit(solution)/shard_map/ppermute | solution.py:257
  37.5 2.0 %shard_map.83 = (f32[8192,128]{1,0:T(8,128)S(1)}, bf16[8192,128]{1,0:T(8,128)(2,1)S(1)}) custom-call(bf16[8192,128]{1,0:T(8,128)(2,1)S(1)} %get-tuple-element.74.refs_0_, bf16[8192,128]{1,0:T(8,128)(2,1)S(1)} %bitcast.9, f32[128,128]{1,0:T(8,128)S(1)} %get-tuple-element.45.refs_2_.refs_1_, bf16[128,176]{1,0:T(8,128)(2,1)S(1)} %get-tuple-element.46.refs_3_.refs_2_, ...), custom_call_target="tpu_custom_call" | custom-call | flops 805306368 | bytes 8388608 | tf_op jit(solution)/shard_map/pallas_call | solution.py:527
  39.6 1.5 %collective-permute-done.16.refs_10_ = bf16[128,128]{1,0:T(8,128)(2,1)S(1)} collective-permute-done((bf16[128,128]{1,0:T(8,128)(2,1)S(1)}, bf16[128,128]{1,0:T(8,128)(2,1)S(1)}, u32[]{:S(2)}, u32[]{:S(2)}) %collective-permute-start.16) | collective-permute-done | bytes 32800 | tf_op jit(solution)/shard_map/ppermute | solution.py:257
  41.0 0.4 collective-permute-done.12.refs_6_
  41.5 2.6 %collective-permute-done.13.refs_7_ = bf16[1024,128]{1,0:T(8,128)(2,1)S(1)} collective-permute-done((bf16[1024,128]{1,0:T(8,128)(2,1)S(1)}, bf16[1024,128]{1,0:T(8,128)(2,1)S(1)}, u32[]{:S(2)}, u32[]{:S(2)}) %collective-permute-start.13) | collective-permute-done | bytes 262176 | tf_op jit(solution)/shard_map/ppermute | solution.py:257
  44.0 3.0 %shard_map.84 = (bf16[8192,128]{1,0:T(8,128)(2,1)S(1)}, bf16[1024,128]{1,0:T(8,128)(2,1)S(1)}, bf16[1024,128]{1,0:T(8,128)(2,1)S(1)}, bf16[1024,128]{1,0:T(8,128)(2,1)S(1)}, bf16[128,128]{1,0:T(8,128)(2,1)S(1)}) custom-call(f32[8192,128]{1,0:T(8,128)S(1)} %get-tuple-element.76.refs_0_, f32[128,128]{1,0:T(8,128)S(1)} %get-tuple-element.45.refs_2_.refs_1_, ...), custom_call_target="tpu_custom_call" | custom-call | flops 536870912 | bytes 8388608 | tf_op jit(solution)/shard_map/pallas_call | solution.py:664
  47.0 0.6 collective-permute-start.17
  47.6 0.8 %collective-permute-start.19 = (bf16[1024,128]{1,0:T(8,128)(2,1)S(1)}, bf16[1024,128]{1,0:T(8,128)(2,1)S(1)}, u32[]{:S(2)}, u32[]{:S(2)}) collective-permute-start(bf16[1024,128]{1,0:T(8,128)(2,1)S(1)} %get-tuple-element.85), channel_id=1, source_target_pairs={{0,8},{1,9},{2,10},{3,11},{4,12},{5,13},{6,14},{7,15},{8,0},{9,1},... | collective-permute-start | bytes 786440 | tf_op jit(solution)/shard_map/ppermute | solution.py:257
  48.4 0.5 collective-permute-start.21
  48.9 1.5 %shard_map.85.refs_0_ = f32[8192,128]{1,0:T(8,128)S(1)} custom-call(bf16[8192,128]{1,0:T(8,128)(2,1)S(1)} %get-tuple-element.81.refs_0_, bf16[8192,128]{1,0:T(8,128)(2,1)S(1)} %get-tuple-element.82.refs_1_, f32[128,128]{1,0:T(8,128)S(1)} %get-tuple-element.45.refs_2_.refs_1_, bf16[128,176]{1,0:T(8,128)(2,1)S(1)} %get-tuple-element.46.refs_3_.refs_2_, ...), custom_call_target="tpu_custom_call" | custom-call | flops 805306368 | bytes 8388608 | tf_op jit(solution)/shard_map/pallas_call | solution.py:527
  50.4 1.9 %collective-permute-done.21.refs_10_ = bf16[128,128]{1,0:T(8,128)(2,1)S(1)} collective-permute-done((bf16[128,128]{1,0:T(8,128)(2,1)S(1)}, bf16[128,128]{1,0:T(8,128)(2,1)S(1)}, u32[]{:S(2)}, u32[]{:S(2)}) %collective-permute-start.21) | collective-permute-done | bytes 32800 | tf_op jit(solution)/shard_map/ppermute | solution.py:257
  52.3 3.1 %collective-permute-done.17.refs_6_ = bf16[1024,128]{1,0:T(8,128)(2,1)S(1)} collective-permute-done((bf16[1024,128]{1,0:T(8,128)(2,1)S(1)}, bf16[1024,128]{1,0:T(8,128)(2,1)S(1)}, u32[]{:S(2)}, u32[]{:S(2)}) %collective-permute-start.17) | collective-permute-done | bytes 262176 | tf_op jit(solution)/shard_map/ppermute | solution.py:257
  55.4 0.8 %collective-permute-done.18.refs_7_ = bf16[1024,128]{1,0:T(8,128)(2,1)S(1)} collective-permute-done((bf16[1024,128]{1,0:T(8,128)(2,1)S(1)}, bf16[1024,128]{1,0:T(8,128)(2,1)S(1)}, u32[]{:S(2)}, u32[]{:S(2)}) %collective-permute-start.18) | collective-permute-done | bytes 262176 | tf_op jit(solution)/shard_map/ppermute | solution.py:257
  56.2 2.3 %shard_map.86 = bf16[8192,128]{1,0:T(8,128)(2,1)} custom-call(f32[8192,128]{1,0:T(8,128)S(1)} %shard_map.85.refs_0_, f32[128,128]{1,0:T(8,128)S(1)} %get-tuple-element.45.refs_2_.refs_1_, bf16[128,176]{1,0:T(8,128)(2,1)S(1)} %get-tuple-element.46.refs_3_.refs_2_, bf16[512,256]{1,0:T(8,128)(2,1)S(1)} %get-tuple-element.47.refs_4_.refs_3_, ...), custom_call_target="tpu_custom_call" | custom-call | flops 536870912 | bytes 8388608 | tf_op jit(solution)/shard_map/pallas_call | solution.py:664
  (32 shorter events, 0.7 us)
Async XLA Ops:
  0.6 8.3 %copy-start.2 = (f32[8,8,128]{2,1,0:T(8,128)S(1)}, f32[8,8,128]{2,1,0:T(8,128)}, u32[]{:S(2)}) copy-start(f32[8,8,128]{2,1,0:T(8,128)} %param.8) | copy-start | bytes 98308
  0.6 0.7 %copy-start.3 = (s32[1,1,1,1024]{3,2,1,0:T(1,128)S(1)}, s32[1,1,1,1024]{3,2,1,0:T(1,128)}, u32[]{:S(2)}) copy-start(s32[1,1,1,1024]{3,2,1,0:T(1,128)} %cell_ref.1) | copy-start | bytes 12292
  4.4 9.3 %collective-permute-start.1 = (bf16[1024,128]{1,0:T(8,128)(2,1)S(1)}, bf16[1024,128]{1,0:T(8,128)(2,1)S(1)}, u32[]{:S(2)}, u32[]{:S(2)}) collective-permute-start(bf16[1024,128]{1,0:T(8,128)(2,1)S(1)} %get-tuple-element.53.refs_0_), channel_id=1, source_target_pairs={{0,16},{8,24},{16,0},{24,8},{1,17},{9,25},{17,1},{25,9},{2,18},{10... | collective-permute-start | bytes 786440 | tf_op jit(solution)/shard_map/ppermute | solution.py:691
  7.4 8.7 %collective-permute-start = (bf16[1024,128]{1,0:T(8,128)(2,1)S(1)}, bf16[1024,128]{1,0:T(8,128)(2,1)S(1)}, u32[]{:S(2)}, u32[]{:S(2)}) collective-permute-start(bf16[1024,128]{1,0:T(8,128)(2,1)S(1)} %get-tuple-element.53.refs_0_), channel_id=1, source_target_pairs={{0,8},{8,0},{16,24},{24,16},{1,9},{9,1},{17,25},{25,17},{2,10},{10... | collective-permute-start | bytes 786440 | tf_op jit(solution)/shard_map/ppermute | solution.py:691
  7.4 8.7 %collective-permute-start.3 = (bf16[1024,128]{1,0:T(8,128)(2,1)S(1)}, bf16[1024,128]{1,0:T(8,128)(2,1)S(1)}, u32[]{:S(2)}, u32[]{:S(2)}) collective-permute-start(bf16[1024,128]{1,0:T(8,128)(2,1)S(1)} %get-tuple-element.52), channel_id=1, source_target_pairs={{0,4},{1,5},{2,6},{3,7},{4,0},{5,1},{6,2},{7,3},{8,12},{9,13},{10,... | collective-permute-start | bytes 786440 | tf_op jit(solution)/shard_map/ppermute | solution.py:257
  8.9 17.6 %copy-start.1 = (bf16[128,8,8,128]{3,2,1,0:T(8,128)(2,1)S(1)}, bf16[128,8,8,128]{3,2,1,0:T(8,128)(2,1)}, u32[]{:S(2)}) copy-start(bf16[128,8,8,128]{3,2,1,0:T(8,128)(2,1)} %param.7) | copy-start | bytes 6291460
  12.4 14.1 %copy-start = (bf16[128,8,8,128]{3,2,1,0:T(8,128)(2,1)S(1)}, bf16[128,8,8,128]{3,2,1,0:T(8,128)(2,1)}, u32[]{:S(2)}) copy-start(bf16[128,8,8,128]{3,2,1,0:T(8,128)(2,1)} %param.6) | copy-start | bytes 6291460
  13.7 2.4 %collective-permute-start.2 = (bf16[1024,128]{1,0:T(8,128)(2,1)S(1)}, bf16[1024,128]{1,0:T(8,128)(2,1)S(1)}, u32[]{:S(2)}, u32[]{:S(2)}) collective-permute-start(bf16[1024,128]{1,0:T(8,128)(2,1)S(1)} %collective-permute-done.1.refs_2_), channel_id=1, source_target_pairs={{0,8},{8,0},{16,24},{24,16},{1,9},{9,1},{17,25},{25,17},{2,10},{10... | collective-permute-start | bytes 786440 | tf_op jit(solution)/shard_map/ppermute | solution.py:691
  13.7 8.2 %collective-permute-start.6 = (bf16[1024,128]{1,0:T(8,128)(2,1)S(1)}, bf16[1024,128]{1,0:T(8,128)(2,1)S(1)}, u32[]{:S(2)}, u32[]{:S(2)}) collective-permute-start(bf16[1024,128]{1,0:T(8,128)(2,1)S(1)} %get-tuple-element.65), channel_id=1, source_target_pairs={{0,24},{1,25},{2,26},{3,27},{4,28},{5,29},{6,30},{7,31},{8,16},{9,... | collective-permute-start | bytes 786440 | tf_op jit(solution)/shard_map/ppermute | solution.py:257
  15.5 6.3 %collective-permute-start.7 = (bf16[1024,128]{1,0:T(8,128)(2,1)S(1)}, bf16[1024,128]{1,0:T(8,128)(2,1)S(1)}, u32[]{:S(2)}, u32[]{:S(2)}) collective-permute-start(bf16[1024,128]{1,0:T(8,128)(2,1)S(1)} %get-tuple-element.66), channel_id=1, source_target_pairs={{0,8},{1,9},{2,10},{3,11},{4,12},{5,13},{6,14},{7,15},{8,0},{9,1},... | collective-permute-start | bytes 786440 | tf_op jit(solution)/shard_map/ppermute | solution.py:257
  16.8 5.1 %collective-permute-start.8 = (f32[128,128]{1,0:T(8,128)S(1)}, f32[128,128]{1,0:T(8,128)S(1)}, u32[]{:S(2)}, u32[]{:S(2)}) collective-permute-start(f32[128,128]{1,0:T(8,128)S(1)} %get-tuple-element.68), channel_id=1, source_target_pairs={{0,4},{4,0},{1,5},{5,1},{2,6},{6,2},{3,7},{7,3},{8,12},{12,8},{9,1... | collective-permute-start | bytes 196616 | tf_op jit(solution)/shard_map/ppermute | solution.py:210
  18.4 8.0 %collective-permute-start.5 = (bf16[128,128]{1,0:T(8,128)(2,1)S(1)}, bf16[128,128]{1,0:T(8,128)(2,1)S(1)}, u32[]{:S(2)}, u32[]{:S(2)}) collective-permute-start(bf16[128,128]{1,0:T(8,128)(2,1)S(1)} %get-tuple-element.61), channel_id=1, source_target_pairs={{0,1},{1,0},{2,3},{3,2},{4,5},{5,4},{6,7},{7,6},{8,9},{9,8},{10,11... | collective-permute-start | bytes 98312 | tf_op jit(solution)/shard_map/ppermute | solution.py:257
  20.0 6.5 %collective-permute-start.4 = (bf16[128,128]{1,0:T(8,128)(2,1)S(1)}, bf16[128,128]{1,0:T(8,128)(2,1)S(1)}, u32[]{:S(2)}, u32[]{:S(2)}) collective-permute-start(bf16[128,128]{1,0:T(8,128)(2,1)S(1)} %get-tuple-element.61), channel_id=1, source_target_pairs={{0,8},{1,2},{2,1},{3,11},{4,12},{5,6},{6,5},{7,15},{8,0},{9,10},{1... | collective-permute-start | bytes 98312 | tf_op jit(solution)/shard_map/ppermute | solution.py:257
  22.0 6.5 %collective-permute-start.9 = (f32[64,128]{1,0:T(8,128)S(1)}, f32[64,128]{1,0:T(8,128)S(1)}, u32[]{:S(2)}, u32[]{:S(2)}) collective-permute-start(f32[64,128]{1,0:T(8,128)S(1)} %get-tuple-element.71), channel_id=1, source_target_pairs={{0,3},{1,2},{2,1},{3,0},{4,7},{5,6},{6,5},{7,4},{8,11},{9,10},{10,... | collective-permute-start | bytes 98312 | tf_op jit(solution)/shard_map/ppermute | solution.py:215
  25.7 4.8 %collective-permute-start.10 = (f32[64,128]{1,0:T(8,128)S(1)}, f32[64,128]{1,0:T(8,128)S(1)}, u32[]{:S(2)}, u32[]{:S(2)}) collective-permute-start(f32[64,128]{1,0:T(8,128)S(1)} %get-tuple-element.72), channel_id=1, source_target_pairs={{0,2},{1,3},{2,0},{3,1},{4,6},{5,7},{6,4},{7,5},{8,10},{9,11},{10,... | collective-permute-start | bytes 98312 | tf_op jit(solution)/shard_map/ppermute | solution.py:215
  25.7 4.8 %collective-permute-start.11 = (f32[64,128]{1,0:T(8,128)S(1)}, f32[64,128]{1,0:T(8,128)S(1)}, u32[]{:S(2)}, u32[]{:S(2)}) collective-permute-start(f32[64,128]{1,0:T(8,128)S(1)} %get-tuple-element.73), channel_id=1, source_target_pairs={{0,1},{1,0},{2,3},{3,2},{4,5},{5,4},{6,7},{7,6},{8,9},{9,8},{10,11... | collective-permute-start | bytes 98312 | tf_op jit(solution)/shard_map/ppermute | solution.py:215
  26.5 4.0 %copy-start.4 = (s32[1,1,1,32]{3,2,1,0:T(1,128)S(1)}, s32[1,1,1,32]{3,2,1,0:T(1,128)}, u32[]{:S(2)}) copy-start(s32[1,1,1,32]{3,2,1,0:T(1,128)} %refs_6_.1) | copy-start | bytes 388
  34.0 7.5 %collective-permute-start.12 = (bf16[1024,128]{1,0:T(8,128)(2,1)S(1)}, bf16[1024,128]{1,0:T(8,128)(2,1)S(1)}, u32[]{:S(2)}, u32[]{:S(2)}) collective-permute-start(bf16[1024,128]{1,0:T(8,128)(2,1)S(1)} %get-tuple-element.77), channel_id=1, source_target_pairs={{0,4},{1,5},{2,6},{3,7},{4,0},{5,1},{6,2},{7,3},{8,12},{9,13},{10,... | collective-permute-start | bytes 786440 | tf_op jit(solution)/shard_map/ppermute | solution.py:257
  35.5 8.6 %collective-permute-start.13 = (bf16[1024,128]{1,0:T(8,128)(2,1)S(1)}, bf16[1024,128]{1,0:T(8,128)(2,1)S(1)}, u32[]{:S(2)}, u32[]{:S(2)}) collective-permute-start(bf16[1024,128]{1,0:T(8,128)(2,1)S(1)} %get-tuple-element.78), channel_id=1, source_target_pairs={{0,24},{1,25},{2,26},{3,27},{4,28},{5,29},{6,30},{7,31},{8,16},{9,... | collective-permute-start | bytes 786440 | tf_op jit(solution)/shard_map/ppermute | solution.py:257
  35.6 8.5 %collective-permute-start.14 = (bf16[1024,128]{1,0:T(8,128)(2,1)S(1)}, bf16[1024,128]{1,0:T(8,128)(2,1)S(1)}, u32[]{:S(2)}, u32[]{:S(2)}) collective-permute-start(bf16[1024,128]{1,0:T(8,128)(2,1)S(1)} %get-tuple-element.79), channel_id=1, source_target_pairs={{0,8},{1,9},{2,10},{3,11},{4,12},{5,13},{6,14},{7,15},{8,0},{9,1},... | collective-permute-start | bytes 786440 | tf_op jit(solution)/shard_map/ppermute | solution.py:257
  37.1 3.9 %collective-permute-start.16 = (bf16[128,128]{1,0:T(8,128)(2,1)S(1)}, bf16[128,128]{1,0:T(8,128)(2,1)S(1)}, u32[]{:S(2)}, u32[]{:S(2)}) collective-permute-start(bf16[128,128]{1,0:T(8,128)(2,1)S(1)} %get-tuple-element.80), channel_id=1, source_target_pairs={{0,1},{1,0},{2,3},{3,2},{4,5},{5,4},{6,7},{7,6},{8,9},{9,8},{10,11... | collective-permute-start | bytes 98312 | tf_op jit(solution)/shard_map/ppermute | solution.py:257
  37.5 3.5 %collective-permute-start.15 = (bf16[128,128]{1,0:T(8,128)(2,1)S(1)}, bf16[128,128]{1,0:T(8,128)(2,1)S(1)}, u32[]{:S(2)}, u32[]{:S(2)}) collective-permute-start(bf16[128,128]{1,0:T(8,128)(2,1)S(1)} %get-tuple-element.80), channel_id=1, source_target_pairs={{0,8},{1,2},{2,1},{3,11},{4,12},{5,6},{6,5},{7,15},{8,0},{9,10},{1... | collective-permute-start | bytes 98312 | tf_op jit(solution)/shard_map/ppermute | solution.py:257
  47.0 8.4 %collective-permute-start.17 = (bf16[1024,128]{1,0:T(8,128)(2,1)S(1)}, bf16[1024,128]{1,0:T(8,128)(2,1)S(1)}, u32[]{:S(2)}, u32[]{:S(2)}) collective-permute-start(bf16[1024,128]{1,0:T(8,128)(2,1)S(1)} %get-tuple-element.83), channel_id=1, source_target_pairs={{0,4},{1,5},{2,6},{3,7},{4,0},{5,1},{6,2},{7,3},{8,12},{9,13},{10,... | collective-permute-start | bytes 786440 | tf_op jit(solution)/shard_map/ppermute | solution.py:257
  47.6 8.6 %collective-permute-start.18 = (bf16[1024,128]{1,0:T(8,128)(2,1)S(1)}, bf16[1024,128]{1,0:T(8,128)(2,1)S(1)}, u32[]{:S(2)}, u32[]{:S(2)}) collective-permute-start(bf16[1024,128]{1,0:T(8,128)(2,1)S(1)} %get-tuple-element.84), channel_id=1, source_target_pairs={{0,24},{1,25},{2,26},{3,27},{4,28},{5,29},{6,30},{7,31},{8,16},{9,... | collective-permute-start | bytes 786440 | tf_op jit(solution)/shard_map/ppermute | solution.py:257
  47.6 8.6 %collective-permute-start.19 = (bf16[1024,128]{1,0:T(8,128)(2,1)S(1)}, bf16[1024,128]{1,0:T(8,128)(2,1)S(1)}, u32[]{:S(2)}, u32[]{:S(2)}) collective-permute-start(bf16[1024,128]{1,0:T(8,128)(2,1)S(1)} %get-tuple-element.85), channel_id=1, source_target_pairs={{0,8},{1,9},{2,10},{3,11},{4,12},{5,13},{6,14},{7,15},{8,0},{9,1},... | collective-permute-start | bytes 786440 | tf_op jit(solution)/shard_map/ppermute | solution.py:257
  48.4 3.9 %collective-permute-start.21 = (bf16[128,128]{1,0:T(8,128)(2,1)S(1)}, bf16[128,128]{1,0:T(8,128)(2,1)S(1)}, u32[]{:S(2)}, u32[]{:S(2)}) collective-permute-start(bf16[128,128]{1,0:T(8,128)(2,1)S(1)} %get-tuple-element.86), channel_id=1, source_target_pairs={{0,1},{1,0},{2,3},{3,2},{4,5},{5,4},{6,7},{7,6},{8,9},{9,8},{10,11... | collective-permute-start | bytes 98312 | tf_op jit(solution)/shard_map/ppermute | solution.py:257
  48.9 3.4 %collective-permute-start.20 = (bf16[128,128]{1,0:T(8,128)(2,1)S(1)}, bf16[128,128]{1,0:T(8,128)(2,1)S(1)}, u32[]{:S(2)}, u32[]{:S(2)}) collective-permute-start(bf16[128,128]{1,0:T(8,128)(2,1)S(1)} %get-tuple-element.86), channel_id=1, source_target_pairs={{0,8},{1,2},{2,1},{3,11},{4,12},{5,6},{6,5},{7,15},{8,0},{9,10},{1... | collective-permute-start | bytes 98312 | tf_op jit(solution)/shard_map/ppermute | solution.py:257

commit v21 on v17

--- a/solution.py
+++ b/solution.py
@@ -211,7 +211,7 @@
         other, late = lax.optimization_barrier((other, late))
         sent = shares(mine, other)
         recv = [sent[0]]
-        for key in range(gzs - 1, 0, -1):
+        for key in range(1, gzs):
             recv.append(lax.ppermute(sent[key], "gz", [(i, i ^ key) for i in range(gzs)]))
         return recv, after
     (total,) = surface(parts, held, 1)

time: 55 us -> 56.4 us (1.025)
  waiting for transfers between devices: 10.9 us -> 12.3 us
    ppermute x3, waiting for transfers between devices: 2.01 us -> 3.42 us  [flux_sums(): lax.ppermute(sent[key], 'gz', [(i, i ^ key) for i in range(gzs)])]
  transfers between devices with their start and end apart: 22 -> 22, of which waited for: 7 -> 8; matrix products, arithmetic and copies ran while one was open for 0% -> 0% of each run, Pallas kernels for 18% -> 17%
where the time goes in v21:
time: 56.4 us; the launch traced here: 56.2 us
  Pallas kernels  21.6 us (38%)
  starting transfers between devices  20.6 us (37%)
  waiting for transfers between devices  12.3 us (22%)
  between operations  0.94 us (2%)
  local copies, waits for them, and re-layouts  0.71 us (1%)
    ppermute x15, starting transfers between devices, swap(): return lax.ppermute(value, axes, pairs)  11.5 us
    pallas_call x3, Pallas kernels, sweep_finish(): pl.pallas_call(functools.partial(finish_kernel, shape, len(ends), len(rec...  8.8 us
    ppermute x15, waiting for transfers between devices, swap(): return lax.ppermute(value, axes, pairs)  6.53 us
    pallas_call x3, Pallas kernels, sweep_base(): pl.pallas_call(functools.partial(base_kernel, shape, len(ends), phi is no...  5.53 us
    ppermute x3, starting transfers between devices, flux_sums(): lax.ppermute(sent[key], 'gz', [(i, i ^ key) for i in range(gzs)])  4.51 us
    pallas_call x1, Pallas kernels, first_faces(): pl.pallas_call(functools.partial(faces_kernel, shape, slots), in_specs=[h...  3.45 us
    ppermute x3, waiting for transfers between devices, flux_sums(): lax.ppermute(sent[key], 'gz', [(i, i ^ key) for i in range(gzs)])  3.42 us
    pallas_call x1, Pallas kernels, traces(): pl.pallas_call(functools.partial(trace_kernel, shape, stride, block), in_...  3.03 us
  transfers between devices with their start and end apart: 22, of which 8 were waited for; matrix products, arithmetic and copies ran while one was open for 0% of the time, Pallas kernels for 17%

profile of v21, /device:TPU:0, one launch (start us, length us, event | category | flops | bytes accessed | tf_op | source)
XLA Modules:
  0.0 56.2 jit_solution(1095313503028312658)
XLA Ops:
  0.6 0.7 %copy-done.3 = s32[1,1,1,1024]{3,2,1,0:T(1,128)S(1)} copy-done((s32[1,1,1,1024]{3,2,1,0:T(1,128)S(1)}, s32[1,1,1,1024]{3,2,1,0:T(1,128)}, u32[]{:S(2)}) %copy-start.3) | copy-done | bytes 4120
  1.3 3.0 %shard_map.78 = (bf16[1024,128]{1,0:T(8,128)(2,1)S(1)}, bf16[1024,128]{1,0:T(8,128)(2,1)S(1)}) custom-call(bf16[128,64,128]{2,1,0:T(8,128)(2,1)} %bitcast.5, s32[1,1,1,1024]{3,2,1,0:T(1,128)S(1)} %copy-done.3), custom_call_target="tpu_custom_call" | custom-call | flops 536870912 | bytes 2097152 | tf_op jit(solution)/shard_map/pallas_call | solution.py:106
  4.4 3.0 %collective-permute-start.1 = (bf16[1024,128]{1,0:T(8,128)(2,1)S(1)}, bf16[1024,128]{1,0:T(8,128)(2,1)S(1)}, u32[]{:S(2)}, u32[]{:S(2)}) collective-permute-start(bf16[1024,128]{1,0:T(8,128)(2,1)S(1)} %get-tuple-element.53.refs_0_), channel_id=1, source_target_pairs={{0,16},{8,24},{16,0},{24,8},{1,17},{9,25},{17,1},{25,9},{2,18},{10... | collective-permute-start | bytes 786440 | tf_op jit(solution)/shard_map/ppermute | solution.py:690
  7.4 1.5 %collective-permute-start.3 = (bf16[1024,128]{1,0:T(8,128)(2,1)S(1)}, bf16[1024,128]{1,0:T(8,128)(2,1)S(1)}, u32[]{:S(2)}, u32[]{:S(2)}) collective-permute-start(bf16[1024,128]{1,0:T(8,128)(2,1)S(1)} %get-tuple-element.52), channel_id=1, source_target_pairs={{0,4},{1,5},{2,6},{3,7},{4,0},{5,1},{6,2},{7,3},{8,12},{9,13},{10,... | collective-permute-start | bytes 786440 | tf_op jit(solution)/shard_map/ppermute | solution.py:256
  8.9 3.5 %shard_map.77 = (bf16[1024,128]{1,0:T(8,128)(2,1)S(1)}, bf16[1024,128]{1,0:T(8,128)(2,1)S(1)}, bf16[128,128]{1,0:T(8,128)(2,1)S(1)}, bf16[4,256,1024]{2,1,0:T(8,...) custom-call(bf16[8192,128]{1,0:T(8,128)(2,1)} %bitcast.6, ...), custom_call_target="tpu_custom_call" | custom-call | flops 134217728 | bytes 4194304 | tf_op jit(solution)/shard_map/pallas_call | solution.py:419
  12.4 1.3 %collective-permute-done.1.refs_2_ = bf16[1024,128]{1,0:T(8,128)(2,1)S(1)} collective-permute-done((bf16[1024,128]{1,0:T(8,128)(2,1)S(1)}, bf16[1024,128]{1,0:T(8,128)(2,1)S(1)}, u32[]{:S(2)}, u32[]{:S(2)}) %collective-permute-start.1) | collective-permute-done | bytes 262176 | tf_op jit(solution)/shard_map/ppermute | solution.py:690
  13.7 1.8 %collective-permute-start.6 = (bf16[1024,128]{1,0:T(8,128)(2,1)S(1)}, bf16[1024,128]{1,0:T(8,128)(2,1)S(1)}, u32[]{:S(2)}, u32[]{:S(2)}) collective-permute-start(bf16[1024,128]{1,0:T(8,128)(2,1)S(1)} %get-tuple-element.65), channel_id=1, source_target_pairs={{0,1},{1,0},{2,3},{3,2},{4,5},{5,4},{6,7},{7,6},{8,16},{9,17},{10,... | collective-permute-start | bytes 786440 | tf_op jit(solution)/shard_map/ppermute | solution.py:256
  15.5 0.6 collective-permute-done.3.refs_6_
  16.1 0.7 %shard_map.79 = (f32[128,128]{1,0:T(8,128)S(1)}, f32[128,128]{1,0:T(8,128)S(1)}) custom-call(bf16[1024,128]{1,0:T(8,128)(2,1)S(1)} %get-tuple-element.53.refs_0_, bf16[1024,128]{1,0:T(8,128)(2,1)S(1)} %collective-permute-done.refs_1_, bf16[1024,128]{1,0:T(8,128)(2,1)S(1)} %collective-permute-done.1.refs_2_, ...), custom_call_target="tpu_custom_call" | custom-call | flops 268435456 | bytes 2097152 | tf_op jit(solution)/shard_map/pallas_call | solution.py:160
  16.8 1.6 %collective-permute-start.8 = (f32[128,128]{1,0:T(8,128)S(1)}, f32[128,128]{1,0:T(8,128)S(1)}, u32[]{:S(2)}, u32[]{:S(2)}) collective-permute-start(f32[128,128]{1,0:T(8,128)S(1)} %get-tuple-element.68), channel_id=1, source_target_pairs={{0,4},{4,0},{1,5},{5,1},{2,6},{6,2},{3,7},{7,3},{8,12},{12,8},{9,1... | collective-permute-start | bytes 196616 | tf_op jit(solution)/shard_map/ppermute | solution.py:210
  18.4 1.6 %collective-permute-start.5 = (bf16[128,128]{1,0:T(8,128)(2,1)S(1)}, bf16[128,128]{1,0:T(8,128)(2,1)S(1)}, u32[]{:S(2)}, u32[]{:S(2)}) collective-permute-start(bf16[128,128]{1,0:T(8,128)(2,1)S(1)} %get-tuple-element.61), channel_id=1, source_target_pairs={{0,1},{1,0},{2,3},{3,2},{4,5},{5,4},{6,7},{7,6},{8,9},{9,8},{10,11... | collective-permute-start | bytes 98312 | tf_op jit(solution)/shard_map/ppermute | solution.py:256
  20.1 1.1 %collective-permute-done.8.other_ref = f32[128,128]{1,0:T(8,128)S(1)} collective-permute-done((f32[128,128]{1,0:T(8,128)S(1)}, f32[128,128]{1,0:T(8,128)S(1)}, u32[]{:S(2)}, u32[]{:S(2)}) %collective-permute-start.8) | collective-permute-done | bytes 65568 | tf_op jit(solution)/shard_map/ppermute | solution.py:210
  21.3 2.1 %collective-permute-start.9 = (f32[64,128]{1,0:T(8,128)S(1)}, f32[64,128]{1,0:T(8,128)S(1)}, u32[]{:S(2)}, u32[]{:S(2)}) collective-permute-start(f32[64,128]{1,0:T(8,128)S(1)} %get-tuple-element.71), channel_id=1, source_target_pairs={{0,1},{1,0},{2,3},{3,2},{4,5},{5,4},{6,7},{7,6},{8,9},{9,8},{10,11... | collective-permute-start | bytes 98312 | tf_op jit(solution)/shard_map/ppermute | solution.py:215
  23.3 2.2 %collective-permute-start.10 = (f32[64,128]{1,0:T(8,128)S(1)}, f32[64,128]{1,0:T(8,128)S(1)}, u32[]{:S(2)}, u32[]{:S(2)}) collective-permute-start(f32[64,128]{1,0:T(8,128)S(1)} %get-tuple-element.72), channel_id=1, source_target_pairs={{0,2},{1,3},{2,0},{3,1},{4,6},{5,7},{6,4},{7,5},{8,10},{9,11},{10,... | collective-permute-start | bytes 98312 | tf_op jit(solution)/shard_map/ppermute | solution.py:215
  25.5 0.3 collective-permute-start.11
  25.8 2.0 %shard_map.80.refs_0_ = f32[8192,128]{1,0:T(8,128)S(1)} custom-call(bf16[8192,128]{1,0:T(8,128)(2,1)S(1)} %bitcast.7, bf16[8192,128]{1,0:T(8,128)(2,1)S(1)} %bitcast.8, f32[128,128]{1,0:T(8,128)S(1)} %get-tuple-element.45.refs_2_.refs_1_, bf16[128,176]{1,0:T(8,128)(2,1)S(1)} %get-tuple-element.46.refs_3_.refs_2_, ...), custom_call_target="tpu_custom_call" | custom-call | flops 805306368 | bytes 8388608 | tf_op jit(solution)/shard_map/pallas_call | solution.py:526
  27.8 0.4 collective-permute-done.10.refs_12_
  28.1 3.1 %collective-permute-done.11.refs_13_ = f32[64,128]{1,0:T(8,128)S(1)} collective-permute-done((f32[64,128]{1,0:T(8,128)S(1)}, f32[64,128]{1,0:T(8,128)S(1)}, u32[]{:S(2)}, u32[]{:S(2)}) %collective-permute-start.11) | collective-permute-done | bytes 32800 | tf_op jit(solution)/shard_map/ppermute | solution.py:215
  31.2 3.5 %shard_map.82 = (bf16[8192,128]{1,0:T(8,128)(2,1)S(1)}, bf16[1024,128]{1,0:T(8,128)(2,1)S(1)}, bf16[1024,128]{1,0:T(8,128)(2,1)S(1)}, bf16[1024,128]{1,0:T(8,128...) custom-call(f32[8192,128]{1,0:T(8,128)S(1)} %shard_map.80.refs_0_, ...), custom_call_target="tpu_custom_call" | custom-call | flops 536870912 | bytes 8388608 | tf_op jit(solution)/shard_map/pallas_call | solution.py:663
  34.7 1.5 %collective-permute-start.12 = (bf16[1024,128]{1,0:T(8,128)(2,1)S(1)}, bf16[1024,128]{1,0:T(8,128)(2,1)S(1)}, u32[]{:S(2)}, u32[]{:S(2)}) collective-permute-start(bf16[1024,128]{1,0:T(8,128)(2,1)S(1)} %get-tuple-element.77), channel_id=1, source_target_pairs={{0,4},{1,5},{2,6},{3,7},{4,0},{5,1},{6,2},{7,3},{8,12},{9,13},{10,... | collective-permute-start | bytes 786440 | tf_op jit(solution)/shard_map/ppermute | solution.py:256
  36.2 1.0 %collective-permute-start.14 = (bf16[1024,128]{1,0:T(8,128)(2,1)S(1)}, bf16[1024,128]{1,0:T(8,128)(2,1)S(1)}, u32[]{:S(2)}, u32[]{:S(2)}) collective-permute-start(bf16[1024,128]{1,0:T(8,128)(2,1)S(1)} %get-tuple-element.79), channel_id=1, source_target_pairs={{0,8},{1,9},{2,10},{3,11},{4,12},{5,13},{6,14},{7,15},{8,0},{9,1},... | collective-permute-start | bytes 786440 | tf_op jit(solution)/shard_map/ppermute | solution.py:256
  37.2 1.1 %collective-permute-start.16 = (bf16[128,128]{1,0:T(8,128)(2,1)S(1)}, bf16[128,128]{1,0:T(8,128)(2,1)S(1)}, u32[]{:S(2)}, u32[]{:S(2)}) collective-permute-start(bf16[128,128]{1,0:T(8,128)(2,1)S(1)} %get-tuple-element.80), channel_id=1, source_target_pairs={{0,1},{1,0},{2,3},{3,2},{4,5},{5,4},{6,7},{7,6},{8,9},{9,8},{10,11... | collective-permute-start | bytes 98312 | tf_op jit(solution)/shard_map/ppermute | solution.py:256
  38.2 0.2 collective-permute-start.15
  38.5 2.0 %shard_map.83 = (f32[8192,128]{1,0:T(8,128)S(1)}, bf16[8192,128]{1,0:T(8,128)(2,1)S(1)}) custom-call(bf16[8192,128]{1,0:T(8,128)(2,1)S(1)} %get-tuple-element.74.refs_0_, bf16[8192,128]{1,0:T(8,128)(2,1)S(1)} %bitcast.9, f32[128,128]{1,0:T(8,128)S(1)} %get-tuple-element.45.refs_2_.refs_1_, bf16[128,176]{1,0:T(8,128)(2,1)S(1)} %get-tuple-element.46.refs_3_.refs_2_, ...), custom_call_target="tpu_custom_call" | custom-call | flops 805306368 | bytes 8388608 | tf_op jit(solution)/shard_map/pallas_call | solution.py:526
  40.5 2.8 %collective-permute-done.16.refs_10_ = bf16[128,128]{1,0:T(8,128)(2,1)S(1)} collective-permute-done((bf16[128,128]{1,0:T(8,128)(2,1)S(1)}, bf16[128,128]{1,0:T(8,128)(2,1)S(1)}, u32[]{:S(2)}, u32[]{:S(2)}) %collective-permute-start.16) | collective-permute-done | bytes 32800 | tf_op jit(solution)/shard_map/ppermute | solution.py:256
  43.3 3.0 %shard_map.84 = (bf16[8192,128]{1,0:T(8,128)(2,1)S(1)}, bf16[1024,128]{1,0:T(8,128)(2,1)S(1)}, bf16[1024,128]{1,0:T(8,128)(2,1)S(1)}, bf16[1024,128]{1,0:T(8,128)(2,1)S(1)}, bf16[128,128]{1,0:T(8,128)(2,1)S(1)}) custom-call(f32[8192,128]{1,0:T(8,128)S(1)} %get-tuple-element.76.refs_0_, f32[128,128]{1,0:T(8,128)S(1)} %get-tuple-element.45.refs_2_.refs_1_, ...), custom_call_target="tpu_custom_call" | custom-call | flops 536870912 | bytes 8388608 | tf_op jit(solution)/shard_map/pallas_call | solution.py:663
  46.3 0.5 collective-permute-start.17
  46.8 2.0 %collective-permute-start.21 = (bf16[128,128]{1,0:T(8,128)(2,1)S(1)}, bf16[128,128]{1,0:T(8,128)(2,1)S(1)}, u32[]{:S(2)}, u32[]{:S(2)}) collective-permute-start(bf16[128,128]{1,0:T(8,128)(2,1)S(1)} %get-tuple-element.86), channel_id=1, source_target_pairs={{0,1},{1,0},{2,3},{3,2},{4,5},{5,4},{6,7},{7,6},{8,9},{9,8},{10,11... | collective-permute-start | bytes 98312 | tf_op jit(solution)/shard_map/ppermute | solution.py:256
  48.9 0.2 collective-permute-start.20
  49.1 1.5 %shard_map.85.refs_0_ = f32[8192,128]{1,0:T(8,128)S(1)} custom-call(bf16[8192,128]{1,0:T(8,128)(2,1)S(1)} %get-tuple-element.81.refs_0_, bf16[8192,128]{1,0:T(8,128)(2,1)S(1)} %get-tuple-element.82.refs_1_, f32[128,128]{1,0:T(8,128)S(1)} %get-tuple-element.45.refs_2_.refs_1_, bf16[128,176]{1,0:T(8,128)(2,1)S(1)} %get-tuple-element.46.refs_3_.refs_2_, ...), custom_call_target="tpu_custom_call" | custom-call | flops 805306368 | bytes 8388608 | tf_op jit(solution)/shard_map/pallas_call | solution.py:526
  50.6 3.1 %collective-permute-done.21.refs_10_ = bf16[128,128]{1,0:T(8,128)(2,1)S(1)} collective-permute-done((bf16[128,128]{1,0:T(8,128)(2,1)S(1)}, bf16[128,128]{1,0:T(8,128)(2,1)S(1)}, u32[]{:S(2)}, u32[]{:S(2)}) %collective-permute-start.21) | collective-permute-done | bytes 32800 | tf_op jit(solution)/shard_map/ppermute | solution.py:256
  53.8 2.3 %shard_map.86 = bf16[8192,128]{1,0:T(8,128)(2,1)} custom-call(f32[8192,128]{1,0:T(8,128)S(1)} %shard_map.85.refs_0_, f32[128,128]{1,0:T(8,128)S(1)} %get-tuple-element.45.refs_2_.refs_1_, bf16[128,176]{1,0:T(8,128)(2,1)S(1)} %get-tuple-element.46.refs_3_.refs_2_, bf16[512,256]{1,0:T(8,128)(2,1)S(1)} %get-tuple-element.47.refs_4_.refs_3_, ...), custom_call_target="tpu_custom_call" | custom-call | flops 536870912 | bytes 8388608 | tf_op jit(solution)/shard_map/pallas_call | solution.py:663
  (32 shorter events, 0.3 us)
Async XLA Ops:
  0.6 8.3 %copy-start.2 = (f32[8,8,128]{2,1,0:T(8,128)S(1)}, f32[8,8,128]{2,1,0:T(8,128)}, u32[]{:S(2)}) copy-start(f32[8,8,128]{2,1,0:T(8,128)} %param.8) | copy-start | bytes 98308
  0.6 0.7 %copy-start.3 = (s32[1,1,1,1024]{3,2,1,0:T(1,128)S(1)}, s32[1,1,1,1024]{3,2,1,0:T(1,128)}, u32[]{:S(2)}) copy-start(s32[1,1,1,1024]{3,2,1,0:T(1,128)} %cell_ref.1) | copy-start | bytes 12292
  4.4 9.3 %collective-permute-start.1 = (bf16[1024,128]{1,0:T(8,128)(2,1)S(1)}, bf16[1024,128]{1,0:T(8,128)(2,1)S(1)}, u32[]{:S(2)}, u32[]{:S(2)}) collective-permute-start(bf16[1024,128]{1,0:T(8,128)(2,1)S(1)} %get-tuple-element.53.refs_0_), channel_id=1, source_target_pairs={{0,16},{8,24},{16,0},{24,8},{1,17},{9,25},{17,1},{25,9},{2,18},{10... | collective-permute-start | bytes 786440 | tf_op jit(solution)/shard_map/ppermute | solution.py:690
  7.4 8.7 %collective-permute-start = (bf16[1024,128]{1,0:T(8,128)(2,1)S(1)}, bf16[1024,128]{1,0:T(8,128)(2,1)S(1)}, u32[]{:S(2)}, u32[]{:S(2)}) collective-permute-start(bf16[1024,128]{1,0:T(8,128)(2,1)S(1)} %get-tuple-element.53.refs_0_), channel_id=1, source_target_pairs={{0,8},{8,0},{16,24},{24,16},{1,9},{9,1},{17,25},{25,17},{2,10},{10... | collective-permute-start | bytes 786440 | tf_op jit(solution)/shard_map/ppermute | solution.py:690
  7.4 8.7 %collective-permute-start.3 = (bf16[1024,128]{1,0:T(8,128)(2,1)S(1)}, bf16[1024,128]{1,0:T(8,128)(2,1)S(1)}, u32[]{:S(2)}, u32[]{:S(2)}) collective-permute-start(bf16[1024,128]{1,0:T(8,128)(2,1)S(1)} %get-tuple-element.52), channel_id=1, source_target_pairs={{0,4},{1,5},{2,6},{3,7},{4,0},{5,1},{6,2},{7,3},{8,12},{9,13},{10,... | collective-permute-start | bytes 786440 | tf_op jit(solution)/shard_map/ppermute | solution.py:256
  8.9 16.9 %copy-start.1 = (bf16[128,8,8,128]{3,2,1,0:T(8,128)(2,1)S(1)}, bf16[128,8,8,128]{3,2,1,0:T(8,128)(2,1)}, u32[]{:S(2)}) copy-start(bf16[128,8,8,128]{3,2,1,0:T(8,128)(2,1)} %param.7) | copy-start | bytes 6291460
  12.4 13.4 %copy-start = (bf16[128,8,8,128]{3,2,1,0:T(8,128)(2,1)S(1)}, bf16[128,8,8,128]{3,2,1,0:T(8,128)(2,1)}, u32[]{:S(2)}) copy-start(bf16[128,8,8,128]{3,2,1,0:T(8,128)(2,1)} %param.6) | copy-start | bytes 6291460
  13.7 2.4 %collective-permute-start.2 = (bf16[1024,128]{1,0:T(8,128)(2,1)S(1)}, bf16[1024,128]{1,0:T(8,128)(2,1)S(1)}, u32[]{:S(2)}, u32[]{:S(2)}) collective-permute-start(bf16[1024,128]{1,0:T(8,128)(2,1)S(1)} %collective-permute-done.1.refs_2_), channel_id=1, source_target_pairs={{0,8},{8,0},{16,24},{24,16},{1,9},{9,1},{17,25},{25,17},{2,10},{10... | collective-permute-start | bytes 786440 | tf_op jit(solution)/shard_map/ppermute | solution.py:690
  13.7 6.4 %collective-permute-start.6 = (bf16[1024,128]{1,0:T(8,128)(2,1)S(1)}, bf16[1024,128]{1,0:T(8,128)(2,1)S(1)}, u32[]{:S(2)}, u32[]{:S(2)}) collective-permute-start(bf16[1024,128]{1,0:T(8,128)(2,1)S(1)} %get-tuple-element.65), channel_id=1, source_target_pairs={{0,1},{1,0},{2,3},{3,2},{4,5},{5,4},{6,7},{7,6},{8,16},{9,17},{10,... | collective-permute-start | bytes 786440 | tf_op jit(solution)/shard_map/ppermute | solution.py:256
  15.5 4.5 %collective-permute-start.7 = (bf16[1024,128]{1,0:T(8,128)(2,1)S(1)}, bf16[1024,128]{1,0:T(8,128)(2,1)S(1)}, u32[]{:S(2)}, u32[]{:S(2)}) collective-permute-start(bf16[1024,128]{1,0:T(8,128)(2,1)S(1)} %get-tuple-element.66), channel_id=1, source_target_pairs={{0,8},{1,9},{2,10},{3,11},{4,12},{5,13},{6,14},{7,15},{8,0},{9,1},... | collective-permute-start | bytes 786440 | tf_op jit(solution)/shard_map/ppermute | solution.py:256
  16.8 4.3 %collective-permute-start.8 = (f32[128,128]{1,0:T(8,128)S(1)}, f32[128,128]{1,0:T(8,128)S(1)}, u32[]{:S(2)}, u32[]{:S(2)}) collective-permute-start(f32[128,128]{1,0:T(8,128)S(1)} %get-tuple-element.68), channel_id=1, source_target_pairs={{0,4},{4,0},{1,5},{5,1},{2,6},{6,2},{3,7},{7,3},{8,12},{12,8},{9,1... | collective-permute-start | bytes 196616 | tf_op jit(solution)/shard_map/ppermute | solution.py:210
  18.4 7.4 %collective-permute-start.5 = (bf16[128,128]{1,0:T(8,128)(2,1)S(1)}, bf16[128,128]{1,0:T(8,128)(2,1)S(1)}, u32[]{:S(2)}, u32[]{:S(2)}) collective-permute-start(bf16[128,128]{1,0:T(8,128)(2,1)S(1)} %get-tuple-element.61), channel_id=1, source_target_pairs={{0,1},{1,0},{2,3},{3,2},{4,5},{5,4},{6,7},{7,6},{8,9},{9,8},{10,11... | collective-permute-start | bytes 98312 | tf_op jit(solution)/shard_map/ppermute | solution.py:256
  20.0 5.8 %collective-permute-start.4 = (bf16[128,128]{1,0:T(8,128)(2,1)S(1)}, bf16[128,128]{1,0:T(8,128)(2,1)S(1)}, u32[]{:S(2)}, u32[]{:S(2)}) collective-permute-start(bf16[128,128]{1,0:T(8,128)(2,1)S(1)} %get-tuple-element.61), channel_id=1, source_target_pairs={{0,8},{1,2},{2,1},{3,11},{4,12},{5,6},{6,5},{7,15},{8,0},{9,10},{1... | collective-permute-start | bytes 98312 | tf_op jit(solution)/shard_map/ppermute | solution.py:256
  21.3 6.5 %collective-permute-start.9 = (f32[64,128]{1,0:T(8,128)S(1)}, f32[64,128]{1,0:T(8,128)S(1)}, u32[]{:S(2)}, u32[]{:S(2)}) collective-permute-start(f32[64,128]{1,0:T(8,128)S(1)} %get-tuple-element.71), channel_id=1, source_target_pairs={{0,1},{1,0},{2,3},{3,2},{4,5},{5,4},{6,7},{7,6},{8,9},{9,8},{10,11... | collective-permute-start | bytes 98312 | tf_op jit(solution)/shard_map/ppermute | solution.py:215
  23.3 4.8 %collective-permute-start.10 = (f32[64,128]{1,0:T(8,128)S(1)}, f32[64,128]{1,0:T(8,128)S(1)}, u32[]{:S(2)}, u32[]{:S(2)}) collective-permute-start(f32[64,128]{1,0:T(8,128)S(1)} %get-tuple-element.72), channel_id=1, source_target_pairs={{0,2},{1,3},{2,0},{3,1},{4,6},{5,7},{6,4},{7,5},{8,10},{9,11},{10,... | collective-permute-start | bytes 98312 | tf_op jit(solution)/shard_map/ppermute | solution.py:215
  25.5 5.7 %collective-permute-start.11 = (f32[64,128]{1,0:T(8,128)S(1)}, f32[64,128]{1,0:T(8,128)S(1)}, u32[]{:S(2)}, u32[]{:S(2)}) collective-permute-start(f32[64,128]{1,0:T(8,128)S(1)} %get-tuple-element.73), channel_id=1, source_target_pairs={{0,3},{1,2},{2,1},{3,0},{4,7},{5,6},{6,5},{7,4},{8,11},{9,10},{10,... | collective-permute-start | bytes 98312 | tf_op jit(solution)/shard_map/ppermute | solution.py:215
  25.8 5.4 %copy-start.4 = (s32[1,1,1,32]{3,2,1,0:T(1,128)S(1)}, s32[1,1,1,32]{3,2,1,0:T(1,128)}, u32[]{:S(2)}) copy-start(s32[1,1,1,32]{3,2,1,0:T(1,128)} %refs_6_.1) | copy-start | bytes 388
  34.7 8.6 %collective-permute-start.12 = (bf16[1024,128]{1,0:T(8,128)(2,1)S(1)}, bf16[1024,128]{1,0:T(8,128)(2,1)S(1)}, u32[]{:S(2)}, u32[]{:S(2)}) collective-permute-start(bf16[1024,128]{1,0:T(8,128)(2,1)S(1)} %get-tuple-element.77), channel_id=1, source_target_pairs={{0,4},{1,5},{2,6},{3,7},{4,0},{5,1},{6,2},{7,3},{8,12},{9,13},{10,... | collective-permute-start | bytes 786440 | tf_op jit(solution)/shard_map/ppermute | solution.py:256
  36.2 7.1 %collective-permute-start.13 = (bf16[1024,128]{1,0:T(8,128)(2,1)S(1)}, bf16[1024,128]{1,0:T(8,128)(2,1)S(1)}, u32[]{:S(2)}, u32[]{:S(2)}) collective-permute-start(bf16[1024,128]{1,0:T(8,128)(2,1)S(1)} %get-tuple-element.78), channel_id=1, source_target_pairs={{0,1},{1,0},{2,3},{3,2},{4,5},{5,4},{6,7},{7,6},{8,16},{9,17},{10,... | collective-permute-start | bytes 786440 | tf_op jit(solution)/shard_map/ppermute | solution.py:256
  36.2 7.1 %collective-permute-start.14 = (bf16[1024,128]{1,0:T(8,128)(2,1)S(1)}, bf16[1024,128]{1,0:T(8,128)(2,1)S(1)}, u32[]{:S(2)}, u32[]{:S(2)}) collective-permute-start(bf16[1024,128]{1,0:T(8,128)(2,1)S(1)} %get-tuple-element.79), channel_id=1, source_target_pairs={{0,8},{1,9},{2,10},{3,11},{4,12},{5,13},{6,14},{7,15},{8,0},{9,1},... | collective-permute-start | bytes 786440 | tf_op jit(solution)/shard_map/ppermute | solution.py:256
  37.2 6.1 %collective-permute-start.16 = (bf16[128,128]{1,0:T(8,128)(2,1)S(1)}, bf16[128,128]{1,0:T(8,128)(2,1)S(1)}, u32[]{:S(2)}, u32[]{:S(2)}) collective-permute-start(bf16[128,128]{1,0:T(8,128)(2,1)S(1)} %get-tuple-element.80), channel_id=1, source_target_pairs={{0,1},{1,0},{2,3},{3,2},{4,5},{5,4},{6,7},{7,6},{8,9},{9,8},{10,11... | collective-permute-start | bytes 98312 | tf_op jit(solution)/shard_map/ppermute | solution.py:256
  38.2 5.0 %collective-permute-start.15 = (bf16[128,128]{1,0:T(8,128)(2,1)S(1)}, bf16[128,128]{1,0:T(8,128)(2,1)S(1)}, u32[]{:S(2)}, u32[]{:S(2)}) collective-permute-start(bf16[128,128]{1,0:T(8,128)(2,1)S(1)} %get-tuple-element.80), channel_id=1, source_target_pairs={{0,8},{1,2},{2,1},{3,11},{4,12},{5,6},{6,5},{7,15},{8,0},{9,10},{1... | collective-permute-start | bytes 98312 | tf_op jit(solution)/shard_map/ppermute | solution.py:256
  46.3 7.4 %collective-permute-start.17 = (bf16[1024,128]{1,0:T(8,128)(2,1)S(1)}, bf16[1024,128]{1,0:T(8,128)(2,1)S(1)}, u32[]{:S(2)}, u32[]{:S(2)}) collective-permute-start(bf16[1024,128]{1,0:T(8,128)(2,1)S(1)} %get-tuple-element.83), channel_id=1, source_target_pairs={{0,4},{1,5},{2,6},{3,7},{4,0},{5,1},{6,2},{7,3},{8,12},{9,13},{10,... | collective-permute-start | bytes 786440 | tf_op jit(solution)/shard_map/ppermute | solution.py:256
  46.8 6.9 %collective-permute-start.18 = (bf16[1024,128]{1,0:T(8,128)(2,1)S(1)}, bf16[1024,128]{1,0:T(8,128)(2,1)S(1)}, u32[]{:S(2)}, u32[]{:S(2)}) collective-permute-start(bf16[1024,128]{1,0:T(8,128)(2,1)S(1)} %get-tuple-element.84), channel_id=1, source_target_pairs={{0,1},{1,0},{2,3},{3,2},{4,5},{5,4},{6,7},{7,6},{8,16},{9,17},{10,... | collective-permute-start | bytes 786440 | tf_op jit(solution)/shard_map/ppermute | solution.py:256
  46.8 6.9 %collective-permute-start.19 = (bf16[1024,128]{1,0:T(8,128)(2,1)S(1)}, bf16[1024,128]{1,0:T(8,128)(2,1)S(1)}, u32[]{:S(2)}, u32[]{:S(2)}) collective-permute-start(bf16[1024,128]{1,0:T(8,128)(2,1)S(1)} %get-tuple-element.85), channel_id=1, source_target_pairs={{0,8},{1,9},{2,10},{3,11},{4,12},{5,13},{6,14},{7,15},{8,0},{9,1},... | collective-permute-start | bytes 786440 | tf_op jit(solution)/shard_map/ppermute | solution.py:256
  46.8 6.9 %collective-permute-start.21 = (bf16[128,128]{1,0:T(8,128)(2,1)S(1)}, bf16[128,128]{1,0:T(8,128)(2,1)S(1)}, u32[]{:S(2)}, u32[]{:S(2)}) collective-permute-start(bf16[128,128]{1,0:T(8,128)(2,1)S(1)} %get-tuple-element.86), channel_id=1, source_target_pairs={{0,1},{1,0},{2,3},{3,2},{4,5},{5,4},{6,7},{7,6},{8,9},{9,8},{10,11... | collective-permute-start | bytes 98312 | tf_op jit(solution)/shard_map/ppermute | solution.py:256
  48.9 4.9 %collective-permute-start.20 = (bf16[128,128]{1,0:T(8,128)(2,1)S(1)}, bf16[128,128]{1,0:T(8,128)(2,1)S(1)}, u32[]{:S(2)}, u32[]{:S(2)}) collective-permute-start(bf16[128,128]{1,0:T(8,128)(2,1)S(1)} %get-tuple-element.86), channel_id=1, source_target_pairs={{0,8},{1,2},{2,1},{3,11},{4,12},{5,6},{6,5},{7,15},{8,0},{9,10},{1... | collective-permute-start | bytes 98312 | tf_op jit(solution)/shard_map/ppermute | solution.py:256

commit v22 on v17

--- a/solution.py
+++ b/solution.py
@@ -262,7 +262,7 @@
         self.cells = first * second
         self.chunk = max(1, 128 // self.cells)
         self.rows = self.chunk * self.cells
-        self.block = min(sides, 32)
+        self.block = min(sides, 16)
         self.half = self.block // 2
         self.half_rows = self.half * self.cells
         self.outer = [("col", i) for i in range(turns("col"))]

time: 55 us -> 55.1 us (level)
  Pallas kernels: 21.6 us -> 22.9 us
  waiting for transfers between devices: 10.9 us -> 9.83 us
    ppermute x3, waiting for transfers between devices: 1.31 us -> 0.28 us  [row_gather(): lax.ppermute(held[key], 'row', pairs)]
    pallas_call x1, Pallas kernels: 3.45 us -> 4.48 us  [first_faces(): pl.pallas_call(functools.partial(faces_kernel, shape, slots), in_specs=[h...]
  transfers between devices with their start and end apart: 22 -> 22, of which waited for: 7 -> 7; matrix products, arithmetic and copies ran while one was open for 0% -> 0% of each run, Pallas kernels for 18% -> 20%
where the time goes in v22:
time: 55.1 us; the launch traced here: 54.9 us
  Pallas kernels  22.9 us (42%)
  starting transfers between devices  20.5 us (37%)
  waiting for transfers between devices  9.83 us (18%)
  between operations  0.94 us (2%)
  local copies, waits for them, and re-layouts  0.71 us (1%)
    ppermute x15, starting transfers between devices, swap(): return lax.ppermute(value, axes, pairs)  11.5 us
    pallas_call x3, Pallas kernels, sweep_finish(): pl.pallas_call(functools.partial(finish_kernel, shape, len(ends), len(rec...  8.94 us
    ppermute x15, waiting for transfers between devices, swap(): return lax.ppermute(value, axes, pairs)  6.5 us
    pallas_call x3, Pallas kernels, sweep_base(): pl.pallas_call(functools.partial(base_kernel, shape, len(ends), phi is no...  5.61 us
    pallas_call x1, Pallas kernels, first_faces(): pl.pallas_call(functools.partial(faces_kernel, shape, slots), in_specs=[h...  4.48 us
    ppermute x3, starting transfers between devices, flux_sums(): lax.ppermute(sent[key], 'gz', [(i, i ^ key) for i in range(gzs)])  4.45 us
    pallas_call x1, Pallas kernels, traces(): pl.pallas_call(functools.partial(trace_kernel, shape, stride, block), in_...  3.03 us
    ppermute x3, starting transfers between devices, row_gather(): lax.ppermute(held[key], 'row', pairs)  3.03 us
  transfers between devices with their start and end apart: 22, of which 7 were waited for; matrix products, arithmetic and copies ran while one was open for 0% of the time, Pallas kernels for 20%

profile of v22, /device:TPU:0, one launch (start us, length us, event | category | flops | bytes accessed | tf_op | source)
XLA Modules:
  0.0 54.9 jit_solution(9388351017002438814)
XLA Ops:
  0.6 0.7 %copy-done.3 = s32[1,1,1,1024]{3,2,1,0:T(1,128)S(1)} copy-done((s32[1,1,1,1024]{3,2,1,0:T(1,128)S(1)}, s32[1,1,1,1024]{3,2,1,0:T(1,128)}, u32[]{:S(2)}) %copy-start.3) | copy-done | bytes 4120
  1.3 3.0 %shard_map.78 = (bf16[1024,128]{1,0:T(8,128)(2,1)S(1)}, bf16[1024,128]{1,0:T(8,128)(2,1)S(1)}) custom-call(bf16[128,64,128]{2,1,0:T(8,128)(2,1)} %bitcast.5, s32[1,1,1,1024]{3,2,1,0:T(1,128)S(1)} %copy-done.3), custom_call_target="tpu_custom_call" | custom-call | flops 536870912 | bytes 2097152 | tf_op jit(solution)/shard_map/pallas_call | solution.py:106
  4.4 3.0 %collective-permute-start.1 = (bf16[1024,128]{1,0:T(8,128)(2,1)S(1)}, bf16[1024,128]{1,0:T(8,128)(2,1)S(1)}, u32[]{:S(2)}, u32[]{:S(2)}) collective-permute-start(bf16[1024,128]{1,0:T(8,128)(2,1)S(1)} %get-tuple-element.53.refs_0_), channel_id=1, source_target_pairs={{0,16},{8,24},{16,0},{24,8},{1,17},{9,25},{17,1},{25,9},{2,18},{10... | collective-permute-start | bytes 786440 | tf_op jit(solution)/shard_map/ppermute | solution.py:690
  7.4 1.5 %collective-permute-start.3 = (bf16[1024,128]{1,0:T(8,128)(2,1)S(1)}, bf16[1024,128]{1,0:T(8,128)(2,1)S(1)}, u32[]{:S(2)}, u32[]{:S(2)}) collective-permute-start(bf16[1024,128]{1,0:T(8,128)(2,1)S(1)} %get-tuple-element.52), channel_id=1, source_target_pairs={{0,4},{1,5},{2,6},{3,7},{4,0},{5,1},{6,2},{7,3},{8,12},{9,13},{10,... | collective-permute-start | bytes 786440 | tf_op jit(solution)/shard_map/ppermute | solution.py:256
  8.9 4.5 %shard_map.77 = (bf16[1024,128]{1,0:T(8,128)(2,1)S(1)}, bf16[1024,128]{1,0:T(8,128)(2,1)S(1)}, bf16[128,128]{1,0:T(8,128)(2,1)S(1)}, bf16[4,256,1024]{2,1,0:T(8,...) custom-call(bf16[8192,128]{1,0:T(8,128)(2,1)} %bitcast.6, ...), custom_call_target="tpu_custom_call" | custom-call | flops 134217728 | bytes 4194304 | tf_op jit(solution)/shard_map/pallas_call | solution.py:419
  13.4 0.3 collective-permute-done.1.refs_2_
  13.7 1.8 %collective-permute-start.6 = (bf16[1024,128]{1,0:T(8,128)(2,1)S(1)}, bf16[1024,128]{1,0:T(8,128)(2,1)S(1)}, u32[]{:S(2)}, u32[]{:S(2)}) collective-permute-start(bf16[1024,128]{1,0:T(8,128)(2,1)S(1)} %get-tuple-element.65), channel_id=1, source_target_pairs={{0,1},{1,0},{2,3},{3,2},{4,5},{5,4},{6,7},{7,6},{8,16},{9,17},{10,... | collective-permute-start | bytes 786440 | tf_op jit(solution)/shard_map/ppermute | solution.py:256
  15.5 0.6 %collective-permute-done.3.refs_6_ = bf16[1024,128]{1,0:T(8,128)(2,1)S(1)} collective-permute-done((bf16[1024,128]{1,0:T(8,128)(2,1)S(1)}, bf16[1024,128]{1,0:T(8,128)(2,1)S(1)}, u32[]{:S(2)}, u32[]{:S(2)}) %collective-permute-start.3) | collective-permute-done | bytes 262176 | tf_op jit(solution)/shard_map/ppermute | solution.py:256
  16.1 0.7 %shard_map.79 = (f32[128,128]{1,0:T(8,128)S(1)}, f32[128,128]{1,0:T(8,128)S(1)}) custom-call(bf16[1024,128]{1,0:T(8,128)(2,1)S(1)} %get-tuple-element.53.refs_0_, bf16[1024,128]{1,0:T(8,128)(2,1)S(1)} %collective-permute-done.refs_1_, bf16[1024,128]{1,0:T(8,128)(2,1)S(1)} %collective-permute-done.1.refs_2_, ...), custom_call_target="tpu_custom_call" | custom-call | flops 268435456 | bytes 2097152 | tf_op jit(solution)/shard_map/pallas_call | solution.py:160
  16.8 1.6 %collective-permute-start.8 = (f32[128,128]{1,0:T(8,128)S(1)}, f32[128,128]{1,0:T(8,128)S(1)}, u32[]{:S(2)}, u32[]{:S(2)}) collective-permute-start(f32[128,128]{1,0:T(8,128)S(1)} %get-tuple-element.68), channel_id=1, source_target_pairs={{0,4},{4,0},{1,5},{5,1},{2,6},{6,2},{3,7},{7,3},{8,12},{12,8},{9,1... | collective-permute-start | bytes 196616 | tf_op jit(solution)/shard_map/ppermute | solution.py:210
  18.4 1.6 %collective-permute-start.5 = (bf16[128,128]{1,0:T(8,128)(2,1)S(1)}, bf16[128,128]{1,0:T(8,128)(2,1)S(1)}, u32[]{:S(2)}, u32[]{:S(2)}) collective-permute-start(bf16[128,128]{1,0:T(8,128)(2,1)S(1)} %get-tuple-element.61), channel_id=1, source_target_pairs={{0,1},{1,0},{2,3},{3,2},{4,5},{5,4},{6,7},{7,6},{8,9},{9,8},{10,11... | collective-permute-start | bytes 98312 | tf_op jit(solution)/shard_map/ppermute | solution.py:256
  20.0 0.1 collective-permute-done.6.refs_7_
  20.1 1.1 %collective-permute-done.8.other_ref = f32[128,128]{1,0:T(8,128)S(1)} collective-permute-done((f32[128,128]{1,0:T(8,128)S(1)}, f32[128,128]{1,0:T(8,128)S(1)}, u32[]{:S(2)}, u32[]{:S(2)}) %collective-permute-start.8) | collective-permute-done | bytes 65568 | tf_op jit(solution)/shard_map/ppermute | solution.py:210
  21.2 0.1 shard_map.81
  21.3 3.7 %collective-permute-start.9 = (f32[64,128]{1,0:T(8,128)S(1)}, f32[64,128]{1,0:T(8,128)S(1)}, u32[]{:S(2)}, u32[]{:S(2)}) collective-permute-start(f32[64,128]{1,0:T(8,128)S(1)} %get-tuple-element.71), channel_id=1, source_target_pairs={{0,3},{1,2},{2,1},{3,0},{4,7},{5,6},{6,5},{7,4},{8,11},{9,10},{10,... | collective-permute-start | bytes 98312 | tf_op jit(solution)/shard_map/ppermute | solution.py:215
  24.9 0.8 %collective-permute-start.11 = (f32[64,128]{1,0:T(8,128)S(1)}, f32[64,128]{1,0:T(8,128)S(1)}, u32[]{:S(2)}, u32[]{:S(2)}) collective-permute-start(f32[64,128]{1,0:T(8,128)S(1)} %get-tuple-element.73), channel_id=1, source_target_pairs={{0,1},{1,0},{2,3},{3,2},{4,5},{5,4},{6,7},{7,6},{8,9},{9,8},{10,11... | collective-permute-start | bytes 98312 | tf_op jit(solution)/shard_map/ppermute | solution.py:215
  25.8 2.0 %shard_map.80.refs_0_ = f32[8192,128]{1,0:T(8,128)S(1)} custom-call(bf16[8192,128]{1,0:T(8,128)(2,1)S(1)} %bitcast.7, bf16[8192,128]{1,0:T(8,128)(2,1)S(1)} %bitcast.8, f32[128,128]{1,0:T(8,128)S(1)} %get-tuple-element.45.refs_2_.refs_1_, bf16[128,176]{1,0:T(8,128)(2,1)S(1)} %get-tuple-element.46.refs_3_.refs_2_, ...), custom_call_target="tpu_custom_call" | custom-call | flops 805306368 | bytes 8388608 | tf_op jit(solution)/shard_map/pallas_call | solution.py:526
  27.8 2.0 %collective-permute-done.10.refs_12_ = f32[64,128]{1,0:T(8,128)S(1)} collective-permute-done((f32[64,128]{1,0:T(8,128)S(1)}, f32[64,128]{1,0:T(8,128)S(1)}, u32[]{:S(2)}, u32[]{:S(2)}) %collective-permute-start.10) | collective-permute-done | bytes 32800 | tf_op jit(solution)/shard_map/ppermute | solution.py:215
  29.8 3.6 %shard_map.82 = (bf16[8192,128]{1,0:T(8,128)(2,1)S(1)}, bf16[1024,128]{1,0:T(8,128)(2,1)S(1)}, bf16[1024,128]{1,0:T(8,128)(2,1)S(1)}, bf16[1024,128]{1,0:T(8,128...) custom-call(f32[8192,128]{1,0:T(8,128)S(1)} %shard_map.80.refs_0_, ...), custom_call_target="tpu_custom_call" | custom-call | flops 536870912 | bytes 8388608 | tf_op jit(solution)/shard_map/pallas_call | solution.py:663
  33.4 1.5 %collective-permute-start.12 = (bf16[1024,128]{1,0:T(8,128)(2,1)S(1)}, bf16[1024,128]{1,0:T(8,128)(2,1)S(1)}, u32[]{:S(2)}, u32[]{:S(2)}) collective-permute-start(bf16[1024,128]{1,0:T(8,128)(2,1)S(1)} %get-tuple-element.77), channel_id=1, source_target_pairs={{0,4},{1,5},{2,6},{3,7},{4,0},{5,1},{6,2},{7,3},{8,12},{9,13},{10,... | collective-permute-start | bytes 786440 | tf_op jit(solution)/shard_map/ppermute | solution.py:256
  34.9 1.0 %collective-permute-start.14 = (bf16[1024,128]{1,0:T(8,128)(2,1)S(1)}, bf16[1024,128]{1,0:T(8,128)(2,1)S(1)}, u32[]{:S(2)}, u32[]{:S(2)}) collective-permute-start(bf16[1024,128]{1,0:T(8,128)(2,1)S(1)} %get-tuple-element.79), channel_id=1, source_target_pairs={{0,8},{1,9},{2,10},{3,11},{4,12},{5,13},{6,14},{7,15},{8,0},{9,1},... | collective-permute-start | bytes 786440 | tf_op jit(solution)/shard_map/ppermute | solution.py:256
  35.9 1.1 %collective-permute-start.16 = (bf16[128,128]{1,0:T(8,128)(2,1)S(1)}, bf16[128,128]{1,0:T(8,128)(2,1)S(1)}, u32[]{:S(2)}, u32[]{:S(2)}) collective-permute-start(bf16[128,128]{1,0:T(8,128)(2,1)S(1)} %get-tuple-element.80), channel_id=1, source_target_pairs={{0,1},{1,0},{2,3},{3,2},{4,5},{5,4},{6,7},{7,6},{8,9},{9,8},{10,11... | collective-permute-start | bytes 98312 | tf_op jit(solution)/shard_map/ppermute | solution.py:256
  36.9 0.2 collective-permute-start.15
  37.1 2.1 %shard_map.83 = (f32[8192,128]{1,0:T(8,128)S(1)}, bf16[8192,128]{1,0:T(8,128)(2,1)S(1)}) custom-call(bf16[8192,128]{1,0:T(8,128)(2,1)S(1)} %get-tuple-element.74.refs_0_, bf16[8192,128]{1,0:T(8,128)(2,1)S(1)} %bitcast.9, f32[128,128]{1,0:T(8,128)S(1)} %get-tuple-element.45.refs_2_.refs_1_, bf16[128,176]{1,0:T(8,128)(2,1)S(1)} %get-tuple-element.46.refs_3_.refs_2_, ...), custom_call_target="tpu_custom_call" | custom-call | flops 805306368 | bytes 8388608 | tf_op jit(solution)/shard_map/pallas_call | solution.py:526
  39.3 2.7 %collective-permute-done.16.refs_10_ = bf16[128,128]{1,0:T(8,128)(2,1)S(1)} collective-permute-done((bf16[128,128]{1,0:T(8,128)(2,1)S(1)}, bf16[128,128]{1,0:T(8,128)(2,1)S(1)}, u32[]{:S(2)}, u32[]{:S(2)}) %collective-permute-start.16) | collective-permute-done | bytes 32800 | tf_op jit(solution)/shard_map/ppermute | solution.py:256
  42.0 3.1 %shard_map.84 = (bf16[8192,128]{1,0:T(8,128)(2,1)S(1)}, bf16[1024,128]{1,0:T(8,128)(2,1)S(1)}, bf16[1024,128]{1,0:T(8,128)(2,1)S(1)}, bf16[1024,128]{1,0:T(8,128)(2,1)S(1)}, bf16[128,128]{1,0:T(8,128)(2,1)S(1)}) custom-call(f32[8192,128]{1,0:T(8,128)S(1)} %get-tuple-element.76.refs_0_, f32[128,128]{1,0:T(8,128)S(1)} %get-tuple-element.45.refs_2_.refs_1_, ...), custom_call_target="tpu_custom_call" | custom-call | flops 536870912 | bytes 8388608 | tf_op jit(solution)/shard_map/pallas_call | solution.py:663
  45.1 0.5 collective-permute-start.17
  45.6 2.0 %collective-permute-start.21 = (bf16[128,128]{1,0:T(8,128)(2,1)S(1)}, bf16[128,128]{1,0:T(8,128)(2,1)S(1)}, u32[]{:S(2)}, u32[]{:S(2)}) collective-permute-start(bf16[128,128]{1,0:T(8,128)(2,1)S(1)} %get-tuple-element.86), channel_id=1, source_target_pairs={{0,1},{1,0},{2,3},{3,2},{4,5},{5,4},{6,7},{7,6},{8,9},{9,8},{10,11... | collective-permute-start | bytes 98312 | tf_op jit(solution)/shard_map/ppermute | solution.py:256
  47.6 0.2 collective-permute-start.20
  47.9 1.5 %shard_map.85.refs_0_ = f32[8192,128]{1,0:T(8,128)S(1)} custom-call(bf16[8192,128]{1,0:T(8,128)(2,1)S(1)} %get-tuple-element.81.refs_0_, bf16[8192,128]{1,0:T(8,128)(2,1)S(1)} %get-tuple-element.82.refs_1_, f32[128,128]{1,0:T(8,128)S(1)} %get-tuple-element.45.refs_2_.refs_1_, bf16[128,176]{1,0:T(8,128)(2,1)S(1)} %get-tuple-element.46.refs_3_.refs_2_, ...), custom_call_target="tpu_custom_call" | custom-call | flops 805306368 | bytes 8388608 | tf_op jit(solution)/shard_map/pallas_call | solution.py:526
  49.4 3.1 %collective-permute-done.21.refs_10_ = bf16[128,128]{1,0:T(8,128)(2,1)S(1)} collective-permute-done((bf16[128,128]{1,0:T(8,128)(2,1)S(1)}, bf16[128,128]{1,0:T(8,128)(2,1)S(1)}, u32[]{:S(2)}, u32[]{:S(2)}) %collective-permute-start.21) | collective-permute-done | bytes 32800 | tf_op jit(solution)/shard_map/ppermute | solution.py:256
  52.5 2.2 %shard_map.86 = bf16[8192,128]{1,0:T(8,128)(2,1)} custom-call(f32[8192,128]{1,0:T(8,128)S(1)} %shard_map.85.refs_0_, f32[128,128]{1,0:T(8,128)S(1)} %get-tuple-element.45.refs_2_.refs_1_, bf16[128,176]{1,0:T(8,128)(2,1)S(1)} %get-tuple-element.46.refs_3_.refs_2_, bf16[512,256]{1,0:T(8,128)(2,1)S(1)} %get-tuple-element.47.refs_4_.refs_3_, ...), custom_call_target="tpu_custom_call" | custom-call | flops 536870912 | bytes 8388608 | tf_op jit(solution)/shard_map/pallas_call | solution.py:663
  (32 shorter events, 0.1 us)
Async XLA Ops:
  0.6 8.3 %copy-start.2 = (f32[8,8,128]{2,1,0:T(8,128)S(1)}, f32[8,8,128]{2,1,0:T(8,128)}, u32[]{:S(2)}) copy-start(f32[8,8,128]{2,1,0:T(8,128)} %param.8) | copy-start | bytes 98308
  0.6 0.7 %copy-start.3 = (s32[1,1,1,1024]{3,2,1,0:T(1,128)S(1)}, s32[1,1,1,1024]{3,2,1,0:T(1,128)}, u32[]{:S(2)}) copy-start(s32[1,1,1,1024]{3,2,1,0:T(1,128)} %cell_ref.1) | copy-start | bytes 12292
  4.4 9.3 %collective-permute-start.1 = (bf16[1024,128]{1,0:T(8,128)(2,1)S(1)}, bf16[1024,128]{1,0:T(8,128)(2,1)S(1)}, u32[]{:S(2)}, u32[]{:S(2)}) collective-permute-start(bf16[1024,128]{1,0:T(8,128)(2,1)S(1)} %get-tuple-element.53.refs_0_), channel_id=1, source_target_pairs={{0,16},{8,24},{16,0},{24,8},{1,17},{9,25},{17,1},{25,9},{2,18},{10... | collective-permute-start | bytes 786440 | tf_op jit(solution)/shard_map/ppermute | solution.py:690
  7.4 8.7 %collective-permute-start = (bf16[1024,128]{1,0:T(8,128)(2,1)S(1)}, bf16[1024,128]{1,0:T(8,128)(2,1)S(1)}, u32[]{:S(2)}, u32[]{:S(2)}) collective-permute-start(bf16[1024,128]{1,0:T(8,128)(2,1)S(1)} %get-tuple-element.53.refs_0_), channel_id=1, source_target_pairs={{0,8},{8,0},{16,24},{24,16},{1,9},{9,1},{17,25},{25,17},{2,10},{10... | collective-permute-start | bytes 786440 | tf_op jit(solution)/shard_map/ppermute | solution.py:690
  7.4 8.7 %collective-permute-start.3 = (bf16[1024,128]{1,0:T(8,128)(2,1)S(1)}, bf16[1024,128]{1,0:T(8,128)(2,1)S(1)}, u32[]{:S(2)}, u32[]{:S(2)}) collective-permute-start(bf16[1024,128]{1,0:T(8,128)(2,1)S(1)} %get-tuple-element.52), channel_id=1, source_target_pairs={{0,4},{1,5},{2,6},{3,7},{4,0},{5,1},{6,2},{7,3},{8,12},{9,13},{10,... | collective-permute-start | bytes 786440 | tf_op jit(solution)/shard_map/ppermute | solution.py:256
  8.9 16.8 %copy-start.1 = (bf16[128,8,8,128]{3,2,1,0:T(8,128)(2,1)S(1)}, bf16[128,8,8,128]{3,2,1,0:T(8,128)(2,1)}, u32[]{:S(2)}) copy-start(bf16[128,8,8,128]{3,2,1,0:T(8,128)(2,1)} %param.7) | copy-start | bytes 6291460
  13.4 12.3 %copy-start = (bf16[128,8,8,128]{3,2,1,0:T(8,128)(2,1)S(1)}, bf16[128,8,8,128]{3,2,1,0:T(8,128)(2,1)}, u32[]{:S(2)}) copy-start(bf16[128,8,8,128]{3,2,1,0:T(8,128)(2,1)} %param.6) | copy-start | bytes 6291460
  13.7 2.4 %collective-permute-start.2 = (bf16[1024,128]{1,0:T(8,128)(2,1)S(1)}, bf16[1024,128]{1,0:T(8,128)(2,1)S(1)}, u32[]{:S(2)}, u32[]{:S(2)}) collective-permute-start(bf16[1024,128]{1,0:T(8,128)(2,1)S(1)} %collective-permute-done.1.refs_2_), channel_id=1, source_target_pairs={{0,8},{8,0},{16,24},{24,16},{1,9},{9,1},{17,25},{25,17},{2,10},{10... | collective-permute-start | bytes 786440 | tf_op jit(solution)/shard_map/ppermute | solution.py:690
  13.7 6.4 %collective-permute-start.6 = (bf16[1024,128]{1,0:T(8,128)(2,1)S(1)}, bf16[1024,128]{1,0:T(8,128)(2,1)S(1)}, u32[]{:S(2)}, u32[]{:S(2)}) collective-permute-start(bf16[1024,128]{1,0:T(8,128)(2,1)S(1)} %get-tuple-element.65), channel_id=1, source_target_pairs={{0,1},{1,0},{2,3},{3,2},{4,5},{5,4},{6,7},{7,6},{8,16},{9,17},{10,... | collective-permute-start | bytes 786440 | tf_op jit(solution)/shard_map/ppermute | solution.py:256
  15.5 4.6 %collective-permute-start.7 = (bf16[1024,128]{1,0:T(8,128)(2,1)S(1)}, bf16[1024,128]{1,0:T(8,128)(2,1)S(1)}, u32[]{:S(2)}, u32[]{:S(2)}) collective-permute-start(bf16[1024,128]{1,0:T(8,128)(2,1)S(1)} %get-tuple-element.66), channel_id=1, source_target_pairs={{0,8},{1,9},{2,10},{3,11},{4,12},{5,13},{6,14},{7,15},{8,0},{9,1},... | collective-permute-start | bytes 786440 | tf_op jit(solution)/shard_map/ppermute | solution.py:256
  16.8 4.3 %collective-permute-start.8 = (f32[128,128]{1,0:T(8,128)S(1)}, f32[128,128]{1,0:T(8,128)S(1)}, u32[]{:S(2)}, u32[]{:S(2)}) collective-permute-start(f32[128,128]{1,0:T(8,128)S(1)} %get-tuple-element.68), channel_id=1, source_target_pairs={{0,4},{4,0},{1,5},{5,1},{2,6},{6,2},{3,7},{7,3},{8,12},{12,8},{9,1... | collective-permute-start | bytes 196616 | tf_op jit(solution)/shard_map/ppermute | solution.py:210
  18.4 7.3 %collective-permute-start.5 = (bf16[128,128]{1,0:T(8,128)(2,1)S(1)}, bf16[128,128]{1,0:T(8,128)(2,1)S(1)}, u32[]{:S(2)}, u32[]{:S(2)}) collective-permute-start(bf16[128,128]{1,0:T(8,128)(2,1)S(1)} %get-tuple-element.61), channel_id=1, source_target_pairs={{0,1},{1,0},{2,3},{3,2},{4,5},{5,4},{6,7},{7,6},{8,9},{9,8},{10,11... | collective-permute-start | bytes 98312 | tf_op jit(solution)/shard_map/ppermute | solution.py:256
  20.0 5.7 %collective-permute-start.4 = (bf16[128,128]{1,0:T(8,128)(2,1)S(1)}, bf16[128,128]{1,0:T(8,128)(2,1)S(1)}, u32[]{:S(2)}, u32[]{:S(2)}) collective-permute-start(bf16[128,128]{1,0:T(8,128)(2,1)S(1)} %get-tuple-element.61), channel_id=1, source_target_pairs={{0,8},{1,2},{2,1},{3,11},{4,12},{5,6},{6,5},{7,15},{8,0},{9,10},{1... | collective-permute-start | bytes 98312 | tf_op jit(solution)/shard_map/ppermute | solution.py:256
  21.3 6.5 %collective-permute-start.9 = (f32[64,128]{1,0:T(8,128)S(1)}, f32[64,128]{1,0:T(8,128)S(1)}, u32[]{:S(2)}, u32[]{:S(2)}) collective-permute-start(f32[64,128]{1,0:T(8,128)S(1)} %get-tuple-element.71), channel_id=1, source_target_pairs={{0,3},{1,2},{2,1},{3,0},{4,7},{5,6},{6,5},{7,4},{8,11},{9,10},{10,... | collective-permute-start | bytes 98312 | tf_op jit(solution)/shard_map/ppermute | solution.py:215
  24.9 4.8 %collective-permute-start.10 = (f32[64,128]{1,0:T(8,128)S(1)}, f32[64,128]{1,0:T(8,128)S(1)}, u32[]{:S(2)}, u32[]{:S(2)}) collective-permute-start(f32[64,128]{1,0:T(8,128)S(1)} %get-tuple-element.72), channel_id=1, source_target_pairs={{0,2},{1,3},{2,0},{3,1},{4,6},{5,7},{6,4},{7,5},{8,10},{9,11},{10,... | collective-permute-start | bytes 98312 | tf_op jit(solution)/shard_map/ppermute | solution.py:215
  24.9 4.8 %collective-permute-start.11 = (f32[64,128]{1,0:T(8,128)S(1)}, f32[64,128]{1,0:T(8,128)S(1)}, u32[]{:S(2)}, u32[]{:S(2)}) collective-permute-start(f32[64,128]{1,0:T(8,128)S(1)} %get-tuple-element.73), channel_id=1, source_target_pairs={{0,1},{1,0},{2,3},{3,2},{4,5},{5,4},{6,7},{7,6},{8,9},{9,8},{10,11... | collective-permute-start | bytes 98312 | tf_op jit(solution)/shard_map/ppermute | solution.py:215
  25.7 4.0 %copy-start.4 = (s32[1,1,1,32]{3,2,1,0:T(1,128)S(1)}, s32[1,1,1,32]{3,2,1,0:T(1,128)}, u32[]{:S(2)}) copy-start(s32[1,1,1,32]{3,2,1,0:T(1,128)} %refs_6_.1) | copy-start | bytes 388
  33.4 8.6 %collective-permute-start.12 = (bf16[1024,128]{1,0:T(8,128)(2,1)S(1)}, bf16[1024,128]{1,0:T(8,128)(2,1)S(1)}, u32[]{:S(2)}, u32[]{:S(2)}) collective-permute-start(bf16[1024,128]{1,0:T(8,128)(2,1)S(1)} %get-tuple-element.77), channel_id=1, source_target_pairs={{0,4},{1,5},{2,6},{3,7},{4,0},{5,1},{6,2},{7,3},{8,12},{9,13},{10,... | collective-permute-start | bytes 786440 | tf_op jit(solution)/shard_map/ppermute | solution.py:256
  34.9 7.1 %collective-permute-start.13 = (bf16[1024,128]{1,0:T(8,128)(2,1)S(1)}, bf16[1024,128]{1,0:T(8,128)(2,1)S(1)}, u32[]{:S(2)}, u32[]{:S(2)}) collective-permute-start(bf16[1024,128]{1,0:T(8,128)(2,1)S(1)} %get-tuple-element.78), channel_id=1, source_target_pairs={{0,1},{1,0},{2,3},{3,2},{4,5},{5,4},{6,7},{7,6},{8,16},{9,17},{10,... | collective-permute-start | bytes 786440 | tf_op jit(solution)/shard_map/ppermute | solution.py:256
  34.9 7.1 %collective-permute-start.14 = (bf16[1024,128]{1,0:T(8,128)(2,1)S(1)}, bf16[1024,128]{1,0:T(8,128)(2,1)S(1)}, u32[]{:S(2)}, u32[]{:S(2)}) collective-permute-start(bf16[1024,128]{1,0:T(8,128)(2,1)S(1)} %get-tuple-element.79), channel_id=1, source_target_pairs={{0,8},{1,9},{2,10},{3,11},{4,12},{5,13},{6,14},{7,15},{8,0},{9,1},... | collective-permute-start | bytes 786440 | tf_op jit(solution)/shard_map/ppermute | solution.py:256
  35.9 6.1 %collective-permute-start.16 = (bf16[128,128]{1,0:T(8,128)(2,1)S(1)}, bf16[128,128]{1,0:T(8,128)(2,1)S(1)}, u32[]{:S(2)}, u32[]{:S(2)}) collective-permute-start(bf16[128,128]{1,0:T(8,128)(2,1)S(1)} %get-tuple-element.80), channel_id=1, source_target_pairs={{0,1},{1,0},{2,3},{3,2},{4,5},{5,4},{6,7},{7,6},{8,9},{9,8},{10,11... | collective-permute-start | bytes 98312 | tf_op jit(solution)/shard_map/ppermute | solution.py:256
  36.9 5.0 %collective-permute-start.15 = (bf16[128,128]{1,0:T(8,128)(2,1)S(1)}, bf16[128,128]{1,0:T(8,128)(2,1)S(1)}, u32[]{:S(2)}, u32[]{:S(2)}) collective-permute-start(bf16[128,128]{1,0:T(8,128)(2,1)S(1)} %get-tuple-element.80), channel_id=1, source_target_pairs={{0,8},{1,2},{2,1},{3,11},{4,12},{5,6},{6,5},{7,15},{8,0},{9,10},{1... | collective-permute-start | bytes 98312 | tf_op jit(solution)/shard_map/ppermute | solution.py:256
  45.1 7.4 %collective-permute-start.17 = (bf16[1024,128]{1,0:T(8,128)(2,1)S(1)}, bf16[1024,128]{1,0:T(8,128)(2,1)S(1)}, u32[]{:S(2)}, u32[]{:S(2)}) collective-permute-start(bf16[1024,128]{1,0:T(8,128)(2,1)S(1)} %get-tuple-element.83), channel_id=1, source_target_pairs={{0,4},{1,5},{2,6},{3,7},{4,0},{5,1},{6,2},{7,3},{8,12},{9,13},{10,... | collective-permute-start | bytes 786440 | tf_op jit(solution)/shard_map/ppermute | solution.py:256
  45.6 6.9 %collective-permute-start.18 = (bf16[1024,128]{1,0:T(8,128)(2,1)S(1)}, bf16[1024,128]{1,0:T(8,128)(2,1)S(1)}, u32[]{:S(2)}, u32[]{:S(2)}) collective-permute-start(bf16[1024,128]{1,0:T(8,128)(2,1)S(1)} %get-tuple-element.84), channel_id=1, source_target_pairs={{0,1},{1,0},{2,3},{3,2},{4,5},{5,4},{6,7},{7,6},{8,16},{9,17},{10,... | collective-permute-start | bytes 786440 | tf_op jit(solution)/shard_map/ppermute | solution.py:256
  45.6 6.9 %collective-permute-start.19 = (bf16[1024,128]{1,0:T(8,128)(2,1)S(1)}, bf16[1024,128]{1,0:T(8,128)(2,1)S(1)}, u32[]{:S(2)}, u32[]{:S(2)}) collective-permute-start(bf16[1024,128]{1,0:T(8,128)(2,1)S(1)} %get-tuple-element.85), channel_id=1, source_target_pairs={{0,8},{1,9},{2,10},{3,11},{4,12},{5,13},{6,14},{7,15},{8,0},{9,1},... | collective-permute-start | bytes 786440 | tf_op jit(solution)/shard_map/ppermute | solution.py:256
  45.6 6.9 %collective-permute-start.21 = (bf16[128,128]{1,0:T(8,128)(2,1)S(1)}, bf16[128,128]{1,0:T(8,128)(2,1)S(1)}, u32[]{:S(2)}, u32[]{:S(2)}) collective-permute-start(bf16[128,128]{1,0:T(8,128)(2,1)S(1)} %get-tuple-element.86), channel_id=1, source_target_pairs={{0,1},{1,0},{2,3},{3,2},{4,5},{5,4},{6,7},{7,6},{8,9},{9,8},{10,11... | collective-permute-start | bytes 98312 | tf_op jit(solution)/shard_map/ppermute | solution.py:256
  47.6 4.9 %collective-permute-start.20 = (bf16[128,128]{1,0:T(8,128)(2,1)S(1)}, bf16[128,128]{1,0:T(8,128)(2,1)S(1)}, u32[]{:S(2)}, u32[]{:S(2)}) collective-permute-start(bf16[128,128]{1,0:T(8,128)(2,1)S(1)} %get-tuple-element.86), channel_id=1, source_target_pairs={{0,8},{1,2},{2,1},{3,11},{4,12},{5,6},{6,5},{7,15},{8,0},{9,10},{1... | collective-permute-start | bytes 98312 | tf_op jit(solution)/shard_map/ppermute | solution.py:256
